TPU v7x, 32 devices: a whole 2x2x4 slice. The times are simulated.
32 devices in a mesh: seq: 8 (over z, x), dp: 4 (over y, core).
Axes of the slice: x: 2, y: 2, z: 4, core: 2. Of those that a mesh axis runs over, the one named last changes fastest.
Arguments:
- tokens: bfloat16 [8, 1024, 2048], P('dp', 'seq'), may hold values from -6 to 6
- per_layer: bfloat16 [8, 1024, 256], P('dp', 'seq'), may hold values from -6 to 6
- positions: int32 [8, 1024], P('dp', 'seq'), may hold values from 0 to 1023, as said below
- span_start: int32 [8, 2], P('dp'), may hold values from 0 to 768, as said below
- cotangent: bfloat16 [8, 1024, 2048], P('dp', 'seq'), may hold values from -6 to 6
- query_weight: bfloat16 [2048, 2048], P(('seq', 'dp')), may hold values from -0.125 to 0.125
- key_weight: bfloat16 [2048, 512], P(('seq', 'dp')), may hold values from -0.125 to 0.125
- value_weight: bfloat16 [2048, 512], P(('seq', 'dp')), may hold values from -0.125 to 0.125
- output_weight: bfloat16 [2048, 2048], P(('seq', 'dp')), may hold values from -0.125 to 0.125
- laurel_left: bfloat16 [2048, 64], P(('seq', 'dp')), may hold values from -0.125 to 0.125
- laurel_right: bfloat16 [2048, 64], P(('seq', 'dp')), may hold values from -0.75 to 0.75
- gate_weight: bfloat16 [2048, 8192], P(('seq', 'dp')), may hold values from -0.125 to 0.125
- up_weight: bfloat16 [2048, 8192], P(('seq', 'dp')), may hold values from -0.125 to 0.125
- down_weight: bfloat16 [2048, 8192], P(('seq', 'dp')), may hold values from -0.0625 to 0.0625
- side_gate: bfloat16 [2048, 256], P(('seq', 'dp')), may hold values from -0.125 to 0.125
- side_output: bfloat16 [2048, 256], P(('seq', 'dp')), may hold values from -0.375 to 0.375
- norm_input: float32 [2048], replicated, may hold values from 0.25 to 1.75
- norm_attn: float32 [2048], replicated, may hold values from 0.25 to 1.75
- norm_laurel: float32 [2048], replicated, may hold values from 0.25 to 1.75
- norm_before: float32 [2048], replicated, may hold values from 0.25 to 1.75
- norm_after: float32 [2048], replicated, may hold values from 0.25 to 1.75
- norm_layer: float32 [2048], replicated, may hold values from 0.25 to 1.75
- norm_query: float32 [256], replicated, may hold values from 0.2 to 0.5
- norm_key: float32 [256], replicated, may hold values from 0.2 to 0.5
Outputs:
- output: bfloat16 [8, 1024, 2048], P('dp', 'seq')
- grad_tokens: float32 [8, 1024, 2048], P('dp', 'seq')
- grad_per_layer: float32 [8, 1024, 256], P('dp', 'seq')
- grad_query: float32 [2048, 2048], P(('seq', 'dp'))
- grad_key: float32 [2048, 512], P(('seq', 'dp'))
- grad_value: float32 [2048, 512], P(('seq', 'dp'))
- grad_output: float32 [2048, 2048], P(('seq', 'dp'))
- grad_left: float32 [2048, 64], P(('seq', 'dp'))
- grad_right: float32 [2048, 64], P(('seq', 'dp'))
- grad_gate: float32 [2048, 8192], P(('seq', 'dp'))
- grad_up: float32 [2048, 8192], P(('seq', 'dp'))
- grad_down: float32 [2048, 8192], P(('seq', 'dp'))
- grad_side_gate: float32 [2048, 256], P(('seq', 'dp'))
- grad_side_output: float32 [2048, 256], P(('seq', 'dp'))
- grad_norm_input: float32 [2048], replicated
- grad_norm_attn: float32 [2048], replicated
- grad_norm_laurel: float32 [2048], replicated
- grad_norm_before: float32 [2048], replicated
- grad_norm_after: float32 [2048], replicated
- grad_norm_layer: float32 [2048], replicated
- grad_norm_query: float32 [256], replicated
- grad_norm_key: float32 [256], replicated
Inputs may be any that keep to these rules, and one draw needn't show every extreme that they name: Each sequence is a pack of documents: a token's position is the number of tokens before it in its own document, so positions rise by 1 and fall to 0 where a new document begins; the first token of a sequence has position 0, and one sequence is a single document. `span_start`: each sequence holds 2 picture spans of 256 tokens; span s starts within tokens [4 * s * 128, 4 * (s + 1) * 128 - 256], so spans never intersect.
All inputs are finite; a program needn't handle non-finite values.
Results may differ from a plain program's by a relative error of at most 0.019.
Values may be sent and summed in bfloat16 or wider, within the bound.
No kernel may reach another device: no remote copies, remote signals or barrier semaphores. Data moves between devices by JAX's collectives and lax.ppermute only.
A program may use at most 448 MiB of HBM per device.

v0:
```python
import math

import jax
import jax.numpy as jnp
from jax import lax
from jax.sharding import PartitionSpec as P

WINDOW = 512
SPAN = 256


EPS = 1e-06
HALF_ROOT = 1.0 / math.sqrt(2.0)


def passed_along(value, axis, steps):
    count = lax.axis_size(axis)
    initial, last = (max(0, -steps), min(count, count - steps))
    return lax.ppermute(value, axis, [(source, source + steps) for source in range(initial, last)])


def rms(values, gain):
    return values * lax.rsqrt(jnp.mean(values * values, axis=-1, keepdims=True) + EPS) * gain


def gelu_tanh(values):
    return jax.nn.gelu(values, approximate=True)


def product(left, right):
    return jnp.dot(left, right, preferred_element_type=jnp.float32)


def product_nt(left, right):
    return lax.dot_general(
        left, right, (((1,), (1,)), ((), ())), preferred_element_type=jnp.float32
    )


def product_tn(left, right):
    return lax.dot_general(
        left, right, (((0,), (0,)), ((), ())), preferred_element_type=jnp.float32
    )


def rotate(values, places):
    size = values.shape[-1]
    half = size // 2
    freq = 10000.0 ** (-(2.0 * jnp.arange(half, dtype=jnp.float32)) / size)
    angle = places.astype(jnp.float32)[..., None] * freq
    cosine = jnp.cos(angle)[..., None, :]
    sine = jnp.sin(angle)[..., None, :]
    first = values[..., :half]
    second = values[..., half:]
    return jnp.concatenate(
        [first * cosine - second * sine, second * cosine + first * sine], axis=-1
    )


def middle(inputs, normed, attn_proj, laurel, gain_attn, gain_laurel, gain_before):
    resid = (inputs + rms(attn_proj, gain_attn) + normed + rms(laurel, gain_laurel)) * HALF_ROOT
    return (resid, rms(resid, gain_before))


def gate_act(gate_val, up_val):
    return gelu_tanh(gate_val) * up_val


def after_feed(resid_one, feed_out, gain_after):
    return resid_one + rms(feed_out, gain_after)


def side_act(side_pre, side_in):
    return gelu_tanh(side_pre) * side_in


def finish(resid_two, side_out, gain_layer):
    return resid_two + rms(side_out, gain_layer)


def terms_from(pairs):
    parts = [product_tn(first, second) for first, second in pairs]
    return jnp.concatenate(parts, axis=1)


def split_columns(whole, widths):
    pieces = []
    offset = 0
    for width_one in widths:
        pieces.append(whole[:, offset : offset + width_one])
        offset = offset + width_one
    return pieces


def one_micro(
    tokens, per_layer, positions, span_start, cotangent, attn_local, feed_local, gain_list
):
    (
        norm_input,
        norm_attn,
        norm_laurel,
        norm_before,
        norm_after,
        norm_layer,
        norm_query,
        norm_key,
    ) = gain_list
    batch, block, width = tokens.shape
    rows = batch * block
    head_size = norm_query.shape[0]
    heads = attn_local[0].shape[1] // head_size
    kv_heads = attn_local[1].shape[1] // head_size
    group = heads // kv_heads
    inputs = tokens.astype(jnp.float32).reshape(rows, width)
    side_in = per_layer.astype(jnp.float32).reshape(rows, -1)
    upstream = cotangent.astype(jnp.float32).reshape(rows, width)
    attn_full = (
        lax.all_gather(attn_local[0], ("seq", "dp"), axis=0, tiled=True),
        lax.all_gather(attn_local[1], ("seq", "dp"), axis=0, tiled=True),
        lax.all_gather(attn_local[2], ("seq", "dp"), axis=0, tiled=True),
        lax.all_gather(attn_local[3], ("seq", "dp"), axis=0, tiled=True),
        lax.all_gather(attn_local[4], ("seq", "dp"), axis=0, tiled=True),
        lax.all_gather(attn_local[5], ("seq", "dp"), axis=0, tiled=True),
    )
    feed_full = (
        lax.all_gather(feed_local[0], ("seq", "dp"), axis=0, tiled=True),
        lax.all_gather(feed_local[1], ("seq", "dp"), axis=0, tiled=True),
        lax.all_gather(feed_local[2], ("seq", "dp"), axis=0, tiled=True),
        lax.all_gather(feed_local[3], ("seq", "dp"), axis=0, tiled=True),
        lax.all_gather(feed_local[4], ("seq", "dp"), axis=0, tiled=True),
    )
    normed, pre_pull = jax.vjp(rms, inputs, norm_input)
    normed_low = normed.astype(jnp.bfloat16)
    queries = product(normed_low, attn_full[0]).reshape(batch, block, heads, head_size)
    keys = product(normed_low, attn_full[1]).reshape(batch, block, kv_heads, head_size)
    values = product(normed_low, attn_full[2]).reshape(batch, block, kv_heads, head_size)

    def head_prep(query_in, key_in, value_in, gain_query, gain_key):
        return (
            rotate(rms(query_in, gain_query), positions),
            rotate(rms(key_in, gain_key), positions),
            rms(value_in, 1.0),
        )

    (rot_query, rot_key, rot_value), prep_pull = jax.vjp(
        head_prep, queries, keys, values, norm_query, norm_key
    )
    query_low = rot_query.astype(jnp.bfloat16)
    pair_low = jnp.stack([rot_key.astype(jnp.bfloat16), rot_value.astype(jnp.bfloat16)])
    left_count = WINDOW // block
    right_count = (SPAN + block - 2) // block
    offsets = list(range(left_count, 0, -1)) + [0] + list(range(-1, -right_count - 1, -1))
    gathered = []
    for offset in offsets:
        if offset == 0:
            gathered.append(pair_low)
        else:
            gathered.append(passed_along(pair_low, "seq", offset))
    pairs_all = jnp.concatenate(gathered, axis=2)
    keys_all = pairs_all[0]
    values_all = pairs_all[1]
    key_count = keys_all.shape[1]
    seq_index = lax.axis_index("seq")
    total_length = block * lax.axis_size("seq")
    query_places = seq_index * block + jnp.arange(block, dtype=jnp.int32)
    key_places = (seq_index - left_count) * block + jnp.arange(key_count, dtype=jnp.int32)
    in_query = (query_places[None, :, None] >= span_start[:, None, :]) & (
        query_places[None, :, None] < span_start[:, None, :] + SPAN
    )
    in_key = (key_places[None, :, None] >= span_start[:, None, :]) & (
        key_places[None, :, None] < span_start[:, None, :] + SPAN
    )
    same = jnp.any(in_query[:, :, None, :] & in_key[:, None, :, :], axis=-1)
    near = (key_places[None, :] <= query_places[:, None]) & (
        query_places[:, None] - key_places[None, :] < WINDOW
    )
    valid = (key_places >= 0) & (key_places < total_length)
    allowed = (valid[None, None, :] & (near[None] | same))[:, None, None]
    query_group = query_low.reshape(batch, block, kv_heads, group, head_size)
    scores = jnp.einsum(
        "btkgd,bskd->bkgts", query_group, keys_all, preferred_element_type=jnp.float32
    )
    masked = jnp.where(allowed, scores, -1e30)
    top = jnp.max(masked, axis=-1, keepdims=True)
    expo = jnp.exp(masked - top)
    total = jnp.sum(expo, axis=-1, keepdims=True)
    probs = expo / total
    logsum = top + jnp.log(total)
    probs_low = probs.astype(jnp.bfloat16)
    attended = jnp.einsum(
        "bkgts,bskd->btkgd", probs_low, values_all, preferred_element_type=jnp.float32
    )
    attended_low = attended.reshape(rows, heads * head_size).astype(jnp.bfloat16)
    attn_proj = product_nt(attended_low, attn_full[3])
    latent_low = product(normed_low, attn_full[4]).astype(jnp.bfloat16)
    laurel = product_nt(latent_low, attn_full[5])
    (resid_one, feed_in), mid_pull = jax.vjp(
        middle, inputs, normed, attn_proj, laurel, norm_attn, norm_laurel, norm_before
    )
    feed_low = feed_in.astype(jnp.bfloat16)
    gate_val = product(feed_low, feed_full[0])
    up_val = product(feed_low, feed_full[1])
    hidden, gate_pull = jax.vjp(gate_act, gate_val, up_val)
    hidden_low = hidden.astype(jnp.bfloat16)
    feed_out = product_nt(hidden_low, feed_full[2])
    resid_two, after_pull = jax.vjp(after_feed, resid_one, feed_out, norm_after)
    resid_low = resid_two.astype(jnp.bfloat16)
    side_pre = product(resid_low, feed_full[3])
    side_val, side_pull = jax.vjp(side_act, side_pre, side_in)
    side_low = side_val.astype(jnp.bfloat16)
    side_out = product_nt(side_low, feed_full[4])
    result, final_pull = jax.vjp(finish, resid_two, side_out, norm_layer)
    output = result.astype(jnp.bfloat16).reshape(batch, block, width)
    attn_back = (
        lax.all_gather(attn_local[0], ("seq", "dp"), axis=0, tiled=True),
        lax.all_gather(attn_local[1], ("seq", "dp"), axis=0, tiled=True),
        lax.all_gather(attn_local[2], ("seq", "dp"), axis=0, tiled=True),
        lax.all_gather(attn_local[3], ("seq", "dp"), axis=0, tiled=True),
        lax.all_gather(attn_local[4], ("seq", "dp"), axis=0, tiled=True),
        lax.all_gather(attn_local[5], ("seq", "dp"), axis=0, tiled=True),
    )
    feed_back = (
        lax.all_gather(feed_local[0], ("seq", "dp"), axis=0, tiled=True),
        lax.all_gather(feed_local[1], ("seq", "dp"), axis=0, tiled=True),
        lax.all_gather(feed_local[2], ("seq", "dp"), axis=0, tiled=True),
        lax.all_gather(feed_local[3], ("seq", "dp"), axis=0, tiled=True),
        lax.all_gather(feed_local[4], ("seq", "dp"), axis=0, tiled=True),
    )
    d_resid_two, d_side_out, grad_norm_layer = final_pull(upstream)
    d_side_out_low = d_side_out.astype(jnp.bfloat16)
    d_side = product(d_side_out_low, feed_back[4])
    d_side_pre, d_side_in = side_pull(d_side)
    d_side_pre_low = d_side_pre.astype(jnp.bfloat16)
    d_resid_two = d_resid_two + product_nt(d_side_pre_low, feed_back[3])
    d_resid_one, d_feed_out, grad_norm_after = after_pull(d_resid_two)
    d_feed_out_low = d_feed_out.astype(jnp.bfloat16)
    d_hidden = product(d_feed_out_low, feed_back[2])
    d_gate, d_up = gate_pull(d_hidden)
    d_gate_low = d_gate.astype(jnp.bfloat16)
    d_up_low = d_up.astype(jnp.bfloat16)
    d_feed_in = product_nt(d_gate_low, feed_back[0]) + product_nt(d_up_low, feed_back[1])
    (
        d_inputs,
        d_normed,
        d_attn_proj,
        d_laurel,
        grad_norm_attn,
        grad_norm_laurel,
        grad_norm_before,
    ) = mid_pull((d_resid_one, d_feed_in))
    d_attn_low = d_attn_proj.astype(jnp.bfloat16)
    d_laurel_low = d_laurel.astype(jnp.bfloat16)
    d_attended_low = product(d_attn_low, attn_back[3]).astype(jnp.bfloat16)
    d_latent_low = product(d_laurel_low, attn_back[5]).astype(jnp.bfloat16)
    d_normed = d_normed + product_nt(d_latent_low, attn_back[4])
    d_att = d_attended_low.reshape(batch, block, kv_heads, group, head_size)
    again_scores = jnp.einsum(
        "btkgd,bskd->bkgts", query_group, keys_all, preferred_element_type=jnp.float32
    )
    again_probs = jnp.exp(jnp.where(allowed, again_scores, -1e30) - logsum)
    again_low = again_probs.astype(jnp.bfloat16)
    d_values_all = jnp.einsum(
        "bkgts,btkgd->bskd", again_low, d_att, preferred_element_type=jnp.float32
    )
    d_probs = jnp.einsum("btkgd,bskd->bkgts", d_att, values_all, preferred_element_type=jnp.float32)
    d_scores = again_probs * (d_probs - jnp.sum(again_probs * d_probs, axis=-1, keepdims=True))
    d_scores_low = d_scores.astype(jnp.bfloat16)
    d_query_rot = jnp.einsum(
        "bkgts,bskd->btkgd", d_scores_low, keys_all, preferred_element_type=jnp.float32
    )
    d_keys_all = jnp.einsum(
        "bkgts,btkgd->bskd", d_scores_low, query_group, preferred_element_type=jnp.float32
    )
    d_pairs = jnp.stack([d_keys_all, d_values_all])
    d_pair_total = d_pairs[:, :, left_count * block : (left_count + 1) * block]
    for position, offset in enumerate(offsets):
        if offset != 0:
            piece = d_pairs[:, :, position * block : (position + 1) * block]
            d_pair_total = d_pair_total + passed_along(
                piece.astype(jnp.bfloat16), "seq", -offset
            ).astype(piece.dtype)
    d_queries, d_keys, d_values, grad_norm_query, grad_norm_key = prep_pull(
        (d_query_rot.reshape(batch, block, heads, head_size), d_pair_total[0], d_pair_total[1])
    )
    d_queries_low = d_queries.reshape(rows, -1).astype(jnp.bfloat16)
    d_keys_low = d_keys.reshape(rows, -1).astype(jnp.bfloat16)
    d_values_low = d_values.reshape(rows, -1).astype(jnp.bfloat16)
    d_normed = (
        d_normed
        + product_nt(d_queries_low, attn_back[0])
        + product_nt(d_keys_low, attn_back[1])
        + product_nt(d_values_low, attn_back[2])
    )
    d_inputs_norm, grad_norm_input = pre_pull(d_normed)
    grad_tokens = (d_inputs + d_inputs_norm).reshape(batch, block, width)
    grad_side = d_side_in.reshape(batch, block, -1)
    gain_terms = (
        grad_norm_input,
        grad_norm_attn,
        grad_norm_laurel,
        grad_norm_before,
        grad_norm_after,
        grad_norm_layer,
        grad_norm_query,
        grad_norm_key,
    )
    attn_pairs = (
        (normed_low, d_queries_low),
        (normed_low, d_keys_low),
        (normed_low, d_values_low),
        (d_attn_low, attended_low),
        (normed_low, d_latent_low),
        (d_laurel_low, latent_low),
    )
    feed_pairs = (
        (feed_low, d_gate_low),
        (feed_low, d_up_low),
        (d_feed_out_low, hidden_low),
        (resid_low, d_side_pre_low),
        (d_side_out_low, side_low),
    )
    return (output, grad_tokens, grad_side, gain_terms, attn_pairs, feed_pairs)


def join_pairs(pair_lists):
    joined = []
    for index in range(len(pair_lists[0])):
        firsts = jnp.concatenate([pairs[index][0] for pairs in pair_lists], axis=0)
        seconds = jnp.concatenate([pairs[index][1] for pairs in pair_lists], axis=0)
        joined.append((firsts, seconds))
    return tuple(joined)


def body(
    tokens,
    per_layer,
    positions,
    span_start,
    cotangent,
    query_weight,
    key_weight,
    value_weight,
    output_weight,
    laurel_left,
    laurel_right,
    gate_weight,
    up_weight,
    down_weight,
    side_gate,
    side_output,
    norm_input,
    norm_attn,
    norm_laurel,
    norm_before,
    norm_after,
    norm_layer,
    norm_query,
    norm_key,
):
    attn_local = (query_weight, key_weight, value_weight, output_weight, laurel_left, laurel_right)
    feed_local = (gate_weight, up_weight, down_weight, side_gate, side_output)
    gain_list = (
        norm_input,
        norm_attn,
        norm_laurel,
        norm_before,
        norm_after,
        norm_layer,
        norm_query,
        norm_key,
    )
    micro_count = tokens.shape[0]
    outputs = []
    grads_in = []
    grads_side = []
    gain_total = None
    attn_lists = []
    feed_lists = []
    for micro in range(micro_count):
        output, grad_tokens, grad_side, gain_terms, attn_pairs, feed_pairs = one_micro(
            tokens[micro : micro + 1],
            per_layer[micro : micro + 1],
            positions[micro : micro + 1],
            span_start[micro : micro + 1],
            cotangent[micro : micro + 1],
            attn_local,
            feed_local,
            gain_list,
        )
        outputs.append(output)
        grads_in.append(grad_tokens)
        grads_side.append(grad_side)
        if gain_total is None:
            gain_total = gain_terms
        else:
            gain_total = tuple((first + second for first, second in zip(gain_total, gain_terms)))
        attn_lists.append(attn_pairs)
        feed_lists.append(feed_pairs)
    gains = lax.psum(gain_total, ("seq", "dp"))
    attn_sum = lax.psum_scatter(
        terms_from(join_pairs(attn_lists)), ("seq", "dp"), scatter_dimension=0, tiled=True
    )
    feed_sum = lax.psum_scatter(
        terms_from(join_pairs(feed_lists)), ("seq", "dp"), scatter_dimension=0, tiled=True
    )
    attn_parts = split_columns(attn_sum, [matrix.shape[1] for matrix in attn_local])
    feed_parts = split_columns(feed_sum, [matrix.shape[1] for matrix in feed_local])
    return (
        jnp.concatenate(outputs, axis=0),
        jnp.concatenate(grads_in, axis=0),
        jnp.concatenate(grads_side, axis=0),
        attn_parts[0],
        attn_parts[1],
        attn_parts[2],
        attn_parts[3],
        attn_parts[4],
        attn_parts[5],
        feed_parts[0],
        feed_parts[1],
        feed_parts[2],
        feed_parts[3],
        feed_parts[4],
        gains[0],
        gains[1],
        gains[2],
        gains[3],
        gains[4],
        gains[5],
        gains[6],
        gains[7],
    )


def solution(mesh):
    return jax.shard_map(
        body,
        mesh=mesh,
        in_specs=(
            P("dp", "seq", None),
            P("dp", "seq", None),
            P("dp", "seq"),
            P("dp", None),
            P("dp", "seq", None),
            P(("seq", "dp"), None),
            P(("seq", "dp"), None),
            P(("seq", "dp"), None),
            P(("seq", "dp"), None),
            P(("seq", "dp"), None),
            P(("seq", "dp"), None),
            P(("seq", "dp"), None),
            P(("seq", "dp"), None),
            P(("seq", "dp"), None),
            P(("seq", "dp"), None),
            P(("seq", "dp"), None),
            P(),
            P(),
            P(),
            P(),
            P(),
            P(),
            P(),
            P(),
        ),
        out_specs=(
            P("dp", "seq", None),
            P("dp", "seq", None),
            P("dp", "seq", None),
            P(("seq", "dp"), None),
            P(("seq", "dp"), None),
            P(("seq", "dp"), None),
            P(("seq", "dp"), None),
            P(("seq", "dp"), None),
            P(("seq", "dp"), None),
            P(("seq", "dp"), None),
            P(("seq", "dp"), None),
            P(("seq", "dp"), None),
            P(("seq", "dp"), None),
            P(("seq", "dp"), None),
            P(),
            P(),
            P(),
            P(),
            P(),
            P(),
            P(),
            P(),
        ),
        check_vma=False,
    )
```

profile of v0, /device:TPU:0, one launch (start us, length us, event | category | flops | bytes accessed | tf_op | source)
XLA Modules:
  0.0 3959.5 jit_solution(6625298553561041195)
XLA Ops:
  17.5 45.0 %all_gather.26 = bf16[2048,64]{1,0:T(8,128)(2,1)S(1)} all-gather(bf16[64,64]{1,0:T(8,128)(2,1)S(1)} %copy-done.199), channel_id=1, replica_groups=mesh['seq'=8,'dp'=4] {'seq','dp'}, dimensions={0}, use_global_device_ids=true | all-gather | bytes 270336 | tf_op jit(solution)/shard_map/all_gather | solution.py:122
  62.6 38.3 all_gather.27
  114.2 14.7 all-gather.10.cloned.1.call-done
  157.3 12.9 collective-permute-done.6
  175.2 19.9 collective-permute-start.2
  196.1 5.2 collective-permute-start
  204.6 13.7 collective-permute-done
  220.7 8.1 collective-permute-done.1
  234.6 11.7 collective-permute-done.10
  246.4 8.1 collective-permute-done.11
  256.0 4.7 fusion.258
  262.1 4.6 fusion.262
  275.4 49.9 %all-gather.16.cloned.1.call-done = bf16[2048,2048]{1,0:T(8,128)(2,1)} async-done(((bf16[64,2048]{1,0:T(8,128)(2,1)}), bf16[2048,2048]{1,0:T(8,128)(2,1)}) %all-gather.16.cloned.1.call-update) | async-done | bytes 8388624 | tf_op jit(solution)/shard_map/all_gather | solution.py:121
  325.2 6.4 multiply_reduce_fusion.22
  334.8 4.4 fusion.65
  347.4 174.0 %all-gather.18.cloned.1.call-done = bf16[2048,8192]{1,0:T(8,128)(2,1)} async-done(((bf16[64,8192]{1,0:T(8,128)(2,1)}), bf16[2048,8192]{1,0:T(8,128)(2,1)}) %all-gather.18.cloned.1.call-update) | async-done | bytes 33554448 | tf_op jit(solution)/shard_map/all_gather | solution.py:126
  521.4 17.8 fusion.259
  539.2 17.7 fusion.263
  556.9 160.2 %all-gather.20.cloned.1.call-done = bf16[2048,8192]{1,0:T(8,128)(2,1)} async-done(((bf16[64,8192]{1,0:T(8,128)(2,1)}), bf16[2048,8192]{1,0:T(8,128)(2,1)}) %all-gather.20.cloned.1.call-update) | async-done | bytes 33554448 | tf_op jit(solution)/shard_map/all_gather | solution.py:127
  717.1 18.4 multiply_convert_fusion.2
  735.5 16.6 multiply_convert_fusion.3
  752.1 160.9 %all-gather.22.cloned.1.call-done = bf16[2048,8192]{1,0:T(8,128)(2,1)} async-done(((bf16[64,8192]{1,0:T(8,128)(2,1)}), bf16[2048,8192]{1,0:T(8,128)(2,1)}) %all-gather.22.cloned.1.call-update) | async-done | bytes 33554448 | tf_op jit(solution)/shard_map/all_gather | solution.py:128
  912.9 16.6 multiply_reduce_fusion.19
  929.6 16.8 multiply_reduce_fusion.24
  948.7 19.0 all-gather.24.cloned.1.call-done
  971.9 51.5 %all-gather.26.cloned.1.call-done = bf16[2048,256]{1,0:T(8,128)(2,1)} async-done(((bf16[64,256]{1,0:T(8,128)(2,1)}), bf16[2048,256]{1,0:T(8,128)(2,1)}) %all-gather.26.cloned.1.call-update) | async-done | bytes 1048592 | tf_op jit(solution)/shard_map/all_gather | solution.py:130
  1035.3 18.9 multiply_convert_fusion.1
  1054.2 16.4 fusion.265
  1070.6 20.0 multiply_reduce_fusion.5
  1090.6 18.9 multiply_convert_fusion
  1109.5 17.3 fusion.267
  1126.9 21.2 multiply_reduce_fusion.7
  1155.3 4.7 convolution_convert_fusion.1
  1173.3 4.2 fusion.62
  1213.8 8.2 convolution_dynamic-update-slice_fusion.4
  1228.0 8.1 collective-permute-start.23
  1245.0 11.4 collective-permute-done.18
  1287.4 8.2 convolution_dynamic-update-slice_fusion.3
  1297.8 42.2 %copy.544 = f32[2048,5248]{1,0:T(8,128)} copy(f32[2048,5248]{0,1:T(8,128)} %convolution_dynamic-update-slice_fusion.9) | data formatting | bytes 85983232
  1341.1 26.7 convolution_dynamic-update-slice_fusion.2
  1367.9 23.7 convolution_dynamic-update-slice_fusion.1
  1391.7 24.2 convolution_dynamic-update-slice_fusion
  1422.9 6.4 fusion.266
  1430.4 6.5 fusion.268
  1444.0 59.9 %all-reduce.8 = (f32[2048]{0:T(1024)}, f32[2048]{0:T(1024)}, f32[2048]{0:T(1024)}, f32[2048]{0:T(1024)}, f32[2048]{0:T(1024)}, /*index=5*/f32[2048]{0:T(1024)}, f32[256]{0:T(256)}, f32[256]{0:T(256)}) all-reduce(f32[2048]{0:T(1024)S(1)} %add.539, f32[2048]{0:T(1024)S(1)} %add.540, ...), channel_id=1, replica_groups=mesh['seq'=8,'dp'=4] {'seq','dp'}, use_global_device_ids=true, to_apply=%region_48.49 | all-reduce | flops 12800 | bytes 102400 | tf_op jit(solution)/shard_map/psum | solution.py:399
  1507.7 294.4 %reduce-scatter.7.cloned.1.call-done = f32[64,5248]{1,0:T(8,128)} async-done(((f32[2048,5248]{1,0:T(8,128)}), f32[64,5248]{1,0:T(8,128)}) %reduce-scatter.7.cloned.1.call-update) | async-done | bytes 1343504
  1807.6 2137.7 %reduce-scatter.5.cloned.1.call-done = f32[64,25088]{1,0:T(8,128)} async-done(((f32[2048,25088]{1,0:T(8,128)}), f32[64,25088]{1,0:T(8,128)}) %reduce-scatter.5.cloned.1.call-update) | async-done | bytes 6422544 | tf_op jit(solution)/shard_map/reduce_scatter | solution.py:403
  3946.8 5.7 fusion.246
  (784 shorter events, 239.7 us)
Async XLA Ops:
  7.3 93.6 %copy-start.158 = (f32[2048]{0:T(1024)S(1)}, f32[2048]{0:T(1024)}, u32[]{:S(2)}) copy-start(f32[2048]{0:T(1024)} %param.40) | copy-start | bytes 24580
  7.3 100.4 %all-gather.12.cloned.1.call-start = ((), (), s32[]{:S(2)}) async-start(), calls=%async_computation.3 | async-start | bytes 2162688 | tf_op jit(solution)/shard_map/all_gather | solution.py:120
  8.0 120.9 %all-gather.10.cloned.1.call-start = ((), (), s32[]{:S(2)}) async-start(), calls=%async_computation.2 | async-start | bytes 2162688 | tf_op jit(solution)/shard_map/all_gather | solution.py:119
  8.8 247.2 %all-gather.14.cloned.1.call-start = ((), (), s32[]{:S(2)}) async-start(), calls=%async_computation.4 | async-start | bytes 8650752 | tf_op jit(solution)/shard_map/all_gather | solution.py:118
  9.5 315.7 %all-gather.16.cloned.1.call-start = ((), (), s32[]{:S(2)}) async-start(), calls=%async_computation.5 | async-start | bytes 8650752 | tf_op jit(solution)/shard_map/all_gather | solution.py:121
  10.1 511.3 %all-gather.18.cloned.1.call-start = ((), (), s32[]{:S(2)}) async-start(), calls=%async_computation.6 | async-start | bytes 34603008 | tf_op jit(solution)/shard_map/all_gather | solution.py:126
  10.7 706.4 %all-gather.20.cloned.1.call-start = ((), (), s32[]{:S(2)}) async-start(), calls=%async_computation.7 | async-start | bytes 34603008 | tf_op jit(solution)/shard_map/all_gather | solution.py:127
  11.2 901.7 %all-gather.22.cloned.1.call-start = ((), (), s32[]{:S(2)}) async-start(), calls=%async_computation.8 | async-start | bytes 34603008 | tf_op jit(solution)/shard_map/all_gather | solution.py:128
  12.0 955.7 %all-gather.24.cloned.1.call-start = ((), (), s32[]{:S(2)}) async-start(), calls=%async_computation.9 | async-start | bytes 1081344 | tf_op jit(solution)/shard_map/all_gather | solution.py:129
  12.7 1010.7 %all-gather.26.cloned.1.call-start = ((), (), s32[]{:S(2)}) async-start(), calls=%async_computation.10 | async-start | bytes 1081344 | tf_op jit(solution)/shard_map/all_gather | solution.py:130
  13.5 1788.6 %reduce-scatter.7.cloned.1.call-start = ((), (), s32[]{:S(2)}) async-start(), calls=%async_computation.12 | async-start | bytes 44335104
  17.2 317.5 %copy-start.67 = (pred[128,896]{0,1:T(8,128)(4,1)}, pred[128,896]{0,1:T(8,128)(4,1)S(1)}, u32[]{:S(2)}) copy-start(pred[128,896]{0,1:T(8,128)(4,1)S(1)} %copy.440) | copy-start | bytes 344068
  17.5 255.5 %copy-start.65 = (pred[128,896]{0,1:T(8,128)(4,1)}, pred[128,896]{0,1:T(8,128)(4,1)S(1)}, u32[]{:S(2)}) copy-start(pred[128,896]{0,1:T(8,128)(4,1)S(1)} %copy.452) | copy-start | bytes 344068
  101.8 154.2 %copy-start.4 = (bf16[128,2048]{1,0:T(8,128)(2,1)}, bf16[128,2048]{1,0:T(8,128)(2,1)S(1)}, u32[]{:S(2)}) copy-start(bf16[128,2048]{1,0:T(8,128)(2,1)S(1)} %get-tuple-element.277) | copy-start | bytes 1572868
  101.8 160.3 %copy-start.6 = (bf16[128,2048]{1,0:T(8,128)(2,1)}, bf16[128,2048]{1,0:T(8,128)(2,1)S(1)}, u32[]{:S(2)}) copy-start(bf16[128,2048]{1,0:T(8,128)(2,1)S(1)} %get-tuple-element.278) | copy-start | bytes 1572868
  107.7 163.0 %copy-start.104 = (f32[128,128]{1,0:T(8,128)}, f32[128,128]{1,0:T(8,128)S(1)}, u32[]{:S(2)}) copy-start(f32[128,128]{1,0:T(8,128)S(1)} %get-tuple-element.349) | copy-start | bytes 196612
  107.7 163.0 %copy-start.106 = (f32[128,128]{1,0:T(8,128)}, f32[128,128]{1,0:T(8,128)S(1)}, u32[]{:S(2)}) copy-start(f32[128,128]{1,0:T(8,128)S(1)} %get-tuple-element.350) | copy-start | bytes 196612
  141.2 54.9 %collective-permute-start.8 = (bf16[2,1,128,2,256]{4,2,3,1,0:T(8,128)(2,1)}, bf16[2,1,128,2,256]{4,2,3,1,0:T(8,128)(2,1)}, u32[]{:S(2)}, u32[]{:S(2)}) collective-permute-start(bf16[2,1,128,2,256]{4,2,3,1,0:T(8,128)(2,1)} %pad_maximum_fusion.15), channel_id=1, source_target_pairs={{0,8},{4,12},{8,16},{12,20},{16,24},{20,28},{1,9},{5,13},{9,17},{1... | collective-permute-start | bytes 786440 | tf_op jit(solution)/shard_map/ppermute | solution.py:19
  144.4 30.8 collective-permute-start.7
  147.9 22.3 collective-permute-start.6
  152.6 102.6 %collective-permute-start.5 = (bf16[2,1,128,2,256]{4,2,3,1,0:T(8,128)(2,1)}, bf16[2,1,128,2,256]{4,2,3,1,0:T(8,128)(2,1)S(1)}, u32[]{:S(2)}, u32[]{:S(2)}) collective-permute-start(bf16[2,1,128,2,256]{4,2,3,1,0:T(8,128)(2,1)} %pad_maximum_fusion.14), channel_id=1, source_target_pairs={{8,0},{12,4},{16,8},{20,12},{24,16},{28,20},{9,1},{13,5},{17,9},{2... | collective-permute-start | bytes 786440 | tf_op jit(solution)/shard_map/ppermute | solution.py:19
  154.1 100.4 %collective-permute-start.4 = (bf16[2,1,128,2,256]{4,2,3,1,0:T(8,128)(2,1)}, bf16[2,1,128,2,256]{4,2,3,1,0:T(8,128)(2,1)S(1)}, u32[]{:S(2)}, u32[]{:S(2)}) collective-permute-start(bf16[2,1,128,2,256]{4,2,3,1,0:T(8,128)(2,1)} %pad_maximum_fusion.14), channel_id=1, source_target_pairs={{4,0},{8,4},{12,8},{16,12},{20,16},{24,20},{28,24},{5,1},{9,5},{13... | collective-permute-start | bytes 786440 | tf_op jit(solution)/shard_map/ppermute | solution.py:19
  155.4 78.5 %copy-start.141 = (bf16[1,1,128,2,128]{4,2,3,1,0:T(8,128)(2,1)S(1)}, bf16[1,1,128,2,128]{4,2,3,1,0:T(8,128)(2,1)}, u32[]{:S(2)}) copy-start(bf16[1,1,128,2,128]{4,2,3,1,0:T(8,128)(2,1)} %copy-done.140) | copy-start | bytes 196612
  170.9 31.4 collective-permute-start.9
  175.2 55.7 %collective-permute-start.2 = (bf16[2,1,128,2,256]{4,2,3,1,0:T(8,128)(2,1)}, bf16[2,1,128,2,256]{4,2,3,1,0:T(8,128)(2,1)S(1)}, u32[]{:S(2)}, u32[]{:S(2)}) collective-permute-start(bf16[2,1,128,2,256]{4,2,3,1,0:T(8,128)(2,1)} %pad_maximum_fusion.14), channel_id=1, source_target_pairs={{0,8},{4,12},{8,16},{12,20},{16,24},{20,28},{1,9},{5,13},{9,17},{1... | collective-permute-start | bytes 786440 | tf_op jit(solution)/shard_map/ppermute | solution.py:19
  196.1 22.3 collective-permute-start
  202.3 26.6 collective-permute-start.1
  218.4 14.7 collective-permute-start.3
  228.9 25.6 collective-permute-start.11
  230.9 15.4 collective-permute-start.10
  344.8 194.4 %copy-start.237 = (f32[128]{0:T(128)}, f32[128]{0:T(128)S(1)}, u32[]{:S(2)}) copy-start(f32[128]{0:T(128)S(1)} %get-tuple-element.267) | copy-start | bytes 1540
  345.9 193.3 %copy-start.225 = (f32[128]{0:T(128)}, f32[128]{0:T(128)S(1)}, u32[]{:S(2)}) copy-start(f32[128]{0:T(128)S(1)} %get-tuple-element.346) | copy-start | bytes 1540
  347.4 369.7 %copy-start.45 = (bf16[128,2048]{1,0:T(8,128)(2,1)}, bf16[128,2048]{1,0:T(8,128)(2,1)S(1)}, u32[]{:S(2)}) copy-start(bf16[128,2048]{1,0:T(8,128)(2,1)S(1)} %get-tuple-element.316) | copy-start | bytes 1572868
  347.4 388.1 %copy-start.43 = (bf16[128,2048]{1,0:T(8,128)(2,1)}, bf16[128,2048]{1,0:T(8,128)(2,1)S(1)}, u32[]{:S(2)}) copy-start(bf16[128,2048]{1,0:T(8,128)(2,1)S(1)} %get-tuple-element.315) | copy-start | bytes 1572868
  1182.9 112.7 %copy-start.173 = (bf16[128,64]{0,1:T(8,128)(2,1)}, bf16[128,64]{0,1:T(8,128)(2,1)S(1)}, u32[]{:S(2)}) copy-start(bf16[128,64]{0,1:T(8,128)(2,1)S(1)} %convolution_convert_fusion.2) | copy-start | bytes 49156
  1189.8 34.4 collective-permute-start.12
  1191.2 35.3 collective-permute-start.17
  1194.5 33.5 collective-permute-start.16
  1198.6 37.6 collective-permute-start.15
  1199.8 40.1 %collective-permute-start.14 = (bf16[2,1,128,2,256]{4,2,3,1,0:T(8,128)(2,1)}, bf16[2,1,128,2,256]{4,2,3,1,0:T(8,128)(2,1)}, u32[]{:S(2)}, u32[]{:S(2)}) collective-permute-start(bf16[2,1,128,2,256]{4,2,3,1,0:T(8,128)(2,1)} %get-tuple-element.245), channel_id=1, source_target_pairs={{8,0},{12,4},{16,8},{20,12},{24,16},{28,20},{9,1},{13,5},{17,9},{2... | collective-permute-start | bytes 786440 | tf_op jit(solution)/shard_map/ppermute | solution.py:19
  1224.2 17.0 collective-permute-start.13
  1226.6 29.8 collective-permute-start.18
  1228.0 33.6 collective-permute-start.23
  1236.1 25.5 collective-permute-start.22
  1240.0 21.7 collective-permute-start.21
  1241.3 24.3 collective-permute-start.20
  1256.4 9.7 collective-permute-start.19
  1340.0 2605.3 %reduce-scatter.5.cloned.1.call-start = ((), (), s32[]{:S(2)}) async-start(), calls=%async_computation.11 | async-start | bytes 211943424 | tf_op jit(solution)/shard_map/reduce_scatter | solution.py:403
  (233 other events, 2518.3 us)
Sparse Core Ops, SparseCore 0:
  11.0 59.6 all-gather.11
  73.5 55.4 all-gather.9
  131.8 102.6 all-gather.13
  237.2 87.9 all-gather.15
  327.9 193.3 all-gather.17
  524.1 192.9 all-gather.19
  719.9 192.9 all-gather.21
  915.8 51.8 all-gather.23
  970.6 52.7 all-gather.25
  1340.1 461.9 reduce-scatter.6
  1804.5 2140.6 reduce-scatter.4
where the time goes:
time: 3980 us; the launch traced here: 3960 us
  waiting for transfers between devices  3140 us (79%)
  matrix products  414 us (10%)
  blocking collectives  143 us (4%)
  local copies, waits for them, and re-layouts  111 us (3%)
  starting transfers between devices  76.1 us (2%)
  other arithmetic  59.1 us (1%)
    reduce_scatter x1, waiting for transfers between devices, body(): lax.psum_scatter(terms_from(join_pairs(feed_lists)), ('seq', 'dp'), scatt...  2140 us
    unnamed x12, waiting for transfers between devices  300 us
    all_gather x1, waiting for transfers between devices, one_micro(): lax.all_gather(feed_local[0], ('seq', 'dp'), axis=0, tiled=True)  174 us
    all_gather x1, waiting for transfers between devices, one_micro(): lax.all_gather(feed_local[2], ('seq', 'dp'), axis=0, tiled=True)  161 us
    all_gather x1, waiting for transfers between devices, one_micro(): lax.all_gather(feed_local[1], ('seq', 'dp'), axis=0, tiled=True)  160 us
    dot_general x22, matrix products, product_nt(): lax.dot_general(left, right, (((1,), (1,)), ((), ())), preferred_element_...  145 us
    dot_general x22, matrix products, product(): return jnp.dot(left, right, preferred_element_type=jnp.float32)  140 us
    dot_general x11, matrix products, product_tn(): lax.dot_general(left, right, (((0,), (0,)), ((), ())), preferred_element_...  103 us
  transfers between devices with their start and end apart: 35, of which 17 were waited for; matrix products, arithmetic and copies ran while one was open for 8% of the time, Pallas kernels for 0%

commit v1 on v0

v1 whole, which is shorter than its diff:
```python
import math

import jax
import jax.numpy as jnp
from jax import lax
from jax.sharding import Mesh
from jax.sharding import PartitionSpec as P

WINDOW = 512
SPAN = 256
EPS = 1e-06
HALF_ROOT = 1.0 / math.sqrt(2.0)
F32 = jnp.float32
BF16 = jnp.bfloat16


def rms(values, gain):
    return values * lax.rsqrt(jnp.mean(values * values, axis=-1, keepdims=True) + EPS) * gain


def gelu_tanh(values):
    return jax.nn.gelu(values, approximate=True)


def product(left, right):
    return jnp.dot(left, right, preferred_element_type=F32)


def product_nt(left, right):
    return lax.dot_general(left, right, (((1,), (1,)), ((), ())), preferred_element_type=F32)


def product_tn(left, right):
    return lax.dot_general(left, right, (((0,), (0,)), ((), ())), preferred_element_type=F32)


def rotate(values, places):
    size = values.shape[-1]
    half = size // 2
    freq = 10000.0 ** (-(2.0 * jnp.arange(half, dtype=F32)) / size)
    angle = places.astype(F32)[..., None] * freq
    cosine = jnp.cos(angle)[..., None, :]
    sine = jnp.sin(angle)[..., None, :]
    first = values[..., :half]
    second = values[..., half:]
    return jnp.concatenate(
        [first * cosine - second * sine, second * cosine + first * sine], axis=-1
    )


def middle(inputs, normed, attn_proj, laurel, gain_attn, gain_laurel, gain_before):
    resid = (inputs + rms(attn_proj, gain_attn) + normed + rms(laurel, gain_laurel)) * HALF_ROOT
    return (resid, rms(resid, gain_before))


def gate_act(gate_val, up_val):
    return gelu_tanh(gate_val) * up_val


def after_feed(resid_one, feed_out, gain_after):
    return resid_one + rms(feed_out, gain_after)


def side_act(side_pre, side_in):
    return gelu_tanh(side_pre) * side_in


def finish(resid_two, side_out, gain_layer):
    return resid_two + rms(side_out, gain_layer)


def swap(value, axis):
    return lax.ppermute(value, axis, [(0, 1), (1, 0)])


def split_columns(whole, widths):
    pieces = []
    offset = 0
    for width_one in widths:
        pieces.append(whole[..., offset : offset + width_one])
        offset = offset + width_one
    return pieces


class Plan:
    def __init__(self, seq_bits, dp_bits):
        self.seq = tuple("s%d" % i for i in range(seq_bits))
        self.dp = tuple("d%d" % i for i in range(dp_bits))
        self.every = self.seq + self.dp
        self.l, self.x = self.seq[-2:]
        self.c = self.dp[-1]
        self.team = (self.l, self.x, self.c)
        self.far_seq = self.seq[:-2]
        self.far_dp = self.dp[:-1]
        self.far = self.far_seq + self.far_dp

    def flips(self, value, first_dims):
        for axis, dim in zip(self.far, first_dims):
            value = jnp.where(lax.axis_index(axis) == 1, jnp.flip(value, dim), value)
        return value

    def to_relative(self, value):
        rows, width = value.shape
        n_seq, n_dp = len(self.far_seq), len(self.far_dp)
        parts = value.reshape((rows,) + (2,) * n_seq + (4,) + (2,) * n_dp + (-1,))
        dims = list(range(1, 1 + n_seq)) + list(range(2 + n_seq, 2 + n_seq + n_dp))
        parts = self.flips(parts, dims)
        order = [0] + dims + [1 + n_seq, 2 + n_seq + n_dp]
        return parts.transpose(order).reshape(rows, width)

    def from_relative(self, value):
        rows, width = value.shape
        n_seq, n_dp = len(self.far_seq), len(self.far_dp)
        parts = value.reshape((rows,) + (2,) * (n_seq + n_dp) + (4, -1))
        parts = self.flips(parts, list(range(1, 1 + n_seq + n_dp)))
        order = [0] + list(range(1, 1 + n_seq)) + [1 + n_seq + n_dp]
        order += list(range(1 + n_seq, 1 + n_seq + n_dp)) + [2 + n_seq + n_dp]
        return parts.transpose(order).reshape(rows, width)

    def far_gather(self, block):
        pieces = {(): block}
        for axis in self.far:
            pieces.update({key + (axis,): swap(piece, axis) for key, piece in list(pieces.items())})
        return [pieces[key] for key in self.far_keys()]

    def far_keys(self):
        keys = [()]
        for axis in self.far:
            keys = [key + extra for key in keys for extra in ((), (axis,))]
        return keys

    def far_scatter(self, pieces):
        held = dict(zip(self.far_keys(), pieces))
        for axis in reversed(self.far):
            for key in [key for key in held if axis in key]:
                into = tuple(one for one in key if one != axis)
                moved = swap(held.pop(key), axis).astype(F32)
                held[into] = (held[into].astype(F32) + moved).astype(BF16)
        return held[()]

    def team_gather(self, own):
        by_x, by_l = swap(own, self.x), swap(own, self.l)
        half = own.shape[0] // 2
        both = jnp.concatenate([swap(by_x[:half], self.l), swap(by_l[half:], self.x)], axis=0)
        return [jnp.concatenate([p, swap(p, self.c)], axis=0) for p in (own, by_x, by_l, both)]

    def team_scatter(self, chunks):
        sums = []
        for chunk in chunks:
            rows = chunk.shape[0] // 2
            other = swap(chunk[rows:].astype(BF16), self.c)
            sums.append(chunk[:rows].astype(F32) + other.astype(F32))
        own, by_x, by_l, both = sums
        half = own.shape[0] // 2
        both = both.astype(BF16)
        first = by_l[:half] + swap(both[:half], self.x).astype(F32)
        second = by_x[half:] + swap(both[half:], self.l).astype(F32)
        by_l = jnp.concatenate([first, by_l[half:]], axis=0).astype(BF16)
        by_x = jnp.concatenate([by_x[:half], second], axis=0).astype(BF16)
        return own + swap(by_l, self.l).astype(F32) + swap(by_x, self.x).astype(F32)


def passed_along(value, axes, count, steps):
    initial, last = (max(0, -steps), min(count, count - steps))
    return lax.ppermute(value, axes, [(source, source + steps) for source in range(initial, last)])


def body(
    plan,
    tokens,
    per_layer,
    positions,
    span_start,
    cotangent,
    query_weight,
    key_weight,
    value_weight,
    output_weight,
    laurel_left,
    laurel_right,
    gate_weight,
    up_weight,
    down_weight,
    side_gate,
    side_output,
    norm_input,
    norm_attn,
    norm_laurel,
    norm_before,
    norm_after,
    norm_layer,
    norm_query,
    norm_key,
):
    batch, block, width = tokens.shape
    rows = batch * block
    head_size = norm_query.shape[0]
    heads = query_weight.shape[1] // head_size
    kv_heads = key_weight.shape[1] // head_size
    group = heads // kv_heads
    seq_count = 2 ** len(plan.seq)
    local_rows = gate_weight.shape[0]
    team_size = 2 ** len(plan.team)
    hidden_own = gate_weight.shape[1] // team_size

    one_widths = [query_weight.shape[1], key_weight.shape[1], value_weight.shape[1], laurel_left.shape[1]]
    two_widths = [output_weight.shape[1], laurel_right.shape[1], side_gate.shape[1], side_output.shape[1]]
    one_local = jnp.concatenate([query_weight, key_weight, value_weight, laurel_left], axis=1)
    two_local = jnp.concatenate([output_weight, laurel_right, side_gate, side_output], axis=1)
    one_full = lax.all_gather(one_local, plan.every, axis=0, tiled=True)
    two_full = lax.all_gather(two_local, plan.every, axis=0, tiled=True)
    output_full, right_full, side_gate_full, side_output_full = split_columns(two_full, two_widths)

    feed_local = jnp.stack([gate_weight, up_weight, down_weight], axis=1)
    feed_local = feed_local.reshape(local_rows, 3, team_size, hidden_own).transpose(2, 0, 1, 3)
    feed_local = feed_local.reshape(team_size * local_rows, 3 * hidden_own)
    feed_team = lax.all_to_all(feed_local, plan.team, split_axis=0, concat_axis=0, tiled=True)
    gate_up_full = jnp.concatenate(
        [
            jnp.concatenate(plan.far_gather(feed_team[:, :hidden_own]), axis=0),
            jnp.concatenate(plan.far_gather(feed_team[:, hidden_own : 2 * hidden_own]), axis=0),
        ],
        axis=1,
    )
    down_full = jnp.concatenate(plan.far_gather(feed_team[:, 2 * hidden_own :]), axis=0)

    inputs = tokens.astype(F32).reshape(rows, width)
    side_in = per_layer.astype(F32).reshape(rows, -1)
    upstream = cotangent.astype(F32).reshape(rows, width)
    normed, pre_pull = jax.vjp(rms, inputs, norm_input)
    normed_low = normed.astype(BF16)
    one_out = product(normed_low, one_full)
    queries, keys, values, latent = split_columns(one_out, one_widths)
    queries = queries.reshape(batch, block, heads, head_size)
    keys = keys.reshape(batch, block, kv_heads, head_size)
    values = values.reshape(batch, block, kv_heads, head_size)
    latent_low = latent.astype(BF16)

    def head_prep(query_in, key_in, value_in, gain_query, gain_key):
        return (
            rotate(rms(query_in, gain_query), positions),
            rotate(rms(key_in, gain_key), positions),
            rms(value_in, 1.0),
        )

    (rot_query, rot_key, rot_value), prep_pull = jax.vjp(
        head_prep, queries, keys, values, norm_query, norm_key
    )
    query_low = rot_query.astype(BF16)
    pair_low = jnp.stack([rot_key.astype(BF16), rot_value.astype(BF16)])
    left_count = WINDOW // block
    right_count = (SPAN + block - 2) // block
    offsets = list(range(left_count, 0, -1)) + [0] + list(range(-1, -right_count - 1, -1))
    gathered = []
    for offset in offsets:
        if offset == 0:
            gathered.append(pair_low)
        else:
            gathered.append(passed_along(pair_low, plan.seq, seq_count, offset))
    pairs_all = jnp.concatenate(gathered, axis=2)
    keys_all = pairs_all[0]
    values_all = pairs_all[1]
    key_count = keys_all.shape[1]
    seq_index = lax.axis_index(plan.seq)
    total_length = block * seq_count
    query_places = seq_index * block + jnp.arange(block, dtype=jnp.int32)
    key_places = (seq_index - left_count) * block + jnp.arange(key_count, dtype=jnp.int32)
    in_query = (query_places[None, :, None] >= span_start[:, None, :]) & (
        query_places[None, :, None] < span_start[:, None, :] + SPAN
    )
    in_key = (key_places[None, :, None] >= span_start[:, None, :]) & (
        key_places[None, :, None] < span_start[:, None, :] + SPAN
    )
    same = jnp.any(in_query[:, :, None, :] & in_key[:, None, :, :], axis=-1)
    near = (key_places[None, :] <= query_places[:, None]) & (
        query_places[:, None] - key_places[None, :] < WINDOW
    )
    valid = (key_places >= 0) & (key_places < total_length)
    allowed = (valid[None, None, :] & (near[None] | same))[:, None, None]
    query_group = query_low.reshape(batch, block, kv_heads, group, head_size)
    scores = jnp.einsum("btkgd,bskd->bkgts", query_group, keys_all, preferred_element_type=F32)
    masked = jnp.where(allowed, scores, -1e30)
    top = jnp.max(masked, axis=-1, keepdims=True)
    expo = jnp.exp(masked - top)
    total = jnp.sum(expo, axis=-1, keepdims=True)
    probs = expo / total
    probs_low = probs.astype(BF16)
    attended = jnp.einsum("bkgts,bskd->btkgd", probs_low, values_all, preferred_element_type=F32)
    attended_low = attended.reshape(rows, heads * head_size).astype(BF16)
    attn_proj = product_nt(attended_low, output_full)
    laurel = product_nt(latent_low, right_full)
    (resid_one, feed_in), mid_pull = jax.vjp(
        middle, inputs, normed, attn_proj, laurel, norm_attn, norm_laurel, norm_before
    )

    feed_chunks = plan.team_gather(plan.to_relative(feed_in.astype(BF16)))
    pulls = []
    hidden_chunks = []
    feed_parts = []
    for chunk in feed_chunks:
        gate_up = product(chunk, gate_up_full)
        hidden, pull = jax.vjp(gate_act, gate_up[:, :hidden_own], gate_up[:, hidden_own:])
        hidden_low = hidden.astype(BF16)
        pulls.append(pull)
        hidden_chunks.append(hidden_low)
        feed_parts.append(product_nt(hidden_low, down_full).astype(BF16))
    feed_out = plan.from_relative(plan.team_scatter(feed_parts))

    resid_two, after_pull = jax.vjp(after_feed, resid_one, feed_out, norm_after)
    resid_low = resid_two.astype(BF16)
    side_pre = product(resid_low, side_gate_full)
    side_val, side_pull = jax.vjp(side_act, side_pre, side_in)
    side_low = side_val.astype(BF16)
    side_out = product_nt(side_low, side_output_full)
    result, final_pull = jax.vjp(finish, resid_two, side_out, norm_layer)
    output = result.astype(BF16).reshape(batch, block, width)

    d_resid_two, d_side_out, grad_norm_layer = final_pull(upstream)
    d_side_out_low = d_side_out.astype(BF16)
    d_side = product(d_side_out_low, side_output_full)
    d_side_pre, d_side_in = side_pull(d_side)
    d_side_pre_low = d_side_pre.astype(BF16)
    d_resid_two = d_resid_two + product_nt(d_side_pre_low, side_gate_full)
    d_resid_one, d_feed_out, grad_norm_after = after_pull(d_resid_two)

    d_out_chunks = plan.team_gather(plan.to_relative(d_feed_out.astype(BF16)))
    d_gate_up_chunks = []
    d_feed_parts = []
    for chunk, pull in zip(d_out_chunks, pulls):
        d_gate, d_up = pull(product(chunk, down_full))
        d_gate_up = jnp.concatenate([d_gate.astype(BF16), d_up.astype(BF16)], axis=1)
        d_gate_up_chunks.append(d_gate_up)
        d_feed_parts.append(product_nt(d_gate_up, gate_up_full).astype(BF16))
    d_feed_in = plan.from_relative(plan.team_scatter(d_feed_parts))

    far_count = 2 ** len(plan.far)
    piece_width = width // far_count
    feed_all = jnp.concatenate(feed_chunks, axis=0)
    hidden_all = jnp.concatenate(hidden_chunks, axis=0)
    d_out_all = jnp.concatenate(d_out_chunks, axis=0)
    d_gate_up_all = jnp.concatenate(d_gate_up_chunks, axis=0)
    down_pieces = []
    gate_up_pieces = []
    for index in range(far_count):
        part = slice(index * piece_width, (index + 1) * piece_width)
        down_pieces.append(product_tn(d_out_all[:, part], hidden_all).astype(BF16))
        gate_up_pieces.append(product_tn(feed_all[:, part], d_gate_up_all).astype(BF16))
    grad_down_team = plan.far_scatter(down_pieces)
    grad_gate_up_team = plan.far_scatter(gate_up_pieces)
    feed_grads = lax.all_to_all(
        jnp.concatenate([grad_gate_up_team, grad_down_team], axis=1),
        plan.team,
        split_axis=0,
        concat_axis=0,
        tiled=True,
    )
    feed_grads = feed_grads.reshape(team_size, local_rows, 3, hidden_own).transpose(2, 1, 0, 3)
    feed_grads = feed_grads.reshape(3, local_rows, team_size * hidden_own).astype(F32)

    (
        d_inputs,
        d_normed,
        d_attn_proj,
        d_laurel,
        grad_norm_attn,
        grad_norm_laurel,
        grad_norm_before,
    ) = mid_pull((d_resid_one, d_feed_in))
    d_attn_low = d_attn_proj.astype(BF16)
    d_laurel_low = d_laurel.astype(BF16)
    d_attended_low = product(d_attn_low, output_full).astype(BF16)
    d_latent_low = product(d_laurel_low, right_full).astype(BF16)
    two_terms = jnp.concatenate(
        [
            product_tn(d_attn_low, attended_low).astype(BF16),
            product_tn(d_laurel_low, latent_low).astype(BF16),
            product_tn(resid_low, d_side_pre_low).astype(BF16),
            product_tn(d_side_out_low, side_low).astype(BF16),
        ],
        axis=1,
    )
    two_sum = lax.psum_scatter(two_terms, plan.every, scatter_dimension=0, tiled=True).astype(F32)

    d_att = d_attended_low.reshape(batch, block, kv_heads, group, head_size)
    d_values_all = jnp.einsum("bkgts,btkgd->bskd", probs_low, d_att, preferred_element_type=F32)
    d_probs = jnp.einsum("btkgd,bskd->bkgts", d_att, values_all, preferred_element_type=F32)
    d_scores = probs * (d_probs - jnp.sum(probs * d_probs, axis=-1, keepdims=True))
    d_scores_low = d_scores.astype(BF16)
    d_query_rot = jnp.einsum("bkgts,bskd->btkgd", d_scores_low, keys_all, preferred_element_type=F32)
    d_keys_all = jnp.einsum(
        "bkgts,btkgd->bskd", d_scores_low, query_group, preferred_element_type=F32
    )
    d_pairs = jnp.stack([d_keys_all, d_values_all])
    d_pair_total = d_pairs[:, :, left_count * block : (left_count + 1) * block]
    for position, offset in enumerate(offsets):
        if offset != 0:
            piece = d_pairs[:, :, position * block : (position + 1) * block].astype(BF16)
            d_pair_total = d_pair_total + passed_along(piece, plan.seq, seq_count, -offset).astype(F32)
    d_queries, d_keys, d_values, grad_norm_query, grad_norm_key = prep_pull(
        (d_query_rot.reshape(batch, block, heads, head_size), d_pair_total[0], d_pair_total[1])
    )
    d_one_low = jnp.concatenate(
        [
            d_queries.reshape(rows, -1).astype(BF16),
            d_keys.reshape(rows, -1).astype(BF16),
            d_values.reshape(rows, -1).astype(BF16),
            d_latent_low,
        ],
        axis=1,
    )
    one_terms = product_tn(normed_low, d_one_low).astype(BF16)
    one_sum = lax.psum_scatter(one_terms, plan.every, scatter_dimension=0, tiled=True).astype(F32)
    d_normed = d_normed + product_nt(d_one_low, one_full)
    d_inputs_norm, grad_norm_input = pre_pull(d_normed)
    grad_tokens = (d_inputs + d_inputs_norm).reshape(batch, block, width)
    grad_side = d_side_in.reshape(batch, block, -1)
    gains = lax.psum(
        jnp.concatenate(
            [
                grad_norm_input,
                grad_norm_attn,
                grad_norm_laurel,
                grad_norm_before,
                grad_norm_after,
                grad_norm_layer,
                grad_norm_query,
                grad_norm_key,
            ]
        ),
        plan.every,
    )
    gain_parts = split_columns(gains, [width] * 6 + [head_size] * 2)
    one_parts = split_columns(one_sum, one_widths)
    two_parts = split_columns(two_sum, two_widths)
    return (
        output,
        grad_tokens,
        grad_side,
        one_parts[0],
        one_parts[1],
        one_parts[2],
        two_parts[0],
        one_parts[3],
        two_parts[1],
        feed_grads[0],
        feed_grads[1],
        feed_grads[2],
        two_parts[2],
        two_parts[3],
    ) + tuple(gain_parts)


def solution(mesh):
    seq_bits = int(math.log2(mesh.shape["seq"]))
    dp_bits = int(math.log2(mesh.shape["dp"]))
    plan = Plan(seq_bits, dp_bits)
    binary = Mesh(mesh.devices.reshape((2,) * (seq_bits + dp_bits)), plan.every)
    token_spec = P(plan.dp, plan.seq, None)
    weight_spec = P(plan.every, None)

    def step(*arrays):
        return body(plan, *arrays)

    return jax.shard_map(
        step,
        mesh=binary,
        in_specs=(token_spec, token_spec, P(plan.dp, plan.seq), P(plan.dp, None), token_spec)
        + (weight_spec,) * 11
        + (P(),) * 8,
        out_specs=(token_spec,) * 3 + (weight_spec,) * 11 + (P(),) * 8,
        check_vma=False,
    )
```

time: 3980 us -> 1470 us (0.37)
  waiting for transfers between devices: 3140 us -> 576 us
  matrix products: 414 us -> 203 us
  starting transfers between devices: 76.1 us -> 224 us
  local copies, waits for them, and re-layouts: 111 us -> 219 us
  other arithmetic: 59.1 us -> 165 us
  blocking collectives: 143 us -> 59.3 us
    reduce_scatter x1, waiting for transfers between devices: 2140 us -> 0.01 us  [body(): lax.psum_scatter(one_terms, plan.every, scatter_dimension=0, tiled=True)]
    all_gather x9 -> x2, waiting for transfers between devices: 630 us -> 184 us  [the longest x1 102 us: body(): one_full = lax.all_gather(one_local, plan.every, axis=0, tiled=True)]
    unnamed x12 -> x5, waiting for transfers between devices: 300 us -> 0.07 us
    ppermute x24 -> x59, waiting for transfers between devices: 70.4 us -> 342 us  [the longest x47 281 us: swap(): return lax.ppermute(value, axis, [(0, 1), (1, 0)])]
    ppermute x24 -> x59, starting transfers between devices: 75.4 us -> 186 us  [the longest x47 159 us: swap(): return lax.ppermute(value, axis, [(0, 1), (1, 0)])]
    all_gather x2 -> x0, blocking collectives: 83.4 us -> none  [the longest x1 45 us: one_micro(): lax.all_gather(attn_local[4], ('seq', 'dp'), axis=0, tiled=True)]
    dot_general x34 -> x19, matrix products: 167 us -> 84 us  [the longest x13 69.1 us: product(): return jnp.dot(left, right, preferred_element_type=F32)]
    dot_general x22 -> x13, matrix products: 145 us -> 68.5 us  [product_nt(): lax.dot_general(left, right, (((1,), (1,)), ((), ())), preferred_element_...]
  transfers between devices with their start and end apart: 35 -> 65, of which waited for: 17 -> 21; matrix products, arithmetic and copies ran while one was open for 8% -> 28% of each run, Pallas kernels for 0% -> 0%
where the time goes in v1:
time: 1470 us; the launch traced here: 1460 us
  waiting for transfers between devices  576 us (39%)
  starting transfers between devices  224 us (15%)
  local copies, waits for them, and re-layouts  219 us (15%)
  matrix products  203 us (14%)
  other arithmetic  165 us (11%)
  blocking collectives  59.3 us (4%)
  between operations  17.1 us (1%)
    ppermute x47, waiting for transfers between devices, swap(): return lax.ppermute(value, axis, [(0, 1), (1, 0)])  281 us
    ppermute x47, starting transfers between devices, swap(): return lax.ppermute(value, axis, [(0, 1), (1, 0)])  159 us
    all_gather x1, waiting for transfers between devices, body(): one_full = lax.all_gather(one_local, plan.every, axis=0, tiled=True)  102 us
    all_gather x1, waiting for transfers between devices, body(): two_full = lax.all_gather(two_local, plan.every, axis=0, tiled=True)  82.7 us
    unnamed x402, local copies, waits for them, and re-layouts  80.2 us
    dot_general x13, matrix products, product(): return jnp.dot(left, right, preferred_element_type=F32)  69.1 us
    dot_general x13, matrix products, product_nt(): lax.dot_general(left, right, (((1,), (1,)), ((), ())), preferred_element_...  68.5 us
    ppermute x12, waiting for transfers between devices, passed_along(): lax.ppermute(value, axes, [(source, source + steps) for source in range(i...  60.9 us
  transfers between devices with their start and end apart: 65, of which 21 were waited for; matrix products, arithmetic and copies ran while one was open for 28% of the time, Pallas kernels for 0%

profile of v1, /device:TPU:0, one launch (start us, length us, event | category | flops | bytes accessed | tf_op | source)
XLA Modules:
  0.0 1463.4 jit_solution(4956534530272930794)
XLA Ops:
  17.8 8.1 maximum_bitcast_fusion
  25.9 9.6 all_to_all.14
  45.1 49.7 %all-to-all-done = bf16[8,64,3072]{2,1,0:T(8,128)(2,1)} async-done(((bf16[8,64,3072]{2,1,0:T(8,128)(2,1)}), bf16[8,64,3072]{2,1,0:T(8,128)(2,1)}, u32[]{:S(2)}, u32[]{:S(2)}) %all-to-all-start) | async-done | bytes 3145760 | tf_op jit(solution)/shard_map/all_to_all | solution.py:217
  101.3 101.8 %all-gather.3.cloned.1.call-done = bf16[2048,3136]{1,0:T(8,128)(2,1)} async-done(((bf16[64,3136]{1,0:T(8,128)(2,1)}), bf16[2048,3136]{1,0:T(8,128)(2,1)}) %all-gather.3.cloned.1.call-update) | async-done | bytes 12845072 | tf_op jit(solution)/shard_map/all_gather | solution.py:210
  203.1 8.8 fusion.225
  244.2 82.7 %all-gather.5.cloned.1.call-done = bf16[2048,2624]{1,0:T(8,128)(2,1)} async-done(((bf16[64,2624]{1,0:T(8,128)(2,1)}), bf16[2048,2624]{1,0:T(8,128)(2,1)}) %all-gather.5.cloned.1.call-update) | async-done | bytes 10747920 | tf_op jit(solution)/shard_map/all_gather | solution.py:211
  339.0 11.2 collective-permute-done.4
  351.8 17.9 %collective-permute-start.14 = (bf16[512,1024]{1,0:T(8,128)(2,1)}, bf16[512,1024]{1,0:T(8,128)(2,1)}, u32[]{:S(2)}, u32[]{:S(2)}) collective-permute-start(bf16[512,1024]{1,0:T(8,128)(2,1)} %get-tuple-element.240), channel_id=1, source_target_pairs={{0,16},{16,0},{1,17},{17,1},{2,18},{18,2},{3,19},{19,3},{4,20},{20... | collective-permute-start | bytes 3145736 | tf_op jit(solution)/shard_map/ppermute | solution.py:73
  382.5 6.2 multiply_reduce_fusion.14
  396.5 27.5 %collective-permute-done.14 = bf16[512,1024]{1,0:T(8,128)(2,1)} collective-permute-done((bf16[512,1024]{1,0:T(8,128)(2,1)}, bf16[512,1024]{1,0:T(8,128)(2,1)}, u32[]{:S(2)}, u32[]{:S(2)}) %collective-permute-start.14) | collective-permute-done | bytes 1048608 | tf_op jit(solution)/shard_map/ppermute | solution.py:73
  429.5 10.2 maximum_maximum_fusion
  439.7 10.0 collective-permute-done.20
  451.7 12.3 collective-permute-start.22
  519.0 6.3 collective-permute-start.25
  525.7 17.6 %collective-permute-start.29 = (bf16[128,2048]{1,0:T(8,128)(2,1)S(1)}, bf16[128,2048]{1,0:T(8,128)(2,1)S(1)}, u32[]{:S(2)}, u32[]{:S(2)}) collective-permute-start(bf16[128,2048]{1,0:T(8,128)(2,1)S(1)} %get-tuple-element.258), channel_id=1, source_target_pairs={{0,8},{8,0},{1,9},{9,1},{2,10},{10,2},{3,11},{11,3},{4,12},{12,4},... | collective-permute-start | bytes 1572872 | tf_op jit(solution)/shard_map/ppermute | solution.py:73
  543.5 11.7 collective-permute-start.26
  557.3 20.8 %collective-permute-done.26 = bf16[256,2048]{1,0:T(8,128)(2,1)S(1)} collective-permute-done((bf16[256,2048]{1,0:T(8,128)(2,1)S(1)}, bf16[256,2048]{1,0:T(8,128)(2,1)S(1)}, u32[]{:S(2)}, u32[]{:S(2)}) %collective-permute-start.26) | collective-permute-done | bytes 1048608 | tf_op jit(solution)/shard_map/ppermute | solution.py:73
  592.5 11.0 rev.31
  643.6 20.8 %collective-permute-done.36 = bf16[256,2048]{0,1:T(8,128)(2,1)S(1)} collective-permute-done((bf16[256,2048]{0,1:T(8,128)(2,1)S(1)}, bf16[256,2048]{0,1:T(8,128)(2,1)S(1)}, u32[]{:S(2)}, u32[]{:S(2)}) %collective-permute-start.36) | collective-permute-done | bytes 1048608 | tf_op jit(solution)/shard_map/ppermute | solution.py:73
  669.0 7.0 fusion.24
  676.1 7.7 convolution_convert_fusion.13
  689.1 6.5 fusion.31
  695.6 6.3 convolution_convert_fusion.12
  703.9 7.4 fusion.45
  711.3 6.9 fusion.38
  719.2 6.0 convolution_convert_fusion.11
  726.8 6.4 convolution_convert_fusion.10
  739.3 12.0 collective-permute-done.41
  755.8 19.9 %collective-permute-done.42 = bf16[256,2048]{1,0:T(8,128)(2,1)S(1)} collective-permute-done((bf16[256,2048]{1,0:T(8,128)(2,1)S(1)}, bf16[256,2048]{1,0:T(8,128)(2,1)S(1)}, u32[]{:S(2)}, u32[]{:S(2)}) %collective-permute-start.42) | collective-permute-done | bytes 1048608 | tf_op jit(solution)/shard_map/ppermute | solution.py:73
  789.7 11.0 rev.35
  822.8 20.5 %pad_maximum_fusion = bf16[2048,2624]{0,1:T(8,128)(2,1)} fusion(bf16[2048,256]{0,1:T(8,128)(2,1)S(1)} %copy-done.48, bf16[2048,256]{0,1:T(8,128)(2,1)S(1)} %convolution_convert_fusion.15, bf16[2048,64]{0,1:T(8,128)(2,1)S(1)} %convolution_convert_fusion.16, bf16[2048,2048]{0,1:T(8,128)(2,1)S(1)} %convolution_convert_fusion.1), kind=kLoop, calls=%fused_computation.2 | loop fusion | flops 42991616 | bytes 21495808 | tf_op jit(solution)/shard_map/concatenate | solution.py:373
  843.3 14.2 copy.439
  869.8 8.8 fusion.6
  907.5 6.4 collective-permute-done.47
  928.0 31.4 %collective-permute-done.49 = bf16[2,2,128,2,256]{4,2,3,1,0:T(8,128)(2,1)S(1)} collective-permute-done((bf16[2,2,128,2,256]{4,2,3,1,0:T(8,128)(2,1)S(1)}, bf16[2,2,128,2,256]{4,2,3,1,0:T(8,128)(2,1)S(1)}, u32[]{:S(2)}, u32[]{:S(2)}) %collective-permute-start.49) | collective-permute-done | bytes 524320 | tf_op jit(solution)/shard_map/ppermute | solution.py:165
  959.4 6.2 collective-permute-done.48
  973.7 6.9 convolution_convert_fusion
  1001.5 32.7 %maximum_maximum_fusion.1 = bf16[2048,2048]{1,0:T(8,128)(2,1)S(1)} fusion(bf16[512,1024]{1,0:T(8,128)(2,1)S(1)} %copy-done.96, bf16[512,1024]{1,0:T(8,128)(2,1)S(1)} %copy-done.95, bf16[512,1024]{1,0:T(8,128)(2,1)S(1)} %copy-done.90, bf16[512,1024]{1,0:T(8,128)(2,1)S(1)} %copy-done.89, bf16[512,1024]{1,0:T(8,128)(2,1)S(1)} %copy-done.93, ...), kind=kLoop, calls=%fused_computation.7 | loop fusion | flops 67108864 | bytes 16777216 | tf_op jit(solution)/shard_map/concatenate | solution.py:341
  1070.7 52.7 %collective-permute-done.54 = bf16[512,2048]{1,0:T(8,128)(2,1)S(1)} collective-permute-done((bf16[512,2048]{1,0:T(8,128)(2,1)S(1)}, bf16[512,2048]{1,0:T(8,128)(2,1)S(1)}, u32[]{:S(2)}, u32[]{:S(2)}) %collective-permute-start.54) | collective-permute-done | bytes 2097184 | tf_op jit(solution)/shard_map/ppermute | solution.py:73
  1124.3 32.8 %collective-permute-start.55 = (bf16[512,2048]{1,0:T(8,128)(2,1)S(1)}, bf16[512,2048]{1,0:T(8,128)(2,1)S(1)}, u32[]{:S(2)}, u32[]{:S(2)}) collective-permute-start(bf16[512,2048]{1,0:T(8,128)(2,1)S(1)} %add_convert_fusion.1), channel_id=1, source_target_pairs={{0,16},{16,0},{1,17},{17,1},{2,18},{18,2},{3,19},{19,3},{4,20},{20... | collective-permute-start | bytes 6291464 | tf_op jit(solution)/shard_map/ppermute | solution.py:73
  1161.1 7.4 collective-permute-done.57
  1168.9 27.6 %collective-permute-start.58 = (bf16[512,1024]{1,0:T(8,128)(2,1)S(1)}, bf16[512,1024]{1,0:T(8,128)(2,1)S(1)}, u32[]{:S(2)}, u32[]{:S(2)}) collective-permute-start(bf16[512,1024]{1,0:T(8,128)(2,1)S(1)} %add_convert_fusion.4), channel_id=1, source_target_pairs={{0,16},{16,0},{1,17},{17,1},{2,18},{18,2},{3,19},{19,3},{4,20},{20... | collective-permute-start | bytes 3145736 | tf_op jit(solution)/shard_map/ppermute | solution.py:73
  1201.2 99.7 %collective-permute-done.56 = bf16[512,1024]{1,0:T(8,128)(2,1)S(1)} collective-permute-done((bf16[512,1024]{1,0:T(8,128)(2,1)S(1)}, bf16[512,1024]{1,0:T(8,128)(2,1)S(1)}, u32[]{:S(2)}, u32[]{:S(2)}) %collective-permute-start.56) | collective-permute-done | bytes 1048608 | tf_op jit(solution)/shard_map/ppermute | solution.py:73
  1304.6 31.8 %all-to-all-start.1 = ((bf16[8,64,3072]{2,1,0:T(8,128)(2,1)}), bf16[8,64,3072]{2,1,0:T(8,128)(2,1)}, u32[]{:S(2)}, u32[]{:S(2)}) async-start(bf16[8,64,3072]{2,1,0:T(8,128)(2,1)} %bitcast.241), calls=%async_computation.2 | async-start | bytes 6291456 | tf_op jit(solution)/shard_map/all_to_all | solution.py:350
  1336.5 10.5 fusion.118
  1347.2 59.3 %psum.7 = f32[12800]{0:T(1024)S(1)} all-reduce(f32[12800]{0:T(1024)S(1)} %constant_dynamic-update-slice_fusion.26), channel_id=1, replica_groups=mesh['s0'=2,'s1'=2,'s2'=2,'d0'=2,'d1'=2] {'s0','s1','s2','d0','d1'}, use_global_device_ids=true, to_apply=%region_32.33 | all-reduce | flops 12800 | bytes 102400 | tf_op jit(solution)/shard_map/psum | solution.py:417
  1411.2 10.6 reshape.509
  1421.8 14.2 fusion.213
  (724 shorter events, 431.4 us)
Async XLA Ops:
  7.2 195.9 %all-gather.3.cloned.1.call-start = ((), (), s32[]{:S(2)}) async-start(), calls=%async_computation.4 | async-start | bytes 13516800 | tf_op jit(solution)/shard_map/all_gather | solution.py:210
  9.2 317.7 %all-gather.5.cloned.1.call-start = ((), (), s32[]{:S(2)}) async-start(), calls=%async_computation.5 | async-start | bytes 11354112 | tf_op jit(solution)/shard_map/all_gather | solution.py:211
  35.5 59.3 %all-to-all-start = ((bf16[8,64,3072]{2,1,0:T(8,128)(2,1)}), bf16[8,64,3072]{2,1,0:T(8,128)(2,1)}, u32[]{:S(2)}, u32[]{:S(2)}) async-start(bf16[8,64,3072]{2,1,0:T(8,128)(2,1)} %all_to_all.14), calls=%async_computation | async-start | bytes 6291456 | tf_op jit(solution)/shard_map/all_to_all | solution.py:217
  40.9 1406.4 %reduce-scatter.7.cloned.1.call-start = ((), (), s32[]{:S(2)}) async-start(), calls=%async_computation.7 | async-start | bytes 11354112
  98.4 253.4 %collective-permute-start.11 = (bf16[512,1024]{1,0:T(8,128)(2,1)}, bf16[512,1024]{1,0:T(8,128)(2,1)}, u32[]{:S(2)}, u32[]{:S(2)}) collective-permute-start(bf16[512,1024]{1,0:T(8,128)(2,1)} %get-tuple-element.241), channel_id=1, source_target_pairs={{0,16},{16,0},{1,17},{17,1},{2,18},{18,2},{3,19},{19,3},{4,20},{20... | collective-permute-start | bytes 3145736 | tf_op jit(solution)/shard_map/ppermute | solution.py:73
  99.5 270.1 %collective-permute-start.8 = (bf16[512,1024]{1,0:T(8,128)(2,1)}, bf16[512,1024]{1,0:T(8,128)(2,1)}, u32[]{:S(2)}, u32[]{:S(2)}) collective-permute-start(bf16[512,1024]{1,0:T(8,128)(2,1)} %get-tuple-element.242), channel_id=1, source_target_pairs={{0,16},{16,0},{1,17},{17,1},{2,18},{18,2},{3,19},{19,3},{4,20},{20... | collective-permute-start | bytes 3145736 | tf_op jit(solution)/shard_map/ppermute | solution.py:73
  222.1 110.2 %collective-permute-start.1 = (bf16[2,2,128,2,256]{4,2,3,1,0:T(8,128)(2,1)}, bf16[2,2,128,2,256]{4,2,3,1,0:T(8,128)(2,1)}, u32[]{:S(2)}, u32[]{:S(2)}) collective-permute-start(bf16[2,2,128,2,256]{4,2,3,1,0:T(8,128)(2,1)} %pad_maximum_fusion.15), channel_id=1, source_target_pairs={{0,12},{4,16},{8,20},{12,24},{16,28},{1,13},{5,17},{9,21},{13,25},... | collective-permute-start | bytes 1572872 | tf_op jit(solution)/shard_map/ppermute | solution.py:165
  224.2 105.6 %collective-permute-start = (bf16[2,2,128,2,256]{4,2,3,1,0:T(8,128)(2,1)}, bf16[2,2,128,2,256]{4,2,3,1,0:T(8,128)(2,1)}, u32[]{:S(2)}, u32[]{:S(2)}) collective-permute-start(bf16[2,2,128,2,256]{4,2,3,1,0:T(8,128)(2,1)} %pad_maximum_fusion.15), channel_id=1, source_target_pairs={{0,16},{4,20},{8,24},{12,28},{1,17},{5,21},{9,25},{13,29},{2,18},{... | collective-permute-start | bytes 1572872 | tf_op jit(solution)/shard_map/ppermute | solution.py:165
  240.2 95.6 %collective-permute-start.3 = (bf16[2,2,128,2,256]{4,2,3,1,0:T(8,128)(2,1)}, bf16[2,2,128,2,256]{4,2,3,1,0:T(8,128)(2,1)}, u32[]{:S(2)}, u32[]{:S(2)}) collective-permute-start(bf16[2,2,128,2,256]{4,2,3,1,0:T(8,128)(2,1)} %pad_maximum_fusion.15), channel_id=1, source_target_pairs={{0,4},{4,8},{8,12},{12,16},{16,20},{20,24},{24,28},{1,5},{5,9},{9,... | collective-permute-start | bytes 1572872 | tf_op jit(solution)/shard_map/ppermute | solution.py:165
  332.3 37.9 %collective-permute-start.5 = (bf16[2,2,128,2,256]{4,2,3,1,0:T(8,128)(2,1)}, bf16[2,2,128,2,256]{4,2,3,1,0:T(8,128)(2,1)S(1)}, u32[]{:S(2)}, u32[]{:S(2)}) collective-permute-start(bf16[2,2,128,2,256]{4,2,3,1,0:T(8,128)(2,1)} %pad_maximum_fusion.15), channel_id=1, source_target_pairs={{8,0},{12,4},{16,8},{20,12},{24,16},{28,20},{9,1},{13,5},{17,9},{2... | collective-permute-start | bytes 1572872 | tf_op jit(solution)/shard_map/ppermute | solution.py:165
  335.8 60.1 %collective-permute-start.10 = (bf16[512,1024]{1,0:T(8,128)(2,1)}, bf16[512,1024]{1,0:T(8,128)(2,1)}, u32[]{:S(2)}, u32[]{:S(2)}) collective-permute-start(bf16[512,1024]{1,0:T(8,128)(2,1)} %get-tuple-element.241), channel_id=1, source_target_pairs={{0,2},{2,0},{1,3},{3,1},{4,6},{6,4},{5,7},{7,5},{8,10},{10,8},{9,1... | collective-permute-start | bytes 3145736 | tf_op jit(solution)/shard_map/ppermute | solution.py:73
  350.2 75.3 %collective-permute-start.7 = (bf16[512,1024]{1,0:T(8,128)(2,1)}, bf16[512,1024]{1,0:T(8,128)(2,1)}, u32[]{:S(2)}, u32[]{:S(2)}) collective-permute-start(bf16[512,1024]{1,0:T(8,128)(2,1)} %get-tuple-element.242), channel_id=1, source_target_pairs={{0,2},{2,0},{1,3},{3,1},{4,6},{6,4},{5,7},{7,5},{8,10},{10,8},{9,1... | collective-permute-start | bytes 3145736 | tf_op jit(solution)/shard_map/ppermute | solution.py:73
  351.8 72.3 %collective-permute-start.14 = (bf16[512,1024]{1,0:T(8,128)(2,1)}, bf16[512,1024]{1,0:T(8,128)(2,1)}, u32[]{:S(2)}, u32[]{:S(2)}) collective-permute-start(bf16[512,1024]{1,0:T(8,128)(2,1)} %get-tuple-element.240), channel_id=1, source_target_pairs={{0,16},{16,0},{1,17},{17,1},{2,18},{18,2},{3,19},{19,3},{4,20},{20... | collective-permute-start | bytes 3145736 | tf_op jit(solution)/shard_map/ppermute | solution.py:73
  369.7 55.9 %collective-permute-start.12 = (bf16[512,1024]{1,0:T(8,128)(2,1)}, bf16[512,1024]{1,0:T(8,128)(2,1)}, u32[]{:S(2)}, u32[]{:S(2)}) collective-permute-start(bf16[512,1024]{1,0:T(8,128)(2,1)} %collective-permute-done.11), channel_id=1, source_target_pairs={{0,2},{2,0},{1,3},{3,1},{4,6},{6,4},{5,7},{7,5},{8,10},{10,8},{9,1... | collective-permute-start | bytes 3145736 | tf_op jit(solution)/shard_map/ppermute | solution.py:73
  370.2 59.3 %collective-permute-start.9 = (bf16[512,1024]{1,0:T(8,128)(2,1)}, bf16[512,1024]{1,0:T(8,128)(2,1)}, u32[]{:S(2)}, u32[]{:S(2)}) collective-permute-start(bf16[512,1024]{1,0:T(8,128)(2,1)} %collective-permute-done.8), channel_id=1, source_target_pairs={{0,2},{2,0},{1,3},{3,1},{4,6},{6,4},{5,7},{7,5},{8,10},{10,8},{9,1... | collective-permute-start | bytes 3145736 | tf_op jit(solution)/shard_map/ppermute | solution.py:73
  395.9 74.9 %collective-permute-start.13 = (bf16[512,1024]{1,0:T(8,128)(2,1)}, bf16[512,1024]{1,0:T(8,128)(2,1)S(1)}, u32[]{:S(2)}, u32[]{:S(2)}) collective-permute-start(bf16[512,1024]{1,0:T(8,128)(2,1)} %get-tuple-element.240), channel_id=1, source_target_pairs={{0,2},{2,0},{1,3},{3,1},{4,6},{6,4},{5,7},{7,5},{8,10},{10,8},{9,1... | collective-permute-start | bytes 3145736 | tf_op jit(solution)/shard_map/ppermute | solution.py:73
  424.0 50.0 %collective-permute-start.15 = (bf16[512,1024]{1,0:T(8,128)(2,1)}, bf16[512,1024]{1,0:T(8,128)(2,1)S(1)}, u32[]{:S(2)}, u32[]{:S(2)}) collective-permute-start(bf16[512,1024]{1,0:T(8,128)(2,1)} %collective-permute-done.14), channel_id=1, source_target_pairs={{0,2},{2,0},{1,3},{3,1},{4,6},{6,4},{5,7},{7,5},{8,10},{10,8},{9,1... | collective-permute-start | bytes 3145736 | tf_op jit(solution)/shard_map/ppermute | solution.py:73
  425.5 24.2 %collective-permute-start.20 = (bf16[256,2048]{0,1:T(8,128)(2,1)S(1)}, bf16[256,2048]{0,1:T(8,128)(2,1)S(1)}, u32[]{:S(2)}, u32[]{:S(2)}) collective-permute-start(bf16[256,2048]{0,1:T(8,128)(2,1)S(1)} %bitcast.256), channel_id=1, source_target_pairs={{0,4},{4,0},{1,5},{5,1},{2,6},{6,2},{3,7},{7,3},{8,12},{12,8},{9,1... | collective-permute-start | bytes 3145736 | tf_op jit(solution)/shard_map/ppermute | solution.py:73
  425.5 26.2 %collective-permute-start.17 = (bf16[256,2048]{0,1:T(8,128)(2,1)S(1)}, bf16[256,2048]{0,1:T(8,128)(2,1)S(1)}, u32[]{:S(2)}, u32[]{:S(2)}) collective-permute-start(bf16[256,2048]{0,1:T(8,128)(2,1)S(1)} %bitcast.257), channel_id=1, source_target_pairs={{0,8},{8,0},{1,9},{9,1},{2,10},{10,2},{3,11},{11,3},{4,12},{12,4},... | collective-permute-start | bytes 3145736 | tf_op jit(solution)/shard_map/ppermute | solution.py:73
  429.5 34.5 %collective-permute-start.6 = (bf16[256,2048]{0,1:T(8,128)(2,1)S(1)}, bf16[256,2048]{0,1:T(8,128)(2,1)S(1)}, u32[]{:S(2)}, u32[]{:S(2)}) collective-permute-start(bf16[256,2048]{0,1:T(8,128)(2,1)S(1)} %bitcast.258), channel_id=1, source_target_pairs={{0,1},{1,0},{2,3},{3,2},{4,5},{5,4},{6,7},{7,6},{8,9},{9,8},{10,11... | collective-permute-start | bytes 3145736 | tf_op jit(solution)/shard_map/ppermute | solution.py:73
  449.8 29.2 %collective-permute-start.21 = (bf16[128,2048]{0,1:T(8,128)(2,1)S(1)}, bf16[128,2048]{0,1:T(8,128)(2,1)S(1)}, u32[]{:S(2)}, u32[]{:S(2)}) collective-permute-start(bf16[128,2048]{0,1:T(8,128)(2,1)S(1)} %slice.410), channel_id=1, source_target_pairs={{0,8},{8,0},{1,9},{9,1},{2,10},{10,2},{3,11},{11,3},{4,12},{12,4},... | collective-permute-start | bytes 1572872 | tf_op jit(solution)/shard_map/ppermute | solution.py:73
  451.7 27.3 %collective-permute-start.22 = (bf16[128,2048]{0,1:T(8,128)(2,1)S(1)}, bf16[128,2048]{0,1:T(8,128)(2,1)S(1)}, u32[]{:S(2)}, u32[]{:S(2)}) collective-permute-start(bf16[128,2048]{0,1:T(8,128)(2,1)S(1)} %slice.411), channel_id=1, source_target_pairs={{0,4},{4,0},{1,5},{5,1},{2,6},{6,2},{3,7},{7,3},{8,12},{12,8},{9,1... | collective-permute-start | bytes 1572872 | tf_op jit(solution)/shard_map/ppermute | solution.py:73
  478.4 78.9 %collective-permute-start.16 = (bf16[256,2048]{1,0:T(8,128)(2,1)S(1)}, bf16[256,2048]{1,0:T(8,128)(2,1)S(1)}, u32[]{:S(2)}, u32[]{:S(2)}) collective-permute-start(bf16[256,2048]{1,0:T(8,128)(2,1)S(1)} %slice.404), channel_id=1, source_target_pairs={{0,1},{1,0},{2,3},{3,2},{4,5},{5,4},{6,7},{7,6},{8,9},{9,8},{10,11... | collective-permute-start | bytes 3145736 | tf_op jit(solution)/shard_map/ppermute | solution.py:73
  491.6 26.5 %collective-permute-start.19 = (bf16[256,2048]{1,0:T(8,128)(2,1)S(1)}, bf16[256,2048]{1,0:T(8,128)(2,1)S(1)}, u32[]{:S(2)}, u32[]{:S(2)}) collective-permute-start(bf16[256,2048]{1,0:T(8,128)(2,1)S(1)} %slice.408), channel_id=1, source_target_pairs={{0,1},{1,0},{2,3},{3,2},{4,5},{5,4},{6,7},{7,6},{8,9},{9,8},{10,11... | collective-permute-start | bytes 3145736 | tf_op jit(solution)/shard_map/ppermute | solution.py:73
  519.0 24.3 %collective-permute-start.25 = (bf16[128,2048]{1,0:T(8,128)(2,1)S(1)}, bf16[128,2048]{1,0:T(8,128)(2,1)S(1)}, u32[]{:S(2)}, u32[]{:S(2)}) collective-permute-start(bf16[128,2048]{1,0:T(8,128)(2,1)S(1)} %get-tuple-element.257), channel_id=1, source_target_pairs={{0,4},{4,0},{1,5},{5,1},{2,6},{6,2},{3,7},{7,3},{8,12},{12,8},{9,1... | collective-permute-start | bytes 1572872 | tf_op jit(solution)/shard_map/ppermute | solution.py:73
  525.7 29.6 %collective-permute-start.29 = (bf16[128,2048]{1,0:T(8,128)(2,1)S(1)}, bf16[128,2048]{1,0:T(8,128)(2,1)S(1)}, u32[]{:S(2)}, u32[]{:S(2)}) collective-permute-start(bf16[128,2048]{1,0:T(8,128)(2,1)S(1)} %get-tuple-element.258), channel_id=1, source_target_pairs={{0,8},{8,0},{1,9},{9,1},{2,10},{10,2},{3,11},{11,3},{4,12},{12,4},... | collective-permute-start | bytes 1572872 | tf_op jit(solution)/shard_map/ppermute | solution.py:73
  543.5 34.6 %collective-permute-start.26 = (bf16[256,2048]{1,0:T(8,128)(2,1)S(1)}, bf16[256,2048]{1,0:T(8,128)(2,1)S(1)}, u32[]{:S(2)}, u32[]{:S(2)}) collective-permute-start(bf16[256,2048]{1,0:T(8,128)(2,1)S(1)} %pad_maximum_fusion.8), channel_id=1, source_target_pairs={{0,8},{8,0},{1,9},{9,1},{2,10},{10,2},{3,11},{11,3},{4,12},{12,4},... | collective-permute-start | bytes 3145736 | tf_op jit(solution)/shard_map/ppermute | solution.py:73
  555.5 25.0 %collective-permute-start.30 = (bf16[256,2048]{1,0:T(8,128)(2,1)S(1)}, bf16[256,2048]{1,0:T(8,128)(2,1)S(1)}, u32[]{:S(2)}, u32[]{:S(2)}) collective-permute-start(bf16[256,2048]{1,0:T(8,128)(2,1)S(1)} %pad_maximum_fusion.9), channel_id=1, source_target_pairs={{0,4},{4,0},{1,5},{5,1},{2,6},{6,2},{3,7},{7,3},{8,12},{12,8},{9,1... | collective-permute-start | bytes 3145736 | tf_op jit(solution)/shard_map/ppermute | solution.py:73
  640.2 24.1 %collective-permute-start.36 = (bf16[256,2048]{0,1:T(8,128)(2,1)S(1)}, bf16[256,2048]{0,1:T(8,128)(2,1)S(1)}, u32[]{:S(2)}, u32[]{:S(2)}) collective-permute-start(bf16[256,2048]{0,1:T(8,128)(2,1)S(1)} %bitcast.261), channel_id=1, source_target_pairs={{0,4},{4,0},{1,5},{5,1},{2,6},{6,2},{3,7},{7,3},{8,12},{12,8},{9,1... | collective-permute-start | bytes 3145736 | tf_op jit(solution)/shard_map/ppermute | solution.py:73
  642.1 24.5 %collective-permute-start.33 = (bf16[256,2048]{0,1:T(8,128)(2,1)S(1)}, bf16[256,2048]{0,1:T(8,128)(2,1)S(1)}, u32[]{:S(2)}, u32[]{:S(2)}) collective-permute-start(bf16[256,2048]{0,1:T(8,128)(2,1)S(1)} %bitcast.262), channel_id=1, source_target_pairs={{0,8},{8,0},{1,9},{9,1},{2,10},{10,2},{3,11},{11,3},{4,12},{12,4},... | collective-permute-start | bytes 3145736 | tf_op jit(solution)/shard_map/ppermute | solution.py:73
  643.6 25.4 %collective-permute-start.31 = (bf16[256,2048]{0,1:T(8,128)(2,1)S(1)}, bf16[256,2048]{0,1:T(8,128)(2,1)S(1)}, u32[]{:S(2)}, u32[]{:S(2)}) collective-permute-start(bf16[256,2048]{0,1:T(8,128)(2,1)S(1)} %bitcast.263), channel_id=1, source_target_pairs={{0,1},{1,0},{2,3},{3,2},{4,5},{5,4},{6,7},{7,6},{8,9},{9,8},{10,11... | collective-permute-start | bytes 3145736 | tf_op jit(solution)/shard_map/ppermute | solution.py:73
  686.2 69.6 %collective-permute-start.32 = (bf16[256,2048]{1,0:T(8,128)(2,1)}, bf16[256,2048]{1,0:T(8,128)(2,1)}, u32[]{:S(2)}, u32[]{:S(2)}) collective-permute-start(bf16[256,2048]{1,0:T(8,128)(2,1)} %slice.428), channel_id=1, source_target_pairs={{0,1},{1,0},{2,3},{3,2},{4,5},{5,4},{6,7},{7,6},{8,9},{9,8},{10,11... | collective-permute-start | bytes 3145736 | tf_op jit(solution)/shard_map/ppermute | solution.py:73
  703.0 30.9 %collective-permute-start.35 = (bf16[256,2048]{1,0:T(8,128)(2,1)}, bf16[256,2048]{1,0:T(8,128)(2,1)}, u32[]{:S(2)}, u32[]{:S(2)}) collective-permute-start(bf16[256,2048]{1,0:T(8,128)(2,1)} %slice.430), channel_id=1, source_target_pairs={{0,1},{1,0},{2,3},{3,2},{4,5},{5,4},{6,7},{7,6},{8,9},{9,8},{10,11... | collective-permute-start | bytes 3145736 | tf_op jit(solution)/shard_map/ppermute | solution.py:73
  751.5 24.3 %collective-permute-start.42 = (bf16[256,2048]{1,0:T(8,128)(2,1)S(1)}, bf16[256,2048]{1,0:T(8,128)(2,1)S(1)}, u32[]{:S(2)}, u32[]{:S(2)}) collective-permute-start(bf16[256,2048]{1,0:T(8,128)(2,1)S(1)} %pad_maximum_fusion.11), channel_id=1, source_target_pairs={{0,8},{8,0},{1,9},{9,1},{2,10},{10,2},{3,11},{11,3},{4,12},{12,4},... | collective-permute-start | bytes 3145736 | tf_op jit(solution)/shard_map/ppermute | solution.py:73
  752.5 24.0 %collective-permute-start.46 = (bf16[256,2048]{1,0:T(8,128)(2,1)S(1)}, bf16[256,2048]{1,0:T(8,128)(2,1)S(1)}, u32[]{:S(2)}, u32[]{:S(2)}) collective-permute-start(bf16[256,2048]{1,0:T(8,128)(2,1)S(1)} %pad_maximum_fusion.12), channel_id=1, source_target_pairs={{0,4},{4,0},{1,5},{5,1},{2,6},{6,2},{3,7},{7,3},{8,12},{12,8},{9,1... | collective-permute-start | bytes 3145736 | tf_op jit(solution)/shard_map/ppermute | solution.py:73
  857.5 594.5 %reduce-scatter.5.cloned.1.call-start = ((), (), s32[]{:S(2)}) async-start(), calls=%async_computation.6 | async-start | bytes 13516800 | tf_op jit(solution)/shard_map/reduce_scatter | solution.py:412
  887.0 27.0 %collective-permute-start.47 = (bf16[2,2,128,2,256]{4,2,3,1,0:T(8,128)(2,1)S(1)}, bf16[2,2,128,2,256]{4,2,3,1,0:T(8,128)(2,1)S(1)}, u32[]{:S(2)}, u32[]{:S(2)}) collective-permute-start(bf16[2,2,128,2,256]{4,2,3,1,0:T(8,128)(2,1)S(1)} %get-tuple-element.232), channel_id=1, source_target_pairs={{16,0},{20,4},{24,8},{28,12},{17,1},{21,5},{25,9},{29,13},{18,2},{... | collective-permute-start | bytes 1572872 | tf_op jit(solution)/shard_map/ppermute | solution.py:165
  899.0 23.3 %collective-permute-start.52 = (bf16[2,2,128,2,256]{4,2,3,1,0:T(8,128)(2,1)S(1)}, bf16[2,2,128,2,256]{4,2,3,1,0:T(8,128)(2,1)S(1)}, u32[]{:S(2)}, u32[]{:S(2)}) collective-permute-start(bf16[2,2,128,2,256]{4,2,3,1,0:T(8,128)(2,1)S(1)} %get-tuple-element.233), channel_id=1, source_target_pairs={{0,8},{4,12},{8,16},{12,20},{16,24},{20,28},{1,9},{5,13},{9,17},{1... | collective-permute-start | bytes 1572872 | tf_op jit(solution)/shard_map/ppermute | solution.py:165
  904.9 23.1 %collective-permute-start.50 = (bf16[2,2,128,2,256]{4,2,3,1,0:T(8,128)(2,1)S(1)}, bf16[2,2,128,2,256]{4,2,3,1,0:T(8,128)(2,1)S(1)}, u32[]{:S(2)}, u32[]{:S(2)}) collective-permute-start(bf16[2,2,128,2,256]{4,2,3,1,0:T(8,128)(2,1)S(1)} %get-tuple-element.235), channel_id=1, source_target_pairs={{4,0},{8,4},{12,8},{16,12},{20,16},{24,20},{28,24},{5,1},{9,5},{13... | collective-permute-start | bytes 1572872 | tf_op jit(solution)/shard_map/ppermute | solution.py:165
  906.2 53.2 %collective-permute-start.49 = (bf16[2,2,128,2,256]{4,2,3,1,0:T(8,128)(2,1)S(1)}, bf16[2,2,128,2,256]{4,2,3,1,0:T(8,128)(2,1)S(1)}, u32[]{:S(2)}, u32[]{:S(2)}) collective-permute-start(bf16[2,2,128,2,256]{4,2,3,1,0:T(8,128)(2,1)S(1)} %get-tuple-element.236), channel_id=1, source_target_pairs={{8,0},{12,4},{16,8},{20,12},{24,16},{28,20},{9,1},{13,5},{17,9},{2... | collective-permute-start | bytes 1572872 | tf_op jit(solution)/shard_map/ppermute | solution.py:165
  914.0 51.7 %collective-permute-start.48 = (bf16[2,2,128,2,256]{4,2,3,1,0:T(8,128)(2,1)S(1)}, bf16[2,2,128,2,256]{4,2,3,1,0:T(8,128)(2,1)S(1)}, u32[]{:S(2)}, u32[]{:S(2)}) collective-permute-start(bf16[2,2,128,2,256]{4,2,3,1,0:T(8,128)(2,1)S(1)} %get-tuple-element.237), channel_id=1, source_target_pairs={{12,0},{16,4},{20,8},{24,12},{28,16},{13,1},{17,5},{21,9},{25,13},... | collective-permute-start | bytes 1572872 | tf_op jit(solution)/shard_map/ppermute | solution.py:165
  1039.0 84.4 %collective-permute-start.54 = (bf16[512,2048]{1,0:T(8,128)(2,1)S(1)}, bf16[512,2048]{1,0:T(8,128)(2,1)S(1)}, u32[]{:S(2)}, u32[]{:S(2)}) collective-permute-start(bf16[512,2048]{1,0:T(8,128)(2,1)S(1)} %convolution_convert_fusion.6), channel_id=1, source_target_pairs={{0,2},{2,0},{1,3},{3,1},{4,6},{6,4},{5,7},{7,5},{8,10},{10,8},{9,1... | collective-permute-start | bytes 6291464 | tf_op jit(solution)/shard_map/ppermute | solution.py:73
  1058.8 109.7 %collective-permute-start.57 = (bf16[512,1024]{1,0:T(8,128)(2,1)}, bf16[512,1024]{1,0:T(8,128)(2,1)S(1)}, u32[]{:S(2)}, u32[]{:S(2)}) collective-permute-start(bf16[512,1024]{1,0:T(8,128)(2,1)} %fusion.139), channel_id=1, source_target_pairs={{0,2},{2,0},{1,3},{3,1},{4,6},{6,4},{5,7},{7,5},{8,10},{10,8},{9,1... | collective-permute-start | bytes 3145736 | tf_op jit(solution)/shard_map/ppermute | solution.py:73
  1058.9 242.6 %collective-permute-start.53 = (bf16[512,2048]{1,0:T(8,128)(2,1)}, bf16[512,2048]{1,0:T(8,128)(2,1)S(1)}, u32[]{:S(2)}, u32[]{:S(2)}) collective-permute-start(bf16[512,2048]{1,0:T(8,128)(2,1)} %convolution_convert_fusion.8), channel_id=1, source_target_pairs={{0,2},{2,0},{1,3},{3,1},{4,6},{6,4},{5,7},{7,5},{8,10},{10,8},{9,1... | collective-permute-start | bytes 6291464 | tf_op jit(solution)/shard_map/ppermute | solution.py:73
  1124.3 177.3 %collective-permute-start.55 = (bf16[512,2048]{1,0:T(8,128)(2,1)S(1)}, bf16[512,2048]{1,0:T(8,128)(2,1)S(1)}, u32[]{:S(2)}, u32[]{:S(2)}) collective-permute-start(bf16[512,2048]{1,0:T(8,128)(2,1)S(1)} %add_convert_fusion.1), channel_id=1, source_target_pairs={{0,16},{16,0},{1,17},{17,1},{2,18},{18,2},{3,19},{19,3},{4,20},{20... | collective-permute-start | bytes 6291464 | tf_op jit(solution)/shard_map/ppermute | solution.py:73
  1161.0 139.8 %collective-permute-start.56 = (bf16[512,1024]{1,0:T(8,128)(2,1)S(1)}, bf16[512,1024]{1,0:T(8,128)(2,1)S(1)}, u32[]{:S(2)}, u32[]{:S(2)}) collective-permute-start(bf16[512,1024]{1,0:T(8,128)(2,1)S(1)} %copy-done.173), channel_id=1, source_target_pairs={{0,2},{2,0},{1,3},{3,1},{4,6},{6,4},{5,7},{7,5},{8,10},{10,8},{9,1... | collective-permute-start | bytes 3145736 | tf_op jit(solution)/shard_map/ppermute | solution.py:73
  1168.9 132.0 %collective-permute-start.58 = (bf16[512,1024]{1,0:T(8,128)(2,1)S(1)}, bf16[512,1024]{1,0:T(8,128)(2,1)S(1)}, u32[]{:S(2)}, u32[]{:S(2)}) collective-permute-start(bf16[512,1024]{1,0:T(8,128)(2,1)S(1)} %add_convert_fusion.4), channel_id=1, source_target_pairs={{0,16},{16,0},{1,17},{17,1},{2,18},{18,2},{3,19},{19,3},{4,20},{20... | collective-permute-start | bytes 3145736 | tf_op jit(solution)/shard_map/ppermute | solution.py:73
  1304.6 106.6 %all-to-all-start.1 = ((bf16[8,64,3072]{2,1,0:T(8,128)(2,1)}), bf16[8,64,3072]{2,1,0:T(8,128)(2,1)}, u32[]{:S(2)}, u32[]{:S(2)}) async-start(bf16[8,64,3072]{2,1,0:T(8,128)(2,1)} %bitcast.241), calls=%async_computation.2 | async-start | bytes 6291456 | tf_op jit(solution)/shard_map/all_to_all | solution.py:350
  (197 other events, 3164.3 us)
Sparse Core Ops, SparseCore 0:
  11.4 191.5 all-gather.2
  206.5 120.2 all-gather.4
  857.6 189.6 reduce-scatter.6
  1049.5 264.3 reduce-scatter.4

commit v2 on v1

--- a/solution.py
+++ b/solution.py
@@ -116,6 +116,56 @@
         order = [0] + list(range(1, 1 + n_seq)) + [1 + n_seq + n_dp]
         order += list(range(1 + n_seq, 1 + n_seq + n_dp)) + [2 + n_seq + n_dp]
         return parts.transpose(order).reshape(rows, width)
+
+    def source_in_natural(self, width):
+        return self.to_relative(jnp.arange(width, dtype=jnp.int32)[None])[0]
+
+    def spread_order(self, width):
+        n_seq, n_dp = len(self.far_seq), len(self.far_dp)
+        own = jnp.arange(width, dtype=jnp.int32).reshape((2,) * (n_seq + n_dp + 3) + (-1,))
+        for dim, axis in enumerate(self.team):
+            at = n_seq + n_dp + dim
+            own = jnp.where(lax.axis_index(axis) == 1, jnp.flip(own, at), own)
+        far_seq = list(range(n_seq))
+        far_dp = list(range(n_seq, n_seq + n_dp))
+        at_l, at_x, at_c = (n_seq + n_dp + dim for dim in range(3))
+        return own.transpose([at_c] + far_dp + [at_x, at_l] + far_seq + [n_seq + n_dp + 3]).reshape(-1)
+
+    def gather(self, block, x_first):
+        canon = self.far_seq + self.far_dp + self.team
+        middle_axes = (self.x,) + self.far_dp if x_first else self.far_dp + (self.x,)
+        held = []
+        for axis in self.far_seq + (self.l,) + middle_axes + (self.c,):
+            other = swap(block, axis)
+            place = sum(canon.index(one) < canon.index(axis) for one in held)
+            held.append(axis)
+            if axis in self.team:
+                second = lax.axis_index(axis) == 1
+                block, other = jnp.where(second, other, block), jnp.where(second, block, other)
+            block = jnp.stack([block, other], axis=place)
+        return block.reshape((-1, block.shape[-1]))
+
+    def spread_sum(self, pairs, y_first):
+        half = pairs[0][0].shape[1] // 2
+        away = jnp.concatenate([product_tn(one[:, half:], two).astype(BF16) for one, two in pairs], axis=1)
+        kept = jnp.concatenate([product_tn(one[:, :half], two).astype(BF16) for one, two in pairs], axis=1)
+        total = (kept.astype(F32) + swap(away, self.c).astype(F32)).astype(BF16)
+        names = list(self.far_dp) + [self.x, self.l] + list(self.far_seq)
+        total = total.reshape((2,) * len(names) + (-1, total.shape[1]))
+        order = list(self.far_dp) + [self.x] if y_first else [self.x] + list(self.far_dp)
+        for axis in order + [self.l] + list(reversed(self.far_seq)):
+            dim = names.index(axis)
+            names.remove(axis)
+            away = swap(lax.index_in_dim(total, 1, dim, False), axis).astype(F32)
+            total = lax.index_in_dim(total, 0, dim, False).astype(F32) + away
+            if names:
+                total = total.astype(BF16)
+        return total
+
+    def total(self, value):
+        for axis in reversed(self.every):
+            value = value + swap(value, axis)
+        return value
 
     def far_gather(self, block):
         pieces = {(): block}
@@ -203,35 +253,42 @@
     team_size = 2 ** len(plan.team)
     hidden_own = gate_weight.shape[1] // team_size
 
-    one_widths = [query_weight.shape[1], key_weight.shape[1], value_weight.shape[1], laurel_left.shape[1]]
-    two_widths = [output_weight.shape[1], laurel_right.shape[1], side_gate.shape[1], side_output.shape[1]]
-    one_local = jnp.concatenate([query_weight, key_weight, value_weight, laurel_left], axis=1)
-    two_local = jnp.concatenate([output_weight, laurel_right, side_gate, side_output], axis=1)
-    one_full = lax.all_gather(one_local, plan.every, axis=0, tiled=True)
-    two_full = lax.all_gather(two_local, plan.every, axis=0, tiled=True)
-    output_full, right_full, side_gate_full, side_output_full = split_columns(two_full, two_widths)
-
-    feed_local = jnp.stack([gate_weight, up_weight, down_weight], axis=1)
-    feed_local = feed_local.reshape(local_rows, 3, team_size, hidden_own).transpose(2, 0, 1, 3)
-    feed_local = feed_local.reshape(team_size * local_rows, 3 * hidden_own)
-    feed_team = lax.all_to_all(feed_local, plan.team, split_axis=0, concat_axis=0, tiled=True)
-    gate_up_full = jnp.concatenate(
+    kvl_widths = [key_weight.shape[1], value_weight.shape[1], laurel_left.shape[1]]
+    rest_widths = [laurel_right.shape[1], side_gate.shape[1], side_output.shape[1]]
+    query_full = plan.gather(query_weight, True)
+    kvl_full = plan.gather(jnp.concatenate([key_weight, value_weight, laurel_left], axis=1), False)
+    output_full = plan.gather(output_weight, False)
+    rest_full = plan.gather(jnp.concatenate([laurel_right, side_gate, side_output], axis=1), True)
+    right_full, side_gate_full, side_output_full = split_columns(rest_full, rest_widths)
+
+    feed_local = jnp.concatenate(
         [
-            jnp.concatenate(plan.far_gather(feed_team[:, :hidden_own]), axis=0),
-            jnp.concatenate(plan.far_gather(feed_team[:, hidden_own : 2 * hidden_own]), axis=0),
+            one.reshape(local_rows, team_size, hidden_own).transpose(1, 0, 2)
+            for one in (gate_weight, up_weight, down_weight)
         ],
         axis=1,
     )
-    down_full = jnp.concatenate(plan.far_gather(feed_team[:, 2 * hidden_own :]), axis=0)
-
-    inputs = tokens.astype(F32).reshape(rows, width)
+    feed_team = lax.all_to_all(feed_local, plan.team, split_axis=0, concat_axis=0, tiled=True)
+    feed_team = [
+        feed_team[:, index * local_rows : (index + 1) * local_rows].reshape(-1, hidden_own)
+        for index in range(3)
+    ]
+    feed_pieces = [plan.far_gather(one) for one in feed_team]
+
+    places = jnp.arange(width, dtype=jnp.int32)
+    natural = plan.source_in_natural(width)
+    to_relative = (places[:, None] == natural[None, :]).astype(BF16)
+    to_spread = (places[:, None] == plan.spread_order(width)[None, :]).astype(BF16)
+    gains = jnp.stack([norm_input, norm_attn, norm_laurel, norm_before, norm_after, norm_layer])
+    norm_input, norm_attn, norm_laurel, norm_before, norm_after, norm_layer = plan.to_relative(gains)
+    inputs = product(tokens.reshape(rows, width), to_relative)
+    upstream = product(cotangent.reshape(rows, width), to_relative)
     side_in = per_layer.astype(F32).reshape(rows, -1)
-    upstream = cotangent.astype(F32).reshape(rows, width)
     normed, pre_pull = jax.vjp(rms, inputs, norm_input)
     normed_low = normed.astype(BF16)
-    one_out = product(normed_low, one_full)
-    queries, keys, values, latent = split_columns(one_out, one_widths)
-    queries = queries.reshape(batch, block, heads, head_size)
+    normed_spread = product(normed_low, to_spread).astype(BF16)
+    queries = product(normed_low, query_full).reshape(batch, block, heads, head_size)
+    keys, values, latent = split_columns(product(normed_low, kvl_full), kvl_widths)
     keys = keys.reshape(batch, block, kv_heads, head_size)
     values = values.reshape(batch, block, kv_heads, head_size)
     latent_low = latent.astype(BF16)
@@ -257,7 +314,10 @@
             gathered.append(pair_low)
         else:
             gathered.append(passed_along(pair_low, plan.seq, seq_count, offset))
-    pairs_all = jnp.concatenate(gathered, axis=2)
+    pairs_all, feed_pieces = lax.optimization_barrier(
+        (jnp.concatenate(gathered, axis=2), feed_pieces)
+    )
+    gate_full, up_full, down_full = [jnp.concatenate(pieces, axis=0) for pieces in feed_pieces]
     keys_all = pairs_all[0]
     values_all = pairs_all[1]
     key_count = keys_all.shape[1]
@@ -293,18 +353,17 @@
         middle, inputs, normed, attn_proj, laurel, norm_attn, norm_laurel, norm_before
     )
 
-    feed_chunks = plan.team_gather(plan.to_relative(feed_in.astype(BF16)))
+    feed_chunks = plan.team_gather(feed_in.astype(BF16))
     pulls = []
     hidden_chunks = []
     feed_parts = []
     for chunk in feed_chunks:
-        gate_up = product(chunk, gate_up_full)
-        hidden, pull = jax.vjp(gate_act, gate_up[:, :hidden_own], gate_up[:, hidden_own:])
+        hidden, pull = jax.vjp(gate_act, product(chunk, gate_full), product(chunk, up_full))
         hidden_low = hidden.astype(BF16)
         pulls.append(pull)
         hidden_chunks.append(hidden_low)
         feed_parts.append(product_nt(hidden_low, down_full).astype(BF16))
-    feed_out = plan.from_relative(plan.team_scatter(feed_parts))
+    feed_out = plan.team_scatter(feed_parts)
 
     resid_two, after_pull = jax.vjp(after_feed, resid_one, feed_out, norm_after)
     resid_low = resid_two.astype(BF16)
@@ -313,7 +372,7 @@
     side_low = side_val.astype(BF16)
     side_out = product_nt(side_low, side_output_full)
     result, final_pull = jax.vjp(finish, resid_two, side_out, norm_layer)
-    output = result.astype(BF16).reshape(batch, block, width)
+    output = product_nt(result.astype(BF16), to_relative).astype(BF16).reshape(batch, block, width)
 
     d_resid_two, d_side_out, grad_norm_layer = final_pull(upstream)
     d_side_out_low = d_side_out.astype(BF16)
@@ -323,39 +382,50 @@
     d_resid_two = d_resid_two + product_nt(d_side_pre_low, side_gate_full)
     d_resid_one, d_feed_out, grad_norm_after = after_pull(d_resid_two)
 
-    d_out_chunks = plan.team_gather(plan.to_relative(d_feed_out.astype(BF16)))
-    d_gate_up_chunks = []
+    d_out_chunks = plan.team_gather(d_feed_out.astype(BF16))
+    d_gate_chunks = []
+    d_up_chunks = []
     d_feed_parts = []
     for chunk, pull in zip(d_out_chunks, pulls):
         d_gate, d_up = pull(product(chunk, down_full))
-        d_gate_up = jnp.concatenate([d_gate.astype(BF16), d_up.astype(BF16)], axis=1)
-        d_gate_up_chunks.append(d_gate_up)
-        d_feed_parts.append(product_nt(d_gate_up, gate_up_full).astype(BF16))
-    d_feed_in = plan.from_relative(plan.team_scatter(d_feed_parts))
+        d_gate_chunks.append(d_gate.astype(BF16))
+        d_up_chunks.append(d_up.astype(BF16))
+        part = product_nt(d_gate_chunks[-1], gate_full) + product_nt(d_up_chunks[-1], up_full)
+        d_feed_parts.append(part.astype(BF16))
+    d_feed_in = plan.team_scatter(d_feed_parts)
 
     far_count = 2 ** len(plan.far)
     piece_width = width // far_count
     feed_all = jnp.concatenate(feed_chunks, axis=0)
-    hidden_all = jnp.concatenate(hidden_chunks, axis=0)
     d_out_all = jnp.concatenate(d_out_chunks, axis=0)
-    d_gate_up_all = jnp.concatenate(d_gate_up_chunks, axis=0)
-    down_pieces = []
-    gate_up_pieces = []
-    for index in range(far_count):
-        part = slice(index * piece_width, (index + 1) * piece_width)
-        down_pieces.append(product_tn(d_out_all[:, part], hidden_all).astype(BF16))
-        gate_up_pieces.append(product_tn(feed_all[:, part], d_gate_up_all).astype(BF16))
-    grad_down_team = plan.far_scatter(down_pieces)
-    grad_gate_up_team = plan.far_scatter(gate_up_pieces)
+    pairs = (
+        (d_out_all, jnp.concatenate(hidden_chunks, axis=0)),
+        (feed_all, jnp.concatenate(d_gate_chunks, axis=0)),
+        (feed_all, jnp.concatenate(d_up_chunks, axis=0)),
+    )
+    grad_pieces = [
+        [
+            product_tn(left[:, index * piece_width : (index + 1) * piece_width], right).astype(BF16)
+            for index in range(far_count)
+        ]
+        for left, right in pairs
+    ]
+    d_feed_in, grad_pieces = lax.optimization_barrier((d_feed_in, grad_pieces))
+    team_grads = [plan.far_scatter(pieces) for pieces in grad_pieces]
     feed_grads = lax.all_to_all(
-        jnp.concatenate([grad_gate_up_team, grad_down_team], axis=1),
+        jnp.concatenate([one.reshape(team_size, local_rows, hidden_own) for one in team_grads], axis=1),
         plan.team,
         split_axis=0,
         concat_axis=0,
         tiled=True,
     )
-    feed_grads = feed_grads.reshape(team_size, local_rows, 3, hidden_own).transpose(2, 1, 0, 3)
-    feed_grads = feed_grads.reshape(3, local_rows, team_size * hidden_own).astype(F32)
+    grad_down, grad_gate, grad_up = [
+        jnp.concatenate(
+            [feed_grads[at, index * local_rows : (index + 1) * local_rows] for at in range(team_size)],
+            axis=1,
+        ).astype(F32)
+        for index in range(3)
+    ]
 
     (
         d_inputs,
@@ -370,16 +440,21 @@
     d_laurel_low = d_laurel.astype(BF16)
     d_attended_low = product(d_attn_low, output_full).astype(BF16)
     d_latent_low = product(d_laurel_low, right_full).astype(BF16)
-    two_terms = jnp.concatenate(
-        [
-            product_tn(d_attn_low, attended_low).astype(BF16),
-            product_tn(d_laurel_low, latent_low).astype(BF16),
-            product_tn(resid_low, d_side_pre_low).astype(BF16),
-            product_tn(d_side_out_low, side_low).astype(BF16),
-        ],
-        axis=1,
-    )
-    two_sum = lax.psum_scatter(two_terms, plan.every, scatter_dimension=0, tiled=True).astype(F32)
+    spread = product(
+        jnp.concatenate([d_attn_low, d_laurel_low, resid_low, d_side_out_low], axis=0), to_spread
+    ).astype(BF16)
+    grad_output = plan.spread_sum([(spread[:rows], attended_low)], False)
+    grad_right, grad_side_gate, grad_side_output = split_columns(
+        plan.spread_sum(
+            [
+                (spread[rows : 2 * rows], latent_low),
+                (spread[2 * rows : 3 * rows], d_side_pre_low),
+                (spread[3 * rows :], side_low),
+            ],
+            True,
+        ),
+        rest_widths,
+    )
 
     d_att = d_attended_low.reshape(batch, block, kv_heads, group, head_size)
     d_values_all = jnp.einsum("bkgts,btkgd->bskd", probs_low, d_att, preferred_element_type=F32)
@@ -399,55 +474,58 @@
     d_queries, d_keys, d_values, grad_norm_query, grad_norm_key = prep_pull(
         (d_query_rot.reshape(batch, block, heads, head_size), d_pair_total[0], d_pair_total[1])
     )
-    d_one_low = jnp.concatenate(
+    d_queries_low = d_queries.reshape(rows, -1).astype(BF16)
+    d_kvl_low = jnp.concatenate(
         [
-            d_queries.reshape(rows, -1).astype(BF16),
             d_keys.reshape(rows, -1).astype(BF16),
             d_values.reshape(rows, -1).astype(BF16),
             d_latent_low,
         ],
         axis=1,
     )
-    one_terms = product_tn(normed_low, d_one_low).astype(BF16)
-    one_sum = lax.psum_scatter(one_terms, plan.every, scatter_dimension=0, tiled=True).astype(F32)
-    d_normed = d_normed + product_nt(d_one_low, one_full)
+    grad_query = plan.spread_sum([(normed_spread, d_queries_low)], True)
+    grad_key, grad_value, grad_left = split_columns(
+        plan.spread_sum([(normed_spread, d_kvl_low)], False), kvl_widths
+    )
+    d_normed = d_normed + product_nt(d_queries_low, query_full) + product_nt(d_kvl_low, kvl_full)
     d_inputs_norm, grad_norm_input = pre_pull(d_normed)
-    grad_tokens = (d_inputs + d_inputs_norm).reshape(batch, block, width)
+    d_tokens = d_inputs + d_inputs_norm
+    high = lax.reduce_precision(d_tokens, 8, 7)
+    halves = jnp.concatenate([high.astype(BF16), (d_tokens - high).astype(BF16)], axis=0)
+    halves = product_nt(halves, to_relative)
+    grad_tokens = (halves[:rows] + halves[rows:]).reshape(batch, block, width)
     grad_side = d_side_in.reshape(batch, block, -1)
-    gains = lax.psum(
-        jnp.concatenate(
-            [
-                grad_norm_input,
-                grad_norm_attn,
-                grad_norm_laurel,
-                grad_norm_before,
-                grad_norm_after,
-                grad_norm_layer,
-                grad_norm_query,
-                grad_norm_key,
-            ]
-        ),
-        plan.every,
-    )
-    gain_parts = split_columns(gains, [width] * 6 + [head_size] * 2)
-    one_parts = split_columns(one_sum, one_widths)
-    two_parts = split_columns(two_sum, two_widths)
+    early = jnp.stack(
+        [grad_norm_attn, grad_norm_laurel, grad_norm_before, grad_norm_after, grad_norm_layer]
+    )
+    early = plan.total(plan.from_relative(early))
+    late = jnp.concatenate([plan.from_relative(grad_norm_input[None])[0], grad_norm_query, grad_norm_key])
+    late = plan.total(late)
+    late_parts = split_columns(late, [width, head_size, head_size])
     return (
         output,
         grad_tokens,
         grad_side,
-        one_parts[0],
-        one_parts[1],
-        one_parts[2],
-        two_parts[0],
-        one_parts[3],
-        two_parts[1],
-        feed_grads[0],
-        feed_grads[1],
-        feed_grads[2],
-        two_parts[2],
-        two_parts[3],
-    ) + tuple(gain_parts)
+        grad_query,
+        grad_key,
+        grad_value,
+        grad_output,
+        grad_left,
+        grad_right,
+        grad_gate,
+        grad_up,
+        grad_down,
+        grad_side_gate,
+        grad_side_output,
+        late_parts[0],
+        early[0],
+        early[1],
+        early[2],
+        early[3],
+        early[4],
+        late_parts[1],
+        late_parts[2],
+    )
 
 
 def solution(mesh):

time: 1470 us -> 1510 us (1.027)
  waiting for transfers between devices: 576 us -> 658 us
  blocking collectives: 59.3 us -> 0 us
  matrix products: 203 us -> 262 us
  local copies, waits for them, and re-layouts: 219 us -> 168 us
  starting transfers between devices: 224 us -> 262 us
    ppermute x47 -> x100, waiting for transfers between devices: 281 us -> 606 us  [swap(): return lax.ppermute(value, axis, [(0, 1), (1, 0)])]
    all_gather x2 -> x0, waiting for transfers between devices: 184 us -> none  [the longest x1 102 us: body(): one_full = lax.all_gather(one_local, plan.every, axis=0, tiled=True)]
    ppermute x47 -> x100, starting transfers between devices: 159 us -> 223 us  [swap(): return lax.ppermute(value, axis, [(0, 1), (1, 0)])]
    concatenate x5 -> x4, other arithmetic: 67.1 us -> 3.3 us  [the longest x1 1.79 us: body(): jnp.concatenate([one.reshape(team_size, local_rows, hidden_own) for one i...]
    another operation x6 -> x40, other arithmetic: 3.18 us -> 64.9 us  [the longest x33 63.5 us: gather(): block = jnp.stack([block, other], axis=place)]
    psum x1 -> x0, blocking collectives: 59.3 us -> none  [body(): lax.psum(jnp.concatenate([grad_norm_input, grad_norm_attn, grad_norm_laur...]
    all_to_all x1, waiting for transfers between devices: 49.7 us -> 0.01 us  [body(): lax.all_to_all(feed_local, plan.team, split_axis=0, concat_axis=0, tiled=...]
    dot_general x13 -> x24, matrix products: 50.4 us -> 85.5 us  [product_tn(): lax.dot_general(left, right, (((0,), (0,)), ((), ())), preferred_element_...]
  transfers between devices with their start and end apart: 65 -> 114, of which waited for: 21 -> 48; matrix products, arithmetic and copies ran while one was open for 28% -> 29% of each run, Pallas kernels for 0% -> 0%
where the time goes in v2:
time: 1510 us
  waiting for transfers between devices  658 us (44%)
  starting transfers between devices  262 us (17%)
  matrix products  262 us (17%)
  local copies, waits for them, and re-layouts  168 us (11%)
  other arithmetic  151 us (10%)
    ppermute x100, waiting for transfers between devices, swap(): return lax.ppermute(value, axis, [(0, 1), (1, 0)])  606 us
    ppermute x100, starting transfers between devices, swap(): return lax.ppermute(value, axis, [(0, 1), (1, 0)])  223 us
    dot_general x22, matrix products, product(): return jnp.dot(left, right, preferred_element_type=F32)  86.1 us
    dot_general x24, matrix products, product_tn(): lax.dot_general(left, right, (((0,), (0,)), ((), ())), preferred_element_...  85.5 us
    unnamed x494, local copies, waits for them, and re-layouts  75.2 us
    another operation x33, other arithmetic, gather(): block = jnp.stack([block, other], axis=place)  63.5 us
    dot_general x20, matrix products, product_nt(): lax.dot_general(left, right, (((1,), (1,)), ((), ())), preferred_element_...  63.3 us
    ppermute x12, waiting for transfers between devices, passed_along(): lax.ppermute(value, axes, [(source, source + steps) for source in range(i...  52.5 us
  transfers between devices with their start and end apart: 114, of which 48 were waited for; matrix products, arithmetic and copies ran while one was open for 29% of the time, Pallas kernels for 0%

profile of v2, /device:TPU:0, one launch (start us, length us, event | category | flops | bytes accessed | tf_op | source)
XLA Modules:
  0.0 1505.8 jit_solution(2336546136562856188)
XLA Ops:
  34.9 42.6 %collective-permute-done.31 = bf16[2,64,576]{2,1,0:T(8,128)(2,1)S(1)} collective-permute-done((bf16[2,64,576]{2,1,0:T(8,128)(2,1)S(1)}, bf16[2,64,576]{2,1,0:T(8,128)(2,1)S(1)}, u32[]{:S(2)}, u32[]{:S(2)}) %collective-permute-start.31) | collective-permute-done | bytes 147488 | tf_op jit(solution)/shard_map/ppermute | solution.py:73
  88.4 17.9 %collective-permute-done.26 = bf16[2,64,2048]{2,1,0:T(8,128)(2,1)S(1)} collective-permute-done((bf16[2,64,2048]{2,1,0:T(8,128)(2,1)S(1)}, bf16[2,64,2048]{2,1,0:T(8,128)(2,1)S(1)}, u32[]{:S(2)}, u32[]{:S(2)}) %collective-permute-start.26) | collective-permute-done | bytes 524320 | tf_op jit(solution)/shard_map/ppermute | solution.py:73
  115.2 18.5 %collective-permute-done.27 = bf16[2,2,64,2048]{3,2,0,1:T(8,128)(2,1)S(1)} collective-permute-done((bf16[2,2,64,2048]{3,2,0,1:T(8,128)(2,1)S(1)}, bf16[2,2,64,2048]{3,2,0,1:T(8,128)(2,1)S(1)}, u32[]{:S(2)}, u32[]{:S(2)}) %collective-permute-start.27) | collective-permute-done | bytes 1048608 | tf_op jit(solution)/shard_map/ppermute | solution.py:73
  148.2 12.6 collective-permute-done.22
  164.2 40.0 %collective-permute-done.28 = bf16[2,2,2,64,2048]{4,3,0,2,1:T(8,128)(2,1)} collective-permute-done((bf16[2,2,2,64,2048]{4,3,0,2,1:T(8,128)(2,1)}, bf16[2,2,2,64,2048]{4,3,0,2,1:T(8,128)(2,1)}, u32[]{:S(2)}, u32[]{:S(2)}) %collective-permute-start.28) | collective-permute-done | bytes 2097184 | tf_op jit(solution)/shard_map/ppermute | solution.py:73
  256.4 10.5 collective-permute-start.15
  267.4 13.1 collective-permute-start.18
  291.2 35.3 %collective-permute-done.5 = bf16[2,2,128,2,256]{4,2,3,1,0:T(8,128)(2,1)S(1)} collective-permute-done((bf16[2,2,128,2,256]{4,2,3,1,0:T(8,128)(2,1)}, bf16[2,2,128,2,256]{4,2,3,1,0:T(8,128)(2,1)S(1)}, u32[]{:S(2)}, u32[]{:S(2)}) %collective-permute-start.5) | collective-permute-done | bytes 524320 | tf_op jit(solution)/shard_map/ppermute | solution.py:215
  327.6 8.6 collective-permute-done.15
  336.7 22.0 %collective-permute-done.18 = bf16[512,1024]{1,0:T(8,128)(2,1)} collective-permute-done((bf16[512,1024]{1,0:T(8,128)(2,1)}, bf16[512,1024]{1,0:T(8,128)(2,1)}, u32[]{:S(2)}, u32[]{:S(2)}) %collective-permute-start.18) | collective-permute-done | bytes 1048608 | tf_op jit(solution)/shard_map/ppermute | solution.py:73
  366.5 13.7 collective-permute-done.12
  400.0 7.6 collective-permute-done.16
  407.5 22.5 %collective-permute-done.19 = bf16[512,1024]{1,0:T(8,128)(2,1)} collective-permute-done((bf16[512,1024]{1,0:T(8,128)(2,1)}, bf16[512,1024]{1,0:T(8,128)(2,1)}, u32[]{:S(2)}, u32[]{:S(2)}) %collective-permute-start.19) | collective-permute-done | bytes 1048608 | tf_op jit(solution)/shard_map/ppermute | solution.py:73
  430.0 19.6 %collective-permute-done.13 = bf16[512,1024]{1,0:T(8,128)(2,1)} collective-permute-done((bf16[512,1024]{1,0:T(8,128)(2,1)}, bf16[512,1024]{1,0:T(8,128)(2,1)}, u32[]{:S(2)}, u32[]{:S(2)}) %collective-permute-start.13) | collective-permute-done | bytes 1048608 | tf_op jit(solution)/shard_map/ppermute | solution.py:73
  462.0 7.6 pad_maximum_fusion.2
  469.6 8.3 copy.281
  483.5 7.6 pad_maximum_fusion.1
  491.1 12.4 copy.277
  525.9 6.2 multiply_reduce_fusion.18
  535.3 7.4 collective-permute-start.40
  542.7 87.7 %collective-permute-start.37 = (bf16[256,2048]{1,0:T(8,128)(2,1)S(1)}, bf16[256,2048]{1,0:T(8,128)(2,1)S(1)}, u32[]{:S(2)}, u32[]{:S(2)}) collective-permute-start(bf16[256,2048]{1,0:T(8,128)(2,1)S(1)} %get-tuple-element.96), channel_id=1, source_target_pairs={{0,8},{8,0},{1,9},{9,1},{2,10},{10,2},{3,11},{11,3},{4,12},{12,4},... | collective-permute-start | bytes 3145736 | tf_op jit(solution)/shard_map/ppermute | solution.py:73
  643.4 9.3 collective-permute-start.41
  707.0 11.7 collective-permute-done.45
  723.4 21.6 %collective-permute-done.46 = bf16[256,2048]{1,0:T(8,128)(2,1)} collective-permute-done((bf16[256,2048]{1,0:T(8,128)(2,1)}, bf16[256,2048]{1,0:T(8,128)(2,1)}, u32[]{:S(2)}, u32[]{:S(2)}) %collective-permute-start.46) | collective-permute-done | bytes 1048608 | tf_op jit(solution)/shard_map/ppermute | solution.py:73
  771.3 7.4 fusion.35
  778.6 8.5 collective-permute-done.56
  909.7 11.6 collective-permute-done.65
  927.4 18.8 %collective-permute-done.66 = bf16[256,2048]{1,0:T(8,128)(2,1)S(1)} collective-permute-done((bf16[256,2048]{1,0:T(8,128)(2,1)S(1)}, bf16[256,2048]{1,0:T(8,128)(2,1)S(1)}, u32[]{:S(2)}, u32[]{:S(2)}) %collective-permute-start.66) | collective-permute-done | bytes 1048608 | tf_op jit(solution)/shard_map/ppermute | solution.py:73
  959.2 9.1 fusion.27
  979.1 6.4 convolution_bitcast_fusion.1
  985.5 7.7 fusion.14
  993.2 6.5 fusion.16
  1045.8 12.0 collective-permute-start.110
  1072.5 6.9 collective-permute-done.69
  1079.4 8.8 collective-permute-done.68
  1101.2 6.6 multiply_reduce_fusion.6
  1109.7 27.4 %collective-permute-done.103 = f32[2560]{0:T(1024)S(1)} collective-permute-done((f32[2560]{0:T(1024)S(1)}, f32[2560]{0:T(1024)S(1)}, u32[]{:S(2)}, u32[]{:S(2)}) %collective-permute-start.103) | collective-permute-done | bytes 10272 | tf_op jit(solution)/shard_map/ppermute | solution.py:73
  1163.2 16.8 %collective-permute-done.97 = bf16[512,1024]{1,0:T(8,128)(2,1)} collective-permute-done((bf16[512,1024]{1,0:T(8,128)(2,1)}, bf16[512,1024]{1,0:T(8,128)(2,1)}, u32[]{:S(2)}, u32[]{:S(2)}) %collective-permute-start.97) | collective-permute-done | bytes 1048608 | tf_op jit(solution)/shard_map/ppermute | solution.py:73
  1183.0 26.3 %collective-permute-done.89 = bf16[2,2,2,64,576]{4,3,2,1,0:T(8,128)(2,1)} collective-permute-done((bf16[2,2,2,64,576]{4,3,2,1,0:T(8,128)(2,1)}, bf16[2,2,2,64,576]{4,3,2,1,0:T(8,128)(2,1)}, u32[]{:S(2)}, u32[]{:S(2)}) %collective-permute-start.89) | collective-permute-done | bytes 589856 | tf_op jit(solution)/shard_map/ppermute | solution.py:73
  1222.2 51.3 %collective-permute-done.95 = bf16[512,1024]{1,0:T(8,128)(2,1)S(1)} collective-permute-done((bf16[512,1024]{1,0:T(8,128)(2,1)}, bf16[512,1024]{1,0:T(8,128)(2,1)S(1)}, u32[]{:S(2)}, u32[]{:S(2)}) %collective-permute-start.95) | collective-permute-done | bytes 1048608 | tf_op jit(solution)/shard_map/ppermute | solution.py:73
  1276.9 19.0 %collective-permute-done.98 = bf16[512,1024]{1,0:T(8,128)(2,1)S(1)} collective-permute-done((bf16[512,1024]{1,0:T(8,128)(2,1)S(1)}, bf16[512,1024]{1,0:T(8,128)(2,1)S(1)}, u32[]{:S(2)}, u32[]{:S(2)}) %collective-permute-start.98) | collective-permute-done | bytes 1048608 | tf_op jit(solution)/shard_map/ppermute | solution.py:73
  1308.5 33.2 %collective-permute-done.101 = bf16[512,1024]{1,0:T(8,128)(2,1)} collective-permute-done((bf16[512,1024]{1,0:T(8,128)(2,1)}, bf16[512,1024]{1,0:T(8,128)(2,1)}, u32[]{:S(2)}, u32[]{:S(2)}) %collective-permute-start.101) | collective-permute-done | bytes 1048608 | tf_op jit(solution)/shard_map/ppermute | solution.py:73
  1375.2 21.2 %collective-permute-done.81 = bf16[2,64,1088]{2,1,0:T(8,128)(2,1)S(1)} collective-permute-done((bf16[2,64,1088]{2,1,0:T(8,128)(2,1)S(1)}, bf16[2,64,1088]{2,1,0:T(8,128)(2,1)S(1)}, u32[]{:S(2)}, u32[]{:S(2)}) %collective-permute-start.81) | collective-permute-done | bytes 278560 | tf_op jit(solution)/shard_map/ppermute | solution.py:73
  1399.7 6.1 collective-permute-done.82
  1405.8 29.2 %collective-permute-done.84 = bf16[2,2,2,64,2048]{4,3,2,1,0:T(8,128)(2,1)S(1)} collective-permute-done((bf16[2,2,2,64,2048]{4,3,2,1,0:T(8,128)(2,1)S(1)}, bf16[2,2,2,64,2048]{4,3,2,1,0:T(8,128)(2,1)S(1)}, u32[]{:S(2)}, u32[]{:S(2)}) %collective-permute-start.84) | collective-permute-done | bytes 2097184 | tf_op jit(solution)/shard_map/ppermute | solution.py:73
  1439.1 21.6 %collective-permute-done.85 = bf16[2,2,64,2048]{3,2,1,0:T(8,128)(2,1)S(1)} collective-permute-done((bf16[2,2,64,2048]{3,2,1,0:T(8,128)(2,1)S(1)}, bf16[2,2,64,2048]{3,2,1,0:T(8,128)(2,1)S(1)}, u32[]{:S(2)}, u32[]{:S(2)}) %collective-permute-start.85) | collective-permute-done | bytes 1048608 | tf_op jit(solution)/shard_map/ppermute | solution.py:73
  1480.7 10.8 collective-permute-done.76
  1494.2 10.4 collective-permute-done.77
  (1010 shorter events, 653.8 us)
Async XLA Ops:
  8.8 71.4 %collective-permute-start.20 = (bf16[64,2048]{1,0:T(8,128)(2,1)}, bf16[64,2048]{1,0:T(8,128)(2,1)}, u32[]{:S(2)}, u32[]{:S(2)}) collective-permute-start(bf16[64,2048]{1,0:T(8,128)(2,1)} %param.29), channel_id=1, source_target_pairs={{0,16},{16,0},{1,17},{17,1},{2,18},{18,2},{3,19},{19,3},{4,20},{20... | collective-permute-start | bytes 786440 | tf_op jit(solution)/shard_map/ppermute | solution.py:73
  11.7 69.5 %collective-permute-start.25 = (bf16[64,2048]{1,0:T(8,128)(2,1)}, bf16[64,2048]{1,0:T(8,128)(2,1)}, u32[]{:S(2)}, u32[]{:S(2)}) collective-permute-start(bf16[64,2048]{1,0:T(8,128)(2,1)} %param.32), channel_id=1, source_target_pairs={{0,16},{16,0},{1,17},{17,1},{2,18},{18,2},{3,19},{19,3},{4,20},{20... | collective-permute-start | bytes 786440 | tf_op jit(solution)/shard_map/ppermute | solution.py:73
  18.8 234.1 %all-to-all-start = ((bf16[8,192,1024]{2,1,0:T(8,128)(2,1)}), bf16[8,192,1024]{2,1,0:T(8,128)(2,1)}, u32[]{:S(2)}, u32[]{:S(2)}) async-start(bf16[8,192,1024]{2,1,0:T(8,128)(2,1)} %copy.269), calls=%async_computation | async-start | bytes 6291456 | tf_op jit(solution)/shard_map/all_to_all | solution.py:271
  31.8 45.7 %collective-permute-start.31 = (bf16[2,64,576]{2,1,0:T(8,128)(2,1)S(1)}, bf16[2,64,576]{2,1,0:T(8,128)(2,1)S(1)}, u32[]{:S(2)}, u32[]{:S(2)}) collective-permute-start(bf16[2,64,576]{2,1,0:T(8,128)(2,1)S(1)} %pad_maximum_fusion.40), channel_id=1, source_target_pairs={{0,8},{8,0},{1,9},{9,1},{2,10},{10,2},{3,11},{11,3},{4,12},{12,4},... | collective-permute-start | bytes 442376 | tf_op jit(solution)/shard_map/ppermute | solution.py:73
  34.7 49.6 %collective-permute-start.1 = (bf16[2,64,1088]{2,1,0:T(8,128)(2,1)S(1)}, bf16[2,64,1088]{2,1,0:T(8,128)(2,1)S(1)}, u32[]{:S(2)}, u32[]{:S(2)}) collective-permute-start(bf16[2,64,1088]{2,1,0:T(8,128)(2,1)S(1)} %pad_maximum_fusion.39), channel_id=1, source_target_pairs={{0,8},{8,0},{1,9},{9,1},{2,10},{10,2},{3,11},{11,3},{4,12},{12,4},... | collective-permute-start | bytes 835592 | tf_op jit(solution)/shard_map/ppermute | solution.py:73
  114.7 46.1 %collective-permute-start.22 = (bf16[2,2,64,2048]{3,2,1,0:T(8,128)(2,1)}, bf16[2,2,64,2048]{3,2,1,0:T(8,128)(2,1)}, u32[]{:S(2)}, u32[]{:S(2)}) collective-permute-start(bf16[2,2,64,2048]{3,2,1,0:T(8,128)(2,1)} %pad_maximum_fusion.21), channel_id=1, source_target_pairs={{0,4},{4,0},{1,5},{5,1},{2,6},{6,2},{3,7},{7,3},{8,12},{12,8},{9,1... | collective-permute-start | bytes 3145736 | tf_op jit(solution)/shard_map/ppermute | solution.py:73
  135.3 68.9 %collective-permute-start.28 = (bf16[2,2,2,64,2048]{4,3,0,2,1:T(8,128)(2,1)}, bf16[2,2,2,64,2048]{4,3,0,2,1:T(8,128)(2,1)}, u32[]{:S(2)}, u32[]{:S(2)}) collective-permute-start(bf16[2,2,2,64,2048]{4,3,0,2,1:T(8,128)(2,1)} %pad_maximum_fusion.14), channel_id=1, source_target_pairs={{0,4},{4,0},{1,5},{5,1},{2,6},{6,2},{3,7},{7,3},{8,12},{12,8},{9,1... | collective-permute-start | bytes 6291464 | tf_op jit(solution)/shard_map/ppermute | solution.py:73
  140.6 67.6 %collective-permute-start.4 = (bf16[2,2,2,2,64,1088]{5,4,0,2,1,3:T(8,128)(2,1)}, bf16[2,2,2,2,64,1088]{5,4,0,2,1,3:T(8,128)(2,1)}, u32[]{:S(2)}, u32[]{:S(2)}) collective-permute-start(bf16[2,2,2,2,64,1088]{5,4,0,2,1,3:T(8,128)(2,1)} %pad_maximum_fusion.12), channel_id=1, source_target_pairs={{0,1},{1,0},{2,3},{3,2},{4,5},{5,4},{6,7},{7,6},{8,9},{9,8},{10,11... | collective-permute-start | bytes 6684680 | tf_op jit(solution)/shard_map/ppermute | solution.py:73
  148.2 90.1 %collective-permute-start.34 = (bf16[2,2,2,2,64,576]{5,4,0,2,3,1:T(8,128)(2,1)}, bf16[2,2,2,2,64,576]{5,4,0,2,3,1:T(8,128)(2,1)}, u32[]{:S(2)}, u32[]{:S(2)}) collective-permute-start(bf16[2,2,2,2,64,576]{5,4,0,2,3,1:T(8,128)(2,1)} %pad_maximum_fusion.18), channel_id=1, source_target_pairs={{0,1},{1,0},{2,3},{3,2},{4,5},{5,4},{6,7},{7,6},{8,9},{9,8},{10,11... | collective-permute-start | bytes 3538952 | tf_op jit(solution)/shard_map/ppermute | solution.py:73
  163.8 79.8 %collective-permute-start.23 = (bf16[2,2,2,64,2048]{4,3,2,1,0:T(8,128)(2,1)}, bf16[2,2,2,64,2048]{4,3,2,1,0:T(8,128)(2,1)}, u32[]{:S(2)}, u32[]{:S(2)}) collective-permute-start(bf16[2,2,2,64,2048]{4,3,2,1,0:T(8,128)(2,1)} %get-tuple-element.165), channel_id=1, source_target_pairs={{0,2},{2,0},{1,3},{3,1},{4,6},{6,4},{5,7},{7,5},{8,10},{10,8},{9,1... | collective-permute-start | bytes 6291464 | tf_op jit(solution)/shard_map/ppermute | solution.py:73
  236.9 219.7 %collective-permute-start.29 = (bf16[2,2,2,2,64,2048]{5,4,0,2,1,3:T(8,128)(2,1)}, bf16[2,2,2,2,64,2048]{5,4,0,2,1,3:T(8,128)(2,1)}, u32[]{:S(2)}, u32[]{:S(2)}) collective-permute-start(bf16[2,2,2,2,64,2048]{5,4,0,2,1,3:T(8,128)(2,1)} %pad_maximum_fusion.5), channel_id=1, source_target_pairs={{0,1},{1,0},{2,3},{3,2},{4,5},{5,4},{6,7},{7,6},{8,9},{9,8},{10,11... | collective-permute-start | bytes 12582920 | tf_op jit(solution)/shard_map/ppermute | solution.py:73
  256.4 79.8 %collective-permute-start.15 = (bf16[512,1024]{1,0:T(8,128)(2,1)}, bf16[512,1024]{1,0:T(8,128)(2,1)}, u32[]{:S(2)}, u32[]{:S(2)}) collective-permute-start(bf16[512,1024]{1,0:T(8,128)(2,1)} %bitcast.29), channel_id=1, source_target_pairs={{0,16},{16,0},{1,17},{17,1},{2,18},{18,2},{3,19},{19,3},{4,20},{20... | collective-permute-start | bytes 3145736 | tf_op jit(solution)/shard_map/ppermute | solution.py:73
  266.9 69.8 %collective-permute-start.14 = (bf16[512,1024]{1,0:T(8,128)(2,1)}, bf16[512,1024]{1,0:T(8,128)(2,1)}, u32[]{:S(2)}, u32[]{:S(2)}) collective-permute-start(bf16[512,1024]{1,0:T(8,128)(2,1)} %bitcast.29), channel_id=1, source_target_pairs={{0,2},{2,0},{1,3},{3,1},{4,6},{6,4},{5,7},{7,5},{8,10},{10,8},{9,1... | collective-permute-start | bytes 3145736 | tf_op jit(solution)/shard_map/ppermute | solution.py:73
  267.4 91.2 %collective-permute-start.18 = (bf16[512,1024]{1,0:T(8,128)(2,1)}, bf16[512,1024]{1,0:T(8,128)(2,1)}, u32[]{:S(2)}, u32[]{:S(2)}) collective-permute-start(bf16[512,1024]{1,0:T(8,128)(2,1)} %bitcast.30), channel_id=1, source_target_pairs={{0,16},{16,0},{1,17},{17,1},{2,18},{18,2},{3,19},{19,3},{4,20},{20... | collective-permute-start | bytes 3145736 | tf_op jit(solution)/shard_map/ppermute | solution.py:73
  284.3 42.2 %collective-permute-start.5 = (bf16[2,2,128,2,256]{4,2,3,1,0:T(8,128)(2,1)}, bf16[2,2,128,2,256]{4,2,3,1,0:T(8,128)(2,1)S(1)}, u32[]{:S(2)}, u32[]{:S(2)}) collective-permute-start(bf16[2,2,128,2,256]{4,2,3,1,0:T(8,128)(2,1)} %pad_maximum_fusion.35), channel_id=1, source_target_pairs={{0,16},{4,20},{8,24},{12,28},{1,17},{5,21},{9,25},{13,29},{2,18},{... | collective-permute-start | bytes 1572872 | tf_op jit(solution)/shard_map/ppermute | solution.py:215
  326.5 151.4 %collective-permute-start.24 = (bf16[2,2,2,2,64,2048]{5,4,3,2,1,0:T(8,128)(2,1)}, bf16[2,2,2,2,64,2048]{5,4,3,2,1,0:T(8,128)(2,1)}, u32[]{:S(2)}, u32[]{:S(2)}) collective-permute-start(bf16[2,2,2,2,64,2048]{5,4,3,2,1,0:T(8,128)(2,1)} %pad_maximum_fusion.4), channel_id=1, source_target_pairs={{0,1},{1,0},{2,3},{3,2},{4,5},{5,4},{6,7},{7,6},{8,9},{9,8},{10,11... | collective-permute-start | bytes 12582920 | tf_op jit(solution)/shard_map/ppermute | solution.py:73
  336.7 43.5 %collective-permute-start.12 = (bf16[512,1024]{1,0:T(8,128)(2,1)}, bf16[512,1024]{1,0:T(8,128)(2,1)}, u32[]{:S(2)}, u32[]{:S(2)}) collective-permute-start(bf16[512,1024]{1,0:T(8,128)(2,1)} %bitcast.28), channel_id=1, source_target_pairs={{0,16},{16,0},{1,17},{17,1},{2,18},{18,2},{3,19},{19,3},{4,20},{20... | collective-permute-start | bytes 3145736 | tf_op jit(solution)/shard_map/ppermute | solution.py:73
  364.9 42.6 %collective-permute-start.16 = (bf16[512,1024]{1,0:T(8,128)(2,1)}, bf16[512,1024]{1,0:T(8,128)(2,1)}, u32[]{:S(2)}, u32[]{:S(2)}) collective-permute-start(bf16[512,1024]{1,0:T(8,128)(2,1)} %collective-permute-done.15), channel_id=1, source_target_pairs={{0,2},{2,0},{1,3},{3,1},{4,6},{6,4},{5,7},{7,5},{8,10},{10,8},{9,1... | collective-permute-start | bytes 3145736 | tf_op jit(solution)/shard_map/ppermute | solution.py:73
  380.2 49.8 %collective-permute-start.19 = (bf16[512,1024]{1,0:T(8,128)(2,1)}, bf16[512,1024]{1,0:T(8,128)(2,1)}, u32[]{:S(2)}, u32[]{:S(2)}) collective-permute-start(bf16[512,1024]{1,0:T(8,128)(2,1)} %collective-permute-done.18), channel_id=1, source_target_pairs={{0,2},{2,0},{1,3},{3,1},{4,6},{6,4},{5,7},{7,5},{8,10},{10,8},{9,1... | collective-permute-start | bytes 3145736 | tf_op jit(solution)/shard_map/ppermute | solution.py:73
  385.1 64.6 %collective-permute-start.13 = (bf16[512,1024]{1,0:T(8,128)(2,1)}, bf16[512,1024]{1,0:T(8,128)(2,1)}, u32[]{:S(2)}, u32[]{:S(2)}) collective-permute-start(bf16[512,1024]{1,0:T(8,128)(2,1)} %collective-permute-done.12), channel_id=1, source_target_pairs={{0,2},{2,0},{1,3},{3,1},{4,6},{6,4},{5,7},{7,5},{8,10},{10,8},{9,1... | collective-permute-start | bytes 3145736 | tf_op jit(solution)/shard_map/ppermute | solution.py:73
  535.3 108.0 %collective-permute-start.40 = (bf16[256,2048]{1,0:T(8,128)(2,1)S(1)}, bf16[256,2048]{1,0:T(8,128)(2,1)S(1)}, u32[]{:S(2)}, u32[]{:S(2)}) collective-permute-start(bf16[256,2048]{1,0:T(8,128)(2,1)S(1)} %get-tuple-element.96), channel_id=1, source_target_pairs={{0,4},{4,0},{1,5},{5,1},{2,6},{6,2},{3,7},{7,3},{8,12},{12,8},{9,1... | collective-permute-start | bytes 3145736 | tf_op jit(solution)/shard_map/ppermute | solution.py:73
  542.7 110.0 %collective-permute-start.37 = (bf16[256,2048]{1,0:T(8,128)(2,1)S(1)}, bf16[256,2048]{1,0:T(8,128)(2,1)S(1)}, u32[]{:S(2)}, u32[]{:S(2)}) collective-permute-start(bf16[256,2048]{1,0:T(8,128)(2,1)S(1)} %get-tuple-element.96), channel_id=1, source_target_pairs={{0,8},{8,0},{1,9},{9,1},{2,10},{10,2},{3,11},{11,3},{4,12},{12,4},... | collective-permute-start | bytes 3145736 | tf_op jit(solution)/shard_map/ppermute | solution.py:73
  664.5 58.9 %collective-permute-start.36 = (bf16[256,2048]{1,0:T(8,128)(2,1)}, bf16[256,2048]{1,0:T(8,128)(2,1)}, u32[]{:S(2)}, u32[]{:S(2)}) collective-permute-start(bf16[256,2048]{1,0:T(8,128)(2,1)} %slice.635), channel_id=1, source_target_pairs={{0,1},{1,0},{2,3},{3,2},{4,5},{5,4},{6,7},{7,6},{8,9},{9,8},{10,11... | collective-permute-start | bytes 3145736 | tf_op jit(solution)/shard_map/ppermute | solution.py:73
  803.2 124.2 %collective-permute-start.52 = (bf16[256,2048]{1,0:T(8,128)(2,1)}, bf16[256,2048]{1,0:T(8,128)(2,1)}, u32[]{:S(2)}, u32[]{:S(2)}) collective-permute-start(bf16[256,2048]{1,0:T(8,128)(2,1)} %slice.653), channel_id=1, source_target_pairs={{0,1},{1,0},{2,3},{3,2},{4,5},{5,4},{6,7},{7,6},{8,9},{9,8},{10,11... | collective-permute-start | bytes 3145736 | tf_op jit(solution)/shard_map/ppermute | solution.py:73
  819.1 86.9 %collective-permute-start.64 = (bf16[256,2048]{1,0:T(8,128)(2,1)S(1)}, bf16[256,2048]{1,0:T(8,128)(2,1)S(1)}, u32[]{:S(2)}, u32[]{:S(2)}) collective-permute-start(bf16[256,2048]{1,0:T(8,128)(2,1)S(1)} %slice.664), channel_id=1, source_target_pairs={{0,1},{1,0},{2,3},{3,2},{4,5},{5,4},{6,7},{7,6},{8,9},{9,8},{10,11... | collective-permute-start | bytes 3145736 | tf_op jit(solution)/shard_map/ppermute | solution.py:73
  831.1 77.6 %collective-permute-start.55 = (bf16[256,2048]{1,0:T(8,128)(2,1)S(1)}, bf16[256,2048]{1,0:T(8,128)(2,1)S(1)}, u32[]{:S(2)}, u32[]{:S(2)}) collective-permute-start(bf16[256,2048]{1,0:T(8,128)(2,1)S(1)} %slice.655), channel_id=1, source_target_pairs={{0,1},{1,0},{2,3},{3,2},{4,5},{5,4},{6,7},{7,6},{8,9},{9,8},{10,11... | collective-permute-start | bytes 3145736 | tf_op jit(solution)/shard_map/ppermute | solution.py:73
  1020.0 46.9 %collective-permute-start.67 = (bf16[2,2,128,2,256]{4,2,3,1,0:T(8,128)(2,1)S(1)}, bf16[2,2,128,2,256]{4,2,3,1,0:T(8,128)(2,1)S(1)}, u32[]{:S(2)}, u32[]{:S(2)}) collective-permute-start(bf16[2,2,128,2,256]{4,2,3,1,0:T(8,128)(2,1)S(1)} %get-tuple-element.121), channel_id=1, source_target_pairs={{16,0},{20,4},{24,8},{28,12},{17,1},{21,5},{25,9},{29,13},{18,2},{... | collective-permute-start | bytes 1572872 | tf_op jit(solution)/shard_map/ppermute | solution.py:215
  1021.3 48.7 %collective-permute-start.72 = (bf16[2,2,128,2,256]{4,2,3,1,0:T(8,128)(2,1)S(1)}, bf16[2,2,128,2,256]{4,2,3,1,0:T(8,128)(2,1)S(1)}, u32[]{:S(2)}, u32[]{:S(2)}) collective-permute-start(bf16[2,2,128,2,256]{4,2,3,1,0:T(8,128)(2,1)S(1)} %get-tuple-element.122), channel_id=1, source_target_pairs={{0,8},{4,12},{8,16},{12,20},{16,24},{20,28},{1,9},{5,13},{9,17},{1... | collective-permute-start | bytes 1572872 | tf_op jit(solution)/shard_map/ppermute | solution.py:215
  1023.8 46.7 %collective-permute-start.71 = (bf16[2,2,128,2,256]{4,2,3,1,0:T(8,128)(2,1)S(1)}, bf16[2,2,128,2,256]{4,2,3,1,0:T(8,128)(2,1)S(1)}, u32[]{:S(2)}, u32[]{:S(2)}) collective-permute-start(bf16[2,2,128,2,256]{4,2,3,1,0:T(8,128)(2,1)S(1)} %get-tuple-element.123), channel_id=1, source_target_pairs={{0,4},{4,8},{8,12},{12,16},{16,20},{20,24},{24,28},{1,5},{5,9},{9,... | collective-permute-start | bytes 1572872 | tf_op jit(solution)/shard_map/ppermute | solution.py:215
  1027.2 44.8 %collective-permute-start.70 = (bf16[2,2,128,2,256]{4,2,3,1,0:T(8,128)(2,1)S(1)}, bf16[2,2,128,2,256]{4,2,3,1,0:T(8,128)(2,1)S(1)}, u32[]{:S(2)}, u32[]{:S(2)}) collective-permute-start(bf16[2,2,128,2,256]{4,2,3,1,0:T(8,128)(2,1)S(1)} %get-tuple-element.124), channel_id=1, source_target_pairs={{4,0},{8,4},{12,8},{16,12},{20,16},{24,20},{28,24},{5,1},{9,5},{13... | collective-permute-start | bytes 1572872 | tf_op jit(solution)/shard_map/ppermute | solution.py:215
  1069.9 142.3 %collective-permute-start.93 = (bf16[512,1024]{1,0:T(8,128)(2,1)}, bf16[512,1024]{1,0:T(8,128)(2,1)}, u32[]{:S(2)}, u32[]{:S(2)}) collective-permute-start(bf16[512,1024]{1,0:T(8,128)(2,1)} %fusion.169), channel_id=1, source_target_pairs={{0,2},{2,0},{1,3},{3,1},{4,6},{6,4},{5,7},{7,5},{8,10},{10,8},{9,1... | collective-permute-start | bytes 3145736 | tf_op jit(solution)/shard_map/ppermute | solution.py:73
  1070.4 89.4 %collective-permute-start.94 = (bf16[512,1024]{1,0:T(8,128)(2,1)}, bf16[512,1024]{1,0:T(8,128)(2,1)}, u32[]{:S(2)}, u32[]{:S(2)}) collective-permute-start(bf16[512,1024]{1,0:T(8,128)(2,1)} %fusion.175), channel_id=1, source_target_pairs={{0,2},{2,0},{1,3},{3,1},{4,6},{6,4},{5,7},{7,5},{8,10},{10,8},{9,1... | collective-permute-start | bytes 3145736 | tf_op jit(solution)/shard_map/ppermute | solution.py:73
  1072.0 204.8 %collective-permute-start.96 = (bf16[512,1024]{1,0:T(8,128)(2,1)}, bf16[512,1024]{1,0:T(8,128)(2,1)}, u32[]{:S(2)}, u32[]{:S(2)}) collective-permute-start(bf16[512,1024]{1,0:T(8,128)(2,1)} %fusion.148), channel_id=1, source_target_pairs={{0,2},{2,0},{1,3},{3,1},{4,6},{6,4},{5,7},{7,5},{8,10},{10,8},{9,1... | collective-permute-start | bytes 3145736 | tf_op jit(solution)/shard_map/ppermute | solution.py:73
  1079.4 75.9 %collective-permute-start.88 = (bf16[1024,576]{0,1:T(8,128)(2,1)}, bf16[1024,576]{0,1:T(8,128)(2,1)}, u32[]{:S(2)}, u32[]{:S(2)}) collective-permute-start(bf16[1024,576]{0,1:T(8,128)(2,1)} %pad_maximum_fusion.20), channel_id=1, source_target_pairs={{0,1},{1,0},{2,3},{3,2},{4,5},{5,4},{6,7},{7,6},{8,9},{9,8},{10,11... | collective-permute-start | bytes 3538952 | tf_op jit(solution)/shard_map/ppermute | solution.py:73
  1155.3 58.4 %collective-permute-start.100 = (bf16[512,1024]{1,0:T(8,128)(2,1)}, bf16[512,1024]{1,0:T(8,128)(2,1)}, u32[]{:S(2)}, u32[]{:S(2)}) collective-permute-start(bf16[512,1024]{1,0:T(8,128)(2,1)} %fusion.163), channel_id=1, source_target_pairs={{0,2},{2,0},{1,3},{3,1},{4,6},{6,4},{5,7},{7,5},{8,10},{10,8},{9,1... | collective-permute-start | bytes 3145736 | tf_op jit(solution)/shard_map/ppermute | solution.py:73
  1159.8 49.5 %collective-permute-start.89 = (bf16[2,2,2,64,576]{4,3,2,1,0:T(8,128)(2,1)}, bf16[2,2,2,64,576]{4,3,2,1,0:T(8,128)(2,1)}, u32[]{:S(2)}, u32[]{:S(2)}) collective-permute-start(bf16[2,2,2,64,576]{4,3,2,1,0:T(8,128)(2,1)} %bitcast.137), channel_id=1, source_target_pairs={{0,2},{2,0},{1,3},{3,1},{4,6},{6,4},{5,7},{7,5},{8,10},{10,8},{9,1... | collective-permute-start | bytes 1769480 | tf_op jit(solution)/shard_map/ppermute | solution.py:73
  1180.0 118.6 %collective-permute-start.78 = (bf16[1024,1088]{0,1:T(8,128)(2,1)}, bf16[1024,1088]{0,1:T(8,128)(2,1)}, u32[]{:S(2)}, u32[]{:S(2)}) collective-permute-start(bf16[1024,1088]{0,1:T(8,128)(2,1)} %convolution_convert_fusion), channel_id=1, source_target_pairs={{0,1},{1,0},{2,3},{3,2},{4,5},{5,4},{6,7},{7,6},{8,9},{9,8},{10,11... | collective-permute-start | bytes 6684680 | tf_op jit(solution)/shard_map/ppermute | solution.py:73
  1209.3 64.1 %collective-permute-start.95 = (bf16[512,1024]{1,0:T(8,128)(2,1)}, bf16[512,1024]{1,0:T(8,128)(2,1)S(1)}, u32[]{:S(2)}, u32[]{:S(2)}) collective-permute-start(bf16[512,1024]{1,0:T(8,128)(2,1)} %add_convert_fusion.15), channel_id=1, source_target_pairs={{0,16},{16,0},{1,17},{17,1},{2,18},{18,2},{3,19},{19,3},{4,20},{20... | collective-permute-start | bytes 3145736 | tf_op jit(solution)/shard_map/ppermute | solution.py:73
  1212.2 83.6 %collective-permute-start.98 = (bf16[512,1024]{1,0:T(8,128)(2,1)S(1)}, bf16[512,1024]{1,0:T(8,128)(2,1)S(1)}, u32[]{:S(2)}, u32[]{:S(2)}) collective-permute-start(bf16[512,1024]{1,0:T(8,128)(2,1)S(1)} %copy-done.84), channel_id=1, source_target_pairs={{0,16},{16,0},{1,17},{17,1},{2,18},{18,2},{3,19},{19,3},{4,20},{20... | collective-permute-start | bytes 3145736 | tf_op jit(solution)/shard_map/ppermute | solution.py:73
  1220.7 136.2 %collective-permute-start.83 = (bf16[1024,2048]{1,0:T(8,128)(2,1)}, bf16[1024,2048]{1,0:T(8,128)(2,1)}, u32[]{:S(2)}, u32[]{:S(2)}) collective-permute-start(bf16[1024,2048]{1,0:T(8,128)(2,1)} %convolution_convert_fusion.2), channel_id=1, source_target_pairs={{0,1},{1,0},{2,3},{3,2},{4,5},{5,4},{6,7},{7,6},{8,9},{9,8},{10,11... | collective-permute-start | bytes 12582920 | tf_op jit(solution)/shard_map/ppermute | solution.py:73
  1273.5 34.4 %collective-permute-start.99 = (bf16[512,1024]{1,0:T(8,128)(2,1)}, bf16[512,1024]{1,0:T(8,128)(2,1)}, u32[]{:S(2)}, u32[]{:S(2)}) collective-permute-start(bf16[512,1024]{1,0:T(8,128)(2,1)} %fusion.151), channel_id=1, source_target_pairs={{0,2},{2,0},{1,3},{3,1},{4,6},{6,4},{5,7},{7,5},{8,10},{10,8},{9,1... | collective-permute-start | bytes 3145736 | tf_op jit(solution)/shard_map/ppermute | solution.py:73
  1276.8 86.2 %collective-permute-start.73 = (bf16[1024,2048]{1,0:T(8,128)(2,1)}, bf16[1024,2048]{1,0:T(8,128)(2,1)}, u32[]{:S(2)}, u32[]{:S(2)}) collective-permute-start(bf16[1024,2048]{1,0:T(8,128)(2,1)} %convolution_convert_fusion.3), channel_id=1, source_target_pairs={{0,1},{1,0},{2,3},{3,2},{4,5},{5,4},{6,7},{7,6},{8,9},{9,8},{10,11... | collective-permute-start | bytes 12582920 | tf_op jit(solution)/shard_map/ppermute | solution.py:73
  1295.8 45.9 %collective-permute-start.101 = (bf16[512,1024]{1,0:T(8,128)(2,1)}, bf16[512,1024]{1,0:T(8,128)(2,1)}, u32[]{:S(2)}, u32[]{:S(2)}) collective-permute-start(bf16[512,1024]{1,0:T(8,128)(2,1)} %add_convert_fusion.9), channel_id=1, source_target_pairs={{0,16},{16,0},{1,17},{17,1},{2,18},{18,2},{3,19},{19,3},{4,20},{20... | collective-permute-start | bytes 3145736 | tf_op jit(solution)/shard_map/ppermute | solution.py:73
  1298.7 45.2 %collective-permute-start.91 = (bf16[2,64,576]{2,1,0:T(8,128)(2,1)}, bf16[2,64,576]{2,1,0:T(8,128)(2,1)}, u32[]{:S(2)}, u32[]{:S(2)}) collective-permute-start(bf16[2,64,576]{2,1,0:T(8,128)(2,1)} %slice_bitcast_fusion.23), channel_id=1, source_target_pairs={{0,8},{8,0},{1,9},{9,1},{2,10},{10,2},{3,11},{11,3},{4,12},{12,4},... | collective-permute-start | bytes 442376 | tf_op jit(solution)/shard_map/ppermute | solution.py:73
  1307.9 46.8 %collective-permute-start.79 = (bf16[2,2,2,64,1088]{4,3,2,1,0:T(8,128)(2,1)}, bf16[2,2,2,64,1088]{4,3,2,1,0:T(8,128)(2,1)}, u32[]{:S(2)}, u32[]{:S(2)}) collective-permute-start(bf16[2,2,2,64,1088]{4,3,2,1,0:T(8,128)(2,1)} %slice_bitcast_fusion.2), channel_id=1, source_target_pairs={{0,4},{4,0},{1,5},{5,1},{2,6},{6,2},{3,7},{7,3},{8,12},{12,8},{9,1... | collective-permute-start | bytes 3342344 | tf_op jit(solution)/shard_map/ppermute | solution.py:73
  1348.0 117.2 %all-to-all-start.1 = ((bf16[8,192,1024]{2,1,0:T(8,128)(2,1)}), bf16[8,192,1024]{2,1,0:T(8,128)(2,1)}, u32[]{:S(2)}, u32[]{:S(2)}) async-start(bf16[8,192,1024]{2,1,0:T(8,128)(2,1)} %pad_maximum_fusion.10), calls=%async_computation.1 | async-start | bytes 6291456 | tf_op jit(solution)/shard_map/all_to_all | solution.py:415
  1360.9 74.1 %collective-permute-start.84 = (bf16[2,2,2,64,2048]{4,3,2,1,0:T(8,128)(2,1)S(1)}, bf16[2,2,2,64,2048]{4,3,2,1,0:T(8,128)(2,1)S(1)}, u32[]{:S(2)}, u32[]{:S(2)}) collective-permute-start(bf16[2,2,2,64,2048]{4,3,2,1,0:T(8,128)(2,1)S(1)} %slice_bitcast_fusion), channel_id=1, source_target_pairs={{0,4},{4,0},{1,5},{5,1},{2,6},{6,2},{3,7},{7,3},{8,12},{12,8},{9,1... | collective-permute-start | bytes 6291464 | tf_op jit(solution)/shard_map/ppermute | solution.py:73
  1374.7 61.7 %collective-permute-start.74 = (bf16[2,2,2,64,2048]{4,3,2,1,0:T(8,128)(2,1)S(1)}, bf16[2,2,2,64,2048]{4,3,2,1,0:T(8,128)(2,1)S(1)}, u32[]{:S(2)}, u32[]{:S(2)}) collective-permute-start(bf16[2,2,2,64,2048]{4,3,2,1,0:T(8,128)(2,1)S(1)} %bitcast.601), channel_id=1, source_target_pairs={{0,2},{2,0},{1,3},{3,1},{4,6},{6,4},{5,7},{7,5},{8,10},{10,8},{9,1... | collective-permute-start | bytes 6291464 | tf_op jit(solution)/shard_map/ppermute | solution.py:73
  (288 other events, 6438.4 us)

commit v3 on v2

--- a/solution.py
+++ b/solution.py
@@ -93,100 +93,65 @@
         self.far_seq = self.seq[:-2]
         self.far_dp = self.dp[:-1]
         self.far = self.far_seq + self.far_dp
-
-    def flips(self, value, first_dims):
-        for axis, dim in zip(self.far, first_dims):
-            value = jnp.where(lax.axis_index(axis) == 1, jnp.flip(value, dim), value)
-        return value
-
-    def to_relative(self, value):
+        self.canon = self.far + self.team
+        self.order_x = self.far_seq + (self.l, self.x) + self.far_dp
+        self.order_y = self.far_seq + (self.l,) + self.far_dp + (self.x,)
+
+    def to_far_team(self, value):
         rows, width = value.shape
-        n_seq, n_dp = len(self.far_seq), len(self.far_dp)
-        parts = value.reshape((rows,) + (2,) * n_seq + (4,) + (2,) * n_dp + (-1,))
-        dims = list(range(1, 1 + n_seq)) + list(range(2 + n_seq, 2 + n_seq + n_dp))
-        parts = self.flips(parts, dims)
-        order = [0] + dims + [1 + n_seq, 2 + n_seq + n_dp]
+        parts = value.reshape((rows,) + (2,) * len(self.every) + (-1,))
+        order = [0] + [1 + self.every.index(axis) for axis in self.canon] + [1 + len(self.every)]
         return parts.transpose(order).reshape(rows, width)
 
-    def from_relative(self, value):
+    def from_far_team(self, value):
         rows, width = value.shape
-        n_seq, n_dp = len(self.far_seq), len(self.far_dp)
-        parts = value.reshape((rows,) + (2,) * (n_seq + n_dp) + (4, -1))
-        parts = self.flips(parts, list(range(1, 1 + n_seq + n_dp)))
-        order = [0] + list(range(1, 1 + n_seq)) + [1 + n_seq + n_dp]
-        order += list(range(1 + n_seq, 1 + n_seq + n_dp)) + [2 + n_seq + n_dp]
+        parts = value.reshape((rows,) + (2,) * len(self.every) + (-1,))
+        order = [0] + [1 + self.canon.index(axis) for axis in self.every] + [1 + len(self.every)]
         return parts.transpose(order).reshape(rows, width)
 
-    def source_in_natural(self, width):
-        return self.to_relative(jnp.arange(width, dtype=jnp.int32)[None])[0]
-
-    def spread_order(self, width):
-        n_seq, n_dp = len(self.far_seq), len(self.far_dp)
-        own = jnp.arange(width, dtype=jnp.int32).reshape((2,) * (n_seq + n_dp + 3) + (-1,))
-        for dim, axis in enumerate(self.team):
-            at = n_seq + n_dp + dim
+    def spread_order(self, width, order):
+        own = jnp.arange(width, dtype=jnp.int32).reshape((2,) * len(self.canon) + (-1,))
+        for at, axis in enumerate(self.canon):
             own = jnp.where(lax.axis_index(axis) == 1, jnp.flip(own, at), own)
-        far_seq = list(range(n_seq))
-        far_dp = list(range(n_seq, n_seq + n_dp))
-        at_l, at_x, at_c = (n_seq + n_dp + dim for dim in range(3))
-        return own.transpose([at_c] + far_dp + [at_x, at_l] + far_seq + [n_seq + n_dp + 3]).reshape(-1)
-
-    def gather(self, block, x_first):
-        canon = self.far_seq + self.far_dp + self.team
-        middle_axes = (self.x,) + self.far_dp if x_first else self.far_dp + (self.x,)
-        held = []
-        for axis in self.far_seq + (self.l,) + middle_axes + (self.c,):
-            other = swap(block, axis)
-            place = sum(canon.index(one) < canon.index(axis) for one in held)
-            held.append(axis)
-            if axis in self.team:
-                second = lax.axis_index(axis) == 1
-                block, other = jnp.where(second, other, block), jnp.where(second, block, other)
-            block = jnp.stack([block, other], axis=place)
+        axes = (self.c,) + tuple(reversed(order))
+        return own.transpose([self.canon.index(axis) for axis in axes] + [len(self.canon)]).reshape(-1)
+
+    def grow(self, block, axes):
+        for axis in axes:
+            block = jnp.concatenate([block, swap(block, axis)], axis=0)
+        return block
+
+    def gather_pieces(self, block, axes):
+        block = self.grow(block, axes[:-1])
+        other = swap(block, axes[-1])
+        return [block, other, swap(block, self.c), swap(other, self.c)]
+
+    def gather(self, block, done, axes):
+        held = list(reversed(done))
+        block = block.reshape((2,) * len(held) + (-1, block.shape[-1]))
+        for axis in axes:
+            block = jnp.stack([block, swap(block, axis)], axis=0)
+            held = [axis] + held
+        block = block.transpose([held.index(axis) for axis in self.canon] + [len(held), len(held) + 1])
+        for at, axis in enumerate(self.canon):
+            block = jnp.where(lax.axis_index(axis) == 1, jnp.flip(block, at), block)
         return block.reshape((-1, block.shape[-1]))
 
-    def spread_sum(self, pairs, y_first):
+    def spread_sum(self, pairs, order):
         half = pairs[0][0].shape[1] // 2
         away = jnp.concatenate([product_tn(one[:, half:], two).astype(BF16) for one, two in pairs], axis=1)
         kept = jnp.concatenate([product_tn(one[:, :half], two).astype(BF16) for one, two in pairs], axis=1)
-        total = (kept.astype(F32) + swap(away, self.c).astype(F32)).astype(BF16)
-        names = list(self.far_dp) + [self.x, self.l] + list(self.far_seq)
-        total = total.reshape((2,) * len(names) + (-1, total.shape[1]))
-        order = list(self.far_dp) + [self.x] if y_first else [self.x] + list(self.far_dp)
-        for axis in order + [self.l] + list(reversed(self.far_seq)):
-            dim = names.index(axis)
-            names.remove(axis)
-            away = swap(lax.index_in_dim(total, 1, dim, False), axis).astype(F32)
-            total = lax.index_in_dim(total, 0, dim, False).astype(F32) + away
-            if names:
-                total = total.astype(BF16)
+        total = kept.astype(F32) + swap(away, self.c).astype(F32)
+        for axis in reversed(order):
+            half = total.shape[0] // 2
+            total = total.astype(BF16)
+            total = total[:half].astype(F32) + swap(total[half:], axis).astype(F32)
         return total
 
     def total(self, value):
         for axis in reversed(self.every):
             value = value + swap(value, axis)
         return value
-
-    def far_gather(self, block):
-        pieces = {(): block}
-        for axis in self.far:
-            pieces.update({key + (axis,): swap(piece, axis) for key, piece in list(pieces.items())})
-        return [pieces[key] for key in self.far_keys()]
-
-    def far_keys(self):
-        keys = [()]
-        for axis in self.far:
-            keys = [key + extra for key in keys for extra in ((), (axis,))]
-        return keys
-
-    def far_scatter(self, pieces):
-        held = dict(zip(self.far_keys(), pieces))
-        for axis in reversed(self.far):
-            for key in [key for key in held if axis in key]:
-                into = tuple(one for one in key if one != axis)
-                moved = swap(held.pop(key), axis).astype(F32)
-                held[into] = (held[into].astype(F32) + moved).astype(BF16)
-        return held[()]
 
     def team_gather(self, own):
         by_x, by_l = swap(own, self.x), swap(own, self.l)
@@ -208,6 +173,23 @@
         by_l = jnp.concatenate([first, by_l[half:]], axis=0).astype(BF16)
         by_x = jnp.concatenate([by_x[:half], second], axis=0).astype(BF16)
         return own + swap(by_l, self.l).astype(F32) + swap(by_x, self.x).astype(F32)
+
+
+def product_split(left, pieces):
+    width = left.shape[1] // len(pieces)
+    return sum(product(left[:, i * width : (i + 1) * width], one) for i, one in enumerate(pieces))
+
+
+def product_nt_split(left, pieces):
+    return jnp.concatenate([product_nt(left, one) for one in pieces], axis=1)
+
+
+def reorder(values, matrix):
+    rows = values.shape[0]
+    high = lax.reduce_precision(values, 8, 7)
+    parts = jnp.concatenate([high.astype(BF16), (values - high).astype(BF16)], axis=0)
+    parts = product_nt(parts, matrix)
+    return parts[:rows] + parts[rows:]
 
 
 def passed_along(value, axes, count, steps):
@@ -255,12 +237,6 @@
 
     kvl_widths = [key_weight.shape[1], value_weight.shape[1], laurel_left.shape[1]]
     rest_widths = [laurel_right.shape[1], side_gate.shape[1], side_output.shape[1]]
-    query_full = plan.gather(query_weight, True)
-    kvl_full = plan.gather(jnp.concatenate([key_weight, value_weight, laurel_left], axis=1), False)
-    output_full = plan.gather(output_weight, False)
-    rest_full = plan.gather(jnp.concatenate([laurel_right, side_gate, side_output], axis=1), True)
-    right_full, side_gate_full, side_output_full = split_columns(rest_full, rest_widths)
-
     feed_local = jnp.concatenate(
         [
             one.reshape(local_rows, team_size, hidden_own).transpose(1, 0, 2)
@@ -269,26 +245,40 @@
         axis=1,
     )
     feed_team = lax.all_to_all(feed_local, plan.team, split_axis=0, concat_axis=0, tiled=True)
-    feed_team = [
-        feed_team[:, index * local_rows : (index + 1) * local_rows].reshape(-1, hidden_own)
-        for index in range(3)
-    ]
-    feed_pieces = [plan.far_gather(one) for one in feed_team]
+    feed_team = feed_team.reshape(team_size, 3, local_rows, hidden_own).transpose(1, 0, 2, 3)
+    blocks = (
+        query_weight,
+        jnp.concatenate([key_weight, value_weight, laurel_left], axis=1),
+        output_weight,
+        jnp.concatenate([laurel_right, side_gate, side_output], axis=1),
+    )
+    blocks = [plan.grow(block, plan.far_seq) for block in blocks]
+    blocks, feed_team = lax.optimization_barrier((blocks, feed_team))
+    feed_full = lax.all_gather(feed_team.reshape(-1, hidden_own), plan.far, axis=0, tiled=True)
+    feed_full = feed_full.reshape(-1, 3, team_size * local_rows, hidden_own)
+    steps_x, steps_y = plan.order_x[len(plan.far_seq) :], plan.order_y[len(plan.far_seq) :]
+    query_full = plan.gather_pieces(blocks[0], steps_x)
+    kvl_full = plan.gather_pieces(blocks[1], steps_y)
+    output_full = plan.gather_pieces(blocks[2], steps_y)
+    rest_full = plan.gather(blocks[3], plan.far_seq, steps_x + (plan.c,))
+    right_full, side_gate_full, side_output_full = split_columns(rest_full, rest_widths)
 
     places = jnp.arange(width, dtype=jnp.int32)
-    natural = plan.source_in_natural(width)
-    to_relative = (places[:, None] == natural[None, :]).astype(BF16)
-    to_spread = (places[:, None] == plan.spread_order(width)[None, :]).astype(BF16)
+    far_team = plan.to_far_team(places[None])[0]
+    to_far_team = (places[:, None] == far_team[None, :]).astype(BF16)
+    spread_x = (places[:, None] == plan.spread_order(width, plan.order_x)[None, :]).astype(BF16)
+    spread_y = (places[:, None] == plan.spread_order(width, plan.order_y)[None, :]).astype(BF16)
     gains = jnp.stack([norm_input, norm_attn, norm_laurel, norm_before, norm_after, norm_layer])
-    norm_input, norm_attn, norm_laurel, norm_before, norm_after, norm_layer = plan.to_relative(gains)
-    inputs = product(tokens.reshape(rows, width), to_relative)
-    upstream = product(cotangent.reshape(rows, width), to_relative)
+    norm_input, norm_attn, norm_laurel, norm_before, norm_after, norm_layer = plan.to_far_team(gains)
+    inputs = product(tokens.reshape(rows, width), to_far_team)
+    upstream = product(cotangent.reshape(rows, width), to_far_team)
     side_in = per_layer.astype(F32).reshape(rows, -1)
     normed, pre_pull = jax.vjp(rms, inputs, norm_input)
     normed_low = normed.astype(BF16)
-    normed_spread = product(normed_low, to_spread).astype(BF16)
-    queries = product(normed_low, query_full).reshape(batch, block, heads, head_size)
-    keys, values, latent = split_columns(product(normed_low, kvl_full), kvl_widths)
+    normed_x = product(normed_low, spread_x).astype(BF16)
+    normed_y = product(normed_low, spread_y).astype(BF16)
+    queries = product_split(normed_x, query_full).reshape(batch, block, heads, head_size)
+    keys, values, latent = split_columns(product_split(normed_y, kvl_full), kvl_widths)
     keys = keys.reshape(batch, block, kv_heads, head_size)
     values = values.reshape(batch, block, kv_heads, head_size)
     latent_low = latent.astype(BF16)
@@ -314,10 +304,7 @@
             gathered.append(pair_low)
         else:
             gathered.append(passed_along(pair_low, plan.seq, seq_count, offset))
-    pairs_all, feed_pieces = lax.optimization_barrier(
-        (jnp.concatenate(gathered, axis=2), feed_pieces)
-    )
-    gate_full, up_full, down_full = [jnp.concatenate(pieces, axis=0) for pieces in feed_pieces]
+    pairs_all = jnp.concatenate(gathered, axis=2)
     keys_all = pairs_all[0]
     values_all = pairs_all[1]
     key_count = keys_all.shape[1]
@@ -347,13 +334,16 @@
     probs_low = probs.astype(BF16)
     attended = jnp.einsum("bkgts,bskd->btkgd", probs_low, values_all, preferred_element_type=F32)
     attended_low = attended.reshape(rows, heads * head_size).astype(BF16)
-    attn_proj = product_nt(attended_low, output_full)
+    attn_proj = reorder(product_nt_split(attended_low, output_full), spread_y)
     laurel = product_nt(latent_low, right_full)
     (resid_one, feed_in), mid_pull = jax.vjp(
         middle, inputs, normed, attn_proj, laurel, norm_attn, norm_laurel, norm_before
     )
 
-    feed_chunks = plan.team_gather(feed_in.astype(BF16))
+    feed_low = feed_in.astype(BF16)
+    feed_full, feed_low = lax.optimization_barrier((feed_full, feed_low))
+    gate_full, up_full, down_full = [feed_full[:, at].reshape(width, hidden_own) for at in range(3)]
+    feed_chunks = plan.team_gather(feed_low)
     pulls = []
     hidden_chunks = []
     feed_parts = []
@@ -372,7 +362,7 @@
     side_low = side_val.astype(BF16)
     side_out = product_nt(side_low, side_output_full)
     result, final_pull = jax.vjp(finish, resid_two, side_out, norm_layer)
-    output = product_nt(result.astype(BF16), to_relative).astype(BF16).reshape(batch, block, width)
+    output = product_nt(result.astype(BF16), to_far_team).astype(BF16).reshape(batch, block, width)
 
     d_resid_two, d_side_out, grad_norm_layer = final_pull(upstream)
     d_side_out_low = d_side_out.astype(BF16)
@@ -394,32 +384,32 @@
         d_feed_parts.append(part.astype(BF16))
     d_feed_in = plan.team_scatter(d_feed_parts)
 
-    far_count = 2 ** len(plan.far)
-    piece_width = width // far_count
     feed_all = jnp.concatenate(feed_chunks, axis=0)
     d_out_all = jnp.concatenate(d_out_chunks, axis=0)
-    pairs = (
-        (d_out_all, jnp.concatenate(hidden_chunks, axis=0)),
-        (feed_all, jnp.concatenate(d_gate_chunks, axis=0)),
-        (feed_all, jnp.concatenate(d_up_chunks, axis=0)),
-    )
-    grad_pieces = [
+    feed_terms = jnp.stack(
         [
-            product_tn(left[:, index * piece_width : (index + 1) * piece_width], right).astype(BF16)
-            for index in range(far_count)
-        ]
-        for left, right in pairs
-    ]
-    d_feed_in, grad_pieces = lax.optimization_barrier((d_feed_in, grad_pieces))
-    team_grads = [plan.far_scatter(pieces) for pieces in grad_pieces]
+            product_tn(left, jnp.concatenate(right, axis=0)).astype(BF16).reshape(-1, team_size * local_rows, hidden_own)
+            for left, right in (
+                (feed_all, d_gate_chunks),
+                (feed_all, d_up_chunks),
+                (d_out_all, hidden_chunks),
+            )
+        ],
+        axis=1,
+    )
+    d_feed_in, feed_terms = lax.optimization_barrier((d_feed_in, feed_terms))
+    feed_sum = lax.psum_scatter(
+        feed_terms.reshape(-1, hidden_own), plan.far, scatter_dimension=0, tiled=True
+    )
+    feed_sum = feed_sum.reshape(3, team_size, local_rows, hidden_own).transpose(1, 0, 2, 3)
     feed_grads = lax.all_to_all(
-        jnp.concatenate([one.reshape(team_size, local_rows, hidden_own) for one in team_grads], axis=1),
+        feed_sum.reshape(team_size, 3 * local_rows, hidden_own),
         plan.team,
         split_axis=0,
         concat_axis=0,
         tiled=True,
     )
-    grad_down, grad_gate, grad_up = [
+    grad_gate, grad_up, grad_down = [
         jnp.concatenate(
             [feed_grads[at, index * local_rows : (index + 1) * local_rows] for at in range(team_size)],
             axis=1,
@@ -438,20 +428,20 @@
     ) = mid_pull((d_resid_one, d_feed_in))
     d_attn_low = d_attn_proj.astype(BF16)
     d_laurel_low = d_laurel.astype(BF16)
-    d_attended_low = product(d_attn_low, output_full).astype(BF16)
+    d_attn_y = product(d_attn_low, spread_y).astype(BF16)
+    d_attended_low = product_split(d_attn_y, output_full).astype(BF16)
     d_latent_low = product(d_laurel_low, right_full).astype(BF16)
-    spread = product(
-        jnp.concatenate([d_attn_low, d_laurel_low, resid_low, d_side_out_low], axis=0), to_spread
-    ).astype(BF16)
-    grad_output = plan.spread_sum([(spread[:rows], attended_low)], False)
+    spread = jnp.concatenate([d_laurel_low, resid_low, d_side_out_low], axis=0)
+    spread = product(spread, spread_x).astype(BF16)
+    grad_output = plan.spread_sum([(d_attn_y, attended_low)], plan.order_y)
     grad_right, grad_side_gate, grad_side_output = split_columns(
         plan.spread_sum(
             [
-                (spread[rows : 2 * rows], latent_low),
-                (spread[2 * rows : 3 * rows], d_side_pre_low),
-                (spread[3 * rows :], side_low),
+                (spread[:rows], latent_low),
+                (spread[rows : 2 * rows], d_side_pre_low),
+                (spread[2 * rows :], side_low),
             ],
-            True,
+            plan.order_x,
         ),
         rest_widths,
     )
@@ -483,23 +473,20 @@
         ],
         axis=1,
     )
-    grad_query = plan.spread_sum([(normed_spread, d_queries_low)], True)
+    grad_query = plan.spread_sum([(normed_x, d_queries_low)], plan.order_x)
     grad_key, grad_value, grad_left = split_columns(
-        plan.spread_sum([(normed_spread, d_kvl_low)], False), kvl_widths
-    )
-    d_normed = d_normed + product_nt(d_queries_low, query_full) + product_nt(d_kvl_low, kvl_full)
+        plan.spread_sum([(normed_y, d_kvl_low)], plan.order_y), kvl_widths
+    )
+    d_normed = d_normed + reorder(product_nt_split(d_queries_low, query_full), spread_x)
+    d_normed = d_normed + reorder(product_nt_split(d_kvl_low, kvl_full), spread_y)
     d_inputs_norm, grad_norm_input = pre_pull(d_normed)
-    d_tokens = d_inputs + d_inputs_norm
-    high = lax.reduce_precision(d_tokens, 8, 7)
-    halves = jnp.concatenate([high.astype(BF16), (d_tokens - high).astype(BF16)], axis=0)
-    halves = product_nt(halves, to_relative)
-    grad_tokens = (halves[:rows] + halves[rows:]).reshape(batch, block, width)
+    grad_tokens = reorder(d_inputs + d_inputs_norm, to_far_team).reshape(batch, block, width)
     grad_side = d_side_in.reshape(batch, block, -1)
     early = jnp.stack(
         [grad_norm_attn, grad_norm_laurel, grad_norm_before, grad_norm_after, grad_norm_layer]
     )
-    early = plan.total(plan.from_relative(early))
-    late = jnp.concatenate([plan.from_relative(grad_norm_input[None])[0], grad_norm_query, grad_norm_key])
+    early = plan.total(plan.from_far_team(early))
+    late = jnp.concatenate([plan.from_far_team(grad_norm_input[None])[0], grad_norm_query, grad_norm_key])
     late = plan.total(late)
     late_parts = split_columns(late, [width, head_size, head_size])
     return (

time: 1510 us -> 1210 us (0.80)
  waiting for transfers between devices: 658 us -> 438 us
  other arithmetic: 151 us -> 103 us
  starting transfers between devices: 262 us -> 228 us
  local copies, waits for them, and re-layouts: 168 us -> 147 us
    ppermute x100 -> x85, waiting for transfers between devices: 606 us -> 326 us  [swap(): return lax.ppermute(value, axis, [(0, 1), (1, 0)])]
    ppermute x100 -> x85, starting transfers between devices: 223 us -> 131 us  [swap(): return lax.ppermute(value, axis, [(0, 1), (1, 0)])]
    ppermute x12, starting transfers between devices: 28.3 us -> 87.6 us  [passed_along(): lax.ppermute(value, axes, [(source, source + steps) for source in range(i...]
    another operation x40 -> x10, other arithmetic: 64.9 us -> 7.34 us  [the longest x1 5.51 us: body(): jnp.stack([product_tn(left, jnp.concatenate(right, axis=0)).astype(BF16)....]
    all_to_all x1, waiting for transfers between devices: 0.01 us -> 30.6 us  [body(): lax.all_to_all(feed_local, plan.team, split_axis=0, concat_axis=0, tiled=...]
    ppermute x12, waiting for transfers between devices: 52.5 us -> 81.2 us  [passed_along(): lax.ppermute(value, axes, [(source, source + steps) for source in range(i...]
    dot_general x24 -> x15, matrix products: 85.5 us -> 59.7 us  [product_tn(): lax.dot_general(left, right, (((0,), (0,)), ((), ())), preferred_element_...]
    dot_general x20 -> x32, matrix products: 63.3 us -> 87.5 us  [product_nt(): lax.dot_general(left, right, (((1,), (1,)), ((), ())), preferred_element_...]
  transfers between devices with their start and end apart: 114 -> 101, of which waited for: 48 -> 43; matrix products, arithmetic and copies ran while one was open for 29% -> 37% of each run, Pallas kernels for 0% -> 0%
where the time goes in v3:
time: 1210 us; the launch traced here: 1200 us
  waiting for transfers between devices  438 us (36%)
  matrix products  265 us (22%)
  starting transfers between devices  228 us (19%)
  local copies, waits for them, and re-layouts  147 us (12%)
  other arithmetic  103 us (9%)
  between operations  18.3 us (2%)
    ppermute x85, waiting for transfers between devices, swap(): return lax.ppermute(value, axis, [(0, 1), (1, 0)])  326 us
    ppermute x85, starting transfers between devices, swap(): return lax.ppermute(value, axis, [(0, 1), (1, 0)])  131 us
    dot_general x33, matrix products, product(): return jnp.dot(left, right, preferred_element_type=F32)  100 us
    ppermute x12, starting transfers between devices, passed_along(): lax.ppermute(value, axes, [(source, source + steps) for source in range(i...  87.6 us
    dot_general x32, matrix products, product_nt(): lax.dot_general(left, right, (((1,), (1,)), ((), ())), preferred_element_...  87.5 us
    ppermute x12, waiting for transfers between devices, passed_along(): lax.ppermute(value, axes, [(source, source + steps) for source in range(i...  81.2 us
    unnamed x458, local copies, waits for them, and re-layouts  79.5 us
    dot_general x15, matrix products, product_tn(): lax.dot_general(left, right, (((0,), (0,)), ((), ())), preferred_element_...  59.7 us
  transfers between devices with their start and end apart: 101, of which 43 were waited for; matrix products, arithmetic and copies ran while one was open for 37% of the time, Pallas kernels for 0%

profile of v3, /device:TPU:0, one launch (start us, length us, event | category | flops | bytes accessed | tf_op | source)
XLA Modules:
  0.0 1199.8 jit_solution(3289758171197390024)
XLA Ops:
  25.8 4.6 all-to-all-start
  42.3 4.5 fusion.83
  54.1 30.6 %all-to-all-done = bf16[8,192,1024]{2,1,0:T(8,128)(2,1)} async-done(((bf16[8,192,1024]{2,1,0:T(8,128)(2,1)}), bf16[8,192,1024]{2,1,0:T(8,128)(2,1)}, u32[]{:S(2)}, u32[]{:S(2)}) %all-to-all-start) | async-done | bytes 3145760 | tf_op jit(solution)/shard_map/all_to_all | solution.py:247
  105.5 16.9 %collective-permute-done.15 = bf16[128,2048]{1,0:T(8,128)(2,1)S(1)} collective-permute-done((bf16[128,2048]{1,0:T(8,128)(2,1)S(1)}, bf16[128,2048]{1,0:T(8,128)(2,1)S(1)}, u32[]{:S(2)}, u32[]{:S(2)}) %collective-permute-start.15) | collective-permute-done | bytes 524320 | tf_op jit(solution)/shard_map/ppermute | solution.py:73
  124.5 17.7 %collective-permute-done.20 = bf16[128,2048]{1,0:T(8,128)(2,1)S(1)} collective-permute-done((bf16[128,2048]{1,0:T(8,128)(2,1)S(1)}, bf16[128,2048]{1,0:T(8,128)(2,1)S(1)}, u32[]{:S(2)}, u32[]{:S(2)}) %collective-permute-start.20) | collective-permute-done | bytes 524320 | tf_op jit(solution)/shard_map/ppermute | solution.py:73
  148.1 9.6 collective-permute-done.27
  159.6 32.4 %collective-permute-done.21 = bf16[256,2048]{1,0:T(8,128)(2,1)S(1)} collective-permute-done((bf16[256,2048]{1,0:T(8,128)(2,1)S(1)}, bf16[256,2048]{1,0:T(8,128)(2,1)S(1)}, u32[]{:S(2)}, u32[]{:S(2)}) %collective-permute-start.21) | collective-permute-done | bytes 1048608 | tf_op jit(solution)/shard_map/ppermute | solution.py:73
  216.7 32.5 %collective-permute-done.12 = bf16[2,2,128,2,256]{4,2,3,1,0:T(8,128)(2,1)S(1)} collective-permute-done((bf16[2,2,128,2,256]{4,2,3,1,0:T(8,128)(2,1)}, bf16[2,2,128,2,256]{4,2,3,1,0:T(8,128)(2,1)S(1)}, u32[]{:S(2)}, u32[]{:S(2)}) %collective-permute-start.12) | collective-permute-done | bytes 524320 | tf_op jit(solution)/shard_map/ppermute | solution.py:197
  249.2 42.6 %collective-permute-start.9 = (bf16[2,2,128,2,256]{4,2,3,1,0:T(8,128)(2,1)}, bf16[2,2,128,2,256]{4,2,3,1,0:T(8,128)(2,1)}, u32[]{:S(2)}, u32[]{:S(2)}) collective-permute-start(bf16[2,2,128,2,256]{4,2,3,1,0:T(8,128)(2,1)} %pad_maximum_fusion.24), channel_id=1, source_target_pairs={{0,16},{4,20},{8,24},{12,28},{1,17},{5,21},{9,25},{13,29},{2,18},{... | collective-permute-start | bytes 1572872 | tf_op jit(solution)/shard_map/ppermute | solution.py:197
  292.6 25.5 %collective-permute-start.10 = (bf16[2,2,128,2,256]{4,2,3,1,0:T(8,128)(2,1)}, bf16[2,2,128,2,256]{4,2,3,1,0:T(8,128)(2,1)}, u32[]{:S(2)}, u32[]{:S(2)}) collective-permute-start(bf16[2,2,128,2,256]{4,2,3,1,0:T(8,128)(2,1)} %pad_maximum_fusion.24), channel_id=1, source_target_pairs={{0,12},{4,16},{8,20},{12,24},{16,28},{1,13},{5,17},{9,21},{13,25},... | collective-permute-start | bytes 1572872 | tf_op jit(solution)/shard_map/ppermute | solution.py:197
  330.9 7.7 collective-permute-done.13
  338.7 17.1 %collective-permute-done.14 = bf16[2,2,128,2,256]{4,2,3,1,0:T(8,128)(2,1)S(1)} collective-permute-done((bf16[2,2,128,2,256]{4,2,3,1,0:T(8,128)(2,1)}, bf16[2,2,128,2,256]{4,2,3,1,0:T(8,128)(2,1)S(1)}, u32[]{:S(2)}, u32[]{:S(2)}) %collective-permute-start.14) | collective-permute-done | bytes 524320 | tf_op jit(solution)/shard_map/ppermute | solution.py:197
  396.1 4.5 fusion.6
  407.1 18.8 %collective-permute-start.34 = (bf16[256,2048]{0,1:T(8,128)(2,1)}, bf16[256,2048]{0,1:T(8,128)(2,1)S(1)}, u32[]{:S(2)}, u32[]{:S(2)}) collective-permute-start(bf16[256,2048]{0,1:T(8,128)(2,1)} %multiply_convert_fusion.8), channel_id=1, source_target_pairs={{0,4},{4,0},{1,5},{5,1},{2,6},{6,2},{3,7},{7,3},{8,12},{12,8},{9,1... | collective-permute-start | bytes 3145736 | tf_op jit(solution)/shard_map/ppermute | solution.py:73
  430.1 6.2 fusion.284
  436.3 13.6 %collective-permute-done.34 = bf16[256,2048]{0,1:T(8,128)(2,1)S(1)} collective-permute-done((bf16[256,2048]{0,1:T(8,128)(2,1)}, bf16[256,2048]{0,1:T(8,128)(2,1)S(1)}, u32[]{:S(2)}, u32[]{:S(2)}) %collective-permute-start.34) | collective-permute-done | bytes 1048608 | tf_op jit(solution)/shard_map/ppermute | solution.py:73
  506.6 11.8 collective-permute-done.39
  522.6 22.0 %collective-permute-done.40 = bf16[256,2048]{0,1:T(8,128)(2,1)} collective-permute-done((bf16[256,2048]{0,1:T(8,128)(2,1)}, bf16[256,2048]{0,1:T(8,128)(2,1)}, u32[]{:S(2)}, u32[]{:S(2)}) %collective-permute-start.40) | collective-permute-done | bytes 1048608 | tf_op jit(solution)/shard_map/ppermute | solution.py:73
  558.1 5.1 multiply_reduce_fusion
  573.1 7.6 fusion.82
  580.8 13.2 %collective-permute-done.50 = bf16[256,2048]{0,1:T(8,128)(2,1)} collective-permute-done((bf16[256,2048]{0,1:T(8,128)(2,1)}, bf16[256,2048]{0,1:T(8,128)(2,1)}, u32[]{:S(2)}, u32[]{:S(2)}) %collective-permute-start.50) | collective-permute-done | bytes 1048608 | tf_op jit(solution)/shard_map/ppermute | solution.py:73
  598.1 5.6 multiply_convert_fusion.3
  614.9 4.9 multiply_convert_fusion
  626.6 4.9 multiply_convert_fusion.2
  651.8 11.2 fusion.58
  663.0 4.9 add_convert_fusion.6
  668.2 13.3 %fusion.61 = bf16[2048,1024]{1,0:T(8,128)(2,1)S(1)} fusion(bf16[2048,2048]{0,1:T(8,128)(2,1)} %get-tuple-element.327, bf16[512,1024]{1,0:T(8,128)(2,1)} %copy-done.199, bf16[512,1024]{1,0:T(8,128)(2,1)} %copy-done.198, bf16[512,1024]{1,0:T(8,128)(2,1)} %copy-done.197, bf16[512,1024]{1,0:T(8,128)(2,1)} %copy-done.196), kind=kOutput, calls=%fused_computation.80 | convolution fusion | flops 8608808960 | bytes 16777216 | tf_op jit(solution)/shard_map/dot_general | solution.py:34
  688.5 10.4 collective-permute-done.59
  702.5 12.1 %fusion.55 = bf16[2048,1024]{1,0:T(8,128)(2,1)S(1)} fusion(bf16[2048,2048]{0,1:T(8,128)(2,1)} %constant_dynamic-update-slice_fusion.40, bf16[512,1024]{1,0:T(8,128)(2,1)} %copy-done.188, bf16[512,1024]{1,0:T(8,128)(2,1)} %copy-done.186, bf16[512,1024]{1,0:T(8,128)(2,1)} %copy-done.187, bf16[512,1024]{1,0:T(8,128)(2,1)S(1)} %copy-done.185), kind=kOutput, calls=%fused_computation.78 | convolution fusion | flops 8608808960 | bytes 16777216 | tf_op jit(solution)/shard_map/dot_general | solution.py:34
  714.6 5.5 pad_maximum_fusion
  732.7 4.7 multiply_reduce_fusion.3
  754.8 5.1 fusion.27
  759.9 4.7 fusion.29
  799.6 7.3 fusion.66
  826.7 6.5 fusion.2
  847.7 50.3 %collective-permute-done.95 = f32[5,2048]{1,0:T(8,128)S(1)} collective-permute-done((f32[5,2048]{1,0:T(8,128)S(1)}, f32[5,2048]{1,0:T(8,128)S(1)}, u32[]{:S(2)}, u32[]{:S(2)}) %collective-permute-start.95) | collective-permute-done | bytes 40992 | tf_op jit(solution)/shard_map/ppermute | solution.py:73
  908.6 6.3 collective-permute-done.64
  914.9 10.4 collective-permute-done.63
  945.1 4.5 fusion.4
  961.9 39.3 %collective-permute-start.89 = (f32[2560]{0:T(1024)S(1)}, f32[2560]{0:T(1024)S(1)}, u32[]{:S(2)}, u32[]{:S(2)}) collective-permute-start(f32[2560]{0:T(1024)S(1)} %add.570), channel_id=1, source_target_pairs={{0,4},{4,0},{1,5},{5,1},{2,6},{6,2},{3,7},{7,3},{8,12},{12,8},{9,1... | collective-permute-start | bytes 30728 | tf_op jit(solution)/shard_map/ppermute | solution.py:73
  1011.1 4.6 fusion.8
  1023.2 17.8 %collective-permute-done.84 = bf16[256,576]{0,1:T(8,128)(2,1)S(1)} collective-permute-done((bf16[256,576]{0,1:T(8,128)(2,1)S(1)}, bf16[256,576]{0,1:T(8,128)(2,1)S(1)}, u32[]{:S(2)}, u32[]{:S(2)}) %collective-permute-start.84) | collective-permute-done | bytes 294944 | tf_op jit(solution)/shard_map/ppermute | solution.py:73
  1061.1 5.8 collective-permute-done.86
  1077.5 37.5 %collective-permute-done.78 = bf16[512,2048]{1,0:T(8,128)(2,1)} collective-permute-done((bf16[512,2048]{1,0:T(8,128)(2,1)S(1)}, bf16[512,2048]{1,0:T(8,128)(2,1)}, u32[]{:S(2)}, u32[]{:S(2)}) %collective-permute-start.78) | collective-permute-done | bytes 2097184 | tf_op jit(solution)/shard_map/ppermute | solution.py:73
  1129.5 6.3 collective-permute-done.79
  1141.0 9.6 collective-permute-done.69
  1156.4 10.2 collective-permute-done.70
  1173.0 5.9 collective-permute-done.71
  (965 shorter events, 527.0 us)
Async XLA Ops:
  8.9 41.0 %collective-permute-start.3 = (bf16[64,576]{1,0:T(8,128)(2,1)}, bf16[64,576]{1,0:T(8,128)(2,1)S(1)}, u32[]{:S(2)}, u32[]{:S(2)}) collective-permute-start(bf16[64,576]{1,0:T(8,128)(2,1)} %pad_maximum_fusion.29), channel_id=1, source_target_pairs={{0,16},{16,0},{1,17},{17,1},{2,18},{18,2},{3,19},{19,3},{4,20},{20... | collective-permute-start | bytes 221192 | tf_op jit(solution)/shard_map/ppermute | solution.py:73
  12.9 39.1 %collective-permute-start = (bf16[64,2048]{1,0:T(8,128)(2,1)}, bf16[64,2048]{1,0:T(8,128)(2,1)}, u32[]{:S(2)}, u32[]{:S(2)}) collective-permute-start(bf16[64,2048]{1,0:T(8,128)(2,1)} %param.29), channel_id=1, source_target_pairs={{0,16},{16,0},{1,17},{17,1},{2,18},{18,2},{3,19},{19,3},{4,20},{20... | collective-permute-start | bytes 786440 | tf_op jit(solution)/shard_map/ppermute | solution.py:73
  12.9 40.1 %collective-permute-start.2 = (bf16[64,2048]{1,0:T(8,128)(2,1)}, bf16[64,2048]{1,0:T(8,128)(2,1)}, u32[]{:S(2)}, u32[]{:S(2)}) collective-permute-start(bf16[64,2048]{1,0:T(8,128)(2,1)} %param.32), channel_id=1, source_target_pairs={{0,16},{16,0},{1,17},{17,1},{2,18},{18,2},{3,19},{19,3},{4,20},{20... | collective-permute-start | bytes 786440 | tf_op jit(solution)/shard_map/ppermute | solution.py:73
  18.6 33.2 %collective-permute-start.1 = (bf16[64,1088]{0,1:T(8,128)(2,1)S(1)}, bf16[64,1088]{0,1:T(8,128)(2,1)S(1)}, u32[]{:S(2)}, u32[]{:S(2)}) collective-permute-start(bf16[64,1088]{0,1:T(8,128)(2,1)S(1)} %pad_maximum_fusion.26), channel_id=1, source_target_pairs={{0,16},{16,0},{1,17},{17,1},{2,18},{18,2},{3,19},{19,3},{4,20},{20... | collective-permute-start | bytes 417800 | tf_op jit(solution)/shard_map/ppermute | solution.py:73
  25.8 58.9 %all-to-all-start = ((bf16[8,192,1024]{2,1,0:T(8,128)(2,1)}), bf16[8,192,1024]{2,1,0:T(8,128)(2,1)}, u32[]{:S(2)}, u32[]{:S(2)}) async-start(bf16[8,192,1024]{2,1,0:T(8,128)(2,1)} %copy.653), calls=%async_computation | async-start | bytes 6291456 | tf_op jit(solution)/shard_map/all_to_all | solution.py:247
  30.4 376.6 %all-gather.2.cloned.1.call-start = ((), (), s32[]{:S(2)}) async-start(), calls=%async_computation.3 | async-start | bytes 15728640 | tf_op jit(solution)/shard_map/all_gather | solution.py:257
  88.7 978.3 %reduce-scatter.2.cloned.1.call-start = ((), (), s32[]{:S(2)}) async-start(), calls=%async_computation.4 | async-start | bytes 15728640 | tf_op jit(solution)/shard_map/reduce_scatter | solution.py:401
  91.1 31.4 %collective-permute-start.15 = (bf16[128,2048]{1,0:T(8,128)(2,1)S(1)}, bf16[128,2048]{1,0:T(8,128)(2,1)S(1)}, u32[]{:S(2)}, u32[]{:S(2)}) collective-permute-start(bf16[128,2048]{1,0:T(8,128)(2,1)S(1)} %pad_maximum_fusion.22), channel_id=1, source_target_pairs={{0,8},{8,0},{1,9},{9,1},{2,10},{10,2},{3,11},{11,3},{4,12},{12,4},... | collective-permute-start | bytes 1572872 | tf_op jit(solution)/shard_map/ppermute | solution.py:73
  91.2 51.0 %collective-permute-start.20 = (bf16[128,2048]{1,0:T(8,128)(2,1)S(1)}, bf16[128,2048]{1,0:T(8,128)(2,1)S(1)}, u32[]{:S(2)}, u32[]{:S(2)}) collective-permute-start(bf16[128,2048]{1,0:T(8,128)(2,1)S(1)} %pad_maximum_fusion.23), channel_id=1, source_target_pairs={{0,8},{8,0},{1,9},{9,1},{2,10},{10,2},{3,11},{11,3},{4,12},{12,4},... | collective-permute-start | bytes 1572872 | tf_op jit(solution)/shard_map/ppermute | solution.py:73
  102.2 42.7 %collective-permute-start.5 = (bf16[256,1088]{0,1:T(8,128)(2,1)S(1)}, bf16[256,1088]{0,1:T(8,128)(2,1)S(1)}, u32[]{:S(2)}, u32[]{:S(2)}) collective-permute-start(bf16[256,1088]{0,1:T(8,128)(2,1)S(1)} %pad_maximum_fusion.20), channel_id=1, source_target_pairs={{0,2},{2,0},{1,3},{3,1},{4,6},{6,4},{5,7},{7,5},{8,10},{10,8},{9,1... | collective-permute-start | bytes 1671176 | tf_op jit(solution)/shard_map/ppermute | solution.py:73
  104.4 53.3 %collective-permute-start.27 = (bf16[2,2,2,64,576]{4,3,0,1,2:T(8,128)(2,1)S(1)}, bf16[2,2,2,64,576]{4,3,0,1,2:T(8,128)(2,1)S(1)}, u32[]{:S(2)}, u32[]{:S(2)}) collective-permute-start(bf16[2,2,2,64,576]{4,3,0,1,2:T(8,128)(2,1)S(1)} %get-tuple-element.350), channel_id=1, source_target_pairs={{0,2},{2,0},{1,3},{3,1},{4,6},{6,4},{5,7},{7,5},{8,10},{10,8},{9,1... | collective-permute-start | bytes 1769480 | tf_op jit(solution)/shard_map/ppermute | solution.py:73
  122.5 35.5 %collective-permute-start.16 = (bf16[256,2048]{1,0:T(8,128)(2,1)S(1)}, bf16[256,2048]{1,0:T(8,128)(2,1)S(1)}, u32[]{:S(2)}, u32[]{:S(2)}) collective-permute-start(bf16[256,2048]{1,0:T(8,128)(2,1)S(1)} %pad_maximum_fusion.8), channel_id=1, source_target_pairs={{0,4},{4,0},{1,5},{5,1},{2,6},{6,2},{3,7},{7,3},{8,12},{12,8},{9,1... | collective-permute-start | bytes 3145736 | tf_op jit(solution)/shard_map/ppermute | solution.py:73
  142.3 49.7 %collective-permute-start.21 = (bf16[256,2048]{1,0:T(8,128)(2,1)S(1)}, bf16[256,2048]{1,0:T(8,128)(2,1)S(1)}, u32[]{:S(2)}, u32[]{:S(2)}) collective-permute-start(bf16[256,2048]{1,0:T(8,128)(2,1)S(1)} %pad_maximum_fusion.10), channel_id=1, source_target_pairs={{0,2},{2,0},{1,3},{3,1},{4,6},{6,4},{5,7},{7,5},{8,10},{10,8},{9,1... | collective-permute-start | bytes 3145736 | tf_op jit(solution)/shard_map/ppermute | solution.py:73
  144.9 50.4 %collective-permute-start.6 = (bf16[512,1088]{0,1:T(8,128)(2,1)S(1)}, bf16[512,1088]{0,1:T(8,128)(2,1)S(1)}, u32[]{:S(2)}, u32[]{:S(2)}) collective-permute-start(bf16[512,1088]{0,1:T(8,128)(2,1)S(1)} %constant_dynamic-update-slice_fusion.6), channel_id=1, source_target_pairs={{0,4},{4,0},{1,5},{5,1},{2,6},{6,2},{3,7},{7,3},{8,12},{12,8},{9,1... | collective-permute-start | bytes 3342344 | tf_op jit(solution)/shard_map/ppermute | solution.py:73
  147.3 50.1 %collective-permute-start.7 = (bf16[512,1088]{0,1:T(8,128)(2,1)S(1)}, bf16[512,1088]{0,1:T(8,128)(2,1)S(1)}, u32[]{:S(2)}, u32[]{:S(2)}) collective-permute-start(bf16[512,1088]{0,1:T(8,128)(2,1)S(1)} %constant_dynamic-update-slice_fusion.6), channel_id=1, source_target_pairs={{0,1},{1,0},{2,3},{3,2},{4,5},{5,4},{6,7},{7,6},{8,9},{9,8},{10,11... | collective-permute-start | bytes 3342344 | tf_op jit(solution)/shard_map/ppermute | solution.py:73
  157.9 41.6 %collective-permute-start.28 = (bf16[2,2,2,2,64,576]{5,4,1,2,0,3:T(8,128)(2,1)S(1)}, bf16[2,2,2,2,64,576]{5,4,1,2,0,3:T(8,128)(2,1)S(1)}, u32[]{:S(2)}, u32[]{:S(2)}) collective-permute-start(bf16[2,2,2,2,64,576]{5,4,1,2,0,3:T(8,128)(2,1)S(1)} %get-tuple-element.322), channel_id=1, source_target_pairs={{0,1},{1,0},{2,3},{3,2},{4,5},{5,4},{6,7},{7,6},{8,9},{9,8},{10,11... | collective-permute-start | bytes 3538952 | tf_op jit(solution)/shard_map/ppermute | solution.py:73
  159.1 200.8 %collective-permute-start.18 = (bf16[512,2048]{1,0:T(8,128)(2,1)}, bf16[512,2048]{1,0:T(8,128)(2,1)}, u32[]{:S(2)}, u32[]{:S(2)}) collective-permute-start(bf16[512,2048]{1,0:T(8,128)(2,1)} %constant_dynamic-update-slice_fusion.16), channel_id=1, source_target_pairs={{0,1},{1,0},{2,3},{3,2},{4,5},{5,4},{6,7},{7,6},{8,9},{9,8},{10,11... | collective-permute-start | bytes 6291464 | tf_op jit(solution)/shard_map/ppermute | solution.py:73
  191.9 127.6 %collective-permute-start.17 = (bf16[512,2048]{1,0:T(8,128)(2,1)}, bf16[512,2048]{1,0:T(8,128)(2,1)}, u32[]{:S(2)}, u32[]{:S(2)}) collective-permute-start(bf16[512,2048]{1,0:T(8,128)(2,1)} %constant_dynamic-update-slice_fusion.16), channel_id=1, source_target_pairs={{0,2},{2,0},{1,3},{3,1},{4,6},{6,4},{5,7},{7,5},{8,10},{10,8},{9,1... | collective-permute-start | bytes 6291464 | tf_op jit(solution)/shard_map/ppermute | solution.py:73
  195.4 160.4 %collective-permute-start.22 = (bf16[512,2048]{1,0:T(8,128)(2,1)}, bf16[512,2048]{1,0:T(8,128)(2,1)}, u32[]{:S(2)}, u32[]{:S(2)}) collective-permute-start(bf16[512,2048]{1,0:T(8,128)(2,1)} %constant_dynamic-update-slice_fusion.19), channel_id=1, source_target_pairs={{0,4},{4,0},{1,5},{5,1},{2,6},{6,2},{3,7},{7,3},{8,12},{12,8},{9,1... | collective-permute-start | bytes 6291464 | tf_op jit(solution)/shard_map/ppermute | solution.py:73
  210.6 38.7 %collective-permute-start.12 = (bf16[2,2,128,2,256]{4,2,3,1,0:T(8,128)(2,1)}, bf16[2,2,128,2,256]{4,2,3,1,0:T(8,128)(2,1)S(1)}, u32[]{:S(2)}, u32[]{:S(2)}) collective-permute-start(bf16[2,2,128,2,256]{4,2,3,1,0:T(8,128)(2,1)} %pad_maximum_fusion.24), channel_id=1, source_target_pairs={{0,4},{4,8},{8,12},{12,16},{16,20},{20,24},{24,28},{1,5},{5,9},{9,... | collective-permute-start | bytes 1572872 | tf_op jit(solution)/shard_map/ppermute | solution.py:197
  213.6 79.0 %collective-permute-start.11 = (bf16[2,2,128,2,256]{4,2,3,1,0:T(8,128)(2,1)}, bf16[2,2,128,2,256]{4,2,3,1,0:T(8,128)(2,1)S(1)}, u32[]{:S(2)}, u32[]{:S(2)}) collective-permute-start(bf16[2,2,128,2,256]{4,2,3,1,0:T(8,128)(2,1)} %pad_maximum_fusion.24), channel_id=1, source_target_pairs={{0,8},{4,12},{8,16},{12,20},{16,24},{20,28},{1,9},{5,13},{9,17},{1... | collective-permute-start | bytes 1572872 | tf_op jit(solution)/shard_map/ppermute | solution.py:197
  249.2 73.3 %collective-permute-start.9 = (bf16[2,2,128,2,256]{4,2,3,1,0:T(8,128)(2,1)}, bf16[2,2,128,2,256]{4,2,3,1,0:T(8,128)(2,1)}, u32[]{:S(2)}, u32[]{:S(2)}) collective-permute-start(bf16[2,2,128,2,256]{4,2,3,1,0:T(8,128)(2,1)} %pad_maximum_fusion.24), channel_id=1, source_target_pairs={{0,16},{4,20},{8,24},{12,28},{1,17},{5,21},{9,25},{13,29},{2,18},{... | collective-permute-start | bytes 1572872 | tf_op jit(solution)/shard_map/ppermute | solution.py:197
  292.6 35.7 %collective-permute-start.10 = (bf16[2,2,128,2,256]{4,2,3,1,0:T(8,128)(2,1)}, bf16[2,2,128,2,256]{4,2,3,1,0:T(8,128)(2,1)}, u32[]{:S(2)}, u32[]{:S(2)}) collective-permute-start(bf16[2,2,128,2,256]{4,2,3,1,0:T(8,128)(2,1)} %pad_maximum_fusion.24), channel_id=1, source_target_pairs={{0,12},{4,16},{8,20},{12,24},{16,28},{1,13},{5,17},{9,21},{13,25},... | collective-permute-start | bytes 1572872 | tf_op jit(solution)/shard_map/ppermute | solution.py:197
  319.6 45.0 %collective-permute-start.19 = (bf16[512,2048]{1,0:T(8,128)(2,1)}, bf16[512,2048]{1,0:T(8,128)(2,1)}, u32[]{:S(2)}, u32[]{:S(2)}) collective-permute-start(bf16[512,2048]{1,0:T(8,128)(2,1)} %collective-permute-done.17), channel_id=1, source_target_pairs={{0,1},{1,0},{2,3},{3,2},{4,5},{5,4},{6,7},{7,6},{8,9},{9,8},{10,11... | collective-permute-start | bytes 6291464 | tf_op jit(solution)/shard_map/ppermute | solution.py:73
  328.4 27.3 %collective-permute-start.14 = (bf16[2,2,128,2,256]{4,2,3,1,0:T(8,128)(2,1)}, bf16[2,2,128,2,256]{4,2,3,1,0:T(8,128)(2,1)S(1)}, u32[]{:S(2)}, u32[]{:S(2)}) collective-permute-start(bf16[2,2,128,2,256]{4,2,3,1,0:T(8,128)(2,1)} %pad_maximum_fusion.24), channel_id=1, source_target_pairs={{8,0},{12,4},{16,8},{20,12},{24,16},{28,20},{9,1},{13,5},{17,9},{2... | collective-permute-start | bytes 1572872 | tf_op jit(solution)/shard_map/ppermute | solution.py:197
  338.6 54.4 %collective-permute-start.23 = (bf16[512,2048]{1,0:T(8,128)(2,1)}, bf16[512,2048]{1,0:T(8,128)(2,1)}, u32[]{:S(2)}, u32[]{:S(2)}) collective-permute-start(bf16[512,2048]{1,0:T(8,128)(2,1)} %constant_dynamic-update-slice_fusion.19), channel_id=1, source_target_pairs={{0,1},{1,0},{2,3},{3,2},{4,5},{5,4},{6,7},{7,6},{8,9},{9,8},{10,11... | collective-permute-start | bytes 6291464 | tf_op jit(solution)/shard_map/ppermute | solution.py:73
  357.6 33.1 %collective-permute-start.24 = (bf16[512,2048]{1,0:T(8,128)(2,1)}, bf16[512,2048]{1,0:T(8,128)(2,1)}, u32[]{:S(2)}, u32[]{:S(2)}) collective-permute-start(bf16[512,2048]{1,0:T(8,128)(2,1)} %collective-permute-done.22), channel_id=1, source_target_pairs={{0,1},{1,0},{2,3},{3,2},{4,5},{5,4},{6,7},{7,6},{8,9},{9,8},{10,11... | collective-permute-start | bytes 6291464 | tf_op jit(solution)/shard_map/ppermute | solution.py:73
  407.1 42.9 %collective-permute-start.34 = (bf16[256,2048]{0,1:T(8,128)(2,1)}, bf16[256,2048]{0,1:T(8,128)(2,1)S(1)}, u32[]{:S(2)}, u32[]{:S(2)}) collective-permute-start(bf16[256,2048]{0,1:T(8,128)(2,1)} %multiply_convert_fusion.8), channel_id=1, source_target_pairs={{0,4},{4,0},{1,5},{5,1},{2,6},{6,2},{3,7},{7,3},{8,12},{12,8},{9,1... | collective-permute-start | bytes 3145736 | tf_op jit(solution)/shard_map/ppermute | solution.py:73
  466.1 56.6 %collective-permute-start.30 = (bf16[256,2048]{0,1:T(8,128)(2,1)}, bf16[256,2048]{0,1:T(8,128)(2,1)}, u32[]{:S(2)}, u32[]{:S(2)}) collective-permute-start(bf16[256,2048]{0,1:T(8,128)(2,1)} %slice.679), channel_id=1, source_target_pairs={{0,1},{1,0},{2,3},{3,2},{4,5},{5,4},{6,7},{7,6},{8,9},{9,8},{10,11... | collective-permute-start | bytes 3145736 | tf_op jit(solution)/shard_map/ppermute | solution.py:73
  609.1 111.0 %collective-permute-start.46 = (bf16[256,2048]{0,1:T(8,128)(2,1)S(1)}, bf16[256,2048]{0,1:T(8,128)(2,1)}, u32[]{:S(2)}, u32[]{:S(2)}) collective-permute-start(bf16[256,2048]{0,1:T(8,128)(2,1)S(1)} %slice.697), channel_id=1, source_target_pairs={{0,1},{1,0},{2,3},{3,2},{4,5},{5,4},{6,7},{7,6},{8,9},{9,8},{10,11... | collective-permute-start | bytes 3145736 | tf_op jit(solution)/shard_map/ppermute | solution.py:73
  614.7 28.6 %collective-permute-start.53 = (bf16[256,2048]{0,1:T(8,128)(2,1)S(1)}, bf16[256,2048]{0,1:T(8,128)(2,1)S(1)}, u32[]{:S(2)}, u32[]{:S(2)}) collective-permute-start(bf16[256,2048]{0,1:T(8,128)(2,1)S(1)} %pad_maximum_fusion.14), channel_id=1, source_target_pairs={{0,1},{1,0},{2,3},{3,2},{4,5},{5,4},{6,7},{7,6},{8,9},{9,8},{10,11... | collective-permute-start | bytes 3145736 | tf_op jit(solution)/shard_map/ppermute | solution.py:73
  625.1 57.5 %collective-permute-start.58 = (bf16[256,2048]{0,1:T(8,128)(2,1)S(1)}, bf16[256,2048]{0,1:T(8,128)(2,1)}, u32[]{:S(2)}, u32[]{:S(2)}) collective-permute-start(bf16[256,2048]{0,1:T(8,128)(2,1)S(1)} %slice.708), channel_id=1, source_target_pairs={{0,1},{1,0},{2,3},{3,2},{4,5},{5,4},{6,7},{7,6},{8,9},{9,8},{10,11... | collective-permute-start | bytes 3145736 | tf_op jit(solution)/shard_map/ppermute | solution.py:73
  636.4 49.5 %collective-permute-start.49 = (bf16[256,2048]{0,1:T(8,128)(2,1)S(1)}, bf16[256,2048]{0,1:T(8,128)(2,1)}, u32[]{:S(2)}, u32[]{:S(2)}) collective-permute-start(bf16[256,2048]{0,1:T(8,128)(2,1)S(1)} %slice.699), channel_id=1, source_target_pairs={{0,1},{1,0},{2,3},{3,2},{4,5},{5,4},{6,7},{7,6},{8,9},{9,8},{10,11... | collective-permute-start | bytes 3145736 | tf_op jit(solution)/shard_map/ppermute | solution.py:73
  754.8 79.6 %collective-permute-start.92 = (f32[5,2048]{1,0:T(8,128)}, f32[5,2048]{1,0:T(8,128)}, u32[]{:S(2)}, u32[]{:S(2)}) collective-permute-start(f32[5,2048]{1,0:T(8,128)} %reshape.649), channel_id=1, source_target_pairs={{0,1},{1,0},{2,3},{3,2},{4,5},{5,4},{6,7},{7,6},{8,9},{9,8},{10,11... | collective-permute-start | bytes 122888 | tf_op jit(solution)/shard_map/ppermute | solution.py:73
  789.9 115.2 %collective-permute-start.61 = (bf16[2,2,128,2,256]{4,2,3,1,0:T(8,128)(2,1)S(1)}, bf16[2,2,128,2,256]{4,2,3,1,0:T(8,128)(2,1)S(1)}, u32[]{:S(2)}, u32[]{:S(2)}) collective-permute-start(bf16[2,2,128,2,256]{4,2,3,1,0:T(8,128)(2,1)S(1)} %get-tuple-element.279), channel_id=1, source_target_pairs={{16,0},{20,4},{24,8},{28,12},{17,1},{21,5},{25,9},{29,13},{18,2},{... | collective-permute-start | bytes 1572872 | tf_op jit(solution)/shard_map/ppermute | solution.py:197
  791.4 116.7 %collective-permute-start.66 = (bf16[2,2,128,2,256]{4,2,3,1,0:T(8,128)(2,1)S(1)}, bf16[2,2,128,2,256]{4,2,3,1,0:T(8,128)(2,1)S(1)}, u32[]{:S(2)}, u32[]{:S(2)}) collective-permute-start(bf16[2,2,128,2,256]{4,2,3,1,0:T(8,128)(2,1)S(1)} %get-tuple-element.280), channel_id=1, source_target_pairs={{0,8},{4,12},{8,16},{12,20},{16,24},{20,28},{1,9},{5,13},{9,17},{1... | collective-permute-start | bytes 1572872 | tf_op jit(solution)/shard_map/ppermute | solution.py:197
  794.5 113.6 %collective-permute-start.65 = (bf16[2,2,128,2,256]{4,2,3,1,0:T(8,128)(2,1)S(1)}, bf16[2,2,128,2,256]{4,2,3,1,0:T(8,128)(2,1)S(1)}, u32[]{:S(2)}, u32[]{:S(2)}) collective-permute-start(bf16[2,2,128,2,256]{4,2,3,1,0:T(8,128)(2,1)S(1)} %get-tuple-element.281), channel_id=1, source_target_pairs={{0,4},{4,8},{8,12},{12,16},{16,20},{20,24},{24,28},{1,5},{5,9},{9,... | collective-permute-start | bytes 1572872 | tf_op jit(solution)/shard_map/ppermute | solution.py:197
  845.1 52.9 %collective-permute-start.95 = (f32[5,2048]{1,0:T(8,128)S(1)}, f32[5,2048]{1,0:T(8,128)S(1)}, u32[]{:S(2)}, u32[]{:S(2)}) collective-permute-start(f32[5,2048]{1,0:T(8,128)S(1)} %add.576), channel_id=1, source_target_pairs={{0,8},{8,0},{1,9},{9,1},{2,10},{10,2},{3,11},{11,3},{4,12},{12,4},... | collective-permute-start | bytes 122888 | tf_op jit(solution)/shard_map/ppermute | solution.py:73
  908.1 94.9 %collective-permute-start.82 = (bf16[1024,576]{0,1:T(8,128)(2,1)}, bf16[1024,576]{0,1:T(8,128)(2,1)}, u32[]{:S(2)}, u32[]{:S(2)}) collective-permute-start(bf16[1024,576]{0,1:T(8,128)(2,1)} %pad_maximum_fusion.7), channel_id=1, source_target_pairs={{0,1},{1,0},{2,3},{3,2},{4,5},{5,4},{6,7},{7,6},{8,9},{9,8},{10,11... | collective-permute-start | bytes 3538952 | tf_op jit(solution)/shard_map/ppermute | solution.py:73
  908.1 135.7 %collective-permute-start.77 = (bf16[1024,2048]{1,0:T(8,128)(2,1)}, bf16[1024,2048]{1,0:T(8,128)(2,1)}, u32[]{:S(2)}, u32[]{:S(2)}) collective-permute-start(bf16[1024,2048]{1,0:T(8,128)(2,1)} %convolution_convert_fusion.2), channel_id=1, source_target_pairs={{0,1},{1,0},{2,3},{3,2},{4,5},{5,4},{6,7},{7,6},{8,9},{9,8},{10,11... | collective-permute-start | bytes 12582920 | tf_op jit(solution)/shard_map/ppermute | solution.py:73
  914.9 136.2 %collective-permute-start.67 = (bf16[1024,2048]{1,0:T(8,128)(2,1)}, bf16[1024,2048]{1,0:T(8,128)(2,1)}, u32[]{:S(2)}, u32[]{:S(2)}) collective-permute-start(bf16[1024,2048]{1,0:T(8,128)(2,1)} %convolution_convert_fusion.3), channel_id=1, source_target_pairs={{0,1},{1,0},{2,3},{3,2},{4,5},{5,4},{6,7},{7,6},{8,9},{9,8},{10,11... | collective-permute-start | bytes 12582920 | tf_op jit(solution)/shard_map/ppermute | solution.py:73
  942.0 64.5 %collective-permute-start.72 = (bf16[1024,1088]{0,1:T(8,128)(2,1)}, bf16[1024,1088]{0,1:T(8,128)(2,1)}, u32[]{:S(2)}, u32[]{:S(2)}) collective-permute-start(bf16[1024,1088]{0,1:T(8,128)(2,1)} %convolution_convert_fusion), channel_id=1, source_target_pairs={{0,1},{1,0},{2,3},{3,2},{4,5},{5,4},{6,7},{7,6},{8,9},{9,8},{10,11... | collective-permute-start | bytes 6684680 | tf_op jit(solution)/shard_map/ppermute | solution.py:73
  961.9 41.0 %collective-permute-start.89 = (f32[2560]{0:T(1024)S(1)}, f32[2560]{0:T(1024)S(1)}, u32[]{:S(2)}, u32[]{:S(2)}) collective-permute-start(f32[2560]{0:T(1024)S(1)} %add.570), channel_id=1, source_target_pairs={{0,4},{4,0},{1,5},{5,1},{2,6},{6,2},{3,7},{7,3},{8,12},{12,8},{9,1... | collective-permute-start | bytes 30728 | tf_op jit(solution)/shard_map/ppermute | solution.py:73
  1009.0 33.9 %collective-permute-start.73 = (bf16[512,1088]{0,1:T(8,128)(2,1)S(1)}, bf16[512,1088]{0,1:T(8,128)(2,1)S(1)}, u32[]{:S(2)}, u32[]{:S(2)}) collective-permute-start(bf16[512,1088]{0,1:T(8,128)(2,1)S(1)} %slice.745), channel_id=1, source_target_pairs={{0,4},{4,0},{1,5},{5,1},{2,6},{6,2},{3,7},{7,3},{8,12},{12,8},{9,1... | collective-permute-start | bytes 3342344 | tf_op jit(solution)/shard_map/ppermute | solution.py:73
  1049.4 65.5 %collective-permute-start.78 = (bf16[512,2048]{1,0:T(8,128)(2,1)S(1)}, bf16[512,2048]{1,0:T(8,128)(2,1)}, u32[]{:S(2)}, u32[]{:S(2)}) collective-permute-start(bf16[512,2048]{1,0:T(8,128)(2,1)S(1)} %slice.757), channel_id=1, source_target_pairs={{0,4},{4,0},{1,5},{5,1},{2,6},{6,2},{3,7},{7,3},{8,12},{12,8},{9,1... | collective-permute-start | bytes 6291464 | tf_op jit(solution)/shard_map/ppermute | solution.py:73
  1057.3 63.5 %collective-permute-start.68 = (bf16[512,2048]{1,0:T(8,128)(2,1)}, bf16[512,2048]{1,0:T(8,128)(2,1)}, u32[]{:S(2)}, u32[]{:S(2)}) collective-permute-start(bf16[512,2048]{1,0:T(8,128)(2,1)} %slice.735), channel_id=1, source_target_pairs={{0,2},{2,0},{1,3},{3,1},{4,6},{6,4},{5,7},{7,5},{8,10},{10,8},{9,1... | collective-permute-start | bytes 6291464 | tf_op jit(solution)/shard_map/ppermute | solution.py:73
  1071.1 108.7 %all-to-all-start.1 = ((bf16[8,192,1024]{2,1,0:T(8,128)(2,1)}), bf16[8,192,1024]{2,1,0:T(8,128)(2,1)}, u32[]{:S(2)}, u32[]{:S(2)}) async-start(bf16[8,192,1024]{2,1,0:T(8,128)(2,1)} %bitcast.422), calls=%async_computation.2 | async-start | bytes 6291456 | tf_op jit(solution)/shard_map/all_to_all | solution.py:405
  1077.5 52.0 %collective-permute-start.76 = (bf16[64,1088]{0,1:T(8,128)(2,1)}, bf16[64,1088]{0,1:T(8,128)(2,1)S(1)}, u32[]{:S(2)}, u32[]{:S(2)}) collective-permute-start(bf16[64,1088]{0,1:T(8,128)(2,1)} %slice.751), channel_id=1, source_target_pairs={{0,16},{16,0},{1,17},{17,1},{2,18},{18,2},{3,19},{19,3},{4,20},{20... | collective-permute-start | bytes 417800 | tf_op jit(solution)/shard_map/ppermute | solution.py:73
  (253 other events, 4055.4 us)
Sparse Core Ops, SparseCore 0:
  88.9 226.4 all-gather.1
  729.2 289.5 reduce-scatter.1

commit v4 on v3

--- a/solution.py
+++ b/solution.py
@@ -71,6 +71,10 @@
 
 def swap(value, axis):
     return lax.ppermute(value, axis, [(0, 1), (1, 0)])
+
+
+def together(*values):
+    return lax.optimization_barrier(values)
 
 
 def split_columns(whole, widths):
@@ -126,6 +130,7 @@
         other = swap(block, axes[-1])
         return [block, other, swap(block, self.c), swap(other, self.c)]
 
+
     def gather(self, block, done, axes):
         held = list(reversed(done))
         block = block.reshape((2,) * len(held) + (-1, block.shape[-1]))
@@ -137,11 +142,13 @@
             block = jnp.where(lax.axis_index(axis) == 1, jnp.flip(block, at), block)
         return block.reshape((-1, block.shape[-1]))
 
-    def spread_sum(self, pairs, order):
+    def spread_begin(self, pairs):
         half = pairs[0][0].shape[1] // 2
         away = jnp.concatenate([product_tn(one[:, half:], two).astype(BF16) for one, two in pairs], axis=1)
         kept = jnp.concatenate([product_tn(one[:, :half], two).astype(BF16) for one, two in pairs], axis=1)
-        total = kept.astype(F32) + swap(away, self.c).astype(F32)
+        return (kept.astype(F32) + swap(away, self.c).astype(F32)).astype(BF16)
+
+    def spread_end(self, total, order):
         for axis in reversed(order):
             half = total.shape[0] // 2
             total = total.astype(BF16)
@@ -153,11 +160,20 @@
             value = value + swap(value, axis)
         return value
 
-    def team_gather(self, own):
+    def team_map(self, own, function):
+        def chunk_of(piece):
+            return jnp.concatenate([piece, swap(piece, self.c)], axis=0)
+
         by_x, by_l = swap(own, self.x), swap(own, self.l)
+        chunks = [chunk_of(own)]
+        results = [function(chunks[0])]
+        by_x, by_l, results = together(by_x, by_l, results)
         half = own.shape[0] // 2
         both = jnp.concatenate([swap(by_x[:half], self.l), swap(by_l[half:], self.x)], axis=0)
-        return [jnp.concatenate([p, swap(p, self.c)], axis=0) for p in (own, by_x, by_l, both)]
+        for piece in (by_x, by_l, both):
+            chunks.append(chunk_of(piece))
+            results.append(function(chunks[-1]))
+        return chunks, results
 
     def team_scatter(self, chunks):
         sums = []
@@ -252,15 +268,21 @@
         output_weight,
         jnp.concatenate([laurel_right, side_gate, side_output], axis=1),
     )
-    blocks = [plan.grow(block, plan.far_seq) for block in blocks]
-    blocks, feed_team = lax.optimization_barrier((blocks, feed_team))
+    first_axes = plan.far_seq + (plan.l,)
+    steps_x, steps_y = plan.order_x[len(first_axes) :], plan.order_y[len(first_axes) :]
+    query_block, kvl_block = [plan.grow(block, first_axes) for block in blocks[:2]]
+    output_block, rest_block = [plan.grow(block, plan.far_seq) for block in blocks[2:]]
+    kvl_block, query_block, output_block, rest_block, feed_team = lax.optimization_barrier(
+        (kvl_block, query_block, output_block, rest_block, feed_team)
+    )
     feed_full = lax.all_gather(feed_team.reshape(-1, hidden_own), plan.far, axis=0, tiled=True)
     feed_full = feed_full.reshape(-1, 3, team_size * local_rows, hidden_own)
-    steps_x, steps_y = plan.order_x[len(plan.far_seq) :], plan.order_y[len(plan.far_seq) :]
-    query_full = plan.gather_pieces(blocks[0], steps_x)
-    kvl_full = plan.gather_pieces(blocks[1], steps_y)
-    output_full = plan.gather_pieces(blocks[2], steps_y)
-    rest_full = plan.gather(blocks[3], plan.far_seq, steps_x + (plan.c,))
+    kvl_full = plan.gather_pieces(kvl_block, steps_y)
+    query_full = plan.gather_pieces(query_block, steps_x)
+    output_block, kvl_full = together(output_block, kvl_full)
+    output_full = plan.gather_pieces(plan.grow(output_block, (plan.l,)), steps_y)
+    rest_block, query_full = together(rest_block, query_full)
+    rest_full = plan.gather(rest_block, plan.far_seq, (plan.l,) + steps_x + (plan.c,))
     right_full, side_gate_full, side_output_full = split_columns(rest_full, rest_widths)
 
     places = jnp.arange(width, dtype=jnp.int32)
@@ -343,16 +365,17 @@
     feed_low = feed_in.astype(BF16)
     feed_full, feed_low = lax.optimization_barrier((feed_full, feed_low))
     gate_full, up_full, down_full = [feed_full[:, at].reshape(width, hidden_own) for at in range(3)]
-    feed_chunks = plan.team_gather(feed_low)
     pulls = []
     hidden_chunks = []
-    feed_parts = []
-    for chunk in feed_chunks:
+
+    def forward_chunk(chunk):
         hidden, pull = jax.vjp(gate_act, product(chunk, gate_full), product(chunk, up_full))
         hidden_low = hidden.astype(BF16)
         pulls.append(pull)
         hidden_chunks.append(hidden_low)
-        feed_parts.append(product_nt(hidden_low, down_full).astype(BF16))
+        return product_nt(hidden_low, down_full).astype(BF16)
+
+    feed_chunks, feed_parts = plan.team_map(feed_low, forward_chunk)
     feed_out = plan.team_scatter(feed_parts)
 
     resid_two, after_pull = jax.vjp(after_feed, resid_one, feed_out, norm_after)
@@ -372,16 +395,20 @@
     d_resid_two = d_resid_two + product_nt(d_side_pre_low, side_gate_full)
     d_resid_one, d_feed_out, grad_norm_after = after_pull(d_resid_two)
 
-    d_out_chunks = plan.team_gather(d_feed_out.astype(BF16))
     d_gate_chunks = []
     d_up_chunks = []
-    d_feed_parts = []
-    for chunk, pull in zip(d_out_chunks, pulls):
-        d_gate, d_up = pull(product(chunk, down_full))
+
+    def backward_chunk(chunk):
+        d_gate, d_up = pulls[len(d_gate_chunks)](product(chunk, down_full))
         d_gate_chunks.append(d_gate.astype(BF16))
         d_up_chunks.append(d_up.astype(BF16))
         part = product_nt(d_gate_chunks[-1], gate_full) + product_nt(d_up_chunks[-1], up_full)
-        d_feed_parts.append(part.astype(BF16))
+        return part.astype(BF16)
+
+    d_out_chunks, d_feed_parts = plan.team_map(d_feed_out.astype(BF16), backward_chunk)
+    d_gate_chunks, d_up_chunks, feed_chunks, d_out_chunks, hidden_chunks, d_feed_parts = together(
+        d_gate_chunks, d_up_chunks, feed_chunks, d_out_chunks, hidden_chunks, d_feed_parts
+    )
     d_feed_in = plan.team_scatter(d_feed_parts)
 
     feed_all = jnp.concatenate(feed_chunks, axis=0)
@@ -397,7 +424,7 @@
         ],
         axis=1,
     )
-    d_feed_in, feed_terms = lax.optimization_barrier((d_feed_in, feed_terms))
+    d_feed_in, feed_terms = together(d_feed_in, feed_terms)
     feed_sum = lax.psum_scatter(
         feed_terms.reshape(-1, hidden_own), plan.far, scatter_dimension=0, tiled=True
     )
@@ -433,18 +460,9 @@
     d_latent_low = product(d_laurel_low, right_full).astype(BF16)
     spread = jnp.concatenate([d_laurel_low, resid_low, d_side_out_low], axis=0)
     spread = product(spread, spread_x).astype(BF16)
-    grad_output = plan.spread_sum([(d_attn_y, attended_low)], plan.order_y)
-    grad_right, grad_side_gate, grad_side_output = split_columns(
-        plan.spread_sum(
-            [
-                (spread[:rows], latent_low),
-                (spread[rows : 2 * rows], d_side_pre_low),
-                (spread[2 * rows :], side_low),
-            ],
-            plan.order_x,
-        ),
-        rest_widths,
-    )
+    output_sum = plan.spread_begin([(d_attn_y, attended_low)])
+    d_attended_low, output_sum = together(d_attended_low, output_sum)
+    grad_output = plan.spread_end(output_sum, plan.order_y)
 
     d_att = d_attended_low.reshape(batch, block, kv_heads, group, head_size)
     d_values_all = jnp.einsum("bkgts,btkgd->bskd", probs_low, d_att, preferred_element_type=F32)
@@ -465,6 +483,8 @@
         (d_query_rot.reshape(batch, block, heads, head_size), d_pair_total[0], d_pair_total[1])
     )
     d_queries_low = d_queries.reshape(rows, -1).astype(BF16)
+    query_sum = plan.spread_begin([(normed_x, d_queries_low)])
+    d_keys, d_values, query_sum = together(d_keys, d_values, query_sum)
     d_kvl_low = jnp.concatenate(
         [
             d_keys.reshape(rows, -1).astype(BF16),
@@ -473,22 +493,43 @@
         ],
         axis=1,
     )
-    grad_query = plan.spread_sum([(normed_x, d_queries_low)], plan.order_x)
-    grad_key, grad_value, grad_left = split_columns(
-        plan.spread_sum([(normed_y, d_kvl_low)], plan.order_y), kvl_widths
+    spread, d_kvl_low = together(spread, d_kvl_low)
+    rest_sum = plan.spread_begin(
+        [
+            (spread[:rows], latent_low),
+            (spread[rows : 2 * rows], d_side_pre_low),
+            (spread[2 * rows :], side_low),
+        ]
+    )
+    kvl_sum = plan.spread_begin([(normed_y, d_kvl_low)])
+    grad_right, grad_side_gate, grad_side_output = split_columns(
+        plan.spread_end(rest_sum, plan.order_x), rest_widths
     )
     d_normed = d_normed + reorder(product_nt_split(d_queries_low, query_full), spread_x)
     d_normed = d_normed + reorder(product_nt_split(d_kvl_low, kvl_full), spread_y)
     d_inputs_norm, grad_norm_input = pre_pull(d_normed)
     grad_tokens = reorder(d_inputs + d_inputs_norm, to_far_team).reshape(batch, block, width)
     grad_side = d_side_in.reshape(batch, block, -1)
-    early = jnp.stack(
-        [grad_norm_attn, grad_norm_laurel, grad_norm_before, grad_norm_after, grad_norm_layer]
-    )
-    early = plan.total(plan.from_far_team(early))
-    late = jnp.concatenate([plan.from_far_team(grad_norm_input[None])[0], grad_norm_query, grad_norm_key])
-    late = plan.total(late)
-    late_parts = split_columns(late, [width, head_size, head_size])
+    norm_grads = jnp.stack(
+        [
+            grad_norm_input,
+            grad_norm_attn,
+            grad_norm_laurel,
+            grad_norm_before,
+            grad_norm_after,
+            grad_norm_layer,
+        ]
+    )
+    gain_grads = jnp.concatenate(
+        [plan.from_far_team(norm_grads).reshape(-1), grad_norm_query, grad_norm_key]
+    )
+    gain_grads, kvl_sum = together(gain_grads, kvl_sum)
+    grad_query = plan.spread_end(query_sum, plan.order_x)
+    grad_key, grad_value, grad_left = split_columns(
+        plan.spread_end(kvl_sum, plan.order_y), kvl_widths
+    )
+    gain_grads = plan.total(gain_grads)
+    gain_parts = split_columns(gain_grads, [width] * 6 + [head_size] * 2)
     return (
         output,
         grad_tokens,
@@ -504,15 +545,7 @@
         grad_down,
         grad_side_gate,
         grad_side_output,
-        late_parts[0],
-        early[0],
-        early[1],
-        early[2],
-        early[3],
-        early[4],
-        late_parts[1],
-        late_parts[2],
-    )
+    ) + tuple(gain_parts)
 
 
 def solution(mesh):

time: 1210 us -> 1360 us (1.12)
  waiting for transfers between devices: 438 us -> 592 us
    ppermute x85 -> x80, waiting for transfers between devices: 326 us -> 484 us  [swap(): return lax.ppermute(value, axis, [(0, 1), (1, 0)])]
    ppermute x12, starting transfers between devices: 87.6 us -> 32.5 us  [passed_along(): lax.ppermute(value, axes, [(source, source + steps) for source in range(i...]
    ppermute x85 -> x80, starting transfers between devices: 131 us -> 182 us  [swap(): return lax.ppermute(value, axis, [(0, 1), (1, 0)])]
    all_to_all x1, waiting for transfers between devices: 30.6 us -> 0.01 us  [body(): lax.all_to_all(feed_local, plan.team, split_axis=0, concat_axis=0, tiled=...]
    ppermute x12, waiting for transfers between devices: 81.2 us -> 108 us  [passed_along(): lax.ppermute(value, axes, [(source, source + steps) for source in range(i...]
    unnamed x458 -> x498, local copies, waits for them, and re-layouts: 79.5 us -> 71.7 us
  transfers between devices with their start and end apart: 101 -> 96, of which waited for: 43 -> 45; matrix products, arithmetic and copies ran while one was open for 37% -> 31% of each run, Pallas kernels for 0% -> 0%
where the time goes in v4:
time: 1360 us
  waiting for transfers between devices  592 us (44%)
  matrix products  272 us (20%)
  starting transfers between devices  225 us (17%)
  local copies, waits for them, and re-layouts  147 us (11%)
  other arithmetic  102 us (8%)
  between operations  18.5 us (1%)
    ppermute x80, waiting for transfers between devices, swap(): return lax.ppermute(value, axis, [(0, 1), (1, 0)])  484 us
    ppermute x80, starting transfers between devices, swap(): return lax.ppermute(value, axis, [(0, 1), (1, 0)])  182 us
    ppermute x12, waiting for transfers between devices, passed_along(): lax.ppermute(value, axes, [(source, source + steps) for source in range(i...  108 us
    dot_general x33, matrix products, product(): return jnp.dot(left, right, preferred_element_type=F32)  106 us
    dot_general x32, matrix products, product_nt(): lax.dot_general(left, right, (((1,), (1,)), ((), ())), preferred_element_...  88.2 us
    unnamed x498, local copies, waits for them, and re-layouts  71.7 us
    dot_general x15, matrix products, product_tn(): lax.dot_general(left, right, (((0,), (0,)), ((), ())), preferred_element_...  58 us
    ppermute x12, starting transfers between devices, passed_along(): lax.ppermute(value, axes, [(source, source + steps) for source in range(i...  32.5 us
  transfers between devices with their start and end apart: 96, of which 45 were waited for; matrix products, arithmetic and copies ran while one was open for 31% of the time, Pallas kernels for 0%

profile of v4, /device:TPU:0, one launch (start us, length us, event | category | flops | bytes accessed | tf_op | source)
XLA Modules:
  0.0 1356.5 jit_solution(4667299260309321259)
XLA Ops:
  14.4 5.4 all-to-all-start
  38.0 22.8 %collective-permute-done = bf16[64,1088]{0,1:T(8,128)(2,1)} collective-permute-done((bf16[64,1088]{0,1:T(8,128)(2,1)}, bf16[64,1088]{0,1:T(8,128)(2,1)}, u32[]{:S(2)}, u32[]{:S(2)}) %collective-permute-start) | collective-permute-done | bytes 139296 | tf_op jit(solution)/shard_map/ppermute | solution.py:73
  62.0 5.6 collective-permute-start.1
  84.2 8.6 collective-permute-done.3
  99.7 10.0 collective-permute-done.6
  118.8 19.6 %collective-permute-done.7 = bf16[512,1088]{0,1:T(8,128)(2,1)} collective-permute-done((bf16[512,1088]{0,1:T(8,128)(2,1)}, bf16[512,1088]{0,1:T(8,128)(2,1)}, u32[]{:S(2)}, u32[]{:S(2)}) %collective-permute-start.7) | collective-permute-done | bytes 1114144 | tf_op jit(solution)/shard_map/ppermute | solution.py:73
  150.5 8.4 collective-permute-done.16
  182.2 53.4 %collective-permute-done.17 = bf16[512,2048]{1,0:T(8,128)(2,1)} collective-permute-done((bf16[512,2048]{1,0:T(8,128)(2,1)}, bf16[512,2048]{1,0:T(8,128)(2,1)}, u32[]{:S(2)}, u32[]{:S(2)}) %collective-permute-start.17) | collective-permute-done | bytes 2097184 | tf_op jit(solution)/shard_map/ppermute | solution.py:73
  235.7 5.1 collective-permute-start.11
  254.1 9.3 collective-permute-done.12
  264.8 9.8 collective-permute-done.13
  282.6 17.1 %collective-permute-done.15 = bf16[2,2,128,2,256]{4,2,3,1,0:T(8,128)(2,1)S(1)} collective-permute-done((bf16[2,2,128,2,256]{4,2,3,1,0:T(8,128)(2,1)}, bf16[2,2,128,2,256]{4,2,3,1,0:T(8,128)(2,1)S(1)}, u32[]{:S(2)}, u32[]{:S(2)}) %collective-permute-start.15) | collective-permute-done | bytes 524320 | tf_op jit(solution)/shard_map/ppermute | solution.py:213
  306.9 104.3 %collective-permute-start.22 = (bf16[512,2048]{1,0:T(8,128)(2,1)}, bf16[512,2048]{1,0:T(8,128)(2,1)}, u32[]{:S(2)}, u32[]{:S(2)}) collective-permute-start(bf16[512,2048]{1,0:T(8,128)(2,1)} %constant_dynamic-update-slice_fusion.17), channel_id=1, source_target_pairs={{0,4},{4,0},{1,5},{5,1},{2,6},{6,2},{3,7},{7,3},{8,12},{12,8},{9,1... | collective-permute-start | bytes 6291464 | tf_op jit(solution)/shard_map/ppermute | solution.py:73
  427.2 6.3 collective-permute-done.25
  437.3 27.0 %collective-permute-done.26 = bf16[2,2,64,576]{3,2,0,1:T(8,128)(2,1)S(1)} collective-permute-done((bf16[2,2,64,576]{3,2,0,1:T(8,128)(2,1)S(1)}, bf16[2,2,64,576]{3,2,0,1:T(8,128)(2,1)S(1)}, u32[]{:S(2)}, u32[]{:S(2)}) %collective-permute-start.26) | collective-permute-done | bytes 294944 | tf_op jit(solution)/shard_map/ppermute | solution.py:73
  469.2 11.4 collective-permute-done.27
  527.8 6.5 fusion.267
  543.4 7.4 collective-permute-done.29
  555.3 10.0 collective-permute-done.35
  599.4 11.3 collective-permute-done.43
  615.7 20.7 %collective-permute-done.44 = bf16[256,2048]{0,1:T(8,128)(2,1)} collective-permute-done((bf16[256,2048]{0,1:T(8,128)(2,1)}, bf16[256,2048]{0,1:T(8,128)(2,1)}, u32[]{:S(2)}, u32[]{:S(2)}) %collective-permute-start.44) | collective-permute-done | bytes 1048608 | tf_op jit(solution)/shard_map/ppermute | solution.py:73
  664.3 7.9 multiply_convert_fusion.3
  677.6 9.3 collective-permute-done.46
  695.8 8.1 collective-permute-done.50
  751.0 11.3 fusion.62
  762.3 14.6 %fusion.65 = bf16[2048,1024]{1,0:T(8,128)(2,1)} fusion(bf16[2048,2048]{0,1:T(8,128)(2,1)} %constant_dynamic-update-slice_fusion.36, bf16[512,1024]{1,0:T(8,128)(2,1)} %copy-done.220, bf16[512,1024]{1,0:T(8,128)(2,1)} %copy-done.219, bf16[512,1024]{1,0:T(8,128)(2,1)} %copy-done.218, bf16[512,1024]{1,0:T(8,128)(2,1)S(1)} %copy-done.217), kind=kOutput, calls=%fused_computation.86 | convolution fusion | flops 8608808960 | bytes 16777216 | tf_op jit(solution)/shard_map/dot_general | solution.py:34
  780.0 11.9 collective-permute-done.59
  796.4 13.8 %fusion.68 = bf16[2048,1024]{1,0:T(8,128)(2,1)} fusion(bf16[512,1024]{1,0:T(8,128)(2,1)} %copy-done.209, bf16[512,1024]{1,0:T(8,128)(2,1)} %copy-done.208, bf16[512,1024]{1,0:T(8,128)(2,1)} %copy-done.207, bf16[512,1024]{1,0:T(8,128)(2,1)} %copy-done.206, bf16[512,2048]{0,1:T(8,128)(2,1)} %copy-done.110, bf16[512,2048]{0,1:T(8,128)(2,1)} %copy-done.98, ...), kind=kOutput, calls=%fused_computation.87 | convolution fusion | flops 8642363392 | bytes 16777216 | tf_op jit(solution)/shard_map/dot_general | solution.py:34
  810.2 9.2 pad_maximum_fusion
  835.2 5.3 fusion.93
  855.8 8.8 fusion.75
  864.6 5.5 add_convert_fusion.1
  872.6 5.2 fusion.35
  883.5 5.6 convolution_bitcast_fusion.1
  932.7 33.9 %collective-permute-done.78 = bf16[512,2048]{1,0:T(8,128)(2,1)S(1)} collective-permute-done((bf16[512,2048]{1,0:T(8,128)(2,1)S(1)}, bf16[512,2048]{1,0:T(8,128)(2,1)S(1)}, u32[]{:S(2)}, u32[]{:S(2)}) %collective-permute-start.78) | collective-permute-done | bytes 2097184 | tf_op jit(solution)/shard_map/ppermute | solution.py:73
  977.5 13.9 %collective-permute-done.63 = bf16[2,2,128,2,256]{4,2,3,1,0:T(8,128)(2,1)S(1)} collective-permute-done((bf16[2,2,128,2,256]{4,2,3,1,0:T(8,128)(2,1)S(1)}, bf16[2,2,128,2,256]{4,2,3,1,0:T(8,128)(2,1)S(1)}, u32[]{:S(2)}, u32[]{:S(2)}) %collective-permute-start.63) | collective-permute-done | bytes 524320 | tf_op jit(solution)/shard_map/ppermute | solution.py:213
  991.5 57.6 %collective-permute-done.62 = bf16[2,2,128,2,256]{4,2,3,1,0:T(8,128)(2,1)S(1)} collective-permute-done((bf16[2,2,128,2,256]{4,2,3,1,0:T(8,128)(2,1)S(1)}, bf16[2,2,128,2,256]{4,2,3,1,0:T(8,128)(2,1)S(1)}, u32[]{:S(2)}, u32[]{:S(2)}) %collective-permute-start.62) | collective-permute-done | bytes 524320 | tf_op jit(solution)/shard_map/ppermute | solution.py:213
  1053.9 15.4 %collective-permute-done.80 = bf16[128,2048]{1,0:T(8,128)(2,1)S(1)} collective-permute-done((bf16[128,2048]{1,0:T(8,128)(2,1)S(1)}, bf16[128,2048]{1,0:T(8,128)(2,1)S(1)}, u32[]{:S(2)}, u32[]{:S(2)}) %collective-permute-start.80) | collective-permute-done | bytes 524320 | tf_op jit(solution)/shard_map/ppermute | solution.py:73
  1069.8 32.8 %collective-permute-done.81 = bf16[64,2048]{1,0:T(8,128)(2,1)S(1)} collective-permute-done((bf16[64,2048]{1,0:T(8,128)(2,1)S(1)}, bf16[64,2048]{1,0:T(8,128)(2,1)S(1)}, u32[]{:S(2)}, u32[]{:S(2)}) %collective-permute-start.81) | collective-permute-done | bytes 262176 | tf_op jit(solution)/shard_map/ppermute | solution.py:73
  1107.5 10.1 collective-permute-start.69
  1140.9 6.3 fusion.8
  1147.4 33.9 %collective-permute-done.83 = bf16[512,576]{0,1:T(8,128)(2,1)} collective-permute-done((bf16[512,576]{0,1:T(8,128)(2,1)}, bf16[512,576]{0,1:T(8,128)(2,1)}, u32[]{:S(2)}, u32[]{:S(2)}) %collective-permute-start.83) | collective-permute-done | bytes 589856 | tf_op jit(solution)/shard_map/ppermute | solution.py:73
  1183.8 8.7 collective-permute-done.84
  1220.9 49.7 %collective-permute-done.89 = f32[12800]{0:T(1024)S(1)} collective-permute-done((f32[12800]{0:T(1024)S(1)}, f32[12800]{0:T(1024)S(1)}, u32[]{:S(2)}, u32[]{:S(2)}) %collective-permute-start.89) | collective-permute-done | bytes 51232 | tf_op jit(solution)/shard_map/ppermute | solution.py:73
  1284.3 8.4 collective-permute-done.70
  1296.7 12.5 collective-permute-done.71
  1311.3 6.8 collective-permute-done.76
  1318.8 10.8 collective-permute-done.72
  (994 shorter events, 540.8 us)
Async XLA Ops:
  14.4 80.6 %all-to-all-start = ((bf16[8,192,1024]{2,1,0:T(8,128)(2,1)}), bf16[8,192,1024]{2,1,0:T(8,128)(2,1)}, u32[]{:S(2)}, u32[]{:S(2)}) async-start(bf16[8,192,1024]{2,1,0:T(8,128)(2,1)} %copy.661), calls=%async_computation | async-start | bytes 6291456 | tf_op jit(solution)/shard_map/all_to_all | solution.py:263
  19.8 505.2 %all-gather.2.cloned.1.call-start = ((), (), s32[]{:S(2)}) async-start(), calls=%async_computation.3 | async-start | bytes 15728640 | tf_op jit(solution)/shard_map/all_gather | solution.py:278
  21.3 39.6 %collective-permute-start = (bf16[64,1088]{0,1:T(8,128)(2,1)}, bf16[64,1088]{0,1:T(8,128)(2,1)}, u32[]{:S(2)}, u32[]{:S(2)}) collective-permute-start(bf16[64,1088]{0,1:T(8,128)(2,1)} %pad_maximum_fusion.27), channel_id=1, source_target_pairs={{0,16},{16,0},{1,17},{17,1},{2,18},{18,2},{3,19},{19,3},{4,20},{20... | collective-permute-start | bytes 417800 | tf_op jit(solution)/shard_map/ppermute | solution.py:73
  24.5 43.1 %collective-permute-start.2 = (bf16[64,2048]{1,0:T(8,128)(2,1)}, bf16[64,2048]{1,0:T(8,128)(2,1)}, u32[]{:S(2)}, u32[]{:S(2)}) collective-permute-start(bf16[64,2048]{1,0:T(8,128)(2,1)} %param.29), channel_id=1, source_target_pairs={{0,16},{16,0},{1,17},{17,1},{2,18},{18,2},{3,19},{19,3},{4,20},{20... | collective-permute-start | bytes 786440 | tf_op jit(solution)/shard_map/ppermute | solution.py:73
  24.6 51.0 %collective-permute-start.4 = (bf16[64,2048]{1,0:T(8,128)(2,1)}, bf16[64,2048]{1,0:T(8,128)(2,1)}, u32[]{:S(2)}, u32[]{:S(2)}) collective-permute-start(bf16[64,2048]{1,0:T(8,128)(2,1)} %param.32), channel_id=1, source_target_pairs={{0,16},{16,0},{1,17},{17,1},{2,18},{18,2},{3,19},{19,3},{4,20},{20... | collective-permute-start | bytes 786440 | tf_op jit(solution)/shard_map/ppermute | solution.py:73
  28.2 45.7 %collective-permute-start.5 = (bf16[64,576]{1,0:T(8,128)(2,1)}, bf16[64,576]{1,0:T(8,128)(2,1)}, u32[]{:S(2)}, u32[]{:S(2)}) collective-permute-start(bf16[64,576]{1,0:T(8,128)(2,1)} %pad_maximum_fusion.30), channel_id=1, source_target_pairs={{0,16},{16,0},{1,17},{17,1},{2,18},{18,2},{3,19},{19,3},{4,20},{20... | collective-permute-start | bytes 221192 | tf_op jit(solution)/shard_map/ppermute | solution.py:73
  110.6 27.8 %collective-permute-start.7 = (bf16[512,1088]{0,1:T(8,128)(2,1)}, bf16[512,1088]{0,1:T(8,128)(2,1)}, u32[]{:S(2)}, u32[]{:S(2)}) collective-permute-start(bf16[512,1088]{0,1:T(8,128)(2,1)} %constant_dynamic-update-slice_fusion.6), channel_id=1, source_target_pairs={{0,4},{4,0},{1,5},{5,1},{2,6},{6,2},{3,7},{7,3},{8,12},{12,8},{9,1... | collective-permute-start | bytes 3342344 | tf_op jit(solution)/shard_map/ppermute | solution.py:73
  117.4 41.5 %collective-permute-start.16 = (bf16[256,2048]{1,0:T(8,128)(2,1)}, bf16[256,2048]{1,0:T(8,128)(2,1)}, u32[]{:S(2)}, u32[]{:S(2)}) collective-permute-start(bf16[256,2048]{1,0:T(8,128)(2,1)} %pad_maximum_fusion.9), channel_id=1, source_target_pairs={{0,4},{4,0},{1,5},{5,1},{2,6},{6,2},{3,7},{7,3},{8,12},{12,8},{9,1... | collective-permute-start | bytes 3145736 | tf_op jit(solution)/shard_map/ppermute | solution.py:73
  118.8 43.8 %collective-permute-start.8 = (bf16[512,1088]{0,1:T(8,128)(2,1)}, bf16[512,1088]{0,1:T(8,128)(2,1)}, u32[]{:S(2)}, u32[]{:S(2)}) collective-permute-start(bf16[512,1088]{0,1:T(8,128)(2,1)} %constant_dynamic-update-slice_fusion.6), channel_id=1, source_target_pairs={{0,1},{1,0},{2,3},{3,2},{4,5},{5,4},{6,7},{7,6},{8,9},{9,8},{10,11... | collective-permute-start | bytes 3342344 | tf_op jit(solution)/shard_map/ppermute | solution.py:73
  143.2 1056.4 %reduce-scatter.2.cloned.1.call-start = ((), (), s32[]{:S(2)}) async-start(), calls=%async_computation.4 | async-start | bytes 15728640 | tf_op jit(solution)/shard_map/reduce_scatter | solution.py:428
  161.2 74.5 %collective-permute-start.17 = (bf16[512,2048]{1,0:T(8,128)(2,1)}, bf16[512,2048]{1,0:T(8,128)(2,1)}, u32[]{:S(2)}, u32[]{:S(2)}) collective-permute-start(bf16[512,2048]{1,0:T(8,128)(2,1)} %constant_dynamic-update-slice_fusion.15), channel_id=1, source_target_pairs={{0,2},{2,0},{1,3},{3,1},{4,6},{6,4},{5,7},{7,5},{8,10},{10,8},{9,1... | collective-permute-start | bytes 6291464 | tf_op jit(solution)/shard_map/ppermute | solution.py:73
  176.3 64.5 %collective-permute-start.10 = (bf16[2,2,128,2,256]{4,2,3,1,0:T(8,128)(2,1)}, bf16[2,2,128,2,256]{4,2,3,1,0:T(8,128)(2,1)S(1)}, u32[]{:S(2)}, u32[]{:S(2)}) collective-permute-start(bf16[2,2,128,2,256]{4,2,3,1,0:T(8,128)(2,1)} %pad_maximum_fusion.25), channel_id=1, source_target_pairs={{0,16},{4,20},{8,24},{12,28},{1,17},{5,21},{9,25},{13,29},{2,18},{... | collective-permute-start | bytes 1572872 | tf_op jit(solution)/shard_map/ppermute | solution.py:213
  180.9 68.2 %collective-permute-start.20 = (bf16[128,2048]{1,0:T(8,128)(2,1)S(1)}, bf16[128,2048]{1,0:T(8,128)(2,1)S(1)}, u32[]{:S(2)}, u32[]{:S(2)}) collective-permute-start(bf16[128,2048]{1,0:T(8,128)(2,1)S(1)} %copy-done.57), channel_id=1, source_target_pairs={{0,8},{8,0},{1,9},{9,1},{2,10},{10,2},{3,11},{11,3},{4,12},{12,4},... | collective-permute-start | bytes 1572872 | tf_op jit(solution)/shard_map/ppermute | solution.py:73
  182.1 229.1 %collective-permute-start.18 = (bf16[512,2048]{1,0:T(8,128)(2,1)}, bf16[512,2048]{1,0:T(8,128)(2,1)}, u32[]{:S(2)}, u32[]{:S(2)}) collective-permute-start(bf16[512,2048]{1,0:T(8,128)(2,1)} %constant_dynamic-update-slice_fusion.15), channel_id=1, source_target_pairs={{0,1},{1,0},{2,3},{3,2},{4,5},{5,4},{6,7},{7,6},{8,9},{9,8},{10,11... | collective-permute-start | bytes 6291464 | tf_op jit(solution)/shard_map/ppermute | solution.py:73
  235.7 175.5 %collective-permute-start.19 = (bf16[512,2048]{1,0:T(8,128)(2,1)}, bf16[512,2048]{1,0:T(8,128)(2,1)}, u32[]{:S(2)}, u32[]{:S(2)}) collective-permute-start(bf16[512,2048]{1,0:T(8,128)(2,1)} %collective-permute-done.17), channel_id=1, source_target_pairs={{0,1},{1,0},{2,3},{3,2},{4,5},{5,4},{6,7},{7,6},{8,9},{9,8},{10,11... | collective-permute-start | bytes 6291464 | tf_op jit(solution)/shard_map/ppermute | solution.py:73
  252.6 29.2 %collective-permute-start.14 = (bf16[2,2,128,2,256]{4,2,3,1,0:T(8,128)(2,1)}, bf16[2,2,128,2,256]{4,2,3,1,0:T(8,128)(2,1)S(1)}, u32[]{:S(2)}, u32[]{:S(2)}) collective-permute-start(bf16[2,2,128,2,256]{4,2,3,1,0:T(8,128)(2,1)} %pad_maximum_fusion.25), channel_id=1, source_target_pairs={{4,0},{8,4},{12,8},{16,12},{20,16},{24,20},{28,24},{5,1},{9,5},{13... | collective-permute-start | bytes 1572872 | tf_op jit(solution)/shard_map/ppermute | solution.py:213
  263.4 42.5 %collective-permute-start.21 = (bf16[256,2048]{1,0:T(8,128)(2,1)S(1)}, bf16[256,2048]{1,0:T(8,128)(2,1)S(1)}, u32[]{:S(2)}, u32[]{:S(2)}) collective-permute-start(bf16[256,2048]{1,0:T(8,128)(2,1)S(1)} %pad_maximum_fusion.11), channel_id=1, source_target_pairs={{0,2},{2,0},{1,3},{3,1},{4,6},{6,4},{5,7},{7,5},{8,10},{10,8},{9,1... | collective-permute-start | bytes 3145736 | tf_op jit(solution)/shard_map/ppermute | solution.py:73
  306.9 184.9 %collective-permute-start.22 = (bf16[512,2048]{1,0:T(8,128)(2,1)}, bf16[512,2048]{1,0:T(8,128)(2,1)}, u32[]{:S(2)}, u32[]{:S(2)}) collective-permute-start(bf16[512,2048]{1,0:T(8,128)(2,1)} %constant_dynamic-update-slice_fusion.17), channel_id=1, source_target_pairs={{0,4},{4,0},{1,5},{5,1},{2,6},{6,2},{3,7},{7,3},{8,12},{12,8},{9,1... | collective-permute-start | bytes 6291464 | tf_op jit(solution)/shard_map/ppermute | solution.py:73
  411.2 84.2 %collective-permute-start.23 = (bf16[512,2048]{1,0:T(8,128)(2,1)}, bf16[512,2048]{1,0:T(8,128)(2,1)}, u32[]{:S(2)}, u32[]{:S(2)}) collective-permute-start(bf16[512,2048]{1,0:T(8,128)(2,1)} %constant_dynamic-update-slice_fusion.17), channel_id=1, source_target_pairs={{0,1},{1,0},{2,3},{3,2},{4,5},{5,4},{6,7},{7,6},{8,9},{9,8},{10,11... | collective-permute-start | bytes 6291464 | tf_op jit(solution)/shard_map/ppermute | solution.py:73
  434.5 29.8 %collective-permute-start.26 = (bf16[2,2,64,576]{3,2,0,1:T(8,128)(2,1)S(1)}, bf16[2,2,64,576]{3,2,0,1:T(8,128)(2,1)S(1)}, u32[]{:S(2)}, u32[]{:S(2)}) collective-permute-start(bf16[2,2,64,576]{3,2,0,1:T(8,128)(2,1)S(1)} %get-tuple-element.436), channel_id=1, source_target_pairs={{0,4},{4,0},{1,5},{5,1},{2,6},{6,2},{3,7},{7,3},{8,12},{12,8},{9,1... | collective-permute-start | bytes 884744 | tf_op jit(solution)/shard_map/ppermute | solution.py:73
  525.0 25.8 %collective-permute-start.29 = (bf16[256,2048]{0,1:T(8,128)(2,1)}, bf16[256,2048]{0,1:T(8,128)(2,1)S(1)}, u32[]{:S(2)}, u32[]{:S(2)}) collective-permute-start(bf16[256,2048]{0,1:T(8,128)(2,1)} %multiply_convert_fusion.8), channel_id=1, source_target_pairs={{0,4},{4,0},{1,5},{5,1},{2,6},{6,2},{3,7},{7,3},{8,12},{12,8},{9,1... | collective-permute-start | bytes 3145736 | tf_op jit(solution)/shard_map/ppermute | solution.py:73
  526.4 25.5 %collective-permute-start.30 = (bf16[256,2048]{0,1:T(8,128)(2,1)}, bf16[256,2048]{0,1:T(8,128)(2,1)S(1)}, u32[]{:S(2)}, u32[]{:S(2)}) collective-permute-start(bf16[256,2048]{0,1:T(8,128)(2,1)} %multiply_convert_fusion.8), channel_id=1, source_target_pairs={{0,8},{8,0},{1,9},{9,1},{2,10},{10,2},{3,11},{11,3},{4,12},{12,4},... | collective-permute-start | bytes 3145736 | tf_op jit(solution)/shard_map/ppermute | solution.py:73
  555.2 60.5 %collective-permute-start.32 = (bf16[256,2048]{0,1:T(8,128)(2,1)}, bf16[256,2048]{0,1:T(8,128)(2,1)}, u32[]{:S(2)}, u32[]{:S(2)}) collective-permute-start(bf16[256,2048]{0,1:T(8,128)(2,1)} %slice.524), channel_id=1, source_target_pairs={{0,1},{1,0},{2,3},{3,2},{4,5},{5,4},{6,7},{7,6},{8,9},{9,8},{10,11... | collective-permute-start | bytes 3145736 | tf_op jit(solution)/shard_map/ppermute | solution.py:73
  661.0 25.9 %collective-permute-start.46 = (bf16[256,2048]{0,1:T(8,128)(2,1)}, bf16[256,2048]{0,1:T(8,128)(2,1)}, u32[]{:S(2)}, u32[]{:S(2)}) collective-permute-start(bf16[256,2048]{0,1:T(8,128)(2,1)} %fusion.130), channel_id=1, source_target_pairs={{0,4},{4,0},{1,5},{5,1},{2,6},{6,2},{3,7},{7,3},{8,12},{12,8},{9,1... | collective-permute-start | bytes 3145736 | tf_op jit(solution)/shard_map/ppermute | solution.py:73
  661.6 25.5 %collective-permute-start.47 = (bf16[256,2048]{0,1:T(8,128)(2,1)}, bf16[256,2048]{0,1:T(8,128)(2,1)S(1)}, u32[]{:S(2)}, u32[]{:S(2)}) collective-permute-start(bf16[256,2048]{0,1:T(8,128)(2,1)} %fusion.130), channel_id=1, source_target_pairs={{0,8},{8,0},{1,9},{9,1},{2,10},{10,2},{3,11},{11,3},{4,12},{12,4},... | collective-permute-start | bytes 3145736 | tf_op jit(solution)/shard_map/ppermute | solution.py:73
  739.7 38.2 %collective-permute-start.58 = (bf16[256,2048]{0,1:T(8,128)(2,1)S(1)}, bf16[256,2048]{0,1:T(8,128)(2,1)S(1)}, u32[]{:S(2)}, u32[]{:S(2)}) collective-permute-start(bf16[256,2048]{0,1:T(8,128)(2,1)S(1)} %slice.553), channel_id=1, source_target_pairs={{0,1},{1,0},{2,3},{3,2},{4,5},{5,4},{6,7},{7,6},{8,9},{9,8},{10,11... | collective-permute-start | bytes 3145736 | tf_op jit(solution)/shard_map/ppermute | solution.py:73
  739.9 37.0 %collective-permute-start.55 = (bf16[256,2048]{0,1:T(8,128)(2,1)S(1)}, bf16[256,2048]{0,1:T(8,128)(2,1)S(1)}, u32[]{:S(2)}, u32[]{:S(2)}) collective-permute-start(bf16[256,2048]{0,1:T(8,128)(2,1)S(1)} %slice.549), channel_id=1, source_target_pairs={{0,1},{1,0},{2,3},{3,2},{4,5},{5,4},{6,7},{7,6},{8,9},{9,8},{10,11... | collective-permute-start | bytes 3145736 | tf_op jit(solution)/shard_map/ppermute | solution.py:73
  740.5 37.7 %collective-permute-start.54 = (bf16[256,2048]{0,1:T(8,128)(2,1)S(1)}, bf16[256,2048]{0,1:T(8,128)(2,1)S(1)}, u32[]{:S(2)}, u32[]{:S(2)}) collective-permute-start(bf16[256,2048]{0,1:T(8,128)(2,1)S(1)} %slice.546), channel_id=1, source_target_pairs={{0,1},{1,0},{2,3},{3,2},{4,5},{5,4},{6,7},{7,6},{8,9},{9,8},{10,11... | collective-permute-start | bytes 3145736 | tf_op jit(solution)/shard_map/ppermute | solution.py:73
  741.7 77.7 %collective-permute-start.53 = (bf16[256,2048]{0,1:T(8,128)(2,1)}, bf16[256,2048]{0,1:T(8,128)(2,1)}, u32[]{:S(2)}, u32[]{:S(2)}) collective-permute-start(bf16[256,2048]{0,1:T(8,128)(2,1)} %slice.544), channel_id=1, source_target_pairs={{0,1},{1,0},{2,3},{3,2},{4,5},{5,4},{6,7},{7,6},{8,9},{9,8},{10,11... | collective-permute-start | bytes 3145736 | tf_op jit(solution)/shard_map/ppermute | solution.py:73
  793.1 26.3 %collective-permute-start.60 = (bf16[256,2048]{0,1:T(8,128)(2,1)}, bf16[256,2048]{0,1:T(8,128)(2,1)}, u32[]{:S(2)}, u32[]{:S(2)}) collective-permute-start(bf16[256,2048]{0,1:T(8,128)(2,1)} %pad_maximum_fusion.17), channel_id=1, source_target_pairs={{0,4},{4,0},{1,5},{5,1},{2,6},{6,2},{3,7},{7,3},{8,12},{12,8},{9,1... | collective-permute-start | bytes 3145736 | tf_op jit(solution)/shard_map/ppermute | solution.py:73
  835.2 29.4 %collective-permute-start.61 = (bf16[1024,2048]{1,0:T(8,128)(2,1)}, bf16[1024,2048]{1,0:T(8,128)(2,1)}, u32[]{:S(2)}, u32[]{:S(2)}) collective-permute-start(bf16[1024,2048]{1,0:T(8,128)(2,1)} %convolution_convert_fusion.3), channel_id=1, source_target_pairs={{0,1},{1,0},{2,3},{3,2},{4,5},{5,4},{6,7},{7,6},{8,9},{9,8},{10,11... | collective-permute-start | bytes 12582920 | tf_op jit(solution)/shard_map/ppermute | solution.py:73
  892.6 76.3 %collective-permute-start.67 = (bf16[2,2,128,2,256]{4,2,3,1,0:T(8,128)(2,1)}, bf16[2,2,128,2,256]{4,2,3,1,0:T(8,128)(2,1)}, u32[]{:S(2)}, u32[]{:S(2)}) collective-permute-start(bf16[2,2,128,2,256]{4,2,3,1,0:T(8,128)(2,1)} %get-tuple-element.376), channel_id=1, source_target_pairs={{0,8},{4,12},{8,16},{12,20},{16,24},{20,28},{1,9},{5,13},{9,17},{1... | collective-permute-start | bytes 1572872 | tf_op jit(solution)/shard_map/ppermute | solution.py:213
  897.0 74.3 %collective-permute-start.66 = (bf16[2,2,128,2,256]{4,2,3,1,0:T(8,128)(2,1)}, bf16[2,2,128,2,256]{4,2,3,1,0:T(8,128)(2,1)}, u32[]{:S(2)}, u32[]{:S(2)}) collective-permute-start(bf16[2,2,128,2,256]{4,2,3,1,0:T(8,128)(2,1)} %get-tuple-element.377), channel_id=1, source_target_pairs={{0,4},{4,8},{8,12},{12,16},{16,20},{20,24},{24,28},{1,5},{5,9},{9,... | collective-permute-start | bytes 1572872 | tf_op jit(solution)/shard_map/ppermute | solution.py:213
  899.8 71.6 %collective-permute-start.65 = (bf16[2,2,128,2,256]{4,2,3,1,0:T(8,128)(2,1)}, bf16[2,2,128,2,256]{4,2,3,1,0:T(8,128)(2,1)}, u32[]{:S(2)}, u32[]{:S(2)}) collective-permute-start(bf16[2,2,128,2,256]{4,2,3,1,0:T(8,128)(2,1)} %get-tuple-element.378), channel_id=1, source_target_pairs={{4,0},{8,4},{12,8},{16,12},{20,16},{24,20},{28,24},{5,1},{9,5},{13... | collective-permute-start | bytes 1572872 | tf_op jit(solution)/shard_map/ppermute | solution.py:213
  901.1 76.4 %collective-permute-start.64 = (bf16[2,2,128,2,256]{4,2,3,1,0:T(8,128)(2,1)}, bf16[2,2,128,2,256]{4,2,3,1,0:T(8,128)(2,1)}, u32[]{:S(2)}, u32[]{:S(2)}) collective-permute-start(bf16[2,2,128,2,256]{4,2,3,1,0:T(8,128)(2,1)} %get-tuple-element.379), channel_id=1, source_target_pairs={{8,0},{12,4},{16,8},{20,12},{24,16},{28,20},{9,1},{13,5},{17,9},{2... | collective-permute-start | bytes 1572872 | tf_op jit(solution)/shard_map/ppermute | solution.py:213
  917.3 49.4 %collective-permute-start.78 = (bf16[512,2048]{1,0:T(8,128)(2,1)S(1)}, bf16[512,2048]{1,0:T(8,128)(2,1)S(1)}, u32[]{:S(2)}, u32[]{:S(2)}) collective-permute-start(bf16[512,2048]{1,0:T(8,128)(2,1)S(1)} %slice.601), channel_id=1, source_target_pairs={{0,4},{4,0},{1,5},{5,1},{2,6},{6,2},{3,7},{7,3},{8,12},{12,8},{9,1... | collective-permute-start | bytes 6291464 | tf_op jit(solution)/shard_map/ppermute | solution.py:73
  969.8 79.3 %collective-permute-start.62 = (bf16[2,2,128,2,256]{4,2,3,1,0:T(8,128)(2,1)S(1)}, bf16[2,2,128,2,256]{4,2,3,1,0:T(8,128)(2,1)S(1)}, u32[]{:S(2)}, u32[]{:S(2)}) collective-permute-start(bf16[2,2,128,2,256]{4,2,3,1,0:T(8,128)(2,1)S(1)} %copy-done.94), channel_id=1, source_target_pairs={{16,0},{20,4},{24,8},{28,12},{17,1},{21,5},{25,9},{29,13},{18,2},{... | collective-permute-start | bytes 1572872 | tf_op jit(solution)/shard_map/ppermute | solution.py:213
  971.3 132.1 %collective-permute-start.68 = (bf16[1024,2048]{1,0:T(8,128)(2,1)S(1)}, bf16[1024,2048]{1,0:T(8,128)(2,1)S(1)}, u32[]{:S(2)}, u32[]{:S(2)}) collective-permute-start(bf16[1024,2048]{1,0:T(8,128)(2,1)S(1)} %convolution_convert_fusion.2), channel_id=1, source_target_pairs={{0,1},{1,0},{2,3},{3,2},{4,5},{5,4},{6,7},{7,6},{8,9},{9,8},{10,11... | collective-permute-start | bytes 12582920 | tf_op jit(solution)/shard_map/ppermute | solution.py:73
  971.4 81.0 %collective-permute-start.79 = (bf16[256,2048]{1,0:T(8,128)(2,1)S(1)}, bf16[256,2048]{1,0:T(8,128)(2,1)S(1)}, u32[]{:S(2)}, u32[]{:S(2)}) collective-permute-start(bf16[256,2048]{1,0:T(8,128)(2,1)S(1)} %slice.739), channel_id=1, source_target_pairs={{0,2},{2,0},{1,3},{3,1},{4,6},{6,4},{5,7},{7,5},{8,10},{10,8},{9,1... | collective-permute-start | bytes 3145736 | tf_op jit(solution)/shard_map/ppermute | solution.py:73
  1069.4 33.2 %collective-permute-start.81 = (bf16[64,2048]{1,0:T(8,128)(2,1)S(1)}, bf16[64,2048]{1,0:T(8,128)(2,1)S(1)}, u32[]{:S(2)}, u32[]{:S(2)}) collective-permute-start(bf16[64,2048]{1,0:T(8,128)(2,1)S(1)} %slice.743), channel_id=1, source_target_pairs={{0,16},{16,0},{1,17},{17,1},{2,18},{18,2},{3,19},{19,3},{4,20},{20... | collective-permute-start | bytes 786440 | tf_op jit(solution)/shard_map/ppermute | solution.py:73
  1107.5 106.0 %collective-permute-start.69 = (bf16[512,2048]{1,0:T(8,128)(2,1)}, bf16[512,2048]{1,0:T(8,128)(2,1)}, u32[]{:S(2)}, u32[]{:S(2)}) collective-permute-start(bf16[512,2048]{1,0:T(8,128)(2,1)} %slice.581), channel_id=1, source_target_pairs={{0,2},{2,0},{1,3},{3,1},{4,6},{6,4},{5,7},{7,5},{8,10},{10,8},{9,1... | collective-permute-start | bytes 6291464 | tf_op jit(solution)/shard_map/ppermute | solution.py:73
  1118.4 75.9 %collective-permute-start.73 = (bf16[1024,1088]{0,1:T(8,128)(2,1)S(1)}, bf16[1024,1088]{0,1:T(8,128)(2,1)}, u32[]{:S(2)}, u32[]{:S(2)}) collective-permute-start(bf16[1024,1088]{0,1:T(8,128)(2,1)S(1)} %convolution_convert_fusion), channel_id=1, source_target_pairs={{0,1},{1,0},{2,3},{3,2},{4,5},{5,4},{6,7},{7,6},{8,9},{9,8},{10,11... | collective-permute-start | bytes 6684680 | tf_op jit(solution)/shard_map/ppermute | solution.py:73
  1139.8 41.4 %collective-permute-start.83 = (bf16[512,576]{0,1:T(8,128)(2,1)}, bf16[512,576]{0,1:T(8,128)(2,1)}, u32[]{:S(2)}, u32[]{:S(2)}) collective-permute-start(bf16[512,576]{0,1:T(8,128)(2,1)} %slice.746), channel_id=1, source_target_pairs={{0,2},{2,0},{1,3},{3,1},{4,6},{6,4},{5,7},{7,5},{8,10},{10,8},{9,1... | collective-permute-start | bytes 1769480 | tf_op jit(solution)/shard_map/ppermute | solution.py:73
  1203.7 132.9 %all-to-all-start.1 = ((bf16[8,192,1024]{2,1,0:T(8,128)(2,1)}), bf16[8,192,1024]{2,1,0:T(8,128)(2,1)}, u32[]{:S(2)}, u32[]{:S(2)}) async-start(bf16[8,192,1024]{2,1,0:T(8,128)(2,1)} %bitcast.403), calls=%async_computation.2 | async-start | bytes 6291456 | tf_op jit(solution)/shard_map/all_to_all | solution.py:432
  1208.5 63.7 %collective-permute-start.86 = (bf16[64,576]{0,1:T(8,128)(2,1)S(1)}, bf16[64,576]{0,1:T(8,128)(2,1)S(1)}, u32[]{:S(2)}, u32[]{:S(2)}) collective-permute-start(bf16[64,576]{0,1:T(8,128)(2,1)S(1)} %slice.752), channel_id=1, source_target_pairs={{0,16},{16,0},{1,17},{17,1},{2,18},{18,2},{3,19},{19,3},{4,20},{20... | collective-permute-start | bytes 221192 | tf_op jit(solution)/shard_map/ppermute | solution.py:73
  1211.4 69.1 %collective-permute-start.74 = (bf16[512,1088]{0,1:T(8,128)(2,1)}, bf16[512,1088]{0,1:T(8,128)(2,1)}, u32[]{:S(2)}, u32[]{:S(2)}) collective-permute-start(bf16[512,1088]{0,1:T(8,128)(2,1)} %slice.591), channel_id=1, source_target_pairs={{0,4},{4,0},{1,5},{5,1},{2,6},{6,2},{3,7},{7,3},{8,12},{12,8},{9,1... | collective-permute-start | bytes 3342344 | tf_op jit(solution)/shard_map/ppermute | solution.py:73
  1213.4 57.2 %collective-permute-start.89 = (f32[12800]{0:T(1024)S(1)}, f32[12800]{0:T(1024)S(1)}, u32[]{:S(2)}, u32[]{:S(2)}) collective-permute-start(f32[12800]{0:T(1024)S(1)} %add.555), channel_id=1, source_target_pairs={{0,4},{4,0},{1,5},{5,1},{2,6},{6,2},{3,7},{7,3},{8,12},{12,8},{9,1... | collective-permute-start | bytes 153608 | tf_op jit(solution)/shard_map/ppermute | solution.py:73
  1218.9 73.8 %collective-permute-start.70 = (bf16[256,2048]{1,0:T(8,128)(2,1)}, bf16[256,2048]{1,0:T(8,128)(2,1)}, u32[]{:S(2)}, u32[]{:S(2)}) collective-permute-start(bf16[256,2048]{1,0:T(8,128)(2,1)} %slice.723), channel_id=1, source_target_pairs={{0,4},{4,0},{1,5},{5,1},{2,6},{6,2},{3,7},{7,3},{8,12},{12,8},{9,1... | collective-permute-start | bytes 3145736 | tf_op jit(solution)/shard_map/ppermute | solution.py:73
  (269 other events, 4940.2 us)
Sparse Core Ops, SparseCore 0:
  143.3 286.9 all-gather.1
  846.3 296.9 reduce-scatter.1

commit v5 on v4

--- a/solution.py
+++ b/solution.py
@@ -98,49 +98,62 @@
         self.far_dp = self.dp[:-1]
         self.far = self.far_seq + self.far_dp
         self.canon = self.far + self.team
-        self.order_x = self.far_seq + (self.l, self.x) + self.far_dp
-        self.order_y = self.far_seq + (self.l,) + self.far_dp + (self.x,)
+        self.order = self.far_seq + (self.l,) + self.far_dp + (self.x,)
+
+    def flipped(self, value, axes, dims):
+        for axis, dim in zip(axes, dims):
+            value = jnp.where(lax.axis_index(axis) == 1, jnp.flip(value, dim), value)
+        return value
 
     def to_far_team(self, value):
         rows, width = value.shape
         parts = value.reshape((rows,) + (2,) * len(self.every) + (-1,))
+        parts = self.flipped(parts, self.far, [1 + self.every.index(axis) for axis in self.far])
         order = [0] + [1 + self.every.index(axis) for axis in self.canon] + [1 + len(self.every)]
         return parts.transpose(order).reshape(rows, width)
 
     def from_far_team(self, value):
         rows, width = value.shape
         parts = value.reshape((rows,) + (2,) * len(self.every) + (-1,))
+        parts = self.flipped(parts, self.far, [1 + self.canon.index(axis) for axis in self.far])
         order = [0] + [1 + self.canon.index(axis) for axis in self.every] + [1 + len(self.every)]
         return parts.transpose(order).reshape(rows, width)
 
-    def spread_order(self, width, order):
+    def spread_order(self, width):
         own = jnp.arange(width, dtype=jnp.int32).reshape((2,) * len(self.canon) + (-1,))
-        for at, axis in enumerate(self.canon):
-            own = jnp.where(lax.axis_index(axis) == 1, jnp.flip(own, at), own)
-        axes = (self.c,) + tuple(reversed(order))
+        own = self.flipped(own, self.team, [self.canon.index(axis) for axis in self.team])
+        axes = (self.c,) + tuple(reversed(self.order))
         return own.transpose([self.canon.index(axis) for axis in axes] + [len(self.canon)]).reshape(-1)
+
+    def pieces(self, blocks, axes):
+        for axis in axes:
+            blocks = [one for block in blocks for one in (block, swap(block, axis))]
+        return blocks
 
     def grow(self, block, axes):
         for axis in axes:
             block = jnp.concatenate([block, swap(block, axis)], axis=0)
         return block
 
-    def gather_pieces(self, block, axes):
-        block = self.grow(block, axes[:-1])
-        other = swap(block, axes[-1])
+    def gather_pieces(self, block):
+        other = swap(block, self.order[-1])
         return [block, other, swap(block, self.c), swap(other, self.c)]
 
-
-    def gather(self, block, done, axes):
-        held = list(reversed(done))
-        block = block.reshape((2,) * len(held) + (-1, block.shape[-1]))
-        for axis in axes:
-            block = jnp.stack([block, swap(block, axis)], axis=0)
-            held = [axis] + held
-        block = block.transpose([held.index(axis) for axis in self.canon] + [len(held), len(held) + 1])
-        for at, axis in enumerate(self.canon):
-            block = jnp.where(lax.axis_index(axis) == 1, jnp.flip(block, at), block)
-        return block.reshape((-1, block.shape[-1]))
+    def far_team_rows(self, pieces):
+        axes = (self.c,) + tuple(reversed(self.order))
+        whole = jnp.concatenate(pieces, axis=0)
+        whole = whole.reshape((2,) * len(axes) + (-1, whole.shape[-1]))
+        whole = whole.transpose([axes.index(axis) for axis in self.canon] + [len(axes), len(axes) + 1])
+        whole = self.flipped(whole, self.team, [self.canon.index(axis) for axis in self.team])
+        return whole.reshape((-1, whole.shape[-1]))
+
+    def fold(self, pieces, axes):
+        for axis in reversed(axes):
+            pieces = [
+                (kept.astype(F32) + swap(away, axis).astype(F32)).astype(BF16)
+                for kept, away in zip(pieces[::2], pieces[1::2])
+            ]
+        return pieces
 
     def spread_begin(self, pairs):
         half = pairs[0][0].shape[1] // 2
@@ -148,12 +161,56 @@
         kept = jnp.concatenate([product_tn(one[:, :half], two).astype(BF16) for one, two in pairs], axis=1)
         return (kept.astype(F32) + swap(away, self.c).astype(F32)).astype(BF16)
 
-    def spread_end(self, total, order):
-        for axis in reversed(order):
+    def spread_step(self, total, axes):
+        for axis in axes:
             half = total.shape[0] // 2
+            total = total[:half].astype(F32) + swap(total[half:], axis).astype(F32)
+            if axis != self.order[0]:
+                total = total.astype(BF16)
+        return total
+
+    def near_gather(self, key, value):
+        pair = jnp.stack([key, value])[:, None]
+        for axis in reversed(self.far_seq):
+            pair = jnp.concatenate([pair, swap(pair, axis)], axis=1)
+        key, value = pair[0][None], pair[1][None]
+        key = jnp.concatenate([key, swap(key, self.x)], axis=0)
+        key = jnp.stack([key, swap(key, self.l)], axis=0)
+        value = jnp.concatenate([value, swap(value, self.l)], axis=0)
+        value = jnp.stack([value, swap(value, self.x)], axis=1)
+        return [one.reshape((-1,) + one.shape[3:]) for one in (key, value)]
+
+    def near_sum(self, key, value):
+        def step(total, dim, axis):
             total = total.astype(BF16)
-            total = total[:half].astype(F32) + swap(total[half:], axis).astype(F32)
-        return total
+            away = swap(lax.index_in_dim(total, 1, dim, False), axis).astype(F32)
+            return lax.index_in_dim(total, 0, dim, False).astype(F32) + away
+
+        shape = (2, 2) + (2,) * len(self.far_seq)
+        key, value = [one.reshape(shape + one.shape[1:]) for one in (key, value)]
+        key = step(step(key, 0, self.l), 0, self.x)
+        value = step(step(value, 1, self.x), 0, self.l)
+        pair = jnp.stack([key, value])
+        for axis in self.far_seq:
+            pair = step(pair, 1, axis)
+        return pair
+
+    def near_places(self):
+        place = jnp.zeros((1,), jnp.int32)
+        for axis in (self.l, self.x) + self.far_seq:
+            bit = lax.axis_index(axis)
+            weight = 2 ** (len(self.seq) - 1 - self.seq.index(axis))
+            place = (place[:, None] + weight * jnp.stack([bit, 1 - bit])[None, :]).reshape(-1)
+        return place
+
+    def own_rows(self, sums, local_rows):
+        size = 2 ** len(self.team)
+        sums = jnp.concatenate([one.reshape(size, local_rows, -1) for one in sums], axis=1)
+        moved = lax.all_to_all(sums, self.team, split_axis=0, concat_axis=0, tiled=True)
+        return [
+            jnp.concatenate([moved[at, first : first + local_rows] for at in range(size)], axis=1).astype(F32)
+            for first in range(0, moved.shape[1], local_rows)
+        ]
 
     def total(self, value):
         for axis in reversed(self.every):
@@ -261,35 +318,37 @@
         axis=1,
     )
     feed_team = lax.all_to_all(feed_local, plan.team, split_axis=0, concat_axis=0, tiled=True)
-    feed_team = feed_team.reshape(team_size, 3, local_rows, hidden_own).transpose(1, 0, 2, 3)
-    blocks = (
-        query_weight,
-        jnp.concatenate([key_weight, value_weight, laurel_left], axis=1),
-        output_weight,
-        jnp.concatenate([laurel_right, side_gate, side_output], axis=1),
-    )
-    first_axes = plan.far_seq + (plan.l,)
-    steps_x, steps_y = plan.order_x[len(first_axes) :], plan.order_y[len(first_axes) :]
-    query_block, kvl_block = [plan.grow(block, first_axes) for block in blocks[:2]]
-    output_block, rest_block = [plan.grow(block, plan.far_seq) for block in blocks[2:]]
-    kvl_block, query_block, output_block, rest_block, feed_team = lax.optimization_barrier(
-        (kvl_block, query_block, output_block, rest_block, feed_team)
-    )
-    feed_full = lax.all_gather(feed_team.reshape(-1, hidden_own), plan.far, axis=0, tiled=True)
-    feed_full = feed_full.reshape(-1, 3, team_size * local_rows, hidden_own)
-    kvl_full = plan.gather_pieces(kvl_block, steps_y)
-    query_full = plan.gather_pieces(query_block, steps_x)
-    output_block, kvl_full = together(output_block, kvl_full)
-    output_full = plan.gather_pieces(plan.grow(output_block, (plan.l,)), steps_y)
-    rest_block, query_full = together(rest_block, query_full)
-    rest_full = plan.gather(rest_block, plan.far_seq, (plan.l,) + steps_x + (plan.c,))
-    right_full, side_gate_full, side_output_full = split_columns(rest_full, rest_widths)
+    gate_own, up_own, down_own = [
+        feed_team[:, index * local_rows : (index + 1) * local_rows].reshape(-1, hidden_own)
+        for index in range(3)
+    ]
+    block_widths = [sum(kvl_widths), query_weight.shape[1], output_weight.shape[1] + sum(rest_widths)]
+    attn_block = jnp.concatenate(
+        [key_weight, value_weight, laurel_left, query_weight, output_weight]
+        + [laurel_right, side_gate, side_output],
+        axis=1,
+    )
+    attn_block = plan.grow(attn_block, plan.far_seq)
+    attn_block, gate_own, up_own, down_own = together(attn_block, gate_own, up_own, down_own)
+    attn_block = plan.grow(attn_block, (plan.l,))
+    gate_far = plan.pieces([gate_own], plan.far_seq)
+    gate_first = plan.pieces(gate_far[:1], plan.far_dp)
+    up_first = plan.pieces([up_own], plan.far_dp)
+    attn_block, gate_far, gate_first, up_first = together(attn_block, gate_far, gate_first, up_first)
+    kvl_block, query_block, rest_block = split_columns(attn_block, block_widths)
+    kvl_block = plan.grow(kvl_block, plan.far_dp)
+    query_block = plan.grow(query_block, plan.far_dp)
+    up_far = plan.pieces([up_own], plan.far_seq)
+    kvl_full = plan.gather_pieces(kvl_block)
+    kvl_full, query_block, up_far = together(kvl_full, query_block, up_far)
+    query_full = plan.gather_pieces(query_block)
+    down_far = plan.pieces([down_own], plan.far_seq)
+    rest_block = plan.grow(rest_block, plan.far_dp)
 
     places = jnp.arange(width, dtype=jnp.int32)
     far_team = plan.to_far_team(places[None])[0]
     to_far_team = (places[:, None] == far_team[None, :]).astype(BF16)
-    spread_x = (places[:, None] == plan.spread_order(width, plan.order_x)[None, :]).astype(BF16)
-    spread_y = (places[:, None] == plan.spread_order(width, plan.order_y)[None, :]).astype(BF16)
+    to_spread = (places[:, None] == plan.spread_order(width)[None, :]).astype(BF16)
     gains = jnp.stack([norm_input, norm_attn, norm_laurel, norm_before, norm_after, norm_layer])
     norm_input, norm_attn, norm_laurel, norm_before, norm_after, norm_layer = plan.to_far_team(gains)
     inputs = product(tokens.reshape(rows, width), to_far_team)
@@ -297,10 +356,9 @@
     side_in = per_layer.astype(F32).reshape(rows, -1)
     normed, pre_pull = jax.vjp(rms, inputs, norm_input)
     normed_low = normed.astype(BF16)
-    normed_x = product(normed_low, spread_x).astype(BF16)
-    normed_y = product(normed_low, spread_y).astype(BF16)
-    queries = product_split(normed_x, query_full).reshape(batch, block, heads, head_size)
-    keys, values, latent = split_columns(product_split(normed_y, kvl_full), kvl_widths)
+    normed_spread = product(normed_low, to_spread).astype(BF16)
+    keys, values, latent = split_columns(product_split(normed_spread, kvl_full), kvl_widths)
+    queries = product_split(normed_spread, query_full).reshape(batch, block, heads, head_size)
     keys = keys.reshape(batch, block, kv_heads, head_size)
     values = values.reshape(batch, block, kv_heads, head_size)
     latent_low = latent.astype(BF16)
@@ -316,24 +374,37 @@
         head_prep, queries, keys, values, norm_query, norm_key
     )
     query_low = rot_query.astype(BF16)
-    pair_low = jnp.stack([rot_key.astype(BF16), rot_value.astype(BF16)])
+    key_low = rot_key.astype(BF16)
+    value_low = rot_value.astype(BF16)
     left_count = WINDOW // block
     right_count = (SPAN + block - 2) // block
     offsets = list(range(left_count, 0, -1)) + [0] + list(range(-1, -right_count - 1, -1))
-    gathered = []
-    for offset in offsets:
-        if offset == 0:
-            gathered.append(pair_low)
-        else:
-            gathered.append(passed_along(pair_low, plan.seq, seq_count, offset))
-    pairs_all = jnp.concatenate(gathered, axis=2)
-    keys_all = pairs_all[0]
-    values_all = pairs_all[1]
-    key_count = keys_all.shape[1]
+    whole_sequence = seq_count <= len(offsets) + 1
     seq_index = lax.axis_index(plan.seq)
     total_length = block * seq_count
+    if whole_sequence:
+        keys_all, values_all = [
+            one.swapaxes(0, 1).reshape(batch, total_length, kv_heads, head_size)
+            for one in plan.near_gather(key_low, value_low)
+        ]
+        key_blocks = plan.near_places()
+    else:
+        pair_low = jnp.stack([key_low, value_low])
+        gathered = [
+            passed_along(pair_low, plan.seq, seq_count, offset) if offset else pair_low
+            for offset in offsets
+        ]
+        keys_all, values_all = jnp.concatenate(gathered, axis=2)
+        key_blocks = seq_index - jnp.array(offsets, dtype=jnp.int32)
+    key_count = keys_all.shape[1]
+    keys_all, values_all, query_full, down_far, rest_block = together(
+        keys_all, values_all, query_full, down_far, rest_block
+    )
+    rest_full = plan.gather_pieces(rest_block)
+    gate_last = plan.pieces(gate_far[1:], plan.far_dp)
+    down_first = plan.pieces(down_far[:1], plan.far_dp)
     query_places = seq_index * block + jnp.arange(block, dtype=jnp.int32)
-    key_places = (seq_index - left_count) * block + jnp.arange(key_count, dtype=jnp.int32)
+    key_places = (key_blocks[:, None] * block + jnp.arange(block, dtype=jnp.int32)).reshape(-1)
     in_query = (query_places[None, :, None] >= span_start[:, None, :]) & (
         query_places[None, :, None] < span_start[:, None, :] + SPAN
     )
@@ -356,15 +427,25 @@
     probs_low = probs.astype(BF16)
     attended = jnp.einsum("bkgts,bskd->btkgd", probs_low, values_all, preferred_element_type=F32)
     attended_low = attended.reshape(rows, heads * head_size).astype(BF16)
-    attn_proj = reorder(product_nt_split(attended_low, output_full), spread_y)
+    attended_low, rest_full, gate_last, down_first = together(
+        attended_low, rest_full, gate_last, down_first
+    )
+    up_last = plan.pieces(up_far[1:], plan.far_dp)
+    down_last = plan.pieces(down_far[1:], plan.far_dp)
+    gate_full, up_full, down_full = [
+        jnp.concatenate(first + last, axis=0)
+        for first, last in ((gate_first, gate_last), (up_first, up_last), (down_first, down_last))
+    ]
+    output_full = [one[:, : output_weight.shape[1]] for one in rest_full]
+    rest_full = plan.far_team_rows([one[:, output_weight.shape[1] :] for one in rest_full])
+    right_full, side_gate_full, side_output_full = split_columns(rest_full, rest_widths)
+    attn_proj = reorder(product_nt_split(attended_low, output_full), to_spread)
     laurel = product_nt(latent_low, right_full)
     (resid_one, feed_in), mid_pull = jax.vjp(
         middle, inputs, normed, attn_proj, laurel, norm_attn, norm_laurel, norm_before
     )
 
     feed_low = feed_in.astype(BF16)
-    feed_full, feed_low = lax.optimization_barrier((feed_full, feed_low))
-    gate_full, up_full, down_full = [feed_full[:, at].reshape(width, hidden_own) for at in range(3)]
     pulls = []
     hidden_chunks = []
 
@@ -413,36 +494,21 @@
 
     feed_all = jnp.concatenate(feed_chunks, axis=0)
     d_out_all = jnp.concatenate(d_out_chunks, axis=0)
-    feed_terms = jnp.stack(
-        [
-            product_tn(left, jnp.concatenate(right, axis=0)).astype(BF16).reshape(-1, team_size * local_rows, hidden_own)
-            for left, right in (
-                (feed_all, d_gate_chunks),
-                (feed_all, d_up_chunks),
-                (d_out_all, hidden_chunks),
-            )
-        ],
-        axis=1,
-    )
-    d_feed_in, feed_terms = together(d_feed_in, feed_terms)
-    feed_sum = lax.psum_scatter(
-        feed_terms.reshape(-1, hidden_own), plan.far, scatter_dimension=0, tiled=True
-    )
-    feed_sum = feed_sum.reshape(3, team_size, local_rows, hidden_own).transpose(1, 0, 2, 3)
-    feed_grads = lax.all_to_all(
-        feed_sum.reshape(team_size, 3 * local_rows, hidden_own),
-        plan.team,
-        split_axis=0,
-        concat_axis=0,
-        tiled=True,
-    )
-    grad_gate, grad_up, grad_down = [
-        jnp.concatenate(
-            [feed_grads[at, index * local_rows : (index + 1) * local_rows] for at in range(team_size)],
-            axis=1,
-        ).astype(F32)
-        for index in range(3)
-    ]
+    far_count = 2 ** len(plan.far)
+
+    def far_terms(left, right):
+        right = jnp.concatenate(right, axis=0)
+        part = width // far_count
+        return [
+            product_tn(left[:, at * part : (at + 1) * part], right).astype(BF16)
+            for at in range(far_count)
+        ]
+
+    gate_terms = far_terms(feed_all, d_gate_chunks)
+    up_terms = far_terms(feed_all, d_up_chunks)
+    down_terms = far_terms(d_out_all, hidden_chunks)
+    gate_terms = plan.fold(gate_terms, plan.far_dp)
+    d_feed_in, gate_terms, up_terms, down_terms = together(d_feed_in, gate_terms, up_terms, down_terms)
 
     (
         d_inputs,
@@ -455,14 +521,26 @@
     ) = mid_pull((d_resid_one, d_feed_in))
     d_attn_low = d_attn_proj.astype(BF16)
     d_laurel_low = d_laurel.astype(BF16)
-    d_attn_y = product(d_attn_low, spread_y).astype(BF16)
-    d_attended_low = product_split(d_attn_y, output_full).astype(BF16)
+    d_attn_spread = product(d_attn_low, to_spread).astype(BF16)
+    d_attended_low = product_split(d_attn_spread, output_full).astype(BF16)
     d_latent_low = product(d_laurel_low, right_full).astype(BF16)
     spread = jnp.concatenate([d_laurel_low, resid_low, d_side_out_low], axis=0)
-    spread = product(spread, spread_x).astype(BF16)
-    output_sum = plan.spread_begin([(d_attn_y, attended_low)])
-    d_attended_low, output_sum = together(d_attended_low, output_sum)
-    grad_output = plan.spread_end(output_sum, plan.order_y)
+    spread = product(spread, to_spread).astype(BF16)
+    output_sum = plan.spread_begin(
+        [
+            (d_attn_spread, attended_low),
+            (spread[:rows], latent_low),
+            (spread[rows : 2 * rows], d_side_pre_low),
+            (spread[2 * rows :], side_low),
+        ]
+    )
+    d_attended_low, output_sum, gate_terms, up_terms = together(
+        d_attended_low, output_sum, gate_terms, up_terms
+    )
+    steps = tuple(reversed(plan.order))
+    output_sum = plan.spread_step(output_sum, steps[:1])
+    gate_terms = plan.fold(gate_terms, plan.far_seq)
+    up_terms = plan.fold(up_terms, plan.far_dp)
 
     d_att = d_attended_low.reshape(batch, block, kv_heads, group, head_size)
     d_values_all = jnp.einsum("bkgts,btkgd->bskd", probs_low, d_att, preferred_element_type=F32)
@@ -473,18 +551,38 @@
     d_keys_all = jnp.einsum(
         "bkgts,btkgd->bskd", d_scores_low, query_group, preferred_element_type=F32
     )
-    d_pairs = jnp.stack([d_keys_all, d_values_all])
-    d_pair_total = d_pairs[:, :, left_count * block : (left_count + 1) * block]
-    for position, offset in enumerate(offsets):
-        if offset != 0:
-            piece = d_pairs[:, :, position * block : (position + 1) * block].astype(BF16)
-            d_pair_total = d_pair_total + passed_along(piece, plan.seq, seq_count, -offset).astype(F32)
+    d_keys_all, d_values_all, d_query_rot, gate_terms, up_terms, down_terms = together(
+        d_keys_all, d_values_all, d_query_rot, gate_terms, up_terms, down_terms
+    )
+    up_terms = plan.fold(up_terms, plan.far_seq)
+    down_terms = plan.fold(down_terms, plan.far_dp)
+    if whole_sequence:
+        d_pair_total = plan.near_sum(
+            *[
+                one.reshape(batch, seq_count, block, kv_heads, head_size).swapaxes(0, 1)
+                for one in (d_keys_all, d_values_all)
+            ]
+        )
+    else:
+        d_pairs = jnp.stack([d_keys_all, d_values_all])
+        d_pair_total = d_pairs[:, :, left_count * block : (left_count + 1) * block]
+        for position, offset in enumerate(offsets):
+            if offset != 0:
+                piece = d_pairs[:, :, position * block : (position + 1) * block].astype(BF16)
+                moved = passed_along(piece, plan.seq, seq_count, -offset)
+                d_pair_total = d_pair_total + moved.astype(F32)
     d_queries, d_keys, d_values, grad_norm_query, grad_norm_key = prep_pull(
         (d_query_rot.reshape(batch, block, heads, head_size), d_pair_total[0], d_pair_total[1])
     )
     d_queries_low = d_queries.reshape(rows, -1).astype(BF16)
-    query_sum = plan.spread_begin([(normed_x, d_queries_low)])
-    d_keys, d_values, query_sum = together(d_keys, d_values, query_sum)
+    query_sum = plan.spread_begin([(normed_spread, d_queries_low)])
+    d_keys, d_values, output_sum, query_sum, up_terms, down_terms = together(
+        d_keys, d_values, output_sum, query_sum, up_terms, down_terms
+    )
+    query_sum = plan.spread_step(query_sum, steps[:1])
+    down_terms = plan.fold(down_terms, plan.far_seq)
+    grad_gate, grad_up = plan.own_rows(gate_terms + up_terms, local_rows)
+    (grad_down,) = plan.own_rows(down_terms, local_rows)
     d_kvl_low = jnp.concatenate(
         [
             d_keys.reshape(rows, -1).astype(BF16),
@@ -493,20 +591,9 @@
         ],
         axis=1,
     )
-    spread, d_kvl_low = together(spread, d_kvl_low)
-    rest_sum = plan.spread_begin(
-        [
-            (spread[:rows], latent_low),
-            (spread[rows : 2 * rows], d_side_pre_low),
-            (spread[2 * rows :], side_low),
-        ]
-    )
-    kvl_sum = plan.spread_begin([(normed_y, d_kvl_low)])
-    grad_right, grad_side_gate, grad_side_output = split_columns(
-        plan.spread_end(rest_sum, plan.order_x), rest_widths
-    )
-    d_normed = d_normed + reorder(product_nt_split(d_queries_low, query_full), spread_x)
-    d_normed = d_normed + reorder(product_nt_split(d_kvl_low, kvl_full), spread_y)
+    kvl_sum = plan.spread_begin([(normed_spread, d_kvl_low)])
+    d_spread = product_nt_split(d_queries_low, query_full) + product_nt_split(d_kvl_low, kvl_full)
+    d_normed = d_normed + reorder(d_spread, to_spread)
     d_inputs_norm, grad_norm_input = pre_pull(d_normed)
     grad_tokens = reorder(d_inputs + d_inputs_norm, to_far_team).reshape(batch, block, width)
     grad_side = d_side_in.reshape(batch, block, -1)
@@ -523,11 +610,12 @@
     gain_grads = jnp.concatenate(
         [plan.from_far_team(norm_grads).reshape(-1), grad_norm_query, grad_norm_key]
     )
-    gain_grads, kvl_sum = together(gain_grads, kvl_sum)
-    grad_query = plan.spread_end(query_sum, plan.order_x)
-    grad_key, grad_value, grad_left = split_columns(
-        plan.spread_end(kvl_sum, plan.order_y), kvl_widths
-    )
+    gain_grads, kvl_sum, grad_gate, grad_up = together(gain_grads, kvl_sum, grad_gate, grad_up)
+    grad_query = plan.spread_step(query_sum, steps[1:])
+    grad_output, grad_right, grad_side_gate, grad_side_output = split_columns(
+        plan.spread_step(output_sum, steps[1:]), [output_weight.shape[1]] + rest_widths
+    )
+    grad_key, grad_value, grad_left = split_columns(plan.spread_step(kvl_sum, steps), kvl_widths)
     gain_grads = plan.total(gain_grads)
     gain_parts = split_columns(gain_grads, [width] * 6 + [head_size] * 2)
     return (

time: 1360 us -> 1330 us (0.978)
  starting transfers between devices: 225 us -> 90.9 us
  local copies, waits for them, and re-layouts: 147 us -> 232 us
  other arithmetic: 102 us -> 127 us
    ppermute x80 -> x94, waiting for transfers between devices: 484 us -> 593 us  [swap(): return lax.ppermute(value, axis, [(0, 1), (1, 0)])]
    ppermute x12 -> x0, waiting for transfers between devices: 108 us -> none  [passed_along(): lax.ppermute(value, axes, [(source, source + steps) for source in range(i...]
    ppermute x80 -> x94, starting transfers between devices: 182 us -> 77.4 us  [swap(): return lax.ppermute(value, axis, [(0, 1), (1, 0)])]
    ppermute x12 -> x0, starting transfers between devices: 32.5 us -> none  [passed_along(): lax.ppermute(value, axes, [(source, source + steps) for source in range(i...]
    concatenate x2 -> x13, local copies, waits for them, and re-layouts: 1.91 us -> 34 us  [the longest x2 17.1 us: spread_begin(): jnp.concatenate([product_tn(one[:, half:], two).astype(BF16) for one, two...]
    ppermute x0 -> x6, local copies, waits for them, and re-layouts: none -> 20.2 us  [swap(): return lax.ppermute(value, axis, [(0, 1), (1, 0)])]
    convert_element_type x16 -> x22, other arithmetic: 15.1 us -> 34.9 us  [the longest x7 13.6 us: fold(): (kept.astype(F32) + swap(away, axis).astype(F32)).astype(BF16)]
    dot_general x33 -> x32, matrix products: 106 us -> 89.6 us  [product(): return jnp.dot(left, right, preferred_element_type=F32)]
  transfers between devices with their start and end apart: 96 -> 97, of which waited for: 45 -> 45; matrix products, arithmetic and copies ran while one was open for 31% -> 31% of each run, Pallas kernels for 0% -> 0%
where the time goes in v5:
time: 1330 us; the launch traced here: 1320 us
  waiting for transfers between devices  594 us (45%)
  matrix products  273 us (21%)
  local copies, waits for them, and re-layouts  232 us (17%)
  other arithmetic  127 us (10%)
  starting transfers between devices  90.9 us (7%)
    ppermute x94, waiting for transfers between devices, swap(): return lax.ppermute(value, axis, [(0, 1), (1, 0)])  593 us
    dot_general x31, matrix products, product_nt(): lax.dot_general(left, right, (((1,), (1,)), ((), ())), preferred_element_...  95.8 us
    dot_general x32, matrix products, product(): return jnp.dot(left, right, preferred_element_type=F32)  89.6 us
    unnamed x575, local copies, waits for them, and re-layouts  78.5 us
    ppermute x94, starting transfers between devices, swap(): return lax.ppermute(value, axis, [(0, 1), (1, 0)])  77.4 us
    dot_general x24, matrix products, product_tn(): lax.dot_general(left, right, (((0,), (0,)), ((), ())), preferred_element_...  64.3 us
  transfers between devices with their start and end apart: 97, of which 45 were waited for; matrix products, arithmetic and copies ran while one was open for 31% of the time, Pallas kernels for 0%

profile of v5, /device:TPU:0, one launch (start us, length us, event | category | flops | bytes accessed | tf_op | source)
XLA Modules:
  0.0 1322.1 jit_solution(18439979880528377729)
XLA Ops:
  7.9 5.4 all-to-all-start
  17.8 46.1 %collective-permute-done = bf16[64,5760]{1,0:T(8,128)(2,1)} collective-permute-done((bf16[64,5760]{1,0:T(8,128)(2,1)S(1)}, bf16[64,5760]{1,0:T(8,128)(2,1)}, u32[]{:S(2)}, u32[]{:S(2)}) %collective-permute-start) | collective-permute-done | bytes 737312 | tf_op jit(solution)/shard_map/ppermute | solution.py:73
  76.5 52.3 %collective-permute-done.1 = bf16[128,5760]{1,0:T(8,128)(2,1)} collective-permute-done((bf16[128,5760]{1,0:T(8,128)(2,1)S(1)}, bf16[128,5760]{1,0:T(8,128)(2,1)}, u32[]{:S(2)}, u32[]{:S(2)}) %collective-permute-start.1) | collective-permute-done | bytes 1474592 | tf_op jit(solution)/shard_map/ppermute | solution.py:73
  135.9 11.3 collective-permute-done.5
  161.8 14.2 %collective-permute-done.6 = bf16[512,1088]{0,1:T(8,128)(2,1)} collective-permute-done((bf16[512,1088]{0,1:T(8,128)(2,1)}, bf16[512,1088]{0,1:T(8,128)(2,1)}, u32[]{:S(2)}, u32[]{:S(2)}) %collective-permute-start.6) | collective-permute-done | bytes 1114144 | tf_op jit(solution)/shard_map/ppermute | solution.py:73
  184.5 39.5 %collective-permute-done.10 = bf16[512,1024]{1,0:T(8,128)(2,1)} collective-permute-done((bf16[512,1024]{1,0:T(8,128)(2,1)S(1)}, bf16[512,1024]{1,0:T(8,128)(2,1)}, u32[]{:S(2)}, u32[]{:S(2)}) %collective-permute-start.10) | collective-permute-done | bytes 1048608 | tf_op jit(solution)/shard_map/ppermute | solution.py:73
  245.1 17.8 %collective-permute-done.11 = bf16[2,1,2,128,2,256]{5,3,4,2,1,0:T(8,128)(2,1)} collective-permute-done((bf16[2,1,2,128,2,256]{5,3,4,2,1,0:T(8,128)(2,1)}, bf16[2,1,2,128,2,256]{5,3,4,2,1,0:T(8,128)(2,1)}, u32[]{:S(2)}, u32[]{:S(2)}) %collective-permute-start.11) | collective-permute-done | bytes 524320 | tf_op jit(solution)/shard_map/ppermute | solution.py:73
  264.7 14.3 %collective-permute-done.16 = bf16[512,2048]{1,0:T(8,128)(2,1)} collective-permute-done((bf16[512,2048]{1,0:T(8,128)(2,1)}, bf16[512,2048]{1,0:T(8,128)(2,1)}, u32[]{:S(2)}, u32[]{:S(2)}) %collective-permute-start.16) | collective-permute-done | bytes 2097184 | tf_op jit(solution)/shard_map/ppermute | solution.py:73
  280.0 9.3 collective-permute-done.12
  310.2 21.5 %collective-permute-done.13 = bf16[2,2,2,128,2,256]{5,3,4,2,1,0:T(8,128)(2,1)} collective-permute-done((bf16[2,2,2,128,2,256]{5,3,4,2,1,0:T(8,128)(2,1)}, bf16[2,2,2,128,2,256]{5,3,4,2,1,0:T(8,128)(2,1)}, u32[]{:S(2)}, u32[]{:S(2)}) %collective-permute-start.13) | collective-permute-done | bytes 1048608 | tf_op jit(solution)/shard_map/ppermute | solution.py:73
  366.1 41.9 %collective-permute-done.21 = bf16[512,2624]{0,1:T(8,128)(2,1)} collective-permute-done((bf16[512,2624]{0,1:T(8,128)(2,1)}, bf16[512,2624]{0,1:T(8,128)(2,1)}, u32[]{:S(2)}, u32[]{:S(2)}) %collective-permute-start.21) | collective-permute-done | bytes 2687008 | tf_op jit(solution)/shard_map/ppermute | solution.py:73
  424.5 10.4 collective-permute-done.25
  458.0 6.3 pad_maximum_fusion.3
  502.1 5.5 collective-permute-done.26
  511.6 8.7 collective-permute-done.34
  554.0 10.4 collective-permute-done.42
  569.9 20.2 %collective-permute-done.43 = bf16[256,2048]{1,0:T(8,128)(2,1)} collective-permute-done((bf16[256,2048]{1,0:T(8,128)(2,1)}, bf16[256,2048]{1,0:T(8,128)(2,1)}, u32[]{:S(2)}, u32[]{:S(2)}) %collective-permute-start.43) | collective-permute-done | bytes 1048608 | tf_op jit(solution)/shard_map/ppermute | solution.py:73
  622.8 12.9 collective-permute-done.45
  639.8 11.6 collective-permute-done.49
  669.5 5.8 add_convert_fusion.7
  679.7 5.8 add_convert_fusion.6
  687.2 6.5 multiply_convert_fusion
  698.1 5.8 add_convert_fusion.5
  751.2 11.4 collective-permute-done.58
  766.2 6.5 collective-permute-done.60
  776.0 18.2 %collective-permute-done.61 = bf16[512,1024]{1,0:T(8,128)(2,1)S(1)} collective-permute-done((bf16[512,1024]{1,0:T(8,128)(2,1)S(1)}, bf16[512,1024]{1,0:T(8,128)(2,1)S(1)}, u32[]{:S(2)}, u32[]{:S(2)}) %collective-permute-start.61) | collective-permute-done | bytes 1048608 | tf_op jit(solution)/shard_map/ppermute | solution.py:73
  807.0 7.2 fusion.25
  825.9 8.7 concatenate.228
  834.6 8.4 copy.654
  846.6 7.3 fusion.37
  865.8 8.6 concatenate.227
  882.4 8.0 copy.655
  890.4 8.0 add_convert_fusion
  900.6 8.7 fusion.10
  909.3 6.0 convolution_bitcast_fusion
  924.5 6.5 fusion.12
  935.4 29.1 %collective-permute-done.63 = bf16[512,1024]{1,0:T(8,128)(2,1)} collective-permute-done((bf16[512,1024]{1,0:T(8,128)(2,1)}, bf16[512,1024]{1,0:T(8,128)(2,1)}, u32[]{:S(2)}, u32[]{:S(2)}) %collective-permute-start.63) | collective-permute-done | bytes 1048608 | tf_op jit(solution)/shard_map/ppermute | solution.py:73
  1022.0 31.3 %collective-permute-done.73 = bf16[512,1024]{1,0:T(8,128)(2,1)S(1)} collective-permute-done((bf16[512,1024]{1,0:T(8,128)(2,1)S(1)}, bf16[512,1024]{1,0:T(8,128)(2,1)S(1)}, u32[]{:S(2)}, u32[]{:S(2)}) %collective-permute-start.73) | collective-permute-done | bytes 1048608 | tf_op jit(solution)/shard_map/ppermute | solution.py:73
  1057.6 6.8 collective-permute-done.75
  1080.3 14.1 %collective-permute-done.70 = bf16[2,2,128,2,256]{4,2,3,1,0:T(8,128)(2,1)} collective-permute-done((bf16[2,2,128,2,256]{4,2,3,1,0:T(8,128)(2,1)}, bf16[2,2,128,2,256]{4,2,3,1,0:T(8,128)(2,1)}, u32[]{:S(2)}, u32[]{:S(2)}) %collective-permute-start.70) | collective-permute-done | bytes 524320 | tf_op jit(solution)/shard_map/ppermute | solution.py:73
  1126.3 8.0 fusion.6
  1134.4 38.6 %collective-permute-done.88 = bf16[512,1024]{1,0:T(8,128)(2,1)S(1)} collective-permute-done((bf16[512,1024]{1,0:T(8,128)(2,1)S(1)}, bf16[512,1024]{1,0:T(8,128)(2,1)S(1)}, u32[]{:S(2)}, u32[]{:S(2)}) %collective-permute-start.88) | collective-permute-done | bytes 1048608 | tf_op jit(solution)/shard_map/ppermute | solution.py:73
  1201.4 6.2 collective-permute-done.86
  1217.4 18.6 %collective-permute-done.87 = bf16[64,2624]{1,0:T(8,128)(2,1)S(1)} collective-permute-done((bf16[64,2624]{1,0:T(8,128)(2,1)S(1)}, bf16[64,2624]{1,0:T(8,128)(2,1)S(1)}, u32[]{:S(2)}, u32[]{:S(2)}) %collective-permute-start.87) | collective-permute-done | bytes 335904 | tf_op jit(solution)/shard_map/ppermute | solution.py:73
  1263.8 15.2 %collective-permute-done.91 = f32[12800]{0:T(1024)S(1)} collective-permute-done((f32[12800]{0:T(1024)S(1)}, f32[12800]{0:T(1024)S(1)}, u32[]{:S(2)}, u32[]{:S(2)}) %collective-permute-start.91) | collective-permute-done | bytes 51232 | tf_op jit(solution)/shard_map/ppermute | solution.py:73
  1289.6 8.5 collective-permute-done.93
  1299.6 6.1 collective-permute-done.83
  1308.1 11.2 collective-permute-done.84
  (1128 shorter events, 625.8 us)
Async XLA Ops:
  7.9 58.2 %all-to-all-start = ((bf16[8,192,1024]{2,1,0:T(8,128)(2,1)}), bf16[8,192,1024]{2,1,0:T(8,128)(2,1)}, u32[]{:S(2)}, u32[]{:S(2)}) async-start(bf16[8,192,1024]{2,1,0:T(8,128)(2,1)} %copy.615), calls=%async_computation | async-start | bytes 6291456 | tf_op jit(solution)/shard_map/all_to_all | solution.py:320
  13.9 50.0 %collective-permute-start = (bf16[64,5760]{1,0:T(8,128)(2,1)S(1)}, bf16[64,5760]{1,0:T(8,128)(2,1)}, u32[]{:S(2)}, u32[]{:S(2)}) collective-permute-start(bf16[64,5760]{1,0:T(8,128)(2,1)S(1)} %concatenate.185), channel_id=1, source_target_pairs={{0,16},{16,0},{1,17},{17,1},{2,18},{18,2},{3,19},{19,3},{4,20},{20... | collective-permute-start | bytes 2211848 | tf_op jit(solution)/shard_map/ppermute | solution.py:73
  69.7 59.1 %collective-permute-start.1 = (bf16[128,5760]{1,0:T(8,128)(2,1)S(1)}, bf16[128,5760]{1,0:T(8,128)(2,1)}, u32[]{:S(2)}, u32[]{:S(2)}) collective-permute-start(bf16[128,5760]{1,0:T(8,128)(2,1)S(1)} %pad_maximum_fusion.11), channel_id=1, source_target_pairs={{0,8},{8,0},{1,9},{9,1},{2,10},{10,2},{3,11},{11,3},{4,12},{12,4},... | collective-permute-start | bytes 4423688 | tf_op jit(solution)/shard_map/ppermute | solution.py:73
  74.3 56.1 %collective-permute-start.2 = (bf16[512,1024]{1,0:T(8,128)(2,1)}, bf16[512,1024]{1,0:T(8,128)(2,1)}, u32[]{:S(2)}, u32[]{:S(2)}) collective-permute-start(bf16[512,1024]{1,0:T(8,128)(2,1)} %bitcast.472), channel_id=1, source_target_pairs={{0,16},{16,0},{1,17},{17,1},{2,18},{18,2},{3,19},{19,3},{4,20},{20... | collective-permute-start | bytes 3145736 | tf_op jit(solution)/shard_map/ppermute | solution.py:73
  74.4 56.0 %collective-permute-start.3 = (bf16[512,1024]{1,0:T(8,128)(2,1)}, bf16[512,1024]{1,0:T(8,128)(2,1)S(1)}, u32[]{:S(2)}, u32[]{:S(2)}) collective-permute-start(bf16[512,1024]{1,0:T(8,128)(2,1)} %bitcast.473), channel_id=1, source_target_pairs={{0,2},{2,0},{1,3},{3,1},{4,6},{6,4},{5,7},{7,5},{8,10},{10,8},{9,1... | collective-permute-start | bytes 3145736 | tf_op jit(solution)/shard_map/ppermute | solution.py:73
  75.9 55.5 %collective-permute-start.4 = (bf16[512,1024]{1,0:T(8,128)(2,1)}, bf16[512,1024]{1,0:T(8,128)(2,1)S(1)}, u32[]{:S(2)}, u32[]{:S(2)}) collective-permute-start(bf16[512,1024]{1,0:T(8,128)(2,1)} %bitcast.469), channel_id=1, source_target_pairs={{0,2},{2,0},{1,3},{3,1},{4,6},{6,4},{5,7},{7,5},{8,10},{10,8},{9,1... | collective-permute-start | bytes 3145736 | tf_op jit(solution)/shard_map/ppermute | solution.py:73
  161.7 62.3 %collective-permute-start.7 = (bf16[512,1088]{0,1:T(8,128)(2,1)S(1)}, bf16[512,1088]{0,1:T(8,128)(2,1)S(1)}, u32[]{:S(2)}, u32[]{:S(2)}) collective-permute-start(bf16[512,1088]{0,1:T(8,128)(2,1)S(1)} %copy-done.92), channel_id=1, source_target_pairs={{0,1},{1,0},{2,3},{3,2},{4,5},{5,4},{6,7},{7,6},{8,9},{9,8},{10,11... | collective-permute-start | bytes 3342344 | tf_op jit(solution)/shard_map/ppermute | solution.py:73
  176.0 48.0 %collective-permute-start.8 = (bf16[512,1088]{0,1:T(8,128)(2,1)}, bf16[512,1088]{0,1:T(8,128)(2,1)S(1)}, u32[]{:S(2)}, u32[]{:S(2)}) collective-permute-start(bf16[512,1088]{0,1:T(8,128)(2,1)} %collective-permute-done.6), channel_id=1, source_target_pairs={{0,1},{1,0},{2,3},{3,2},{4,5},{5,4},{6,7},{7,6},{8,9},{9,8},{10,11... | collective-permute-start | bytes 3342344 | tf_op jit(solution)/shard_map/ppermute | solution.py:73
  176.0 48.0 %collective-permute-start.10 = (bf16[512,1024]{1,0:T(8,128)(2,1)S(1)}, bf16[512,1024]{1,0:T(8,128)(2,1)}, u32[]{:S(2)}, u32[]{:S(2)}) collective-permute-start(bf16[512,1024]{1,0:T(8,128)(2,1)S(1)} %bitcast.470), channel_id=1, source_target_pairs={{0,16},{16,0},{1,17},{17,1},{2,18},{18,2},{3,19},{19,3},{4,20},{20... | collective-permute-start | bytes 3145736 | tf_op jit(solution)/shard_map/ppermute | solution.py:73
  230.2 48.9 %collective-permute-start.16 = (bf16[512,2048]{1,0:T(8,128)(2,1)}, bf16[512,2048]{1,0:T(8,128)(2,1)}, u32[]{:S(2)}, u32[]{:S(2)}) collective-permute-start(bf16[512,2048]{1,0:T(8,128)(2,1)} %pad_maximum_fusion.4), channel_id=1, source_target_pairs={{0,4},{4,0},{1,5},{5,1},{2,6},{6,2},{3,7},{7,3},{8,12},{12,8},{9,1... | collective-permute-start | bytes 6291464 | tf_op jit(solution)/shard_map/ppermute | solution.py:73
  243.4 53.4 %collective-permute-start.20 = (bf16[256,2624]{0,1:T(8,128)(2,1)}, bf16[256,2624]{0,1:T(8,128)(2,1)}, u32[]{:S(2)}, u32[]{:S(2)}) collective-permute-start(bf16[256,2624]{0,1:T(8,128)(2,1)} %copy.627), channel_id=1, source_target_pairs={{0,2},{2,0},{1,3},{3,1},{4,6},{6,4},{5,7},{7,5},{8,10},{10,8},{9,1... | collective-permute-start | bytes 4030472 | tf_op jit(solution)/shard_map/ppermute | solution.py:73
  245.0 99.7 %collective-permute-start.17 = (bf16[512,2048]{1,0:T(8,128)(2,1)}, bf16[512,2048]{1,0:T(8,128)(2,1)}, u32[]{:S(2)}, u32[]{:S(2)}) collective-permute-start(bf16[512,2048]{1,0:T(8,128)(2,1)} %pad_maximum_fusion.4), channel_id=1, source_target_pairs={{0,1},{1,0},{2,3},{3,2},{4,5},{5,4},{6,7},{7,6},{8,9},{9,8},{10,11... | collective-permute-start | bytes 6291464 | tf_op jit(solution)/shard_map/ppermute | solution.py:73
  279.1 65.6 %collective-permute-start.18 = (bf16[512,2048]{1,0:T(8,128)(2,1)}, bf16[512,2048]{1,0:T(8,128)(2,1)}, u32[]{:S(2)}, u32[]{:S(2)}) collective-permute-start(bf16[512,2048]{1,0:T(8,128)(2,1)} %collective-permute-done.16), channel_id=1, source_target_pairs={{0,1},{1,0},{2,3},{3,2},{4,5},{5,4},{6,7},{7,6},{8,9},{9,8},{10,11... | collective-permute-start | bytes 6291464 | tf_op jit(solution)/shard_map/ppermute | solution.py:73
  290.8 41.0 %collective-permute-start.13 = (bf16[2,2,2,128,2,256]{5,3,4,2,1,0:T(8,128)(2,1)}, bf16[2,2,2,128,2,256]{5,3,4,2,1,0:T(8,128)(2,1)}, u32[]{:S(2)}, u32[]{:S(2)}) collective-permute-start(bf16[2,2,2,128,2,256]{5,3,4,2,1,0:T(8,128)(2,1)} %get-tuple-element.528), channel_id=1, source_target_pairs={{0,8},{8,0},{1,9},{9,1},{2,10},{10,2},{3,11},{11,3},{4,12},{12,4},... | collective-permute-start | bytes 3145736 | tf_op jit(solution)/shard_map/ppermute | solution.py:73
  295.2 40.9 %collective-permute-start.15 = (bf16[2,2,2,128,2,256]{5,3,4,2,1,0:T(8,128)(2,1)}, bf16[2,2,2,128,2,256]{5,3,4,2,1,0:T(8,128)(2,1)}, u32[]{:S(2)}, u32[]{:S(2)}) collective-permute-start(bf16[2,2,2,128,2,256]{5,3,4,2,1,0:T(8,128)(2,1)} %get-tuple-element.524), channel_id=1, source_target_pairs={{0,4},{4,0},{1,5},{5,1},{2,6},{6,2},{3,7},{7,3},{8,12},{12,8},{9,1... | collective-permute-start | bytes 3145736 | tf_op jit(solution)/shard_map/ppermute | solution.py:73
  296.8 47.9 %collective-permute-start.19 = (bf16[512,1024]{1,0:T(8,128)(2,1)}, bf16[512,1024]{1,0:T(8,128)(2,1)}, u32[]{:S(2)}, u32[]{:S(2)}) collective-permute-start(bf16[512,1024]{1,0:T(8,128)(2,1)} %bitcast.10), channel_id=1, source_target_pairs={{0,16},{16,0},{1,17},{17,1},{2,18},{18,2},{3,19},{19,3},{4,20},{20... | collective-permute-start | bytes 3145736 | tf_op jit(solution)/shard_map/ppermute | solution.py:73
  331.8 91.9 %collective-permute-start.24 = (bf16[512,1024]{1,0:T(8,128)(2,1)}, bf16[512,1024]{1,0:T(8,128)(2,1)}, u32[]{:S(2)}, u32[]{:S(2)}) collective-permute-start(bf16[512,1024]{1,0:T(8,128)(2,1)} %collective-permute-done.2), channel_id=1, source_target_pairs={{0,2},{2,0},{1,3},{3,1},{4,6},{6,4},{5,7},{7,5},{8,10},{10,8},{9,1... | collective-permute-start | bytes 3145736 | tf_op jit(solution)/shard_map/ppermute | solution.py:73
  349.3 58.7 %collective-permute-start.21 = (bf16[512,2624]{0,1:T(8,128)(2,1)}, bf16[512,2624]{0,1:T(8,128)(2,1)}, u32[]{:S(2)}, u32[]{:S(2)}) collective-permute-start(bf16[512,2624]{0,1:T(8,128)(2,1)} %copy.637), channel_id=1, source_target_pairs={{0,4},{4,0},{1,5},{5,1},{2,6},{6,2},{3,7},{7,3},{8,12},{12,8},{9,1... | collective-permute-start | bytes 8060936 | tf_op jit(solution)/shard_map/ppermute | solution.py:73
  353.8 127.5 %collective-permute-start.29 = (bf16[512,1024]{1,0:T(8,128)(2,1)}, bf16[512,1024]{1,0:T(8,128)(2,1)}, u32[]{:S(2)}, u32[]{:S(2)}) collective-permute-start(bf16[512,1024]{1,0:T(8,128)(2,1)} %collective-permute-done.10), channel_id=1, source_target_pairs={{0,2},{2,0},{1,3},{3,1},{4,6},{6,4},{5,7},{7,5},{8,10},{10,8},{9,1... | collective-permute-start | bytes 3145736 | tf_op jit(solution)/shard_map/ppermute | solution.py:73
  361.4 73.5 %collective-permute-start.22 = (bf16[512,2624]{0,1:T(8,128)(2,1)}, bf16[512,2624]{0,1:T(8,128)(2,1)}, u32[]{:S(2)}, u32[]{:S(2)}) collective-permute-start(bf16[512,2624]{0,1:T(8,128)(2,1)} %copy.637), channel_id=1, source_target_pairs={{0,1},{1,0},{2,3},{3,2},{4,5},{5,4},{6,7},{7,6},{8,9},{9,8},{10,11... | collective-permute-start | bytes 8060936 | tf_op jit(solution)/shard_map/ppermute | solution.py:73
  408.0 26.9 %collective-permute-start.23 = (bf16[512,2624]{0,1:T(8,128)(2,1)}, bf16[512,2624]{0,1:T(8,128)(2,1)}, u32[]{:S(2)}, u32[]{:S(2)}) collective-permute-start(bf16[512,2624]{0,1:T(8,128)(2,1)} %collective-permute-done.21), channel_id=1, source_target_pairs={{0,1},{1,0},{2,3},{3,2},{4,5},{5,4},{6,7},{7,6},{8,9},{9,8},{10,11... | collective-permute-start | bytes 8060936 | tf_op jit(solution)/shard_map/ppermute | solution.py:73
  408.5 26.3 %collective-permute-start.25 = (bf16[512,1024]{1,0:T(8,128)(2,1)}, bf16[512,1024]{1,0:T(8,128)(2,1)}, u32[]{:S(2)}, u32[]{:S(2)}) collective-permute-start(bf16[512,1024]{1,0:T(8,128)(2,1)} %bitcast.10), channel_id=1, source_target_pairs={{0,2},{2,0},{1,3},{3,1},{4,6},{6,4},{5,7},{7,5},{8,10},{10,8},{9,1... | collective-permute-start | bytes 3145736 | tf_op jit(solution)/shard_map/ppermute | solution.py:73
  423.6 67.3 %collective-permute-start.30 = (bf16[512,1024]{1,0:T(8,128)(2,1)}, bf16[512,1024]{1,0:T(8,128)(2,1)}, u32[]{:S(2)}, u32[]{:S(2)}) collective-permute-start(bf16[512,1024]{1,0:T(8,128)(2,1)} %collective-permute-done.19), channel_id=1, source_target_pairs={{0,2},{2,0},{1,3},{3,1},{4,6},{6,4},{5,7},{7,5},{8,10},{10,8},{9,1... | collective-permute-start | bytes 3145736 | tf_op jit(solution)/shard_map/ppermute | solution.py:73
  511.4 58.5 %collective-permute-start.31 = (bf16[256,2048]{1,0:T(8,128)(2,1)}, bf16[256,2048]{1,0:T(8,128)(2,1)}, u32[]{:S(2)}, u32[]{:S(2)}) collective-permute-start(bf16[256,2048]{1,0:T(8,128)(2,1)} %slice.558), channel_id=1, source_target_pairs={{0,1},{1,0},{2,3},{3,2},{4,5},{5,4},{6,7},{7,6},{8,9},{9,8},{10,11... | collective-permute-start | bytes 3145736 | tf_op jit(solution)/shard_map/ppermute | solution.py:73
  652.9 32.6 %collective-permute-start.51 = (bf16[256,2048]{1,0:T(8,128)(2,1)S(1)}, bf16[256,2048]{1,0:T(8,128)(2,1)S(1)}, u32[]{:S(2)}, u32[]{:S(2)}) collective-permute-start(bf16[256,2048]{1,0:T(8,128)(2,1)S(1)} %pad_maximum_fusion.19), channel_id=1, source_target_pairs={{0,1},{1,0},{2,3},{3,2},{4,5},{5,4},{6,7},{7,6},{8,9},{9,8},{10,11... | collective-permute-start | bytes 3145736 | tf_op jit(solution)/shard_map/ppermute | solution.py:73
  746.1 51.6 %collective-permute-start.52 = (bf16[256,2048]{1,0:T(8,128)(2,1)S(1)}, bf16[256,2048]{1,0:T(8,128)(2,1)S(1)}, u32[]{:S(2)}, u32[]{:S(2)}) collective-permute-start(bf16[256,2048]{1,0:T(8,128)(2,1)S(1)} %slice.578), channel_id=1, source_target_pairs={{0,1},{1,0},{2,3},{3,2},{4,5},{5,4},{6,7},{7,6},{8,9},{9,8},{10,11... | collective-permute-start | bytes 3145736 | tf_op jit(solution)/shard_map/ppermute | solution.py:73
  748.1 46.1 %collective-permute-start.61 = (bf16[512,1024]{1,0:T(8,128)(2,1)S(1)}, bf16[512,1024]{1,0:T(8,128)(2,1)S(1)}, u32[]{:S(2)}, u32[]{:S(2)}) collective-permute-start(bf16[512,1024]{1,0:T(8,128)(2,1)S(1)} %fusion.160), channel_id=1, source_target_pairs={{0,2},{2,0},{1,3},{3,1},{4,6},{6,4},{5,7},{7,5},{8,10},{10,8},{9,1... | collective-permute-start | bytes 3145736 | tf_op jit(solution)/shard_map/ppermute | solution.py:73
  762.8 34.9 %collective-permute-start.59 = (bf16[256,2048]{1,0:T(8,128)(2,1)S(1)}, bf16[256,2048]{1,0:T(8,128)(2,1)S(1)}, u32[]{:S(2)}, u32[]{:S(2)}) collective-permute-start(bf16[256,2048]{1,0:T(8,128)(2,1)S(1)} %pad_maximum_fusion.21), channel_id=1, source_target_pairs={{0,4},{4,0},{1,5},{5,1},{2,6},{6,2},{3,7},{7,3},{8,12},{12,8},{9,1... | collective-permute-start | bytes 3145736 | tf_op jit(solution)/shard_map/ppermute | solution.py:73
  763.8 33.9 %collective-permute-start.56 = (bf16[256,2048]{1,0:T(8,128)(2,1)S(1)}, bf16[256,2048]{1,0:T(8,128)(2,1)S(1)}, u32[]{:S(2)}, u32[]{:S(2)}) collective-permute-start(bf16[256,2048]{1,0:T(8,128)(2,1)S(1)} %pad_maximum_fusion.20), channel_id=1, source_target_pairs={{0,8},{8,0},{1,9},{9,1},{2,10},{10,2},{3,11},{11,3},{4,12},{12,4},... | collective-permute-start | bytes 3145736 | tf_op jit(solution)/shard_map/ppermute | solution.py:73
  843.1 39.3 %collective-permute-start.62 = (bf16[1024,2624]{0,1:T(8,128)(2,1)}, bf16[1024,2624]{0,1:T(8,128)(2,1)}, u32[]{:S(2)}, u32[]{:S(2)}) collective-permute-start(bf16[1024,2624]{0,1:T(8,128)(2,1)} %copy.654), channel_id=1, source_target_pairs={{0,1},{1,0},{2,3},{3,2},{4,5},{5,4},{6,7},{7,6},{8,9},{9,8},{10,11... | collective-permute-start | bytes 16121864 | tf_op jit(solution)/shard_map/ppermute | solution.py:73
  915.3 49.1 %collective-permute-start.63 = (bf16[512,1024]{1,0:T(8,128)(2,1)}, bf16[512,1024]{1,0:T(8,128)(2,1)}, u32[]{:S(2)}, u32[]{:S(2)}) collective-permute-start(bf16[512,1024]{1,0:T(8,128)(2,1)} %add_convert_fusion.19), channel_id=1, source_target_pairs={{0,16},{16,0},{1,17},{17,1},{2,18},{18,2},{3,19},{19,3},{4,20},{20... | collective-permute-start | bytes 3145736 | tf_op jit(solution)/shard_map/ppermute | solution.py:73
  915.4 51.7 %collective-permute-start.64 = (bf16[512,1024]{1,0:T(8,128)(2,1)}, bf16[512,1024]{1,0:T(8,128)(2,1)}, u32[]{:S(2)}, u32[]{:S(2)}) collective-permute-start(bf16[512,1024]{1,0:T(8,128)(2,1)} %fusion.151), channel_id=1, source_target_pairs={{0,2},{2,0},{1,3},{3,1},{4,6},{6,4},{5,7},{7,5},{8,10},{10,8},{9,1... | collective-permute-start | bytes 3145736 | tf_op jit(solution)/shard_map/ppermute | solution.py:73
  916.9 52.8 %collective-permute-start.65 = (bf16[512,1024]{1,0:T(8,128)(2,1)}, bf16[512,1024]{1,0:T(8,128)(2,1)}, u32[]{:S(2)}, u32[]{:S(2)}) collective-permute-start(bf16[512,1024]{1,0:T(8,128)(2,1)} %fusion.163), channel_id=1, source_target_pairs={{0,2},{2,0},{1,3},{3,1},{4,6},{6,4},{5,7},{7,5},{8,10},{10,8},{9,1... | collective-permute-start | bytes 3145736 | tf_op jit(solution)/shard_map/ppermute | solution.py:73
  923.9 147.0 %collective-permute-start.71 = (bf16[512,2624]{0,1:T(8,128)(2,1)}, bf16[512,2624]{0,1:T(8,128)(2,1)}, u32[]{:S(2)}, u32[]{:S(2)}) collective-permute-start(bf16[512,2624]{0,1:T(8,128)(2,1)} %copy.681), channel_id=1, source_target_pairs={{0,4},{4,0},{1,5},{5,1},{2,6},{6,2},{3,7},{7,3},{8,12},{12,8},{9,1... | collective-permute-start | bytes 8060936 | tf_op jit(solution)/shard_map/ppermute | solution.py:73
  981.0 35.5 %collective-permute-start.68 = (bf16[2,2,2,128,2,256]{5,3,4,2,1,0:T(8,128)(2,1)}, bf16[2,2,2,128,2,256]{5,3,4,2,1,0:T(8,128)(2,1)}, u32[]{:S(2)}, u32[]{:S(2)}) collective-permute-start(bf16[2,2,2,128,2,256]{5,3,4,2,1,0:T(8,128)(2,1)} %slice_bitcast_fusion), channel_id=1, source_target_pairs={{0,4},{4,0},{1,5},{5,1},{2,6},{6,2},{3,7},{7,3},{8,12},{12,8},{9,1... | collective-permute-start | bytes 3145736 | tf_op jit(solution)/shard_map/ppermute | solution.py:73
  987.4 32.3 %collective-permute-start.66 = (bf16[2,2,2,128,2,256]{5,3,4,2,1,0:T(8,128)(2,1)}, bf16[2,2,2,128,2,256]{5,3,4,2,1,0:T(8,128)(2,1)}, u32[]{:S(2)}, u32[]{:S(2)}) collective-permute-start(bf16[2,2,2,128,2,256]{5,3,4,2,1,0:T(8,128)(2,1)} %bitcast.61), channel_id=1, source_target_pairs={{0,8},{8,0},{1,9},{9,1},{2,10},{10,2},{3,11},{11,3},{4,12},{12,4},... | collective-permute-start | bytes 3145736 | tf_op jit(solution)/shard_map/ppermute | solution.py:73
  1004.3 93.0 %collective-permute-start.72 = (bf16[1024,2048]{1,0:T(8,128)(2,1)}, bf16[1024,2048]{1,0:T(8,128)(2,1)}, u32[]{:S(2)}, u32[]{:S(2)}) collective-permute-start(bf16[1024,2048]{1,0:T(8,128)(2,1)} %convolution_convert_fusion.2), channel_id=1, source_target_pairs={{0,1},{1,0},{2,3},{3,2},{4,5},{5,4},{6,7},{7,6},{8,9},{9,8},{10,11... | collective-permute-start | bytes 12582920 | tf_op jit(solution)/shard_map/ppermute | solution.py:73
  1004.3 49.0 %collective-permute-start.73 = (bf16[512,1024]{1,0:T(8,128)(2,1)S(1)}, bf16[512,1024]{1,0:T(8,128)(2,1)S(1)}, u32[]{:S(2)}, u32[]{:S(2)}) collective-permute-start(bf16[512,1024]{1,0:T(8,128)(2,1)S(1)} %copy-done.102), channel_id=1, source_target_pairs={{0,16},{16,0},{1,17},{17,1},{2,18},{18,2},{3,19},{19,3},{4,20},{20... | collective-permute-start | bytes 3145736 | tf_op jit(solution)/shard_map/ppermute | solution.py:73
  1016.5 38.2 %collective-permute-start.74 = (bf16[512,1024]{1,0:T(8,128)(2,1)S(1)}, bf16[512,1024]{1,0:T(8,128)(2,1)S(1)}, u32[]{:S(2)}, u32[]{:S(2)}) collective-permute-start(bf16[512,1024]{1,0:T(8,128)(2,1)S(1)} %copy-done.235), channel_id=1, source_target_pairs={{0,2},{2,0},{1,3},{3,1},{4,6},{6,4},{5,7},{7,5},{8,10},{10,8},{9,1... | collective-permute-start | bytes 3145736 | tf_op jit(solution)/shard_map/ppermute | solution.py:73
  1019.7 44.7 %collective-permute-start.75 = (bf16[512,1024]{1,0:T(8,128)(2,1)S(1)}, bf16[512,1024]{1,0:T(8,128)(2,1)S(1)}, u32[]{:S(2)}, u32[]{:S(2)}) collective-permute-start(bf16[512,1024]{1,0:T(8,128)(2,1)S(1)} %copy-done.236), channel_id=1, source_target_pairs={{0,2},{2,0},{1,3},{3,1},{4,6},{6,4},{5,7},{7,5},{8,10},{10,8},{9,1... | collective-permute-start | bytes 3145736 | tf_op jit(solution)/shard_map/ppermute | solution.py:73
  1120.3 90.0 %collective-permute-start.76 = (bf16[512,2048]{1,0:T(8,128)(2,1)}, bf16[512,2048]{1,0:T(8,128)(2,1)}, u32[]{:S(2)}, u32[]{:S(2)}) collective-permute-start(bf16[512,2048]{1,0:T(8,128)(2,1)} %slice.632), channel_id=1, source_target_pairs={{0,4},{4,0},{1,5},{5,1},{2,6},{6,2},{3,7},{7,3},{8,12},{12,8},{9,1... | collective-permute-start | bytes 6291464 | tf_op jit(solution)/shard_map/ppermute | solution.py:73
  1122.6 92.4 %collective-permute-start.80 = (bf16[1024,1088]{0,1:T(8,128)(2,1)}, bf16[1024,1088]{0,1:T(8,128)(2,1)}, u32[]{:S(2)}, u32[]{:S(2)}) collective-permute-start(bf16[1024,1088]{0,1:T(8,128)(2,1)} %convolution_convert_fusion), channel_id=1, source_target_pairs={{0,1},{1,0},{2,3},{3,2},{4,5},{5,4},{6,7},{7,6},{8,9},{9,8},{10,11... | collective-permute-start | bytes 6684680 | tf_op jit(solution)/shard_map/ppermute | solution.py:73
  1124.1 57.6 %collective-permute-start.85 = (bf16[256,2624]{0,1:T(8,128)(2,1)}, bf16[256,2624]{0,1:T(8,128)(2,1)}, u32[]{:S(2)}, u32[]{:S(2)}) collective-permute-start(bf16[256,2624]{0,1:T(8,128)(2,1)} %copy.687), channel_id=1, source_target_pairs={{0,2},{2,0},{1,3},{3,1},{4,6},{6,4},{5,7},{7,5},{8,10},{10,8},{9,1... | collective-permute-start | bytes 4030472 | tf_op jit(solution)/shard_map/ppermute | solution.py:73
  1125.6 47.3 %collective-permute-start.88 = (bf16[512,1024]{1,0:T(8,128)(2,1)S(1)}, bf16[512,1024]{1,0:T(8,128)(2,1)S(1)}, u32[]{:S(2)}, u32[]{:S(2)}) collective-permute-start(bf16[512,1024]{1,0:T(8,128)(2,1)S(1)} %copy-done.101), channel_id=1, source_target_pairs={{0,16},{16,0},{1,17},{17,1},{2,18},{18,2},{3,19},{19,3},{4,20},{20... | collective-permute-start | bytes 3145736 | tf_op jit(solution)/shard_map/ppermute | solution.py:73
  1196.2 44.8 %all-to-all-start.1 = ((bf16[8,128,1024]{2,1,0:T(8,128)(2,1)}), bf16[8,128,1024]{2,1,0:T(8,128)(2,1)}, u32[]{:S(2)}, u32[]{:S(2)}) async-start(bf16[8,128,1024]{2,1,0:T(8,128)(2,1)} %pad_maximum_fusion.10), calls=%async_computation.1 | async-start | bytes 4194304 | tf_op jit(solution)/shard_map/all_to_all | solution.py:209
  1209.2 26.9 %collective-permute-start.87 = (bf16[64,2624]{1,0:T(8,128)(2,1)S(1)}, bf16[64,2624]{1,0:T(8,128)(2,1)S(1)}, u32[]{:S(2)}, u32[]{:S(2)}) collective-permute-start(bf16[64,2624]{1,0:T(8,128)(2,1)S(1)} %slice.805), channel_id=1, source_target_pairs={{0,16},{16,0},{1,17},{17,1},{2,18},{18,2},{3,19},{19,3},{4,20},{20... | collective-permute-start | bytes 1007624 | tf_op jit(solution)/shard_map/ppermute | solution.py:73
  1214.5 45.8 %collective-permute-start.77 = (bf16[256,2048]{1,0:T(8,128)(2,1)}, bf16[256,2048]{1,0:T(8,128)(2,1)}, u32[]{:S(2)}, u32[]{:S(2)}) collective-permute-start(bf16[256,2048]{1,0:T(8,128)(2,1)} %slice.773), channel_id=1, source_target_pairs={{0,2},{2,0},{1,3},{3,1},{4,6},{6,4},{5,7},{7,5},{8,10},{10,8},{9,1... | collective-permute-start | bytes 3145736 | tf_op jit(solution)/shard_map/ppermute | solution.py:73
  1252.0 29.1 %collective-permute-start.81 = (bf16[512,1088]{0,1:T(8,128)(2,1)S(1)}, bf16[512,1088]{0,1:T(8,128)(2,1)S(1)}, u32[]{:S(2)}, u32[]{:S(2)}) collective-permute-start(bf16[512,1088]{0,1:T(8,128)(2,1)S(1)} %slice.656), channel_id=1, source_target_pairs={{0,4},{4,0},{1,5},{5,1},{2,6},{6,2},{3,7},{7,3},{8,12},{12,8},{9,1... | collective-permute-start | bytes 3342344 | tf_op jit(solution)/shard_map/ppermute | solution.py:73
  (307 other events, 4444.2 us)

commit v6 on v5

--- a/solution.py
+++ b/solution.py
@@ -169,10 +169,13 @@
                 total = total.astype(BF16)
         return total
 
-    def near_gather(self, key, value):
+    def near_far(self, key, value):
         pair = jnp.stack([key, value])[:, None]
         for axis in reversed(self.far_seq):
             pair = jnp.concatenate([pair, swap(pair, axis)], axis=1)
+        return pair
+
+    def near_gather(self, pair):
         key, value = pair[0][None], pair[1][None]
         key = jnp.concatenate([key, swap(key, self.x)], axis=0)
         key = jnp.stack([key, swap(key, self.l)], axis=0)
@@ -232,12 +235,15 @@
             results.append(function(chunks[-1]))
         return chunks, results
 
-    def team_scatter(self, chunks):
+    def core_sums(self, chunks):
         sums = []
         for chunk in chunks:
             rows = chunk.shape[0] // 2
             other = swap(chunk[rows:].astype(BF16), self.c)
             sums.append(chunk[:rows].astype(F32) + other.astype(F32))
+        return sums
+
+    def team_near(self, sums):
         own, by_x, by_l, both = sums
         half = own.shape[0] // 2
         both = both.astype(BF16)
@@ -245,6 +251,10 @@
         second = by_x[half:] + swap(both[half:], self.l).astype(F32)
         by_l = jnp.concatenate([first, by_l[half:]], axis=0).astype(BF16)
         by_x = jnp.concatenate([by_x[:half], second], axis=0).astype(BF16)
+        return own, by_l, by_x
+
+    def team_far(self, sums):
+        own, by_l, by_x = sums
         return own + swap(by_l, self.l).astype(F32) + swap(by_x, self.x).astype(F32)
 
 
@@ -308,8 +318,13 @@
     team_size = 2 ** len(plan.team)
     hidden_own = gate_weight.shape[1] // team_size
 
-    kvl_widths = [key_weight.shape[1], value_weight.shape[1], laurel_left.shape[1]]
-    rest_widths = [laurel_right.shape[1], side_gate.shape[1], side_output.shape[1]]
+    kvl_widths = [
+        key_weight.shape[1],
+        value_weight.shape[1],
+        laurel_left.shape[1],
+        laurel_right.shape[1],
+    ]
+    rest_widths = [output_weight.shape[1], side_gate.shape[1], side_output.shape[1]]
     feed_local = jnp.concatenate(
         [
             one.reshape(local_rows, team_size, hidden_own).transpose(1, 0, 2)
@@ -322,28 +337,32 @@
         feed_team[:, index * local_rows : (index + 1) * local_rows].reshape(-1, hidden_own)
         for index in range(3)
     ]
-    block_widths = [sum(kvl_widths), query_weight.shape[1], output_weight.shape[1] + sum(rest_widths)]
+    block_widths = [sum(kvl_widths), query_weight.shape[1], sum(rest_widths)]
     attn_block = jnp.concatenate(
-        [key_weight, value_weight, laurel_left, query_weight, output_weight]
-        + [laurel_right, side_gate, side_output],
+        [key_weight, value_weight, laurel_left, laurel_right, query_weight]
+        + [output_weight, side_gate, side_output],
         axis=1,
     )
     attn_block = plan.grow(attn_block, plan.far_seq)
     attn_block, gate_own, up_own, down_own = together(attn_block, gate_own, up_own, down_own)
     attn_block = plan.grow(attn_block, (plan.l,))
-    gate_far = plan.pieces([gate_own], plan.far_seq)
-    gate_first = plan.pieces(gate_far[:1], plan.far_dp)
+    gate_first = plan.pieces([gate_own], plan.far_dp)
     up_first = plan.pieces([up_own], plan.far_dp)
-    attn_block, gate_far, gate_first, up_first = together(attn_block, gate_far, gate_first, up_first)
+    attn_block, gate_own, gate_first, up_first = together(attn_block, gate_own, gate_first, up_first)
     kvl_block, query_block, rest_block = split_columns(attn_block, block_widths)
     kvl_block = plan.grow(kvl_block, plan.far_dp)
     query_block = plan.grow(query_block, plan.far_dp)
+    gate_far = plan.pieces([gate_own], plan.far_seq)
+    kvl_full = plan.gather_pieces(kvl_block)
+    kvl_full, query_block, gate_far, up_own, rest_block = together(
+        kvl_full, query_block, gate_far, up_own, rest_block
+    )
     up_far = plan.pieces([up_own], plan.far_seq)
-    kvl_full = plan.gather_pieces(kvl_block)
-    kvl_full, query_block, up_far = together(kvl_full, query_block, up_far)
+    gate_last = plan.pieces(gate_far[1:], plan.far_dp)
     query_full = plan.gather_pieces(query_block)
-    down_far = plan.pieces([down_own], plan.far_seq)
     rest_block = plan.grow(rest_block, plan.far_dp)
+    right_full = plan.far_team_rows([one[:, -kvl_widths[3] :] for one in kvl_full])
+    kvl_full = [one[:, : -kvl_widths[3]] for one in kvl_full]
 
     places = jnp.arange(width, dtype=jnp.int32)
     far_team = plan.to_far_team(places[None])[0]
@@ -357,7 +376,9 @@
     normed, pre_pull = jax.vjp(rms, inputs, norm_input)
     normed_low = normed.astype(BF16)
     normed_spread = product(normed_low, to_spread).astype(BF16)
-    keys, values, latent = split_columns(product_split(normed_spread, kvl_full), kvl_widths)
+    keys, values, latent = split_columns(
+        product_split(normed_spread, kvl_full), kvl_widths[:3]
+    )
     queries = product_split(normed_spread, query_full).reshape(batch, block, heads, head_size)
     keys = keys.reshape(batch, block, kv_heads, head_size)
     values = values.reshape(batch, block, kv_heads, head_size)
@@ -383,9 +404,11 @@
     seq_index = lax.axis_index(plan.seq)
     total_length = block * seq_count
     if whole_sequence:
+        pair_low = plan.near_far(key_low, value_low)
+        pair_low, up_far, down_own = together(pair_low, up_far, down_own)
         keys_all, values_all = [
             one.swapaxes(0, 1).reshape(batch, total_length, kv_heads, head_size)
-            for one in plan.near_gather(key_low, value_low)
+            for one in plan.near_gather(pair_low)
         ]
         key_blocks = plan.near_places()
     else:
@@ -397,11 +420,10 @@
         keys_all, values_all = jnp.concatenate(gathered, axis=2)
         key_blocks = seq_index - jnp.array(offsets, dtype=jnp.int32)
     key_count = keys_all.shape[1]
-    keys_all, values_all, query_full, down_far, rest_block = together(
-        keys_all, values_all, query_full, down_far, rest_block
-    )
+    down_far = plan.pieces([down_own], plan.far_seq)
+    keys_all, values_all, rest_block = together(keys_all, values_all, rest_block)
     rest_full = plan.gather_pieces(rest_block)
-    gate_last = plan.pieces(gate_far[1:], plan.far_dp)
+    up_last = plan.pieces(up_far[1:], plan.far_dp)
     down_first = plan.pieces(down_far[:1], plan.far_dp)
     query_places = seq_index * block + jnp.arange(block, dtype=jnp.int32)
     key_places = (key_blocks[:, None] * block + jnp.arange(block, dtype=jnp.int32)).reshape(-1)
@@ -427,18 +449,17 @@
     probs_low = probs.astype(BF16)
     attended = jnp.einsum("bkgts,bskd->btkgd", probs_low, values_all, preferred_element_type=F32)
     attended_low = attended.reshape(rows, heads * head_size).astype(BF16)
-    attended_low, rest_full, gate_last, down_first = together(
-        attended_low, rest_full, gate_last, down_first
-    )
-    up_last = plan.pieces(up_far[1:], plan.far_dp)
+    attended_low, gate_last, up_last, down_first = together(
+        attended_low, gate_last, up_last, down_first
+    )
     down_last = plan.pieces(down_far[1:], plan.far_dp)
     gate_full, up_full, down_full = [
         jnp.concatenate(first + last, axis=0)
         for first, last in ((gate_first, gate_last), (up_first, up_last), (down_first, down_last))
     ]
-    output_full = [one[:, : output_weight.shape[1]] for one in rest_full]
-    rest_full = plan.far_team_rows([one[:, output_weight.shape[1] :] for one in rest_full])
-    right_full, side_gate_full, side_output_full = split_columns(rest_full, rest_widths)
+    output_full = [one[:, : rest_widths[0]] for one in rest_full]
+    side_full = plan.far_team_rows([one[:, rest_widths[0] :] for one in rest_full])
+    side_gate_full, side_output_full = split_columns(side_full, rest_widths[1:])
     attn_proj = reorder(product_nt_split(attended_low, output_full), to_spread)
     laurel = product_nt(latent_low, right_full)
     (resid_one, feed_in), mid_pull = jax.vjp(
@@ -457,7 +478,7 @@
         return product_nt(hidden_low, down_full).astype(BF16)
 
     feed_chunks, feed_parts = plan.team_map(feed_low, forward_chunk)
-    feed_out = plan.team_scatter(feed_parts)
+    feed_out = plan.team_far(plan.team_near(plan.core_sums(feed_parts)))
 
     resid_two, after_pull = jax.vjp(after_feed, resid_one, feed_out, norm_after)
     resid_low = resid_two.astype(BF16)
@@ -476,6 +497,11 @@
     d_resid_two = d_resid_two + product_nt(d_side_pre_low, side_gate_full)
     d_resid_one, d_feed_out, grad_norm_after = after_pull(d_resid_two)
 
+    d_out_low = d_feed_out.astype(BF16)
+    side_spread = product(jnp.concatenate([resid_low, d_side_out_low], axis=0), to_spread).astype(BF16)
+    side_sum = plan.spread_begin(
+        [(side_spread[:rows], d_side_pre_low), (side_spread[rows:], side_low)]
+    )
     d_gate_chunks = []
     d_up_chunks = []
 
@@ -486,14 +512,11 @@
         part = product_nt(d_gate_chunks[-1], gate_full) + product_nt(d_up_chunks[-1], up_full)
         return part.astype(BF16)
 
-    d_out_chunks, d_feed_parts = plan.team_map(d_feed_out.astype(BF16), backward_chunk)
-    d_gate_chunks, d_up_chunks, feed_chunks, d_out_chunks, hidden_chunks, d_feed_parts = together(
-        d_gate_chunks, d_up_chunks, feed_chunks, d_out_chunks, hidden_chunks, d_feed_parts
-    )
-    d_feed_in = plan.team_scatter(d_feed_parts)
-
-    feed_all = jnp.concatenate(feed_chunks, axis=0)
-    d_out_all = jnp.concatenate(d_out_chunks, axis=0)
+    d_out_chunks, d_feed_parts = plan.team_map(d_out_low, backward_chunk)
+    d_feed_sums = plan.core_sums(d_feed_parts)
+    d_gate_chunks, d_up_chunks, feed_chunks, d_out_chunks, hidden_chunks, d_feed_sums = together(
+        d_gate_chunks, d_up_chunks, feed_chunks, d_out_chunks, hidden_chunks, d_feed_sums
+    )
     far_count = 2 ** len(plan.far)
 
     def far_terms(left, right):
@@ -504,11 +527,21 @@
             for at in range(far_count)
         ]
 
+    feed_all = jnp.concatenate(feed_chunks, axis=0)
     gate_terms = far_terms(feed_all, d_gate_chunks)
+    d_feed_sums = plan.team_near(d_feed_sums)
+    d_feed_sums, d_up_chunks, feed_all, gate_terms = together(
+        d_feed_sums, d_up_chunks, feed_all, gate_terms
+    )
     up_terms = far_terms(feed_all, d_up_chunks)
-    down_terms = far_terms(d_out_all, hidden_chunks)
     gate_terms = plan.fold(gate_terms, plan.far_dp)
-    d_feed_in, gate_terms, up_terms, down_terms = together(d_feed_in, gate_terms, up_terms, down_terms)
+    d_feed_in = plan.team_far(d_feed_sums)
+    d_feed_in, up_terms, hidden_chunks, side_sum = together(
+        d_feed_in, up_terms, hidden_chunks, side_sum
+    )
+    steps = tuple(reversed(plan.order))
+    side_sum = plan.spread_step(side_sum, steps[:1])
+    down_terms = far_terms(jnp.concatenate(d_out_chunks, axis=0), hidden_chunks)
 
     (
         d_inputs,
@@ -524,20 +557,10 @@
     d_attn_spread = product(d_attn_low, to_spread).astype(BF16)
     d_attended_low = product_split(d_attn_spread, output_full).astype(BF16)
     d_latent_low = product(d_laurel_low, right_full).astype(BF16)
-    spread = jnp.concatenate([d_laurel_low, resid_low, d_side_out_low], axis=0)
-    spread = product(spread, to_spread).astype(BF16)
-    output_sum = plan.spread_begin(
-        [
-            (d_attn_spread, attended_low),
-            (spread[:rows], latent_low),
-            (spread[rows : 2 * rows], d_side_pre_low),
-            (spread[2 * rows :], side_low),
-        ]
-    )
-    d_attended_low, output_sum, gate_terms, up_terms = together(
-        d_attended_low, output_sum, gate_terms, up_terms
-    )
-    steps = tuple(reversed(plan.order))
+    output_sum = plan.spread_begin([(d_attn_spread, attended_low)])
+    d_attended_low, output_sum, gate_terms, up_terms, down_terms = together(
+        d_attended_low, output_sum, gate_terms, up_terms, down_terms
+    )
     output_sum = plan.spread_step(output_sum, steps[:1])
     gate_terms = plan.fold(gate_terms, plan.far_seq)
     up_terms = plan.fold(up_terms, plan.far_dp)
@@ -551,9 +574,10 @@
     d_keys_all = jnp.einsum(
         "bkgts,btkgd->bskd", d_scores_low, query_group, preferred_element_type=F32
     )
-    d_keys_all, d_values_all, d_query_rot, gate_terms, up_terms, down_terms = together(
-        d_keys_all, d_values_all, d_query_rot, gate_terms, up_terms, down_terms
-    )
+    d_keys_all, d_values_all, d_query_rot, gate_terms, up_terms, down_terms, output_sum, side_sum = together(
+        d_keys_all, d_values_all, d_query_rot, gate_terms, up_terms, down_terms, output_sum, side_sum
+    )
+    output_sum = jnp.concatenate([output_sum, side_sum], axis=1)
     up_terms = plan.fold(up_terms, plan.far_seq)
     down_terms = plan.fold(down_terms, plan.far_dp)
     if whole_sequence:
@@ -576,13 +600,12 @@
     )
     d_queries_low = d_queries.reshape(rows, -1).astype(BF16)
     query_sum = plan.spread_begin([(normed_spread, d_queries_low)])
-    d_keys, d_values, output_sum, query_sum, up_terms, down_terms = together(
-        d_keys, d_values, output_sum, query_sum, up_terms, down_terms
+    d_keys, d_values, query_sum, output_sum, up_terms, down_terms = together(
+        d_keys, d_values, query_sum, output_sum, up_terms, down_terms
     )
     query_sum = plan.spread_step(query_sum, steps[:1])
     down_terms = plan.fold(down_terms, plan.far_seq)
-    grad_gate, grad_up = plan.own_rows(gate_terms + up_terms, local_rows)
-    (grad_down,) = plan.own_rows(down_terms, local_rows)
+    grad_gate, grad_up, grad_down = plan.own_rows(gate_terms + up_terms + down_terms, local_rows)
     d_kvl_low = jnp.concatenate(
         [
             d_keys.reshape(rows, -1).astype(BF16),
@@ -591,7 +614,8 @@
         ],
         axis=1,
     )
-    kvl_sum = plan.spread_begin([(normed_spread, d_kvl_low)])
+    laurel_spread = product(d_laurel_low, to_spread).astype(BF16)
+    kvl_sum = plan.spread_begin([(normed_spread, d_kvl_low), (laurel_spread, latent_low)])
     d_spread = product_nt_split(d_queries_low, query_full) + product_nt_split(d_kvl_low, kvl_full)
     d_normed = d_normed + reorder(d_spread, to_spread)
     d_inputs_norm, grad_norm_input = pre_pull(d_normed)
@@ -610,12 +634,14 @@
     gain_grads = jnp.concatenate(
         [plan.from_far_team(norm_grads).reshape(-1), grad_norm_query, grad_norm_key]
     )
-    gain_grads, kvl_sum, grad_gate, grad_up = together(gain_grads, kvl_sum, grad_gate, grad_up)
+    gain_grads, kvl_sum = together(gain_grads, kvl_sum)
     grad_query = plan.spread_step(query_sum, steps[1:])
-    grad_output, grad_right, grad_side_gate, grad_side_output = split_columns(
-        plan.spread_step(output_sum, steps[1:]), [output_weight.shape[1]] + rest_widths
-    )
-    grad_key, grad_value, grad_left = split_columns(plan.spread_step(kvl_sum, steps), kvl_widths)
+    grad_output, grad_side_gate, grad_side_output = split_columns(
+        plan.spread_step(output_sum, steps[1:]), rest_widths
+    )
+    grad_key, grad_value, grad_left, grad_right = split_columns(
+        plan.spread_step(kvl_sum, steps), kvl_widths
+    )
     gain_grads = plan.total(gain_grads)
     gain_parts = split_columns(gain_grads, [width] * 6 + [head_size] * 2)
     return (

time: 1330 us -> 1280 us (0.962)
  local copies, waits for them, and re-layouts: 232 us -> 189 us
  waiting for transfers between devices: 594 us -> 563 us
    ppermute x94 -> x96, waiting for transfers between devices: 593 us -> 562 us  [swap(): return lax.ppermute(value, axis, [(0, 1), (1, 0)])]
    concatenate x6 -> x2, local copies, waits for them, and re-layouts: 28.1 us -> 2.3 us  [the longest x1 1.54 us: body(): down_terms = far_terms(jnp.concatenate(d_out_chunks, axis=0), hidden_chunks)]
    ppermute x6 -> x0, local copies, waits for them, and re-layouts: 20.2 us -> none  [swap(): return lax.ppermute(value, axis, [(0, 1), (1, 0)])]
    optimization_barrier x4 -> x1, local copies, waits for them, and re-layouts: 18.3 us -> 2.07 us  [together(): return lax.optimization_barrier(values)]
    ppermute x94 -> x96, starting transfers between devices: 77.4 us -> 87.6 us  [swap(): return lax.ppermute(value, axis, [(0, 1), (1, 0)])]
    dot_general x32 -> x33, matrix products: 89.6 us -> 97.7 us  [product(): return jnp.dot(left, right, preferred_element_type=F32)]
    unnamed x575 -> x520, local copies, waits for them, and re-layouts: 78.5 us -> 84.3 us
  transfers between devices with their start and end apart: 97 -> 98, of which waited for: 45 -> 42; matrix products, arithmetic and copies ran while one was open for 31% -> 33% of each run, Pallas kernels for 0% -> 0%
where the time goes in v6:
time: 1280 us; the launch traced here: 1270 us
  waiting for transfers between devices  563 us (44%)
  matrix products  281 us (22%)
  local copies, waits for them, and re-layouts  189 us (15%)
  other arithmetic  136 us (11%)
  starting transfers between devices  97.7 us (8%)
    ppermute x96, waiting for transfers between devices, swap(): return lax.ppermute(value, axis, [(0, 1), (1, 0)])  562 us
    dot_general x33, matrix products, product(): return jnp.dot(left, right, preferred_element_type=F32)  97.7 us
    dot_general x31, matrix products, product_nt(): lax.dot_general(left, right, (((1,), (1,)), ((), ())), preferred_element_...  97.6 us
    ppermute x96, starting transfers between devices, swap(): return lax.ppermute(value, axis, [(0, 1), (1, 0)])  87.6 us
    unnamed x520, local copies, waits for them, and re-layouts  84.3 us
    dot_general x24, matrix products, product_tn(): lax.dot_general(left, right, (((0,), (0,)), ((), ())), preferred_element_...  66.3 us
  transfers between devices with their start and end apart: 98, of which 42 were waited for; matrix products, arithmetic and copies ran while one was open for 33% of the time, Pallas kernels for 0%

profile of v6, /device:TPU:0, one launch (start us, length us, event | category | flops | bytes accessed | tf_op | source)
XLA Modules:
  0.0 1272.3 jit_solution(16032922308807383070)
XLA Ops:
  7.9 5.4 all-to-all-start
  18.8 45.1 %collective-permute-done = bf16[64,5760]{1,0:T(8,128)(2,1)} collective-permute-done((bf16[64,5760]{1,0:T(8,128)(2,1)S(1)}, bf16[64,5760]{1,0:T(8,128)(2,1)}, u32[]{:S(2)}, u32[]{:S(2)}) %collective-permute-start) | collective-permute-done | bytes 737312 | tf_op jit(solution)/shard_map/ppermute | solution.py:73
  74.3 5.9 multiply_reduce_fusion.18
  82.4 23.9 %collective-permute-done.1 = bf16[128,5760]{1,0:T(8,128)(2,1)} collective-permute-done((bf16[128,5760]{1,0:T(8,128)(2,1)S(1)}, bf16[128,5760]{1,0:T(8,128)(2,1)}, u32[]{:S(2)}, u32[]{:S(2)}) %collective-permute-start.1) | collective-permute-done | bytes 1474592 | tf_op jit(solution)/shard_map/ppermute | solution.py:73
  107.9 19.3 %collective-permute-done.3 = bf16[512,1024]{1,0:T(8,128)(2,1)S(1)} collective-permute-done((bf16[512,1024]{1,0:T(8,128)(2,1)S(1)}, bf16[512,1024]{1,0:T(8,128)(2,1)S(1)}, u32[]{:S(2)}, u32[]{:S(2)}) %collective-permute-start.3) | collective-permute-done | bytes 1048608 | tf_op jit(solution)/shard_map/ppermute | solution.py:73
  130.2 10.8 collective-permute-done.4
  144.0 5.1 fusion.33
  179.1 38.1 %collective-permute-done.9 = bf16[512,1024]{1,0:T(8,128)(2,1)} collective-permute-done((bf16[512,1024]{1,0:T(8,128)(2,1)}, bf16[512,1024]{1,0:T(8,128)(2,1)}, u32[]{:S(2)}, u32[]{:S(2)}) %collective-permute-start.9) | collective-permute-done | bytes 1048608 | tf_op jit(solution)/shard_map/ppermute | solution.py:73
  251.7 5.6 rev.68
  259.0 49.3 %collective-permute-done.10 = bf16[2,1,2,128,2,256]{5,3,4,2,1,0:T(8,128)(2,1)} collective-permute-done((bf16[2,1,2,128,2,256]{5,3,4,2,1,0:T(8,128)(2,1)}, bf16[2,1,2,128,2,256]{5,3,4,2,1,0:T(8,128)(2,1)}, u32[]{:S(2)}, u32[]{:S(2)}) %collective-permute-start.10) | collective-permute-done | bytes 524320 | tf_op jit(solution)/shard_map/ppermute | solution.py:73
  335.8 14.6 %collective-permute-done.13 = bf16[2,2,2,128,2,256]{5,3,4,2,1,0:T(8,128)(2,1)S(1)} collective-permute-done((bf16[2,2,2,128,2,256]{5,3,4,2,1,0:T(8,128)(2,1)S(1)}, bf16[2,2,2,128,2,256]{5,3,4,2,1,0:T(8,128)(2,1)S(1)}, u32[]{:S(2)}, u32[]{:S(2)}) %collective-permute-start.13) | collective-permute-done | bytes 1048608 | tf_op jit(solution)/shard_map/ppermute | solution.py:73
  372.3 44.0 %collective-permute-done.23 = bf16[512,2560]{1,0:T(8,128)(2,1)} collective-permute-done((bf16[512,2560]{1,0:T(8,128)(2,1)}, bf16[512,2560]{1,0:T(8,128)(2,1)}, u32[]{:S(2)}, u32[]{:S(2)}) %collective-permute-start.23) | collective-permute-done | bytes 2621472 | tf_op jit(solution)/shard_map/ppermute | solution.py:73
  429.9 16.5 %collective-permute-done.21 = bf16[512,1024]{1,0:T(8,128)(2,1)} collective-permute-done((bf16[512,1024]{1,0:T(8,128)(2,1)}, bf16[512,1024]{1,0:T(8,128)(2,1)}, u32[]{:S(2)}, u32[]{:S(2)}) %collective-permute-start.21) | collective-permute-done | bytes 1048608 | tf_op jit(solution)/shard_map/ppermute | solution.py:73
  492.5 13.0 %collective-permute-done.26 = bf16[256,2048]{1,0:T(8,128)(2,1)S(1)} collective-permute-done((bf16[256,2048]{1,0:T(8,128)(2,1)S(1)}, bf16[256,2048]{1,0:T(8,128)(2,1)S(1)}, u32[]{:S(2)}, u32[]{:S(2)}) %collective-permute-start.26) | collective-permute-done | bytes 1048608 | tf_op jit(solution)/shard_map/ppermute | solution.py:73
  508.9 10.2 collective-permute-done.34
  552.8 11.1 collective-permute-done.42
  571.4 17.2 %collective-permute-done.43 = bf16[256,2048]{1,0:T(8,128)(2,1)S(1)} collective-permute-done((bf16[256,2048]{1,0:T(8,128)(2,1)S(1)}, bf16[256,2048]{1,0:T(8,128)(2,1)S(1)}, u32[]{:S(2)}, u32[]{:S(2)}) %collective-permute-start.43) | collective-permute-done | bytes 1048608 | tf_op jit(solution)/shard_map/ppermute | solution.py:73
  603.8 5.2 fusion.27
  614.7 7.4 fusion.32
  622.1 5.1 multiply_convert_fusion.3
  659.3 6.0 add_convert_fusion.7
  667.5 5.6 multiply_convert_fusion.1
  677.5 5.8 add_convert_fusion.6
  686.5 5.3 multiply_convert_fusion
  691.8 6.6 fusion.315
  698.4 6.2 add_convert_fusion.5
  719.4 5.0 fusion.158
  724.4 4.9 fusion.161
  729.3 4.9 fusion.164
  743.7 4.9 fusion.167
  770.7 12.9 %collective-permute-done.59 = bf16[256,2048]{1,0:T(8,128)(2,1)S(1)} collective-permute-done((bf16[256,2048]{1,0:T(8,128)(2,1)S(1)}, bf16[256,2048]{1,0:T(8,128)(2,1)S(1)}, u32[]{:S(2)}, u32[]{:S(2)}) %collective-permute-start.59) | collective-permute-done | bytes 1048608 | tf_op jit(solution)/shard_map/ppermute | solution.py:73
  792.6 5.4 fusion.34
  849.3 6.1 add_convert_fusion.1
  857.5 5.3 fusion.11
  862.8 6.2 convolution_bitcast_fusion
  881.9 34.8 %collective-permute-done.64 = bf16[512,1024]{1,0:T(8,128)(2,1)S(1)} collective-permute-done((bf16[512,1024]{1,0:T(8,128)(2,1)S(1)}, bf16[512,1024]{1,0:T(8,128)(2,1)S(1)}, u32[]{:S(2)}, u32[]{:S(2)}) %collective-permute-start.64) | collective-permute-done | bytes 1048608 | tf_op jit(solution)/shard_map/ppermute | solution.py:73
  976.2 24.8 %collective-permute-done.69 = bf16[2,2,2,128,2,256]{5,3,4,2,1,0:T(8,128)(2,1)} collective-permute-done((bf16[2,2,2,128,2,256]{5,3,4,2,1,0:T(8,128)(2,1)}, bf16[2,2,2,128,2,256]{5,3,4,2,1,0:T(8,128)(2,1)}, u32[]{:S(2)}, u32[]{:S(2)}) %collective-permute-start.69) | collective-permute-done | bytes 1048608 | tf_op jit(solution)/shard_map/ppermute | solution.py:73
  1010.1 6.0 collective-permute-done.72
  1024.7 20.0 %collective-permute-done.73 = bf16[2,2,128,2,256]{4,2,3,1,0:T(8,128)(2,1)S(1)} collective-permute-done((bf16[2,2,128,2,256]{4,2,3,1,0:T(8,128)(2,1)S(1)}, bf16[2,2,128,2,256]{4,2,3,1,0:T(8,128)(2,1)S(1)}, u32[]{:S(2)}, u32[]{:S(2)}) %collective-permute-start.73) | collective-permute-done | bytes 524320 | tf_op jit(solution)/shard_map/ppermute | solution.py:73
  1058.5 4.9 fusion.2
  1079.8 6.4 fusion.7
  1090.7 36.7 %collective-permute-done.90 = bf16[512,1024]{1,0:T(8,128)(2,1)} collective-permute-done((bf16[512,1024]{1,0:T(8,128)(2,1)}, bf16[512,1024]{1,0:T(8,128)(2,1)}, u32[]{:S(2)}, u32[]{:S(2)}) %collective-permute-start.90) | collective-permute-done | bytes 1048608 | tf_op jit(solution)/shard_map/ppermute | solution.py:73
  1136.9 4.7 all-to-all-start.1
  1143.5 6.1 collective-permute-done.88
  1157.7 47.2 %collective-permute-done.93 = f32[12800]{0:T(1024)S(1)} collective-permute-done((f32[12800]{0:T(1024)S(1)}, f32[12800]{0:T(1024)S(1)}, u32[]{:S(2)}, u32[]{:S(2)}) %collective-permute-start.93) | collective-permute-done | bytes 51232 | tf_op jit(solution)/shard_map/ppermute | solution.py:73
  1218.9 9.0 collective-permute-done.84
  1229.9 4.8 collective-permute-start.81
  1240.3 10.5 collective-permute-done.81
  (1071 shorter events, 607.6 us)
Async XLA Ops:
  7.9 58.2 %all-to-all-start = ((bf16[8,192,1024]{2,1,0:T(8,128)(2,1)}), bf16[8,192,1024]{2,1,0:T(8,128)(2,1)}, u32[]{:S(2)}, u32[]{:S(2)}) async-start(bf16[8,192,1024]{2,1,0:T(8,128)(2,1)} %copy.424), calls=%async_computation | async-start | bytes 6291456 | tf_op jit(solution)/shard_map/all_to_all | solution.py:335
  14.1 49.8 %collective-permute-start = (bf16[64,5760]{1,0:T(8,128)(2,1)S(1)}, bf16[64,5760]{1,0:T(8,128)(2,1)}, u32[]{:S(2)}, u32[]{:S(2)}) collective-permute-start(bf16[64,5760]{1,0:T(8,128)(2,1)S(1)} %concatenate.197), channel_id=1, source_target_pairs={{0,16},{16,0},{1,17},{17,1},{2,18},{18,2},{3,19},{19,3},{4,20},{20... | collective-permute-start | bytes 2211848 | tf_op jit(solution)/shard_map/ppermute | solution.py:73
  69.7 36.6 %collective-permute-start.1 = (bf16[128,5760]{1,0:T(8,128)(2,1)S(1)}, bf16[128,5760]{1,0:T(8,128)(2,1)}, u32[]{:S(2)}, u32[]{:S(2)}) collective-permute-start(bf16[128,5760]{1,0:T(8,128)(2,1)S(1)} %pad_maximum_fusion.13), channel_id=1, source_target_pairs={{0,8},{8,0},{1,9},{9,1},{2,10},{10,2},{3,11},{11,3},{4,12},{12,4},... | collective-permute-start | bytes 4423688 | tf_op jit(solution)/shard_map/ppermute | solution.py:73
  81.8 45.4 %collective-permute-start.3 = (bf16[512,1024]{1,0:T(8,128)(2,1)S(1)}, bf16[512,1024]{1,0:T(8,128)(2,1)S(1)}, u32[]{:S(2)}, u32[]{:S(2)}) collective-permute-start(bf16[512,1024]{1,0:T(8,128)(2,1)S(1)} %bitcast.466), channel_id=1, source_target_pairs={{0,2},{2,0},{1,3},{3,1},{4,6},{6,4},{5,7},{7,5},{8,10},{10,8},{9,1... | collective-permute-start | bytes 3145736 | tf_op jit(solution)/shard_map/ppermute | solution.py:73
  163.2 54.0 %collective-permute-start.6 = (bf16[512,1152]{1,0:T(8,128)(2,1)S(1)}, bf16[512,1152]{1,0:T(8,128)(2,1)S(1)}, u32[]{:S(2)}, u32[]{:S(2)}) collective-permute-start(bf16[512,1152]{1,0:T(8,128)(2,1)S(1)} %pad_maximum_fusion.14), channel_id=1, source_target_pairs={{0,1},{1,0},{2,3},{3,2},{4,5},{5,4},{6,7},{7,6},{8,9},{9,8},{10,11... | collective-permute-start | bytes 3538952 | tf_op jit(solution)/shard_map/ppermute | solution.py:73
  166.6 50.6 %collective-permute-start.7 = (bf16[512,1152]{1,0:T(8,128)(2,1)}, bf16[512,1152]{1,0:T(8,128)(2,1)S(1)}, u32[]{:S(2)}, u32[]{:S(2)}) collective-permute-start(bf16[512,1152]{1,0:T(8,128)(2,1)} %collective-permute-done.5), channel_id=1, source_target_pairs={{0,1},{1,0},{2,3},{3,2},{4,5},{5,4},{6,7},{7,6},{8,9},{9,8},{10,11... | collective-permute-start | bytes 3538952 | tf_op jit(solution)/shard_map/ppermute | solution.py:73
  167.9 49.3 %collective-permute-start.9 = (bf16[512,1024]{1,0:T(8,128)(2,1)}, bf16[512,1024]{1,0:T(8,128)(2,1)}, u32[]{:S(2)}, u32[]{:S(2)}) collective-permute-start(bf16[512,1024]{1,0:T(8,128)(2,1)} %bitcast.468), channel_id=1, source_target_pairs={{0,16},{16,0},{1,17},{17,1},{2,18},{18,2},{3,19},{19,3},{4,20},{20... | collective-permute-start | bytes 3145736 | tf_op jit(solution)/shard_map/ppermute | solution.py:73
  234.0 123.8 %collective-permute-start.18 = (bf16[512,2048]{1,0:T(8,128)(2,1)}, bf16[512,2048]{1,0:T(8,128)(2,1)}, u32[]{:S(2)}, u32[]{:S(2)}) collective-permute-start(bf16[512,2048]{1,0:T(8,128)(2,1)} %pad_maximum_fusion.6), channel_id=1, source_target_pairs={{0,1},{1,0},{2,3},{3,2},{4,5},{5,4},{6,7},{7,6},{8,9},{9,8},{10,11... | collective-permute-start | bytes 6291464 | tf_op jit(solution)/shard_map/ppermute | solution.py:73
  234.0 92.2 %collective-permute-start.17 = (bf16[512,2048]{1,0:T(8,128)(2,1)}, bf16[512,2048]{1,0:T(8,128)(2,1)}, u32[]{:S(2)}, u32[]{:S(2)}) collective-permute-start(bf16[512,2048]{1,0:T(8,128)(2,1)} %pad_maximum_fusion.6), channel_id=1, source_target_pairs={{0,4},{4,0},{1,5},{5,1},{2,6},{6,2},{3,7},{7,3},{8,12},{12,8},{9,1... | collective-permute-start | bytes 6291464 | tf_op jit(solution)/shard_map/ppermute | solution.py:73
  238.7 70.9 %collective-permute-start.11 = (bf16[512,1024]{1,0:T(8,128)(2,1)}, bf16[512,1024]{1,0:T(8,128)(2,1)}, u32[]{:S(2)}, u32[]{:S(2)}) collective-permute-start(bf16[512,1024]{1,0:T(8,128)(2,1)} %bitcast.465), channel_id=1, source_target_pairs={{0,16},{16,0},{1,17},{17,1},{2,18},{18,2},{3,19},{19,3},{4,20},{20... | collective-permute-start | bytes 3145736 | tf_op jit(solution)/shard_map/ppermute | solution.py:73
  241.7 66.5 %collective-permute-start.10 = (bf16[2,1,2,128,2,256]{5,3,4,2,1,0:T(8,128)(2,1)}, bf16[2,1,2,128,2,256]{5,3,4,2,1,0:T(8,128)(2,1)}, u32[]{:S(2)}, u32[]{:S(2)}) collective-permute-start(bf16[2,1,2,128,2,256]{5,3,4,2,1,0:T(8,128)(2,1)} %maximum_bitcast_fusion), channel_id=1, source_target_pairs={{0,16},{16,0},{1,17},{17,1},{2,18},{18,2},{3,19},{19,3},{4,20},{20... | collective-permute-start | bytes 1572872 | tf_op jit(solution)/shard_map/ppermute | solution.py:73
  257.4 71.9 %collective-permute-start.16 = (bf16[256,2560]{1,0:T(8,128)(2,1)S(1)}, bf16[256,2560]{1,0:T(8,128)(2,1)}, u32[]{:S(2)}, u32[]{:S(2)}) collective-permute-start(bf16[256,2560]{1,0:T(8,128)(2,1)S(1)} %copy-done.41), channel_id=1, source_target_pairs={{0,2},{2,0},{1,3},{3,1},{4,6},{6,4},{5,7},{7,5},{8,10},{10,8},{9,1... | collective-permute-start | bytes 3932168 | tf_op jit(solution)/shard_map/ppermute | solution.py:73
  326.2 38.1 %collective-permute-start.19 = (bf16[512,2048]{1,0:T(8,128)(2,1)}, bf16[512,2048]{1,0:T(8,128)(2,1)S(1)}, u32[]{:S(2)}, u32[]{:S(2)}) collective-permute-start(bf16[512,2048]{1,0:T(8,128)(2,1)} %collective-permute-done.17), channel_id=1, source_target_pairs={{0,1},{1,0},{2,3},{3,2},{4,5},{5,4},{6,7},{7,6},{8,9},{9,8},{10,11... | collective-permute-start | bytes 6291464 | tf_op jit(solution)/shard_map/ppermute | solution.py:73
  329.3 90.7 %collective-permute-start.20 = (bf16[512,1024]{1,0:T(8,128)(2,1)}, bf16[512,1024]{1,0:T(8,128)(2,1)}, u32[]{:S(2)}, u32[]{:S(2)}) collective-permute-start(bf16[512,1024]{1,0:T(8,128)(2,1)} %collective-permute-done.9), channel_id=1, source_target_pairs={{0,2},{2,0},{1,3},{3,1},{4,6},{6,4},{5,7},{7,5},{8,10},{10,8},{9,1... | collective-permute-start | bytes 3145736 | tf_op jit(solution)/shard_map/ppermute | solution.py:73
  350.4 95.9 %collective-permute-start.22 = (bf16[512,1024]{1,0:T(8,128)(2,1)}, bf16[512,1024]{1,0:T(8,128)(2,1)}, u32[]{:S(2)}, u32[]{:S(2)}) collective-permute-start(bf16[512,1024]{1,0:T(8,128)(2,1)} %bitcast.10), channel_id=1, source_target_pairs={{0,2},{2,0},{1,3},{3,1},{4,6},{6,4},{5,7},{7,5},{8,10},{10,8},{9,1... | collective-permute-start | bytes 3145736 | tf_op jit(solution)/shard_map/ppermute | solution.py:73
  353.5 75.0 %collective-permute-start.29 = (bf16[512,1024]{1,0:T(8,128)(2,1)}, bf16[512,1024]{1,0:T(8,128)(2,1)}, u32[]{:S(2)}, u32[]{:S(2)}) collective-permute-start(bf16[512,1024]{1,0:T(8,128)(2,1)} %bitcast.10), channel_id=1, source_target_pairs={{0,16},{16,0},{1,17},{17,1},{2,18},{18,2},{3,19},{19,3},{4,20},{20... | collective-permute-start | bytes 3145736 | tf_op jit(solution)/shard_map/ppermute | solution.py:73
  357.7 58.6 %collective-permute-start.23 = (bf16[512,2560]{1,0:T(8,128)(2,1)}, bf16[512,2560]{1,0:T(8,128)(2,1)}, u32[]{:S(2)}, u32[]{:S(2)}) collective-permute-start(bf16[512,2560]{1,0:T(8,128)(2,1)} %pad_maximum_fusion.3), channel_id=1, source_target_pairs={{0,4},{4,0},{1,5},{5,1},{2,6},{6,2},{3,7},{7,3},{8,12},{12,8},{9,1... | collective-permute-start | bytes 7864328 | tf_op jit(solution)/shard_map/ppermute | solution.py:73
  364.3 86.8 %collective-permute-start.24 = (bf16[512,2560]{1,0:T(8,128)(2,1)}, bf16[512,2560]{1,0:T(8,128)(2,1)}, u32[]{:S(2)}, u32[]{:S(2)}) collective-permute-start(bf16[512,2560]{1,0:T(8,128)(2,1)} %pad_maximum_fusion.3), channel_id=1, source_target_pairs={{0,1},{1,0},{2,3},{3,2},{4,5},{5,4},{6,7},{7,6},{8,9},{9,8},{10,11... | collective-permute-start | bytes 7864328 | tf_op jit(solution)/shard_map/ppermute | solution.py:73
  416.4 37.0 %collective-permute-start.25 = (bf16[512,2560]{1,0:T(8,128)(2,1)}, bf16[512,2560]{1,0:T(8,128)(2,1)}, u32[]{:S(2)}, u32[]{:S(2)}) collective-permute-start(bf16[512,2560]{1,0:T(8,128)(2,1)} %collective-permute-done.23), channel_id=1, source_target_pairs={{0,1},{1,0},{2,3},{3,2},{4,5},{5,4},{6,7},{7,6},{8,9},{9,8},{10,11... | collective-permute-start | bytes 7864328 | tf_op jit(solution)/shard_map/ppermute | solution.py:73
  428.5 49.5 %collective-permute-start.30 = (bf16[512,1024]{1,0:T(8,128)(2,1)}, bf16[512,1024]{1,0:T(8,128)(2,1)S(1)}, u32[]{:S(2)}, u32[]{:S(2)}) collective-permute-start(bf16[512,1024]{1,0:T(8,128)(2,1)} %collective-permute-done.29), channel_id=1, source_target_pairs={{0,2},{2,0},{1,3},{3,1},{4,6},{6,4},{5,7},{7,5},{8,10},{10,8},{9,1... | collective-permute-start | bytes 3145736 | tf_op jit(solution)/shard_map/ppermute | solution.py:73
  508.7 62.7 %collective-permute-start.31 = (bf16[256,2048]{1,0:T(8,128)(2,1)S(1)}, bf16[256,2048]{1,0:T(8,128)(2,1)S(1)}, u32[]{:S(2)}, u32[]{:S(2)}) collective-permute-start(bf16[256,2048]{1,0:T(8,128)(2,1)S(1)} %slice.593), channel_id=1, source_target_pairs={{0,1},{1,0},{2,3},{3,2},{4,5},{5,4},{6,7},{7,6},{8,9},{9,8},{10,11... | collective-permute-start | bytes 3145736 | tf_op jit(solution)/shard_map/ppermute | solution.py:73
  601.4 30.5 %collective-permute-start.45 = (bf16[256,2048]{1,0:T(8,128)(2,1)S(1)}, bf16[256,2048]{1,0:T(8,128)(2,1)}, u32[]{:S(2)}, u32[]{:S(2)}) collective-permute-start(bf16[256,2048]{1,0:T(8,128)(2,1)S(1)} %fusion.68), channel_id=1, source_target_pairs={{0,4},{4,0},{1,5},{5,1},{2,6},{6,2},{3,7},{7,3},{8,12},{12,8},{9,1... | collective-permute-start | bytes 3145736 | tf_op jit(solution)/shard_map/ppermute | solution.py:73
  602.0 30.1 %collective-permute-start.46 = (bf16[256,2048]{1,0:T(8,128)(2,1)S(1)}, bf16[256,2048]{1,0:T(8,128)(2,1)}, u32[]{:S(2)}, u32[]{:S(2)}) collective-permute-start(bf16[256,2048]{1,0:T(8,128)(2,1)S(1)} %fusion.68), channel_id=1, source_target_pairs={{0,8},{8,0},{1,9},{9,1},{2,10},{10,2},{3,11},{11,3},{4,12},{12,4},... | collective-permute-start | bytes 3145736 | tf_op jit(solution)/shard_map/ppermute | solution.py:73
  641.0 42.6 %collective-permute-start.52 = (bf16[256,2048]{1,0:T(8,128)(2,1)S(1)}, bf16[256,2048]{1,0:T(8,128)(2,1)S(1)}, u32[]{:S(2)}, u32[]{:S(2)}) collective-permute-start(bf16[256,2048]{1,0:T(8,128)(2,1)S(1)} %slice.617), channel_id=1, source_target_pairs={{0,1},{1,0},{2,3},{3,2},{4,5},{5,4},{6,7},{7,6},{8,9},{9,8},{10,11... | collective-permute-start | bytes 3145736 | tf_op jit(solution)/shard_map/ppermute | solution.py:73
  649.0 35.0 %collective-permute-start.51 = (bf16[256,2048]{1,0:T(8,128)(2,1)S(1)}, bf16[256,2048]{1,0:T(8,128)(2,1)S(1)}, u32[]{:S(2)}, u32[]{:S(2)}) collective-permute-start(bf16[256,2048]{1,0:T(8,128)(2,1)S(1)} %pad_maximum_fusion.22), channel_id=1, source_target_pairs={{0,1},{1,0},{2,3},{3,2},{4,5},{5,4},{6,7},{7,6},{8,9},{9,8},{10,11... | collective-permute-start | bytes 3145736 | tf_op jit(solution)/shard_map/ppermute | solution.py:73
  665.4 39.9 %collective-permute-start.53 = (bf16[256,2048]{1,0:T(8,128)(2,1)S(1)}, bf16[256,2048]{1,0:T(8,128)(2,1)}, u32[]{:S(2)}, u32[]{:S(2)}) collective-permute-start(bf16[256,2048]{1,0:T(8,128)(2,1)S(1)} %slice.774), channel_id=1, source_target_pairs={{0,1},{1,0},{2,3},{3,2},{4,5},{5,4},{6,7},{7,6},{8,9},{9,8},{10,11... | collective-permute-start | bytes 3145736 | tf_op jit(solution)/shard_map/ppermute | solution.py:73
  761.9 52.2 %collective-permute-start.62 = (bf16[512,1024]{1,0:T(8,128)(2,1)}, bf16[512,1024]{1,0:T(8,128)(2,1)}, u32[]{:S(2)}, u32[]{:S(2)}) collective-permute-start(bf16[512,1024]{1,0:T(8,128)(2,1)} %fusion.161), channel_id=1, source_target_pairs={{0,2},{2,0},{1,3},{3,1},{4,6},{6,4},{5,7},{7,5},{8,10},{10,8},{9,1... | collective-permute-start | bytes 3145736 | tf_op jit(solution)/shard_map/ppermute | solution.py:73
  763.0 57.8 %collective-permute-start.63 = (bf16[512,1024]{1,0:T(8,128)(2,1)}, bf16[512,1024]{1,0:T(8,128)(2,1)}, u32[]{:S(2)}, u32[]{:S(2)}) collective-permute-start(bf16[512,1024]{1,0:T(8,128)(2,1)} %fusion.167), channel_id=1, source_target_pairs={{0,2},{2,0},{1,3},{3,1},{4,6},{6,4},{5,7},{7,5},{8,10},{10,8},{9,1... | collective-permute-start | bytes 3145736 | tf_op jit(solution)/shard_map/ppermute | solution.py:73
  801.4 48.0 %collective-permute-start.61 = (bf16[1024,2048]{1,0:T(8,128)(2,1)}, bf16[1024,2048]{1,0:T(8,128)(2,1)}, u32[]{:S(2)}, u32[]{:S(2)}) collective-permute-start(bf16[1024,2048]{1,0:T(8,128)(2,1)} %convolution_convert_fusion.3), channel_id=1, source_target_pairs={{0,1},{1,0},{2,3},{3,2},{4,5},{5,4},{6,7},{7,6},{8,9},{9,8},{10,11... | collective-permute-start | bytes 12582920 | tf_op jit(solution)/shard_map/ppermute | solution.py:73
  803.4 43.9 %collective-permute-start.68 = (bf16[512,512]{0,1:T(8,128)(2,1)}, bf16[512,512]{0,1:T(8,128)(2,1)}, u32[]{:S(2)}, u32[]{:S(2)}) collective-permute-start(bf16[512,512]{0,1:T(8,128)(2,1)} %slice.655), channel_id=1, source_target_pairs={{0,4},{4,0},{1,5},{5,1},{2,6},{6,2},{3,7},{7,3},{8,12},{12,8},{9,1... | collective-permute-start | bytes 1572872 | tf_op jit(solution)/shard_map/ppermute | solution.py:73
  868.9 47.7 %collective-permute-start.64 = (bf16[512,1024]{1,0:T(8,128)(2,1)S(1)}, bf16[512,1024]{1,0:T(8,128)(2,1)S(1)}, u32[]{:S(2)}, u32[]{:S(2)}) collective-permute-start(bf16[512,1024]{1,0:T(8,128)(2,1)S(1)} %copy-done.99), channel_id=1, source_target_pairs={{0,16},{16,0},{1,17},{17,1},{2,18},{18,2},{3,19},{19,3},{4,20},{20... | collective-permute-start | bytes 3145736 | tf_op jit(solution)/shard_map/ppermute | solution.py:73
  870.3 47.8 %collective-permute-start.65 = (bf16[512,1024]{1,0:T(8,128)(2,1)S(1)}, bf16[512,1024]{1,0:T(8,128)(2,1)S(1)}, u32[]{:S(2)}, u32[]{:S(2)}) collective-permute-start(bf16[512,1024]{1,0:T(8,128)(2,1)S(1)} %copy-done.213), channel_id=1, source_target_pairs={{0,2},{2,0},{1,3},{3,1},{4,6},{6,4},{5,7},{7,5},{8,10},{10,8},{9,1... | collective-permute-start | bytes 3145736 | tf_op jit(solution)/shard_map/ppermute | solution.py:73
  871.6 47.8 %collective-permute-start.66 = (bf16[512,1024]{1,0:T(8,128)(2,1)}, bf16[512,1024]{1,0:T(8,128)(2,1)S(1)}, u32[]{:S(2)}, u32[]{:S(2)}) collective-permute-start(bf16[512,1024]{1,0:T(8,128)(2,1)} %fusion.150), channel_id=1, source_target_pairs={{0,2},{2,0},{1,3},{3,1},{4,6},{6,4},{5,7},{7,5},{8,10},{10,8},{9,1... | collective-permute-start | bytes 3145736 | tf_op jit(solution)/shard_map/ppermute | solution.py:73
  872.5 48.3 %collective-permute-start.67 = (bf16[512,2048]{1,0:T(8,128)(2,1)S(1)}, bf16[512,2048]{1,0:T(8,128)(2,1)S(1)}, u32[]{:S(2)}, u32[]{:S(2)}) collective-permute-start(bf16[512,2048]{1,0:T(8,128)(2,1)S(1)} %slice.653), channel_id=1, source_target_pairs={{0,4},{4,0},{1,5},{5,1},{2,6},{6,2},{3,7},{7,3},{8,12},{12,8},{9,1... | collective-permute-start | bytes 6291464 | tf_op jit(solution)/shard_map/ppermute | solution.py:73
  957.3 43.7 %collective-permute-start.69 = (bf16[2,2,2,128,2,256]{5,3,4,2,1,0:T(8,128)(2,1)}, bf16[2,2,2,128,2,256]{5,3,4,2,1,0:T(8,128)(2,1)}, u32[]{:S(2)}, u32[]{:S(2)}) collective-permute-start(bf16[2,2,2,128,2,256]{5,3,4,2,1,0:T(8,128)(2,1)} %bitcast.63), channel_id=1, source_target_pairs={{0,8},{8,0},{1,9},{9,1},{2,10},{10,2},{3,11},{11,3},{4,12},{12,4},... | collective-permute-start | bytes 3145736 | tf_op jit(solution)/shard_map/ppermute | solution.py:73
  957.3 89.2 %collective-permute-start.74 = (bf16[1024,2048]{1,0:T(8,128)(2,1)}, bf16[1024,2048]{1,0:T(8,128)(2,1)}, u32[]{:S(2)}, u32[]{:S(2)}) collective-permute-start(bf16[1024,2048]{1,0:T(8,128)(2,1)} %convolution_convert_fusion.2), channel_id=1, source_target_pairs={{0,1},{1,0},{2,3},{3,2},{4,5},{5,4},{6,7},{7,6},{8,9},{9,8},{10,11... | collective-permute-start | bytes 12582920 | tf_op jit(solution)/shard_map/ppermute | solution.py:73
  957.3 49.4 %collective-permute-start.75 = (bf16[512,1024]{1,0:T(8,128)(2,1)}, bf16[512,1024]{1,0:T(8,128)(2,1)}, u32[]{:S(2)}, u32[]{:S(2)}) collective-permute-start(bf16[512,1024]{1,0:T(8,128)(2,1)} %add_convert_fusion.16), channel_id=1, source_target_pairs={{0,16},{16,0},{1,17},{17,1},{2,18},{18,2},{3,19},{19,3},{4,20},{20... | collective-permute-start | bytes 3145736 | tf_op jit(solution)/shard_map/ppermute | solution.py:73
  959.1 61.4 %collective-permute-start.76 = (bf16[512,1024]{1,0:T(8,128)(2,1)}, bf16[512,1024]{1,0:T(8,128)(2,1)}, u32[]{:S(2)}, u32[]{:S(2)}) collective-permute-start(bf16[512,1024]{1,0:T(8,128)(2,1)} %fusion.173), channel_id=1, source_target_pairs={{0,2},{2,0},{1,3},{3,1},{4,6},{6,4},{5,7},{7,5},{8,10},{10,8},{9,1... | collective-permute-start | bytes 3145736 | tf_op jit(solution)/shard_map/ppermute | solution.py:73
  973.8 49.5 %collective-permute-start.77 = (bf16[512,1024]{1,0:T(8,128)(2,1)S(1)}, bf16[512,1024]{1,0:T(8,128)(2,1)S(1)}, u32[]{:S(2)}, u32[]{:S(2)}) collective-permute-start(bf16[512,1024]{1,0:T(8,128)(2,1)S(1)} %copy-done.212), channel_id=1, source_target_pairs={{0,2},{2,0},{1,3},{3,1},{4,6},{6,4},{5,7},{7,5},{8,10},{10,8},{9,1... | collective-permute-start | bytes 3145736 | tf_op jit(solution)/shard_map/ppermute | solution.py:73
  1069.6 84.0 %collective-permute-start.78 = (bf16[512,2048]{1,0:T(8,128)(2,1)}, bf16[512,2048]{1,0:T(8,128)(2,1)}, u32[]{:S(2)}, u32[]{:S(2)}) collective-permute-start(bf16[512,2048]{1,0:T(8,128)(2,1)} %slice.675), channel_id=1, source_target_pairs={{0,4},{4,0},{1,5},{5,1},{2,6},{6,2},{3,7},{7,3},{8,12},{12,8},{9,1... | collective-permute-start | bytes 6291464 | tf_op jit(solution)/shard_map/ppermute | solution.py:73
  1078.2 53.9 %collective-permute-start.82 = (bf16[1024,1152]{0,1:T(8,128)(2,1)}, bf16[1024,1152]{0,1:T(8,128)(2,1)}, u32[]{:S(2)}, u32[]{:S(2)}) collective-permute-start(bf16[1024,1152]{0,1:T(8,128)(2,1)} %pad_maximum_fusion.5), channel_id=1, source_target_pairs={{0,1},{1,0},{2,3},{3,2},{4,5},{5,4},{6,7},{7,6},{8,9},{9,8},{10,11... | collective-permute-start | bytes 7077896 | tf_op jit(solution)/shard_map/ppermute | solution.py:73
  1078.3 50.7 %collective-permute-start.87 = (bf16[256,2560]{1,0:T(8,128)(2,1)S(1)}, bf16[256,2560]{1,0:T(8,128)(2,1)}, u32[]{:S(2)}, u32[]{:S(2)}) collective-permute-start(bf16[256,2560]{1,0:T(8,128)(2,1)S(1)} %slice.695), channel_id=1, source_target_pairs={{0,2},{2,0},{1,3},{3,1},{4,6},{6,4},{5,7},{7,5},{8,10},{10,8},{9,1... | collective-permute-start | bytes 3932168 | tf_op jit(solution)/shard_map/ppermute | solution.py:73
  1078.9 48.5 %collective-permute-start.90 = (bf16[512,1024]{1,0:T(8,128)(2,1)}, bf16[512,1024]{1,0:T(8,128)(2,1)}, u32[]{:S(2)}, u32[]{:S(2)}) collective-permute-start(bf16[512,1024]{1,0:T(8,128)(2,1)} %add_convert_fusion.13), channel_id=1, source_target_pairs={{0,16},{16,0},{1,17},{17,1},{2,18},{18,2},{3,19},{19,3},{4,20},{20... | collective-permute-start | bytes 3145736 | tf_op jit(solution)/shard_map/ppermute | solution.py:73
  1136.9 122.3 %all-to-all-start.1 = ((bf16[8,192,1024]{2,1,0:T(8,128)(2,1)}), bf16[8,192,1024]{2,1,0:T(8,128)(2,1)}, u32[]{:S(2)}, u32[]{:S(2)}) async-start(bf16[8,192,1024]{2,1,0:T(8,128)(2,1)} %pad_maximum_fusion.1), calls=%async_computation.1 | async-start | bytes 6291456 | tf_op jit(solution)/shard_map/all_to_all | solution.py:212
  1151.1 55.3 %collective-permute-start.89 = (bf16[64,2560]{1,0:T(8,128)(2,1)S(1)}, bf16[64,2560]{1,0:T(8,128)(2,1)S(1)}, u32[]{:S(2)}, u32[]{:S(2)}) collective-permute-start(bf16[64,2560]{1,0:T(8,128)(2,1)S(1)} %slice.838), channel_id=1, source_target_pairs={{0,16},{16,0},{1,17},{17,1},{2,18},{18,2},{3,19},{19,3},{4,20},{20... | collective-permute-start | bytes 983048 | tf_op jit(solution)/shard_map/ppermute | solution.py:73
  1151.5 63.3 %collective-permute-start.83 = (bf16[512,1152]{0,1:T(8,128)(2,1)S(1)}, bf16[512,1152]{0,1:T(8,128)(2,1)S(1)}, u32[]{:S(2)}, u32[]{:S(2)}) collective-permute-start(bf16[512,1152]{0,1:T(8,128)(2,1)S(1)} %slice.685), channel_id=1, source_target_pairs={{0,4},{4,0},{1,5},{5,1},{2,6},{6,2},{3,7},{7,3},{8,12},{12,8},{9,1... | collective-permute-start | bytes 3538952 | tf_op jit(solution)/shard_map/ppermute | solution.py:73
  1153.2 51.7 %collective-permute-start.93 = (f32[12800]{0:T(1024)S(1)}, f32[12800]{0:T(1024)S(1)}, u32[]{:S(2)}, u32[]{:S(2)}) collective-permute-start(f32[12800]{0:T(1024)S(1)} %add.627), channel_id=1, source_target_pairs={{0,4},{4,0},{1,5},{5,1},{2,6},{6,2},{3,7},{7,3},{8,12},{12,8},{9,1... | collective-permute-start | bytes 153608 | tf_op jit(solution)/shard_map/ppermute | solution.py:73
  1156.2 60.8 %collective-permute-start.79 = (bf16[256,2048]{1,0:T(8,128)(2,1)S(1)}, bf16[256,2048]{1,0:T(8,128)(2,1)S(1)}, u32[]{:S(2)}, u32[]{:S(2)}) collective-permute-start(bf16[256,2048]{1,0:T(8,128)(2,1)S(1)} %slice.820), channel_id=1, source_target_pairs={{0,2},{2,0},{1,3},{3,1},{4,6},{6,4},{5,7},{7,5},{8,10},{10,8},{9,1... | collective-permute-start | bytes 3145736 | tf_op jit(solution)/shard_map/ppermute | solution.py:73
  (279 other events, 4145.4 us)

commit v7 on v6

--- a/solution.py
+++ b/solution.py
@@ -108,27 +108,20 @@
     def to_far_team(self, value):
         rows, width = value.shape
         parts = value.reshape((rows,) + (2,) * len(self.every) + (-1,))
-        parts = self.flipped(parts, self.far, [1 + self.every.index(axis) for axis in self.far])
         order = [0] + [1 + self.every.index(axis) for axis in self.canon] + [1 + len(self.every)]
         return parts.transpose(order).reshape(rows, width)
 
     def from_far_team(self, value):
         rows, width = value.shape
         parts = value.reshape((rows,) + (2,) * len(self.every) + (-1,))
-        parts = self.flipped(parts, self.far, [1 + self.canon.index(axis) for axis in self.far])
         order = [0] + [1 + self.canon.index(axis) for axis in self.every] + [1 + len(self.every)]
         return parts.transpose(order).reshape(rows, width)
 
     def spread_order(self, width):
         own = jnp.arange(width, dtype=jnp.int32).reshape((2,) * len(self.canon) + (-1,))
-        own = self.flipped(own, self.team, [self.canon.index(axis) for axis in self.team])
+        own = self.flipped(own, self.canon, range(len(self.canon)))
         axes = (self.c,) + tuple(reversed(self.order))
         return own.transpose([self.canon.index(axis) for axis in axes] + [len(self.canon)]).reshape(-1)
-
-    def pieces(self, blocks, axes):
-        for axis in axes:
-            blocks = [one for block in blocks for one in (block, swap(block, axis))]
-        return blocks
 
     def grow(self, block, axes):
         for axis in axes:
@@ -144,16 +137,8 @@
         whole = jnp.concatenate(pieces, axis=0)
         whole = whole.reshape((2,) * len(axes) + (-1, whole.shape[-1]))
         whole = whole.transpose([axes.index(axis) for axis in self.canon] + [len(axes), len(axes) + 1])
-        whole = self.flipped(whole, self.team, [self.canon.index(axis) for axis in self.team])
+        whole = self.flipped(whole, self.canon, range(len(self.canon)))
         return whole.reshape((-1, whole.shape[-1]))
-
-    def fold(self, pieces, axes):
-        for axis in reversed(axes):
-            pieces = [
-                (kept.astype(F32) + swap(away, axis).astype(F32)).astype(BF16)
-                for kept, away in zip(pieces[::2], pieces[1::2])
-            ]
-        return pieces
 
     def spread_begin(self, pairs):
         half = pairs[0][0].shape[1] // 2
@@ -333,10 +318,7 @@
         axis=1,
     )
     feed_team = lax.all_to_all(feed_local, plan.team, split_axis=0, concat_axis=0, tiled=True)
-    gate_own, up_own, down_own = [
-        feed_team[:, index * local_rows : (index + 1) * local_rows].reshape(-1, hidden_own)
-        for index in range(3)
-    ]
+    feed_team = feed_team.reshape(team_size, 3, local_rows, hidden_own).transpose(1, 0, 2, 3)
     block_widths = [sum(kvl_widths), query_weight.shape[1], sum(rest_widths)]
     attn_block = jnp.concatenate(
         [key_weight, value_weight, laurel_left, laurel_right, query_weight]
@@ -344,21 +326,14 @@
         axis=1,
     )
     attn_block = plan.grow(attn_block, plan.far_seq)
-    attn_block, gate_own, up_own, down_own = together(attn_block, gate_own, up_own, down_own)
+    attn_block, feed_team = together(attn_block, feed_team)
+    feed_full = lax.all_gather(feed_team.reshape(-1, hidden_own), plan.far, axis=0, tiled=True)
     attn_block = plan.grow(attn_block, (plan.l,))
-    gate_first = plan.pieces([gate_own], plan.far_dp)
-    up_first = plan.pieces([up_own], plan.far_dp)
-    attn_block, gate_own, gate_first, up_first = together(attn_block, gate_own, gate_first, up_first)
     kvl_block, query_block, rest_block = split_columns(attn_block, block_widths)
     kvl_block = plan.grow(kvl_block, plan.far_dp)
     query_block = plan.grow(query_block, plan.far_dp)
-    gate_far = plan.pieces([gate_own], plan.far_seq)
     kvl_full = plan.gather_pieces(kvl_block)
-    kvl_full, query_block, gate_far, up_own, rest_block = together(
-        kvl_full, query_block, gate_far, up_own, rest_block
-    )
-    up_far = plan.pieces([up_own], plan.far_seq)
-    gate_last = plan.pieces(gate_far[1:], plan.far_dp)
+    kvl_full, query_block, rest_block = together(kvl_full, query_block, rest_block)
     query_full = plan.gather_pieces(query_block)
     rest_block = plan.grow(rest_block, plan.far_dp)
     right_full = plan.far_team_rows([one[:, -kvl_widths[3] :] for one in kvl_full])
@@ -405,7 +380,6 @@
     total_length = block * seq_count
     if whole_sequence:
         pair_low = plan.near_far(key_low, value_low)
-        pair_low, up_far, down_own = together(pair_low, up_far, down_own)
         keys_all, values_all = [
             one.swapaxes(0, 1).reshape(batch, total_length, kv_heads, head_size)
             for one in plan.near_gather(pair_low)
@@ -420,11 +394,8 @@
         keys_all, values_all = jnp.concatenate(gathered, axis=2)
         key_blocks = seq_index - jnp.array(offsets, dtype=jnp.int32)
     key_count = keys_all.shape[1]
-    down_far = plan.pieces([down_own], plan.far_seq)
     keys_all, values_all, rest_block = together(keys_all, values_all, rest_block)
     rest_full = plan.gather_pieces(rest_block)
-    up_last = plan.pieces(up_far[1:], plan.far_dp)
-    down_first = plan.pieces(down_far[:1], plan.far_dp)
     query_places = seq_index * block + jnp.arange(block, dtype=jnp.int32)
     key_places = (key_blocks[:, None] * block + jnp.arange(block, dtype=jnp.int32)).reshape(-1)
     in_query = (query_places[None, :, None] >= span_start[:, None, :]) & (
@@ -449,14 +420,7 @@
     probs_low = probs.astype(BF16)
     attended = jnp.einsum("bkgts,bskd->btkgd", probs_low, values_all, preferred_element_type=F32)
     attended_low = attended.reshape(rows, heads * head_size).astype(BF16)
-    attended_low, gate_last, up_last, down_first = together(
-        attended_low, gate_last, up_last, down_first
-    )
-    down_last = plan.pieces(down_far[1:], plan.far_dp)
-    gate_full, up_full, down_full = [
-        jnp.concatenate(first + last, axis=0)
-        for first, last in ((gate_first, gate_last), (up_first, up_last), (down_first, down_last))
-    ]
+    attended_low, feed_full = together(attended_low, feed_full)
     output_full = [one[:, : rest_widths[0]] for one in rest_full]
     side_full = plan.far_team_rows([one[:, rest_widths[0] :] for one in rest_full])
     side_gate_full, side_output_full = split_columns(side_full, rest_widths[1:])
@@ -467,6 +431,8 @@
     )
 
     feed_low = feed_in.astype(BF16)
+    feed_full = feed_full.reshape(-1, 3, team_size * local_rows, hidden_own)
+    gate_full, up_full, down_full = [feed_full[:, at].reshape(width, hidden_own) for at in range(3)]
     pulls = []
     hidden_chunks = []
 
@@ -517,31 +483,29 @@
     d_gate_chunks, d_up_chunks, feed_chunks, d_out_chunks, hidden_chunks, d_feed_sums = together(
         d_gate_chunks, d_up_chunks, feed_chunks, d_out_chunks, hidden_chunks, d_feed_sums
     )
-    far_count = 2 ** len(plan.far)
-
-    def far_terms(left, right):
-        right = jnp.concatenate(right, axis=0)
-        part = width // far_count
-        return [
-            product_tn(left[:, at * part : (at + 1) * part], right).astype(BF16)
-            for at in range(far_count)
-        ]
-
     feed_all = jnp.concatenate(feed_chunks, axis=0)
-    gate_terms = far_terms(feed_all, d_gate_chunks)
-    d_feed_sums = plan.team_near(d_feed_sums)
-    d_feed_sums, d_up_chunks, feed_all, gate_terms = together(
-        d_feed_sums, d_up_chunks, feed_all, gate_terms
-    )
-    up_terms = far_terms(feed_all, d_up_chunks)
-    gate_terms = plan.fold(gate_terms, plan.far_dp)
-    d_feed_in = plan.team_far(d_feed_sums)
-    d_feed_in, up_terms, hidden_chunks, side_sum = together(
-        d_feed_in, up_terms, hidden_chunks, side_sum
-    )
+    d_out_all = jnp.concatenate(d_out_chunks, axis=0)
+    feed_terms = jnp.stack(
+        [
+            product_tn(left, jnp.concatenate(right, axis=0))
+            .astype(BF16)
+            .reshape(-1, team_size * local_rows, hidden_own)
+            for left, right in (
+                (feed_all, d_gate_chunks),
+                (feed_all, d_up_chunks),
+                (d_out_all, hidden_chunks),
+            )
+        ],
+        axis=1,
+    )
+    d_feed_in = plan.team_far(plan.team_near(d_feed_sums))
+    d_feed_in, feed_terms = together(d_feed_in, feed_terms)
+    feed_sum = lax.psum_scatter(
+        feed_terms.reshape(-1, hidden_own), plan.far, scatter_dimension=0, tiled=True
+    )
+    feed_sum = jnp.split(feed_sum, 3)
     steps = tuple(reversed(plan.order))
     side_sum = plan.spread_step(side_sum, steps[:1])
-    down_terms = far_terms(jnp.concatenate(d_out_chunks, axis=0), hidden_chunks)
 
     (
         d_inputs,
@@ -558,12 +522,8 @@
     d_attended_low = product_split(d_attn_spread, output_full).astype(BF16)
     d_latent_low = product(d_laurel_low, right_full).astype(BF16)
     output_sum = plan.spread_begin([(d_attn_spread, attended_low)])
-    d_attended_low, output_sum, gate_terms, up_terms, down_terms = together(
-        d_attended_low, output_sum, gate_terms, up_terms, down_terms
-    )
+    d_attended_low, output_sum = together(d_attended_low, output_sum)
     output_sum = plan.spread_step(output_sum, steps[:1])
-    gate_terms = plan.fold(gate_terms, plan.far_seq)
-    up_terms = plan.fold(up_terms, plan.far_dp)
 
     d_att = d_attended_low.reshape(batch, block, kv_heads, group, head_size)
     d_values_all = jnp.einsum("bkgts,btkgd->bskd", probs_low, d_att, preferred_element_type=F32)
@@ -574,12 +534,10 @@
     d_keys_all = jnp.einsum(
         "bkgts,btkgd->bskd", d_scores_low, query_group, preferred_element_type=F32
     )
-    d_keys_all, d_values_all, d_query_rot, gate_terms, up_terms, down_terms, output_sum, side_sum = together(
-        d_keys_all, d_values_all, d_query_rot, gate_terms, up_terms, down_terms, output_sum, side_sum
+    d_keys_all, d_values_all, d_query_rot, output_sum, side_sum = together(
+        d_keys_all, d_values_all, d_query_rot, output_sum, side_sum
     )
     output_sum = jnp.concatenate([output_sum, side_sum], axis=1)
-    up_terms = plan.fold(up_terms, plan.far_seq)
-    down_terms = plan.fold(down_terms, plan.far_dp)
     if whole_sequence:
         d_pair_total = plan.near_sum(
             *[
@@ -600,12 +558,9 @@
     )
     d_queries_low = d_queries.reshape(rows, -1).astype(BF16)
     query_sum = plan.spread_begin([(normed_spread, d_queries_low)])
-    d_keys, d_values, query_sum, output_sum, up_terms, down_terms = together(
-        d_keys, d_values, query_sum, output_sum, up_terms, down_terms
-    )
     query_sum = plan.spread_step(query_sum, steps[:1])
-    down_terms = plan.fold(down_terms, plan.far_seq)
-    grad_gate, grad_up, grad_down = plan.own_rows(gate_terms + up_terms + down_terms, local_rows)
+    d_keys, d_values, query_sum, output_sum = together(d_keys, d_values, query_sum, output_sum)
+    grad_gate, grad_up, grad_down = plan.own_rows(feed_sum, local_rows)
     d_kvl_low = jnp.concatenate(
         [
             d_keys.reshape(rows, -1).astype(BF16),
@@ -616,6 +571,8 @@
     )
     laurel_spread = product(d_laurel_low, to_spread).astype(BF16)
     kvl_sum = plan.spread_begin([(normed_spread, d_kvl_low), (laurel_spread, latent_low)])
+    kvl_sum = plan.spread_step(kvl_sum, steps[:1])
+    kvl_sum, d_queries_low, d_kvl_low = together(kvl_sum, d_queries_low, d_kvl_low)
     d_spread = product_nt_split(d_queries_low, query_full) + product_nt_split(d_kvl_low, kvl_full)
     d_normed = d_normed + reorder(d_spread, to_spread)
     d_inputs_norm, grad_norm_input = pre_pull(d_normed)
@@ -640,7 +597,7 @@
         plan.spread_step(output_sum, steps[1:]), rest_widths
     )
     grad_key, grad_value, grad_left, grad_right = split_columns(
-        plan.spread_step(kvl_sum, steps), kvl_widths
+        plan.spread_step(kvl_sum, steps[1:]), kvl_widths
     )
     gain_grads = plan.total(gain_grads)
     gain_parts = split_columns(gain_grads, [width] * 6 + [head_size] * 2)

time: 1280 us -> 1250 us (0.977)
  waiting for transfers between devices: 563 us -> 639 us
  local copies, waits for them, and re-layouts: 189 us -> 146 us
  other arithmetic: 136 us -> 109 us
  matrix products: 281 us -> 257 us
  starting transfers between devices: 97.7 us -> 74 us
  between operations: 5.04 us -> 18.4 us
    ppermute x96 -> x78, waiting for transfers between devices: 562 us -> 638 us  [swap(): return lax.ppermute(value, axis, [(0, 1), (1, 0)])]
    unnamed x520 -> x463, local copies, waits for them, and re-layouts: 84.3 us -> 56.9 us
    ppermute x96 -> x78, starting transfers between devices: 87.6 us -> 63.3 us  [swap(): return lax.ppermute(value, axis, [(0, 1), (1, 0)])]
    convert_element_type x9 -> x0, other arithmetic: 17.2 us -> none  [fold(): (kept.astype(F32) + swap(away, axis).astype(F32)).astype(BF16)]
    dot_general x31, matrix products: 97.6 us -> 84.4 us  [product_nt(): lax.dot_general(left, right, (((1,), (1,)), ((), ())), preferred_element_...]
    dot_general x24 -> x15, matrix products: 66.3 us -> 56.4 us  [product_tn(): lax.dot_general(left, right, (((0,), (0,)), ((), ())), preferred_element_...]
  transfers between devices with their start and end apart: 98 -> 82, of which waited for: 42 -> 45; matrix products, arithmetic and copies ran while one was open for 33% -> 33% of each run, Pallas kernels for 0% -> 0%
where the time goes in v7:
time: 1250 us; the launch traced here: 1240 us
  waiting for transfers between devices  639 us (51%)
  matrix products  257 us (21%)
  local copies, waits for them, and re-layouts  146 us (12%)
  other arithmetic  109 us (9%)
  starting transfers between devices  74 us (6%)
  between operations  18.4 us (1%)
    ppermute x78, waiting for transfers between devices, swap(): return lax.ppermute(value, axis, [(0, 1), (1, 0)])  638 us
    dot_general x33, matrix products, product(): return jnp.dot(left, right, preferred_element_type=F32)  100 us
    dot_general x31, matrix products, product_nt(): lax.dot_general(left, right, (((1,), (1,)), ((), ())), preferred_element_...  84.4 us
    ppermute x78, starting transfers between devices, swap(): return lax.ppermute(value, axis, [(0, 1), (1, 0)])  63.3 us
    unnamed x463, local copies, waits for them, and re-layouts  56.9 us
    dot_general x15, matrix products, product_tn(): lax.dot_general(left, right, (((0,), (0,)), ((), ())), preferred_element_...  56.4 us
  transfers between devices with their start and end apart: 82, of which 45 were waited for; matrix products, arithmetic and copies ran while one was open for 33% of the time, Pallas kernels for 0%

profile of v7, /device:TPU:0, one launch (start us, length us, event | category | flops | bytes accessed | tf_op | source)
XLA Modules:
  0.0 1243.0 jit_solution(14967495831260905614)
XLA Ops:
  14.4 5.4 all-to-all-start
  24.1 46.3 %collective-permute-done = bf16[64,5760]{1,0:T(8,128)(2,1)} collective-permute-done((bf16[64,5760]{1,0:T(8,128)(2,1)S(1)}, bf16[64,5760]{1,0:T(8,128)(2,1)}, u32[]{:S(2)}, u32[]{:S(2)}) %collective-permute-start) | collective-permute-done | bytes 737312 | tf_op jit(solution)/shard_map/ppermute | solution.py:73
  82.9 56.2 %collective-permute-done.1 = bf16[128,5760]{1,0:T(8,128)(2,1)} collective-permute-done((bf16[128,5760]{1,0:T(8,128)(2,1)S(1)}, bf16[128,5760]{1,0:T(8,128)(2,1)}, u32[]{:S(2)}, u32[]{:S(2)}) %collective-permute-start.1) | collective-permute-done | bytes 1474592 | tf_op jit(solution)/shard_map/ppermute | solution.py:73
  144.1 9.6 collective-permute-done.2
  156.7 5.8 multiply_reduce_fusion.18
  166.4 11.7 collective-permute-done.3
  183.2 5.2 fusion.75
  191.2 16.8 %collective-permute-done.6 = bf16[256,2048]{1,0:T(8,128)(2,1)} collective-permute-done((bf16[256,2048]{1,0:T(8,128)(2,1)}, bf16[256,2048]{1,0:T(8,128)(2,1)}, u32[]{:S(2)}, u32[]{:S(2)}) %collective-permute-start.6) | collective-permute-done | bytes 1048608 | tf_op jit(solution)/shard_map/ppermute | solution.py:73
  241.4 33.5 %collective-permute-done.7 = bf16[2,1,2,128,2,256]{5,3,4,2,1,0:T(8,128)(2,1)S(1)} collective-permute-done((bf16[2,1,2,128,2,256]{5,3,4,2,1,0:T(8,128)(2,1)S(1)}, bf16[2,1,2,128,2,256]{5,3,4,2,1,0:T(8,128)(2,1)S(1)}, u32[]{:S(2)}, u32[]{:S(2)}) %collective-permute-start.7) | collective-permute-done | bytes 524320 | tf_op jit(solution)/shard_map/ppermute | solution.py:73
  283.6 6.0 collective-permute-done.8
  291.2 45.8 %collective-permute-done.10 = bf16[1,2,2,128,2,256]{5,3,4,2,1,0:T(8,128)(2,1)} collective-permute-done((bf16[1,2,2,128,2,256]{5,3,4,2,1,0:T(8,128)(2,1)}, bf16[1,2,2,128,2,256]{5,3,4,2,1,0:T(8,128)(2,1)}, u32[]{:S(2)}, u32[]{:S(2)}) %collective-permute-start.10) | collective-permute-done | bytes 524320 | tf_op jit(solution)/shard_map/ppermute | solution.py:73
  346.4 12.8 %collective-permute-done.9 = bf16[2,2,2,128,2,256]{5,3,4,2,1,0:T(8,128)(2,1)S(1)} collective-permute-done((bf16[2,2,2,128,2,256]{5,3,4,2,1,0:T(8,128)(2,1)S(1)}, bf16[2,2,2,128,2,256]{5,3,4,2,1,0:T(8,128)(2,1)S(1)}, u32[]{:S(2)}, u32[]{:S(2)}) %collective-permute-start.9) | collective-permute-done | bytes 1048608 | tf_op jit(solution)/shard_map/ppermute | solution.py:73
  382.4 41.1 %collective-permute-done.16 = bf16[512,2560]{1,0:T(8,128)(2,1)} collective-permute-done((bf16[512,2560]{1,0:T(8,128)(2,1)}, bf16[512,2560]{1,0:T(8,128)(2,1)}, u32[]{:S(2)}, u32[]{:S(2)}) %collective-permute-start.16) | collective-permute-done | bytes 2621472 | tf_op jit(solution)/shard_map/ppermute | solution.py:73
  467.0 4.9 fusion.298
  478.3 7.8 collective-permute-done.19
  490.8 9.2 collective-permute-done.25
  535.6 11.4 collective-permute-done.33
  553.2 18.3 %collective-permute-done.34 = bf16[256,2048]{1,0:T(8,128)(2,1)S(1)} collective-permute-done((bf16[256,2048]{1,0:T(8,128)(2,1)S(1)}, bf16[256,2048]{1,0:T(8,128)(2,1)S(1)}, u32[]{:S(2)}, u32[]{:S(2)}) %collective-permute-start.34) | collective-permute-done | bytes 1048608 | tf_op jit(solution)/shard_map/ppermute | solution.py:73
  590.1 5.8 fusion.69
  605.4 7.5 collective-permute-done.36
  619.8 7.9 collective-permute-done.40
  641.0 5.0 add_convert_fusion.7
  648.2 6.4 multiply_convert_fusion.1
  685.7 10.9 fusion.58
  696.6 10.8 fusion.61
  714.0 13.9 %fusion.64 = bf16[2048,1024]{1,0:T(8,128)(2,1)} fusion(bf16[512,1024]{1,0:T(8,128)(2,1)} %copy-done.200, bf16[512,1024]{1,0:T(8,128)(2,1)} %get-tuple-element.124, bf16[512,1024]{1,0:T(8,128)(2,1)} %copy-done.198, bf16[512,1024]{1,0:T(8,128)(2,1)} %copy-done.197, bf16[512,2048]{1,0:T(8,128)(2,1)} %copy-done.97, bf16[512,2048]{1,0:T(8,128)(2,1)} %copy-done.86, ...), kind=kOutput, calls=%fused_computation.77 | convolution fusion | flops 8642363392 | bytes 16777216 | tf_op jit(solution)/shard_map/dot_general | solution.py:34
  727.9 9.0 pad_maximum_fusion
  754.3 6.6 collective-permute-done.53
  764.6 12.6 %collective-permute-done.54 = bf16[512,512]{1,0:T(8,128)(2,1)S(1)} collective-permute-done((bf16[512,512]{1,0:T(8,128)(2,1)}, bf16[512,512]{1,0:T(8,128)(2,1)S(1)}, u32[]{:S(2)}, u32[]{:S(2)}) %collective-permute-start.54) | collective-permute-done | bytes 524320 | tf_op jit(solution)/shard_map/ppermute | solution.py:73
  789.0 5.4 add_convert_fusion.1
  797.1 5.1 fusion.19
  815.2 34.1 %collective-permute-done.52 = bf16[512,2048]{1,0:T(8,128)(2,1)S(1)} collective-permute-done((bf16[512,2048]{1,0:T(8,128)(2,1)S(1)}, bf16[512,2048]{1,0:T(8,128)(2,1)S(1)}, u32[]{:S(2)}, u32[]{:S(2)}) %collective-permute-start.52) | collective-permute-done | bytes 2097184 | tf_op jit(solution)/shard_map/ppermute | solution.py:73
  869.4 5.0 fusion.74
  898.2 10.6 collective-permute-done.57
  912.9 32.5 %collective-permute-done.55 = bf16[2,2,2,128,2,256]{5,3,4,2,1,0:T(8,128)(2,1)S(1)} collective-permute-done((bf16[2,2,2,128,2,256]{5,3,4,2,1,0:T(8,128)(2,1)S(1)}, bf16[2,2,2,128,2,256]{5,3,4,2,1,0:T(8,128)(2,1)S(1)}, u32[]{:S(2)}, u32[]{:S(2)}) %collective-permute-start.55) | collective-permute-done | bytes 1048608 | tf_op jit(solution)/shard_map/ppermute | solution.py:73
  949.9 6.8 collective-permute-done.58
  967.9 38.2 %collective-permute-done.59 = bf16[2,2,128,2,256]{4,2,3,1,0:T(8,128)(2,1)S(1)} collective-permute-done((bf16[2,2,128,2,256]{4,2,3,1,0:T(8,128)(2,1)S(1)}, bf16[2,2,128,2,256]{4,2,3,1,0:T(8,128)(2,1)S(1)}, u32[]{:S(2)}, u32[]{:S(2)}) %collective-permute-start.59) | collective-permute-done | bytes 524320 | tf_op jit(solution)/shard_map/ppermute | solution.py:73
  1007.9 5.1 collective-permute-done.61
  1019.8 20.3 %collective-permute-done.64 = bf16[256,2048]{1,0:T(8,128)(2,1)S(1)} collective-permute-done((bf16[256,2048]{1,0:T(8,128)(2,1)S(1)}, bf16[256,2048]{1,0:T(8,128)(2,1)S(1)}, u32[]{:S(2)}, u32[]{:S(2)}) %collective-permute-start.64) | collective-permute-done | bytes 1048608 | tf_op jit(solution)/shard_map/ppermute | solution.py:73
  1040.8 24.9 %collective-permute-done.70 = bf16[256,2560]{1,0:T(8,128)(2,1)S(1)} collective-permute-done((bf16[256,2560]{1,0:T(8,128)(2,1)S(1)}, bf16[256,2560]{1,0:T(8,128)(2,1)S(1)}, u32[]{:S(2)}, u32[]{:S(2)}) %collective-permute-start.70) | collective-permute-done | bytes 1310752 | tf_op jit(solution)/shard_map/ppermute | solution.py:73
  1068.8 18.9 %collective-permute-done.71 = bf16[128,2560]{1,0:T(8,128)(2,1)S(1)} collective-permute-done((bf16[128,2560]{1,0:T(8,128)(2,1)S(1)}, bf16[128,2560]{1,0:T(8,128)(2,1)S(1)}, u32[]{:S(2)}, u32[]{:S(2)}) %collective-permute-start.71) | collective-permute-done | bytes 655392 | tf_op jit(solution)/shard_map/ppermute | solution.py:73
  1094.1 9.1 collective-permute-done.72
  1104.8 13.1 %collective-permute-done.63 = bf16[512,1152]{0,1:T(8,128)(2,1)S(1)} collective-permute-done((bf16[512,1152]{0,1:T(8,128)(2,1)S(1)}, bf16[512,1152]{0,1:T(8,128)(2,1)S(1)}, u32[]{:S(2)}, u32[]{:S(2)}) %collective-permute-start.63) | collective-permute-done | bytes 1179680 | tf_op jit(solution)/shard_map/ppermute | solution.py:73
  1133.4 4.9 fusion.1
  1144.8 5.0 all-to-all-start.1
  1158.7 29.1 %collective-permute-done.75 = f32[12800]{0:T(1024)S(1)} collective-permute-done((f32[12800]{0:T(1024)S(1)}, f32[12800]{0:T(1024)S(1)}, u32[]{:S(2)}, u32[]{:S(2)}) %collective-permute-start.75) | collective-permute-done | bytes 51232 | tf_op jit(solution)/shard_map/ppermute | solution.py:73
  1200.4 4.7 collective-permute-done.68
  1206.7 13.3 %collective-permute-done.69 = bf16[64,1152]{0,1:T(8,128)(2,1)S(1)} collective-permute-done((bf16[64,1152]{0,1:T(8,128)(2,1)S(1)}, bf16[64,1152]{0,1:T(8,128)(2,1)S(1)}, u32[]{:S(2)}, u32[]{:S(2)}) %collective-permute-start.69) | collective-permute-done | bytes 147488 | tf_op jit(solution)/shard_map/ppermute | solution.py:73
  (961 shorter events, 494.2 us)
Async XLA Ops:
  14.4 58.2 %all-to-all-start = ((bf16[8,192,1024]{2,1,0:T(8,128)(2,1)}), bf16[8,192,1024]{2,1,0:T(8,128)(2,1)}, u32[]{:S(2)}, u32[]{:S(2)}) async-start(bf16[8,192,1024]{2,1,0:T(8,128)(2,1)} %copy.519), calls=%async_computation | async-start | bytes 6291456 | tf_op jit(solution)/shard_map/all_to_all | solution.py:320
  19.8 415.5 %all-gather.2.cloned.1.call-start = ((), (), s32[]{:S(2)}) async-start(), calls=%async_computation.3 | async-start | bytes 15728640 | tf_op jit(solution)/shard_map/all_gather | solution.py:330
  20.1 50.3 %collective-permute-start = (bf16[64,5760]{1,0:T(8,128)(2,1)S(1)}, bf16[64,5760]{1,0:T(8,128)(2,1)}, u32[]{:S(2)}, u32[]{:S(2)}) collective-permute-start(bf16[64,5760]{1,0:T(8,128)(2,1)S(1)} %concatenate.188), channel_id=1, source_target_pairs={{0,16},{16,0},{1,17},{17,1},{2,18},{18,2},{3,19},{19,3},{4,20},{20... | collective-permute-start | bytes 2211848 | tf_op jit(solution)/shard_map/ppermute | solution.py:73
  76.7 1064.0 %reduce-scatter.2.cloned.1.call-start = ((), (), s32[]{:S(2)}) async-start(), calls=%async_computation.4 | async-start | bytes 15728640 | tf_op jit(solution)/shard_map/reduce_scatter | solution.py:503
  78.3 60.9 %collective-permute-start.1 = (bf16[128,5760]{1,0:T(8,128)(2,1)S(1)}, bf16[128,5760]{1,0:T(8,128)(2,1)}, u32[]{:S(2)}, u32[]{:S(2)}) collective-permute-start(bf16[128,5760]{1,0:T(8,128)(2,1)S(1)} %pad_maximum_fusion.13), channel_id=1, source_target_pairs={{0,8},{8,0},{1,9},{9,1},{2,10},{10,2},{3,11},{11,3},{4,12},{12,4},... | collective-permute-start | bytes 4423688 | tf_op jit(solution)/shard_map/ppermute | solution.py:73
  164.8 43.3 %collective-permute-start.6 = (bf16[256,2048]{1,0:T(8,128)(2,1)}, bf16[256,2048]{1,0:T(8,128)(2,1)}, u32[]{:S(2)}, u32[]{:S(2)}) collective-permute-start(bf16[256,2048]{1,0:T(8,128)(2,1)} %slice.691), channel_id=1, source_target_pairs={{0,2},{2,0},{1,3},{3,1},{4,6},{6,4},{5,7},{7,5},{8,10},{10,8},{9,1... | collective-permute-start | bytes 3145736 | tf_op jit(solution)/shard_map/ppermute | solution.py:73
  166.4 44.8 %collective-permute-start.4 = (bf16[512,1152]{1,0:T(8,128)(2,1)S(1)}, bf16[512,1152]{1,0:T(8,128)(2,1)}, u32[]{:S(2)}, u32[]{:S(2)}) collective-permute-start(bf16[512,1152]{1,0:T(8,128)(2,1)S(1)} %pad_maximum_fusion.14), channel_id=1, source_target_pairs={{0,1},{1,0},{2,3},{3,2},{4,5},{5,4},{6,7},{7,6},{8,9},{9,8},{10,11... | collective-permute-start | bytes 3538952 | tf_op jit(solution)/shard_map/ppermute | solution.py:73
  178.0 33.2 %collective-permute-start.5 = (bf16[512,1152]{1,0:T(8,128)(2,1)}, bf16[512,1152]{1,0:T(8,128)(2,1)}, u32[]{:S(2)}, u32[]{:S(2)}) collective-permute-start(bf16[512,1152]{1,0:T(8,128)(2,1)} %collective-permute-done.3), channel_id=1, source_target_pairs={{0,1},{1,0},{2,3},{3,2},{4,5},{5,4},{6,7},{7,6},{8,9},{9,8},{10,11... | collective-permute-start | bytes 3538952 | tf_op jit(solution)/shard_map/ppermute | solution.py:73
  226.7 142.3 %collective-permute-start.14 = (bf16[512,2048]{1,0:T(8,128)(2,1)}, bf16[512,2048]{1,0:T(8,128)(2,1)}, u32[]{:S(2)}, u32[]{:S(2)}) collective-permute-start(bf16[512,2048]{1,0:T(8,128)(2,1)} %pad_maximum_fusion.6), channel_id=1, source_target_pairs={{0,1},{1,0},{2,3},{3,2},{4,5},{5,4},{6,7},{7,6},{8,9},{9,8},{10,11... | collective-permute-start | bytes 6291464 | tf_op jit(solution)/shard_map/ppermute | solution.py:73
  226.8 113.1 %collective-permute-start.13 = (bf16[512,2048]{1,0:T(8,128)(2,1)}, bf16[512,2048]{1,0:T(8,128)(2,1)}, u32[]{:S(2)}, u32[]{:S(2)}) collective-permute-start(bf16[512,2048]{1,0:T(8,128)(2,1)} %pad_maximum_fusion.6), channel_id=1, source_target_pairs={{0,4},{4,0},{1,5},{5,1},{2,6},{6,2},{3,7},{7,3},{8,12},{12,8},{9,1... | collective-permute-start | bytes 6291464 | tf_op jit(solution)/shard_map/ppermute | solution.py:73
  237.0 38.0 %collective-permute-start.7 = (bf16[2,1,2,128,2,256]{5,3,4,2,1,0:T(8,128)(2,1)S(1)}, bf16[2,1,2,128,2,256]{5,3,4,2,1,0:T(8,128)(2,1)S(1)}, u32[]{:S(2)}, u32[]{:S(2)}) collective-permute-start(bf16[2,1,2,128,2,256]{5,3,4,2,1,0:T(8,128)(2,1)S(1)} %maximum_bitcast_fusion), channel_id=1, source_target_pairs={{0,16},{16,0},{1,17},{17,1},{2,18},{18,2},{3,19},{19,3},{4,20},{20... | collective-permute-start | bytes 1572872 | tf_op jit(solution)/shard_map/ppermute | solution.py:73
  237.8 105.3 %collective-permute-start.12 = (bf16[256,2560]{1,0:T(8,128)(2,1)}, bf16[256,2560]{1,0:T(8,128)(2,1)}, u32[]{:S(2)}, u32[]{:S(2)}) collective-permute-start(bf16[256,2560]{1,0:T(8,128)(2,1)} %slice.692), channel_id=1, source_target_pairs={{0,2},{2,0},{1,3},{3,1},{4,6},{6,4},{5,7},{7,5},{8,10},{10,8},{9,1... | collective-permute-start | bytes 3932168 | tf_op jit(solution)/shard_map/ppermute | solution.py:73
  277.8 59.2 %collective-permute-start.10 = (bf16[1,2,2,128,2,256]{5,3,4,2,1,0:T(8,128)(2,1)}, bf16[1,2,2,128,2,256]{5,3,4,2,1,0:T(8,128)(2,1)}, u32[]{:S(2)}, u32[]{:S(2)}) collective-permute-start(bf16[1,2,2,128,2,256]{5,3,4,2,1,0:T(8,128)(2,1)} %get-tuple-element.450), channel_id=1, source_target_pairs={{0,8},{8,0},{1,9},{9,1},{2,10},{10,2},{3,11},{11,3},{4,12},{12,4},... | collective-permute-start | bytes 1572872 | tf_op jit(solution)/shard_map/ppermute | solution.py:73
  291.0 68.3 %collective-permute-start.9 = (bf16[2,2,2,128,2,256]{5,3,4,2,1,0:T(8,128)(2,1)S(1)}, bf16[2,2,2,128,2,256]{5,3,4,2,1,0:T(8,128)(2,1)S(1)}, u32[]{:S(2)}, u32[]{:S(2)}) collective-permute-start(bf16[2,2,2,128,2,256]{5,3,4,2,1,0:T(8,128)(2,1)S(1)} %get-tuple-element.453), channel_id=1, source_target_pairs={{0,8},{8,0},{1,9},{9,1},{2,10},{10,2},{3,11},{11,3},{4,12},{12,4},... | collective-permute-start | bytes 3145736 | tf_op jit(solution)/shard_map/ppermute | solution.py:73
  338.3 25.1 %collective-permute-start.11 = (bf16[2,2,2,128,2,256]{5,3,4,2,1,0:T(8,128)(2,1)S(1)}, bf16[2,2,2,128,2,256]{5,3,4,2,1,0:T(8,128)(2,1)S(1)}, u32[]{:S(2)}, u32[]{:S(2)}) collective-permute-start(bf16[2,2,2,128,2,256]{5,3,4,2,1,0:T(8,128)(2,1)S(1)} %get-tuple-element.449), channel_id=1, source_target_pairs={{0,4},{4,0},{1,5},{5,1},{2,6},{6,2},{3,7},{7,3},{8,12},{12,8},{9,1... | collective-permute-start | bytes 3145736 | tf_op jit(solution)/shard_map/ppermute | solution.py:73
  339.9 32.4 %collective-permute-start.15 = (bf16[512,2048]{1,0:T(8,128)(2,1)}, bf16[512,2048]{1,0:T(8,128)(2,1)S(1)}, u32[]{:S(2)}, u32[]{:S(2)}) collective-permute-start(bf16[512,2048]{1,0:T(8,128)(2,1)} %collective-permute-done.13), channel_id=1, source_target_pairs={{0,1},{1,0},{2,3},{3,2},{4,5},{5,4},{6,7},{7,6},{8,9},{9,8},{10,11... | collective-permute-start | bytes 6291464 | tf_op jit(solution)/shard_map/ppermute | solution.py:73
  365.3 58.1 %collective-permute-start.16 = (bf16[512,2560]{1,0:T(8,128)(2,1)}, bf16[512,2560]{1,0:T(8,128)(2,1)}, u32[]{:S(2)}, u32[]{:S(2)}) collective-permute-start(bf16[512,2560]{1,0:T(8,128)(2,1)} %pad_maximum_fusion.3), channel_id=1, source_target_pairs={{0,4},{4,0},{1,5},{5,1},{2,6},{6,2},{3,7},{7,3},{8,12},{12,8},{9,1... | collective-permute-start | bytes 7864328 | tf_op jit(solution)/shard_map/ppermute | solution.py:73
  366.7 75.9 %collective-permute-start.17 = (bf16[512,2560]{1,0:T(8,128)(2,1)}, bf16[512,2560]{1,0:T(8,128)(2,1)}, u32[]{:S(2)}, u32[]{:S(2)}) collective-permute-start(bf16[512,2560]{1,0:T(8,128)(2,1)} %pad_maximum_fusion.3), channel_id=1, source_target_pairs={{0,1},{1,0},{2,3},{3,2},{4,5},{5,4},{6,7},{7,6},{8,9},{9,8},{10,11... | collective-permute-start | bytes 7864328 | tf_op jit(solution)/shard_map/ppermute | solution.py:73
  461.0 25.2 %collective-permute-start.19 = (bf16[256,2048]{1,0:T(8,128)(2,1)S(1)}, bf16[256,2048]{1,0:T(8,128)(2,1)S(1)}, u32[]{:S(2)}, u32[]{:S(2)}) collective-permute-start(bf16[256,2048]{1,0:T(8,128)(2,1)S(1)} %multiply_convert_fusion.8), channel_id=1, source_target_pairs={{0,4},{4,0},{1,5},{5,1},{2,6},{6,2},{3,7},{7,3},{8,12},{12,8},{9,1... | collective-permute-start | bytes 3145736 | tf_op jit(solution)/shard_map/ppermute | solution.py:73
  462.5 24.8 %collective-permute-start.20 = (bf16[256,2048]{1,0:T(8,128)(2,1)S(1)}, bf16[256,2048]{1,0:T(8,128)(2,1)S(1)}, u32[]{:S(2)}, u32[]{:S(2)}) collective-permute-start(bf16[256,2048]{1,0:T(8,128)(2,1)S(1)} %multiply_convert_fusion.8), channel_id=1, source_target_pairs={{0,8},{8,0},{1,9},{9,1},{2,10},{10,2},{3,11},{11,3},{4,12},{12,4},... | collective-permute-start | bytes 3145736 | tf_op jit(solution)/shard_map/ppermute | solution.py:73
  490.8 62.5 %collective-permute-start.22 = (bf16[256,2048]{1,0:T(8,128)(2,1)}, bf16[256,2048]{1,0:T(8,128)(2,1)}, u32[]{:S(2)}, u32[]{:S(2)}) collective-permute-start(bf16[256,2048]{1,0:T(8,128)(2,1)} %slice.557), channel_id=1, source_target_pairs={{0,1},{1,0},{2,3},{3,2},{4,5},{5,4},{6,7},{7,6},{8,9},{9,8},{10,11... | collective-permute-start | bytes 3145736 | tf_op jit(solution)/shard_map/ppermute | solution.py:73
  587.9 25.0 %collective-permute-start.36 = (bf16[256,2048]{1,0:T(8,128)(2,1)S(1)}, bf16[256,2048]{1,0:T(8,128)(2,1)S(1)}, u32[]{:S(2)}, u32[]{:S(2)}) collective-permute-start(bf16[256,2048]{1,0:T(8,128)(2,1)S(1)} %fusion.110), channel_id=1, source_target_pairs={{0,4},{4,0},{1,5},{5,1},{2,6},{6,2},{3,7},{7,3},{8,12},{12,8},{9,1... | collective-permute-start | bytes 3145736 | tf_op jit(solution)/shard_map/ppermute | solution.py:73
  588.5 24.6 %collective-permute-start.37 = (bf16[256,2048]{1,0:T(8,128)(2,1)S(1)}, bf16[256,2048]{1,0:T(8,128)(2,1)S(1)}, u32[]{:S(2)}, u32[]{:S(2)}) collective-permute-start(bf16[256,2048]{1,0:T(8,128)(2,1)S(1)} %fusion.110), channel_id=1, source_target_pairs={{0,8},{8,0},{1,9},{9,1},{2,10},{10,2},{3,11},{11,3},{4,12},{12,4},... | collective-permute-start | bytes 3145736 | tf_op jit(solution)/shard_map/ppermute | solution.py:73
  617.7 28.6 %collective-permute-start.39 = (bf16[256,2048]{1,0:T(8,128)(2,1)S(1)}, bf16[256,2048]{1,0:T(8,128)(2,1)S(1)}, u32[]{:S(2)}, u32[]{:S(2)}) collective-permute-start(bf16[256,2048]{1,0:T(8,128)(2,1)S(1)} %collective-permute-done.37), channel_id=1, source_target_pairs={{0,1},{1,0},{2,3},{3,2},{4,5},{5,4},{6,7},{7,6},{8,9},{9,8},{10,11... | collective-permute-start | bytes 3145736 | tf_op jit(solution)/shard_map/ppermute | solution.py:73
  617.7 47.0 %collective-permute-start.43 = (bf16[256,2048]{1,0:T(8,128)(2,1)S(1)}, bf16[256,2048]{1,0:T(8,128)(2,1)S(1)}, u32[]{:S(2)}, u32[]{:S(2)}) collective-permute-start(bf16[256,2048]{1,0:T(8,128)(2,1)S(1)} %slice.581), channel_id=1, source_target_pairs={{0,1},{1,0},{2,3},{3,2},{4,5},{5,4},{6,7},{7,6},{8,9},{9,8},{10,11... | collective-permute-start | bytes 3145736 | tf_op jit(solution)/shard_map/ppermute | solution.py:73
  629.3 35.9 %collective-permute-start.42 = (bf16[256,2048]{1,0:T(8,128)(2,1)S(1)}, bf16[256,2048]{1,0:T(8,128)(2,1)S(1)}, u32[]{:S(2)}, u32[]{:S(2)}) collective-permute-start(bf16[256,2048]{1,0:T(8,128)(2,1)S(1)} %pad_maximum_fusion.21), channel_id=1, source_target_pairs={{0,1},{1,0},{2,3},{3,2},{4,5},{5,4},{6,7},{7,6},{8,9},{9,8},{10,11... | collective-permute-start | bytes 3145736 | tf_op jit(solution)/shard_map/ppermute | solution.py:73
  646.1 31.0 %collective-permute-start.44 = (bf16[256,2048]{1,0:T(8,128)(2,1)S(1)}, bf16[256,2048]{1,0:T(8,128)(2,1)}, u32[]{:S(2)}, u32[]{:S(2)}) collective-permute-start(bf16[256,2048]{1,0:T(8,128)(2,1)S(1)} %slice.731), channel_id=1, source_target_pairs={{0,1},{1,0},{2,3},{3,2},{4,5},{5,4},{6,7},{7,6},{8,9},{9,8},{10,11... | collective-permute-start | bytes 3145736 | tf_op jit(solution)/shard_map/ppermute | solution.py:73
  681.6 25.9 %collective-permute-start.49 = (bf16[128,2048]{1,0:T(8,128)(2,1)}, bf16[128,2048]{1,0:T(8,128)(2,1)}, u32[]{:S(2)}, u32[]{:S(2)}) collective-permute-start(bf16[128,2048]{1,0:T(8,128)(2,1)} %get-tuple-element.445), channel_id=1, source_target_pairs={{0,8},{8,0},{1,9},{9,1},{2,10},{10,2},{3,11},{11,3},{4,12},{12,4},... | collective-permute-start | bytes 1572872 | tf_op jit(solution)/shard_map/ppermute | solution.py:73
  682.0 29.1 %collective-permute-start.47 = (bf16[128,2048]{1,0:T(8,128)(2,1)S(1)}, bf16[128,2048]{1,0:T(8,128)(2,1)S(1)}, u32[]{:S(2)}, u32[]{:S(2)}) collective-permute-start(bf16[128,2048]{1,0:T(8,128)(2,1)S(1)} %get-tuple-element.444), channel_id=1, source_target_pairs={{0,4},{4,0},{1,5},{5,1},{2,6},{6,2},{3,7},{7,3},{8,12},{12,8},{9,1... | collective-permute-start | bytes 1572872 | tf_op jit(solution)/shard_map/ppermute | solution.py:73
  709.8 27.2 %collective-permute-start.50 = (bf16[256,2048]{1,0:T(8,128)(2,1)}, bf16[256,2048]{1,0:T(8,128)(2,1)}, u32[]{:S(2)}, u32[]{:S(2)}) collective-permute-start(bf16[256,2048]{1,0:T(8,128)(2,1)} %pad_maximum_fusion.23), channel_id=1, source_target_pairs={{0,4},{4,0},{1,5},{5,1},{2,6},{6,2},{3,7},{7,3},{8,12},{12,8},{9,1... | collective-permute-start | bytes 3145736 | tf_op jit(solution)/shard_map/ppermute | solution.py:73
  712.5 25.1 %collective-permute-start.48 = (bf16[256,2048]{1,0:T(8,128)(2,1)}, bf16[256,2048]{1,0:T(8,128)(2,1)S(1)}, u32[]{:S(2)}, u32[]{:S(2)}) collective-permute-start(bf16[256,2048]{1,0:T(8,128)(2,1)} %pad_maximum_fusion.22), channel_id=1, source_target_pairs={{0,8},{8,0},{1,9},{9,1},{2,10},{10,2},{3,11},{11,3},{4,12},{12,4},... | collective-permute-start | bytes 3145736 | tf_op jit(solution)/shard_map/ppermute | solution.py:73
  752.2 36.7 %collective-permute-start.51 = (bf16[1024,2048]{1,0:T(8,128)(2,1)}, bf16[1024,2048]{1,0:T(8,128)(2,1)}, u32[]{:S(2)}, u32[]{:S(2)}) collective-permute-start(bf16[1024,2048]{1,0:T(8,128)(2,1)} %convolution_convert_fusion.3), channel_id=1, source_target_pairs={{0,1},{1,0},{2,3},{3,2},{4,5},{5,4},{6,7},{7,6},{8,9},{9,8},{10,11... | collective-permute-start | bytes 12582920 | tf_op jit(solution)/shard_map/ppermute | solution.py:73
  802.5 46.9 %collective-permute-start.52 = (bf16[512,2048]{1,0:T(8,128)(2,1)S(1)}, bf16[512,2048]{1,0:T(8,128)(2,1)S(1)}, u32[]{:S(2)}, u32[]{:S(2)}) collective-permute-start(bf16[512,2048]{1,0:T(8,128)(2,1)S(1)} %slice.602), channel_id=1, source_target_pairs={{0,4},{4,0},{1,5},{5,1},{2,6},{6,2},{3,7},{7,3},{8,12},{12,8},{9,1... | collective-permute-start | bytes 6291464 | tf_op jit(solution)/shard_map/ppermute | solution.py:73
  868.8 93.7 %collective-permute-start.60 = (bf16[1024,2048]{1,0:T(8,128)(2,1)}, bf16[1024,2048]{1,0:T(8,128)(2,1)}, u32[]{:S(2)}, u32[]{:S(2)}) collective-permute-start(bf16[1024,2048]{1,0:T(8,128)(2,1)} %convolution_convert_fusion.2), channel_id=1, source_target_pairs={{0,1},{1,0},{2,3},{3,2},{4,5},{5,4},{6,7},{7,6},{8,9},{9,8},{10,11... | collective-permute-start | bytes 12582920 | tf_op jit(solution)/shard_map/ppermute | solution.py:73
  883.5 25.4 %collective-permute-start.57 = (bf16[2,2,2,128,2,256]{5,3,4,2,1,0:T(8,128)(2,1)}, bf16[2,2,2,128,2,256]{5,3,4,2,1,0:T(8,128)(2,1)}, u32[]{:S(2)}, u32[]{:S(2)}) collective-permute-start(bf16[2,2,2,128,2,256]{5,3,4,2,1,0:T(8,128)(2,1)} %slice_bitcast_fusion), channel_id=1, source_target_pairs={{0,4},{4,0},{1,5},{5,1},{2,6},{6,2},{3,7},{7,3},{8,12},{12,8},{9,1... | collective-permute-start | bytes 3145736 | tf_op jit(solution)/shard_map/ppermute | solution.py:73
  891.8 53.6 %collective-permute-start.55 = (bf16[2,2,2,128,2,256]{5,3,4,2,1,0:T(8,128)(2,1)S(1)}, bf16[2,2,2,128,2,256]{5,3,4,2,1,0:T(8,128)(2,1)S(1)}, u32[]{:S(2)}, u32[]{:S(2)}) collective-permute-start(bf16[2,2,2,128,2,256]{5,3,4,2,1,0:T(8,128)(2,1)S(1)} %bitcast.529), channel_id=1, source_target_pairs={{0,8},{8,0},{1,9},{9,1},{2,10},{10,2},{3,11},{11,3},{4,12},{12,4},... | collective-permute-start | bytes 3145736 | tf_op jit(solution)/shard_map/ppermute | solution.py:73
  911.3 45.4 %collective-permute-start.58 = (bf16[2,2,128,2,256]{4,2,3,1,0:T(8,128)(2,1)}, bf16[2,2,128,2,256]{4,2,3,1,0:T(8,128)(2,1)}, u32[]{:S(2)}, u32[]{:S(2)}) collective-permute-start(bf16[2,2,128,2,256]{4,2,3,1,0:T(8,128)(2,1)} %slice_bitcast_fusion.4), channel_id=1, source_target_pairs={{0,8},{8,0},{1,9},{9,1},{2,10},{10,2},{3,11},{11,3},{4,12},{12,4},... | collective-permute-start | bytes 1572872 | tf_op jit(solution)/shard_map/ppermute | solution.py:73
  962.4 43.7 %collective-permute-start.59 = (bf16[2,2,128,2,256]{4,2,3,1,0:T(8,128)(2,1)S(1)}, bf16[2,2,128,2,256]{4,2,3,1,0:T(8,128)(2,1)S(1)}, u32[]{:S(2)}, u32[]{:S(2)}) collective-permute-start(bf16[2,2,128,2,256]{4,2,3,1,0:T(8,128)(2,1)S(1)} %fusion.208), channel_id=1, source_target_pairs={{0,16},{16,0},{1,17},{17,1},{2,18},{18,2},{3,19},{19,3},{4,20},{20... | collective-permute-start | bytes 1572872 | tf_op jit(solution)/shard_map/ppermute | solution.py:73
  966.3 46.8 %collective-permute-start.61 = (bf16[512,2048]{1,0:T(8,128)(2,1)S(1)}, bf16[512,2048]{1,0:T(8,128)(2,1)S(1)}, u32[]{:S(2)}, u32[]{:S(2)}) collective-permute-start(bf16[512,2048]{1,0:T(8,128)(2,1)S(1)} %slice.767), channel_id=1, source_target_pairs={{0,4},{4,0},{1,5},{5,1},{2,6},{6,2},{3,7},{7,3},{8,12},{12,8},{9,1... | collective-permute-start | bytes 6291464 | tf_op jit(solution)/shard_map/ppermute | solution.py:73
  1014.0 26.2 %collective-permute-start.64 = (bf16[256,2048]{1,0:T(8,128)(2,1)S(1)}, bf16[256,2048]{1,0:T(8,128)(2,1)S(1)}, u32[]{:S(2)}, u32[]{:S(2)}) collective-permute-start(bf16[256,2048]{1,0:T(8,128)(2,1)S(1)} %slice.633), channel_id=1, source_target_pairs={{0,2},{2,0},{1,3},{3,1},{4,6},{6,4},{5,7},{7,5},{8,10},{10,8},{9,1... | collective-permute-start | bytes 3145736 | tf_op jit(solution)/shard_map/ppermute | solution.py:73
  1016.9 48.9 %collective-permute-start.70 = (bf16[256,2560]{1,0:T(8,128)(2,1)S(1)}, bf16[256,2560]{1,0:T(8,128)(2,1)S(1)}, u32[]{:S(2)}, u32[]{:S(2)}) collective-permute-start(bf16[256,2560]{1,0:T(8,128)(2,1)S(1)} %slice.647), channel_id=1, source_target_pairs={{0,2},{2,0},{1,3},{3,1},{4,6},{6,4},{5,7},{7,5},{8,10},{10,8},{9,1... | collective-permute-start | bytes 3932168 | tf_op jit(solution)/shard_map/ppermute | solution.py:73
  1018.9 69.0 %collective-permute-start.62 = (bf16[1024,1152]{0,1:T(8,128)(2,1)S(1)}, bf16[1024,1152]{0,1:T(8,128)(2,1)S(1)}, u32[]{:S(2)}, u32[]{:S(2)}) collective-permute-start(bf16[1024,1152]{0,1:T(8,128)(2,1)S(1)} %pad_maximum_fusion.5), channel_id=1, source_target_pairs={{0,1},{1,0},{2,3},{3,2},{4,5},{5,4},{6,7},{7,6},{8,9},{9,8},{10,11... | collective-permute-start | bytes 7077896 | tf_op jit(solution)/shard_map/ppermute | solution.py:73
  1040.7 25.5 %collective-permute-start.65 = (bf16[128,2048]{1,0:T(8,128)(2,1)S(1)}, bf16[128,2048]{1,0:T(8,128)(2,1)S(1)}, u32[]{:S(2)}, u32[]{:S(2)}) collective-permute-start(bf16[128,2048]{1,0:T(8,128)(2,1)S(1)} %slice.777), channel_id=1, source_target_pairs={{0,8},{8,0},{1,9},{9,1},{2,10},{10,2},{3,11},{11,3},{4,12},{12,4},... | collective-permute-start | bytes 1572872 | tf_op jit(solution)/shard_map/ppermute | solution.py:73
  1066.4 26.8 %collective-permute-start.66 = (bf16[64,2048]{1,0:T(8,128)(2,1)S(1)}, bf16[64,2048]{1,0:T(8,128)(2,1)S(1)}, u32[]{:S(2)}, u32[]{:S(2)}) collective-permute-start(bf16[64,2048]{1,0:T(8,128)(2,1)S(1)} %slice.779), channel_id=1, source_target_pairs={{0,16},{16,0},{1,17},{17,1},{2,18},{18,2},{3,19},{19,3},{4,20},{20... | collective-permute-start | bytes 786440 | tf_op jit(solution)/shard_map/ppermute | solution.py:73
  1089.3 28.6 %collective-permute-start.63 = (bf16[512,1152]{0,1:T(8,128)(2,1)S(1)}, bf16[512,1152]{0,1:T(8,128)(2,1)S(1)}, u32[]{:S(2)}, u32[]{:S(2)}) collective-permute-start(bf16[512,1152]{0,1:T(8,128)(2,1)S(1)} %slice.771), channel_id=1, source_target_pairs={{0,4},{4,0},{1,5},{5,1},{2,6},{6,2},{3,7},{7,3},{8,12},{12,8},{9,1... | collective-permute-start | bytes 3538952 | tf_op jit(solution)/shard_map/ppermute | solution.py:73
  1144.8 78.3 %all-to-all-start.1 = ((bf16[8,192,1024]{2,1,0:T(8,128)(2,1)}), bf16[8,192,1024]{2,1,0:T(8,128)(2,1)}, u32[]{:S(2)}, u32[]{:S(2)}) async-start(bf16[8,192,1024]{2,1,0:T(8,128)(2,1)} %pad_maximum_fusion.2), calls=%async_computation.2 | async-start | bytes 6291456 | tf_op jit(solution)/shard_map/all_to_all | solution.py:197
  1155.8 32.1 %collective-permute-start.75 = (f32[12800]{0:T(1024)S(1)}, f32[12800]{0:T(1024)S(1)}, u32[]{:S(2)}, u32[]{:S(2)}) collective-permute-start(f32[12800]{0:T(1024)S(1)} %add.593), channel_id=1, source_target_pairs={{0,4},{4,0},{1,5},{5,1},{2,6},{6,2},{3,7},{7,3},{8,12},{12,8},{9,1... | collective-permute-start | bytes 153608 | tf_op jit(solution)/shard_map/ppermute | solution.py:73
  1157.8 38.4 %collective-permute-start.67 = (bf16[256,1152]{0,1:T(8,128)(2,1)S(1)}, bf16[256,1152]{0,1:T(8,128)(2,1)S(1)}, u32[]{:S(2)}, u32[]{:S(2)}) collective-permute-start(bf16[256,1152]{0,1:T(8,128)(2,1)S(1)} %slice.639), channel_id=1, source_target_pairs={{0,2},{2,0},{1,3},{3,1},{4,6},{6,4},{5,7},{7,5},{8,10},{10,8},{9,1... | collective-permute-start | bytes 1769480 | tf_op jit(solution)/shard_map/ppermute | solution.py:73
  (244 other events, 3507.0 us)
Sparse Core Ops, SparseCore 0:
  76.8 249.1 all-gather.1
  779.3 248.9 reduce-scatter.1

commit v8 on v7

--- a/solution.py
+++ b/solution.py
@@ -153,6 +153,10 @@
             if axis != self.order[0]:
                 total = total.astype(BF16)
         return total
+
+    def spread_send(self, total, axis):
+        half = total.shape[0] // 2
+        return total[:half].astype(F32), swap(total[half:], axis).astype(F32)
 
     def near_far(self, key, value):
         pair = jnp.stack([key, value])[:, None]
@@ -333,7 +337,7 @@
     kvl_block = plan.grow(kvl_block, plan.far_dp)
     query_block = plan.grow(query_block, plan.far_dp)
     kvl_full = plan.gather_pieces(kvl_block)
-    kvl_full, query_block, rest_block = together(kvl_full, query_block, rest_block)
+    kvl_full, rest_block = together(kvl_full, rest_block)
     query_full = plan.gather_pieces(query_block)
     rest_block = plan.grow(rest_block, plan.far_dp)
     right_full = plan.far_team_rows([one[:, -kvl_widths[3] :] for one in kvl_full])
@@ -394,7 +398,6 @@
         keys_all, values_all = jnp.concatenate(gathered, axis=2)
         key_blocks = seq_index - jnp.array(offsets, dtype=jnp.int32)
     key_count = keys_all.shape[1]
-    keys_all, values_all, rest_block = together(keys_all, values_all, rest_block)
     rest_full = plan.gather_pieces(rest_block)
     query_places = seq_index * block + jnp.arange(block, dtype=jnp.int32)
     key_places = (key_blocks[:, None] * block + jnp.arange(block, dtype=jnp.int32)).reshape(-1)
@@ -503,7 +506,6 @@
     feed_sum = lax.psum_scatter(
         feed_terms.reshape(-1, hidden_own), plan.far, scatter_dimension=0, tiled=True
     )
-    feed_sum = jnp.split(feed_sum, 3)
     steps = tuple(reversed(plan.order))
     side_sum = plan.spread_step(side_sum, steps[:1])
 
@@ -559,8 +561,10 @@
     d_queries_low = d_queries.reshape(rows, -1).astype(BF16)
     query_sum = plan.spread_begin([(normed_spread, d_queries_low)])
     query_sum = plan.spread_step(query_sum, steps[:1])
-    d_keys, d_values, query_sum, output_sum = together(d_keys, d_values, query_sum, output_sum)
-    grad_gate, grad_up, grad_down = plan.own_rows(feed_sum, local_rows)
+    d_keys, d_values, query_sum, output_sum, feed_sum = together(
+        d_keys, d_values, query_sum, output_sum, feed_sum
+    )
+    grad_gate, grad_up, grad_down = plan.own_rows(jnp.split(feed_sum, 3), local_rows)
     d_kvl_low = jnp.concatenate(
         [
             d_keys.reshape(rows, -1).astype(BF16),
@@ -571,7 +575,12 @@
     )
     laurel_spread = product(d_laurel_low, to_spread).astype(BF16)
     kvl_sum = plan.spread_begin([(normed_spread, d_kvl_low), (laurel_spread, latent_low)])
+    query_kept, query_away = plan.spread_send(query_sum, steps[1])
+    output_kept, output_away = plan.spread_send(output_sum, steps[1])
     kvl_sum = plan.spread_step(kvl_sum, steps[:1])
+    kvl_sum, query_kept, output_kept = together(kvl_sum, query_kept, output_kept)
+    query_sum = (query_kept + query_away).astype(BF16)
+    output_sum = (output_kept + output_away).astype(BF16)
     kvl_sum, d_queries_low, d_kvl_low = together(kvl_sum, d_queries_low, d_kvl_low)
     d_spread = product_nt_split(d_queries_low, query_full) + product_nt_split(d_kvl_low, kvl_full)
     d_normed = d_normed + reorder(d_spread, to_spread)
@@ -592,9 +601,9 @@
         [plan.from_far_team(norm_grads).reshape(-1), grad_norm_query, grad_norm_key]
     )
     gain_grads, kvl_sum = together(gain_grads, kvl_sum)
-    grad_query = plan.spread_step(query_sum, steps[1:])
+    grad_query = plan.spread_step(query_sum, steps[2:])
     grad_output, grad_side_gate, grad_side_output = split_columns(
-        plan.spread_step(output_sum, steps[1:]), rest_widths
+        plan.spread_step(output_sum, steps[2:]), rest_widths
     )
     grad_key, grad_value, grad_left, grad_right = split_columns(
         plan.spread_step(kvl_sum, steps[1:]), kvl_widths

time: 1250 us -> 1210 us (0.968)
  waiting for transfers between devices: 639 us -> 558 us
  matrix products: 257 us -> 272 us
  other arithmetic: 109 us -> 124 us
    ppermute x78, waiting for transfers between devices: 638 us -> 557 us  [swap(): return lax.ppermute(value, axis, [(0, 1), (1, 0)])]
    unnamed x463 -> x454, local copies, waits for them, and re-layouts: 56.9 us -> 52.7 us
  transfers between devices with their start and end apart: 82 -> 82, of which waited for: 45 -> 39; matrix products, arithmetic and copies ran while one was open for 33% -> 39% of each run, Pallas kernels for 0% -> 0%
where the time goes in v8:
time: 1210 us; the launch traced here: 1200 us
  waiting for transfers between devices  558 us (46%)
  matrix products  272 us (22%)
  local copies, waits for them, and re-layouts  155 us (13%)
  other arithmetic  124 us (10%)
  starting transfers between devices  71.9 us (6%)
  between operations  18.1 us (1%)
    ppermute x78, waiting for transfers between devices, swap(): return lax.ppermute(value, axis, [(0, 1), (1, 0)])  557 us
    dot_general x33, matrix products, product(): return jnp.dot(left, right, preferred_element_type=F32)  106 us
    dot_general x31, matrix products, product_nt(): lax.dot_general(left, right, (((1,), (1,)), ((), ())), preferred_element_...  95.1 us
    ppermute x78, starting transfers between devices, swap(): return lax.ppermute(value, axis, [(0, 1), (1, 0)])  61.7 us
    dot_general x15, matrix products, product_tn(): lax.dot_general(left, right, (((0,), (0,)), ((), ())), preferred_element_...  55.2 us
    unnamed x454, local copies, waits for them, and re-layouts  52.7 us
  transfers between devices with their start and end apart: 82, of which 39 were waited for; matrix products, arithmetic and copies ran while one was open for 39% of the time, Pallas kernels for 0%

profile of v8, /device:TPU:0, one launch (start us, length us, event | category | flops | bytes accessed | tf_op | source)
XLA Modules:
  0.0 1198.7 jit_solution(3393122848158204067)
XLA Ops:
  14.4 5.4 all-to-all-start
  24.6 45.8 %collective-permute-done = bf16[64,5760]{1,0:T(8,128)(2,1)} collective-permute-done((bf16[64,5760]{1,0:T(8,128)(2,1)S(1)}, bf16[64,5760]{1,0:T(8,128)(2,1)}, u32[]{:S(2)}, u32[]{:S(2)}) %collective-permute-start) | collective-permute-done | bytes 737312 | tf_op jit(solution)/shard_map/ppermute | solution.py:73
  82.3 55.7 %collective-permute-done.1 = bf16[128,5760]{1,0:T(8,128)(2,1)S(1)} collective-permute-done((bf16[128,5760]{1,0:T(8,128)(2,1)S(1)}, bf16[128,5760]{1,0:T(8,128)(2,1)S(1)}, u32[]{:S(2)}, u32[]{:S(2)}) %collective-permute-start.1) | collective-permute-done | bytes 1474592 | tf_op jit(solution)/shard_map/ppermute | solution.py:73
  140.5 9.0 collective-permute-done.2
  158.7 15.3 %collective-permute-done.3 = bf16[512,1152]{1,0:T(8,128)(2,1)} collective-permute-done((bf16[512,1152]{1,0:T(8,128)(2,1)}, bf16[512,1152]{1,0:T(8,128)(2,1)}, u32[]{:S(2)}, u32[]{:S(2)}) %collective-permute-start.3) | collective-permute-done | bytes 1179680 | tf_op jit(solution)/shard_map/ppermute | solution.py:73
  177.3 5.2 fusion.76
  185.4 7.8 collective-permute-done.11
  226.3 6.0 rev.69
  252.8 31.1 %collective-permute-done.6 = bf16[2,1,2,128,2,256]{5,3,4,2,1,0:T(8,128)(2,1)S(1)} collective-permute-done((bf16[2,1,2,128,2,256]{5,3,4,2,1,0:T(8,128)(2,1)S(1)}, bf16[2,1,2,128,2,256]{5,3,4,2,1,0:T(8,128)(2,1)S(1)}, u32[]{:S(2)}, u32[]{:S(2)}) %collective-permute-start.6) | collective-permute-done | bytes 524320 | tf_op jit(solution)/shard_map/ppermute | solution.py:73
  288.9 47.8 %collective-permute-done.7 = bf16[1,2,2,128,2,256]{5,3,4,2,1,0:T(8,128)(2,1)S(1)} collective-permute-done((bf16[1,2,2,128,2,256]{5,3,4,2,1,0:T(8,128)(2,1)S(1)}, bf16[1,2,2,128,2,256]{5,3,4,2,1,0:T(8,128)(2,1)S(1)}, u32[]{:S(2)}, u32[]{:S(2)}) %collective-permute-start.7) | collective-permute-done | bytes 524320 | tf_op jit(solution)/shard_map/ppermute | solution.py:73
  347.3 15.7 %collective-permute-done.8 = bf16[2,2,2,128,2,256]{5,3,4,2,1,0:T(8,128)(2,1)S(1)} collective-permute-done((bf16[2,2,2,128,2,256]{5,3,4,2,1,0:T(8,128)(2,1)S(1)}, bf16[2,2,2,128,2,256]{5,3,4,2,1,0:T(8,128)(2,1)S(1)}, u32[]{:S(2)}, u32[]{:S(2)}) %collective-permute-start.8) | collective-permute-done | bytes 1048608 | tf_op jit(solution)/shard_map/ppermute | solution.py:73
  387.9 30.5 %collective-permute-done.16 = bf16[512,2560]{1,0:T(8,128)(2,1)} collective-permute-done((bf16[512,2560]{1,0:T(8,128)(2,1)}, bf16[512,2560]{1,0:T(8,128)(2,1)}, u32[]{:S(2)}, u32[]{:S(2)}) %collective-permute-start.16) | collective-permute-done | bytes 2621472 | tf_op jit(solution)/shard_map/ppermute | solution.py:73
  440.7 4.7 fusion.5
  457.9 5.8 fusion.296
  467.6 6.3 multiply_convert_fusion.7
  476.3 5.4 collective-permute-done.19
  485.5 10.1 collective-permute-done.25
  532.0 11.8 collective-permute-done.33
  548.7 20.2 %collective-permute-done.34 = bf16[256,2048]{1,0:T(8,128)(2,1)S(1)} collective-permute-done((bf16[256,2048]{1,0:T(8,128)(2,1)S(1)}, bf16[256,2048]{1,0:T(8,128)(2,1)S(1)}, u32[]{:S(2)}, u32[]{:S(2)}) %collective-permute-start.34) | collective-permute-done | bytes 1048608 | tf_op jit(solution)/shard_map/ppermute | solution.py:73
  587.3 4.7 multiply_convert_fusion.3
  600.9 9.6 collective-permute-done.36
  616.6 9.0 collective-permute-done.40
  629.6 5.2 multiply_convert_fusion.2
  639.3 5.0 add_convert_fusion.7
  646.9 5.4 multiply_convert_fusion.1
  656.7 4.6 add_convert_fusion.6
  682.3 10.9 fusion.58
  693.2 11.8 fusion.61
  709.6 13.9 %fusion.64 = bf16[2048,1024]{1,0:T(8,128)(2,1)} fusion(bf16[512,1024]{1,0:T(8,128)(2,1)} %copy-done.198, bf16[512,1024]{1,0:T(8,128)(2,1)} %get-tuple-element.120, bf16[512,1024]{1,0:T(8,128)(2,1)} %copy-done.196, bf16[512,1024]{1,0:T(8,128)(2,1)} %copy-done.195, bf16[512,2048]{1,0:T(8,128)(2,1)} %copy-done.94, bf16[512,2048]{1,0:T(8,128)(2,1)} %copy-done.83, ...), kind=kOutput, calls=%fused_computation.77 | convolution fusion | flops 8642363392 | bytes 16777216 | tf_op jit(solution)/shard_map/dot_general | solution.py:34
  723.5 9.0 pad_maximum_fusion
  736.7 6.2 fusion.69
  756.0 6.6 collective-permute-done.53
  765.1 11.8 collective-permute-done.54
  795.4 4.9 fusion.19
  809.1 32.6 %collective-permute-done.52 = bf16[512,2048]{1,0:T(8,128)(2,1)S(1)} collective-permute-done((bf16[512,2048]{1,0:T(8,128)(2,1)S(1)}, bf16[512,2048]{1,0:T(8,128)(2,1)S(1)}, u32[]{:S(2)}, u32[]{:S(2)}) %collective-permute-start.52) | collective-permute-done | bytes 2097184 | tf_op jit(solution)/shard_map/ppermute | solution.py:73
  883.8 14.7 %collective-permute-done.57 = bf16[2,2,2,128,2,256]{5,3,4,2,1,0:T(8,128)(2,1)} collective-permute-done((bf16[2,2,2,128,2,256]{5,3,4,2,1,0:T(8,128)(2,1)}, bf16[2,2,2,128,2,256]{5,3,4,2,1,0:T(8,128)(2,1)}, u32[]{:S(2)}, u32[]{:S(2)}) %collective-permute-start.57) | collective-permute-done | bytes 1048608 | tf_op jit(solution)/shard_map/ppermute | solution.py:73
  901.5 20.3 %collective-permute-done.55 = bf16[2,2,2,128,2,256]{5,3,4,2,1,0:T(8,128)(2,1)S(1)} collective-permute-done((bf16[2,2,2,128,2,256]{5,3,4,2,1,0:T(8,128)(2,1)S(1)}, bf16[2,2,2,128,2,256]{5,3,4,2,1,0:T(8,128)(2,1)S(1)}, u32[]{:S(2)}, u32[]{:S(2)}) %collective-permute-start.55) | collective-permute-done | bytes 1048608 | tf_op jit(solution)/shard_map/ppermute | solution.py:73
  927.7 15.8 %collective-permute-done.58 = bf16[2,2,128,2,256]{4,2,3,1,0:T(8,128)(2,1)} collective-permute-done((bf16[2,2,128,2,256]{4,2,3,1,0:T(8,128)(2,1)}, bf16[2,2,128,2,256]{4,2,3,1,0:T(8,128)(2,1)}, u32[]{:S(2)}, u32[]{:S(2)}) %collective-permute-start.58) | collective-permute-done | bytes 524320 | tf_op jit(solution)/shard_map/ppermute | solution.py:73
  953.5 23.7 %collective-permute-done.59 = bf16[2,2,128,2,256]{4,2,3,1,0:T(8,128)(2,1)S(1)} collective-permute-done((bf16[2,2,128,2,256]{4,2,3,1,0:T(8,128)(2,1)S(1)}, bf16[2,2,128,2,256]{4,2,3,1,0:T(8,128)(2,1)S(1)}, u32[]{:S(2)}, u32[]{:S(2)}) %collective-permute-start.59) | collective-permute-done | bytes 524320 | tf_op jit(solution)/shard_map/ppermute | solution.py:73
  979.0 16.7 %collective-permute-done.61 = bf16[512,2048]{1,0:T(8,128)(2,1)S(1)} collective-permute-done((bf16[512,2048]{1,0:T(8,128)(2,1)S(1)}, bf16[512,2048]{1,0:T(8,128)(2,1)S(1)}, u32[]{:S(2)}, u32[]{:S(2)}) %collective-permute-start.61) | collective-permute-done | bytes 2097184 | tf_op jit(solution)/shard_map/ppermute | solution.py:73
  1002.6 7.4 fusion.75
  1033.2 33.8 %collective-permute-done.63 = bf16[512,1152]{0,1:T(8,128)(2,1)} collective-permute-done((bf16[512,1152]{0,1:T(8,128)(2,1)}, bf16[512,1152]{0,1:T(8,128)(2,1)}, u32[]{:S(2)}, u32[]{:S(2)}) %collective-permute-start.63) | collective-permute-done | bytes 1179680 | tf_op jit(solution)/shard_map/ppermute | solution.py:73
  1086.9 4.7 fusion.1
  1098.9 4.9 fusion.7
  1119.2 7.1 collective-permute-done.77
  1132.2 15.7 %collective-permute-done.71 = bf16[128,2560]{1,0:T(8,128)(2,1)S(1)} collective-permute-done((bf16[128,2560]{1,0:T(8,128)(2,1)S(1)}, bf16[128,2560]{1,0:T(8,128)(2,1)S(1)}, u32[]{:S(2)}, u32[]{:S(2)}) %collective-permute-start.71) | collective-permute-done | bytes 655392 | tf_op jit(solution)/shard_map/ppermute | solution.py:73
  1149.0 8.2 collective-permute-done.68
  1157.6 14.0 %collective-permute-done.72 = bf16[64,2560]{1,0:T(8,128)(2,1)S(1)} collective-permute-done((bf16[64,2560]{1,0:T(8,128)(2,1)S(1)}, bf16[64,2560]{1,0:T(8,128)(2,1)S(1)}, u32[]{:S(2)}, u32[]{:S(2)}) %collective-permute-start.72) | collective-permute-done | bytes 327712 | tf_op jit(solution)/shard_map/ppermute | solution.py:73
  (952 shorter events, 502.7 us)
Async XLA Ops:
  14.4 58.2 %all-to-all-start = ((bf16[8,192,1024]{2,1,0:T(8,128)(2,1)}), bf16[8,192,1024]{2,1,0:T(8,128)(2,1)}, u32[]{:S(2)}, u32[]{:S(2)}) async-start(bf16[8,192,1024]{2,1,0:T(8,128)(2,1)} %copy.521), calls=%async_computation | async-start | bytes 6291456 | tf_op jit(solution)/shard_map/all_to_all | solution.py:324
  19.8 410.4 %all-gather.2.cloned.1.call-start = ((), (), s32[]{:S(2)}) async-start(), calls=%async_computation.3 | async-start | bytes 15728640 | tf_op jit(solution)/shard_map/all_gather | solution.py:334
  20.1 50.3 %collective-permute-start = (bf16[64,5760]{1,0:T(8,128)(2,1)S(1)}, bf16[64,5760]{1,0:T(8,128)(2,1)}, u32[]{:S(2)}, u32[]{:S(2)}) collective-permute-start(bf16[64,5760]{1,0:T(8,128)(2,1)S(1)} %concatenate.188), channel_id=1, source_target_pairs={{0,16},{16,0},{1,17},{17,1},{2,18},{18,2},{3,19},{19,3},{4,20},{20... | collective-permute-start | bytes 2211848 | tf_op jit(solution)/shard_map/ppermute | solution.py:73
  76.7 921.1 %reduce-scatter.2.cloned.1.call-start = ((), (), s32[]{:S(2)}) async-start(), calls=%async_computation.4 | async-start | bytes 15728640 | tf_op jit(solution)/shard_map/reduce_scatter | solution.py:506
  77.6 60.3 %collective-permute-start.1 = (bf16[128,5760]{1,0:T(8,128)(2,1)S(1)}, bf16[128,5760]{1,0:T(8,128)(2,1)S(1)}, u32[]{:S(2)}, u32[]{:S(2)}) collective-permute-start(bf16[128,5760]{1,0:T(8,128)(2,1)S(1)} %pad_maximum_fusion.12), channel_id=1, source_target_pairs={{0,8},{8,0},{1,9},{9,1},{2,10},{10,2},{3,11},{11,3},{4,12},{12,4},... | collective-permute-start | bytes 4423688 | tf_op jit(solution)/shard_map/ppermute | solution.py:73
  157.1 36.1 %collective-permute-start.11 = (bf16[256,2048]{1,0:T(8,128)(2,1)S(1)}, bf16[256,2048]{1,0:T(8,128)(2,1)}, u32[]{:S(2)}, u32[]{:S(2)}) collective-permute-start(bf16[256,2048]{1,0:T(8,128)(2,1)S(1)} %slice.701), channel_id=1, source_target_pairs={{0,2},{2,0},{1,3},{3,1},{4,6},{6,4},{5,7},{7,5},{8,10},{10,8},{9,1... | collective-permute-start | bytes 3145736 | tf_op jit(solution)/shard_map/ppermute | solution.py:73
  158.7 37.3 %collective-permute-start.4 = (bf16[512,1152]{1,0:T(8,128)(2,1)}, bf16[512,1152]{1,0:T(8,128)(2,1)}, u32[]{:S(2)}, u32[]{:S(2)}) collective-permute-start(bf16[512,1152]{1,0:T(8,128)(2,1)} %pad_maximum_fusion.13), channel_id=1, source_target_pairs={{0,1},{1,0},{2,3},{3,2},{4,5},{5,4},{6,7},{7,6},{8,9},{9,8},{10,11... | collective-permute-start | bytes 3538952 | tf_op jit(solution)/shard_map/ppermute | solution.py:73
  196.0 144.0 %collective-permute-start.13 = (bf16[512,2048]{1,0:T(8,128)(2,1)}, bf16[512,2048]{1,0:T(8,128)(2,1)}, u32[]{:S(2)}, u32[]{:S(2)}) collective-permute-start(bf16[512,2048]{1,0:T(8,128)(2,1)} %pad_maximum_fusion.7), channel_id=1, source_target_pairs={{0,1},{1,0},{2,3},{3,2},{4,5},{5,4},{6,7},{7,6},{8,9},{9,8},{10,11... | collective-permute-start | bytes 6291464 | tf_op jit(solution)/shard_map/ppermute | solution.py:73
  196.0 56.6 %collective-permute-start.12 = (bf16[512,2048]{1,0:T(8,128)(2,1)}, bf16[512,2048]{1,0:T(8,128)(2,1)}, u32[]{:S(2)}, u32[]{:S(2)}) collective-permute-start(bf16[512,2048]{1,0:T(8,128)(2,1)} %pad_maximum_fusion.7), channel_id=1, source_target_pairs={{0,4},{4,0},{1,5},{5,1},{2,6},{6,2},{3,7},{7,3},{8,12},{12,8},{9,1... | collective-permute-start | bytes 6291464 | tf_op jit(solution)/shard_map/ppermute | solution.py:73
  245.9 38.0 %collective-permute-start.6 = (bf16[2,1,2,128,2,256]{5,3,4,2,1,0:T(8,128)(2,1)S(1)}, bf16[2,1,2,128,2,256]{5,3,4,2,1,0:T(8,128)(2,1)S(1)}, u32[]{:S(2)}, u32[]{:S(2)}) collective-permute-start(bf16[2,1,2,128,2,256]{5,3,4,2,1,0:T(8,128)(2,1)S(1)} %maximum_bitcast_fusion), channel_id=1, source_target_pairs={{0,16},{16,0},{1,17},{17,1},{2,18},{18,2},{3,19},{19,3},{4,20},{20... | collective-permute-start | bytes 1572872 | tf_op jit(solution)/shard_map/ppermute | solution.py:73
  245.9 96.3 %collective-permute-start.15 = (bf16[256,2560]{1,0:T(8,128)(2,1)}, bf16[256,2560]{1,0:T(8,128)(2,1)S(1)}, u32[]{:S(2)}, u32[]{:S(2)}) collective-permute-start(bf16[256,2560]{1,0:T(8,128)(2,1)} %slice.691), channel_id=1, source_target_pairs={{0,2},{2,0},{1,3},{3,1},{4,6},{6,4},{5,7},{7,5},{8,10},{10,8},{9,1... | collective-permute-start | bytes 3932168 | tf_op jit(solution)/shard_map/ppermute | solution.py:73
  252.6 123.4 %collective-permute-start.14 = (bf16[512,2048]{1,0:T(8,128)(2,1)}, bf16[512,2048]{1,0:T(8,128)(2,1)}, u32[]{:S(2)}, u32[]{:S(2)}) collective-permute-start(bf16[512,2048]{1,0:T(8,128)(2,1)} %collective-permute-done.12), channel_id=1, source_target_pairs={{0,1},{1,0},{2,3},{3,2},{4,5},{5,4},{6,7},{7,6},{8,9},{9,8},{10,11... | collective-permute-start | bytes 6291464 | tf_op jit(solution)/shard_map/ppermute | solution.py:73
  284.0 52.8 %collective-permute-start.7 = (bf16[1,2,2,128,2,256]{5,3,4,2,1,0:T(8,128)(2,1)S(1)}, bf16[1,2,2,128,2,256]{5,3,4,2,1,0:T(8,128)(2,1)S(1)}, u32[]{:S(2)}, u32[]{:S(2)}) collective-permute-start(bf16[1,2,2,128,2,256]{5,3,4,2,1,0:T(8,128)(2,1)S(1)} %get-tuple-element.455), channel_id=1, source_target_pairs={{0,8},{8,0},{1,9},{9,1},{2,10},{10,2},{3,11},{11,3},{4,12},{12,4},... | collective-permute-start | bytes 1572872 | tf_op jit(solution)/shard_map/ppermute | solution.py:73
  284.1 54.4 %collective-permute-start.9 = (bf16[1,2,2,128,2,256]{5,3,4,2,1,0:T(8,128)(2,1)S(1)}, bf16[1,2,2,128,2,256]{5,3,4,2,1,0:T(8,128)(2,1)S(1)}, u32[]{:S(2)}, u32[]{:S(2)}) collective-permute-start(bf16[1,2,2,128,2,256]{5,3,4,2,1,0:T(8,128)(2,1)S(1)} %get-tuple-element.454), channel_id=1, source_target_pairs={{0,4},{4,0},{1,5},{5,1},{2,6},{6,2},{3,7},{7,3},{8,12},{12,8},{9,1... | collective-permute-start | bytes 1572872 | tf_op jit(solution)/shard_map/ppermute | solution.py:73
  336.9 26.1 %collective-permute-start.8 = (bf16[2,2,2,128,2,256]{5,3,4,2,1,0:T(8,128)(2,1)S(1)}, bf16[2,2,2,128,2,256]{5,3,4,2,1,0:T(8,128)(2,1)S(1)}, u32[]{:S(2)}, u32[]{:S(2)}) collective-permute-start(bf16[2,2,2,128,2,256]{5,3,4,2,1,0:T(8,128)(2,1)S(1)} %get-tuple-element.457), channel_id=1, source_target_pairs={{0,4},{4,0},{1,5},{5,1},{2,6},{6,2},{3,7},{7,3},{8,12},{12,8},{9,1... | collective-permute-start | bytes 3145736 | tf_op jit(solution)/shard_map/ppermute | solution.py:73
  339.9 33.1 %collective-permute-start.10 = (bf16[2,2,2,128,2,256]{5,3,4,2,1,0:T(8,128)(2,1)}, bf16[2,2,2,128,2,256]{5,3,4,2,1,0:T(8,128)(2,1)}, u32[]{:S(2)}, u32[]{:S(2)}) collective-permute-start(bf16[2,2,2,128,2,256]{5,3,4,2,1,0:T(8,128)(2,1)} %get-tuple-element.453), channel_id=1, source_target_pairs={{0,8},{8,0},{1,9},{9,1},{2,10},{10,2},{3,11},{11,3},{4,12},{12,4},... | collective-permute-start | bytes 3145736 | tf_op jit(solution)/shard_map/ppermute | solution.py:73
  343.4 74.9 %collective-permute-start.16 = (bf16[512,2560]{1,0:T(8,128)(2,1)}, bf16[512,2560]{1,0:T(8,128)(2,1)}, u32[]{:S(2)}, u32[]{:S(2)}) collective-permute-start(bf16[512,2560]{1,0:T(8,128)(2,1)} %constant_dynamic-update-slice_fusion.8), channel_id=1, source_target_pairs={{0,4},{4,0},{1,5},{5,1},{2,6},{6,2},{3,7},{7,3},{8,12},{12,8},{9,1... | collective-permute-start | bytes 7864328 | tf_op jit(solution)/shard_map/ppermute | solution.py:73
  347.3 90.3 %collective-permute-start.17 = (bf16[512,2560]{1,0:T(8,128)(2,1)}, bf16[512,2560]{1,0:T(8,128)(2,1)}, u32[]{:S(2)}, u32[]{:S(2)}) collective-permute-start(bf16[512,2560]{1,0:T(8,128)(2,1)} %constant_dynamic-update-slice_fusion.8), channel_id=1, source_target_pairs={{0,1},{1,0},{2,3},{3,2},{4,5},{5,4},{6,7},{7,6},{8,9},{9,8},{10,11... | collective-permute-start | bytes 7864328 | tf_op jit(solution)/shard_map/ppermute | solution.py:73
  456.3 25.4 %collective-permute-start.19 = (bf16[256,2048]{1,0:T(8,128)(2,1)}, bf16[256,2048]{1,0:T(8,128)(2,1)S(1)}, u32[]{:S(2)}, u32[]{:S(2)}) collective-permute-start(bf16[256,2048]{1,0:T(8,128)(2,1)} %multiply_convert_fusion.8), channel_id=1, source_target_pairs={{0,4},{4,0},{1,5},{5,1},{2,6},{6,2},{3,7},{7,3},{8,12},{12,8},{9,1... | collective-permute-start | bytes 3145736 | tf_op jit(solution)/shard_map/ppermute | solution.py:73
  457.9 25.0 %collective-permute-start.20 = (bf16[256,2048]{1,0:T(8,128)(2,1)}, bf16[256,2048]{1,0:T(8,128)(2,1)S(1)}, u32[]{:S(2)}, u32[]{:S(2)}) collective-permute-start(bf16[256,2048]{1,0:T(8,128)(2,1)} %multiply_convert_fusion.8), channel_id=1, source_target_pairs={{0,8},{8,0},{1,9},{9,1},{2,10},{10,2},{3,11},{11,3},{4,12},{12,4},... | collective-permute-start | bytes 3145736 | tf_op jit(solution)/shard_map/ppermute | solution.py:73
  485.4 63.3 %collective-permute-start.22 = (bf16[256,2048]{1,0:T(8,128)(2,1)S(1)}, bf16[256,2048]{1,0:T(8,128)(2,1)}, u32[]{:S(2)}, u32[]{:S(2)}) collective-permute-start(bf16[256,2048]{1,0:T(8,128)(2,1)S(1)} %slice.557), channel_id=1, source_target_pairs={{0,1},{1,0},{2,3},{3,2},{4,5},{5,4},{6,7},{7,6},{8,9},{9,8},{10,11... | collective-permute-start | bytes 3145736 | tf_op jit(solution)/shard_map/ppermute | solution.py:73
  544.0 24.8 %collective-permute-start.34 = (bf16[256,2048]{1,0:T(8,128)(2,1)S(1)}, bf16[256,2048]{1,0:T(8,128)(2,1)S(1)}, u32[]{:S(2)}, u32[]{:S(2)}) collective-permute-start(bf16[256,2048]{1,0:T(8,128)(2,1)S(1)} %pad_maximum_fusion.19), channel_id=1, source_target_pairs={{0,4},{4,0},{1,5},{5,1},{2,6},{6,2},{3,7},{7,3},{8,12},{12,8},{9,1... | collective-permute-start | bytes 3145736 | tf_op jit(solution)/shard_map/ppermute | solution.py:73
  545.6 24.5 %collective-permute-start.30 = (bf16[256,2048]{1,0:T(8,128)(2,1)S(1)}, bf16[256,2048]{1,0:T(8,128)(2,1)S(1)}, u32[]{:S(2)}, u32[]{:S(2)}) collective-permute-start(bf16[256,2048]{1,0:T(8,128)(2,1)S(1)} %pad_maximum_fusion.18), channel_id=1, source_target_pairs={{0,8},{8,0},{1,9},{9,1},{2,10},{10,2},{3,11},{11,3},{4,12},{12,4},... | collective-permute-start | bytes 3145736 | tf_op jit(solution)/shard_map/ppermute | solution.py:73
  585.1 25.5 %collective-permute-start.36 = (bf16[256,2048]{1,0:T(8,128)(2,1)S(1)}, bf16[256,2048]{1,0:T(8,128)(2,1)S(1)}, u32[]{:S(2)}, u32[]{:S(2)}) collective-permute-start(bf16[256,2048]{1,0:T(8,128)(2,1)S(1)} %fusion.111), channel_id=1, source_target_pairs={{0,4},{4,0},{1,5},{5,1},{2,6},{6,2},{3,7},{7,3},{8,12},{12,8},{9,1... | collective-permute-start | bytes 3145736 | tf_op jit(solution)/shard_map/ppermute | solution.py:73
  585.9 25.1 %collective-permute-start.37 = (bf16[256,2048]{1,0:T(8,128)(2,1)S(1)}, bf16[256,2048]{1,0:T(8,128)(2,1)S(1)}, u32[]{:S(2)}, u32[]{:S(2)}) collective-permute-start(bf16[256,2048]{1,0:T(8,128)(2,1)S(1)} %fusion.111), channel_id=1, source_target_pairs={{0,8},{8,0},{1,9},{9,1},{2,10},{10,2},{3,11},{11,3},{4,12},{12,4},... | collective-permute-start | bytes 3145736 | tf_op jit(solution)/shard_map/ppermute | solution.py:73
  614.5 30.9 %collective-permute-start.39 = (bf16[256,2048]{1,0:T(8,128)(2,1)S(1)}, bf16[256,2048]{1,0:T(8,128)(2,1)S(1)}, u32[]{:S(2)}, u32[]{:S(2)}) collective-permute-start(bf16[256,2048]{1,0:T(8,128)(2,1)S(1)} %collective-permute-done.37), channel_id=1, source_target_pairs={{0,1},{1,0},{2,3},{3,2},{4,5},{5,4},{6,7},{7,6},{8,9},{9,8},{10,11... | collective-permute-start | bytes 3145736 | tf_op jit(solution)/shard_map/ppermute | solution.py:73
  614.6 47.8 %collective-permute-start.43 = (bf16[256,2048]{1,0:T(8,128)(2,1)S(1)}, bf16[256,2048]{1,0:T(8,128)(2,1)}, u32[]{:S(2)}, u32[]{:S(2)}) collective-permute-start(bf16[256,2048]{1,0:T(8,128)(2,1)S(1)} %slice.581), channel_id=1, source_target_pairs={{0,1},{1,0},{2,3},{3,2},{4,5},{5,4},{6,7},{7,6},{8,9},{9,8},{10,11... | collective-permute-start | bytes 3145736 | tf_op jit(solution)/shard_map/ppermute | solution.py:73
  626.9 37.2 %collective-permute-start.42 = (bf16[256,2048]{1,0:T(8,128)(2,1)S(1)}, bf16[256,2048]{1,0:T(8,128)(2,1)S(1)}, u32[]{:S(2)}, u32[]{:S(2)}) collective-permute-start(bf16[256,2048]{1,0:T(8,128)(2,1)S(1)} %pad_maximum_fusion.20), channel_id=1, source_target_pairs={{0,1},{1,0},{2,3},{3,2},{4,5},{5,4},{6,7},{7,6},{8,9},{9,8},{10,11... | collective-permute-start | bytes 3145736 | tf_op jit(solution)/shard_map/ppermute | solution.py:73
  645.4 30.6 %collective-permute-start.44 = (bf16[256,2048]{1,0:T(8,128)(2,1)}, bf16[256,2048]{1,0:T(8,128)(2,1)}, u32[]{:S(2)}, u32[]{:S(2)}) collective-permute-start(bf16[256,2048]{1,0:T(8,128)(2,1)} %slice.733), channel_id=1, source_target_pairs={{0,1},{1,0},{2,3},{3,2},{4,5},{5,4},{6,7},{7,6},{8,9},{9,8},{10,11... | collective-permute-start | bytes 3145736 | tf_op jit(solution)/shard_map/ppermute | solution.py:73
  679.6 25.6 %collective-permute-start.49 = (bf16[128,2048]{1,0:T(8,128)(2,1)S(1)}, bf16[128,2048]{1,0:T(8,128)(2,1)S(1)}, u32[]{:S(2)}, u32[]{:S(2)}) collective-permute-start(bf16[128,2048]{1,0:T(8,128)(2,1)S(1)} %get-tuple-element.449), channel_id=1, source_target_pairs={{0,8},{8,0},{1,9},{9,1},{2,10},{10,2},{3,11},{11,3},{4,12},{12,4},... | collective-permute-start | bytes 1572872 | tf_op jit(solution)/shard_map/ppermute | solution.py:73
  680.3 27.4 %collective-permute-start.47 = (bf16[128,2048]{1,0:T(8,128)(2,1)S(1)}, bf16[128,2048]{1,0:T(8,128)(2,1)S(1)}, u32[]{:S(2)}, u32[]{:S(2)}) collective-permute-start(bf16[128,2048]{1,0:T(8,128)(2,1)S(1)} %get-tuple-element.448), channel_id=1, source_target_pairs={{0,4},{4,0},{1,5},{5,1},{2,6},{6,2},{3,7},{7,3},{8,12},{12,8},{9,1... | collective-permute-start | bytes 1572872 | tf_op jit(solution)/shard_map/ppermute | solution.py:73
  706.4 26.2 %collective-permute-start.50 = (bf16[256,2048]{1,0:T(8,128)(2,1)}, bf16[256,2048]{1,0:T(8,128)(2,1)}, u32[]{:S(2)}, u32[]{:S(2)}) collective-permute-start(bf16[256,2048]{1,0:T(8,128)(2,1)} %pad_maximum_fusion.22), channel_id=1, source_target_pairs={{0,4},{4,0},{1,5},{5,1},{2,6},{6,2},{3,7},{7,3},{8,12},{12,8},{9,1... | collective-permute-start | bytes 3145736 | tf_op jit(solution)/shard_map/ppermute | solution.py:73
  708.9 24.8 %collective-permute-start.48 = (bf16[256,2048]{1,0:T(8,128)(2,1)}, bf16[256,2048]{1,0:T(8,128)(2,1)S(1)}, u32[]{:S(2)}, u32[]{:S(2)}) collective-permute-start(bf16[256,2048]{1,0:T(8,128)(2,1)} %pad_maximum_fusion.21), channel_id=1, source_target_pairs={{0,8},{8,0},{1,9},{9,1},{2,10},{10,2},{3,11},{11,3},{4,12},{12,4},... | collective-permute-start | bytes 3145736 | tf_op jit(solution)/shard_map/ppermute | solution.py:73
  753.8 33.7 %collective-permute-start.51 = (bf16[1024,2048]{1,0:T(8,128)(2,1)S(1)}, bf16[1024,2048]{1,0:T(8,128)(2,1)S(1)}, u32[]{:S(2)}, u32[]{:S(2)}) collective-permute-start(bf16[1024,2048]{1,0:T(8,128)(2,1)S(1)} %convolution_convert_fusion.3), channel_id=1, source_target_pairs={{0,1},{1,0},{2,3},{3,2},{4,5},{5,4},{6,7},{7,6},{8,9},{9,8},{10,11... | collective-permute-start | bytes 12582920 | tf_op jit(solution)/shard_map/ppermute | solution.py:73
  794.9 46.9 %collective-permute-start.52 = (bf16[512,2048]{1,0:T(8,128)(2,1)S(1)}, bf16[512,2048]{1,0:T(8,128)(2,1)S(1)}, u32[]{:S(2)}, u32[]{:S(2)}) collective-permute-start(bf16[512,2048]{1,0:T(8,128)(2,1)S(1)} %slice.602), channel_id=1, source_target_pairs={{0,4},{4,0},{1,5},{5,1},{2,6},{6,2},{3,7},{7,3},{8,12},{12,8},{9,1... | collective-permute-start | bytes 6291464 | tf_op jit(solution)/shard_map/ppermute | solution.py:73
  861.1 85.5 %collective-permute-start.60 = (bf16[1024,2048]{1,0:T(8,128)(2,1)}, bf16[1024,2048]{1,0:T(8,128)(2,1)}, u32[]{:S(2)}, u32[]{:S(2)}) collective-permute-start(bf16[1024,2048]{1,0:T(8,128)(2,1)} %convolution_convert_fusion.2), channel_id=1, source_target_pairs={{0,1},{1,0},{2,3},{3,2},{4,5},{5,4},{6,7},{7,6},{8,9},{9,8},{10,11... | collective-permute-start | bytes 12582920 | tf_op jit(solution)/shard_map/ppermute | solution.py:73
  872.8 25.8 %collective-permute-start.57 = (bf16[2,2,2,128,2,256]{5,3,4,2,1,0:T(8,128)(2,1)}, bf16[2,2,2,128,2,256]{5,3,4,2,1,0:T(8,128)(2,1)}, u32[]{:S(2)}, u32[]{:S(2)}) collective-permute-start(bf16[2,2,2,128,2,256]{5,3,4,2,1,0:T(8,128)(2,1)} %slice_bitcast_fusion), channel_id=1, source_target_pairs={{0,4},{4,0},{1,5},{5,1},{2,6},{6,2},{3,7},{7,3},{8,12},{12,8},{9,1... | collective-permute-start | bytes 3145736 | tf_op jit(solution)/shard_map/ppermute | solution.py:73
  878.0 43.8 %collective-permute-start.55 = (bf16[2,2,2,128,2,256]{5,3,4,2,1,0:T(8,128)(2,1)S(1)}, bf16[2,2,2,128,2,256]{5,3,4,2,1,0:T(8,128)(2,1)S(1)}, u32[]{:S(2)}, u32[]{:S(2)}) collective-permute-start(bf16[2,2,2,128,2,256]{5,3,4,2,1,0:T(8,128)(2,1)S(1)} %bitcast.523), channel_id=1, source_target_pairs={{0,8},{8,0},{1,9},{9,1},{2,10},{10,2},{3,11},{11,3},{4,12},{12,4},... | collective-permute-start | bytes 3145736 | tf_op jit(solution)/shard_map/ppermute | solution.py:73
  901.0 42.5 %collective-permute-start.58 = (bf16[2,2,128,2,256]{4,2,3,1,0:T(8,128)(2,1)}, bf16[2,2,128,2,256]{4,2,3,1,0:T(8,128)(2,1)}, u32[]{:S(2)}, u32[]{:S(2)}) collective-permute-start(bf16[2,2,128,2,256]{4,2,3,1,0:T(8,128)(2,1)} %slice_bitcast_fusion.4), channel_id=1, source_target_pairs={{0,8},{8,0},{1,9},{9,1},{2,10},{10,2},{3,11},{11,3},{4,12},{12,4},... | collective-permute-start | bytes 1572872 | tf_op jit(solution)/shard_map/ppermute | solution.py:73
  945.9 31.3 %collective-permute-start.59 = (bf16[2,2,128,2,256]{4,2,3,1,0:T(8,128)(2,1)S(1)}, bf16[2,2,128,2,256]{4,2,3,1,0:T(8,128)(2,1)S(1)}, u32[]{:S(2)}, u32[]{:S(2)}) collective-permute-start(bf16[2,2,128,2,256]{4,2,3,1,0:T(8,128)(2,1)S(1)} %fusion.202), channel_id=1, source_target_pairs={{0,16},{16,0},{1,17},{17,1},{2,18},{18,2},{3,19},{19,3},{4,20},{20... | collective-permute-start | bytes 1572872 | tf_op jit(solution)/shard_map/ppermute | solution.py:73
  950.4 45.3 %collective-permute-start.61 = (bf16[512,2048]{1,0:T(8,128)(2,1)S(1)}, bf16[512,2048]{1,0:T(8,128)(2,1)S(1)}, u32[]{:S(2)}, u32[]{:S(2)}) collective-permute-start(bf16[512,2048]{1,0:T(8,128)(2,1)S(1)} %slice.769), channel_id=1, source_target_pairs={{0,4},{4,0},{1,5},{5,1},{2,6},{6,2},{3,7},{7,3},{8,12},{12,8},{9,1... | collective-permute-start | bytes 6291464 | tf_op jit(solution)/shard_map/ppermute | solution.py:73
  1021.0 46.0 %collective-permute-start.63 = (bf16[512,1152]{0,1:T(8,128)(2,1)}, bf16[512,1152]{0,1:T(8,128)(2,1)}, u32[]{:S(2)}, u32[]{:S(2)}) collective-permute-start(bf16[512,1152]{0,1:T(8,128)(2,1)} %slice.773), channel_id=1, source_target_pairs={{0,4},{4,0},{1,5},{5,1},{2,6},{6,2},{3,7},{7,3},{8,12},{12,8},{9,1... | collective-permute-start | bytes 3538952 | tf_op jit(solution)/shard_map/ppermute | solution.py:73
  1024.3 86.6 %collective-permute-start.64 = (bf16[256,2048]{1,0:T(8,128)(2,1)}, bf16[256,2048]{1,0:T(8,128)(2,1)}, u32[]{:S(2)}, u32[]{:S(2)}) collective-permute-start(bf16[256,2048]{1,0:T(8,128)(2,1)} %get-tuple-element.438), channel_id=1, source_target_pairs={{0,2},{2,0},{1,3},{3,1},{4,6},{6,4},{5,7},{7,5},{8,10},{10,8},{9,1... | collective-permute-start | bytes 3145736 | tf_op jit(solution)/shard_map/ppermute | solution.py:73
  1026.0 89.4 %collective-permute-start.70 = (bf16[256,2560]{1,0:T(8,128)(2,1)}, bf16[256,2560]{1,0:T(8,128)(2,1)}, u32[]{:S(2)}, u32[]{:S(2)}) collective-permute-start(bf16[256,2560]{1,0:T(8,128)(2,1)} %get-tuple-element.432), channel_id=1, source_target_pairs={{0,2},{2,0},{1,3},{3,1},{4,6},{6,4},{5,7},{7,5},{8,10},{10,8},{9,1... | collective-permute-start | bytes 3932168 | tf_op jit(solution)/shard_map/ppermute | solution.py:73
  1028.6 150.2 %all-to-all-start.1 = ((bf16[8,192,1024]{2,1,0:T(8,128)(2,1)}), bf16[8,192,1024]{2,1,0:T(8,128)(2,1)}, u32[]{:S(2)}, u32[]{:S(2)}) async-start(bf16[8,192,1024]{2,1,0:T(8,128)(2,1)} %pad_maximum_fusion.2), calls=%async_computation.2 | async-start | bytes 6291456 | tf_op jit(solution)/shard_map/all_to_all | solution.py:201
  1117.2 30.7 %collective-permute-start.71 = (bf16[128,2560]{1,0:T(8,128)(2,1)S(1)}, bf16[128,2560]{1,0:T(8,128)(2,1)S(1)}, u32[]{:S(2)}, u32[]{:S(2)}) collective-permute-start(bf16[128,2560]{1,0:T(8,128)(2,1)S(1)} %slice.789), channel_id=1, source_target_pairs={{0,8},{8,0},{1,9},{9,1},{2,10},{10,2},{3,11},{11,3},{4,12},{12,4},... | collective-permute-start | bytes 1966088 | tf_op jit(solution)/shard_map/ppermute | solution.py:73
  1131.4 25.9 %collective-permute-start.68 = (bf16[128,1152]{0,1:T(8,128)(2,1)S(1)}, bf16[128,1152]{0,1:T(8,128)(2,1)S(1)}, u32[]{:S(2)}, u32[]{:S(2)}) collective-permute-start(bf16[128,1152]{0,1:T(8,128)(2,1)S(1)} %slice.783), channel_id=1, source_target_pairs={{0,8},{8,0},{1,9},{9,1},{2,10},{10,2},{3,11},{11,3},{4,12},{12,4},... | collective-permute-start | bytes 884744 | tf_op jit(solution)/shard_map/ppermute | solution.py:73
  1148.1 23.5 %collective-permute-start.72 = (bf16[64,2560]{1,0:T(8,128)(2,1)S(1)}, bf16[64,2560]{1,0:T(8,128)(2,1)S(1)}, u32[]{:S(2)}, u32[]{:S(2)}) collective-permute-start(bf16[64,2560]{1,0:T(8,128)(2,1)S(1)} %slice.791), channel_id=1, source_target_pairs={{0,16},{16,0},{1,17},{17,1},{2,18},{18,2},{3,19},{19,3},{4,20},{20... | collective-permute-start | bytes 983048 | tf_op jit(solution)/shard_map/ppermute | solution.py:73
  (239 other events, 3824.9 us)
Sparse Core Ops, SparseCore 0:
  76.9 249.1 all-gather.1
  735.6 237.7 reduce-scatter.1

commit v9 on v8

--- a/solution.py
+++ b/solution.py
@@ -219,9 +219,12 @@
         by_x, by_l, results = together(by_x, by_l, results)
         half = own.shape[0] // 2
         both = jnp.concatenate([swap(by_x[:half], self.l), swap(by_l[half:], self.x)], axis=0)
-        for piece in (by_x, by_l, both):
+        for piece in (by_x, both):
             chunks.append(chunk_of(piece))
             results.append(function(chunks[-1]))
+        by_l, results = together(by_l, results)
+        chunks.append(chunk_of(by_l))
+        results.append(function(chunks[-1]))
         return chunks, results
 
     def core_sums(self, chunks):
@@ -233,7 +236,7 @@
         return sums
 
     def team_near(self, sums):
-        own, by_x, by_l, both = sums
+        own, by_x, both, by_l = sums
         half = own.shape[0] // 2
         both = both.astype(BF16)
         first = by_l[:half] + swap(both[:half], self.x).astype(F32)
@@ -330,9 +333,9 @@
         axis=1,
     )
     attn_block = plan.grow(attn_block, plan.far_seq)
+    attn_block = plan.grow(attn_block, (plan.l,))
     attn_block, feed_team = together(attn_block, feed_team)
     feed_full = lax.all_gather(feed_team.reshape(-1, hidden_own), plan.far, axis=0, tiled=True)
-    attn_block = plan.grow(attn_block, (plan.l,))
     kvl_block, query_block, rest_block = split_columns(attn_block, block_widths)
     kvl_block = plan.grow(kvl_block, plan.far_dp)
     query_block = plan.grow(query_block, plan.far_dp)
@@ -467,10 +470,6 @@
     d_resid_one, d_feed_out, grad_norm_after = after_pull(d_resid_two)
 
     d_out_low = d_feed_out.astype(BF16)
-    side_spread = product(jnp.concatenate([resid_low, d_side_out_low], axis=0), to_spread).astype(BF16)
-    side_sum = plan.spread_begin(
-        [(side_spread[:rows], d_side_pre_low), (side_spread[rows:], side_low)]
-    )
     d_gate_chunks = []
     d_up_chunks = []
 
@@ -507,7 +506,6 @@
         feed_terms.reshape(-1, hidden_own), plan.far, scatter_dimension=0, tiled=True
     )
     steps = tuple(reversed(plan.order))
-    side_sum = plan.spread_step(side_sum, steps[:1])
 
     (
         d_inputs,
@@ -536,10 +534,16 @@
     d_keys_all = jnp.einsum(
         "bkgts,btkgd->bskd", d_scores_low, query_group, preferred_element_type=F32
     )
-    d_keys_all, d_values_all, d_query_rot, output_sum, side_sum = together(
-        d_keys_all, d_values_all, d_query_rot, output_sum, side_sum
-    )
-    output_sum = jnp.concatenate([output_sum, side_sum], axis=1)
+    d_keys_all, d_values_all, d_query_rot, output_sum, side_left = together(
+        d_keys_all,
+        d_values_all,
+        d_query_rot,
+        output_sum,
+        jnp.concatenate([resid_low, d_side_out_low], axis=0),
+    )
+    side_left = product(side_left, to_spread).astype(BF16)
+    side_sum = plan.spread_begin([(side_left[:rows], d_side_pre_low), (side_left[rows:], side_low)])
+    side_sum = plan.spread_step(side_sum, steps[:1])
     if whole_sequence:
         d_pair_total = plan.near_sum(
             *[
@@ -561,9 +565,11 @@
     d_queries_low = d_queries.reshape(rows, -1).astype(BF16)
     query_sum = plan.spread_begin([(normed_spread, d_queries_low)])
     query_sum = plan.spread_step(query_sum, steps[:1])
-    d_keys, d_values, query_sum, output_sum, feed_sum = together(
-        d_keys, d_values, query_sum, output_sum, feed_sum
-    )
+    d_spread = product_nt_split(d_queries_low, query_full)
+    d_keys, d_values, query_sum, output_sum, side_sum, d_spread, feed_sum = together(
+        d_keys, d_values, query_sum, output_sum, side_sum, d_spread, feed_sum
+    )
+    output_sum = jnp.concatenate([output_sum, side_sum], axis=1)
     grad_gate, grad_up, grad_down = plan.own_rows(jnp.split(feed_sum, 3), local_rows)
     d_kvl_low = jnp.concatenate(
         [
@@ -581,8 +587,11 @@
     kvl_sum, query_kept, output_kept = together(kvl_sum, query_kept, output_kept)
     query_sum = (query_kept + query_away).astype(BF16)
     output_sum = (output_kept + output_away).astype(BF16)
-    kvl_sum, d_queries_low, d_kvl_low = together(kvl_sum, d_queries_low, d_kvl_low)
-    d_spread = product_nt_split(d_queries_low, query_full) + product_nt_split(d_kvl_low, kvl_full)
+    kvl_sum = plan.spread_step(kvl_sum, steps[1:2])
+    query_sum = plan.spread_step(query_sum, steps[2:3])
+    output_sum = plan.spread_step(output_sum, steps[2:3])
+    kvl_sum, query_sum, output_sum, d_kvl_low = together(kvl_sum, query_sum, output_sum, d_kvl_low)
+    d_spread = d_spread + product_nt_split(d_kvl_low, kvl_full)
     d_normed = d_normed + reorder(d_spread, to_spread)
     d_inputs_norm, grad_norm_input = pre_pull(d_normed)
     grad_tokens = reorder(d_inputs + d_inputs_norm, to_far_team).reshape(batch, block, width)
@@ -600,13 +609,12 @@
     gain_grads = jnp.concatenate(
         [plan.from_far_team(norm_grads).reshape(-1), grad_norm_query, grad_norm_key]
     )
-    gain_grads, kvl_sum = together(gain_grads, kvl_sum)
-    grad_query = plan.spread_step(query_sum, steps[2:])
+    grad_query = plan.spread_step(query_sum, steps[3:])
     grad_output, grad_side_gate, grad_side_output = split_columns(
-        plan.spread_step(output_sum, steps[2:]), rest_widths
+        plan.spread_step(output_sum, steps[3:]), rest_widths
     )
     grad_key, grad_value, grad_left, grad_right = split_columns(
-        plan.spread_step(kvl_sum, steps[1:]), kvl_widths
+        plan.spread_step(kvl_sum, steps[2:]), kvl_widths
     )
     gain_grads = plan.total(gain_grads)
     gain_parts = split_columns(gain_grads, [width] * 6 + [head_size] * 2)

time: 1210 us -> 1230 us (1.017)
    ppermute x78, waiting for transfers between devices: 557 us -> 569 us  [swap(): return lax.ppermute(value, axis, [(0, 1), (1, 0)])]
    unnamed x454 -> x496, local copies, waits for them, and re-layouts: 52.7 us -> 60.5 us
  transfers between devices with their start and end apart: 82 -> 82, of which waited for: 39 -> 39; matrix products, arithmetic and copies ran while one was open for 39% -> 36% of each run, Pallas kernels for 0% -> 0%
where the time goes in v9:
time: 1230 us; the launch traced here: 1220 us
  waiting for transfers between devices  569 us (46%)
  matrix products  264 us (21%)
  local copies, waits for them, and re-layouts  165 us (13%)
  other arithmetic  125 us (10%)
  starting transfers between devices  80.9 us (7%)
  between operations  18.3 us (1%)
    ppermute x78, waiting for transfers between devices, swap(): return lax.ppermute(value, axis, [(0, 1), (1, 0)])  569 us
    dot_general x33, matrix products, product(): return jnp.dot(left, right, preferred_element_type=F32)  104 us
    dot_general x31, matrix products, product_nt(): lax.dot_general(left, right, (((1,), (1,)), ((), ())), preferred_element_...  90.8 us
    ppermute x78, starting transfers between devices, swap(): return lax.ppermute(value, axis, [(0, 1), (1, 0)])  70.7 us
    unnamed x496, local copies, waits for them, and re-layouts  60.5 us
    dot_general x15, matrix products, product_tn(): lax.dot_general(left, right, (((0,), (0,)), ((), ())), preferred_element_...  55.1 us
  transfers between devices with their start and end apart: 82, of which 39 were waited for; matrix products, arithmetic and copies ran while one was open for 36% of the time, Pallas kernels for 0%

profile of v9, /device:TPU:0, one launch (start us, length us, event | category | flops | bytes accessed | tf_op | source)
XLA Modules:
  0.0 1223.4 jit_solution(16904238217045233784)
XLA Ops:
  14.4 5.4 all-to-all-start
  23.5 46.9 %collective-permute-done = bf16[64,5760]{1,0:T(8,128)(2,1)S(1)} collective-permute-done((bf16[64,5760]{1,0:T(8,128)(2,1)S(1)}, bf16[64,5760]{1,0:T(8,128)(2,1)S(1)}, u32[]{:S(2)}, u32[]{:S(2)}) %collective-permute-start) | collective-permute-done | bytes 737312 | tf_op jit(solution)/shard_map/ppermute | solution.py:73
  70.5 5.3 collective-permute-start.1
  75.8 32.1 %collective-permute-done.1 = bf16[128,5760]{1,0:T(8,128)(2,1)S(1)} collective-permute-done((bf16[128,5760]{1,0:T(8,128)(2,1)S(1)}, bf16[128,5760]{1,0:T(8,128)(2,1)S(1)}, u32[]{:S(2)}, u32[]{:S(2)}) %collective-permute-start.1) | collective-permute-done | bytes 1474592 | tf_op jit(solution)/shard_map/ppermute | solution.py:73
  119.5 19.0 %collective-permute-done.2 = bf16[256,1152]{1,0:T(8,128)(2,1)S(1)} collective-permute-done((bf16[256,1152]{1,0:T(8,128)(2,1)S(1)}, bf16[256,1152]{1,0:T(8,128)(2,1)S(1)}, u32[]{:S(2)}, u32[]{:S(2)}) %collective-permute-start.2) | collective-permute-done | bytes 589856 | tf_op jit(solution)/shard_map/ppermute | solution.py:73
  149.8 12.2 collective-permute-done.3
  165.3 5.2 fusion.76
  173.3 14.4 %collective-permute-done.11 = bf16[256,2048]{1,0:T(8,128)(2,1)} collective-permute-done((bf16[256,2048]{1,0:T(8,128)(2,1)S(1)}, bf16[256,2048]{1,0:T(8,128)(2,1)}, u32[]{:S(2)}, u32[]{:S(2)}) %collective-permute-start.11) | collective-permute-done | bytes 1048608 | tf_op jit(solution)/shard_map/ppermute | solution.py:73
  222.9 6.0 rev.69
  248.2 56.6 %collective-permute-done.6 = bf16[2,1,2,128,2,256]{5,3,4,2,1,0:T(8,128)(2,1)S(1)} collective-permute-done((bf16[2,1,2,128,2,256]{5,3,4,2,1,0:T(8,128)(2,1)S(1)}, bf16[2,1,2,128,2,256]{5,3,4,2,1,0:T(8,128)(2,1)S(1)}, u32[]{:S(2)}, u32[]{:S(2)}) %collective-permute-start.6) | collective-permute-done | bytes 524320 | tf_op jit(solution)/shard_map/ppermute | solution.py:73
  309.4 61.8 %collective-permute-done.7 = bf16[1,2,2,128,2,256]{5,3,4,2,1,0:T(8,128)(2,1)S(1)} collective-permute-done((bf16[1,2,2,128,2,256]{5,3,4,2,1,0:T(8,128)(2,1)S(1)}, bf16[1,2,2,128,2,256]{5,3,4,2,1,0:T(8,128)(2,1)S(1)}, u32[]{:S(2)}, u32[]{:S(2)}) %collective-permute-start.7) | collective-permute-done | bytes 524320 | tf_op jit(solution)/shard_map/ppermute | solution.py:73
  381.8 15.7 %collective-permute-done.8 = bf16[2,2,2,128,2,256]{5,3,4,2,1,0:T(8,128)(2,1)S(1)} collective-permute-done((bf16[2,2,2,128,2,256]{5,3,4,2,1,0:T(8,128)(2,1)S(1)}, bf16[2,2,2,128,2,256]{5,3,4,2,1,0:T(8,128)(2,1)S(1)}, u32[]{:S(2)}, u32[]{:S(2)}) %collective-permute-start.8) | collective-permute-done | bytes 1048608 | tf_op jit(solution)/shard_map/ppermute | solution.py:73
  422.4 30.5 %collective-permute-done.16 = bf16[512,2560]{1,0:T(8,128)(2,1)} collective-permute-done((bf16[512,2560]{1,0:T(8,128)(2,1)}, bf16[512,2560]{1,0:T(8,128)(2,1)}, u32[]{:S(2)}, u32[]{:S(2)}) %collective-permute-start.16) | collective-permute-done | bytes 2621472 | tf_op jit(solution)/shard_map/ppermute | solution.py:73
  475.2 4.7 fusion.5
  495.9 6.0 multiply_convert_fusion.7
  505.5 5.1 collective-permute-done.19
  515.5 10.6 collective-permute-done.23
  574.5 12.0 collective-permute-done.30
  590.6 17.9 %collective-permute-done.34 = bf16[256,2048]{1,0:T(8,128)(2,1)S(1)} collective-permute-done((bf16[256,2048]{1,0:T(8,128)(2,1)S(1)}, bf16[256,2048]{1,0:T(8,128)(2,1)S(1)}, u32[]{:S(2)}, u32[]{:S(2)}) %collective-permute-start.34) | collective-permute-done | bytes 1048608 | tf_op jit(solution)/shard_map/ppermute | solution.py:73
  625.8 4.7 multiply_convert_fusion.3
  635.3 13.4 %collective-permute-done.36 = bf16[256,2048]{1,0:T(8,128)(2,1)S(1)} collective-permute-done((bf16[256,2048]{1,0:T(8,128)(2,1)S(1)}, bf16[256,2048]{1,0:T(8,128)(2,1)S(1)}, u32[]{:S(2)}, u32[]{:S(2)}) %collective-permute-start.36) | collective-permute-done | bytes 1048608 | tf_op jit(solution)/shard_map/ppermute | solution.py:73
  652.3 10.1 collective-permute-done.39
  675.0 4.6 add_convert_fusion.7
  682.0 5.7 multiply_convert_fusion.1
  692.1 4.7 add_convert_fusion.6
  721.1 10.9 fusion.58
  732.0 11.9 fusion.61
  749.3 14.0 %fusion.64 = bf16[2048,1024]{1,0:T(8,128)(2,1)} fusion(bf16[512,1024]{1,0:T(8,128)(2,1)} %copy-done.216, bf16[512,1024]{1,0:T(8,128)(2,1)} %copy-done.215, bf16[512,1024]{1,0:T(8,128)(2,1)} %copy-done.214, bf16[512,1024]{1,0:T(8,128)(2,1)} %copy-done.213, bf16[512,2048]{1,0:T(8,128)(2,1)} %copy-done.106, bf16[512,2048]{1,0:T(8,128)(2,1)} %copy-done.114, ...), kind=kOutput, calls=%fused_computation.77 | convolution fusion | flops 8642363392 | bytes 16777216 | tf_op jit(solution)/shard_map/dot_general | solution.py:34
  763.3 9.0 pad_maximum_fusion
  780.2 5.5 multiply_reduce_fusion.4
  818.0 6.2 add_convert_fusion.1
  828.6 5.0 fusion.19
  841.4 34.8 %collective-permute-done.52 = bf16[512,2048]{1,0:T(8,128)(2,1)S(1)} collective-permute-done((bf16[512,2048]{1,0:T(8,128)(2,1)S(1)}, bf16[512,2048]{1,0:T(8,128)(2,1)S(1)}, u32[]{:S(2)}, u32[]{:S(2)}) %collective-permute-start.52) | collective-permute-done | bytes 2097184 | tf_op jit(solution)/shard_map/ppermute | solution.py:73
  908.8 5.2 fusion.69
  932.9 24.4 %collective-permute-done.53 = bf16[2,2,2,128,2,256]{5,3,4,2,1,0:T(8,128)(2,1)S(1)} collective-permute-done((bf16[2,2,2,128,2,256]{5,3,4,2,1,0:T(8,128)(2,1)S(1)}, bf16[2,2,2,128,2,256]{5,3,4,2,1,0:T(8,128)(2,1)S(1)}, u32[]{:S(2)}, u32[]{:S(2)}) %collective-permute-start.53) | collective-permute-done | bytes 1048608 | tf_op jit(solution)/shard_map/ppermute | solution.py:73
  960.1 19.2 %collective-permute-done.56 = bf16[2,2,128,2,256]{4,2,3,1,0:T(8,128)(2,1)S(1)} collective-permute-done((bf16[2,2,128,2,256]{4,2,3,1,0:T(8,128)(2,1)S(1)}, bf16[2,2,128,2,256]{4,2,3,1,0:T(8,128)(2,1)S(1)}, u32[]{:S(2)}, u32[]{:S(2)}) %collective-permute-start.56) | collective-permute-done | bytes 524320 | tf_op jit(solution)/shard_map/ppermute | solution.py:73
  984.3 33.0 %collective-permute-done.57 = bf16[2,2,128,2,256]{4,2,3,1,0:T(8,128)(2,1)S(1)} collective-permute-done((bf16[2,2,128,2,256]{4,2,3,1,0:T(8,128)(2,1)S(1)}, bf16[2,2,128,2,256]{4,2,3,1,0:T(8,128)(2,1)S(1)}, u32[]{:S(2)}, u32[]{:S(2)}) %collective-permute-start.57) | collective-permute-done | bytes 524320 | tf_op jit(solution)/shard_map/ppermute | solution.py:73
  1019.2 8.1 collective-permute-done.59
  1034.9 5.2 fusion.75
  1057.6 4.6 all-to-all-start.1
  1062.3 33.5 %collective-permute-done.63 = bf16[512,1152]{0,1:T(8,128)(2,1)} collective-permute-done((bf16[512,1152]{0,1:T(8,128)(2,1)}, bf16[512,1152]{0,1:T(8,128)(2,1)}, u32[]{:S(2)}, u32[]{:S(2)}) %collective-permute-start.63) | collective-permute-done | bytes 1179680 | tf_op jit(solution)/shard_map/ppermute | solution.py:73
  1103.2 4.7 collective-permute-done.67
  1119.1 6.0 collective-permute-done.68
  1133.3 4.7 fusion.1
  1151.9 4.9 fusion.7
  1165.9 11.0 collective-permute-done.69
  1178.4 13.0 %collective-permute-done.72 = bf16[64,2560]{1,0:T(8,128)(2,1)S(1)} collective-permute-done((bf16[64,2560]{1,0:T(8,128)(2,1)S(1)}, bf16[64,2560]{1,0:T(8,128)(2,1)S(1)}, u32[]{:S(2)}, u32[]{:S(2)}) %collective-permute-start.72) | collective-permute-done | bytes 327712 | tf_op jit(solution)/shard_map/ppermute | solution.py:73
  1192.9 7.5 collective-permute-done.71
  (997 shorter events, 512.5 us)
Async XLA Ops:
  14.4 95.3 %all-to-all-start = ((bf16[8,192,1024]{2,1,0:T(8,128)(2,1)}), bf16[8,192,1024]{2,1,0:T(8,128)(2,1)}, u32[]{:S(2)}, u32[]{:S(2)}) async-start(bf16[8,192,1024]{2,1,0:T(8,128)(2,1)} %copy.521), calls=%async_computation | async-start | bytes 6291456 | tf_op jit(solution)/shard_map/all_to_all | solution.py:327
  19.7 445.0 %all-gather.2.cloned.1.call-start = ((), (), s32[]{:S(2)}) async-start(), calls=%async_computation.3 | async-start | bytes 15728640 | tf_op jit(solution)/shard_map/all_gather | solution.py:338
  20.1 50.3 %collective-permute-start = (bf16[64,5760]{1,0:T(8,128)(2,1)S(1)}, bf16[64,5760]{1,0:T(8,128)(2,1)S(1)}, u32[]{:S(2)}, u32[]{:S(2)}) collective-permute-start(bf16[64,5760]{1,0:T(8,128)(2,1)S(1)} %concatenate.189), channel_id=1, source_target_pairs={{0,16},{16,0},{1,17},{17,1},{2,18},{18,2},{3,19},{19,3},{4,20},{20... | collective-permute-start | bytes 2211848 | tf_op jit(solution)/shard_map/ppermute | solution.py:73
  70.5 37.4 %collective-permute-start.1 = (bf16[128,5760]{1,0:T(8,128)(2,1)S(1)}, bf16[128,5760]{1,0:T(8,128)(2,1)S(1)}, u32[]{:S(2)}, u32[]{:S(2)}) collective-permute-start(bf16[128,5760]{1,0:T(8,128)(2,1)S(1)} %pad_maximum_fusion.14), channel_id=1, source_target_pairs={{0,8},{8,0},{1,9},{9,1},{2,10},{10,2},{3,11},{11,3},{4,12},{12,4},... | collective-permute-start | bytes 4423688 | tf_op jit(solution)/shard_map/ppermute | solution.py:73
  113.8 915.5 %reduce-scatter.2.cloned.1.call-start = ((), (), s32[]{:S(2)}) async-start(), calls=%async_computation.4 | async-start | bytes 15728640 | tf_op jit(solution)/shard_map/reduce_scatter | solution.py:505
  139.6 22.4 %collective-permute-start.3 = (bf16[512,1152]{1,0:T(8,128)(2,1)}, bf16[512,1152]{1,0:T(8,128)(2,1)}, u32[]{:S(2)}, u32[]{:S(2)}) collective-permute-start(bf16[512,1152]{1,0:T(8,128)(2,1)} %pad_maximum_fusion.15), channel_id=1, source_target_pairs={{0,4},{4,0},{1,5},{5,1},{2,6},{6,2},{3,7},{7,3},{8,12},{12,8},{9,1... | collective-permute-start | bytes 3538952 | tf_op jit(solution)/shard_map/ppermute | solution.py:73
  147.2 40.4 %collective-permute-start.11 = (bf16[256,2048]{1,0:T(8,128)(2,1)S(1)}, bf16[256,2048]{1,0:T(8,128)(2,1)}, u32[]{:S(2)}, u32[]{:S(2)}) collective-permute-start(bf16[256,2048]{1,0:T(8,128)(2,1)S(1)} %slice.539), channel_id=1, source_target_pairs={{0,2},{2,0},{1,3},{3,1},{4,6},{6,4},{5,7},{7,5},{8,10},{10,8},{9,1... | collective-permute-start | bytes 3145736 | tf_op jit(solution)/shard_map/ppermute | solution.py:73
  149.8 42.1 %collective-permute-start.4 = (bf16[512,1152]{1,0:T(8,128)(2,1)}, bf16[512,1152]{1,0:T(8,128)(2,1)}, u32[]{:S(2)}, u32[]{:S(2)}) collective-permute-start(bf16[512,1152]{1,0:T(8,128)(2,1)} %pad_maximum_fusion.15), channel_id=1, source_target_pairs={{0,1},{1,0},{2,3},{3,2},{4,5},{5,4},{6,7},{7,6},{8,9},{9,8},{10,11... | collective-permute-start | bytes 3538952 | tf_op jit(solution)/shard_map/ppermute | solution.py:73
  162.0 29.9 %collective-permute-start.5 = (bf16[512,1152]{1,0:T(8,128)(2,1)}, bf16[512,1152]{1,0:T(8,128)(2,1)}, u32[]{:S(2)}, u32[]{:S(2)}) collective-permute-start(bf16[512,1152]{1,0:T(8,128)(2,1)} %collective-permute-done.3), channel_id=1, source_target_pairs={{0,1},{1,0},{2,3},{3,2},{4,5},{5,4},{6,7},{7,6},{8,9},{9,8},{10,11... | collective-permute-start | bytes 3538952 | tf_op jit(solution)/shard_map/ppermute | solution.py:73
  190.4 184.0 %collective-permute-start.13 = (bf16[512,2048]{1,0:T(8,128)(2,1)}, bf16[512,2048]{1,0:T(8,128)(2,1)}, u32[]{:S(2)}, u32[]{:S(2)}) collective-permute-start(bf16[512,2048]{1,0:T(8,128)(2,1)} %pad_maximum_fusion.7), channel_id=1, source_target_pairs={{0,1},{1,0},{2,3},{3,2},{4,5},{5,4},{6,7},{7,6},{8,9},{9,8},{10,11... | collective-permute-start | bytes 6291464 | tf_op jit(solution)/shard_map/ppermute | solution.py:73
  190.4 57.8 %collective-permute-start.12 = (bf16[512,2048]{1,0:T(8,128)(2,1)}, bf16[512,2048]{1,0:T(8,128)(2,1)}, u32[]{:S(2)}, u32[]{:S(2)}) collective-permute-start(bf16[512,2048]{1,0:T(8,128)(2,1)} %pad_maximum_fusion.7), channel_id=1, source_target_pairs={{0,4},{4,0},{1,5},{5,1},{2,6},{6,2},{3,7},{7,3},{8,12},{12,8},{9,1... | collective-permute-start | bytes 6291464 | tf_op jit(solution)/shard_map/ppermute | solution.py:73
  242.4 62.4 %collective-permute-start.6 = (bf16[2,1,2,128,2,256]{5,3,4,2,1,0:T(8,128)(2,1)S(1)}, bf16[2,1,2,128,2,256]{5,3,4,2,1,0:T(8,128)(2,1)S(1)}, u32[]{:S(2)}, u32[]{:S(2)}) collective-permute-start(bf16[2,1,2,128,2,256]{5,3,4,2,1,0:T(8,128)(2,1)S(1)} %maximum_bitcast_fusion), channel_id=1, source_target_pairs={{0,16},{16,0},{1,17},{17,1},{2,18},{18,2},{3,19},{19,3},{4,20},{20... | collective-permute-start | bytes 1572872 | tf_op jit(solution)/shard_map/ppermute | solution.py:73
  242.5 134.2 %collective-permute-start.15 = (bf16[256,2560]{1,0:T(8,128)(2,1)}, bf16[256,2560]{1,0:T(8,128)(2,1)S(1)}, u32[]{:S(2)}, u32[]{:S(2)}) collective-permute-start(bf16[256,2560]{1,0:T(8,128)(2,1)} %slice.525), channel_id=1, source_target_pairs={{0,2},{2,0},{1,3},{3,1},{4,6},{6,4},{5,7},{7,5},{8,10},{10,8},{9,1... | collective-permute-start | bytes 3932168 | tf_op jit(solution)/shard_map/ppermute | solution.py:73
  248.2 162.2 %collective-permute-start.14 = (bf16[512,2048]{1,0:T(8,128)(2,1)}, bf16[512,2048]{1,0:T(8,128)(2,1)}, u32[]{:S(2)}, u32[]{:S(2)}) collective-permute-start(bf16[512,2048]{1,0:T(8,128)(2,1)} %collective-permute-done.12), channel_id=1, source_target_pairs={{0,1},{1,0},{2,3},{3,2},{4,5},{5,4},{6,7},{7,6},{8,9},{9,8},{10,11... | collective-permute-start | bytes 6291464 | tf_op jit(solution)/shard_map/ppermute | solution.py:73
  304.9 66.3 %collective-permute-start.7 = (bf16[1,2,2,128,2,256]{5,3,4,2,1,0:T(8,128)(2,1)S(1)}, bf16[1,2,2,128,2,256]{5,3,4,2,1,0:T(8,128)(2,1)S(1)}, u32[]{:S(2)}, u32[]{:S(2)}) collective-permute-start(bf16[1,2,2,128,2,256]{5,3,4,2,1,0:T(8,128)(2,1)S(1)} %get-tuple-element.473), channel_id=1, source_target_pairs={{0,8},{8,0},{1,9},{9,1},{2,10},{10,2},{3,11},{11,3},{4,12},{12,4},... | collective-permute-start | bytes 1572872 | tf_op jit(solution)/shard_map/ppermute | solution.py:73
  305.0 67.9 %collective-permute-start.9 = (bf16[1,2,2,128,2,256]{5,3,4,2,1,0:T(8,128)(2,1)S(1)}, bf16[1,2,2,128,2,256]{5,3,4,2,1,0:T(8,128)(2,1)S(1)}, u32[]{:S(2)}, u32[]{:S(2)}) collective-permute-start(bf16[1,2,2,128,2,256]{5,3,4,2,1,0:T(8,128)(2,1)S(1)} %get-tuple-element.472), channel_id=1, source_target_pairs={{0,4},{4,0},{1,5},{5,1},{2,6},{6,2},{3,7},{7,3},{8,12},{12,8},{9,1... | collective-permute-start | bytes 1572872 | tf_op jit(solution)/shard_map/ppermute | solution.py:73
  371.4 26.1 %collective-permute-start.8 = (bf16[2,2,2,128,2,256]{5,3,4,2,1,0:T(8,128)(2,1)S(1)}, bf16[2,2,2,128,2,256]{5,3,4,2,1,0:T(8,128)(2,1)S(1)}, u32[]{:S(2)}, u32[]{:S(2)}) collective-permute-start(bf16[2,2,2,128,2,256]{5,3,4,2,1,0:T(8,128)(2,1)S(1)} %get-tuple-element.475), channel_id=1, source_target_pairs={{0,4},{4,0},{1,5},{5,1},{2,6},{6,2},{3,7},{7,3},{8,12},{12,8},{9,1... | collective-permute-start | bytes 3145736 | tf_op jit(solution)/shard_map/ppermute | solution.py:73
  374.4 33.2 %collective-permute-start.10 = (bf16[2,2,2,128,2,256]{5,3,4,2,1,0:T(8,128)(2,1)}, bf16[2,2,2,128,2,256]{5,3,4,2,1,0:T(8,128)(2,1)}, u32[]{:S(2)}, u32[]{:S(2)}) collective-permute-start(bf16[2,2,2,128,2,256]{5,3,4,2,1,0:T(8,128)(2,1)} %get-tuple-element.471), channel_id=1, source_target_pairs={{0,8},{8,0},{1,9},{9,1},{2,10},{10,2},{3,11},{11,3},{4,12},{12,4},... | collective-permute-start | bytes 3145736 | tf_op jit(solution)/shard_map/ppermute | solution.py:73
  377.9 75.0 %collective-permute-start.16 = (bf16[512,2560]{1,0:T(8,128)(2,1)}, bf16[512,2560]{1,0:T(8,128)(2,1)}, u32[]{:S(2)}, u32[]{:S(2)}) collective-permute-start(bf16[512,2560]{1,0:T(8,128)(2,1)} %constant_dynamic-update-slice_fusion.6), channel_id=1, source_target_pairs={{0,4},{4,0},{1,5},{5,1},{2,6},{6,2},{3,7},{7,3},{8,12},{12,8},{9,1... | collective-permute-start | bytes 7864328 | tf_op jit(solution)/shard_map/ppermute | solution.py:73
  381.8 90.3 %collective-permute-start.17 = (bf16[512,2560]{1,0:T(8,128)(2,1)}, bf16[512,2560]{1,0:T(8,128)(2,1)}, u32[]{:S(2)}, u32[]{:S(2)}) collective-permute-start(bf16[512,2560]{1,0:T(8,128)(2,1)} %constant_dynamic-update-slice_fusion.6), channel_id=1, source_target_pairs={{0,1},{1,0},{2,3},{3,2},{4,5},{5,4},{6,7},{7,6},{8,9},{9,8},{10,11... | collective-permute-start | bytes 7864328 | tf_op jit(solution)/shard_map/ppermute | solution.py:73
  485.4 25.2 %collective-permute-start.19 = (bf16[256,2048]{1,0:T(8,128)(2,1)S(1)}, bf16[256,2048]{1,0:T(8,128)(2,1)}, u32[]{:S(2)}, u32[]{:S(2)}) collective-permute-start(bf16[256,2048]{1,0:T(8,128)(2,1)S(1)} %multiply_convert_fusion.8), channel_id=1, source_target_pairs={{0,4},{4,0},{1,5},{5,1},{2,6},{6,2},{3,7},{7,3},{8,12},{12,8},{9,1... | collective-permute-start | bytes 3145736 | tf_op jit(solution)/shard_map/ppermute | solution.py:73
  486.9 24.9 %collective-permute-start.20 = (bf16[256,2048]{1,0:T(8,128)(2,1)S(1)}, bf16[256,2048]{1,0:T(8,128)(2,1)S(1)}, u32[]{:S(2)}, u32[]{:S(2)}) collective-permute-start(bf16[256,2048]{1,0:T(8,128)(2,1)S(1)} %multiply_convert_fusion.8), channel_id=1, source_target_pairs={{0,8},{8,0},{1,9},{9,1},{2,10},{10,2},{3,11},{11,3},{4,12},{12,4},... | collective-permute-start | bytes 3145736 | tf_op jit(solution)/shard_map/ppermute | solution.py:73
  556.6 34.0 %collective-permute-start.26 = (bf16[256,2048]{1,0:T(8,128)(2,1)S(1)}, bf16[256,2048]{1,0:T(8,128)(2,1)S(1)}, u32[]{:S(2)}, u32[]{:S(2)}) collective-permute-start(bf16[256,2048]{1,0:T(8,128)(2,1)S(1)} %slice.559), channel_id=1, source_target_pairs={{0,1},{1,0},{2,3},{3,2},{4,5},{5,4},{6,7},{7,6},{8,9},{9,8},{10,11... | collective-permute-start | bytes 3145736 | tf_op jit(solution)/shard_map/ppermute | solution.py:73
  573.1 35.5 %collective-permute-start.34 = (bf16[256,2048]{1,0:T(8,128)(2,1)S(1)}, bf16[256,2048]{1,0:T(8,128)(2,1)S(1)}, u32[]{:S(2)}, u32[]{:S(2)}) collective-permute-start(bf16[256,2048]{1,0:T(8,128)(2,1)S(1)} %pad_maximum_fusion.21), channel_id=1, source_target_pairs={{0,4},{4,0},{1,5},{5,1},{2,6},{6,2},{3,7},{7,3},{8,12},{12,8},{9,1... | collective-permute-start | bytes 3145736 | tf_op jit(solution)/shard_map/ppermute | solution.py:73
  586.7 24.4 %collective-permute-start.31 = (bf16[256,2048]{1,0:T(8,128)(2,1)S(1)}, bf16[256,2048]{1,0:T(8,128)(2,1)S(1)}, u32[]{:S(2)}, u32[]{:S(2)}) collective-permute-start(bf16[256,2048]{1,0:T(8,128)(2,1)S(1)} %pad_maximum_fusion.20), channel_id=1, source_target_pairs={{0,8},{8,0},{1,9},{9,1},{2,10},{10,2},{3,11},{11,3},{4,12},{12,4},... | collective-permute-start | bytes 3145736 | tf_op jit(solution)/shard_map/ppermute | solution.py:73
  623.1 25.6 %collective-permute-start.36 = (bf16[256,2048]{1,0:T(8,128)(2,1)S(1)}, bf16[256,2048]{1,0:T(8,128)(2,1)S(1)}, u32[]{:S(2)}, u32[]{:S(2)}) collective-permute-start(bf16[256,2048]{1,0:T(8,128)(2,1)S(1)} %fusion.111), channel_id=1, source_target_pairs={{0,4},{4,0},{1,5},{5,1},{2,6},{6,2},{3,7},{7,3},{8,12},{12,8},{9,1... | collective-permute-start | bytes 3145736 | tf_op jit(solution)/shard_map/ppermute | solution.py:73
  623.7 25.3 %collective-permute-start.37 = (bf16[256,2048]{1,0:T(8,128)(2,1)S(1)}, bf16[256,2048]{1,0:T(8,128)(2,1)S(1)}, u32[]{:S(2)}, u32[]{:S(2)}) collective-permute-start(bf16[256,2048]{1,0:T(8,128)(2,1)S(1)} %fusion.111), channel_id=1, source_target_pairs={{0,8},{8,0},{1,9},{9,1},{2,10},{10,2},{3,11},{11,3},{4,12},{12,4},... | collective-permute-start | bytes 3145736 | tf_op jit(solution)/shard_map/ppermute | solution.py:73
  717.0 27.0 %collective-permute-start.49 = (bf16[128,2048]{1,0:T(8,128)(2,1)S(1)}, bf16[128,2048]{1,0:T(8,128)(2,1)S(1)}, u32[]{:S(2)}, u32[]{:S(2)}) collective-permute-start(bf16[128,2048]{1,0:T(8,128)(2,1)S(1)} %get-tuple-element.467), channel_id=1, source_target_pairs={{0,8},{8,0},{1,9},{9,1},{2,10},{10,2},{3,11},{11,3},{4,12},{12,4},... | collective-permute-start | bytes 1572872 | tf_op jit(solution)/shard_map/ppermute | solution.py:73
  717.6 29.0 %collective-permute-start.47 = (bf16[128,2048]{1,0:T(8,128)(2,1)S(1)}, bf16[128,2048]{1,0:T(8,128)(2,1)S(1)}, u32[]{:S(2)}, u32[]{:S(2)}) collective-permute-start(bf16[128,2048]{1,0:T(8,128)(2,1)S(1)} %get-tuple-element.466), channel_id=1, source_target_pairs={{0,4},{4,0},{1,5},{5,1},{2,6},{6,2},{3,7},{7,3},{8,12},{12,8},{9,1... | collective-permute-start | bytes 1572872 | tf_op jit(solution)/shard_map/ppermute | solution.py:73
  745.2 27.1 %collective-permute-start.50 = (bf16[256,2048]{1,0:T(8,128)(2,1)}, bf16[256,2048]{1,0:T(8,128)(2,1)}, u32[]{:S(2)}, u32[]{:S(2)}) collective-permute-start(bf16[256,2048]{1,0:T(8,128)(2,1)} %pad_maximum_fusion.24), channel_id=1, source_target_pairs={{0,4},{4,0},{1,5},{5,1},{2,6},{6,2},{3,7},{7,3},{8,12},{12,8},{9,1... | collective-permute-start | bytes 3145736 | tf_op jit(solution)/shard_map/ppermute | solution.py:73
  747.8 24.8 %collective-permute-start.48 = (bf16[256,2048]{1,0:T(8,128)(2,1)}, bf16[256,2048]{1,0:T(8,128)(2,1)S(1)}, u32[]{:S(2)}, u32[]{:S(2)}) collective-permute-start(bf16[256,2048]{1,0:T(8,128)(2,1)} %pad_maximum_fusion.23), channel_id=1, source_target_pairs={{0,8},{8,0},{1,9},{9,1},{2,10},{10,2},{3,11},{11,3},{4,12},{12,4},... | collective-permute-start | bytes 3145736 | tf_op jit(solution)/shard_map/ppermute | solution.py:73
  793.1 24.9 %collective-permute-start.51 = (bf16[1024,2048]{1,0:T(8,128)(2,1)}, bf16[1024,2048]{1,0:T(8,128)(2,1)}, u32[]{:S(2)}, u32[]{:S(2)}) collective-permute-start(bf16[1024,2048]{1,0:T(8,128)(2,1)} %convolution_convert_fusion.3), channel_id=1, source_target_pairs={{0,1},{1,0},{2,3},{3,2},{4,5},{5,4},{6,7},{7,6},{8,9},{9,8},{10,11... | collective-permute-start | bytes 12582920 | tf_op jit(solution)/shard_map/ppermute | solution.py:73
  828.3 47.9 %collective-permute-start.52 = (bf16[512,2048]{1,0:T(8,128)(2,1)S(1)}, bf16[512,2048]{1,0:T(8,128)(2,1)S(1)}, u32[]{:S(2)}, u32[]{:S(2)}) collective-permute-start(bf16[512,2048]{1,0:T(8,128)(2,1)S(1)} %slice.601), channel_id=1, source_target_pairs={{0,4},{4,0},{1,5},{5,1},{2,6},{6,2},{3,7},{7,3},{8,12},{12,8},{9,1... | collective-permute-start | bytes 6291464 | tf_op jit(solution)/shard_map/ppermute | solution.py:73
  886.9 42.1 %collective-permute-start.55 = (bf16[2,2,2,128,2,256]{5,3,4,2,1,0:T(8,128)(2,1)}, bf16[2,2,2,128,2,256]{5,3,4,2,1,0:T(8,128)(2,1)}, u32[]{:S(2)}, u32[]{:S(2)}) collective-permute-start(bf16[2,2,2,128,2,256]{5,3,4,2,1,0:T(8,128)(2,1)} %slice_bitcast_fusion), channel_id=1, source_target_pairs={{0,4},{4,0},{1,5},{5,1},{2,6},{6,2},{3,7},{7,3},{8,12},{12,8},{9,1... | collective-permute-start | bytes 3145736 | tf_op jit(solution)/shard_map/ppermute | solution.py:73
  908.5 71.3 %collective-permute-start.58 = (bf16[1024,2048]{1,0:T(8,128)(2,1)S(1)}, bf16[1024,2048]{1,0:T(8,128)(2,1)S(1)}, u32[]{:S(2)}, u32[]{:S(2)}) collective-permute-start(bf16[1024,2048]{1,0:T(8,128)(2,1)S(1)} %convolution_convert_fusion.2), channel_id=1, source_target_pairs={{0,1},{1,0},{2,3},{3,2},{4,5},{5,4},{6,7},{7,6},{8,9},{9,8},{10,11... | collective-permute-start | bytes 12582920 | tf_op jit(solution)/shard_map/ppermute | solution.py:73
  915.8 41.4 %collective-permute-start.53 = (bf16[2,2,2,128,2,256]{5,3,4,2,1,0:T(8,128)(2,1)S(1)}, bf16[2,2,2,128,2,256]{5,3,4,2,1,0:T(8,128)(2,1)S(1)}, u32[]{:S(2)}, u32[]{:S(2)}) collective-permute-start(bf16[2,2,2,128,2,256]{5,3,4,2,1,0:T(8,128)(2,1)S(1)} %bitcast.525), channel_id=1, source_target_pairs={{0,8},{8,0},{1,9},{9,1},{2,10},{10,2},{3,11},{11,3},{4,12},{12,4},... | collective-permute-start | bytes 3145736 | tf_op jit(solution)/shard_map/ppermute | solution.py:73
  917.4 42.1 %collective-permute-start.60 = (bf16[1024,512]{1,0:T(8,128)(2,1)S(1)}, bf16[1024,512]{1,0:T(8,128)(2,1)S(1)}, u32[]{:S(2)}, u32[]{:S(2)}) collective-permute-start(bf16[1024,512]{1,0:T(8,128)(2,1)S(1)} %pad_maximum_fusion.25), channel_id=1, source_target_pairs={{0,1},{1,0},{2,3},{3,2},{4,5},{5,4},{6,7},{7,6},{8,9},{9,8},{10,11... | collective-permute-start | bytes 3145736 | tf_op jit(solution)/shard_map/ppermute | solution.py:73
  931.5 47.9 %collective-permute-start.56 = (bf16[2,2,128,2,256]{4,2,3,1,0:T(8,128)(2,1)S(1)}, bf16[2,2,128,2,256]{4,2,3,1,0:T(8,128)(2,1)S(1)}, u32[]{:S(2)}, u32[]{:S(2)}) collective-permute-start(bf16[2,2,128,2,256]{4,2,3,1,0:T(8,128)(2,1)S(1)} %slice_bitcast_fusion.4), channel_id=1, source_target_pairs={{0,8},{8,0},{1,9},{9,1},{2,10},{10,2},{3,11},{11,3},{4,12},{12,4},... | collective-permute-start | bytes 1572872 | tf_op jit(solution)/shard_map/ppermute | solution.py:73
  957.6 21.9 %collective-permute-start.54 = (bf16[2,2,128,2,256]{4,2,3,1,0:T(8,128)(2,1)S(1)}, bf16[2,2,128,2,256]{4,2,3,1,0:T(8,128)(2,1)S(1)}, u32[]{:S(2)}, u32[]{:S(2)}) collective-permute-start(bf16[2,2,128,2,256]{4,2,3,1,0:T(8,128)(2,1)S(1)} %slice_bitcast_fusion.6), channel_id=1, source_target_pairs={{0,4},{4,0},{1,5},{5,1},{2,6},{6,2},{3,7},{7,3},{8,12},{12,8},{9,1... | collective-permute-start | bytes 1572872 | tf_op jit(solution)/shard_map/ppermute | solution.py:73
  959.9 23.5 %collective-permute-start.61 = (bf16[512,512]{1,0:T(8,128)(2,1)S(1)}, bf16[512,512]{1,0:T(8,128)(2,1)S(1)}, u32[]{:S(2)}, u32[]{:S(2)}) collective-permute-start(bf16[512,512]{1,0:T(8,128)(2,1)S(1)} %slice.758), channel_id=1, source_target_pairs={{0,4},{4,0},{1,5},{5,1},{2,6},{6,2},{3,7},{7,3},{8,12},{12,8},{9,1... | collective-permute-start | bytes 1572872 | tf_op jit(solution)/shard_map/ppermute | solution.py:73
  979.7 37.7 %collective-permute-start.57 = (bf16[2,2,128,2,256]{4,2,3,1,0:T(8,128)(2,1)S(1)}, bf16[2,2,128,2,256]{4,2,3,1,0:T(8,128)(2,1)S(1)}, u32[]{:S(2)}, u32[]{:S(2)}) collective-permute-start(bf16[2,2,128,2,256]{4,2,3,1,0:T(8,128)(2,1)S(1)} %fusion.203), channel_id=1, source_target_pairs={{0,16},{16,0},{1,17},{17,1},{2,18},{18,2},{3,19},{19,3},{4,20},{20... | collective-permute-start | bytes 1572872 | tf_op jit(solution)/shard_map/ppermute | solution.py:73
  981.4 45.9 %collective-permute-start.59 = (bf16[512,2048]{1,0:T(8,128)(2,1)S(1)}, bf16[512,2048]{1,0:T(8,128)(2,1)S(1)}, u32[]{:S(2)}, u32[]{:S(2)}) collective-permute-start(bf16[512,2048]{1,0:T(8,128)(2,1)S(1)} %slice.752), channel_id=1, source_target_pairs={{0,4},{4,0},{1,5},{5,1},{2,6},{6,2},{3,7},{7,3},{8,12},{12,8},{9,1... | collective-permute-start | bytes 6291464 | tf_op jit(solution)/shard_map/ppermute | solution.py:73
  1049.7 46.1 %collective-permute-start.63 = (bf16[512,1152]{0,1:T(8,128)(2,1)}, bf16[512,1152]{0,1:T(8,128)(2,1)}, u32[]{:S(2)}, u32[]{:S(2)}) collective-permute-start(bf16[512,1152]{0,1:T(8,128)(2,1)} %slice.762), channel_id=1, source_target_pairs={{0,4},{4,0},{1,5},{5,1},{2,6},{6,2},{3,7},{7,3},{8,12},{12,8},{9,1... | collective-permute-start | bytes 3538952 | tf_op jit(solution)/shard_map/ppermute | solution.py:73
  1053.4 45.7 %collective-permute-start.65 = (bf16[256,2048]{1,0:T(8,128)(2,1)}, bf16[256,2048]{1,0:T(8,128)(2,1)}, u32[]{:S(2)}, u32[]{:S(2)}) collective-permute-start(bf16[256,2048]{1,0:T(8,128)(2,1)} %get-tuple-element.456), channel_id=1, source_target_pairs={{0,2},{2,0},{1,3},{3,1},{4,6},{6,4},{5,7},{7,5},{8,10},{10,8},{9,1... | collective-permute-start | bytes 3145736 | tf_op jit(solution)/shard_map/ppermute | solution.py:73
  1054.8 53.2 %collective-permute-start.67 = (bf16[256,2560]{1,0:T(8,128)(2,1)}, bf16[256,2560]{1,0:T(8,128)(2,1)}, u32[]{:S(2)}, u32[]{:S(2)}) collective-permute-start(bf16[256,2560]{1,0:T(8,128)(2,1)} %get-tuple-element.450), channel_id=1, source_target_pairs={{0,2},{2,0},{1,3},{3,1},{4,6},{6,4},{5,7},{7,5},{8,10},{10,8},{9,1... | collective-permute-start | bytes 3932168 | tf_op jit(solution)/shard_map/ppermute | solution.py:73
  1057.6 145.8 %all-to-all-start.1 = ((bf16[8,192,1024]{2,1,0:T(8,128)(2,1)}), bf16[8,192,1024]{2,1,0:T(8,128)(2,1)}, u32[]{:S(2)}, u32[]{:S(2)}) async-start(bf16[8,192,1024]{2,1,0:T(8,128)(2,1)} %pad_maximum_fusion.2), calls=%async_computation.2 | async-start | bytes 6291456 | tf_op jit(solution)/shard_map/all_to_all | solution.py:201
  1162.0 29.3 %collective-permute-start.72 = (bf16[64,2560]{1,0:T(8,128)(2,1)S(1)}, bf16[64,2560]{1,0:T(8,128)(2,1)S(1)}, u32[]{:S(2)}, u32[]{:S(2)}) collective-permute-start(bf16[64,2560]{1,0:T(8,128)(2,1)S(1)} %slice.651), channel_id=1, source_target_pairs={{0,16},{16,0},{1,17},{17,1},{2,18},{18,2},{3,19},{19,3},{4,20},{20... | collective-permute-start | bytes 983048 | tf_op jit(solution)/shard_map/ppermute | solution.py:73
  1178.0 22.3 %collective-permute-start.71 = (bf16[64,1152]{0,1:T(8,128)(2,1)S(1)}, bf16[64,1152]{0,1:T(8,128)(2,1)S(1)}, u32[]{:S(2)}, u32[]{:S(2)}) collective-permute-start(bf16[64,1152]{0,1:T(8,128)(2,1)S(1)} %slice.774), channel_id=1, source_target_pairs={{0,16},{16,0},{1,17},{17,1},{2,18},{18,2},{3,19},{19,3},{4,20},{20... | collective-permute-start | bytes 442376 | tf_op jit(solution)/shard_map/ppermute | solution.py:73
  (260 other events, 4052.1 us)
Sparse Core Ops, SparseCore 0:
  113.9 246.4 all-gather.1
  775.9 240.3 reduce-scatter.1

commit v10 on v9

--- a/solution.py
+++ b/solution.py
@@ -129,7 +129,9 @@
         return block
 
     def gather_pieces(self, block):
-        other = swap(block, self.order[-1])
+        return self.core_pieces(block, swap(block, self.order[-1]))
+
+    def core_pieces(self, block, other):
         return [block, other, swap(block, self.c), swap(other, self.c)]
 
     def far_team_rows(self, pieces):
@@ -219,12 +221,9 @@
         by_x, by_l, results = together(by_x, by_l, results)
         half = own.shape[0] // 2
         both = jnp.concatenate([swap(by_x[:half], self.l), swap(by_l[half:], self.x)], axis=0)
-        for piece in (by_x, both):
+        for piece in (by_x, by_l, both):
             chunks.append(chunk_of(piece))
             results.append(function(chunks[-1]))
-        by_l, results = together(by_l, results)
-        chunks.append(chunk_of(by_l))
-        results.append(function(chunks[-1]))
         return chunks, results
 
     def core_sums(self, chunks):
@@ -236,7 +235,7 @@
         return sums
 
     def team_near(self, sums):
-        own, by_x, both, by_l = sums
+        own, by_x, by_l, both = sums
         half = own.shape[0] // 2
         both = both.astype(BF16)
         first = by_l[:half] + swap(both[:half], self.x).astype(F32)
@@ -333,9 +332,9 @@
         axis=1,
     )
     attn_block = plan.grow(attn_block, plan.far_seq)
-    attn_block = plan.grow(attn_block, (plan.l,))
     attn_block, feed_team = together(attn_block, feed_team)
     feed_full = lax.all_gather(feed_team.reshape(-1, hidden_own), plan.far, axis=0, tiled=True)
+    attn_block = plan.grow(attn_block, (plan.l,))
     kvl_block, query_block, rest_block = split_columns(attn_block, block_widths)
     kvl_block = plan.grow(kvl_block, plan.far_dp)
     query_block = plan.grow(query_block, plan.far_dp)
@@ -386,6 +385,7 @@
     seq_index = lax.axis_index(plan.seq)
     total_length = block * seq_count
     if whole_sequence:
+        key_low, value_low, rest_block = together(key_low, value_low, rest_block)
         pair_low = plan.near_far(key_low, value_low)
         keys_all, values_all = [
             one.swapaxes(0, 1).reshape(batch, total_length, kv_heads, head_size)
@@ -401,7 +401,9 @@
         keys_all, values_all = jnp.concatenate(gathered, axis=2)
         key_blocks = seq_index - jnp.array(offsets, dtype=jnp.int32)
     key_count = keys_all.shape[1]
-    rest_full = plan.gather_pieces(rest_block)
+    rest_other = swap(rest_block, plan.order[-1])
+    keys_all, values_all, rest_other = together(keys_all, values_all, rest_other)
+    rest_full = plan.core_pieces(rest_block, rest_other)
     query_places = seq_index * block + jnp.arange(block, dtype=jnp.int32)
     key_places = (key_blocks[:, None] * block + jnp.arange(block, dtype=jnp.int32)).reshape(-1)
     in_query = (query_places[None, :, None] >= span_start[:, None, :]) & (
@@ -519,10 +521,10 @@
     d_attn_low = d_attn_proj.astype(BF16)
     d_laurel_low = d_laurel.astype(BF16)
     d_attn_spread = product(d_attn_low, to_spread).astype(BF16)
-    d_attended_low = product_split(d_attn_spread, output_full).astype(BF16)
     d_latent_low = product(d_laurel_low, right_full).astype(BF16)
     output_sum = plan.spread_begin([(d_attn_spread, attended_low)])
-    d_attended_low, output_sum = together(d_attended_low, output_sum)
+    d_attn_spread, output_sum = together(d_attn_spread, output_sum)
+    d_attended_low = product_split(d_attn_spread, output_full).astype(BF16)
     output_sum = plan.spread_step(output_sum, steps[:1])
 
     d_att = d_attended_low.reshape(batch, block, kv_heads, group, head_size)
@@ -610,11 +612,14 @@
         [plan.from_far_team(norm_grads).reshape(-1), grad_norm_query, grad_norm_key]
     )
     grad_query = plan.spread_step(query_sum, steps[3:])
-    grad_output, grad_side_gate, grad_side_output = split_columns(
-        plan.spread_step(output_sum, steps[3:]), rest_widths
-    )
+    output_sum = plan.spread_step(output_sum, steps[3:])
+    kvl_sum = plan.spread_step(kvl_sum, steps[2:3])
+    gain_grads, grad_query, output_sum, kvl_sum = together(
+        gain_grads, grad_query, output_sum, kvl_sum
+    )
+    grad_output, grad_side_gate, grad_side_output = split_columns(output_sum, rest_widths)
     grad_key, grad_value, grad_left, grad_right = split_columns(
-        plan.spread_step(kvl_sum, steps[2:]), kvl_widths
+        plan.spread_step(kvl_sum, steps[3:]), kvl_widths
     )
     gain_grads = plan.total(gain_grads)
     gain_parts = split_columns(gain_grads, [width] * 6 + [head_size] * 2)

time: 1230 us -> 1150 us (0.935)
  waiting for transfers between devices: 569 us -> 512 us
  local copies, waits for them, and re-layouts: 165 us -> 143 us
    ppermute x78, waiting for transfers between devices: 569 us -> 511 us  [swap(): return lax.ppermute(value, axis, [(0, 1), (1, 0)])]
    unnamed x496 -> x460, local copies, waits for them, and re-layouts: 60.5 us -> 50.7 us
  transfers between devices with their start and end apart: 82 -> 82, of which waited for: 39 -> 41; matrix products, arithmetic and copies ran while one was open for 36% -> 40% of each run, Pallas kernels for 0% -> 0%
where the time goes in v10:
time: 1150 us; the launch traced here: 1140 us
  waiting for transfers between devices  512 us (45%)
  matrix products  264 us (23%)
  local copies, waits for them, and re-layouts  143 us (12%)
  other arithmetic  136 us (12%)
  starting transfers between devices  72.1 us (6%)
  between operations  18.3 us (2%)
    ppermute x78, waiting for transfers between devices, swap(): return lax.ppermute(value, axis, [(0, 1), (1, 0)])  511 us
    dot_general x33, matrix products, product(): return jnp.dot(left, right, preferred_element_type=F32)  102 us
    dot_general x31, matrix products, product_nt(): lax.dot_general(left, right, (((1,), (1,)), ((), ())), preferred_element_...  93.5 us
    ppermute x78, starting transfers between devices, swap(): return lax.ppermute(value, axis, [(0, 1), (1, 0)])  61.4 us
    dot_general x15, matrix products, product_tn(): lax.dot_general(left, right, (((0,), (0,)), ((), ())), preferred_element_...  53.9 us
    unnamed x460, local copies, waits for them, and re-layouts  50.7 us
  transfers between devices with their start and end apart: 82, of which 41 were waited for; matrix products, arithmetic and copies ran while one was open for 40% of the time, Pallas kernels for 0%

profile of v10, /device:TPU:0, one launch (start us, length us, event | category | flops | bytes accessed | tf_op | source)
XLA Modules:
  0.0 1144.7 jit_solution(2738501292931060307)
XLA Ops:
  14.4 5.4 all-to-all-start
  24.6 45.8 %collective-permute-done = bf16[64,5760]{1,0:T(8,128)(2,1)} collective-permute-done((bf16[64,5760]{1,0:T(8,128)(2,1)S(1)}, bf16[64,5760]{1,0:T(8,128)(2,1)}, u32[]{:S(2)}, u32[]{:S(2)}) %collective-permute-start) | collective-permute-done | bytes 737312 | tf_op jit(solution)/shard_map/ppermute | solution.py:73
  82.3 55.7 %collective-permute-done.1 = bf16[128,5760]{1,0:T(8,128)(2,1)S(1)} collective-permute-done((bf16[128,5760]{1,0:T(8,128)(2,1)S(1)}, bf16[128,5760]{1,0:T(8,128)(2,1)S(1)}, u32[]{:S(2)}, u32[]{:S(2)}) %collective-permute-start.1) | collective-permute-done | bytes 1474592 | tf_op jit(solution)/shard_map/ppermute | solution.py:73
  140.5 9.0 collective-permute-done.2
  158.7 15.3 %collective-permute-done.3 = bf16[512,1152]{1,0:T(8,128)(2,1)} collective-permute-done((bf16[512,1152]{1,0:T(8,128)(2,1)}, bf16[512,1152]{1,0:T(8,128)(2,1)}, u32[]{:S(2)}, u32[]{:S(2)}) %collective-permute-start.3) | collective-permute-done | bytes 1179680 | tf_op jit(solution)/shard_map/ppermute | solution.py:73
  177.3 5.2 fusion.76
  185.3 7.9 collective-permute-done.13
  208.0 5.8 rev.69
  246.2 26.5 %collective-permute-done.6 = bf16[256,2560]{1,0:T(8,128)(2,1)} collective-permute-done((bf16[256,2560]{1,0:T(8,128)(2,1)}, bf16[256,2560]{1,0:T(8,128)(2,1)}, u32[]{:S(2)}, u32[]{:S(2)}) %collective-permute-start.6) | collective-permute-done | bytes 1310752 | tf_op jit(solution)/shard_map/ppermute | solution.py:73
  281.2 32.3 %collective-permute-done.7 = bf16[2,1,2,128,2,256]{5,3,4,2,1,0:T(8,128)(2,1)S(1)} collective-permute-done((bf16[2,1,2,128,2,256]{5,3,4,2,1,0:T(8,128)(2,1)S(1)}, bf16[2,1,2,128,2,256]{5,3,4,2,1,0:T(8,128)(2,1)S(1)}, u32[]{:S(2)}, u32[]{:S(2)}) %collective-permute-start.7) | collective-permute-done | bytes 524320 | tf_op jit(solution)/shard_map/ppermute | solution.py:73
  318.9 29.5 %collective-permute-done.8 = bf16[1,2,2,128,2,256]{5,3,4,2,1,0:T(8,128)(2,1)S(1)} collective-permute-done((bf16[1,2,2,128,2,256]{5,3,4,2,1,0:T(8,128)(2,1)S(1)}, bf16[1,2,2,128,2,256]{5,3,4,2,1,0:T(8,128)(2,1)S(1)}, u32[]{:S(2)}, u32[]{:S(2)}) %collective-permute-start.8) | collective-permute-done | bytes 524320 | tf_op jit(solution)/shard_map/ppermute | solution.py:73
  359.5 15.9 %collective-permute-done.9 = bf16[2,2,2,128,2,256]{5,3,4,2,1,0:T(8,128)(2,1)} collective-permute-done((bf16[2,2,2,128,2,256]{5,3,4,2,1,0:T(8,128)(2,1)}, bf16[2,2,2,128,2,256]{5,3,4,2,1,0:T(8,128)(2,1)}, u32[]{:S(2)}, u32[]{:S(2)}) %collective-permute-start.9) | collective-permute-done | bytes 1048608 | tf_op jit(solution)/shard_map/ppermute | solution.py:73
  405.4 4.7 fusion.5
  423.5 5.6 fusion.298
  433.0 6.2 multiply_convert_fusion.7
  441.7 4.8 collective-permute-done.19
  451.7 7.9 collective-permute-done.25
  497.0 12.0 %collective-permute-done.33 = bf16[128,2048]{1,0:T(8,128)(2,1)S(1)} collective-permute-done((bf16[128,2048]{1,0:T(8,128)(2,1)S(1)}, bf16[128,2048]{1,0:T(8,128)(2,1)S(1)}, u32[]{:S(2)}, u32[]{:S(2)}) %collective-permute-start.33) | collective-permute-done | bytes 524320 | tf_op jit(solution)/shard_map/ppermute | solution.py:73
  513.8 20.2 %collective-permute-done.34 = bf16[256,2048]{1,0:T(8,128)(2,1)S(1)} collective-permute-done((bf16[256,2048]{1,0:T(8,128)(2,1)S(1)}, bf16[256,2048]{1,0:T(8,128)(2,1)S(1)}, u32[]{:S(2)}, u32[]{:S(2)}) %collective-permute-start.34) | collective-permute-done | bytes 1048608 | tf_op jit(solution)/shard_map/ppermute | solution.py:73
  553.0 4.7 multiply_convert_fusion.3
  562.1 4.6 add_convert_fusion.8
  566.7 10.0 collective-permute-done.36
  582.5 9.1 collective-permute-done.40
  595.5 5.2 multiply_convert_fusion.2
  605.2 5.0 add_convert_fusion.7
  612.8 5.4 multiply_convert_fusion.1
  648.3 10.9 fusion.58
  659.2 11.8 %fusion.61 = bf16[2048,1024]{1,0:T(8,128)(2,1)} fusion(bf16[2048,2048]{1,0:T(8,128)(2,1)S(1)} %constant_dynamic-update-slice_fusion.22, bf16[512,1024]{1,0:T(8,128)(2,1)} %copy-done.187, bf16[512,1024]{1,0:T(8,128)(2,1)S(1)} %copy-done.186, bf16[512,1024]{1,0:T(8,128)(2,1)S(1)} %copy-done.184, bf16[512,1024]{1,0:T(8,128)(2,1)S(1)} %copy-done.182), kind=kOutput, calls=%fused_computation.76 | convolution fusion | flops 8608808960 | bytes 16777216 | tf_op jit(solution)/shard_map/dot_general | solution.py:34
  675.4 13.9 %fusion.64 = bf16[2048,1024]{1,0:T(8,128)(2,1)} fusion(bf16[512,1024]{1,0:T(8,128)(2,1)} %copy-done.201, bf16[512,1024]{1,0:T(8,128)(2,1)} %get-tuple-element.137, bf16[512,1024]{1,0:T(8,128)(2,1)} %copy-done.199, bf16[512,1024]{1,0:T(8,128)(2,1)} %copy-done.198, bf16[512,2048]{1,0:T(8,128)(2,1)} %copy-done.100, bf16[512,2048]{1,0:T(8,128)(2,1)} %copy-done.89, ...), kind=kOutput, calls=%fused_computation.77 | convolution fusion | flops 8642363392 | bytes 16777216 | tf_op jit(solution)/shard_map/dot_general | solution.py:34
  689.3 9.1 pad_maximum_fusion
  707.3 4.9 multiply_reduce_fusion.4
  730.8 5.4 add_convert_fusion.1
  750.9 4.7 fusion.19
  766.6 31.3 %collective-permute-done.52 = bf16[512,2048]{1,0:T(8,128)(2,1)S(1)} collective-permute-done((bf16[512,2048]{1,0:T(8,128)(2,1)S(1)}, bf16[512,2048]{1,0:T(8,128)(2,1)S(1)}, u32[]{:S(2)}, u32[]{:S(2)}) %collective-permute-start.52) | collective-permute-done | bytes 2097184 | tf_op jit(solution)/shard_map/ppermute | solution.py:73
  830.9 5.0 fusion.69
  852.8 31.1 %collective-permute-done.53 = bf16[2,2,2,128,2,256]{5,3,4,2,1,0:T(8,128)(2,1)S(1)} collective-permute-done((bf16[2,2,2,128,2,256]{5,3,4,2,1,0:T(8,128)(2,1)S(1)}, bf16[2,2,2,128,2,256]{5,3,4,2,1,0:T(8,128)(2,1)S(1)}, u32[]{:S(2)}, u32[]{:S(2)}) %collective-permute-start.53) | collective-permute-done | bytes 1048608 | tf_op jit(solution)/shard_map/ppermute | solution.py:73
  886.8 14.4 %collective-permute-done.56 = bf16[2,2,128,2,256]{4,2,3,1,0:T(8,128)(2,1)S(1)} collective-permute-done((bf16[2,2,128,2,256]{4,2,3,1,0:T(8,128)(2,1)S(1)}, bf16[2,2,128,2,256]{4,2,3,1,0:T(8,128)(2,1)S(1)}, u32[]{:S(2)}, u32[]{:S(2)}) %collective-permute-start.56) | collective-permute-done | bytes 524320 | tf_op jit(solution)/shard_map/ppermute | solution.py:73
  904.0 6.4 collective-permute-done.61
  911.3 32.7 %collective-permute-done.57 = bf16[2,2,128,2,256]{4,2,3,1,0:T(8,128)(2,1)S(1)} collective-permute-done((bf16[2,2,128,2,256]{4,2,3,1,0:T(8,128)(2,1)S(1)}, bf16[2,2,128,2,256]{4,2,3,1,0:T(8,128)(2,1)S(1)}, u32[]{:S(2)}, u32[]{:S(2)}) %collective-permute-start.57) | collective-permute-done | bytes 524320 | tf_op jit(solution)/shard_map/ppermute | solution.py:73
  945.8 8.5 collective-permute-done.59
  961.9 5.4 fusion.75
  984.7 4.8 all-to-all-start.1
  989.6 33.5 %collective-permute-done.63 = bf16[512,1152]{0,1:T(8,128)(2,1)} collective-permute-done((bf16[512,1152]{0,1:T(8,128)(2,1)}, bf16[512,1152]{0,1:T(8,128)(2,1)}, u32[]{:S(2)}, u32[]{:S(2)}) %collective-permute-start.63) | collective-permute-done | bytes 1179680 | tf_op jit(solution)/shard_map/ppermute | solution.py:73
  1028.1 6.9 collective-permute-done.67
  1046.3 5.7 collective-permute-done.68
  1060.2 4.7 fusion.1
  1077.0 6.6 fusion.7
  1104.8 9.0 collective-permute-done.72
  (958 shorter events, 500.1 us)
Async XLA Ops:
  14.4 58.2 %all-to-all-start = ((bf16[8,192,1024]{2,1,0:T(8,128)(2,1)}), bf16[8,192,1024]{2,1,0:T(8,128)(2,1)}, u32[]{:S(2)}, u32[]{:S(2)}) async-start(bf16[8,192,1024]{2,1,0:T(8,128)(2,1)} %copy.514), calls=%async_computation | async-start | bytes 6291456 | tf_op jit(solution)/shard_map/all_to_all | solution.py:326
  19.8 375.1 %all-gather.2.cloned.1.call-start = ((), (), s32[]{:S(2)}) async-start(), calls=%async_computation.3 | async-start | bytes 15728640 | tf_op jit(solution)/shard_map/all_gather | solution.py:336
  20.1 50.3 %collective-permute-start = (bf16[64,5760]{1,0:T(8,128)(2,1)S(1)}, bf16[64,5760]{1,0:T(8,128)(2,1)}, u32[]{:S(2)}, u32[]{:S(2)}) collective-permute-start(bf16[64,5760]{1,0:T(8,128)(2,1)S(1)} %concatenate.177), channel_id=1, source_target_pairs={{0,16},{16,0},{1,17},{17,1},{2,18},{18,2},{3,19},{19,3},{4,20},{20... | collective-permute-start | bytes 2211848 | tf_op jit(solution)/shard_map/ppermute | solution.py:73
  76.7 879.7 %reduce-scatter.2.cloned.1.call-start = ((), (), s32[]{:S(2)}) async-start(), calls=%async_computation.4 | async-start | bytes 15728640 | tf_op jit(solution)/shard_map/reduce_scatter | solution.py:507
  77.6 60.3 %collective-permute-start.1 = (bf16[128,5760]{1,0:T(8,128)(2,1)S(1)}, bf16[128,5760]{1,0:T(8,128)(2,1)S(1)}, u32[]{:S(2)}, u32[]{:S(2)}) collective-permute-start(bf16[128,5760]{1,0:T(8,128)(2,1)S(1)} %pad_maximum_fusion.14), channel_id=1, source_target_pairs={{0,8},{8,0},{1,9},{9,1},{2,10},{10,2},{3,11},{11,3},{4,12},{12,4},... | collective-permute-start | bytes 4423688 | tf_op jit(solution)/shard_map/ppermute | solution.py:73
  150.7 23.4 %collective-permute-start.3 = (bf16[512,1152]{1,0:T(8,128)(2,1)}, bf16[512,1152]{1,0:T(8,128)(2,1)}, u32[]{:S(2)}, u32[]{:S(2)}) collective-permute-start(bf16[512,1152]{1,0:T(8,128)(2,1)} %pad_maximum_fusion.15), channel_id=1, source_target_pairs={{0,4},{4,0},{1,5},{5,1},{2,6},{6,2},{3,7},{7,3},{8,12},{12,8},{9,1... | collective-permute-start | bytes 3538952 | tf_op jit(solution)/shard_map/ppermute | solution.py:73
  157.1 36.1 %collective-permute-start.13 = (bf16[256,2048]{1,0:T(8,128)(2,1)S(1)}, bf16[256,2048]{1,0:T(8,128)(2,1)}, u32[]{:S(2)}, u32[]{:S(2)}) collective-permute-start(bf16[256,2048]{1,0:T(8,128)(2,1)S(1)} %slice.701), channel_id=1, source_target_pairs={{0,2},{2,0},{1,3},{3,1},{4,6},{6,4},{5,7},{7,5},{8,10},{10,8},{9,1... | collective-permute-start | bytes 3145736 | tf_op jit(solution)/shard_map/ppermute | solution.py:73
  158.7 37.2 %collective-permute-start.4 = (bf16[512,1152]{1,0:T(8,128)(2,1)}, bf16[512,1152]{1,0:T(8,128)(2,1)}, u32[]{:S(2)}, u32[]{:S(2)}) collective-permute-start(bf16[512,1152]{1,0:T(8,128)(2,1)} %pad_maximum_fusion.15), channel_id=1, source_target_pairs={{0,1},{1,0},{2,3},{3,2},{4,5},{5,4},{6,7},{7,6},{8,9},{9,8},{10,11... | collective-permute-start | bytes 3538952 | tf_op jit(solution)/shard_map/ppermute | solution.py:73
  195.9 83.0 %collective-permute-start.15 = (bf16[512,2048]{1,0:T(8,128)(2,1)}, bf16[512,2048]{1,0:T(8,128)(2,1)}, u32[]{:S(2)}, u32[]{:S(2)}) collective-permute-start(bf16[512,2048]{1,0:T(8,128)(2,1)} %pad_maximum_fusion.7), channel_id=1, source_target_pairs={{0,1},{1,0},{2,3},{3,2},{4,5},{5,4},{6,7},{7,6},{8,9},{9,8},{10,11... | collective-permute-start | bytes 6291464 | tf_op jit(solution)/shard_map/ppermute | solution.py:73
  196.0 49.7 %collective-permute-start.14 = (bf16[512,2048]{1,0:T(8,128)(2,1)}, bf16[512,2048]{1,0:T(8,128)(2,1)}, u32[]{:S(2)}, u32[]{:S(2)}) collective-permute-start(bf16[512,2048]{1,0:T(8,128)(2,1)} %pad_maximum_fusion.7), channel_id=1, source_target_pairs={{0,4},{4,0},{1,5},{5,1},{2,6},{6,2},{3,7},{7,3},{8,12},{12,8},{9,1... | collective-permute-start | bytes 6291464 | tf_op jit(solution)/shard_map/ppermute | solution.py:73
  232.7 40.0 %collective-permute-start.6 = (bf16[256,2560]{1,0:T(8,128)(2,1)}, bf16[256,2560]{1,0:T(8,128)(2,1)}, u32[]{:S(2)}, u32[]{:S(2)}) collective-permute-start(bf16[256,2560]{1,0:T(8,128)(2,1)} %slice.691), channel_id=1, source_target_pairs={{0,2},{2,0},{1,3},{3,1},{4,6},{6,4},{5,7},{7,5},{8,10},{10,8},{9,1... | collective-permute-start | bytes 3932168 | tf_op jit(solution)/shard_map/ppermute | solution.py:73
  245.7 71.0 %collective-permute-start.16 = (bf16[512,2048]{1,0:T(8,128)(2,1)}, bf16[512,2048]{1,0:T(8,128)(2,1)S(1)}, u32[]{:S(2)}, u32[]{:S(2)}) collective-permute-start(bf16[512,2048]{1,0:T(8,128)(2,1)} %collective-permute-done.14), channel_id=1, source_target_pairs={{0,1},{1,0},{2,3},{3,2},{4,5},{5,4},{6,7},{7,6},{8,9},{9,8},{10,11... | collective-permute-start | bytes 6291464 | tf_op jit(solution)/shard_map/ppermute | solution.py:73
  275.7 37.9 %collective-permute-start.7 = (bf16[2,1,2,128,2,256]{5,3,4,2,1,0:T(8,128)(2,1)S(1)}, bf16[2,1,2,128,2,256]{5,3,4,2,1,0:T(8,128)(2,1)S(1)}, u32[]{:S(2)}, u32[]{:S(2)}) collective-permute-start(bf16[2,1,2,128,2,256]{5,3,4,2,1,0:T(8,128)(2,1)S(1)} %maximum_bitcast_fusion), channel_id=1, source_target_pairs={{0,16},{16,0},{1,17},{17,1},{2,18},{18,2},{3,19},{19,3},{4,20},{20... | collective-permute-start | bytes 1572872 | tf_op jit(solution)/shard_map/ppermute | solution.py:73
  278.1 103.8 %collective-permute-start.12 = (bf16[512,2560]{1,0:T(8,128)(2,1)}, bf16[512,2560]{1,0:T(8,128)(2,1)}, u32[]{:S(2)}, u32[]{:S(2)}) collective-permute-start(bf16[512,2560]{1,0:T(8,128)(2,1)} %pad_maximum_fusion.3), channel_id=1, source_target_pairs={{0,4},{4,0},{1,5},{5,1},{2,6},{6,2},{3,7},{7,3},{8,12},{12,8},{9,1... | collective-permute-start | bytes 7864328 | tf_op jit(solution)/shard_map/ppermute | solution.py:73
  313.7 34.7 %collective-permute-start.8 = (bf16[1,2,2,128,2,256]{5,3,4,2,1,0:T(8,128)(2,1)S(1)}, bf16[1,2,2,128,2,256]{5,3,4,2,1,0:T(8,128)(2,1)S(1)}, u32[]{:S(2)}, u32[]{:S(2)}) collective-permute-start(bf16[1,2,2,128,2,256]{5,3,4,2,1,0:T(8,128)(2,1)S(1)} %get-tuple-element.477), channel_id=1, source_target_pairs={{0,4},{4,0},{1,5},{5,1},{2,6},{6,2},{3,7},{7,3},{8,12},{12,8},{9,1... | collective-permute-start | bytes 1572872 | tf_op jit(solution)/shard_map/ppermute | solution.py:73
  316.5 85.8 %collective-permute-start.17 = (bf16[512,2560]{1,0:T(8,128)(2,1)}, bf16[512,2560]{1,0:T(8,128)(2,1)}, u32[]{:S(2)}, u32[]{:S(2)}) collective-permute-start(bf16[512,2560]{1,0:T(8,128)(2,1)} %pad_maximum_fusion.3), channel_id=1, source_target_pairs={{0,1},{1,0},{2,3},{3,2},{4,5},{5,4},{6,7},{7,6},{8,9},{9,8},{10,11... | collective-permute-start | bytes 7864328 | tf_op jit(solution)/shard_map/ppermute | solution.py:73
  316.6 36.0 %collective-permute-start.10 = (bf16[1,2,2,128,2,256]{5,3,4,2,1,0:T(8,128)(2,1)S(1)}, bf16[1,2,2,128,2,256]{5,3,4,2,1,0:T(8,128)(2,1)S(1)}, u32[]{:S(2)}, u32[]{:S(2)}) collective-permute-start(bf16[1,2,2,128,2,256]{5,3,4,2,1,0:T(8,128)(2,1)S(1)} %get-tuple-element.476), channel_id=1, source_target_pairs={{0,8},{8,0},{1,9},{9,1},{2,10},{10,2},{3,11},{11,3},{4,12},{12,4},... | collective-permute-start | bytes 1572872 | tf_op jit(solution)/shard_map/ppermute | solution.py:73
  349.9 25.5 %collective-permute-start.9 = (bf16[2,2,2,128,2,256]{5,3,4,2,1,0:T(8,128)(2,1)}, bf16[2,2,2,128,2,256]{5,3,4,2,1,0:T(8,128)(2,1)}, u32[]{:S(2)}, u32[]{:S(2)}) collective-permute-start(bf16[2,2,2,128,2,256]{5,3,4,2,1,0:T(8,128)(2,1)} %get-tuple-element.479), channel_id=1, source_target_pairs={{0,8},{8,0},{1,9},{9,1},{2,10},{10,2},{3,11},{11,3},{4,12},{12,4},... | collective-permute-start | bytes 3145736 | tf_op jit(solution)/shard_map/ppermute | solution.py:73
  354.0 24.3 %collective-permute-start.11 = (bf16[2,2,2,128,2,256]{5,3,4,2,1,0:T(8,128)(2,1)}, bf16[2,2,2,128,2,256]{5,3,4,2,1,0:T(8,128)(2,1)}, u32[]{:S(2)}, u32[]{:S(2)}) collective-permute-start(bf16[2,2,2,128,2,256]{5,3,4,2,1,0:T(8,128)(2,1)} %get-tuple-element.475), channel_id=1, source_target_pairs={{0,4},{4,0},{1,5},{5,1},{2,6},{6,2},{3,7},{7,3},{8,12},{12,8},{9,1... | collective-permute-start | bytes 3145736 | tf_op jit(solution)/shard_map/ppermute | solution.py:73
  421.1 25.4 %collective-permute-start.19 = (bf16[256,2048]{1,0:T(8,128)(2,1)}, bf16[256,2048]{1,0:T(8,128)(2,1)S(1)}, u32[]{:S(2)}, u32[]{:S(2)}) collective-permute-start(bf16[256,2048]{1,0:T(8,128)(2,1)} %multiply_convert_fusion.8), channel_id=1, source_target_pairs={{0,4},{4,0},{1,5},{5,1},{2,6},{6,2},{3,7},{7,3},{8,12},{12,8},{9,1... | collective-permute-start | bytes 3145736 | tf_op jit(solution)/shard_map/ppermute | solution.py:73
  421.8 25.1 %collective-permute-start.20 = (bf16[256,2048]{1,0:T(8,128)(2,1)}, bf16[256,2048]{1,0:T(8,128)(2,1)S(1)}, u32[]{:S(2)}, u32[]{:S(2)}) collective-permute-start(bf16[256,2048]{1,0:T(8,128)(2,1)} %multiply_convert_fusion.8), channel_id=1, source_target_pairs={{0,8},{8,0},{1,9},{9,1},{2,10},{10,2},{3,11},{11,3},{4,12},{12,4},... | collective-permute-start | bytes 3145736 | tf_op jit(solution)/shard_map/ppermute | solution.py:73
  451.6 62.2 %collective-permute-start.22 = (bf16[256,2048]{1,0:T(8,128)(2,1)S(1)}, bf16[256,2048]{1,0:T(8,128)(2,1)}, u32[]{:S(2)}, u32[]{:S(2)}) collective-permute-start(bf16[256,2048]{1,0:T(8,128)(2,1)S(1)} %slice.557), channel_id=1, source_target_pairs={{0,1},{1,0},{2,3},{3,2},{4,5},{5,4},{6,7},{7,6},{8,9},{9,8},{10,11... | collective-permute-start | bytes 3145736 | tf_op jit(solution)/shard_map/ppermute | solution.py:73
  509.2 24.8 %collective-permute-start.34 = (bf16[256,2048]{1,0:T(8,128)(2,1)S(1)}, bf16[256,2048]{1,0:T(8,128)(2,1)S(1)}, u32[]{:S(2)}, u32[]{:S(2)}) collective-permute-start(bf16[256,2048]{1,0:T(8,128)(2,1)S(1)} %pad_maximum_fusion.21), channel_id=1, source_target_pairs={{0,4},{4,0},{1,5},{5,1},{2,6},{6,2},{3,7},{7,3},{8,12},{12,8},{9,1... | collective-permute-start | bytes 3145736 | tf_op jit(solution)/shard_map/ppermute | solution.py:73
  510.9 24.5 %collective-permute-start.30 = (bf16[256,2048]{1,0:T(8,128)(2,1)S(1)}, bf16[256,2048]{1,0:T(8,128)(2,1)S(1)}, u32[]{:S(2)}, u32[]{:S(2)}) collective-permute-start(bf16[256,2048]{1,0:T(8,128)(2,1)S(1)} %pad_maximum_fusion.20), channel_id=1, source_target_pairs={{0,8},{8,0},{1,9},{9,1},{2,10},{10,2},{3,11},{11,3},{4,12},{12,4},... | collective-permute-start | bytes 3145736 | tf_op jit(solution)/shard_map/ppermute | solution.py:73
  551.0 25.6 %collective-permute-start.36 = (bf16[256,2048]{1,0:T(8,128)(2,1)S(1)}, bf16[256,2048]{1,0:T(8,128)(2,1)S(1)}, u32[]{:S(2)}, u32[]{:S(2)}) collective-permute-start(bf16[256,2048]{1,0:T(8,128)(2,1)S(1)} %fusion.111), channel_id=1, source_target_pairs={{0,4},{4,0},{1,5},{5,1},{2,6},{6,2},{3,7},{7,3},{8,12},{12,8},{9,1... | collective-permute-start | bytes 3145736 | tf_op jit(solution)/shard_map/ppermute | solution.py:73
  551.7 25.3 %collective-permute-start.37 = (bf16[256,2048]{1,0:T(8,128)(2,1)S(1)}, bf16[256,2048]{1,0:T(8,128)(2,1)S(1)}, u32[]{:S(2)}, u32[]{:S(2)}) collective-permute-start(bf16[256,2048]{1,0:T(8,128)(2,1)S(1)} %fusion.111), channel_id=1, source_target_pairs={{0,8},{8,0},{1,9},{9,1},{2,10},{10,2},{3,11},{11,3},{4,12},{12,4},... | collective-permute-start | bytes 3145736 | tf_op jit(solution)/shard_map/ppermute | solution.py:73
  580.4 30.9 %collective-permute-start.39 = (bf16[256,2048]{1,0:T(8,128)(2,1)S(1)}, bf16[256,2048]{1,0:T(8,128)(2,1)S(1)}, u32[]{:S(2)}, u32[]{:S(2)}) collective-permute-start(bf16[256,2048]{1,0:T(8,128)(2,1)S(1)} %collective-permute-done.37), channel_id=1, source_target_pairs={{0,1},{1,0},{2,3},{3,2},{4,5},{5,4},{6,7},{7,6},{8,9},{9,8},{10,11... | collective-permute-start | bytes 3145736 | tf_op jit(solution)/shard_map/ppermute | solution.py:73
  580.5 47.8 %collective-permute-start.43 = (bf16[256,2048]{1,0:T(8,128)(2,1)S(1)}, bf16[256,2048]{1,0:T(8,128)(2,1)}, u32[]{:S(2)}, u32[]{:S(2)}) collective-permute-start(bf16[256,2048]{1,0:T(8,128)(2,1)S(1)} %slice.581), channel_id=1, source_target_pairs={{0,1},{1,0},{2,3},{3,2},{4,5},{5,4},{6,7},{7,6},{8,9},{9,8},{10,11... | collective-permute-start | bytes 3145736 | tf_op jit(solution)/shard_map/ppermute | solution.py:73
  592.9 37.2 %collective-permute-start.42 = (bf16[256,2048]{1,0:T(8,128)(2,1)S(1)}, bf16[256,2048]{1,0:T(8,128)(2,1)S(1)}, u32[]{:S(2)}, u32[]{:S(2)}) collective-permute-start(bf16[256,2048]{1,0:T(8,128)(2,1)S(1)} %pad_maximum_fusion.22), channel_id=1, source_target_pairs={{0,1},{1,0},{2,3},{3,2},{4,5},{5,4},{6,7},{7,6},{8,9},{9,8},{10,11... | collective-permute-start | bytes 3145736 | tf_op jit(solution)/shard_map/ppermute | solution.py:73
  611.3 30.5 %collective-permute-start.44 = (bf16[256,2048]{1,0:T(8,128)(2,1)}, bf16[256,2048]{1,0:T(8,128)(2,1)}, u32[]{:S(2)}, u32[]{:S(2)}) collective-permute-start(bf16[256,2048]{1,0:T(8,128)(2,1)} %slice.729), channel_id=1, source_target_pairs={{0,1},{1,0},{2,3},{3,2},{4,5},{5,4},{6,7},{7,6},{8,9},{9,8},{10,11... | collective-permute-start | bytes 3145736 | tf_op jit(solution)/shard_map/ppermute | solution.py:73
  645.4 25.7 %collective-permute-start.49 = (bf16[128,2048]{1,0:T(8,128)(2,1)S(1)}, bf16[128,2048]{1,0:T(8,128)(2,1)S(1)}, u32[]{:S(2)}, u32[]{:S(2)}) collective-permute-start(bf16[128,2048]{1,0:T(8,128)(2,1)S(1)} %get-tuple-element.471), channel_id=1, source_target_pairs={{0,8},{8,0},{1,9},{9,1},{2,10},{10,2},{3,11},{11,3},{4,12},{12,4},... | collective-permute-start | bytes 1572872 | tf_op jit(solution)/shard_map/ppermute | solution.py:73
  646.2 27.5 %collective-permute-start.47 = (bf16[128,2048]{1,0:T(8,128)(2,1)S(1)}, bf16[128,2048]{1,0:T(8,128)(2,1)S(1)}, u32[]{:S(2)}, u32[]{:S(2)}) collective-permute-start(bf16[128,2048]{1,0:T(8,128)(2,1)S(1)} %get-tuple-element.470), channel_id=1, source_target_pairs={{0,4},{4,0},{1,5},{5,1},{2,6},{6,2},{3,7},{7,3},{8,12},{12,8},{9,1... | collective-permute-start | bytes 1572872 | tf_op jit(solution)/shard_map/ppermute | solution.py:73
  672.3 26.1 %collective-permute-start.50 = (bf16[256,2048]{1,0:T(8,128)(2,1)}, bf16[256,2048]{1,0:T(8,128)(2,1)}, u32[]{:S(2)}, u32[]{:S(2)}) collective-permute-start(bf16[256,2048]{1,0:T(8,128)(2,1)} %pad_maximum_fusion.24), channel_id=1, source_target_pairs={{0,4},{4,0},{1,5},{5,1},{2,6},{6,2},{3,7},{7,3},{8,12},{12,8},{9,1... | collective-permute-start | bytes 3145736 | tf_op jit(solution)/shard_map/ppermute | solution.py:73
  674.9 24.8 %collective-permute-start.48 = (bf16[256,2048]{1,0:T(8,128)(2,1)}, bf16[256,2048]{1,0:T(8,128)(2,1)S(1)}, u32[]{:S(2)}, u32[]{:S(2)}) collective-permute-start(bf16[256,2048]{1,0:T(8,128)(2,1)} %pad_maximum_fusion.23), channel_id=1, source_target_pairs={{0,8},{8,0},{1,9},{9,1},{2,10},{10,2},{3,11},{11,3},{4,12},{12,4},... | collective-permute-start | bytes 3145736 | tf_op jit(solution)/shard_map/ppermute | solution.py:73
  749.8 48.1 %collective-permute-start.52 = (bf16[512,2048]{1,0:T(8,128)(2,1)S(1)}, bf16[512,2048]{1,0:T(8,128)(2,1)S(1)}, u32[]{:S(2)}, u32[]{:S(2)}) collective-permute-start(bf16[512,2048]{1,0:T(8,128)(2,1)S(1)} %slice.601), channel_id=1, source_target_pairs={{0,4},{4,0},{1,5},{5,1},{2,6},{6,2},{3,7},{7,3},{8,12},{12,8},{9,1... | collective-permute-start | bytes 6291464 | tf_op jit(solution)/shard_map/ppermute | solution.py:73
  808.6 40.9 %collective-permute-start.55 = (bf16[2,2,2,128,2,256]{5,3,4,2,1,0:T(8,128)(2,1)}, bf16[2,2,2,128,2,256]{5,3,4,2,1,0:T(8,128)(2,1)}, u32[]{:S(2)}, u32[]{:S(2)}) collective-permute-start(bf16[2,2,2,128,2,256]{5,3,4,2,1,0:T(8,128)(2,1)} %slice_bitcast_fusion), channel_id=1, source_target_pairs={{0,4},{4,0},{1,5},{5,1},{2,6},{6,2},{3,7},{7,3},{8,12},{12,8},{9,1... | collective-permute-start | bytes 3145736 | tf_op jit(solution)/shard_map/ppermute | solution.py:73
  830.7 70.9 %collective-permute-start.58 = (bf16[1024,2048]{1,0:T(8,128)(2,1)S(1)}, bf16[1024,2048]{1,0:T(8,128)(2,1)S(1)}, u32[]{:S(2)}, u32[]{:S(2)}) collective-permute-start(bf16[1024,2048]{1,0:T(8,128)(2,1)S(1)} %convolution_convert_fusion.2), channel_id=1, source_target_pairs={{0,1},{1,0},{2,3},{3,2},{4,5},{5,4},{6,7},{7,6},{8,9},{9,8},{10,11... | collective-permute-start | bytes 12582920 | tf_op jit(solution)/shard_map/ppermute | solution.py:73
  837.8 46.1 %collective-permute-start.53 = (bf16[2,2,2,128,2,256]{5,3,4,2,1,0:T(8,128)(2,1)S(1)}, bf16[2,2,2,128,2,256]{5,3,4,2,1,0:T(8,128)(2,1)S(1)}, u32[]{:S(2)}, u32[]{:S(2)}) collective-permute-start(bf16[2,2,2,128,2,256]{5,3,4,2,1,0:T(8,128)(2,1)S(1)} %bitcast.522), channel_id=1, source_target_pairs={{0,8},{8,0},{1,9},{9,1},{2,10},{10,2},{3,11},{11,3},{4,12},{12,4},... | collective-permute-start | bytes 3145736 | tf_op jit(solution)/shard_map/ppermute | solution.py:73
  839.5 46.3 %collective-permute-start.60 = (bf16[1024,512]{1,0:T(8,128)(2,1)S(1)}, bf16[1024,512]{1,0:T(8,128)(2,1)S(1)}, u32[]{:S(2)}, u32[]{:S(2)}) collective-permute-start(bf16[1024,512]{1,0:T(8,128)(2,1)S(1)} %pad_maximum_fusion.25), channel_id=1, source_target_pairs={{0,1},{1,0},{2,3},{3,2},{4,5},{5,4},{6,7},{7,6},{8,9},{9,8},{10,11... | collective-permute-start | bytes 3145736 | tf_op jit(solution)/shard_map/ppermute | solution.py:73
  852.0 49.2 %collective-permute-start.56 = (bf16[2,2,128,2,256]{4,2,3,1,0:T(8,128)(2,1)S(1)}, bf16[2,2,128,2,256]{4,2,3,1,0:T(8,128)(2,1)S(1)}, u32[]{:S(2)}, u32[]{:S(2)}) collective-permute-start(bf16[2,2,128,2,256]{4,2,3,1,0:T(8,128)(2,1)S(1)} %slice_bitcast_fusion.4), channel_id=1, source_target_pairs={{0,8},{8,0},{1,9},{9,1},{2,10},{10,2},{3,11},{11,3},{4,12},{12,4},... | collective-permute-start | bytes 1572872 | tf_op jit(solution)/shard_map/ppermute | solution.py:73
  886.1 24.2 %collective-permute-start.61 = (bf16[512,512]{1,0:T(8,128)(2,1)S(1)}, bf16[512,512]{1,0:T(8,128)(2,1)S(1)}, u32[]{:S(2)}, u32[]{:S(2)}) collective-permute-start(bf16[512,512]{1,0:T(8,128)(2,1)S(1)} %slice.761), channel_id=1, source_target_pairs={{0,4},{4,0},{1,5},{5,1},{2,6},{6,2},{3,7},{7,3},{8,12},{12,8},{9,1... | collective-permute-start | bytes 1572872 | tf_op jit(solution)/shard_map/ppermute | solution.py:73
  901.6 42.5 %collective-permute-start.57 = (bf16[2,2,128,2,256]{4,2,3,1,0:T(8,128)(2,1)S(1)}, bf16[2,2,128,2,256]{4,2,3,1,0:T(8,128)(2,1)S(1)}, u32[]{:S(2)}, u32[]{:S(2)}) collective-permute-start(bf16[2,2,128,2,256]{4,2,3,1,0:T(8,128)(2,1)S(1)} %fusion.211), channel_id=1, source_target_pairs={{0,16},{16,0},{1,17},{17,1},{2,18},{18,2},{3,19},{19,3},{4,20},{20... | collective-permute-start | bytes 1572872 | tf_op jit(solution)/shard_map/ppermute | solution.py:73
  903.2 51.1 %collective-permute-start.59 = (bf16[512,2048]{1,0:T(8,128)(2,1)S(1)}, bf16[512,2048]{1,0:T(8,128)(2,1)S(1)}, u32[]{:S(2)}, u32[]{:S(2)}) collective-permute-start(bf16[512,2048]{1,0:T(8,128)(2,1)S(1)} %slice.755), channel_id=1, source_target_pairs={{0,4},{4,0},{1,5},{5,1},{2,6},{6,2},{3,7},{7,3},{8,12},{12,8},{9,1... | collective-permute-start | bytes 6291464 | tf_op jit(solution)/shard_map/ppermute | solution.py:73
  977.0 46.1 %collective-permute-start.63 = (bf16[512,1152]{0,1:T(8,128)(2,1)}, bf16[512,1152]{0,1:T(8,128)(2,1)}, u32[]{:S(2)}, u32[]{:S(2)}) collective-permute-start(bf16[512,1152]{0,1:T(8,128)(2,1)} %slice.765), channel_id=1, source_target_pairs={{0,4},{4,0},{1,5},{5,1},{2,6},{6,2},{3,7},{7,3},{8,12},{12,8},{9,1... | collective-permute-start | bytes 3538952 | tf_op jit(solution)/shard_map/ppermute | solution.py:73
  980.5 46.0 %collective-permute-start.65 = (bf16[256,2048]{1,0:T(8,128)(2,1)}, bf16[256,2048]{1,0:T(8,128)(2,1)}, u32[]{:S(2)}, u32[]{:S(2)}) collective-permute-start(bf16[256,2048]{1,0:T(8,128)(2,1)} %get-tuple-element.460), channel_id=1, source_target_pairs={{0,2},{2,0},{1,3},{3,1},{4,6},{6,4},{5,7},{7,5},{8,10},{10,8},{9,1... | collective-permute-start | bytes 3145736 | tf_op jit(solution)/shard_map/ppermute | solution.py:73
  981.9 53.0 %collective-permute-start.67 = (bf16[256,2560]{1,0:T(8,128)(2,1)}, bf16[256,2560]{1,0:T(8,128)(2,1)}, u32[]{:S(2)}, u32[]{:S(2)}) collective-permute-start(bf16[256,2560]{1,0:T(8,128)(2,1)} %get-tuple-element.454), channel_id=1, source_target_pairs={{0,2},{2,0},{1,3},{3,1},{4,6},{6,4},{5,7},{7,5},{8,10},{10,8},{9,1... | collective-permute-start | bytes 3932168 | tf_op jit(solution)/shard_map/ppermute | solution.py:73
  984.7 140.0 %all-to-all-start.1 = ((bf16[8,192,1024]{2,1,0:T(8,128)(2,1)}), bf16[8,192,1024]{2,1,0:T(8,128)(2,1)}, u32[]{:S(2)}, u32[]{:S(2)}) async-start(bf16[8,192,1024]{2,1,0:T(8,128)(2,1)} %pad_maximum_fusion.2), calls=%async_computation.2 | async-start | bytes 6291456 | tf_op jit(solution)/shard_map/all_to_all | solution.py:203
  1069.5 25.2 %collective-permute-start.70 = (bf16[64,2560]{1,0:T(8,128)(2,1)}, bf16[64,2560]{1,0:T(8,128)(2,1)S(1)}, u32[]{:S(2)}, u32[]{:S(2)}) collective-permute-start(bf16[64,2560]{1,0:T(8,128)(2,1)} %slice.645), channel_id=1, source_target_pairs={{0,16},{16,0},{1,17},{17,1},{2,18},{18,2},{3,19},{19,3},{4,20},{20... | collective-permute-start | bytes 983048 | tf_op jit(solution)/shard_map/ppermute | solution.py:73
  (242 other events, 3741.3 us)
Sparse Core Ops, SparseCore 0:
  76.8 249.1 all-gather.1
  702.9 244.7 reduce-scatter.1

commit v11 on v10

--- a/solution.py
+++ b/solution.py
@@ -197,14 +197,9 @@
             place = (place[:, None] + weight * jnp.stack([bit, 1 - bit])[None, :]).reshape(-1)
         return place
 
-    def own_rows(self, sums, local_rows):
-        size = 2 ** len(self.team)
-        sums = jnp.concatenate([one.reshape(size, local_rows, -1) for one in sums], axis=1)
-        moved = lax.all_to_all(sums, self.team, split_axis=0, concat_axis=0, tiled=True)
-        return [
-            jnp.concatenate([moved[at, first : first + local_rows] for at in range(size)], axis=1).astype(F32)
-            for first in range(0, moved.shape[1], local_rows)
-        ]
+    def to_rows(self, sums, local_rows):
+        blocks = sums.reshape(2 ** len(self.team), local_rows, -1)
+        return lax.all_to_all(blocks, self.team, split_axis=0, concat_axis=0, tiled=True)
 
     def total(self, value):
         for axis in reversed(self.every):
@@ -321,10 +316,9 @@
             one.reshape(local_rows, team_size, hidden_own).transpose(1, 0, 2)
             for one in (gate_weight, up_weight, down_weight)
         ],
-        axis=1,
+        axis=2,
     )
     feed_team = lax.all_to_all(feed_local, plan.team, split_axis=0, concat_axis=0, tiled=True)
-    feed_team = feed_team.reshape(team_size, 3, local_rows, hidden_own).transpose(1, 0, 2, 3)
     block_widths = [sum(kvl_widths), query_weight.shape[1], sum(rest_widths)]
     attn_block = jnp.concatenate(
         [key_weight, value_weight, laurel_left, laurel_right, query_weight]
@@ -333,7 +327,7 @@
     )
     attn_block = plan.grow(attn_block, plan.far_seq)
     attn_block, feed_team = together(attn_block, feed_team)
-    feed_full = lax.all_gather(feed_team.reshape(-1, hidden_own), plan.far, axis=0, tiled=True)
+    feed_full = lax.all_gather(feed_team.reshape(-1, 3 * hidden_own), plan.far, axis=0, tiled=True)
     attn_block = plan.grow(attn_block, (plan.l,))
     kvl_block, query_block, rest_block = split_columns(attn_block, block_widths)
     kvl_block = plan.grow(kvl_block, plan.far_dp)
@@ -439,8 +433,7 @@
     )
 
     feed_low = feed_in.astype(BF16)
-    feed_full = feed_full.reshape(-1, 3, team_size * local_rows, hidden_own)
-    gate_full, up_full, down_full = [feed_full[:, at].reshape(width, hidden_own) for at in range(3)]
+    gate_full, up_full, down_full = split_columns(feed_full, [hidden_own] * 3)
     pulls = []
     hidden_chunks = []
 
@@ -489,11 +482,9 @@
     )
     feed_all = jnp.concatenate(feed_chunks, axis=0)
     d_out_all = jnp.concatenate(d_out_chunks, axis=0)
-    feed_terms = jnp.stack(
+    feed_terms = jnp.concatenate(
         [
-            product_tn(left, jnp.concatenate(right, axis=0))
-            .astype(BF16)
-            .reshape(-1, team_size * local_rows, hidden_own)
+            product_tn(left, jnp.concatenate(right, axis=0)).astype(BF16)
             for left, right in (
                 (feed_all, d_gate_chunks),
                 (feed_all, d_up_chunks),
@@ -504,9 +495,7 @@
     )
     d_feed_in = plan.team_far(plan.team_near(d_feed_sums))
     d_feed_in, feed_terms = together(d_feed_in, feed_terms)
-    feed_sum = lax.psum_scatter(
-        feed_terms.reshape(-1, hidden_own), plan.far, scatter_dimension=0, tiled=True
-    )
+    feed_sum = lax.psum_scatter(feed_terms, plan.far, scatter_dimension=0, tiled=True)
     steps = tuple(reversed(plan.order))
 
     (
@@ -572,7 +561,6 @@
         d_keys, d_values, query_sum, output_sum, side_sum, d_spread, feed_sum
     )
     output_sum = jnp.concatenate([output_sum, side_sum], axis=1)
-    grad_gate, grad_up, grad_down = plan.own_rows(jnp.split(feed_sum, 3), local_rows)
     d_kvl_low = jnp.concatenate(
         [
             d_keys.reshape(rows, -1).astype(BF16),
@@ -586,7 +574,10 @@
     query_kept, query_away = plan.spread_send(query_sum, steps[1])
     output_kept, output_away = plan.spread_send(output_sum, steps[1])
     kvl_sum = plan.spread_step(kvl_sum, steps[:1])
-    kvl_sum, query_kept, output_kept = together(kvl_sum, query_kept, output_kept)
+    kvl_sum, query_kept, output_kept, feed_sum = together(
+        kvl_sum, query_kept, output_kept, feed_sum
+    )
+    feed_grads = plan.to_rows(feed_sum, local_rows)
     query_sum = (query_kept + query_away).astype(BF16)
     output_sum = (output_kept + output_away).astype(BF16)
     kvl_sum = plan.spread_step(kvl_sum, steps[1:2])
@@ -614,9 +605,15 @@
     grad_query = plan.spread_step(query_sum, steps[3:])
     output_sum = plan.spread_step(output_sum, steps[3:])
     kvl_sum = plan.spread_step(kvl_sum, steps[2:3])
-    gain_grads, grad_query, output_sum, kvl_sum = together(
-        gain_grads, grad_query, output_sum, kvl_sum
-    )
+    gain_grads, grad_query, output_sum, kvl_sum, feed_grads = together(
+        gain_grads, grad_query, output_sum, kvl_sum, feed_grads
+    )
+    grad_gate, grad_up, grad_down = [
+        jnp.concatenate(
+            [feed_grads[at, :, first : first + hidden_own] for at in range(team_size)], axis=1
+        ).astype(F32)
+        for first in range(0, 3 * hidden_own, hidden_own)
+    ]
     grad_output, grad_side_gate, grad_side_output = split_columns(output_sum, rest_widths)
     grad_key, grad_value, grad_left, grad_right = split_columns(
         plan.spread_step(kvl_sum, steps[3:]), kvl_widths

time: 1150 us -> 1200 us (1.043)
  matrix products: 264 us -> 306 us
    dot_general x31, matrix products: 93.5 us -> 114 us  [product_nt(): lax.dot_general(left, right, (((1,), (1,)), ((), ())), preferred_element_...]
    dot_general x33, matrix products: 102 us -> 122 us  [product(): return jnp.dot(left, right, preferred_element_type=F32)]
    concatenate x1, other arithmetic: 1.93 us -> 21.3 us  [body(): jnp.concatenate([product_tn(left, jnp.concatenate(right, axis=0)).astype(...]
    unnamed x460 -> x470, local copies, waits for them, and re-layouts: 50.7 us -> 51.4 us
  transfers between devices with their start and end apart: 82 -> 82, of which waited for: 41 -> 37; matrix products, arithmetic and copies ran while one was open for 40% -> 44% of each run, Pallas kernels for 0% -> 0%
where the time goes in v11:
time: 1200 us; the launch traced here: 1190 us
  waiting for transfers between devices  513 us (43%)
  matrix products  306 us (26%)
  other arithmetic  139 us (12%)
  local copies, waits for them, and re-layouts  138 us (12%)
  starting transfers between devices  75.4 us (6%)
  between operations  18.5 us (2%)
    ppermute x78, waiting for transfers between devices, swap(): return lax.ppermute(value, axis, [(0, 1), (1, 0)])  512 us
    dot_general x33, matrix products, product(): return jnp.dot(left, right, preferred_element_type=F32)  122 us
    dot_general x31, matrix products, product_nt(): lax.dot_general(left, right, (((1,), (1,)), ((), ())), preferred_element_...  114 us
    ppermute x78, starting transfers between devices, swap(): return lax.ppermute(value, axis, [(0, 1), (1, 0)])  64.8 us
    dot_general x15, matrix products, product_tn(): lax.dot_general(left, right, (((0,), (0,)), ((), ())), preferred_element_...  56.2 us
    unnamed x470, local copies, waits for them, and re-layouts  51.4 us
  transfers between devices with their start and end apart: 82, of which 37 were waited for; matrix products, arithmetic and copies ran while one was open for 44% of the time, Pallas kernels for 0%

profile of v11, /device:TPU:0, one launch (start us, length us, event | category | flops | bytes accessed | tf_op | source)
XLA Modules:
  0.0 1190.2 jit_solution(14339634467704724954)
XLA Ops:
  14.2 5.4 all-to-all-start
  24.5 45.8 %collective-permute-done = bf16[64,5760]{1,0:T(8,128)(2,1)} collective-permute-done((bf16[64,5760]{1,0:T(8,128)(2,1)S(1)}, bf16[64,5760]{1,0:T(8,128)(2,1)}, u32[]{:S(2)}, u32[]{:S(2)}) %collective-permute-start) | collective-permute-done | bytes 737312 | tf_op jit(solution)/shard_map/ppermute | solution.py:73
  78.1 55.7 %collective-permute-done.1 = bf16[128,5760]{1,0:T(8,128)(2,1)S(1)} collective-permute-done((bf16[128,5760]{1,0:T(8,128)(2,1)S(1)}, bf16[128,5760]{1,0:T(8,128)(2,1)S(1)}, u32[]{:S(2)}, u32[]{:S(2)}) %collective-permute-start.1) | collective-permute-done | bytes 1474592 | tf_op jit(solution)/shard_map/ppermute | solution.py:73
  136.3 9.0 collective-permute-done.2
  154.5 15.3 %collective-permute-done.3 = bf16[512,1152]{1,0:T(8,128)(2,1)} collective-permute-done((bf16[512,1152]{1,0:T(8,128)(2,1)}, bf16[512,1152]{1,0:T(8,128)(2,1)}, u32[]{:S(2)}, u32[]{:S(2)}) %collective-permute-start.3) | collective-permute-done | bytes 1179680 | tf_op jit(solution)/shard_map/ppermute | solution.py:73
  173.1 5.2 fusion.76
  181.1 7.8 collective-permute-done.13
  203.8 5.8 rev.69
  242.0 26.5 %collective-permute-done.6 = bf16[256,2560]{1,0:T(8,128)(2,1)} collective-permute-done((bf16[256,2560]{1,0:T(8,128)(2,1)}, bf16[256,2560]{1,0:T(8,128)(2,1)}, u32[]{:S(2)}, u32[]{:S(2)}) %collective-permute-start.6) | collective-permute-done | bytes 1310752 | tf_op jit(solution)/shard_map/ppermute | solution.py:73
  277.0 32.4 %collective-permute-done.7 = bf16[2,1,2,128,2,256]{5,3,4,2,1,0:T(8,128)(2,1)S(1)} collective-permute-done((bf16[2,1,2,128,2,256]{5,3,4,2,1,0:T(8,128)(2,1)S(1)}, bf16[2,1,2,128,2,256]{5,3,4,2,1,0:T(8,128)(2,1)S(1)}, u32[]{:S(2)}, u32[]{:S(2)}) %collective-permute-start.7) | collective-permute-done | bytes 524320 | tf_op jit(solution)/shard_map/ppermute | solution.py:73
  314.6 29.6 %collective-permute-done.8 = bf16[1,2,2,128,2,256]{5,3,4,2,1,0:T(8,128)(2,1)S(1)} collective-permute-done((bf16[1,2,2,128,2,256]{5,3,4,2,1,0:T(8,128)(2,1)S(1)}, bf16[1,2,2,128,2,256]{5,3,4,2,1,0:T(8,128)(2,1)S(1)}, u32[]{:S(2)}, u32[]{:S(2)}) %collective-permute-start.8) | collective-permute-done | bytes 524320 | tf_op jit(solution)/shard_map/ppermute | solution.py:73
  355.3 15.9 %collective-permute-done.9 = bf16[2,2,2,128,2,256]{5,3,4,2,1,0:T(8,128)(2,1)} collective-permute-done((bf16[2,2,2,128,2,256]{5,3,4,2,1,0:T(8,128)(2,1)}, bf16[2,2,2,128,2,256]{5,3,4,2,1,0:T(8,128)(2,1)}, u32[]{:S(2)}, u32[]{:S(2)}) %collective-permute-start.9) | collective-permute-done | bytes 1048608 | tf_op jit(solution)/shard_map/ppermute | solution.py:73
  419.8 5.2 fusion.238
  425.0 6.5 multiply_convert_fusion.7
  433.9 8.8 collective-permute-done.19
  448.0 7.9 collective-permute-done.25
  462.4 6.9 multiply_convert_fusion.4
  479.7 6.9 multiply_convert_fusion.6
  491.6 6.9 multiply_convert_fusion.5
  513.0 10.6 collective-permute-done.33
  528.8 19.9 %collective-permute-done.34 = bf16[256,2048]{1,0:T(8,128)(2,1)S(1)} collective-permute-done((bf16[256,2048]{1,0:T(8,128)(2,1)S(1)}, bf16[256,2048]{1,0:T(8,128)(2,1)S(1)}, u32[]{:S(2)}, u32[]{:S(2)}) %collective-permute-start.34) | collective-permute-done | bytes 1048608 | tf_op jit(solution)/shard_map/ppermute | solution.py:73
  579.7 11.0 collective-permute-done.36
  595.4 11.0 collective-permute-done.40
  609.6 5.9 multiply_convert_fusion.2
  615.5 7.5 fusion.228
  623.0 5.9 add_convert_fusion.7
  631.9 5.9 multiply_convert_fusion.1
  637.8 7.3 fusion.226
  645.1 5.9 add_convert_fusion.6
  654.2 6.4 multiply_convert_fusion
  660.6 5.3 fusion.224
  684.6 13.6 %fusion.64 = bf16[2048,1024]{0,1:T(8,128)(2,1)} fusion(bf16[512,1024]{1,0:T(8,128)(2,1)} %copy-done.200, bf16[512,1024]{1,0:T(8,128)(2,1)} %copy-done.199, bf16[512,1024]{1,0:T(8,128)(2,1)} %copy-done.198, bf16[512,1024]{1,0:T(8,128)(2,1)S(1)} %copy-done.197, bf16[512,2048]{1,0:T(8,128)(2,1)} %copy-done.89, bf16[512,2048]{1,0:T(8,128)(2,1)} %copy-done.80, ...), kind=kOutput, calls=%fused_computation.77 | convolution fusion | flops 8642363392 | bytes 16777216 | tf_op jit(solution)/shard_map/dot_general | solution.py:34
  698.2 13.6 %fusion.58 = bf16[2048,1024]{0,1:T(8,128)(2,1)S(1)} fusion(bf16[2048,2048]{1,0:T(8,128)(2,1)} %constant_dynamic-update-slice_fusion.22, bf16[512,1024]{1,0:T(8,128)(2,1)} %copy-done.204, bf16[512,1024]{1,0:T(8,128)(2,1)} %copy-done.203, bf16[512,1024]{1,0:T(8,128)(2,1)} %copy-done.202, bf16[512,1024]{1,0:T(8,128)(2,1)} %copy-done.201), kind=kOutput, calls=%fused_computation.75 | convolution fusion | flops 8608808960 | bytes 16777216 | tf_op jit(solution)/shard_map/dot_general | solution.py:34
  718.2 11.6 fusion.61
  729.9 21.3 %pad_maximum_fusion = bf16[2048,3072]{0,1:T(8,128)(2,1)} fusion(bf16[2048,1024]{0,1:T(8,128)(2,1)S(1)} %copy-done.52, bf16[2048,1024]{0,1:T(8,128)(2,1)S(1)} %fusion.58, bf16[2048,1024]{0,1:T(8,128)(2,1)S(1)} %fusion.61), kind=kLoop, calls=%fused_computation.13 | loop fusion | flops 37748736 | bytes 25165824 | tf_op jit(solution)/shard_map/concatenate | solution.py:485
  779.7 5.4 add_convert_fusion.1
  815.6 31.4 %collective-permute-done.52 = bf16[512,2048]{1,0:T(8,128)(2,1)S(1)} collective-permute-done((bf16[512,2048]{1,0:T(8,128)(2,1)S(1)}, bf16[512,2048]{1,0:T(8,128)(2,1)S(1)}, u32[]{:S(2)}, u32[]{:S(2)}) %collective-permute-start.52) | collective-permute-done | bytes 2097184 | tf_op jit(solution)/shard_map/ppermute | solution.py:73
  878.6 5.0 fusion.69
  900.8 35.2 %collective-permute-done.53 = bf16[2,2,2,128,2,256]{5,3,4,2,1,0:T(8,128)(2,1)S(1)} collective-permute-done((bf16[2,2,2,128,2,256]{5,3,4,2,1,0:T(8,128)(2,1)S(1)}, bf16[2,2,2,128,2,256]{5,3,4,2,1,0:T(8,128)(2,1)S(1)}, u32[]{:S(2)}, u32[]{:S(2)}) %collective-permute-start.53) | collective-permute-done | bytes 1048608 | tf_op jit(solution)/shard_map/ppermute | solution.py:73
  938.9 9.8 collective-permute-done.56
  954.6 7.8 collective-permute-done.61
  963.4 28.1 %collective-permute-done.57 = bf16[2,2,128,2,256]{4,2,3,1,0:T(8,128)(2,1)S(1)} collective-permute-done((bf16[2,2,128,2,256]{4,2,3,1,0:T(8,128)(2,1)S(1)}, bf16[2,2,128,2,256]{4,2,3,1,0:T(8,128)(2,1)S(1)}, u32[]{:S(2)}, u32[]{:S(2)}) %collective-permute-start.57) | collective-permute-done | bytes 524320 | tf_op jit(solution)/shard_map/ppermute | solution.py:73
  993.3 13.1 %collective-permute-done.59 = bf16[512,2048]{1,0:T(8,128)(2,1)S(1)} collective-permute-done((bf16[512,2048]{1,0:T(8,128)(2,1)S(1)}, bf16[512,2048]{1,0:T(8,128)(2,1)S(1)}, u32[]{:S(2)}, u32[]{:S(2)}) %collective-permute-start.59) | collective-permute-done | bytes 2097184 | tf_op jit(solution)/shard_map/ppermute | solution.py:73
  1013.3 7.6 fusion.75
  1035.4 24.6 %collective-permute-done.63 = bf16[512,1152]{0,1:T(8,128)(2,1)S(1)} collective-permute-done((bf16[512,1152]{0,1:T(8,128)(2,1)S(1)}, bf16[512,1152]{0,1:T(8,128)(2,1)S(1)}, u32[]{:S(2)}, u32[]{:S(2)}) %collective-permute-start.63) | collective-permute-done | bytes 1179680 | tf_op jit(solution)/shard_map/ppermute | solution.py:73
  1063.6 16.8 %collective-permute-done.67 = bf16[256,2560]{1,0:T(8,128)(2,1)S(1)} collective-permute-done((bf16[256,2560]{1,0:T(8,128)(2,1)S(1)}, bf16[256,2560]{1,0:T(8,128)(2,1)S(1)}, u32[]{:S(2)}, u32[]{:S(2)}) %collective-permute-start.67) | collective-permute-done | bytes 1310752 | tf_op jit(solution)/shard_map/ppermute | solution.py:73
  1130.7 5.8 collective-permute-done.69
  1138.3 12.3 %collective-permute-done.71 = bf16[128,1152]{0,1:T(8,128)(2,1)S(1)} collective-permute-done((bf16[128,1152]{0,1:T(8,128)(2,1)S(1)}, bf16[128,1152]{0,1:T(8,128)(2,1)S(1)}, u32[]{:S(2)}, u32[]{:S(2)}) %collective-permute-start.71) | collective-permute-done | bytes 294944 | tf_op jit(solution)/shard_map/ppermute | solution.py:73
  (967 shorter events, 502.7 us)
Async XLA Ops:
  14.2 58.2 %all-to-all-start = ((bf16[8,64,3072]{2,1,0:T(8,128)(2,1)}), bf16[8,64,3072]{2,1,0:T(8,128)(2,1)}, u32[]{:S(2)}, u32[]{:S(2)}) async-start(bf16[8,64,3072]{2,1,0:T(8,128)(2,1)} %copy.443), calls=%async_computation | async-start | bytes 6291456 | tf_op jit(solution)/shard_map/all_to_all | solution.py:321
  19.6 371.2 %all-gather.2.cloned.1.call-start = ((), (), s32[]{:S(2)}) async-start(), calls=%async_computation.3 | async-start | bytes 15728640 | tf_op jit(solution)/shard_map/all_gather | solution.py:330
  20.0 50.3 %collective-permute-start = (bf16[64,5760]{1,0:T(8,128)(2,1)S(1)}, bf16[64,5760]{1,0:T(8,128)(2,1)}, u32[]{:S(2)}, u32[]{:S(2)}) collective-permute-start(bf16[64,5760]{1,0:T(8,128)(2,1)S(1)} %concatenate.177), channel_id=1, source_target_pairs={{0,16},{16,0},{1,17},{17,1},{2,18},{18,2},{3,19},{19,3},{4,20},{20... | collective-permute-start | bytes 2211848 | tf_op jit(solution)/shard_map/ppermute | solution.py:73
  72.5 936.0 %reduce-scatter.2.cloned.1.call-start = ((), (), s32[]{:S(2)}) async-start(), calls=%async_computation.4 | async-start | bytes 15728640 | tf_op jit(solution)/shard_map/reduce_scatter | solution.py:498
  73.4 60.4 %collective-permute-start.1 = (bf16[128,5760]{1,0:T(8,128)(2,1)S(1)}, bf16[128,5760]{1,0:T(8,128)(2,1)S(1)}, u32[]{:S(2)}, u32[]{:S(2)}) collective-permute-start(bf16[128,5760]{1,0:T(8,128)(2,1)S(1)} %pad_maximum_fusion.13), channel_id=1, source_target_pairs={{0,8},{8,0},{1,9},{9,1},{2,10},{10,2},{3,11},{11,3},{4,12},{12,4},... | collective-permute-start | bytes 4423688 | tf_op jit(solution)/shard_map/ppermute | solution.py:73
  152.9 36.1 %collective-permute-start.13 = (bf16[256,2048]{1,0:T(8,128)(2,1)S(1)}, bf16[256,2048]{1,0:T(8,128)(2,1)}, u32[]{:S(2)}, u32[]{:S(2)}) collective-permute-start(bf16[256,2048]{1,0:T(8,128)(2,1)S(1)} %slice.701), channel_id=1, source_target_pairs={{0,2},{2,0},{1,3},{3,1},{4,6},{6,4},{5,7},{7,5},{8,10},{10,8},{9,1... | collective-permute-start | bytes 3145736 | tf_op jit(solution)/shard_map/ppermute | solution.py:73
  154.5 37.2 %collective-permute-start.4 = (bf16[512,1152]{1,0:T(8,128)(2,1)}, bf16[512,1152]{1,0:T(8,128)(2,1)}, u32[]{:S(2)}, u32[]{:S(2)}) collective-permute-start(bf16[512,1152]{1,0:T(8,128)(2,1)} %pad_maximum_fusion.14), channel_id=1, source_target_pairs={{0,1},{1,0},{2,3},{3,2},{4,5},{5,4},{6,7},{7,6},{8,9},{9,8},{10,11... | collective-permute-start | bytes 3538952 | tf_op jit(solution)/shard_map/ppermute | solution.py:73
  191.7 83.0 %collective-permute-start.15 = (bf16[512,2048]{1,0:T(8,128)(2,1)}, bf16[512,2048]{1,0:T(8,128)(2,1)}, u32[]{:S(2)}, u32[]{:S(2)}) collective-permute-start(bf16[512,2048]{1,0:T(8,128)(2,1)} %pad_maximum_fusion.6), channel_id=1, source_target_pairs={{0,1},{1,0},{2,3},{3,2},{4,5},{5,4},{6,7},{7,6},{8,9},{9,8},{10,11... | collective-permute-start | bytes 6291464 | tf_op jit(solution)/shard_map/ppermute | solution.py:73
  191.7 49.8 %collective-permute-start.14 = (bf16[512,2048]{1,0:T(8,128)(2,1)}, bf16[512,2048]{1,0:T(8,128)(2,1)}, u32[]{:S(2)}, u32[]{:S(2)}) collective-permute-start(bf16[512,2048]{1,0:T(8,128)(2,1)} %pad_maximum_fusion.6), channel_id=1, source_target_pairs={{0,4},{4,0},{1,5},{5,1},{2,6},{6,2},{3,7},{7,3},{8,12},{12,8},{9,1... | collective-permute-start | bytes 6291464 | tf_op jit(solution)/shard_map/ppermute | solution.py:73
  228.4 40.0 %collective-permute-start.6 = (bf16[256,2560]{1,0:T(8,128)(2,1)}, bf16[256,2560]{1,0:T(8,128)(2,1)}, u32[]{:S(2)}, u32[]{:S(2)}) collective-permute-start(bf16[256,2560]{1,0:T(8,128)(2,1)} %slice.691), channel_id=1, source_target_pairs={{0,2},{2,0},{1,3},{3,1},{4,6},{6,4},{5,7},{7,5},{8,10},{10,8},{9,1... | collective-permute-start | bytes 3932168 | tf_op jit(solution)/shard_map/ppermute | solution.py:73
  241.5 71.0 %collective-permute-start.16 = (bf16[512,2048]{1,0:T(8,128)(2,1)}, bf16[512,2048]{1,0:T(8,128)(2,1)S(1)}, u32[]{:S(2)}, u32[]{:S(2)}) collective-permute-start(bf16[512,2048]{1,0:T(8,128)(2,1)} %collective-permute-done.14), channel_id=1, source_target_pairs={{0,1},{1,0},{2,3},{3,2},{4,5},{5,4},{6,7},{7,6},{8,9},{9,8},{10,11... | collective-permute-start | bytes 6291464 | tf_op jit(solution)/shard_map/ppermute | solution.py:73
  271.5 37.9 %collective-permute-start.7 = (bf16[2,1,2,128,2,256]{5,3,4,2,1,0:T(8,128)(2,1)S(1)}, bf16[2,1,2,128,2,256]{5,3,4,2,1,0:T(8,128)(2,1)S(1)}, u32[]{:S(2)}, u32[]{:S(2)}) collective-permute-start(bf16[2,1,2,128,2,256]{5,3,4,2,1,0:T(8,128)(2,1)S(1)} %maximum_bitcast_fusion), channel_id=1, source_target_pairs={{0,16},{16,0},{1,17},{17,1},{2,18},{18,2},{3,19},{19,3},{4,20},{20... | collective-permute-start | bytes 1572872 | tf_op jit(solution)/shard_map/ppermute | solution.py:73
  273.9 103.8 %collective-permute-start.12 = (bf16[512,2560]{1,0:T(8,128)(2,1)}, bf16[512,2560]{1,0:T(8,128)(2,1)}, u32[]{:S(2)}, u32[]{:S(2)}) collective-permute-start(bf16[512,2560]{1,0:T(8,128)(2,1)} %pad_maximum_fusion.2), channel_id=1, source_target_pairs={{0,4},{4,0},{1,5},{5,1},{2,6},{6,2},{3,7},{7,3},{8,12},{12,8},{9,1... | collective-permute-start | bytes 7864328 | tf_op jit(solution)/shard_map/ppermute | solution.py:73
  309.5 34.7 %collective-permute-start.8 = (bf16[1,2,2,128,2,256]{5,3,4,2,1,0:T(8,128)(2,1)S(1)}, bf16[1,2,2,128,2,256]{5,3,4,2,1,0:T(8,128)(2,1)S(1)}, u32[]{:S(2)}, u32[]{:S(2)}) collective-permute-start(bf16[1,2,2,128,2,256]{5,3,4,2,1,0:T(8,128)(2,1)S(1)} %get-tuple-element.453), channel_id=1, source_target_pairs={{0,4},{4,0},{1,5},{5,1},{2,6},{6,2},{3,7},{7,3},{8,12},{12,8},{9,1... | collective-permute-start | bytes 1572872 | tf_op jit(solution)/shard_map/ppermute | solution.py:73
  312.3 86.0 %collective-permute-start.17 = (bf16[512,2560]{1,0:T(8,128)(2,1)}, bf16[512,2560]{1,0:T(8,128)(2,1)}, u32[]{:S(2)}, u32[]{:S(2)}) collective-permute-start(bf16[512,2560]{1,0:T(8,128)(2,1)} %pad_maximum_fusion.2), channel_id=1, source_target_pairs={{0,1},{1,0},{2,3},{3,2},{4,5},{5,4},{6,7},{7,6},{8,9},{9,8},{10,11... | collective-permute-start | bytes 7864328 | tf_op jit(solution)/shard_map/ppermute | solution.py:73
  312.4 36.0 %collective-permute-start.10 = (bf16[1,2,2,128,2,256]{5,3,4,2,1,0:T(8,128)(2,1)S(1)}, bf16[1,2,2,128,2,256]{5,3,4,2,1,0:T(8,128)(2,1)S(1)}, u32[]{:S(2)}, u32[]{:S(2)}) collective-permute-start(bf16[1,2,2,128,2,256]{5,3,4,2,1,0:T(8,128)(2,1)S(1)} %get-tuple-element.452), channel_id=1, source_target_pairs={{0,8},{8,0},{1,9},{9,1},{2,10},{10,2},{3,11},{11,3},{4,12},{12,4},... | collective-permute-start | bytes 1572872 | tf_op jit(solution)/shard_map/ppermute | solution.py:73
  345.7 25.5 %collective-permute-start.9 = (bf16[2,2,2,128,2,256]{5,3,4,2,1,0:T(8,128)(2,1)}, bf16[2,2,2,128,2,256]{5,3,4,2,1,0:T(8,128)(2,1)}, u32[]{:S(2)}, u32[]{:S(2)}) collective-permute-start(bf16[2,2,2,128,2,256]{5,3,4,2,1,0:T(8,128)(2,1)} %get-tuple-element.455), channel_id=1, source_target_pairs={{0,8},{8,0},{1,9},{9,1},{2,10},{10,2},{3,11},{11,3},{4,12},{12,4},... | collective-permute-start | bytes 3145736 | tf_op jit(solution)/shard_map/ppermute | solution.py:73
  417.4 25.4 %collective-permute-start.19 = (bf16[256,2048]{1,0:T(8,128)(2,1)}, bf16[256,2048]{1,0:T(8,128)(2,1)S(1)}, u32[]{:S(2)}, u32[]{:S(2)}) collective-permute-start(bf16[256,2048]{1,0:T(8,128)(2,1)} %multiply_convert_fusion.8), channel_id=1, source_target_pairs={{0,4},{4,0},{1,5},{5,1},{2,6},{6,2},{3,7},{7,3},{8,12},{12,8},{9,1... | collective-permute-start | bytes 3145736 | tf_op jit(solution)/shard_map/ppermute | solution.py:73
  418.1 25.0 %collective-permute-start.20 = (bf16[256,2048]{1,0:T(8,128)(2,1)}, bf16[256,2048]{1,0:T(8,128)(2,1)S(1)}, u32[]{:S(2)}, u32[]{:S(2)}) collective-permute-start(bf16[256,2048]{1,0:T(8,128)(2,1)} %multiply_convert_fusion.8), channel_id=1, source_target_pairs={{0,8},{8,0},{1,9},{9,1},{2,10},{10,2},{3,11},{11,3},{4,12},{12,4},... | collective-permute-start | bytes 3145736 | tf_op jit(solution)/shard_map/ppermute | solution.py:73
  447.2 27.6 %collective-permute-start.23 = (bf16[256,2048]{1,0:T(8,128)(2,1)S(1)}, bf16[256,2048]{1,0:T(8,128)(2,1)S(1)}, u32[]{:S(2)}, u32[]{:S(2)}) collective-permute-start(bf16[256,2048]{1,0:T(8,128)(2,1)S(1)} %collective-permute-done.20), channel_id=1, source_target_pairs={{0,1},{1,0},{2,3},{3,2},{4,5},{5,4},{6,7},{7,6},{8,9},{9,8},{10,11... | collective-permute-start | bytes 3145736 | tf_op jit(solution)/shard_map/ppermute | solution.py:73
  447.9 80.9 %collective-permute-start.22 = (bf16[256,2048]{1,0:T(8,128)(2,1)S(1)}, bf16[256,2048]{1,0:T(8,128)(2,1)S(1)}, u32[]{:S(2)}, u32[]{:S(2)}) collective-permute-start(bf16[256,2048]{1,0:T(8,128)(2,1)S(1)} %slice.557), channel_id=1, source_target_pairs={{0,1},{1,0},{2,3},{3,2},{4,5},{5,4},{6,7},{7,6},{8,9},{9,8},{10,11... | collective-permute-start | bytes 3145736 | tf_op jit(solution)/shard_map/ppermute | solution.py:73
  457.5 29.1 %collective-permute-start.27 = (bf16[256,2048]{1,0:T(8,128)(2,1)S(1)}, bf16[256,2048]{1,0:T(8,128)(2,1)S(1)}, u32[]{:S(2)}, u32[]{:S(2)}) collective-permute-start(bf16[256,2048]{1,0:T(8,128)(2,1)S(1)} %pad_maximum_fusion.18), channel_id=1, source_target_pairs={{0,1},{1,0},{2,3},{3,2},{4,5},{5,4},{6,7},{7,6},{8,9},{9,8},{10,11... | collective-permute-start | bytes 3145736 | tf_op jit(solution)/shard_map/ppermute | solution.py:73
  474.3 34.5 %collective-permute-start.32 = (bf16[256,2048]{1,0:T(8,128)(2,1)S(1)}, bf16[256,2048]{1,0:T(8,128)(2,1)S(1)}, u32[]{:S(2)}, u32[]{:S(2)}) collective-permute-start(bf16[256,2048]{1,0:T(8,128)(2,1)S(1)} %slice.717), channel_id=1, source_target_pairs={{0,1},{1,0},{2,3},{3,2},{4,5},{5,4},{6,7},{7,6},{8,9},{9,8},{10,11... | collective-permute-start | bytes 3145736 | tf_op jit(solution)/shard_map/ppermute | solution.py:73
  526.0 24.7 %collective-permute-start.30 = (bf16[256,2048]{1,0:T(8,128)(2,1)S(1)}, bf16[256,2048]{1,0:T(8,128)(2,1)S(1)}, u32[]{:S(2)}, u32[]{:S(2)}) collective-permute-start(bf16[256,2048]{1,0:T(8,128)(2,1)S(1)} %pad_maximum_fusion.19), channel_id=1, source_target_pairs={{0,8},{8,0},{1,9},{9,1},{2,10},{10,2},{3,11},{11,3},{4,12},{12,4},... | collective-permute-start | bytes 3145736 | tf_op jit(solution)/shard_map/ppermute | solution.py:73
  565.0 25.6 %collective-permute-start.36 = (bf16[256,2048]{1,0:T(8,128)(2,1)S(1)}, bf16[256,2048]{1,0:T(8,128)(2,1)S(1)}, u32[]{:S(2)}, u32[]{:S(2)}) collective-permute-start(bf16[256,2048]{1,0:T(8,128)(2,1)S(1)} %fusion.111), channel_id=1, source_target_pairs={{0,4},{4,0},{1,5},{5,1},{2,6},{6,2},{3,7},{7,3},{8,12},{12,8},{9,1... | collective-permute-start | bytes 3145736 | tf_op jit(solution)/shard_map/ppermute | solution.py:73
  566.5 25.3 %collective-permute-start.37 = (bf16[256,2048]{1,0:T(8,128)(2,1)S(1)}, bf16[256,2048]{1,0:T(8,128)(2,1)S(1)}, u32[]{:S(2)}, u32[]{:S(2)}) collective-permute-start(bf16[256,2048]{1,0:T(8,128)(2,1)S(1)} %fusion.111), channel_id=1, source_target_pairs={{0,8},{8,0},{1,9},{9,1},{2,10},{10,2},{3,11},{11,3},{4,12},{12,4},... | collective-permute-start | bytes 3145736 | tf_op jit(solution)/shard_map/ppermute | solution.py:73
  593.2 35.9 %collective-permute-start.39 = (bf16[256,2048]{1,0:T(8,128)(2,1)S(1)}, bf16[256,2048]{1,0:T(8,128)(2,1)S(1)}, u32[]{:S(2)}, u32[]{:S(2)}) collective-permute-start(bf16[256,2048]{1,0:T(8,128)(2,1)S(1)} %collective-permute-done.37), channel_id=1, source_target_pairs={{0,1},{1,0},{2,3},{3,2},{4,5},{5,4},{6,7},{7,6},{8,9},{9,8},{10,11... | collective-permute-start | bytes 3145736 | tf_op jit(solution)/shard_map/ppermute | solution.py:73
  593.4 57.8 %collective-permute-start.43 = (bf16[256,2048]{1,0:T(8,128)(2,1)S(1)}, bf16[256,2048]{1,0:T(8,128)(2,1)S(1)}, u32[]{:S(2)}, u32[]{:S(2)}) collective-permute-start(bf16[256,2048]{1,0:T(8,128)(2,1)S(1)} %slice.581), channel_id=1, source_target_pairs={{0,1},{1,0},{2,3},{3,2},{4,5},{5,4},{6,7},{7,6},{8,9},{9,8},{10,11... | collective-permute-start | bytes 3145736 | tf_op jit(solution)/shard_map/ppermute | solution.py:73
  606.7 44.9 %collective-permute-start.42 = (bf16[256,2048]{1,0:T(8,128)(2,1)S(1)}, bf16[256,2048]{1,0:T(8,128)(2,1)S(1)}, u32[]{:S(2)}, u32[]{:S(2)}) collective-permute-start(bf16[256,2048]{1,0:T(8,128)(2,1)S(1)} %pad_maximum_fusion.21), channel_id=1, source_target_pairs={{0,1},{1,0},{2,3},{3,2},{4,5},{5,4},{6,7},{7,6},{8,9},{9,8},{10,11... | collective-permute-start | bytes 3145736 | tf_op jit(solution)/shard_map/ppermute | solution.py:73
  629.0 42.2 %collective-permute-start.44 = (bf16[256,2048]{1,0:T(8,128)(2,1)S(1)}, bf16[256,2048]{1,0:T(8,128)(2,1)S(1)}, u32[]{:S(2)}, u32[]{:S(2)}) collective-permute-start(bf16[256,2048]{1,0:T(8,128)(2,1)S(1)} %slice.726), channel_id=1, source_target_pairs={{0,1},{1,0},{2,3},{3,2},{4,5},{5,4},{6,7},{7,6},{8,9},{9,8},{10,11... | collective-permute-start | bytes 3145736 | tf_op jit(solution)/shard_map/ppermute | solution.py:73
  676.1 35.9 %collective-permute-start.49 = (bf16[128,2048]{1,0:T(8,128)(2,1)}, bf16[128,2048]{1,0:T(8,128)(2,1)}, u32[]{:S(2)}, u32[]{:S(2)}) collective-permute-start(bf16[128,2048]{1,0:T(8,128)(2,1)} %get-tuple-element.447), channel_id=1, source_target_pairs={{0,8},{8,0},{1,9},{9,1},{2,10},{10,2},{3,11},{11,3},{4,12},{12,4},... | collective-permute-start | bytes 1572872 | tf_op jit(solution)/shard_map/ppermute | solution.py:73
  677.8 37.8 %collective-permute-start.47 = (bf16[128,2048]{1,0:T(8,128)(2,1)}, bf16[128,2048]{1,0:T(8,128)(2,1)}, u32[]{:S(2)}, u32[]{:S(2)}) collective-permute-start(bf16[128,2048]{1,0:T(8,128)(2,1)} %get-tuple-element.446), channel_id=1, source_target_pairs={{0,4},{4,0},{1,5},{5,1},{2,6},{6,2},{3,7},{7,3},{8,12},{12,8},{9,1... | collective-permute-start | bytes 1572872 | tf_op jit(solution)/shard_map/ppermute | solution.py:73
  714.2 37.0 %collective-permute-start.50 = (bf16[256,2048]{1,0:T(8,128)(2,1)}, bf16[256,2048]{1,0:T(8,128)(2,1)}, u32[]{:S(2)}, u32[]{:S(2)}) collective-permute-start(bf16[256,2048]{1,0:T(8,128)(2,1)} %pad_maximum_fusion.23), channel_id=1, source_target_pairs={{0,4},{4,0},{1,5},{5,1},{2,6},{6,2},{3,7},{7,3},{8,12},{12,8},{9,1... | collective-permute-start | bytes 3145736 | tf_op jit(solution)/shard_map/ppermute | solution.py:73
  717.9 33.3 %collective-permute-start.48 = (bf16[256,2048]{1,0:T(8,128)(2,1)}, bf16[256,2048]{1,0:T(8,128)(2,1)S(1)}, u32[]{:S(2)}, u32[]{:S(2)}) collective-permute-start(bf16[256,2048]{1,0:T(8,128)(2,1)} %pad_maximum_fusion.22), channel_id=1, source_target_pairs={{0,8},{8,0},{1,9},{9,1},{2,10},{10,2},{3,11},{11,3},{4,12},{12,4},... | collective-permute-start | bytes 3145736 | tf_op jit(solution)/shard_map/ppermute | solution.py:73
  798.7 48.3 %collective-permute-start.52 = (bf16[512,2048]{1,0:T(8,128)(2,1)S(1)}, bf16[512,2048]{1,0:T(8,128)(2,1)S(1)}, u32[]{:S(2)}, u32[]{:S(2)}) collective-permute-start(bf16[512,2048]{1,0:T(8,128)(2,1)S(1)} %slice.601), channel_id=1, source_target_pairs={{0,4},{4,0},{1,5},{5,1},{2,6},{6,2},{3,7},{7,3},{8,12},{12,8},{9,1... | collective-permute-start | bytes 6291464 | tf_op jit(solution)/shard_map/ppermute | solution.py:73
  857.8 39.7 %collective-permute-start.55 = (bf16[2,2,2,128,2,256]{5,3,4,2,1,0:T(8,128)(2,1)}, bf16[2,2,2,128,2,256]{5,3,4,2,1,0:T(8,128)(2,1)}, u32[]{:S(2)}, u32[]{:S(2)}) collective-permute-start(bf16[2,2,2,128,2,256]{5,3,4,2,1,0:T(8,128)(2,1)} %slice_bitcast_fusion), channel_id=1, source_target_pairs={{0,4},{4,0},{1,5},{5,1},{2,6},{6,2},{3,7},{7,3},{8,12},{12,8},{9,1... | collective-permute-start | bytes 3145736 | tf_op jit(solution)/shard_map/ppermute | solution.py:73
  878.4 73.1 %collective-permute-start.58 = (bf16[1024,2048]{1,0:T(8,128)(2,1)S(1)}, bf16[1024,2048]{1,0:T(8,128)(2,1)S(1)}, u32[]{:S(2)}, u32[]{:S(2)}) collective-permute-start(bf16[1024,2048]{1,0:T(8,128)(2,1)S(1)} %convolution_convert_fusion.2), channel_id=1, source_target_pairs={{0,1},{1,0},{2,3},{3,2},{4,5},{5,4},{6,7},{7,6},{8,9},{9,8},{10,11... | collective-permute-start | bytes 12582920 | tf_op jit(solution)/shard_map/ppermute | solution.py:73
  885.7 50.3 %collective-permute-start.53 = (bf16[2,2,2,128,2,256]{5,3,4,2,1,0:T(8,128)(2,1)S(1)}, bf16[2,2,2,128,2,256]{5,3,4,2,1,0:T(8,128)(2,1)S(1)}, u32[]{:S(2)}, u32[]{:S(2)}) collective-permute-start(bf16[2,2,2,128,2,256]{5,3,4,2,1,0:T(8,128)(2,1)S(1)} %bitcast.399), channel_id=1, source_target_pairs={{0,8},{8,0},{1,9},{9,1},{2,10},{10,2},{3,11},{11,3},{4,12},{12,4},... | collective-permute-start | bytes 3145736 | tf_op jit(solution)/shard_map/ppermute | solution.py:73
  887.5 50.4 %collective-permute-start.60 = (bf16[1024,512]{1,0:T(8,128)(2,1)S(1)}, bf16[1024,512]{1,0:T(8,128)(2,1)S(1)}, u32[]{:S(2)}, u32[]{:S(2)}) collective-permute-start(bf16[1024,512]{1,0:T(8,128)(2,1)S(1)} %pad_maximum_fusion.24), channel_id=1, source_target_pairs={{0,1},{1,0},{2,3},{3,2},{4,5},{5,4},{6,7},{7,6},{8,9},{9,8},{10,11... | collective-permute-start | bytes 3145736 | tf_op jit(solution)/shard_map/ppermute | solution.py:73
  900.0 48.7 %collective-permute-start.56 = (bf16[2,2,128,2,256]{4,2,3,1,0:T(8,128)(2,1)S(1)}, bf16[2,2,128,2,256]{4,2,3,1,0:T(8,128)(2,1)S(1)}, u32[]{:S(2)}, u32[]{:S(2)}) collective-permute-start(bf16[2,2,128,2,256]{4,2,3,1,0:T(8,128)(2,1)S(1)} %slice_bitcast_fusion.4), channel_id=1, source_target_pairs={{0,8},{8,0},{1,9},{9,1},{2,10},{10,2},{3,11},{11,3},{4,12},{12,4},... | collective-permute-start | bytes 1572872 | tf_op jit(solution)/shard_map/ppermute | solution.py:73
  951.4 40.0 %collective-permute-start.57 = (bf16[2,2,128,2,256]{4,2,3,1,0:T(8,128)(2,1)S(1)}, bf16[2,2,128,2,256]{4,2,3,1,0:T(8,128)(2,1)S(1)}, u32[]{:S(2)}, u32[]{:S(2)}) collective-permute-start(bf16[2,2,128,2,256]{4,2,3,1,0:T(8,128)(2,1)S(1)} %fusion.251), channel_id=1, source_target_pairs={{0,16},{16,0},{1,17},{17,1},{2,18},{18,2},{3,19},{19,3},{4,20},{20... | collective-permute-start | bytes 1572872 | tf_op jit(solution)/shard_map/ppermute | solution.py:73
  953.1 53.3 %collective-permute-start.59 = (bf16[512,2048]{1,0:T(8,128)(2,1)S(1)}, bf16[512,2048]{1,0:T(8,128)(2,1)S(1)}, u32[]{:S(2)}, u32[]{:S(2)}) collective-permute-start(bf16[512,2048]{1,0:T(8,128)(2,1)S(1)} %slice.752), channel_id=1, source_target_pairs={{0,4},{4,0},{1,5},{5,1},{2,6},{6,2},{3,7},{7,3},{8,12},{12,8},{9,1... | collective-permute-start | bytes 6291464 | tf_op jit(solution)/shard_map/ppermute | solution.py:73
  1026.3 36.1 %collective-permute-start.65 = (bf16[256,2048]{1,0:T(8,128)(2,1)S(1)}, bf16[256,2048]{1,0:T(8,128)(2,1)S(1)}, u32[]{:S(2)}, u32[]{:S(2)}) collective-permute-start(bf16[256,2048]{1,0:T(8,128)(2,1)S(1)} %get-tuple-element.436), channel_id=1, source_target_pairs={{0,2},{2,0},{1,3},{3,1},{4,6},{6,4},{5,7},{7,5},{8,10},{10,8},{9,1... | collective-permute-start | bytes 3145736 | tf_op jit(solution)/shard_map/ppermute | solution.py:73
  1031.9 28.2 %collective-permute-start.63 = (bf16[512,1152]{0,1:T(8,128)(2,1)S(1)}, bf16[512,1152]{0,1:T(8,128)(2,1)S(1)}, u32[]{:S(2)}, u32[]{:S(2)}) collective-permute-start(bf16[512,1152]{0,1:T(8,128)(2,1)S(1)} %slice.762), channel_id=1, source_target_pairs={{0,4},{4,0},{1,5},{5,1},{2,6},{6,2},{3,7},{7,3},{8,12},{12,8},{9,1... | collective-permute-start | bytes 3538952 | tf_op jit(solution)/shard_map/ppermute | solution.py:73
  1033.8 46.7 %collective-permute-start.67 = (bf16[256,2560]{1,0:T(8,128)(2,1)S(1)}, bf16[256,2560]{1,0:T(8,128)(2,1)S(1)}, u32[]{:S(2)}, u32[]{:S(2)}) collective-permute-start(bf16[256,2560]{1,0:T(8,128)(2,1)S(1)} %get-tuple-element.430), channel_id=1, source_target_pairs={{0,2},{2,0},{1,3},{3,1},{4,6},{6,4},{5,7},{7,5},{8,10},{10,8},{9,1... | collective-permute-start | bytes 3932168 | tf_op jit(solution)/shard_map/ppermute | solution.py:73
  1061.4 31.5 %collective-permute-start.64 = (bf16[256,1152]{0,1:T(8,128)(2,1)}, bf16[256,1152]{0,1:T(8,128)(2,1)}, u32[]{:S(2)}, u32[]{:S(2)}) collective-permute-start(bf16[256,1152]{0,1:T(8,128)(2,1)} %slice.631), channel_id=1, source_target_pairs={{0,2},{2,0},{1,3},{3,1},{4,6},{6,4},{5,7},{7,5},{8,10},{10,8},{9,1... | collective-permute-start | bytes 1769480 | tf_op jit(solution)/shard_map/ppermute | solution.py:73
  1063.6 27.4 %collective-permute-start.66 = (bf16[128,2048]{1,0:T(8,128)(2,1)}, bf16[128,2048]{1,0:T(8,128)(2,1)}, u32[]{:S(2)}, u32[]{:S(2)}) collective-permute-start(bf16[128,2048]{1,0:T(8,128)(2,1)} %slice.765), channel_id=1, source_target_pairs={{0,8},{8,0},{1,9},{9,1},{2,10},{10,2},{3,11},{11,3},{4,12},{12,4},... | collective-permute-start | bytes 1572872 | tf_op jit(solution)/shard_map/ppermute | solution.py:73
  1086.4 64.4 %all-to-all-start.1 = ((bf16[8,64,3072]{2,1,0:T(8,128)(2,1)}), bf16[8,64,3072]{2,1,0:T(8,128)(2,1)}, u32[]{:S(2)}, u32[]{:S(2)}) async-start(bf16[8,64,3072]{2,1,0:T(8,128)(2,1)} %bitcast.350), calls=%async_computation.2 | async-start | bytes 6291456 | tf_op jit(solution)/shard_map/all_to_all | solution.py:202
  (247 other events, 3889.6 us)
Sparse Core Ops, SparseCore 0:
  72.6 249.1 all-gather.1
  754.3 245.4 reduce-scatter.1

commit v12 on v10

--- a/solution.py
+++ b/solution.py
@@ -572,7 +572,6 @@
         d_keys, d_values, query_sum, output_sum, side_sum, d_spread, feed_sum
     )
     output_sum = jnp.concatenate([output_sum, side_sum], axis=1)
-    grad_gate, grad_up, grad_down = plan.own_rows(jnp.split(feed_sum, 3), local_rows)
     d_kvl_low = jnp.concatenate(
         [
             d_keys.reshape(rows, -1).astype(BF16),
@@ -583,16 +582,19 @@
     )
     laurel_spread = product(d_laurel_low, to_spread).astype(BF16)
     kvl_sum = plan.spread_begin([(normed_spread, d_kvl_low), (laurel_spread, latent_low)])
+    kvl_sum, d_kvl_low = together(kvl_sum, d_kvl_low)
     query_kept, query_away = plan.spread_send(query_sum, steps[1])
     output_kept, output_away = plan.spread_send(output_sum, steps[1])
     kvl_sum = plan.spread_step(kvl_sum, steps[:1])
-    kvl_sum, query_kept, output_kept = together(kvl_sum, query_kept, output_kept)
+    kvl_sum, query_kept, output_kept, feed_sum = together(
+        kvl_sum, query_kept, output_kept, feed_sum
+    )
+    grad_gate, grad_up, grad_down = plan.own_rows(jnp.split(feed_sum, 3), local_rows)
     query_sum = (query_kept + query_away).astype(BF16)
     output_sum = (output_kept + output_away).astype(BF16)
     kvl_sum = plan.spread_step(kvl_sum, steps[1:2])
     query_sum = plan.spread_step(query_sum, steps[2:3])
     output_sum = plan.spread_step(output_sum, steps[2:3])
-    kvl_sum, query_sum, output_sum, d_kvl_low = together(kvl_sum, query_sum, output_sum, d_kvl_low)
     d_spread = d_spread + product_nt_split(d_kvl_low, kvl_full)
     d_normed = d_normed + reorder(d_spread, to_spread)
     d_inputs_norm, grad_norm_input = pre_pull(d_normed)
@@ -611,15 +613,14 @@
     gain_grads = jnp.concatenate(
         [plan.from_far_team(norm_grads).reshape(-1), grad_norm_query, grad_norm_key]
     )
+    gain_grads, query_sum, output_sum, kvl_sum = together(
+        gain_grads, query_sum, output_sum, kvl_sum
+    )
     grad_query = plan.spread_step(query_sum, steps[3:])
     output_sum = plan.spread_step(output_sum, steps[3:])
-    kvl_sum = plan.spread_step(kvl_sum, steps[2:3])
-    gain_grads, grad_query, output_sum, kvl_sum = together(
-        gain_grads, grad_query, output_sum, kvl_sum
-    )
     grad_output, grad_side_gate, grad_side_output = split_columns(output_sum, rest_widths)
     grad_key, grad_value, grad_left, grad_right = split_columns(
-        plan.spread_step(kvl_sum, steps[3:]), kvl_widths
+        plan.spread_step(kvl_sum, steps[2:]), kvl_widths
     )
     gain_grads = plan.total(gain_grads)
     gain_parts = split_columns(gain_grads, [width] * 6 + [head_size] * 2)

time: 1150 us -> 1170 us (1.017)
  waiting for transfers between devices: 512 us -> 530 us
    ppermute x78, waiting for transfers between devices: 511 us -> 529 us  [swap(): return lax.ppermute(value, axis, [(0, 1), (1, 0)])]
    unnamed x460 -> x458, local copies, waits for them, and re-layouts: 50.7 us -> 48.7 us
  transfers between devices with their start and end apart: 82 -> 82, of which waited for: 41 -> 39; matrix products, arithmetic and copies ran while one was open for 40% -> 39% of each run, Pallas kernels for 0% -> 0%
where the time goes in v12:
time: 1170 us; the launch traced here: 1160 us
  waiting for transfers between devices  530 us (45%)
  matrix products  263 us (22%)
  local copies, waits for them, and re-layouts  139 us (12%)
  other arithmetic  134 us (11%)
  starting transfers between devices  81 us (7%)
  between operations  18.3 us (2%)
    ppermute x78, waiting for transfers between devices, swap(): return lax.ppermute(value, axis, [(0, 1), (1, 0)])  529 us
    dot_general x33, matrix products, product(): return jnp.dot(left, right, preferred_element_type=F32)  103 us
    dot_general x31, matrix products, product_nt(): lax.dot_general(left, right, (((1,), (1,)), ((), ())), preferred_element_...  91.8 us
    ppermute x78, starting transfers between devices, swap(): return lax.ppermute(value, axis, [(0, 1), (1, 0)])  70.7 us
    dot_general x15, matrix products, product_tn(): lax.dot_general(left, right, (((0,), (0,)), ((), ())), preferred_element_...  54.3 us
    unnamed x458, local copies, waits for them, and re-layouts  48.7 us
  transfers between devices with their start and end apart: 82, of which 39 were waited for; matrix products, arithmetic and copies ran while one was open for 39% of the time, Pallas kernels for 0%

profile of v12, /device:TPU:0, one launch (start us, length us, event | category | flops | bytes accessed | tf_op | source)
XLA Modules:
  0.0 1164.9 jit_solution(10789432324983437138)
XLA Ops:
  14.4 5.4 all-to-all-start
  24.6 45.8 %collective-permute-done = bf16[64,5760]{1,0:T(8,128)(2,1)} collective-permute-done((bf16[64,5760]{1,0:T(8,128)(2,1)S(1)}, bf16[64,5760]{1,0:T(8,128)(2,1)}, u32[]{:S(2)}, u32[]{:S(2)}) %collective-permute-start) | collective-permute-done | bytes 737312 | tf_op jit(solution)/shard_map/ppermute | solution.py:73
  82.3 55.7 %collective-permute-done.1 = bf16[128,5760]{1,0:T(8,128)(2,1)S(1)} collective-permute-done((bf16[128,5760]{1,0:T(8,128)(2,1)S(1)}, bf16[128,5760]{1,0:T(8,128)(2,1)S(1)}, u32[]{:S(2)}, u32[]{:S(2)}) %collective-permute-start.1) | collective-permute-done | bytes 1474592 | tf_op jit(solution)/shard_map/ppermute | solution.py:73
  140.5 9.0 collective-permute-done.2
  158.7 15.3 %collective-permute-done.3 = bf16[512,1152]{1,0:T(8,128)(2,1)} collective-permute-done((bf16[512,1152]{1,0:T(8,128)(2,1)}, bf16[512,1152]{1,0:T(8,128)(2,1)}, u32[]{:S(2)}, u32[]{:S(2)}) %collective-permute-start.3) | collective-permute-done | bytes 1179680 | tf_op jit(solution)/shard_map/ppermute | solution.py:73
  177.3 5.2 fusion.76
  185.4 7.9 collective-permute-done.13
  208.0 6.0 rev.69
  246.4 26.3 %collective-permute-done.6 = bf16[256,2560]{1,0:T(8,128)(2,1)} collective-permute-done((bf16[256,2560]{1,0:T(8,128)(2,1)}, bf16[256,2560]{1,0:T(8,128)(2,1)}, u32[]{:S(2)}, u32[]{:S(2)}) %collective-permute-start.6) | collective-permute-done | bytes 1310752 | tf_op jit(solution)/shard_map/ppermute | solution.py:73
  281.2 32.3 %collective-permute-done.7 = bf16[2,1,2,128,2,256]{5,3,4,2,1,0:T(8,128)(2,1)S(1)} collective-permute-done((bf16[2,1,2,128,2,256]{5,3,4,2,1,0:T(8,128)(2,1)S(1)}, bf16[2,1,2,128,2,256]{5,3,4,2,1,0:T(8,128)(2,1)S(1)}, u32[]{:S(2)}, u32[]{:S(2)}) %collective-permute-start.7) | collective-permute-done | bytes 524320 | tf_op jit(solution)/shard_map/ppermute | solution.py:73
  318.9 29.5 %collective-permute-done.8 = bf16[1,2,2,128,2,256]{5,3,4,2,1,0:T(8,128)(2,1)S(1)} collective-permute-done((bf16[1,2,2,128,2,256]{5,3,4,2,1,0:T(8,128)(2,1)S(1)}, bf16[1,2,2,128,2,256]{5,3,4,2,1,0:T(8,128)(2,1)S(1)}, u32[]{:S(2)}, u32[]{:S(2)}) %collective-permute-start.8) | collective-permute-done | bytes 524320 | tf_op jit(solution)/shard_map/ppermute | solution.py:73
  359.5 15.9 %collective-permute-done.9 = bf16[2,2,2,128,2,256]{5,3,4,2,1,0:T(8,128)(2,1)} collective-permute-done((bf16[2,2,2,128,2,256]{5,3,4,2,1,0:T(8,128)(2,1)}, bf16[2,2,2,128,2,256]{5,3,4,2,1,0:T(8,128)(2,1)}, u32[]{:S(2)}, u32[]{:S(2)}) %collective-permute-start.9) | collective-permute-done | bytes 1048608 | tf_op jit(solution)/shard_map/ppermute | solution.py:73
  405.2 4.7 fusion.5
  423.3 5.8 fusion.298
  433.0 6.2 multiply_convert_fusion.7
  451.5 7.9 collective-permute-done.25
  496.7 12.0 %collective-permute-done.33 = bf16[128,2048]{1,0:T(8,128)(2,1)S(1)} collective-permute-done((bf16[128,2048]{1,0:T(8,128)(2,1)S(1)}, bf16[128,2048]{1,0:T(8,128)(2,1)S(1)}, u32[]{:S(2)}, u32[]{:S(2)}) %collective-permute-start.33) | collective-permute-done | bytes 524320 | tf_op jit(solution)/shard_map/ppermute | solution.py:73
  513.5 20.2 %collective-permute-done.34 = bf16[256,2048]{1,0:T(8,128)(2,1)S(1)} collective-permute-done((bf16[256,2048]{1,0:T(8,128)(2,1)S(1)}, bf16[256,2048]{1,0:T(8,128)(2,1)S(1)}, u32[]{:S(2)}, u32[]{:S(2)}) %collective-permute-start.34) | collective-permute-done | bytes 1048608 | tf_op jit(solution)/shard_map/ppermute | solution.py:73
  552.7 4.7 multiply_convert_fusion.3
  566.4 10.0 collective-permute-done.36
  582.2 9.1 collective-permute-done.40
  595.2 5.2 multiply_convert_fusion.2
  604.9 5.0 add_convert_fusion.7
  612.5 5.4 multiply_convert_fusion.1
  648.0 10.9 fusion.58
  658.9 11.8 %fusion.61 = bf16[2048,1024]{1,0:T(8,128)(2,1)} fusion(bf16[2048,2048]{1,0:T(8,128)(2,1)S(1)} %constant_dynamic-update-slice_fusion.22, bf16[512,1024]{1,0:T(8,128)(2,1)} %copy-done.186, bf16[512,1024]{1,0:T(8,128)(2,1)S(1)} %copy-done.185, bf16[512,1024]{1,0:T(8,128)(2,1)S(1)} %copy-done.183, bf16[512,1024]{1,0:T(8,128)(2,1)S(1)} %copy-done.181), kind=kOutput, calls=%fused_computation.76 | convolution fusion | flops 8608808960 | bytes 16777216 | tf_op jit(solution)/shard_map/dot_general | solution.py:34
  675.1 13.9 %fusion.64 = bf16[2048,1024]{1,0:T(8,128)(2,1)} fusion(bf16[512,1024]{1,0:T(8,128)(2,1)} %copy-done.200, bf16[512,1024]{1,0:T(8,128)(2,1)} %get-tuple-element.136, bf16[512,1024]{1,0:T(8,128)(2,1)} %copy-done.198, bf16[512,1024]{1,0:T(8,128)(2,1)} %copy-done.197, bf16[512,2048]{1,0:T(8,128)(2,1)} %copy-done.98, bf16[512,2048]{1,0:T(8,128)(2,1)} %copy-done.87, ...), kind=kOutput, calls=%fused_computation.77 | convolution fusion | flops 8642363392 | bytes 16777216 | tf_op jit(solution)/shard_map/dot_general | solution.py:34
  689.0 9.1 pad_maximum_fusion
  707.0 4.8 multiply_reduce_fusion.4
  723.8 5.0 fusion.75
  736.3 5.4 add_convert_fusion.1
  755.9 4.7 fusion.19
  771.6 31.7 %collective-permute-done.52 = bf16[512,2048]{1,0:T(8,128)(2,1)S(1)} collective-permute-done((bf16[512,2048]{1,0:T(8,128)(2,1)S(1)}, bf16[512,2048]{1,0:T(8,128)(2,1)S(1)}, u32[]{:S(2)}, u32[]{:S(2)}) %collective-permute-start.52) | collective-permute-done | bytes 2097184 | tf_op jit(solution)/shard_map/ppermute | solution.py:73
  836.1 5.2 fusion.69
  858.0 25.9 %collective-permute-done.53 = bf16[2,2,2,128,2,256]{5,3,4,2,1,0:T(8,128)(2,1)S(1)} collective-permute-done((bf16[2,2,2,128,2,256]{5,3,4,2,1,0:T(8,128)(2,1)S(1)}, bf16[2,2,2,128,2,256]{5,3,4,2,1,0:T(8,128)(2,1)S(1)}, u32[]{:S(2)}, u32[]{:S(2)}) %collective-permute-start.53) | collective-permute-done | bytes 1048608 | tf_op jit(solution)/shard_map/ppermute | solution.py:73
  886.7 19.2 %collective-permute-done.56 = bf16[2,2,128,2,256]{4,2,3,1,0:T(8,128)(2,1)S(1)} collective-permute-done((bf16[2,2,128,2,256]{4,2,3,1,0:T(8,128)(2,1)S(1)}, bf16[2,2,128,2,256]{4,2,3,1,0:T(8,128)(2,1)S(1)}, u32[]{:S(2)}, u32[]{:S(2)}) %collective-permute-start.56) | collective-permute-done | bytes 524320 | tf_op jit(solution)/shard_map/ppermute | solution.py:73
  911.5 34.1 %collective-permute-done.57 = bf16[2,2,128,2,256]{4,2,3,1,0:T(8,128)(2,1)S(1)} collective-permute-done((bf16[2,2,128,2,256]{4,2,3,1,0:T(8,128)(2,1)S(1)}, bf16[2,2,128,2,256]{4,2,3,1,0:T(8,128)(2,1)S(1)}, u32[]{:S(2)}, u32[]{:S(2)}) %collective-permute-start.57) | collective-permute-done | bytes 524320 | tf_op jit(solution)/shard_map/ppermute | solution.py:73
  948.1 7.6 collective-permute-done.59
  988.1 4.7 fusion.1
  995.3 19.5 %collective-permute-done.63 = bf16[512,1152]{0,1:T(8,128)(2,1)} collective-permute-done((bf16[512,1152]{0,1:T(8,128)(2,1)}, bf16[512,1152]{0,1:T(8,128)(2,1)}, u32[]{:S(2)}, u32[]{:S(2)}) %collective-permute-start.63) | collective-permute-done | bytes 1179680 | tf_op jit(solution)/shard_map/ppermute | solution.py:73
  1028.2 5.3 collective-permute-done.65
  1034.4 6.5 collective-permute-done.68
  1048.4 4.7 all-to-all-start.1
  1059.6 31.4 %collective-permute-done.75 = f32[12800]{0:T(1024)S(1)} collective-permute-done((f32[12800]{0:T(1024)S(1)}, f32[12800]{0:T(1024)S(1)}, u32[]{:S(2)}, u32[]{:S(2)}) %collective-permute-start.75) | collective-permute-done | bytes 51232 | tf_op jit(solution)/shard_map/ppermute | solution.py:73
  1092.6 4.7 fusion.7
  1106.1 10.4 collective-permute-done.69
  1118.6 17.0 %collective-permute-done.72 = bf16[64,2560]{1,0:T(8,128)(2,1)S(1)} collective-permute-done((bf16[64,2560]{1,0:T(8,128)(2,1)S(1)}, bf16[64,2560]{1,0:T(8,128)(2,1)S(1)}, u32[]{:S(2)}, u32[]{:S(2)}) %collective-permute-start.72) | collective-permute-done | bytes 327712 | tf_op jit(solution)/shard_map/ppermute | solution.py:73
  1137.2 4.7 collective-permute-done.71
  (956 shorter events, 498.0 us)
Async XLA Ops:
  14.4 58.2 %all-to-all-start = ((bf16[8,192,1024]{2,1,0:T(8,128)(2,1)}), bf16[8,192,1024]{2,1,0:T(8,128)(2,1)}, u32[]{:S(2)}, u32[]{:S(2)}) async-start(bf16[8,192,1024]{2,1,0:T(8,128)(2,1)} %copy.514), calls=%async_computation | async-start | bytes 6291456 | tf_op jit(solution)/shard_map/all_to_all | solution.py:326
  19.8 374.9 %all-gather.2.cloned.1.call-start = ((), (), s32[]{:S(2)}) async-start(), calls=%async_computation.3 | async-start | bytes 15728640 | tf_op jit(solution)/shard_map/all_gather | solution.py:336
  20.2 50.3 %collective-permute-start = (bf16[64,5760]{1,0:T(8,128)(2,1)S(1)}, bf16[64,5760]{1,0:T(8,128)(2,1)}, u32[]{:S(2)}, u32[]{:S(2)}) collective-permute-start(bf16[64,5760]{1,0:T(8,128)(2,1)S(1)} %concatenate.177), channel_id=1, source_target_pairs={{0,16},{16,0},{1,17},{17,1},{2,18},{18,2},{3,19},{19,3},{4,20},{20... | collective-permute-start | bytes 2211848 | tf_op jit(solution)/shard_map/ppermute | solution.py:73
  76.7 881.1 %reduce-scatter.2.cloned.1.call-start = ((), (), s32[]{:S(2)}) async-start(), calls=%async_computation.4 | async-start | bytes 15728640 | tf_op jit(solution)/shard_map/reduce_scatter | solution.py:507
  77.6 60.3 %collective-permute-start.1 = (bf16[128,5760]{1,0:T(8,128)(2,1)S(1)}, bf16[128,5760]{1,0:T(8,128)(2,1)S(1)}, u32[]{:S(2)}, u32[]{:S(2)}) collective-permute-start(bf16[128,5760]{1,0:T(8,128)(2,1)S(1)} %pad_maximum_fusion.14), channel_id=1, source_target_pairs={{0,8},{8,0},{1,9},{9,1},{2,10},{10,2},{3,11},{11,3},{4,12},{12,4},... | collective-permute-start | bytes 4423688 | tf_op jit(solution)/shard_map/ppermute | solution.py:73
  157.1 36.1 %collective-permute-start.13 = (bf16[256,2048]{1,0:T(8,128)(2,1)S(1)}, bf16[256,2048]{1,0:T(8,128)(2,1)}, u32[]{:S(2)}, u32[]{:S(2)}) collective-permute-start(bf16[256,2048]{1,0:T(8,128)(2,1)S(1)} %slice.701), channel_id=1, source_target_pairs={{0,2},{2,0},{1,3},{3,1},{4,6},{6,4},{5,7},{7,5},{8,10},{10,8},{9,1... | collective-permute-start | bytes 3145736 | tf_op jit(solution)/shard_map/ppermute | solution.py:73
  158.7 37.2 %collective-permute-start.4 = (bf16[512,1152]{1,0:T(8,128)(2,1)}, bf16[512,1152]{1,0:T(8,128)(2,1)}, u32[]{:S(2)}, u32[]{:S(2)}) collective-permute-start(bf16[512,1152]{1,0:T(8,128)(2,1)} %pad_maximum_fusion.15), channel_id=1, source_target_pairs={{0,1},{1,0},{2,3},{3,2},{4,5},{5,4},{6,7},{7,6},{8,9},{9,8},{10,11... | collective-permute-start | bytes 3538952 | tf_op jit(solution)/shard_map/ppermute | solution.py:73
  196.0 83.0 %collective-permute-start.15 = (bf16[512,2048]{1,0:T(8,128)(2,1)}, bf16[512,2048]{1,0:T(8,128)(2,1)}, u32[]{:S(2)}, u32[]{:S(2)}) collective-permute-start(bf16[512,2048]{1,0:T(8,128)(2,1)} %pad_maximum_fusion.7), channel_id=1, source_target_pairs={{0,1},{1,0},{2,3},{3,2},{4,5},{5,4},{6,7},{7,6},{8,9},{9,8},{10,11... | collective-permute-start | bytes 6291464 | tf_op jit(solution)/shard_map/ppermute | solution.py:73
  196.0 50.0 %collective-permute-start.14 = (bf16[512,2048]{1,0:T(8,128)(2,1)}, bf16[512,2048]{1,0:T(8,128)(2,1)}, u32[]{:S(2)}, u32[]{:S(2)}) collective-permute-start(bf16[512,2048]{1,0:T(8,128)(2,1)} %pad_maximum_fusion.7), channel_id=1, source_target_pairs={{0,4},{4,0},{1,5},{5,1},{2,6},{6,2},{3,7},{7,3},{8,12},{12,8},{9,1... | collective-permute-start | bytes 6291464 | tf_op jit(solution)/shard_map/ppermute | solution.py:73
  232.9 39.8 %collective-permute-start.6 = (bf16[256,2560]{1,0:T(8,128)(2,1)}, bf16[256,2560]{1,0:T(8,128)(2,1)}, u32[]{:S(2)}, u32[]{:S(2)}) collective-permute-start(bf16[256,2560]{1,0:T(8,128)(2,1)} %slice.691), channel_id=1, source_target_pairs={{0,2},{2,0},{1,3},{3,1},{4,6},{6,4},{5,7},{7,5},{8,10},{10,8},{9,1... | collective-permute-start | bytes 3932168 | tf_op jit(solution)/shard_map/ppermute | solution.py:73
  245.9 70.7 %collective-permute-start.16 = (bf16[512,2048]{1,0:T(8,128)(2,1)}, bf16[512,2048]{1,0:T(8,128)(2,1)S(1)}, u32[]{:S(2)}, u32[]{:S(2)}) collective-permute-start(bf16[512,2048]{1,0:T(8,128)(2,1)} %collective-permute-done.14), channel_id=1, source_target_pairs={{0,1},{1,0},{2,3},{3,2},{4,5},{5,4},{6,7},{7,6},{8,9},{9,8},{10,11... | collective-permute-start | bytes 6291464 | tf_op jit(solution)/shard_map/ppermute | solution.py:73
  275.7 37.9 %collective-permute-start.7 = (bf16[2,1,2,128,2,256]{5,3,4,2,1,0:T(8,128)(2,1)S(1)}, bf16[2,1,2,128,2,256]{5,3,4,2,1,0:T(8,128)(2,1)S(1)}, u32[]{:S(2)}, u32[]{:S(2)}) collective-permute-start(bf16[2,1,2,128,2,256]{5,3,4,2,1,0:T(8,128)(2,1)S(1)} %maximum_bitcast_fusion), channel_id=1, source_target_pairs={{0,16},{16,0},{1,17},{17,1},{2,18},{18,2},{3,19},{19,3},{4,20},{20... | collective-permute-start | bytes 1572872 | tf_op jit(solution)/shard_map/ppermute | solution.py:73
  278.1 103.6 %collective-permute-start.12 = (bf16[512,2560]{1,0:T(8,128)(2,1)}, bf16[512,2560]{1,0:T(8,128)(2,1)}, u32[]{:S(2)}, u32[]{:S(2)}) collective-permute-start(bf16[512,2560]{1,0:T(8,128)(2,1)} %pad_maximum_fusion.3), channel_id=1, source_target_pairs={{0,4},{4,0},{1,5},{5,1},{2,6},{6,2},{3,7},{7,3},{8,12},{12,8},{9,1... | collective-permute-start | bytes 7864328 | tf_op jit(solution)/shard_map/ppermute | solution.py:73
  313.7 34.7 %collective-permute-start.8 = (bf16[1,2,2,128,2,256]{5,3,4,2,1,0:T(8,128)(2,1)S(1)}, bf16[1,2,2,128,2,256]{5,3,4,2,1,0:T(8,128)(2,1)S(1)}, u32[]{:S(2)}, u32[]{:S(2)}) collective-permute-start(bf16[1,2,2,128,2,256]{5,3,4,2,1,0:T(8,128)(2,1)S(1)} %get-tuple-element.475), channel_id=1, source_target_pairs={{0,4},{4,0},{1,5},{5,1},{2,6},{6,2},{3,7},{7,3},{8,12},{12,8},{9,1... | collective-permute-start | bytes 1572872 | tf_op jit(solution)/shard_map/ppermute | solution.py:73
  316.5 85.6 %collective-permute-start.17 = (bf16[512,2560]{1,0:T(8,128)(2,1)}, bf16[512,2560]{1,0:T(8,128)(2,1)}, u32[]{:S(2)}, u32[]{:S(2)}) collective-permute-start(bf16[512,2560]{1,0:T(8,128)(2,1)} %pad_maximum_fusion.3), channel_id=1, source_target_pairs={{0,1},{1,0},{2,3},{3,2},{4,5},{5,4},{6,7},{7,6},{8,9},{9,8},{10,11... | collective-permute-start | bytes 7864328 | tf_op jit(solution)/shard_map/ppermute | solution.py:73
  316.6 36.0 %collective-permute-start.10 = (bf16[1,2,2,128,2,256]{5,3,4,2,1,0:T(8,128)(2,1)S(1)}, bf16[1,2,2,128,2,256]{5,3,4,2,1,0:T(8,128)(2,1)S(1)}, u32[]{:S(2)}, u32[]{:S(2)}) collective-permute-start(bf16[1,2,2,128,2,256]{5,3,4,2,1,0:T(8,128)(2,1)S(1)} %get-tuple-element.474), channel_id=1, source_target_pairs={{0,8},{8,0},{1,9},{9,1},{2,10},{10,2},{3,11},{11,3},{4,12},{12,4},... | collective-permute-start | bytes 1572872 | tf_op jit(solution)/shard_map/ppermute | solution.py:73
  349.9 25.5 %collective-permute-start.9 = (bf16[2,2,2,128,2,256]{5,3,4,2,1,0:T(8,128)(2,1)}, bf16[2,2,2,128,2,256]{5,3,4,2,1,0:T(8,128)(2,1)}, u32[]{:S(2)}, u32[]{:S(2)}) collective-permute-start(bf16[2,2,2,128,2,256]{5,3,4,2,1,0:T(8,128)(2,1)} %get-tuple-element.477), channel_id=1, source_target_pairs={{0,8},{8,0},{1,9},{9,1},{2,10},{10,2},{3,11},{11,3},{4,12},{12,4},... | collective-permute-start | bytes 3145736 | tf_op jit(solution)/shard_map/ppermute | solution.py:73
  354.0 24.3 %collective-permute-start.11 = (bf16[2,2,2,128,2,256]{5,3,4,2,1,0:T(8,128)(2,1)}, bf16[2,2,2,128,2,256]{5,3,4,2,1,0:T(8,128)(2,1)}, u32[]{:S(2)}, u32[]{:S(2)}) collective-permute-start(bf16[2,2,2,128,2,256]{5,3,4,2,1,0:T(8,128)(2,1)} %get-tuple-element.473), channel_id=1, source_target_pairs={{0,4},{4,0},{1,5},{5,1},{2,6},{6,2},{3,7},{7,3},{8,12},{12,8},{9,1... | collective-permute-start | bytes 3145736 | tf_op jit(solution)/shard_map/ppermute | solution.py:73
  420.9 25.4 %collective-permute-start.19 = (bf16[256,2048]{1,0:T(8,128)(2,1)}, bf16[256,2048]{1,0:T(8,128)(2,1)S(1)}, u32[]{:S(2)}, u32[]{:S(2)}) collective-permute-start(bf16[256,2048]{1,0:T(8,128)(2,1)} %multiply_convert_fusion.8), channel_id=1, source_target_pairs={{0,4},{4,0},{1,5},{5,1},{2,6},{6,2},{3,7},{7,3},{8,12},{12,8},{9,1... | collective-permute-start | bytes 3145736 | tf_op jit(solution)/shard_map/ppermute | solution.py:73
  421.5 25.1 %collective-permute-start.20 = (bf16[256,2048]{1,0:T(8,128)(2,1)}, bf16[256,2048]{1,0:T(8,128)(2,1)S(1)}, u32[]{:S(2)}, u32[]{:S(2)}) collective-permute-start(bf16[256,2048]{1,0:T(8,128)(2,1)} %multiply_convert_fusion.8), channel_id=1, source_target_pairs={{0,8},{8,0},{1,9},{9,1},{2,10},{10,2},{3,11},{11,3},{4,12},{12,4},... | collective-permute-start | bytes 3145736 | tf_op jit(solution)/shard_map/ppermute | solution.py:73
  451.4 62.1 %collective-permute-start.22 = (bf16[256,2048]{1,0:T(8,128)(2,1)S(1)}, bf16[256,2048]{1,0:T(8,128)(2,1)}, u32[]{:S(2)}, u32[]{:S(2)}) collective-permute-start(bf16[256,2048]{1,0:T(8,128)(2,1)S(1)} %slice.557), channel_id=1, source_target_pairs={{0,1},{1,0},{2,3},{3,2},{4,5},{5,4},{6,7},{7,6},{8,9},{9,8},{10,11... | collective-permute-start | bytes 3145736 | tf_op jit(solution)/shard_map/ppermute | solution.py:73
  508.9 24.8 %collective-permute-start.34 = (bf16[256,2048]{1,0:T(8,128)(2,1)S(1)}, bf16[256,2048]{1,0:T(8,128)(2,1)S(1)}, u32[]{:S(2)}, u32[]{:S(2)}) collective-permute-start(bf16[256,2048]{1,0:T(8,128)(2,1)S(1)} %pad_maximum_fusion.21), channel_id=1, source_target_pairs={{0,4},{4,0},{1,5},{5,1},{2,6},{6,2},{3,7},{7,3},{8,12},{12,8},{9,1... | collective-permute-start | bytes 3145736 | tf_op jit(solution)/shard_map/ppermute | solution.py:73
  510.6 24.6 %collective-permute-start.30 = (bf16[256,2048]{1,0:T(8,128)(2,1)S(1)}, bf16[256,2048]{1,0:T(8,128)(2,1)S(1)}, u32[]{:S(2)}, u32[]{:S(2)}) collective-permute-start(bf16[256,2048]{1,0:T(8,128)(2,1)S(1)} %pad_maximum_fusion.20), channel_id=1, source_target_pairs={{0,8},{8,0},{1,9},{9,1},{2,10},{10,2},{3,11},{11,3},{4,12},{12,4},... | collective-permute-start | bytes 3145736 | tf_op jit(solution)/shard_map/ppermute | solution.py:73
  550.7 25.6 %collective-permute-start.36 = (bf16[256,2048]{1,0:T(8,128)(2,1)S(1)}, bf16[256,2048]{1,0:T(8,128)(2,1)S(1)}, u32[]{:S(2)}, u32[]{:S(2)}) collective-permute-start(bf16[256,2048]{1,0:T(8,128)(2,1)S(1)} %fusion.111), channel_id=1, source_target_pairs={{0,4},{4,0},{1,5},{5,1},{2,6},{6,2},{3,7},{7,3},{8,12},{12,8},{9,1... | collective-permute-start | bytes 3145736 | tf_op jit(solution)/shard_map/ppermute | solution.py:73
  551.4 25.3 %collective-permute-start.37 = (bf16[256,2048]{1,0:T(8,128)(2,1)S(1)}, bf16[256,2048]{1,0:T(8,128)(2,1)S(1)}, u32[]{:S(2)}, u32[]{:S(2)}) collective-permute-start(bf16[256,2048]{1,0:T(8,128)(2,1)S(1)} %fusion.111), channel_id=1, source_target_pairs={{0,8},{8,0},{1,9},{9,1},{2,10},{10,2},{3,11},{11,3},{4,12},{12,4},... | collective-permute-start | bytes 3145736 | tf_op jit(solution)/shard_map/ppermute | solution.py:73
  580.1 30.9 %collective-permute-start.39 = (bf16[256,2048]{1,0:T(8,128)(2,1)S(1)}, bf16[256,2048]{1,0:T(8,128)(2,1)S(1)}, u32[]{:S(2)}, u32[]{:S(2)}) collective-permute-start(bf16[256,2048]{1,0:T(8,128)(2,1)S(1)} %collective-permute-done.37), channel_id=1, source_target_pairs={{0,1},{1,0},{2,3},{3,2},{4,5},{5,4},{6,7},{7,6},{8,9},{9,8},{10,11... | collective-permute-start | bytes 3145736 | tf_op jit(solution)/shard_map/ppermute | solution.py:73
  580.2 47.8 %collective-permute-start.43 = (bf16[256,2048]{1,0:T(8,128)(2,1)S(1)}, bf16[256,2048]{1,0:T(8,128)(2,1)}, u32[]{:S(2)}, u32[]{:S(2)}) collective-permute-start(bf16[256,2048]{1,0:T(8,128)(2,1)S(1)} %slice.581), channel_id=1, source_target_pairs={{0,1},{1,0},{2,3},{3,2},{4,5},{5,4},{6,7},{7,6},{8,9},{9,8},{10,11... | collective-permute-start | bytes 3145736 | tf_op jit(solution)/shard_map/ppermute | solution.py:73
  592.5 37.2 %collective-permute-start.42 = (bf16[256,2048]{1,0:T(8,128)(2,1)S(1)}, bf16[256,2048]{1,0:T(8,128)(2,1)S(1)}, u32[]{:S(2)}, u32[]{:S(2)}) collective-permute-start(bf16[256,2048]{1,0:T(8,128)(2,1)S(1)} %pad_maximum_fusion.22), channel_id=1, source_target_pairs={{0,1},{1,0},{2,3},{3,2},{4,5},{5,4},{6,7},{7,6},{8,9},{9,8},{10,11... | collective-permute-start | bytes 3145736 | tf_op jit(solution)/shard_map/ppermute | solution.py:73
  611.0 30.5 %collective-permute-start.44 = (bf16[256,2048]{1,0:T(8,128)(2,1)}, bf16[256,2048]{1,0:T(8,128)(2,1)}, u32[]{:S(2)}, u32[]{:S(2)}) collective-permute-start(bf16[256,2048]{1,0:T(8,128)(2,1)} %slice.729), channel_id=1, source_target_pairs={{0,1},{1,0},{2,3},{3,2},{4,5},{5,4},{6,7},{7,6},{8,9},{9,8},{10,11... | collective-permute-start | bytes 3145736 | tf_op jit(solution)/shard_map/ppermute | solution.py:73
  645.1 25.7 %collective-permute-start.49 = (bf16[128,2048]{1,0:T(8,128)(2,1)S(1)}, bf16[128,2048]{1,0:T(8,128)(2,1)S(1)}, u32[]{:S(2)}, u32[]{:S(2)}) collective-permute-start(bf16[128,2048]{1,0:T(8,128)(2,1)S(1)} %get-tuple-element.469), channel_id=1, source_target_pairs={{0,8},{8,0},{1,9},{9,1},{2,10},{10,2},{3,11},{11,3},{4,12},{12,4},... | collective-permute-start | bytes 1572872 | tf_op jit(solution)/shard_map/ppermute | solution.py:73
  645.9 27.5 %collective-permute-start.47 = (bf16[128,2048]{1,0:T(8,128)(2,1)S(1)}, bf16[128,2048]{1,0:T(8,128)(2,1)S(1)}, u32[]{:S(2)}, u32[]{:S(2)}) collective-permute-start(bf16[128,2048]{1,0:T(8,128)(2,1)S(1)} %get-tuple-element.468), channel_id=1, source_target_pairs={{0,4},{4,0},{1,5},{5,1},{2,6},{6,2},{3,7},{7,3},{8,12},{12,8},{9,1... | collective-permute-start | bytes 1572872 | tf_op jit(solution)/shard_map/ppermute | solution.py:73
  672.0 26.1 %collective-permute-start.50 = (bf16[256,2048]{1,0:T(8,128)(2,1)}, bf16[256,2048]{1,0:T(8,128)(2,1)}, u32[]{:S(2)}, u32[]{:S(2)}) collective-permute-start(bf16[256,2048]{1,0:T(8,128)(2,1)} %pad_maximum_fusion.24), channel_id=1, source_target_pairs={{0,4},{4,0},{1,5},{5,1},{2,6},{6,2},{3,7},{7,3},{8,12},{12,8},{9,1... | collective-permute-start | bytes 3145736 | tf_op jit(solution)/shard_map/ppermute | solution.py:73
  674.6 24.8 %collective-permute-start.48 = (bf16[256,2048]{1,0:T(8,128)(2,1)}, bf16[256,2048]{1,0:T(8,128)(2,1)S(1)}, u32[]{:S(2)}, u32[]{:S(2)}) collective-permute-start(bf16[256,2048]{1,0:T(8,128)(2,1)} %pad_maximum_fusion.23), channel_id=1, source_target_pairs={{0,8},{8,0},{1,9},{9,1},{2,10},{10,2},{3,11},{11,3},{4,12},{12,4},... | collective-permute-start | bytes 3145736 | tf_op jit(solution)/shard_map/ppermute | solution.py:73
  755.5 47.9 %collective-permute-start.52 = (bf16[512,2048]{1,0:T(8,128)(2,1)S(1)}, bf16[512,2048]{1,0:T(8,128)(2,1)S(1)}, u32[]{:S(2)}, u32[]{:S(2)}) collective-permute-start(bf16[512,2048]{1,0:T(8,128)(2,1)S(1)} %slice.601), channel_id=1, source_target_pairs={{0,4},{4,0},{1,5},{5,1},{2,6},{6,2},{3,7},{7,3},{8,12},{12,8},{9,1... | collective-permute-start | bytes 6291464 | tf_op jit(solution)/shard_map/ppermute | solution.py:73
  814.1 39.4 %collective-permute-start.55 = (bf16[2,2,2,128,2,256]{5,3,4,2,1,0:T(8,128)(2,1)}, bf16[2,2,2,128,2,256]{5,3,4,2,1,0:T(8,128)(2,1)}, u32[]{:S(2)}, u32[]{:S(2)}) collective-permute-start(bf16[2,2,2,128,2,256]{5,3,4,2,1,0:T(8,128)(2,1)} %slice_bitcast_fusion), channel_id=1, source_target_pairs={{0,4},{4,0},{1,5},{5,1},{2,6},{6,2},{3,7},{7,3},{8,12},{12,8},{9,1... | collective-permute-start | bytes 3145736 | tf_op jit(solution)/shard_map/ppermute | solution.py:73
  835.8 72.5 %collective-permute-start.58 = (bf16[1024,2048]{1,0:T(8,128)(2,1)S(1)}, bf16[1024,2048]{1,0:T(8,128)(2,1)S(1)}, u32[]{:S(2)}, u32[]{:S(2)}) collective-permute-start(bf16[1024,2048]{1,0:T(8,128)(2,1)S(1)} %convolution_convert_fusion.2), channel_id=1, source_target_pairs={{0,1},{1,0},{2,3},{3,2},{4,5},{5,4},{6,7},{7,6},{8,9},{9,8},{10,11... | collective-permute-start | bytes 12582920 | tf_op jit(solution)/shard_map/ppermute | solution.py:73
  843.1 40.7 %collective-permute-start.53 = (bf16[2,2,2,128,2,256]{5,3,4,2,1,0:T(8,128)(2,1)S(1)}, bf16[2,2,2,128,2,256]{5,3,4,2,1,0:T(8,128)(2,1)S(1)}, u32[]{:S(2)}, u32[]{:S(2)}) collective-permute-start(bf16[2,2,2,128,2,256]{5,3,4,2,1,0:T(8,128)(2,1)S(1)} %bitcast.522), channel_id=1, source_target_pairs={{0,8},{8,0},{1,9},{9,1},{2,10},{10,2},{3,11},{11,3},{4,12},{12,4},... | collective-permute-start | bytes 3145736 | tf_op jit(solution)/shard_map/ppermute | solution.py:73
  844.9 40.7 %collective-permute-start.60 = (bf16[1024,512]{1,0:T(8,128)(2,1)S(1)}, bf16[1024,512]{1,0:T(8,128)(2,1)S(1)}, u32[]{:S(2)}, u32[]{:S(2)}) collective-permute-start(bf16[1024,512]{1,0:T(8,128)(2,1)S(1)} %pad_maximum_fusion.25), channel_id=1, source_target_pairs={{0,1},{1,0},{2,3},{3,2},{4,5},{5,4},{6,7},{7,6},{8,9},{9,8},{10,11... | collective-permute-start | bytes 3145736 | tf_op jit(solution)/shard_map/ppermute | solution.py:73
  856.6 49.3 %collective-permute-start.56 = (bf16[2,2,128,2,256]{4,2,3,1,0:T(8,128)(2,1)S(1)}, bf16[2,2,128,2,256]{4,2,3,1,0:T(8,128)(2,1)S(1)}, u32[]{:S(2)}, u32[]{:S(2)}) collective-permute-start(bf16[2,2,128,2,256]{4,2,3,1,0:T(8,128)(2,1)S(1)} %slice_bitcast_fusion.4), channel_id=1, source_target_pairs={{0,8},{8,0},{1,9},{9,1},{2,10},{10,2},{3,11},{11,3},{4,12},{12,4},... | collective-permute-start | bytes 1572872 | tf_op jit(solution)/shard_map/ppermute | solution.py:73
  886.0 24.6 %collective-permute-start.61 = (bf16[512,512]{1,0:T(8,128)(2,1)S(1)}, bf16[512,512]{1,0:T(8,128)(2,1)S(1)}, u32[]{:S(2)}, u32[]{:S(2)}) collective-permute-start(bf16[512,512]{1,0:T(8,128)(2,1)S(1)} %slice.761), channel_id=1, source_target_pairs={{0,4},{4,0},{1,5},{5,1},{2,6},{6,2},{3,7},{7,3},{8,12},{12,8},{9,1... | collective-permute-start | bytes 1572872 | tf_op jit(solution)/shard_map/ppermute | solution.py:73
  906.3 39.3 %collective-permute-start.57 = (bf16[2,2,128,2,256]{4,2,3,1,0:T(8,128)(2,1)S(1)}, bf16[2,2,128,2,256]{4,2,3,1,0:T(8,128)(2,1)S(1)}, u32[]{:S(2)}, u32[]{:S(2)}) collective-permute-start(bf16[2,2,128,2,256]{4,2,3,1,0:T(8,128)(2,1)S(1)} %fusion.211), channel_id=1, source_target_pairs={{0,16},{16,0},{1,17},{17,1},{2,18},{18,2},{3,19},{19,3},{4,20},{20... | collective-permute-start | bytes 1572872 | tf_op jit(solution)/shard_map/ppermute | solution.py:73
  909.9 45.8 %collective-permute-start.59 = (bf16[512,2048]{1,0:T(8,128)(2,1)S(1)}, bf16[512,2048]{1,0:T(8,128)(2,1)S(1)}, u32[]{:S(2)}, u32[]{:S(2)}) collective-permute-start(bf16[512,2048]{1,0:T(8,128)(2,1)S(1)} %slice.755), channel_id=1, source_target_pairs={{0,4},{4,0},{1,5},{5,1},{2,6},{6,2},{3,7},{7,3},{8,12},{12,8},{9,1... | collective-permute-start | bytes 6291464 | tf_op jit(solution)/shard_map/ppermute | solution.py:73
  968.3 48.4 %collective-permute-start.64 = (bf16[256,2048]{1,0:T(8,128)(2,1)}, bf16[256,2048]{1,0:T(8,128)(2,1)}, u32[]{:S(2)}, u32[]{:S(2)}) collective-permute-start(bf16[256,2048]{1,0:T(8,128)(2,1)} %get-tuple-element.458), channel_id=1, source_target_pairs={{0,2},{2,0},{1,3},{3,1},{4,6},{6,4},{5,7},{7,5},{8,10},{10,8},{9,1... | collective-permute-start | bytes 3145736 | tf_op jit(solution)/shard_map/ppermute | solution.py:73
  972.3 49.9 %collective-permute-start.66 = (bf16[256,2560]{1,0:T(8,128)(2,1)}, bf16[256,2560]{1,0:T(8,128)(2,1)}, u32[]{:S(2)}, u32[]{:S(2)}) collective-permute-start(bf16[256,2560]{1,0:T(8,128)(2,1)} %get-tuple-element.452), channel_id=1, source_target_pairs={{0,2},{2,0},{1,3},{3,1},{4,6},{6,4},{5,7},{7,5},{8,10},{10,8},{9,1... | collective-permute-start | bytes 3932168 | tf_op jit(solution)/shard_map/ppermute | solution.py:73
  986.3 28.4 %collective-permute-start.63 = (bf16[512,1152]{0,1:T(8,128)(2,1)}, bf16[512,1152]{0,1:T(8,128)(2,1)}, u32[]{:S(2)}, u32[]{:S(2)}) collective-permute-start(bf16[512,1152]{0,1:T(8,128)(2,1)} %slice.631), channel_id=1, source_target_pairs={{0,4},{4,0},{1,5},{5,1},{2,6},{6,2},{3,7},{7,3},{8,12},{12,8},{9,1... | collective-permute-start | bytes 3538952 | tf_op jit(solution)/shard_map/ppermute | solution.py:73
  1048.4 96.6 %all-to-all-start.1 = ((bf16[8,192,1024]{2,1,0:T(8,128)(2,1)}), bf16[8,192,1024]{2,1,0:T(8,128)(2,1)}, u32[]{:S(2)}, u32[]{:S(2)}) async-start(bf16[8,192,1024]{2,1,0:T(8,128)(2,1)} %pad_maximum_fusion.2), calls=%async_computation.2 | async-start | bytes 6291456 | tf_op jit(solution)/shard_map/all_to_all | solution.py:203
  1057.3 33.7 %collective-permute-start.75 = (f32[12800]{0:T(1024)S(1)}, f32[12800]{0:T(1024)S(1)}, u32[]{:S(2)}, u32[]{:S(2)}) collective-permute-start(f32[12800]{0:T(1024)S(1)} %add.593), channel_id=1, source_target_pairs={{0,4},{4,0},{1,5},{5,1},{2,6},{6,2},{3,7},{7,3},{8,12},{12,8},{9,1... | collective-permute-start | bytes 153608 | tf_op jit(solution)/shard_map/ppermute | solution.py:73
  1102.7 32.9 %collective-permute-start.72 = (bf16[64,2560]{1,0:T(8,128)(2,1)S(1)}, bf16[64,2560]{1,0:T(8,128)(2,1)S(1)}, u32[]{:S(2)}, u32[]{:S(2)}) collective-permute-start(bf16[64,2560]{1,0:T(8,128)(2,1)S(1)} %slice.651), channel_id=1, source_target_pairs={{0,16},{16,0},{1,17},{17,1},{2,18},{18,2},{3,19},{19,3},{4,20},{20... | collective-permute-start | bytes 983048 | tf_op jit(solution)/shard_map/ppermute | solution.py:73
  (241 other events, 3778.5 us)
Sparse Core Ops, SparseCore 0:
  76.8 249.1 all-gather.1
  702.6 241.3 reduce-scatter.1

commit v13 on v10

--- a/solution.py
+++ b/solution.py
@@ -197,14 +197,10 @@
             place = (place[:, None] + weight * jnp.stack([bit, 1 - bit])[None, :]).reshape(-1)
         return place
 
-    def own_rows(self, sums, local_rows):
+    def to_rows(self, sums, local_rows):
         size = 2 ** len(self.team)
         sums = jnp.concatenate([one.reshape(size, local_rows, -1) for one in sums], axis=1)
-        moved = lax.all_to_all(sums, self.team, split_axis=0, concat_axis=0, tiled=True)
-        return [
-            jnp.concatenate([moved[at, first : first + local_rows] for at in range(size)], axis=1).astype(F32)
-            for first in range(0, moved.shape[1], local_rows)
-        ]
+        return lax.all_to_all(sums, self.team, split_axis=0, concat_axis=0, tiled=True)
 
     def total(self, value):
         for axis in reversed(self.every):
@@ -572,7 +568,6 @@
         d_keys, d_values, query_sum, output_sum, side_sum, d_spread, feed_sum
     )
     output_sum = jnp.concatenate([output_sum, side_sum], axis=1)
-    grad_gate, grad_up, grad_down = plan.own_rows(jnp.split(feed_sum, 3), local_rows)
     d_kvl_low = jnp.concatenate(
         [
             d_keys.reshape(rows, -1).astype(BF16),
@@ -583,16 +578,17 @@
     )
     laurel_spread = product(d_laurel_low, to_spread).astype(BF16)
     kvl_sum = plan.spread_begin([(normed_spread, d_kvl_low), (laurel_spread, latent_low)])
+    kvl_sum, d_kvl_low = together(kvl_sum, d_kvl_low)
     query_kept, query_away = plan.spread_send(query_sum, steps[1])
     output_kept, output_away = plan.spread_send(output_sum, steps[1])
     kvl_sum = plan.spread_step(kvl_sum, steps[:1])
+    feed_rows = plan.to_rows(jnp.split(feed_sum, 3), local_rows)
     kvl_sum, query_kept, output_kept = together(kvl_sum, query_kept, output_kept)
     query_sum = (query_kept + query_away).astype(BF16)
     output_sum = (output_kept + output_away).astype(BF16)
     kvl_sum = plan.spread_step(kvl_sum, steps[1:2])
     query_sum = plan.spread_step(query_sum, steps[2:3])
     output_sum = plan.spread_step(output_sum, steps[2:3])
-    kvl_sum, query_sum, output_sum, d_kvl_low = together(kvl_sum, query_sum, output_sum, d_kvl_low)
     d_spread = d_spread + product_nt_split(d_kvl_low, kvl_full)
     d_normed = d_normed + reorder(d_spread, to_spread)
     d_inputs_norm, grad_norm_input = pre_pull(d_normed)
@@ -614,9 +610,15 @@
     grad_query = plan.spread_step(query_sum, steps[3:])
     output_sum = plan.spread_step(output_sum, steps[3:])
     kvl_sum = plan.spread_step(kvl_sum, steps[2:3])
-    gain_grads, grad_query, output_sum, kvl_sum = together(
-        gain_grads, grad_query, output_sum, kvl_sum
-    )
+    gain_grads, grad_query, output_sum, kvl_sum, feed_rows = together(
+        gain_grads, grad_query, output_sum, kvl_sum, feed_rows
+    )
+    grad_gate, grad_up, grad_down = [
+        jnp.concatenate(
+            [feed_rows[at, first : first + local_rows] for at in range(team_size)], axis=1
+        ).astype(F32)
+        for first in range(0, 3 * local_rows, local_rows)
+    ]
     grad_output, grad_side_gate, grad_side_output = split_columns(output_sum, rest_widths)
     grad_key, grad_value, grad_left, grad_right = split_columns(
         plan.spread_step(kvl_sum, steps[3:]), kvl_widths

time: 1150 us -> 1150 us (level)
    unnamed x460 -> x454, local copies, waits for them, and re-layouts: 50.7 us -> 48.5 us
  transfers between devices with their start and end apart: 82 -> 82, of which waited for: 41 -> 38; matrix products, arithmetic and copies ran while one was open for 40% -> 41% of each run, Pallas kernels for 0% -> 0%
where the time goes in v13:
time: 1150 us; the launch traced here: 1140 us
  waiting for transfers between devices  513 us (45%)
  matrix products  263 us (23%)
  local copies, waits for them, and re-layouts  140 us (12%)
  other arithmetic  126 us (11%)
  starting transfers between devices  77.1 us (7%)
  between operations  18.4 us (2%)
    ppermute x78, waiting for transfers between devices, swap(): return lax.ppermute(value, axis, [(0, 1), (1, 0)])  512 us
    dot_general x33, matrix products, product(): return jnp.dot(left, right, preferred_element_type=F32)  103 us
    dot_general x31, matrix products, product_nt(): lax.dot_general(left, right, (((1,), (1,)), ((), ())), preferred_element_...  91.9 us
    ppermute x78, starting transfers between devices, swap(): return lax.ppermute(value, axis, [(0, 1), (1, 0)])  66.9 us
    dot_general x15, matrix products, product_tn(): lax.dot_general(left, right, (((0,), (0,)), ((), ())), preferred_element_...  54.3 us
    unnamed x454, local copies, waits for them, and re-layouts  48.5 us
  transfers between devices with their start and end apart: 82, of which 38 were waited for; matrix products, arithmetic and copies ran while one was open for 41% of the time, Pallas kernels for 0%

profile of v13, /device:TPU:0, one launch (start us, length us, event | category | flops | bytes accessed | tf_op | source)
XLA Modules:
  0.0 1137.8 jit_solution(13180269562066647445)
XLA Ops:
  14.4 5.4 all-to-all-start
  24.6 45.8 %collective-permute-done = bf16[64,5760]{1,0:T(8,128)(2,1)} collective-permute-done((bf16[64,5760]{1,0:T(8,128)(2,1)S(1)}, bf16[64,5760]{1,0:T(8,128)(2,1)}, u32[]{:S(2)}, u32[]{:S(2)}) %collective-permute-start) | collective-permute-done | bytes 737312 | tf_op jit(solution)/shard_map/ppermute | solution.py:73
  82.3 55.7 %collective-permute-done.1 = bf16[128,5760]{1,0:T(8,128)(2,1)S(1)} collective-permute-done((bf16[128,5760]{1,0:T(8,128)(2,1)S(1)}, bf16[128,5760]{1,0:T(8,128)(2,1)S(1)}, u32[]{:S(2)}, u32[]{:S(2)}) %collective-permute-start.1) | collective-permute-done | bytes 1474592 | tf_op jit(solution)/shard_map/ppermute | solution.py:73
  140.5 9.0 collective-permute-done.2
  158.7 15.3 %collective-permute-done.3 = bf16[512,1152]{1,0:T(8,128)(2,1)} collective-permute-done((bf16[512,1152]{1,0:T(8,128)(2,1)}, bf16[512,1152]{1,0:T(8,128)(2,1)}, u32[]{:S(2)}, u32[]{:S(2)}) %collective-permute-start.3) | collective-permute-done | bytes 1179680 | tf_op jit(solution)/shard_map/ppermute | solution.py:73
  177.3 5.2 fusion.76
  185.4 7.8 collective-permute-done.13
  208.0 6.0 rev.69
  246.4 26.3 %collective-permute-done.6 = bf16[256,2560]{1,0:T(8,128)(2,1)} collective-permute-done((bf16[256,2560]{1,0:T(8,128)(2,1)}, bf16[256,2560]{1,0:T(8,128)(2,1)}, u32[]{:S(2)}, u32[]{:S(2)}) %collective-permute-start.6) | collective-permute-done | bytes 1310752 | tf_op jit(solution)/shard_map/ppermute | solution.py:73
  281.2 32.3 %collective-permute-done.7 = bf16[2,1,2,128,2,256]{5,3,4,2,1,0:T(8,128)(2,1)S(1)} collective-permute-done((bf16[2,1,2,128,2,256]{5,3,4,2,1,0:T(8,128)(2,1)S(1)}, bf16[2,1,2,128,2,256]{5,3,4,2,1,0:T(8,128)(2,1)S(1)}, u32[]{:S(2)}, u32[]{:S(2)}) %collective-permute-start.7) | collective-permute-done | bytes 524320 | tf_op jit(solution)/shard_map/ppermute | solution.py:73
  318.9 29.5 %collective-permute-done.8 = bf16[1,2,2,128,2,256]{5,3,4,2,1,0:T(8,128)(2,1)S(1)} collective-permute-done((bf16[1,2,2,128,2,256]{5,3,4,2,1,0:T(8,128)(2,1)S(1)}, bf16[1,2,2,128,2,256]{5,3,4,2,1,0:T(8,128)(2,1)S(1)}, u32[]{:S(2)}, u32[]{:S(2)}) %collective-permute-start.8) | collective-permute-done | bytes 524320 | tf_op jit(solution)/shard_map/ppermute | solution.py:73
  359.5 15.9 %collective-permute-done.9 = bf16[2,2,2,128,2,256]{5,3,4,2,1,0:T(8,128)(2,1)} collective-permute-done((bf16[2,2,2,128,2,256]{5,3,4,2,1,0:T(8,128)(2,1)}, bf16[2,2,2,128,2,256]{5,3,4,2,1,0:T(8,128)(2,1)}, u32[]{:S(2)}, u32[]{:S(2)}) %collective-permute-start.9) | collective-permute-done | bytes 1048608 | tf_op jit(solution)/shard_map/ppermute | solution.py:73
  405.2 4.7 fusion.5
  423.3 5.8 fusion.274
  433.0 6.3 multiply_convert_fusion.7
  441.7 4.6 collective-permute-done.19
  451.6 7.9 collective-permute-done.25
  496.7 12.0 %collective-permute-done.33 = bf16[128,2048]{1,0:T(8,128)(2,1)S(1)} collective-permute-done((bf16[128,2048]{1,0:T(8,128)(2,1)S(1)}, bf16[128,2048]{1,0:T(8,128)(2,1)S(1)}, u32[]{:S(2)}, u32[]{:S(2)}) %collective-permute-start.33) | collective-permute-done | bytes 524320 | tf_op jit(solution)/shard_map/ppermute | solution.py:73
  513.5 20.2 %collective-permute-done.34 = bf16[256,2048]{1,0:T(8,128)(2,1)S(1)} collective-permute-done((bf16[256,2048]{1,0:T(8,128)(2,1)S(1)}, bf16[256,2048]{1,0:T(8,128)(2,1)S(1)}, u32[]{:S(2)}, u32[]{:S(2)}) %collective-permute-start.34) | collective-permute-done | bytes 1048608 | tf_op jit(solution)/shard_map/ppermute | solution.py:73
  552.8 4.7 multiply_convert_fusion.3
  561.8 4.6 add_convert_fusion.8
  566.4 10.0 collective-permute-done.36
  582.2 9.0 collective-permute-done.40
  595.2 5.2 multiply_convert_fusion.2
  604.9 5.0 add_convert_fusion.7
  612.5 5.4 multiply_convert_fusion.1
  622.3 4.6 add_convert_fusion.6
  648.0 10.9 fusion.58
  658.9 11.8 %fusion.61 = bf16[2048,1024]{1,0:T(8,128)(2,1)} fusion(bf16[2048,2048]{1,0:T(8,128)(2,1)S(1)} %constant_dynamic-update-slice_fusion.22, bf16[512,1024]{1,0:T(8,128)(2,1)} %copy-done.184, bf16[512,1024]{1,0:T(8,128)(2,1)S(1)} %copy-done.183, bf16[512,1024]{1,0:T(8,128)(2,1)S(1)} %copy-done.181, bf16[512,1024]{1,0:T(8,128)(2,1)S(1)} %copy-done.179), kind=kOutput, calls=%fused_computation.76 | convolution fusion | flops 8608808960 | bytes 16777216 | tf_op jit(solution)/shard_map/dot_general | solution.py:34
  675.2 13.9 %fusion.64 = bf16[2048,1024]{1,0:T(8,128)(2,1)} fusion(bf16[512,1024]{1,0:T(8,128)(2,1)} %copy-done.198, bf16[512,1024]{1,0:T(8,128)(2,1)} %get-tuple-element.136, bf16[512,1024]{1,0:T(8,128)(2,1)} %copy-done.196, bf16[512,1024]{1,0:T(8,128)(2,1)} %copy-done.195, bf16[512,2048]{1,0:T(8,128)(2,1)} %copy-done.95, bf16[512,2048]{1,0:T(8,128)(2,1)} %copy-done.84, ...), kind=kOutput, calls=%fused_computation.77 | convolution fusion | flops 8642363392 | bytes 16777216 | tf_op jit(solution)/shard_map/dot_general | solution.py:34
  689.1 9.0 pad_maximum_fusion
  723.2 5.0 fusion.75
  739.4 5.4 add_convert_fusion.1
  759.2 5.1 fusion.19
  775.4 30.9 %collective-permute-done.52 = bf16[512,2048]{1,0:T(8,128)(2,1)S(1)} collective-permute-done((bf16[512,2048]{1,0:T(8,128)(2,1)S(1)}, bf16[512,2048]{1,0:T(8,128)(2,1)S(1)}, u32[]{:S(2)}, u32[]{:S(2)}) %collective-permute-start.52) | collective-permute-done | bytes 2097184 | tf_op jit(solution)/shard_map/ppermute | solution.py:73
  838.1 5.3 fusion.69
  860.1 27.9 %collective-permute-done.53 = bf16[2,2,2,128,2,256]{5,3,4,2,1,0:T(8,128)(2,1)S(1)} collective-permute-done((bf16[2,2,2,128,2,256]{5,3,4,2,1,0:T(8,128)(2,1)S(1)}, bf16[2,2,2,128,2,256]{5,3,4,2,1,0:T(8,128)(2,1)S(1)}, u32[]{:S(2)}, u32[]{:S(2)}) %collective-permute-start.53) | collective-permute-done | bytes 1048608 | tf_op jit(solution)/shard_map/ppermute | solution.py:73
  890.8 18.2 %collective-permute-done.56 = bf16[2,2,128,2,256]{4,2,3,1,0:T(8,128)(2,1)S(1)} collective-permute-done((bf16[2,2,128,2,256]{4,2,3,1,0:T(8,128)(2,1)S(1)}, bf16[2,2,128,2,256]{4,2,3,1,0:T(8,128)(2,1)S(1)}, u32[]{:S(2)}, u32[]{:S(2)}) %collective-permute-start.56) | collective-permute-done | bytes 524320 | tf_op jit(solution)/shard_map/ppermute | solution.py:73
  915.9 29.7 %collective-permute-done.57 = bf16[2,2,128,2,256]{4,2,3,1,0:T(8,128)(2,1)S(1)} collective-permute-done((bf16[2,2,128,2,256]{4,2,3,1,0:T(8,128)(2,1)S(1)}, bf16[2,2,128,2,256]{4,2,3,1,0:T(8,128)(2,1)S(1)}, u32[]{:S(2)}, u32[]{:S(2)}) %collective-permute-start.57) | collective-permute-done | bytes 524320 | tf_op jit(solution)/shard_map/ppermute | solution.py:73
  948.1 11.8 %collective-permute-done.59 = bf16[512,2048]{1,0:T(8,128)(2,1)S(1)} collective-permute-done((bf16[512,2048]{1,0:T(8,128)(2,1)S(1)}, bf16[512,2048]{1,0:T(8,128)(2,1)S(1)}, u32[]{:S(2)}, u32[]{:S(2)}) %collective-permute-start.59) | collective-permute-done | bytes 2097184 | tf_op jit(solution)/shard_map/ppermute | solution.py:73
  975.2 4.6 all-to-all-start.1
  991.6 4.7 fusion.1
  1002.3 4.9 fusion.7
  1009.2 32.8 %collective-permute-done.63 = bf16[512,1152]{0,1:T(8,128)(2,1)} collective-permute-done((bf16[512,1152]{0,1:T(8,128)(2,1)}, bf16[512,1152]{0,1:T(8,128)(2,1)}, u32[]{:S(2)}, u32[]{:S(2)}) %collective-permute-start.63) | collective-permute-done | bytes 1179680 | tf_op jit(solution)/shard_map/ppermute | solution.py:73
  1050.5 9.9 collective-permute-done.65
  1062.7 17.4 %collective-permute-done.68 = bf16[128,2560]{1,0:T(8,128)(2,1)S(1)} collective-permute-done((bf16[128,2560]{1,0:T(8,128)(2,1)S(1)}, bf16[128,2560]{1,0:T(8,128)(2,1)S(1)}, u32[]{:S(2)}, u32[]{:S(2)}) %collective-permute-start.68) | collective-permute-done | bytes 655392 | tf_op jit(solution)/shard_map/ppermute | solution.py:73
  1081.2 7.5 collective-permute-done.71
  1088.7 10.4 collective-permute-done.69
  (952 shorter events, 478.3 us)
Async XLA Ops:
  14.4 58.2 %all-to-all-start = ((bf16[8,192,1024]{2,1,0:T(8,128)(2,1)}), bf16[8,192,1024]{2,1,0:T(8,128)(2,1)}, u32[]{:S(2)}, u32[]{:S(2)}) async-start(bf16[8,192,1024]{2,1,0:T(8,128)(2,1)} %copy.514), calls=%async_computation | async-start | bytes 6291456 | tf_op jit(solution)/shard_map/all_to_all | solution.py:322
  19.8 374.9 %all-gather.2.cloned.1.call-start = ((), (), s32[]{:S(2)}) async-start(), calls=%async_computation.3 | async-start | bytes 15728640 | tf_op jit(solution)/shard_map/all_gather | solution.py:332
  20.1 50.3 %collective-permute-start = (bf16[64,5760]{1,0:T(8,128)(2,1)S(1)}, bf16[64,5760]{1,0:T(8,128)(2,1)}, u32[]{:S(2)}, u32[]{:S(2)}) collective-permute-start(bf16[64,5760]{1,0:T(8,128)(2,1)S(1)} %concatenate.177), channel_id=1, source_target_pairs={{0,16},{16,0},{1,17},{17,1},{2,18},{18,2},{3,19},{19,3},{4,20},{20... | collective-permute-start | bytes 2211848 | tf_op jit(solution)/shard_map/ppermute | solution.py:73
  76.7 884.1 %reduce-scatter.2.cloned.1.call-start = ((), (), s32[]{:S(2)}) async-start(), calls=%async_computation.4 | async-start | bytes 15728640 | tf_op jit(solution)/shard_map/reduce_scatter | solution.py:503
  77.6 60.3 %collective-permute-start.1 = (bf16[128,5760]{1,0:T(8,128)(2,1)S(1)}, bf16[128,5760]{1,0:T(8,128)(2,1)S(1)}, u32[]{:S(2)}, u32[]{:S(2)}) collective-permute-start(bf16[128,5760]{1,0:T(8,128)(2,1)S(1)} %pad_maximum_fusion.14), channel_id=1, source_target_pairs={{0,8},{8,0},{1,9},{9,1},{2,10},{10,2},{3,11},{11,3},{4,12},{12,4},... | collective-permute-start | bytes 4423688 | tf_op jit(solution)/shard_map/ppermute | solution.py:73
  157.1 36.1 %collective-permute-start.13 = (bf16[256,2048]{1,0:T(8,128)(2,1)S(1)}, bf16[256,2048]{1,0:T(8,128)(2,1)}, u32[]{:S(2)}, u32[]{:S(2)}) collective-permute-start(bf16[256,2048]{1,0:T(8,128)(2,1)S(1)} %slice.701), channel_id=1, source_target_pairs={{0,2},{2,0},{1,3},{3,1},{4,6},{6,4},{5,7},{7,5},{8,10},{10,8},{9,1... | collective-permute-start | bytes 3145736 | tf_op jit(solution)/shard_map/ppermute | solution.py:73
  158.7 37.2 %collective-permute-start.4 = (bf16[512,1152]{1,0:T(8,128)(2,1)}, bf16[512,1152]{1,0:T(8,128)(2,1)}, u32[]{:S(2)}, u32[]{:S(2)}) collective-permute-start(bf16[512,1152]{1,0:T(8,128)(2,1)} %pad_maximum_fusion.15), channel_id=1, source_target_pairs={{0,1},{1,0},{2,3},{3,2},{4,5},{5,4},{6,7},{7,6},{8,9},{9,8},{10,11... | collective-permute-start | bytes 3538952 | tf_op jit(solution)/shard_map/ppermute | solution.py:73
  195.9 83.0 %collective-permute-start.15 = (bf16[512,2048]{1,0:T(8,128)(2,1)}, bf16[512,2048]{1,0:T(8,128)(2,1)}, u32[]{:S(2)}, u32[]{:S(2)}) collective-permute-start(bf16[512,2048]{1,0:T(8,128)(2,1)} %pad_maximum_fusion.7), channel_id=1, source_target_pairs={{0,1},{1,0},{2,3},{3,2},{4,5},{5,4},{6,7},{7,6},{8,9},{9,8},{10,11... | collective-permute-start | bytes 6291464 | tf_op jit(solution)/shard_map/ppermute | solution.py:73
  195.9 49.9 %collective-permute-start.14 = (bf16[512,2048]{1,0:T(8,128)(2,1)}, bf16[512,2048]{1,0:T(8,128)(2,1)}, u32[]{:S(2)}, u32[]{:S(2)}) collective-permute-start(bf16[512,2048]{1,0:T(8,128)(2,1)} %pad_maximum_fusion.7), channel_id=1, source_target_pairs={{0,4},{4,0},{1,5},{5,1},{2,6},{6,2},{3,7},{7,3},{8,12},{12,8},{9,1... | collective-permute-start | bytes 6291464 | tf_op jit(solution)/shard_map/ppermute | solution.py:73
  232.9 39.8 %collective-permute-start.6 = (bf16[256,2560]{1,0:T(8,128)(2,1)}, bf16[256,2560]{1,0:T(8,128)(2,1)}, u32[]{:S(2)}, u32[]{:S(2)}) collective-permute-start(bf16[256,2560]{1,0:T(8,128)(2,1)} %slice.691), channel_id=1, source_target_pairs={{0,2},{2,0},{1,3},{3,1},{4,6},{6,4},{5,7},{7,5},{8,10},{10,8},{9,1... | collective-permute-start | bytes 3932168 | tf_op jit(solution)/shard_map/ppermute | solution.py:73
  245.9 70.8 %collective-permute-start.16 = (bf16[512,2048]{1,0:T(8,128)(2,1)}, bf16[512,2048]{1,0:T(8,128)(2,1)S(1)}, u32[]{:S(2)}, u32[]{:S(2)}) collective-permute-start(bf16[512,2048]{1,0:T(8,128)(2,1)} %collective-permute-done.14), channel_id=1, source_target_pairs={{0,1},{1,0},{2,3},{3,2},{4,5},{5,4},{6,7},{7,6},{8,9},{9,8},{10,11... | collective-permute-start | bytes 6291464 | tf_op jit(solution)/shard_map/ppermute | solution.py:73
  275.7 37.9 %collective-permute-start.7 = (bf16[2,1,2,128,2,256]{5,3,4,2,1,0:T(8,128)(2,1)S(1)}, bf16[2,1,2,128,2,256]{5,3,4,2,1,0:T(8,128)(2,1)S(1)}, u32[]{:S(2)}, u32[]{:S(2)}) collective-permute-start(bf16[2,1,2,128,2,256]{5,3,4,2,1,0:T(8,128)(2,1)S(1)} %maximum_bitcast_fusion), channel_id=1, source_target_pairs={{0,16},{16,0},{1,17},{17,1},{2,18},{18,2},{3,19},{19,3},{4,20},{20... | collective-permute-start | bytes 1572872 | tf_op jit(solution)/shard_map/ppermute | solution.py:73
  278.1 103.6 %collective-permute-start.12 = (bf16[512,2560]{1,0:T(8,128)(2,1)}, bf16[512,2560]{1,0:T(8,128)(2,1)}, u32[]{:S(2)}, u32[]{:S(2)}) collective-permute-start(bf16[512,2560]{1,0:T(8,128)(2,1)} %pad_maximum_fusion.3), channel_id=1, source_target_pairs={{0,4},{4,0},{1,5},{5,1},{2,6},{6,2},{3,7},{7,3},{8,12},{12,8},{9,1... | collective-permute-start | bytes 7864328 | tf_op jit(solution)/shard_map/ppermute | solution.py:73
  313.7 34.7 %collective-permute-start.8 = (bf16[1,2,2,128,2,256]{5,3,4,2,1,0:T(8,128)(2,1)S(1)}, bf16[1,2,2,128,2,256]{5,3,4,2,1,0:T(8,128)(2,1)S(1)}, u32[]{:S(2)}, u32[]{:S(2)}) collective-permute-start(bf16[1,2,2,128,2,256]{5,3,4,2,1,0:T(8,128)(2,1)S(1)} %get-tuple-element.475), channel_id=1, source_target_pairs={{0,4},{4,0},{1,5},{5,1},{2,6},{6,2},{3,7},{7,3},{8,12},{12,8},{9,1... | collective-permute-start | bytes 1572872 | tf_op jit(solution)/shard_map/ppermute | solution.py:73
  316.5 85.6 %collective-permute-start.17 = (bf16[512,2560]{1,0:T(8,128)(2,1)}, bf16[512,2560]{1,0:T(8,128)(2,1)}, u32[]{:S(2)}, u32[]{:S(2)}) collective-permute-start(bf16[512,2560]{1,0:T(8,128)(2,1)} %pad_maximum_fusion.3), channel_id=1, source_target_pairs={{0,1},{1,0},{2,3},{3,2},{4,5},{5,4},{6,7},{7,6},{8,9},{9,8},{10,11... | collective-permute-start | bytes 7864328 | tf_op jit(solution)/shard_map/ppermute | solution.py:73
  316.6 36.0 %collective-permute-start.10 = (bf16[1,2,2,128,2,256]{5,3,4,2,1,0:T(8,128)(2,1)S(1)}, bf16[1,2,2,128,2,256]{5,3,4,2,1,0:T(8,128)(2,1)S(1)}, u32[]{:S(2)}, u32[]{:S(2)}) collective-permute-start(bf16[1,2,2,128,2,256]{5,3,4,2,1,0:T(8,128)(2,1)S(1)} %get-tuple-element.474), channel_id=1, source_target_pairs={{0,8},{8,0},{1,9},{9,1},{2,10},{10,2},{3,11},{11,3},{4,12},{12,4},... | collective-permute-start | bytes 1572872 | tf_op jit(solution)/shard_map/ppermute | solution.py:73
  349.9 25.6 %collective-permute-start.9 = (bf16[2,2,2,128,2,256]{5,3,4,2,1,0:T(8,128)(2,1)}, bf16[2,2,2,128,2,256]{5,3,4,2,1,0:T(8,128)(2,1)}, u32[]{:S(2)}, u32[]{:S(2)}) collective-permute-start(bf16[2,2,2,128,2,256]{5,3,4,2,1,0:T(8,128)(2,1)} %get-tuple-element.477), channel_id=1, source_target_pairs={{0,8},{8,0},{1,9},{9,1},{2,10},{10,2},{3,11},{11,3},{4,12},{12,4},... | collective-permute-start | bytes 3145736 | tf_op jit(solution)/shard_map/ppermute | solution.py:73
  354.0 24.3 %collective-permute-start.11 = (bf16[2,2,2,128,2,256]{5,3,4,2,1,0:T(8,128)(2,1)}, bf16[2,2,2,128,2,256]{5,3,4,2,1,0:T(8,128)(2,1)}, u32[]{:S(2)}, u32[]{:S(2)}) collective-permute-start(bf16[2,2,2,128,2,256]{5,3,4,2,1,0:T(8,128)(2,1)} %get-tuple-element.473), channel_id=1, source_target_pairs={{0,4},{4,0},{1,5},{5,1},{2,6},{6,2},{3,7},{7,3},{8,12},{12,8},{9,1... | collective-permute-start | bytes 3145736 | tf_op jit(solution)/shard_map/ppermute | solution.py:73
  420.9 25.4 %collective-permute-start.19 = (bf16[256,2048]{1,0:T(8,128)(2,1)}, bf16[256,2048]{1,0:T(8,128)(2,1)S(1)}, u32[]{:S(2)}, u32[]{:S(2)}) collective-permute-start(bf16[256,2048]{1,0:T(8,128)(2,1)} %multiply_convert_fusion.8), channel_id=1, source_target_pairs={{0,4},{4,0},{1,5},{5,1},{2,6},{6,2},{3,7},{7,3},{8,12},{12,8},{9,1... | collective-permute-start | bytes 3145736 | tf_op jit(solution)/shard_map/ppermute | solution.py:73
  421.5 25.1 %collective-permute-start.20 = (bf16[256,2048]{1,0:T(8,128)(2,1)}, bf16[256,2048]{1,0:T(8,128)(2,1)S(1)}, u32[]{:S(2)}, u32[]{:S(2)}) collective-permute-start(bf16[256,2048]{1,0:T(8,128)(2,1)} %multiply_convert_fusion.8), channel_id=1, source_target_pairs={{0,8},{8,0},{1,9},{9,1},{2,10},{10,2},{3,11},{11,3},{4,12},{12,4},... | collective-permute-start | bytes 3145736 | tf_op jit(solution)/shard_map/ppermute | solution.py:73
  451.4 62.1 %collective-permute-start.22 = (bf16[256,2048]{1,0:T(8,128)(2,1)S(1)}, bf16[256,2048]{1,0:T(8,128)(2,1)}, u32[]{:S(2)}, u32[]{:S(2)}) collective-permute-start(bf16[256,2048]{1,0:T(8,128)(2,1)S(1)} %slice.557), channel_id=1, source_target_pairs={{0,1},{1,0},{2,3},{3,2},{4,5},{5,4},{6,7},{7,6},{8,9},{9,8},{10,11... | collective-permute-start | bytes 3145736 | tf_op jit(solution)/shard_map/ppermute | solution.py:73
  508.9 24.8 %collective-permute-start.34 = (bf16[256,2048]{1,0:T(8,128)(2,1)S(1)}, bf16[256,2048]{1,0:T(8,128)(2,1)S(1)}, u32[]{:S(2)}, u32[]{:S(2)}) collective-permute-start(bf16[256,2048]{1,0:T(8,128)(2,1)S(1)} %pad_maximum_fusion.21), channel_id=1, source_target_pairs={{0,4},{4,0},{1,5},{5,1},{2,6},{6,2},{3,7},{7,3},{8,12},{12,8},{9,1... | collective-permute-start | bytes 3145736 | tf_op jit(solution)/shard_map/ppermute | solution.py:73
  510.6 24.6 %collective-permute-start.30 = (bf16[256,2048]{1,0:T(8,128)(2,1)S(1)}, bf16[256,2048]{1,0:T(8,128)(2,1)S(1)}, u32[]{:S(2)}, u32[]{:S(2)}) collective-permute-start(bf16[256,2048]{1,0:T(8,128)(2,1)S(1)} %pad_maximum_fusion.20), channel_id=1, source_target_pairs={{0,8},{8,0},{1,9},{9,1},{2,10},{10,2},{3,11},{11,3},{4,12},{12,4},... | collective-permute-start | bytes 3145736 | tf_op jit(solution)/shard_map/ppermute | solution.py:73
  550.8 25.6 %collective-permute-start.36 = (bf16[256,2048]{1,0:T(8,128)(2,1)S(1)}, bf16[256,2048]{1,0:T(8,128)(2,1)S(1)}, u32[]{:S(2)}, u32[]{:S(2)}) collective-permute-start(bf16[256,2048]{1,0:T(8,128)(2,1)S(1)} %fusion.111), channel_id=1, source_target_pairs={{0,4},{4,0},{1,5},{5,1},{2,6},{6,2},{3,7},{7,3},{8,12},{12,8},{9,1... | collective-permute-start | bytes 3145736 | tf_op jit(solution)/shard_map/ppermute | solution.py:73
  551.4 25.3 %collective-permute-start.37 = (bf16[256,2048]{1,0:T(8,128)(2,1)S(1)}, bf16[256,2048]{1,0:T(8,128)(2,1)S(1)}, u32[]{:S(2)}, u32[]{:S(2)}) collective-permute-start(bf16[256,2048]{1,0:T(8,128)(2,1)S(1)} %fusion.111), channel_id=1, source_target_pairs={{0,8},{8,0},{1,9},{9,1},{2,10},{10,2},{3,11},{11,3},{4,12},{12,4},... | collective-permute-start | bytes 3145736 | tf_op jit(solution)/shard_map/ppermute | solution.py:73
  580.1 30.9 %collective-permute-start.39 = (bf16[256,2048]{1,0:T(8,128)(2,1)S(1)}, bf16[256,2048]{1,0:T(8,128)(2,1)S(1)}, u32[]{:S(2)}, u32[]{:S(2)}) collective-permute-start(bf16[256,2048]{1,0:T(8,128)(2,1)S(1)} %collective-permute-done.37), channel_id=1, source_target_pairs={{0,1},{1,0},{2,3},{3,2},{4,5},{5,4},{6,7},{7,6},{8,9},{9,8},{10,11... | collective-permute-start | bytes 3145736 | tf_op jit(solution)/shard_map/ppermute | solution.py:73
  580.2 47.8 %collective-permute-start.43 = (bf16[256,2048]{1,0:T(8,128)(2,1)S(1)}, bf16[256,2048]{1,0:T(8,128)(2,1)}, u32[]{:S(2)}, u32[]{:S(2)}) collective-permute-start(bf16[256,2048]{1,0:T(8,128)(2,1)S(1)} %slice.581), channel_id=1, source_target_pairs={{0,1},{1,0},{2,3},{3,2},{4,5},{5,4},{6,7},{7,6},{8,9},{9,8},{10,11... | collective-permute-start | bytes 3145736 | tf_op jit(solution)/shard_map/ppermute | solution.py:73
  592.6 37.2 %collective-permute-start.42 = (bf16[256,2048]{1,0:T(8,128)(2,1)S(1)}, bf16[256,2048]{1,0:T(8,128)(2,1)S(1)}, u32[]{:S(2)}, u32[]{:S(2)}) collective-permute-start(bf16[256,2048]{1,0:T(8,128)(2,1)S(1)} %pad_maximum_fusion.22), channel_id=1, source_target_pairs={{0,1},{1,0},{2,3},{3,2},{4,5},{5,4},{6,7},{7,6},{8,9},{9,8},{10,11... | collective-permute-start | bytes 3145736 | tf_op jit(solution)/shard_map/ppermute | solution.py:73
  611.0 30.6 %collective-permute-start.44 = (bf16[256,2048]{1,0:T(8,128)(2,1)}, bf16[256,2048]{1,0:T(8,128)(2,1)}, u32[]{:S(2)}, u32[]{:S(2)}) collective-permute-start(bf16[256,2048]{1,0:T(8,128)(2,1)} %slice.729), channel_id=1, source_target_pairs={{0,1},{1,0},{2,3},{3,2},{4,5},{5,4},{6,7},{7,6},{8,9},{9,8},{10,11... | collective-permute-start | bytes 3145736 | tf_op jit(solution)/shard_map/ppermute | solution.py:73
  645.2 25.7 %collective-permute-start.49 = (bf16[128,2048]{1,0:T(8,128)(2,1)S(1)}, bf16[128,2048]{1,0:T(8,128)(2,1)S(1)}, u32[]{:S(2)}, u32[]{:S(2)}) collective-permute-start(bf16[128,2048]{1,0:T(8,128)(2,1)S(1)} %get-tuple-element.469), channel_id=1, source_target_pairs={{0,8},{8,0},{1,9},{9,1},{2,10},{10,2},{3,11},{11,3},{4,12},{12,4},... | collective-permute-start | bytes 1572872 | tf_op jit(solution)/shard_map/ppermute | solution.py:73
  646.0 27.5 %collective-permute-start.47 = (bf16[128,2048]{1,0:T(8,128)(2,1)S(1)}, bf16[128,2048]{1,0:T(8,128)(2,1)S(1)}, u32[]{:S(2)}, u32[]{:S(2)}) collective-permute-start(bf16[128,2048]{1,0:T(8,128)(2,1)S(1)} %get-tuple-element.468), channel_id=1, source_target_pairs={{0,4},{4,0},{1,5},{5,1},{2,6},{6,2},{3,7},{7,3},{8,12},{12,8},{9,1... | collective-permute-start | bytes 1572872 | tf_op jit(solution)/shard_map/ppermute | solution.py:73
  672.0 26.1 %collective-permute-start.50 = (bf16[256,2048]{1,0:T(8,128)(2,1)}, bf16[256,2048]{1,0:T(8,128)(2,1)}, u32[]{:S(2)}, u32[]{:S(2)}) collective-permute-start(bf16[256,2048]{1,0:T(8,128)(2,1)} %pad_maximum_fusion.24), channel_id=1, source_target_pairs={{0,4},{4,0},{1,5},{5,1},{2,6},{6,2},{3,7},{7,3},{8,12},{12,8},{9,1... | collective-permute-start | bytes 3145736 | tf_op jit(solution)/shard_map/ppermute | solution.py:73
  674.7 24.8 %collective-permute-start.48 = (bf16[256,2048]{1,0:T(8,128)(2,1)}, bf16[256,2048]{1,0:T(8,128)(2,1)S(1)}, u32[]{:S(2)}, u32[]{:S(2)}) collective-permute-start(bf16[256,2048]{1,0:T(8,128)(2,1)} %pad_maximum_fusion.23), channel_id=1, source_target_pairs={{0,8},{8,0},{1,9},{9,1},{2,10},{10,2},{3,11},{11,3},{4,12},{12,4},... | collective-permute-start | bytes 3145736 | tf_op jit(solution)/shard_map/ppermute | solution.py:73
  758.4 48.0 %collective-permute-start.52 = (bf16[512,2048]{1,0:T(8,128)(2,1)S(1)}, bf16[512,2048]{1,0:T(8,128)(2,1)S(1)}, u32[]{:S(2)}, u32[]{:S(2)}) collective-permute-start(bf16[512,2048]{1,0:T(8,128)(2,1)S(1)} %slice.601), channel_id=1, source_target_pairs={{0,4},{4,0},{1,5},{5,1},{2,6},{6,2},{3,7},{7,3},{8,12},{12,8},{9,1... | collective-permute-start | bytes 6291464 | tf_op jit(solution)/shard_map/ppermute | solution.py:73
  817.2 39.8 %collective-permute-start.55 = (bf16[2,2,2,128,2,256]{5,3,4,2,1,0:T(8,128)(2,1)}, bf16[2,2,2,128,2,256]{5,3,4,2,1,0:T(8,128)(2,1)}, u32[]{:S(2)}, u32[]{:S(2)}) collective-permute-start(bf16[2,2,2,128,2,256]{5,3,4,2,1,0:T(8,128)(2,1)} %slice_bitcast_fusion), channel_id=1, source_target_pairs={{0,4},{4,0},{1,5},{5,1},{2,6},{6,2},{3,7},{7,3},{8,12},{12,8},{9,1... | collective-permute-start | bytes 3145736 | tf_op jit(solution)/shard_map/ppermute | solution.py:73
  837.8 75.1 %collective-permute-start.58 = (bf16[1024,2048]{1,0:T(8,128)(2,1)S(1)}, bf16[1024,2048]{1,0:T(8,128)(2,1)S(1)}, u32[]{:S(2)}, u32[]{:S(2)}) collective-permute-start(bf16[1024,2048]{1,0:T(8,128)(2,1)S(1)} %convolution_convert_fusion.2), channel_id=1, source_target_pairs={{0,1},{1,0},{2,3},{3,2},{4,5},{5,4},{6,7},{7,6},{8,9},{9,8},{10,11... | collective-permute-start | bytes 12582920 | tf_op jit(solution)/shard_map/ppermute | solution.py:73
  845.3 42.6 %collective-permute-start.53 = (bf16[2,2,2,128,2,256]{5,3,4,2,1,0:T(8,128)(2,1)S(1)}, bf16[2,2,2,128,2,256]{5,3,4,2,1,0:T(8,128)(2,1)S(1)}, u32[]{:S(2)}, u32[]{:S(2)}) collective-permute-start(bf16[2,2,2,128,2,256]{5,3,4,2,1,0:T(8,128)(2,1)S(1)} %bitcast.474), channel_id=1, source_target_pairs={{0,8},{8,0},{1,9},{9,1},{2,10},{10,2},{3,11},{11,3},{4,12},{12,4},... | collective-permute-start | bytes 3145736 | tf_op jit(solution)/shard_map/ppermute | solution.py:73
  846.4 43.4 %collective-permute-start.60 = (bf16[1024,512]{1,0:T(8,128)(2,1)S(1)}, bf16[1024,512]{1,0:T(8,128)(2,1)S(1)}, u32[]{:S(2)}, u32[]{:S(2)}) collective-permute-start(bf16[1024,512]{1,0:T(8,128)(2,1)S(1)} %pad_maximum_fusion.25), channel_id=1, source_target_pairs={{0,1},{1,0},{2,3},{3,2},{4,5},{5,4},{6,7},{7,6},{8,9},{9,8},{10,11... | collective-permute-start | bytes 3145736 | tf_op jit(solution)/shard_map/ppermute | solution.py:73
  859.4 49.6 %collective-permute-start.56 = (bf16[2,2,128,2,256]{4,2,3,1,0:T(8,128)(2,1)S(1)}, bf16[2,2,128,2,256]{4,2,3,1,0:T(8,128)(2,1)S(1)}, u32[]{:S(2)}, u32[]{:S(2)}) collective-permute-start(bf16[2,2,128,2,256]{4,2,3,1,0:T(8,128)(2,1)S(1)} %slice_bitcast_fusion.4), channel_id=1, source_target_pairs={{0,8},{8,0},{1,9},{9,1},{2,10},{10,2},{3,11},{11,3},{4,12},{12,4},... | collective-permute-start | bytes 1572872 | tf_op jit(solution)/shard_map/ppermute | solution.py:73
  890.2 24.8 %collective-permute-start.61 = (bf16[512,512]{1,0:T(8,128)(2,1)S(1)}, bf16[512,512]{1,0:T(8,128)(2,1)S(1)}, u32[]{:S(2)}, u32[]{:S(2)}) collective-permute-start(bf16[512,512]{1,0:T(8,128)(2,1)S(1)} %slice.761), channel_id=1, source_target_pairs={{0,4},{4,0},{1,5},{5,1},{2,6},{6,2},{3,7},{7,3},{8,12},{12,8},{9,1... | collective-permute-start | bytes 1572872 | tf_op jit(solution)/shard_map/ppermute | solution.py:73
  909.4 36.3 %collective-permute-start.57 = (bf16[2,2,128,2,256]{4,2,3,1,0:T(8,128)(2,1)S(1)}, bf16[2,2,128,2,256]{4,2,3,1,0:T(8,128)(2,1)S(1)}, u32[]{:S(2)}, u32[]{:S(2)}) collective-permute-start(bf16[2,2,128,2,256]{4,2,3,1,0:T(8,128)(2,1)S(1)} %fusion.211), channel_id=1, source_target_pairs={{0,16},{16,0},{1,17},{17,1},{2,18},{18,2},{3,19},{19,3},{4,20},{20... | collective-permute-start | bytes 1572872 | tf_op jit(solution)/shard_map/ppermute | solution.py:73
  914.6 45.4 %collective-permute-start.59 = (bf16[512,2048]{1,0:T(8,128)(2,1)S(1)}, bf16[512,2048]{1,0:T(8,128)(2,1)S(1)}, u32[]{:S(2)}, u32[]{:S(2)}) collective-permute-start(bf16[512,2048]{1,0:T(8,128)(2,1)S(1)} %slice.755), channel_id=1, source_target_pairs={{0,4},{4,0},{1,5},{5,1},{2,6},{6,2},{3,7},{7,3},{8,12},{12,8},{9,1... | collective-permute-start | bytes 6291464 | tf_op jit(solution)/shard_map/ppermute | solution.py:73
  967.6 76.1 %collective-permute-start.64 = (bf16[256,2048]{1,0:T(8,128)(2,1)}, bf16[256,2048]{1,0:T(8,128)(2,1)}, u32[]{:S(2)}, u32[]{:S(2)}) collective-permute-start(bf16[256,2048]{1,0:T(8,128)(2,1)} %get-tuple-element.458), channel_id=1, source_target_pairs={{0,2},{2,0},{1,3},{3,1},{4,6},{6,4},{5,7},{7,5},{8,10},{10,8},{9,1... | collective-permute-start | bytes 3145736 | tf_op jit(solution)/shard_map/ppermute | solution.py:73
  971.9 76.3 %collective-permute-start.67 = (bf16[256,2560]{1,0:T(8,128)(2,1)}, bf16[256,2560]{1,0:T(8,128)(2,1)}, u32[]{:S(2)}, u32[]{:S(2)}) collective-permute-start(bf16[256,2560]{1,0:T(8,128)(2,1)} %get-tuple-element.452), channel_id=1, source_target_pairs={{0,2},{2,0},{1,3},{3,1},{4,6},{6,4},{5,7},{7,5},{8,10},{10,8},{9,1... | collective-permute-start | bytes 3932168 | tf_op jit(solution)/shard_map/ppermute | solution.py:73
  975.2 124.0 %all-to-all-start.1 = ((bf16[8,192,1024]{2,1,0:T(8,128)(2,1)}), bf16[8,192,1024]{2,1,0:T(8,128)(2,1)}, u32[]{:S(2)}, u32[]{:S(2)}) async-start(bf16[8,192,1024]{2,1,0:T(8,128)(2,1)} %pad_maximum_fusion.2), calls=%async_computation.2 | async-start | bytes 6291456 | tf_op jit(solution)/shard_map/all_to_all | solution.py:203
  1000.4 41.6 %collective-permute-start.63 = (bf16[512,1152]{0,1:T(8,128)(2,1)}, bf16[512,1152]{0,1:T(8,128)(2,1)}, u32[]{:S(2)}, u32[]{:S(2)}) collective-permute-start(bf16[512,1152]{0,1:T(8,128)(2,1)} %slice.631), channel_id=1, source_target_pairs={{0,4},{4,0},{1,5},{5,1},{2,6},{6,2},{3,7},{7,3},{8,12},{12,8},{9,1... | collective-permute-start | bytes 3538952 | tf_op jit(solution)/shard_map/ppermute | solution.py:73
  1049.9 30.1 %collective-permute-start.68 = (bf16[128,2560]{1,0:T(8,128)(2,1)S(1)}, bf16[128,2560]{1,0:T(8,128)(2,1)S(1)}, u32[]{:S(2)}, u32[]{:S(2)}) collective-permute-start(bf16[128,2560]{1,0:T(8,128)(2,1)S(1)} %slice.775), channel_id=1, source_target_pairs={{0,8},{8,0},{1,9},{9,1},{2,10},{10,2},{3,11},{11,3},{4,12},{12,4},... | collective-permute-start | bytes 1966088 | tf_op jit(solution)/shard_map/ppermute | solution.py:73
  1061.9 26.7 %collective-permute-start.71 = (bf16[128,1152]{0,1:T(8,128)(2,1)S(1)}, bf16[128,1152]{0,1:T(8,128)(2,1)S(1)}, u32[]{:S(2)}, u32[]{:S(2)}) collective-permute-start(bf16[128,1152]{0,1:T(8,128)(2,1)S(1)} %slice.779), channel_id=1, source_target_pairs={{0,8},{8,0},{1,9},{9,1},{2,10},{10,2},{3,11},{11,3},{4,12},{12,4},... | collective-permute-start | bytes 884744 | tf_op jit(solution)/shard_map/ppermute | solution.py:73
  (239 other events, 3734.4 us)
Sparse Core Ops, SparseCore 0:
  76.9 249.1 all-gather.1
  702.7 239.1 reduce-scatter.1

commit v14 on v13

--- a/solution.py
+++ b/solution.py
@@ -582,14 +582,16 @@
     query_kept, query_away = plan.spread_send(query_sum, steps[1])
     output_kept, output_away = plan.spread_send(output_sum, steps[1])
     kvl_sum = plan.spread_step(kvl_sum, steps[:1])
+    d_spread = d_spread + product_nt_split(d_kvl_low, kvl_full)
+    kvl_sum, query_kept, output_kept, d_spread = together(
+        kvl_sum, query_kept, output_kept, d_spread
+    )
     feed_rows = plan.to_rows(jnp.split(feed_sum, 3), local_rows)
-    kvl_sum, query_kept, output_kept = together(kvl_sum, query_kept, output_kept)
     query_sum = (query_kept + query_away).astype(BF16)
     output_sum = (output_kept + output_away).astype(BF16)
     kvl_sum = plan.spread_step(kvl_sum, steps[1:2])
     query_sum = plan.spread_step(query_sum, steps[2:3])
     output_sum = plan.spread_step(output_sum, steps[2:3])
-    d_spread = d_spread + product_nt_split(d_kvl_low, kvl_full)
     d_normed = d_normed + reorder(d_spread, to_spread)
     d_inputs_norm, grad_norm_input = pre_pull(d_normed)
     grad_tokens = reorder(d_inputs + d_inputs_norm, to_far_team).reshape(batch, block, width)

time: 1150 us -> 1160 us (level)
  transfers between devices with their start and end apart: 82 -> 82, of which waited for: 38 -> 38; matrix products, arithmetic and copies ran while one was open for 41% -> 40% of each run, Pallas kernels for 0% -> 0%
where the time goes in v14:
time: 1160 us; the launch traced here: 1150 us
  waiting for transfers between devices  518 us (45%)
  matrix products  264 us (23%)
  local copies, waits for them, and re-layouts  141 us (12%)
  other arithmetic  128 us (11%)
  starting transfers between devices  77.8 us (7%)
  between operations  18.4 us (2%)
    ppermute x78, waiting for transfers between devices, swap(): return lax.ppermute(value, axis, [(0, 1), (1, 0)])  517 us
    dot_general x33, matrix products, product(): return jnp.dot(left, right, preferred_element_type=F32)  103 us
    dot_general x31, matrix products, product_nt(): lax.dot_general(left, right, (((1,), (1,)), ((), ())), preferred_element_...  91.7 us
    ppermute x78, starting transfers between devices, swap(): return lax.ppermute(value, axis, [(0, 1), (1, 0)])  67.7 us
    dot_general x15, matrix products, product_tn(): lax.dot_general(left, right, (((0,), (0,)), ((), ())), preferred_element_...  55.2 us
    unnamed x454, local copies, waits for them, and re-layouts  50.3 us
  transfers between devices with their start and end apart: 82, of which 38 were waited for; matrix products, arithmetic and copies ran while one was open for 40% of the time, Pallas kernels for 0%

profile of v14, /device:TPU:0, one launch (start us, length us, event | category | flops | bytes accessed | tf_op | source)
XLA Modules:
  0.0 1147.6 jit_solution(17103812883897486768)
XLA Ops:
  14.4 5.4 all-to-all-start
  24.6 45.8 %collective-permute-done = bf16[64,5760]{1,0:T(8,128)(2,1)} collective-permute-done((bf16[64,5760]{1,0:T(8,128)(2,1)S(1)}, bf16[64,5760]{1,0:T(8,128)(2,1)}, u32[]{:S(2)}, u32[]{:S(2)}) %collective-permute-start) | collective-permute-done | bytes 737312 | tf_op jit(solution)/shard_map/ppermute | solution.py:73
  77.6 4.4 collective-permute-start.1
  82.3 55.7 %collective-permute-done.1 = bf16[128,5760]{1,0:T(8,128)(2,1)S(1)} collective-permute-done((bf16[128,5760]{1,0:T(8,128)(2,1)S(1)}, bf16[128,5760]{1,0:T(8,128)(2,1)S(1)}, u32[]{:S(2)}, u32[]{:S(2)}) %collective-permute-start.1) | collective-permute-done | bytes 1474592 | tf_op jit(solution)/shard_map/ppermute | solution.py:73
  140.5 9.0 collective-permute-done.2
  152.4 4.5 multiply_reduce_fusion.18
  158.7 15.3 %collective-permute-done.3 = bf16[512,1152]{1,0:T(8,128)(2,1)} collective-permute-done((bf16[512,1152]{1,0:T(8,128)(2,1)}, bf16[512,1152]{1,0:T(8,128)(2,1)}, u32[]{:S(2)}, u32[]{:S(2)}) %collective-permute-start.3) | collective-permute-done | bytes 1179680 | tf_op jit(solution)/shard_map/ppermute | solution.py:73
  177.3 5.2 fusion.76
  185.4 7.8 collective-permute-done.13
  208.0 6.0 rev.69
  246.4 26.3 %collective-permute-done.6 = bf16[256,2560]{1,0:T(8,128)(2,1)} collective-permute-done((bf16[256,2560]{1,0:T(8,128)(2,1)}, bf16[256,2560]{1,0:T(8,128)(2,1)}, u32[]{:S(2)}, u32[]{:S(2)}) %collective-permute-start.6) | collective-permute-done | bytes 1310752 | tf_op jit(solution)/shard_map/ppermute | solution.py:73
  281.2 32.3 %collective-permute-done.7 = bf16[2,1,2,128,2,256]{5,3,4,2,1,0:T(8,128)(2,1)S(1)} collective-permute-done((bf16[2,1,2,128,2,256]{5,3,4,2,1,0:T(8,128)(2,1)S(1)}, bf16[2,1,2,128,2,256]{5,3,4,2,1,0:T(8,128)(2,1)S(1)}, u32[]{:S(2)}, u32[]{:S(2)}) %collective-permute-start.7) | collective-permute-done | bytes 524320 | tf_op jit(solution)/shard_map/ppermute | solution.py:73
  318.9 29.5 %collective-permute-done.8 = bf16[1,2,2,128,2,256]{5,3,4,2,1,0:T(8,128)(2,1)S(1)} collective-permute-done((bf16[1,2,2,128,2,256]{5,3,4,2,1,0:T(8,128)(2,1)S(1)}, bf16[1,2,2,128,2,256]{5,3,4,2,1,0:T(8,128)(2,1)S(1)}, u32[]{:S(2)}, u32[]{:S(2)}) %collective-permute-start.8) | collective-permute-done | bytes 524320 | tf_op jit(solution)/shard_map/ppermute | solution.py:73
  359.5 15.9 %collective-permute-done.9 = bf16[2,2,2,128,2,256]{5,3,4,2,1,0:T(8,128)(2,1)} collective-permute-done((bf16[2,2,2,128,2,256]{5,3,4,2,1,0:T(8,128)(2,1)}, bf16[2,2,2,128,2,256]{5,3,4,2,1,0:T(8,128)(2,1)}, u32[]{:S(2)}, u32[]{:S(2)}) %collective-permute-start.9) | collective-permute-done | bytes 1048608 | tf_op jit(solution)/shard_map/ppermute | solution.py:73
  405.2 4.7 fusion.5
  423.3 5.8 fusion.274
  433.0 6.3 multiply_convert_fusion.7
  441.7 4.6 collective-permute-done.19
  451.6 7.9 collective-permute-done.25
  496.7 12.0 %collective-permute-done.33 = bf16[128,2048]{1,0:T(8,128)(2,1)S(1)} collective-permute-done((bf16[128,2048]{1,0:T(8,128)(2,1)S(1)}, bf16[128,2048]{1,0:T(8,128)(2,1)S(1)}, u32[]{:S(2)}, u32[]{:S(2)}) %collective-permute-start.33) | collective-permute-done | bytes 524320 | tf_op jit(solution)/shard_map/ppermute | solution.py:73
  513.5 20.2 %collective-permute-done.34 = bf16[256,2048]{1,0:T(8,128)(2,1)S(1)} collective-permute-done((bf16[256,2048]{1,0:T(8,128)(2,1)S(1)}, bf16[256,2048]{1,0:T(8,128)(2,1)S(1)}, u32[]{:S(2)}, u32[]{:S(2)}) %collective-permute-start.34) | collective-permute-done | bytes 1048608 | tf_op jit(solution)/shard_map/ppermute | solution.py:73
  552.8 4.7 multiply_convert_fusion.3
  561.8 4.6 add_convert_fusion.8
  566.4 10.0 collective-permute-done.36
  582.2 9.0 collective-permute-done.40
  595.2 5.2 multiply_convert_fusion.2
  604.9 5.0 add_convert_fusion.7
  612.5 5.4 multiply_convert_fusion.1
  622.3 4.6 add_convert_fusion.6
  648.0 10.9 fusion.58
  658.9 11.8 %fusion.61 = bf16[2048,1024]{1,0:T(8,128)(2,1)} fusion(bf16[2048,2048]{1,0:T(8,128)(2,1)S(1)} %constant_dynamic-update-slice_fusion.22, bf16[512,1024]{1,0:T(8,128)(2,1)} %copy-done.184, bf16[512,1024]{1,0:T(8,128)(2,1)S(1)} %copy-done.183, bf16[512,1024]{1,0:T(8,128)(2,1)S(1)} %copy-done.181, bf16[512,1024]{1,0:T(8,128)(2,1)S(1)} %copy-done.179), kind=kOutput, calls=%fused_computation.76 | convolution fusion | flops 8608808960 | bytes 16777216 | tf_op jit(solution)/shard_map/dot_general | solution.py:34
  675.2 13.9 %fusion.64 = bf16[2048,1024]{1,0:T(8,128)(2,1)} fusion(bf16[512,1024]{1,0:T(8,128)(2,1)} %copy-done.198, bf16[512,1024]{1,0:T(8,128)(2,1)} %get-tuple-element.137, bf16[512,1024]{1,0:T(8,128)(2,1)} %copy-done.196, bf16[512,1024]{1,0:T(8,128)(2,1)} %copy-done.195, bf16[512,2048]{1,0:T(8,128)(2,1)} %copy-done.95, bf16[512,2048]{1,0:T(8,128)(2,1)} %copy-done.84, ...), kind=kOutput, calls=%fused_computation.77 | convolution fusion | flops 8642363392 | bytes 16777216 | tf_op jit(solution)/shard_map/dot_general | solution.py:34
  689.1 9.0 pad_maximum_fusion
  723.2 5.0 fusion.75
  739.4 5.4 add_convert_fusion.1
  759.2 5.1 fusion.19
  775.4 30.9 %collective-permute-done.52 = bf16[512,2048]{1,0:T(8,128)(2,1)S(1)} collective-permute-done((bf16[512,2048]{1,0:T(8,128)(2,1)S(1)}, bf16[512,2048]{1,0:T(8,128)(2,1)S(1)}, u32[]{:S(2)}, u32[]{:S(2)}) %collective-permute-start.52) | collective-permute-done | bytes 2097184 | tf_op jit(solution)/shard_map/ppermute | solution.py:73
  838.1 5.3 fusion.69
  859.3 28.6 %collective-permute-done.53 = bf16[2,2,2,128,2,256]{5,3,4,2,1,0:T(8,128)(2,1)S(1)} collective-permute-done((bf16[2,2,2,128,2,256]{5,3,4,2,1,0:T(8,128)(2,1)S(1)}, bf16[2,2,2,128,2,256]{5,3,4,2,1,0:T(8,128)(2,1)S(1)}, u32[]{:S(2)}, u32[]{:S(2)}) %collective-permute-start.53) | collective-permute-done | bytes 1048608 | tf_op jit(solution)/shard_map/ppermute | solution.py:73
  890.8 18.2 %collective-permute-done.56 = bf16[2,2,128,2,256]{4,2,3,1,0:T(8,128)(2,1)S(1)} collective-permute-done((bf16[2,2,128,2,256]{4,2,3,1,0:T(8,128)(2,1)S(1)}, bf16[2,2,128,2,256]{4,2,3,1,0:T(8,128)(2,1)S(1)}, u32[]{:S(2)}, u32[]{:S(2)}) %collective-permute-start.56) | collective-permute-done | bytes 524320 | tf_op jit(solution)/shard_map/ppermute | solution.py:73
  915.9 29.7 %collective-permute-done.57 = bf16[2,2,128,2,256]{4,2,3,1,0:T(8,128)(2,1)S(1)} collective-permute-done((bf16[2,2,128,2,256]{4,2,3,1,0:T(8,128)(2,1)S(1)}, bf16[2,2,128,2,256]{4,2,3,1,0:T(8,128)(2,1)S(1)}, u32[]{:S(2)}, u32[]{:S(2)}) %collective-permute-start.57) | collective-permute-done | bytes 524320 | tf_op jit(solution)/shard_map/ppermute | solution.py:73
  948.1 11.8 %collective-permute-done.59 = bf16[512,2048]{1,0:T(8,128)(2,1)S(1)} collective-permute-done((bf16[512,2048]{1,0:T(8,128)(2,1)S(1)}, bf16[512,2048]{1,0:T(8,128)(2,1)S(1)}, u32[]{:S(2)}, u32[]{:S(2)}) %collective-permute-start.59) | collective-permute-done | bytes 2097184 | tf_op jit(solution)/shard_map/ppermute | solution.py:73
  997.1 46.8 %collective-permute-done.63 = bf16[512,1152]{0,1:T(8,128)(2,1)S(1)} collective-permute-done((bf16[512,1152]{0,1:T(8,128)(2,1)S(1)}, bf16[512,1152]{0,1:T(8,128)(2,1)S(1)}, u32[]{:S(2)}, u32[]{:S(2)}) %collective-permute-start.63) | collective-permute-done | bytes 1179680 | tf_op jit(solution)/shard_map/ppermute | solution.py:73
  1045.8 4.7 fusion.1
  1062.0 4.9 fusion.7
  1075.6 14.3 %collective-permute-done.68 = bf16[128,2560]{1,0:T(8,128)(2,1)S(1)} collective-permute-done((bf16[128,2560]{1,0:T(8,128)(2,1)S(1)}, bf16[128,2560]{1,0:T(8,128)(2,1)S(1)}, u32[]{:S(2)}, u32[]{:S(2)}) %collective-permute-start.68) | collective-permute-done | bytes 655392 | tf_op jit(solution)/shard_map/ppermute | solution.py:73
  1091.0 7.4 collective-permute-done.71
  1098.5 10.5 collective-permute-done.69
  (953 shorter events, 481.8 us)
Async XLA Ops:
  14.4 58.2 %all-to-all-start = ((bf16[8,192,1024]{2,1,0:T(8,128)(2,1)}), bf16[8,192,1024]{2,1,0:T(8,128)(2,1)}, u32[]{:S(2)}, u32[]{:S(2)}) async-start(bf16[8,192,1024]{2,1,0:T(8,128)(2,1)} %copy.514), calls=%async_computation | async-start | bytes 6291456 | tf_op jit(solution)/shard_map/all_to_all | solution.py:322
  19.8 374.9 %all-gather.2.cloned.1.call-start = ((), (), s32[]{:S(2)}) async-start(), calls=%async_computation.3 | async-start | bytes 15728640 | tf_op jit(solution)/shard_map/all_gather | solution.py:332
  20.1 50.3 %collective-permute-start = (bf16[64,5760]{1,0:T(8,128)(2,1)S(1)}, bf16[64,5760]{1,0:T(8,128)(2,1)}, u32[]{:S(2)}, u32[]{:S(2)}) collective-permute-start(bf16[64,5760]{1,0:T(8,128)(2,1)S(1)} %concatenate.177), channel_id=1, source_target_pairs={{0,16},{16,0},{1,17},{17,1},{2,18},{18,2},{3,19},{19,3},{4,20},{20... | collective-permute-start | bytes 2211848 | tf_op jit(solution)/shard_map/ppermute | solution.py:73
  76.7 885.4 %reduce-scatter.2.cloned.1.call-start = ((), (), s32[]{:S(2)}) async-start(), calls=%async_computation.4 | async-start | bytes 15728640 | tf_op jit(solution)/shard_map/reduce_scatter | solution.py:503
  77.6 60.3 %collective-permute-start.1 = (bf16[128,5760]{1,0:T(8,128)(2,1)S(1)}, bf16[128,5760]{1,0:T(8,128)(2,1)S(1)}, u32[]{:S(2)}, u32[]{:S(2)}) collective-permute-start(bf16[128,5760]{1,0:T(8,128)(2,1)S(1)} %pad_maximum_fusion.14), channel_id=1, source_target_pairs={{0,8},{8,0},{1,9},{9,1},{2,10},{10,2},{3,11},{11,3},{4,12},{12,4},... | collective-permute-start | bytes 4423688 | tf_op jit(solution)/shard_map/ppermute | solution.py:73
  157.1 36.1 %collective-permute-start.13 = (bf16[256,2048]{1,0:T(8,128)(2,1)S(1)}, bf16[256,2048]{1,0:T(8,128)(2,1)}, u32[]{:S(2)}, u32[]{:S(2)}) collective-permute-start(bf16[256,2048]{1,0:T(8,128)(2,1)S(1)} %slice.701), channel_id=1, source_target_pairs={{0,2},{2,0},{1,3},{3,1},{4,6},{6,4},{5,7},{7,5},{8,10},{10,8},{9,1... | collective-permute-start | bytes 3145736 | tf_op jit(solution)/shard_map/ppermute | solution.py:73
  158.7 37.2 %collective-permute-start.4 = (bf16[512,1152]{1,0:T(8,128)(2,1)}, bf16[512,1152]{1,0:T(8,128)(2,1)}, u32[]{:S(2)}, u32[]{:S(2)}) collective-permute-start(bf16[512,1152]{1,0:T(8,128)(2,1)} %pad_maximum_fusion.15), channel_id=1, source_target_pairs={{0,1},{1,0},{2,3},{3,2},{4,5},{5,4},{6,7},{7,6},{8,9},{9,8},{10,11... | collective-permute-start | bytes 3538952 | tf_op jit(solution)/shard_map/ppermute | solution.py:73
  195.9 83.0 %collective-permute-start.15 = (bf16[512,2048]{1,0:T(8,128)(2,1)}, bf16[512,2048]{1,0:T(8,128)(2,1)}, u32[]{:S(2)}, u32[]{:S(2)}) collective-permute-start(bf16[512,2048]{1,0:T(8,128)(2,1)} %pad_maximum_fusion.7), channel_id=1, source_target_pairs={{0,1},{1,0},{2,3},{3,2},{4,5},{5,4},{6,7},{7,6},{8,9},{9,8},{10,11... | collective-permute-start | bytes 6291464 | tf_op jit(solution)/shard_map/ppermute | solution.py:73
  195.9 49.9 %collective-permute-start.14 = (bf16[512,2048]{1,0:T(8,128)(2,1)}, bf16[512,2048]{1,0:T(8,128)(2,1)}, u32[]{:S(2)}, u32[]{:S(2)}) collective-permute-start(bf16[512,2048]{1,0:T(8,128)(2,1)} %pad_maximum_fusion.7), channel_id=1, source_target_pairs={{0,4},{4,0},{1,5},{5,1},{2,6},{6,2},{3,7},{7,3},{8,12},{12,8},{9,1... | collective-permute-start | bytes 6291464 | tf_op jit(solution)/shard_map/ppermute | solution.py:73
  232.9 39.8 %collective-permute-start.6 = (bf16[256,2560]{1,0:T(8,128)(2,1)}, bf16[256,2560]{1,0:T(8,128)(2,1)}, u32[]{:S(2)}, u32[]{:S(2)}) collective-permute-start(bf16[256,2560]{1,0:T(8,128)(2,1)} %slice.691), channel_id=1, source_target_pairs={{0,2},{2,0},{1,3},{3,1},{4,6},{6,4},{5,7},{7,5},{8,10},{10,8},{9,1... | collective-permute-start | bytes 3932168 | tf_op jit(solution)/shard_map/ppermute | solution.py:73
  245.9 70.8 %collective-permute-start.16 = (bf16[512,2048]{1,0:T(8,128)(2,1)}, bf16[512,2048]{1,0:T(8,128)(2,1)S(1)}, u32[]{:S(2)}, u32[]{:S(2)}) collective-permute-start(bf16[512,2048]{1,0:T(8,128)(2,1)} %collective-permute-done.14), channel_id=1, source_target_pairs={{0,1},{1,0},{2,3},{3,2},{4,5},{5,4},{6,7},{7,6},{8,9},{9,8},{10,11... | collective-permute-start | bytes 6291464 | tf_op jit(solution)/shard_map/ppermute | solution.py:73
  275.7 37.9 %collective-permute-start.7 = (bf16[2,1,2,128,2,256]{5,3,4,2,1,0:T(8,128)(2,1)S(1)}, bf16[2,1,2,128,2,256]{5,3,4,2,1,0:T(8,128)(2,1)S(1)}, u32[]{:S(2)}, u32[]{:S(2)}) collective-permute-start(bf16[2,1,2,128,2,256]{5,3,4,2,1,0:T(8,128)(2,1)S(1)} %maximum_bitcast_fusion), channel_id=1, source_target_pairs={{0,16},{16,0},{1,17},{17,1},{2,18},{18,2},{3,19},{19,3},{4,20},{20... | collective-permute-start | bytes 1572872 | tf_op jit(solution)/shard_map/ppermute | solution.py:73
  278.1 103.6 %collective-permute-start.12 = (bf16[512,2560]{1,0:T(8,128)(2,1)}, bf16[512,2560]{1,0:T(8,128)(2,1)}, u32[]{:S(2)}, u32[]{:S(2)}) collective-permute-start(bf16[512,2560]{1,0:T(8,128)(2,1)} %pad_maximum_fusion.3), channel_id=1, source_target_pairs={{0,4},{4,0},{1,5},{5,1},{2,6},{6,2},{3,7},{7,3},{8,12},{12,8},{9,1... | collective-permute-start | bytes 7864328 | tf_op jit(solution)/shard_map/ppermute | solution.py:73
  313.7 34.7 %collective-permute-start.8 = (bf16[1,2,2,128,2,256]{5,3,4,2,1,0:T(8,128)(2,1)S(1)}, bf16[1,2,2,128,2,256]{5,3,4,2,1,0:T(8,128)(2,1)S(1)}, u32[]{:S(2)}, u32[]{:S(2)}) collective-permute-start(bf16[1,2,2,128,2,256]{5,3,4,2,1,0:T(8,128)(2,1)S(1)} %get-tuple-element.477), channel_id=1, source_target_pairs={{0,4},{4,0},{1,5},{5,1},{2,6},{6,2},{3,7},{7,3},{8,12},{12,8},{9,1... | collective-permute-start | bytes 1572872 | tf_op jit(solution)/shard_map/ppermute | solution.py:73
  316.5 85.6 %collective-permute-start.17 = (bf16[512,2560]{1,0:T(8,128)(2,1)}, bf16[512,2560]{1,0:T(8,128)(2,1)}, u32[]{:S(2)}, u32[]{:S(2)}) collective-permute-start(bf16[512,2560]{1,0:T(8,128)(2,1)} %pad_maximum_fusion.3), channel_id=1, source_target_pairs={{0,1},{1,0},{2,3},{3,2},{4,5},{5,4},{6,7},{7,6},{8,9},{9,8},{10,11... | collective-permute-start | bytes 7864328 | tf_op jit(solution)/shard_map/ppermute | solution.py:73
  316.6 36.0 %collective-permute-start.10 = (bf16[1,2,2,128,2,256]{5,3,4,2,1,0:T(8,128)(2,1)S(1)}, bf16[1,2,2,128,2,256]{5,3,4,2,1,0:T(8,128)(2,1)S(1)}, u32[]{:S(2)}, u32[]{:S(2)}) collective-permute-start(bf16[1,2,2,128,2,256]{5,3,4,2,1,0:T(8,128)(2,1)S(1)} %get-tuple-element.476), channel_id=1, source_target_pairs={{0,8},{8,0},{1,9},{9,1},{2,10},{10,2},{3,11},{11,3},{4,12},{12,4},... | collective-permute-start | bytes 1572872 | tf_op jit(solution)/shard_map/ppermute | solution.py:73
  349.9 25.6 %collective-permute-start.9 = (bf16[2,2,2,128,2,256]{5,3,4,2,1,0:T(8,128)(2,1)}, bf16[2,2,2,128,2,256]{5,3,4,2,1,0:T(8,128)(2,1)}, u32[]{:S(2)}, u32[]{:S(2)}) collective-permute-start(bf16[2,2,2,128,2,256]{5,3,4,2,1,0:T(8,128)(2,1)} %get-tuple-element.479), channel_id=1, source_target_pairs={{0,8},{8,0},{1,9},{9,1},{2,10},{10,2},{3,11},{11,3},{4,12},{12,4},... | collective-permute-start | bytes 3145736 | tf_op jit(solution)/shard_map/ppermute | solution.py:73
  354.0 24.3 %collective-permute-start.11 = (bf16[2,2,2,128,2,256]{5,3,4,2,1,0:T(8,128)(2,1)}, bf16[2,2,2,128,2,256]{5,3,4,2,1,0:T(8,128)(2,1)}, u32[]{:S(2)}, u32[]{:S(2)}) collective-permute-start(bf16[2,2,2,128,2,256]{5,3,4,2,1,0:T(8,128)(2,1)} %get-tuple-element.475), channel_id=1, source_target_pairs={{0,4},{4,0},{1,5},{5,1},{2,6},{6,2},{3,7},{7,3},{8,12},{12,8},{9,1... | collective-permute-start | bytes 3145736 | tf_op jit(solution)/shard_map/ppermute | solution.py:73
  420.9 25.4 %collective-permute-start.19 = (bf16[256,2048]{1,0:T(8,128)(2,1)}, bf16[256,2048]{1,0:T(8,128)(2,1)S(1)}, u32[]{:S(2)}, u32[]{:S(2)}) collective-permute-start(bf16[256,2048]{1,0:T(8,128)(2,1)} %multiply_convert_fusion.8), channel_id=1, source_target_pairs={{0,4},{4,0},{1,5},{5,1},{2,6},{6,2},{3,7},{7,3},{8,12},{12,8},{9,1... | collective-permute-start | bytes 3145736 | tf_op jit(solution)/shard_map/ppermute | solution.py:73
  421.5 25.1 %collective-permute-start.20 = (bf16[256,2048]{1,0:T(8,128)(2,1)}, bf16[256,2048]{1,0:T(8,128)(2,1)S(1)}, u32[]{:S(2)}, u32[]{:S(2)}) collective-permute-start(bf16[256,2048]{1,0:T(8,128)(2,1)} %multiply_convert_fusion.8), channel_id=1, source_target_pairs={{0,8},{8,0},{1,9},{9,1},{2,10},{10,2},{3,11},{11,3},{4,12},{12,4},... | collective-permute-start | bytes 3145736 | tf_op jit(solution)/shard_map/ppermute | solution.py:73
  451.4 62.1 %collective-permute-start.22 = (bf16[256,2048]{1,0:T(8,128)(2,1)S(1)}, bf16[256,2048]{1,0:T(8,128)(2,1)}, u32[]{:S(2)}, u32[]{:S(2)}) collective-permute-start(bf16[256,2048]{1,0:T(8,128)(2,1)S(1)} %slice.557), channel_id=1, source_target_pairs={{0,1},{1,0},{2,3},{3,2},{4,5},{5,4},{6,7},{7,6},{8,9},{9,8},{10,11... | collective-permute-start | bytes 3145736 | tf_op jit(solution)/shard_map/ppermute | solution.py:73
  508.9 24.8 %collective-permute-start.34 = (bf16[256,2048]{1,0:T(8,128)(2,1)S(1)}, bf16[256,2048]{1,0:T(8,128)(2,1)S(1)}, u32[]{:S(2)}, u32[]{:S(2)}) collective-permute-start(bf16[256,2048]{1,0:T(8,128)(2,1)S(1)} %pad_maximum_fusion.21), channel_id=1, source_target_pairs={{0,4},{4,0},{1,5},{5,1},{2,6},{6,2},{3,7},{7,3},{8,12},{12,8},{9,1... | collective-permute-start | bytes 3145736 | tf_op jit(solution)/shard_map/ppermute | solution.py:73
  510.6 24.6 %collective-permute-start.30 = (bf16[256,2048]{1,0:T(8,128)(2,1)S(1)}, bf16[256,2048]{1,0:T(8,128)(2,1)S(1)}, u32[]{:S(2)}, u32[]{:S(2)}) collective-permute-start(bf16[256,2048]{1,0:T(8,128)(2,1)S(1)} %pad_maximum_fusion.20), channel_id=1, source_target_pairs={{0,8},{8,0},{1,9},{9,1},{2,10},{10,2},{3,11},{11,3},{4,12},{12,4},... | collective-permute-start | bytes 3145736 | tf_op jit(solution)/shard_map/ppermute | solution.py:73
  550.8 25.6 %collective-permute-start.36 = (bf16[256,2048]{1,0:T(8,128)(2,1)S(1)}, bf16[256,2048]{1,0:T(8,128)(2,1)S(1)}, u32[]{:S(2)}, u32[]{:S(2)}) collective-permute-start(bf16[256,2048]{1,0:T(8,128)(2,1)S(1)} %fusion.111), channel_id=1, source_target_pairs={{0,4},{4,0},{1,5},{5,1},{2,6},{6,2},{3,7},{7,3},{8,12},{12,8},{9,1... | collective-permute-start | bytes 3145736 | tf_op jit(solution)/shard_map/ppermute | solution.py:73
  551.4 25.3 %collective-permute-start.37 = (bf16[256,2048]{1,0:T(8,128)(2,1)S(1)}, bf16[256,2048]{1,0:T(8,128)(2,1)S(1)}, u32[]{:S(2)}, u32[]{:S(2)}) collective-permute-start(bf16[256,2048]{1,0:T(8,128)(2,1)S(1)} %fusion.111), channel_id=1, source_target_pairs={{0,8},{8,0},{1,9},{9,1},{2,10},{10,2},{3,11},{11,3},{4,12},{12,4},... | collective-permute-start | bytes 3145736 | tf_op jit(solution)/shard_map/ppermute | solution.py:73
  580.1 30.9 %collective-permute-start.39 = (bf16[256,2048]{1,0:T(8,128)(2,1)S(1)}, bf16[256,2048]{1,0:T(8,128)(2,1)S(1)}, u32[]{:S(2)}, u32[]{:S(2)}) collective-permute-start(bf16[256,2048]{1,0:T(8,128)(2,1)S(1)} %collective-permute-done.37), channel_id=1, source_target_pairs={{0,1},{1,0},{2,3},{3,2},{4,5},{5,4},{6,7},{7,6},{8,9},{9,8},{10,11... | collective-permute-start | bytes 3145736 | tf_op jit(solution)/shard_map/ppermute | solution.py:73
  580.2 47.8 %collective-permute-start.43 = (bf16[256,2048]{1,0:T(8,128)(2,1)S(1)}, bf16[256,2048]{1,0:T(8,128)(2,1)}, u32[]{:S(2)}, u32[]{:S(2)}) collective-permute-start(bf16[256,2048]{1,0:T(8,128)(2,1)S(1)} %slice.581), channel_id=1, source_target_pairs={{0,1},{1,0},{2,3},{3,2},{4,5},{5,4},{6,7},{7,6},{8,9},{9,8},{10,11... | collective-permute-start | bytes 3145736 | tf_op jit(solution)/shard_map/ppermute | solution.py:73
  592.6 37.2 %collective-permute-start.42 = (bf16[256,2048]{1,0:T(8,128)(2,1)S(1)}, bf16[256,2048]{1,0:T(8,128)(2,1)S(1)}, u32[]{:S(2)}, u32[]{:S(2)}) collective-permute-start(bf16[256,2048]{1,0:T(8,128)(2,1)S(1)} %pad_maximum_fusion.22), channel_id=1, source_target_pairs={{0,1},{1,0},{2,3},{3,2},{4,5},{5,4},{6,7},{7,6},{8,9},{9,8},{10,11... | collective-permute-start | bytes 3145736 | tf_op jit(solution)/shard_map/ppermute | solution.py:73
  611.0 30.6 %collective-permute-start.44 = (bf16[256,2048]{1,0:T(8,128)(2,1)}, bf16[256,2048]{1,0:T(8,128)(2,1)}, u32[]{:S(2)}, u32[]{:S(2)}) collective-permute-start(bf16[256,2048]{1,0:T(8,128)(2,1)} %slice.729), channel_id=1, source_target_pairs={{0,1},{1,0},{2,3},{3,2},{4,5},{5,4},{6,7},{7,6},{8,9},{9,8},{10,11... | collective-permute-start | bytes 3145736 | tf_op jit(solution)/shard_map/ppermute | solution.py:73
  645.2 25.7 %collective-permute-start.49 = (bf16[128,2048]{1,0:T(8,128)(2,1)S(1)}, bf16[128,2048]{1,0:T(8,128)(2,1)S(1)}, u32[]{:S(2)}, u32[]{:S(2)}) collective-permute-start(bf16[128,2048]{1,0:T(8,128)(2,1)S(1)} %get-tuple-element.471), channel_id=1, source_target_pairs={{0,8},{8,0},{1,9},{9,1},{2,10},{10,2},{3,11},{11,3},{4,12},{12,4},... | collective-permute-start | bytes 1572872 | tf_op jit(solution)/shard_map/ppermute | solution.py:73
  646.0 27.5 %collective-permute-start.47 = (bf16[128,2048]{1,0:T(8,128)(2,1)S(1)}, bf16[128,2048]{1,0:T(8,128)(2,1)S(1)}, u32[]{:S(2)}, u32[]{:S(2)}) collective-permute-start(bf16[128,2048]{1,0:T(8,128)(2,1)S(1)} %get-tuple-element.470), channel_id=1, source_target_pairs={{0,4},{4,0},{1,5},{5,1},{2,6},{6,2},{3,7},{7,3},{8,12},{12,8},{9,1... | collective-permute-start | bytes 1572872 | tf_op jit(solution)/shard_map/ppermute | solution.py:73
  672.0 26.1 %collective-permute-start.50 = (bf16[256,2048]{1,0:T(8,128)(2,1)}, bf16[256,2048]{1,0:T(8,128)(2,1)}, u32[]{:S(2)}, u32[]{:S(2)}) collective-permute-start(bf16[256,2048]{1,0:T(8,128)(2,1)} %pad_maximum_fusion.24), channel_id=1, source_target_pairs={{0,4},{4,0},{1,5},{5,1},{2,6},{6,2},{3,7},{7,3},{8,12},{12,8},{9,1... | collective-permute-start | bytes 3145736 | tf_op jit(solution)/shard_map/ppermute | solution.py:73
  674.7 24.8 %collective-permute-start.48 = (bf16[256,2048]{1,0:T(8,128)(2,1)}, bf16[256,2048]{1,0:T(8,128)(2,1)S(1)}, u32[]{:S(2)}, u32[]{:S(2)}) collective-permute-start(bf16[256,2048]{1,0:T(8,128)(2,1)} %pad_maximum_fusion.23), channel_id=1, source_target_pairs={{0,8},{8,0},{1,9},{9,1},{2,10},{10,2},{3,11},{11,3},{4,12},{12,4},... | collective-permute-start | bytes 3145736 | tf_op jit(solution)/shard_map/ppermute | solution.py:73
  758.4 48.0 %collective-permute-start.52 = (bf16[512,2048]{1,0:T(8,128)(2,1)S(1)}, bf16[512,2048]{1,0:T(8,128)(2,1)S(1)}, u32[]{:S(2)}, u32[]{:S(2)}) collective-permute-start(bf16[512,2048]{1,0:T(8,128)(2,1)S(1)} %slice.602), channel_id=1, source_target_pairs={{0,4},{4,0},{1,5},{5,1},{2,6},{6,2},{3,7},{7,3},{8,12},{12,8},{9,1... | collective-permute-start | bytes 6291464 | tf_op jit(solution)/shard_map/ppermute | solution.py:73
  817.2 38.5 %collective-permute-start.55 = (bf16[2,2,2,128,2,256]{5,3,4,2,1,0:T(8,128)(2,1)}, bf16[2,2,2,128,2,256]{5,3,4,2,1,0:T(8,128)(2,1)}, u32[]{:S(2)}, u32[]{:S(2)}) collective-permute-start(bf16[2,2,2,128,2,256]{5,3,4,2,1,0:T(8,128)(2,1)} %slice_bitcast_fusion), channel_id=1, source_target_pairs={{0,4},{4,0},{1,5},{5,1},{2,6},{6,2},{3,7},{7,3},{8,12},{12,8},{9,1... | collective-permute-start | bytes 3145736 | tf_op jit(solution)/shard_map/ppermute | solution.py:73
  837.8 75.1 %collective-permute-start.58 = (bf16[1024,2048]{1,0:T(8,128)(2,1)S(1)}, bf16[1024,2048]{1,0:T(8,128)(2,1)S(1)}, u32[]{:S(2)}, u32[]{:S(2)}) collective-permute-start(bf16[1024,2048]{1,0:T(8,128)(2,1)S(1)} %convolution_convert_fusion.2), channel_id=1, source_target_pairs={{0,1},{1,0},{2,3},{3,2},{4,5},{5,4},{6,7},{7,6},{8,9},{9,8},{10,11... | collective-permute-start | bytes 12582920 | tf_op jit(solution)/shard_map/ppermute | solution.py:73
  845.3 42.6 %collective-permute-start.53 = (bf16[2,2,2,128,2,256]{5,3,4,2,1,0:T(8,128)(2,1)S(1)}, bf16[2,2,2,128,2,256]{5,3,4,2,1,0:T(8,128)(2,1)S(1)}, u32[]{:S(2)}, u32[]{:S(2)}) collective-permute-start(bf16[2,2,2,128,2,256]{5,3,4,2,1,0:T(8,128)(2,1)S(1)} %bitcast.474), channel_id=1, source_target_pairs={{0,8},{8,0},{1,9},{9,1},{2,10},{10,2},{3,11},{11,3},{4,12},{12,4},... | collective-permute-start | bytes 3145736 | tf_op jit(solution)/shard_map/ppermute | solution.py:73
  846.4 43.4 %collective-permute-start.60 = (bf16[1024,512]{1,0:T(8,128)(2,1)S(1)}, bf16[1024,512]{1,0:T(8,128)(2,1)S(1)}, u32[]{:S(2)}, u32[]{:S(2)}) collective-permute-start(bf16[1024,512]{1,0:T(8,128)(2,1)S(1)} %pad_maximum_fusion.25), channel_id=1, source_target_pairs={{0,1},{1,0},{2,3},{3,2},{4,5},{5,4},{6,7},{7,6},{8,9},{9,8},{10,11... | collective-permute-start | bytes 3145736 | tf_op jit(solution)/shard_map/ppermute | solution.py:73
  858.7 50.3 %collective-permute-start.56 = (bf16[2,2,128,2,256]{4,2,3,1,0:T(8,128)(2,1)S(1)}, bf16[2,2,128,2,256]{4,2,3,1,0:T(8,128)(2,1)S(1)}, u32[]{:S(2)}, u32[]{:S(2)}) collective-permute-start(bf16[2,2,128,2,256]{4,2,3,1,0:T(8,128)(2,1)S(1)} %slice_bitcast_fusion.4), channel_id=1, source_target_pairs={{0,8},{8,0},{1,9},{9,1},{2,10},{10,2},{3,11},{11,3},{4,12},{12,4},... | collective-permute-start | bytes 1572872 | tf_op jit(solution)/shard_map/ppermute | solution.py:73
  890.2 24.8 %collective-permute-start.61 = (bf16[512,512]{1,0:T(8,128)(2,1)S(1)}, bf16[512,512]{1,0:T(8,128)(2,1)S(1)}, u32[]{:S(2)}, u32[]{:S(2)}) collective-permute-start(bf16[512,512]{1,0:T(8,128)(2,1)S(1)} %slice.761), channel_id=1, source_target_pairs={{0,4},{4,0},{1,5},{5,1},{2,6},{6,2},{3,7},{7,3},{8,12},{12,8},{9,1... | collective-permute-start | bytes 1572872 | tf_op jit(solution)/shard_map/ppermute | solution.py:73
  909.4 36.3 %collective-permute-start.57 = (bf16[2,2,128,2,256]{4,2,3,1,0:T(8,128)(2,1)S(1)}, bf16[2,2,128,2,256]{4,2,3,1,0:T(8,128)(2,1)S(1)}, u32[]{:S(2)}, u32[]{:S(2)}) collective-permute-start(bf16[2,2,128,2,256]{4,2,3,1,0:T(8,128)(2,1)S(1)} %fusion.211), channel_id=1, source_target_pairs={{0,16},{16,0},{1,17},{17,1},{2,18},{18,2},{3,19},{19,3},{4,20},{20... | collective-permute-start | bytes 1572872 | tf_op jit(solution)/shard_map/ppermute | solution.py:73
  914.6 45.4 %collective-permute-start.59 = (bf16[512,2048]{1,0:T(8,128)(2,1)S(1)}, bf16[512,2048]{1,0:T(8,128)(2,1)S(1)}, u32[]{:S(2)}, u32[]{:S(2)}) collective-permute-start(bf16[512,2048]{1,0:T(8,128)(2,1)S(1)} %slice.755), channel_id=1, source_target_pairs={{0,4},{4,0},{1,5},{5,1},{2,6},{6,2},{3,7},{7,3},{8,12},{12,8},{9,1... | collective-permute-start | bytes 6291464 | tf_op jit(solution)/shard_map/ppermute | solution.py:73
  969.7 83.2 %collective-permute-start.64 = (bf16[256,2048]{1,0:T(8,128)(2,1)}, bf16[256,2048]{1,0:T(8,128)(2,1)}, u32[]{:S(2)}, u32[]{:S(2)}) collective-permute-start(bf16[256,2048]{1,0:T(8,128)(2,1)} %get-tuple-element.458), channel_id=1, source_target_pairs={{0,2},{2,0},{1,3},{3,1},{4,6},{6,4},{5,7},{7,5},{8,10},{10,8},{9,1... | collective-permute-start | bytes 3145736 | tf_op jit(solution)/shard_map/ppermute | solution.py:73
  974.0 82.8 %collective-permute-start.67 = (bf16[256,2560]{1,0:T(8,128)(2,1)}, bf16[256,2560]{1,0:T(8,128)(2,1)}, u32[]{:S(2)}, u32[]{:S(2)}) collective-permute-start(bf16[256,2560]{1,0:T(8,128)(2,1)} %get-tuple-element.452), channel_id=1, source_target_pairs={{0,2},{2,0},{1,3},{3,1},{4,6},{6,4},{5,7},{7,5},{8,10},{10,8},{9,1... | collective-permute-start | bytes 3932168 | tf_op jit(solution)/shard_map/ppermute | solution.py:73
  977.3 131.7 %all-to-all-start.1 = ((bf16[8,192,1024]{2,1,0:T(8,128)(2,1)}), bf16[8,192,1024]{2,1,0:T(8,128)(2,1)}, u32[]{:S(2)}, u32[]{:S(2)}) async-start(bf16[8,192,1024]{2,1,0:T(8,128)(2,1)} %pad_maximum_fusion.2), calls=%async_computation.2 | async-start | bytes 6291456 | tf_op jit(solution)/shard_map/all_to_all | solution.py:203
  987.6 56.3 %collective-permute-start.63 = (bf16[512,1152]{0,1:T(8,128)(2,1)S(1)}, bf16[512,1152]{0,1:T(8,128)(2,1)S(1)}, u32[]{:S(2)}, u32[]{:S(2)}) collective-permute-start(bf16[512,1152]{0,1:T(8,128)(2,1)S(1)} %slice.627), channel_id=1, source_target_pairs={{0,4},{4,0},{1,5},{5,1},{2,6},{6,2},{3,7},{7,3},{8,12},{12,8},{9,1... | collective-permute-start | bytes 3538952 | tf_op jit(solution)/shard_map/ppermute | solution.py:73
  1058.8 31.1 %collective-permute-start.68 = (bf16[128,2560]{1,0:T(8,128)(2,1)S(1)}, bf16[128,2560]{1,0:T(8,128)(2,1)S(1)}, u32[]{:S(2)}, u32[]{:S(2)}) collective-permute-start(bf16[128,2560]{1,0:T(8,128)(2,1)S(1)} %slice.775), channel_id=1, source_target_pairs={{0,8},{8,0},{1,9},{9,1},{2,10},{10,2},{3,11},{11,3},{4,12},{12,4},... | collective-permute-start | bytes 1966088 | tf_op jit(solution)/shard_map/ppermute | solution.py:73
  1074.0 24.4 %collective-permute-start.71 = (bf16[128,1152]{0,1:T(8,128)(2,1)S(1)}, bf16[128,1152]{0,1:T(8,128)(2,1)S(1)}, u32[]{:S(2)}, u32[]{:S(2)}) collective-permute-start(bf16[128,1152]{0,1:T(8,128)(2,1)S(1)} %slice.779), channel_id=1, source_target_pairs={{0,8},{8,0},{1,9},{9,1},{2,10},{10,2},{3,11},{11,3},{4,12},{12,4},... | collective-permute-start | bytes 884744 | tf_op jit(solution)/shard_map/ppermute | solution.py:73
  (239 other events, 3693.5 us)
Sparse Core Ops, SparseCore 0:
  76.9 249.1 all-gather.1
  702.7 239.1 reduce-scatter.1
